TPU v7x, 32 devices: a whole 2x2x4 slice. The times are simulated.
32 devices in a mesh: section: 4 (over y, x), tensor: 4 (over z), dp: 2 (over core).
Axes of the slice: x: 2, y: 2, z: 4, core: 2. Of those that a mesh axis runs over, the one named last changes fastest.
Arguments:
- patches: bfloat16 [1536, 8192], P(('section', 'dp'), 'tensor'), may hold values from -12 to 12
- teacher: bfloat16 [1536, 8192], P(('section', 'dp'), 'tensor'), may hold values from -6 to 6
- critic_pairs: int32 [1536, 2], P(('section', 'dp')), may hold values from 0 to 3, as said below
- left_factors: bfloat16 [4, 4, 64, 128, 128], P('section', None, 'tensor'), may hold values from -0.5 to 0.5
- right_factors: bfloat16 [4, 4, 64, 128, 128], P('section', None, 'tensor'), may hold values from -0.5 to 0.5
- norm_gains: bfloat16 [4, 5, 8192], P('section', None, 'tensor'), may hold values from 0.099609375 to 1.8984375
Outputs:
- d_patches: bfloat16 [1536, 8192], P(('section', 'dp'), 'tensor')
- grad_left: float32 [4, 4, 64, 128, 128], P('section', None, 'tensor')
- grad_right: float32 [4, 4, 64, 128, 128], P('section', None, 'tensor')
Inputs may be any that keep to these rules, and one draw needn't show every extreme that they name: `critic_pairs`: each row names two different critics. The rows are cut into aligned blocks, each block being the 192 rows of one index of section+dp. In each block, exactly one third of the rows name the pair of critics 0 and 1. Exactly one sixth of the rows name each of the pairs 0 and 2, 0 and 3, 1 and 2, and 1 and 3. No row names critics 2 and 3 together. So critics 0 and 1 are each named by two thirds of a block's rows, and critics 2 and 3 by one third each. Which rows and which column order are random.
All inputs are finite; a program needn't handle non-finite values.
Results may differ from a plain program's by a relative error of at most 0.012.
Values may be sent and summed in bfloat16 or wider, within the bound.
No kernel may reach another device: no remote copies, remote signals or barrier semaphores. Data moves between devices by JAX's collectives and lax.ppermute only.
A program may use at most 128 MiB of HBM per device.

v0:
```python
import math

import jax
import jax.numpy as jnp
from jax import lax
from jax.sharding import PartitionSpec as P

EPSILON = 1e-06
TANH_SLOPE = 0.7978845608028654
CUBIC_TERM = 0.044715


def shifted(value, axis, steps):
    count = lax.axis_size(axis)
    first, last = (max(0, -steps), min(count, count - steps))
    return lax.ppermute(value, axis, [(source, source + steps) for source in range(first, last)])


def gelu_value(values):
    tangent = jnp.tanh(TANH_SLOPE * (values + CUBIC_TERM * values * values * values))
    return 0.5 * values * (1.0 + tangent)


def gelu_slope(values):
    tangent = jnp.tanh(TANH_SLOPE * (values + CUBIC_TERM * values * values * values))
    return 0.5 * (1.0 + tangent) + 0.5 * values * (1.0 - tangent * tangent) * TANH_SLOPE * (
        1.0 + 3.0 * CUBIC_TERM * values * values
    )


def norm_pair(residuals, gain_pair, model_width):
    squares = lax.psum(
        (
            jnp.sum(residuals[0] * residuals[0], axis=(1, 2)),
            jnp.sum(residuals[1] * residuals[1], axis=(1, 2)),
        ),
        "tensor",
    )
    factors = [lax.rsqrt(squares[member] / model_width + EPSILON) for member in range(2)]
    normed = [
        residuals[member] * factors[member][:, None, None] * gain_pair[member][None]
        for member in range(2)
    ]
    return (factors, normed)


def norm_back_pair(residuals, factors, gain_pair, grad_normed, carried, model_width):
    weighted = [grad_normed[member] * gain_pair[member][None] for member in range(2)]
    inners = lax.psum(
        (
            jnp.sum(weighted[0] * residuals[0], axis=(1, 2)),
            jnp.sum(weighted[1] * residuals[1], axis=(1, 2)),
        ),
        "tensor",
    )
    return [
        carried[member]
        + factors[member][:, None, None] * weighted[member]
        - residuals[member] * (factors[member] ** 3 * inners[member] / model_width)[:, None, None]
        for member in range(2)
    ]


def shards(patches, teacher, critic_pairs, left_factors, right_factors, norm_gains):
    sections = lax.axis_size("section")
    tensor_width = lax.axis_size("tensor")
    replicas = lax.axis_size("dp")
    tok_rows = patches.shape[0]
    feat_local = patches.shape[1]
    layer_count = left_factors.shape[1]
    local_blocks = left_factors.shape[2]
    block_size = left_factors.shape[3]
    all_blocks = local_blocks * tensor_width
    fold_ratio = block_size // all_blocks
    model_width = feat_local * tensor_width
    sixth_rows = tok_rows // 6
    leading = 2 * sixth_rows
    critic_ids = jnp.arange(4, dtype=jnp.int32)
    named_by = (
        (critic_pairs[:, 0:1] == critic_ids[None, :])
        | (critic_pairs[:, 1:2] == critic_ids[None, :])
    ).astype(jnp.int32)
    ranking = jnp.cumsum(named_by, axis=0) - 1
    wide_ids = critic_ids[None, :] < 2
    slot_width = 3 * sixth_rows
    spilled = wide_ids & (ranking >= 3 * sixth_rows)
    destination = jnp.where(spilled, critic_ids[None, :] + 2, critic_ids[None, :])
    slot_index = jnp.where(spilled, ranking - sixth_rows, ranking)
    flat_slot = destination * slot_width + slot_index
    chosen = jnp.take_along_axis(flat_slot, critic_pairs, axis=1)
    slot_total = sections * slot_width
    row_ids = jnp.broadcast_to(jnp.arange(tok_rows, dtype=jnp.int32)[:, None], chosen.shape)
    source_row = (
        jnp.full((slot_total,), tok_rows, jnp.int32).at[chosen.reshape(-1)].set(row_ids.reshape(-1))
    )
    send_patch = (
        patches.at[source_row]
        .get(mode="fill", fill_value=0)
        .reshape(sections, slot_width, local_blocks, block_size)
    )
    send_target = (
        teacher.at[source_row]
        .get(mode="fill", fill_value=0)
        .reshape(sections, slot_width, local_blocks, block_size)
    )
    recv_patch, recv_target = (
        lax.all_to_all(send_patch, "section", split_axis=0, concat_axis=0, tiled=True),
        lax.all_to_all(send_target, "section", split_axis=0, concat_axis=0, tiled=True),
    )
    residuals = [
        recv_patch[:, :leading].reshape(-1, local_blocks, block_size).astype(jnp.float32),
        recv_patch[:, leading:].reshape(-1, local_blocks, block_size).astype(jnp.float32),
    ]
    targets = [
        recv_target[:, :leading].reshape(-1, local_blocks, block_size).astype(jnp.float32),
        recv_target[:, leading:].reshape(-1, local_blocks, block_size).astype(jnp.float32),
    ]
    native = (left_factors[0], right_factors[0], norm_gains[0])
    borrowed = shifted((left_factors, right_factors, norm_gains), "section", 2)
    is_wide = lax.axis_index("section") < 2
    second = (
        jnp.where(is_wide, left_factors, borrowed[0])[0],
        jnp.where(is_wide, right_factors, borrowed[1])[0],
        jnp.where(is_wide, norm_gains, borrowed[2])[0],
    )
    left_sets = (native[0], second[0])
    right_sets = (native[1], second[1])
    gain_sets = (
        native[2].astype(jnp.float32).reshape(layer_count + 1, local_blocks, block_size),
        second[2].astype(jnp.float32).reshape(layer_count + 1, local_blocks, block_size),
    )
    stored = []
    for layer_index in range(layer_count):
        gain_pair = [gain_sets[0][layer_index], gain_sets[1][layer_index]]
        factors, normed = norm_pair(residuals, gain_pair, model_width)
        normed = [normed[member].astype(jnp.bfloat16) for member in range(2)]
        first_out = [
            jnp.einsum(
                "nki,kij->nkj",
                normed[member],
                left_sets[member][layer_index],
                preferred_element_type=jnp.float32,
            ).astype(jnp.bfloat16)
            for member in range(2)
        ]
        permuted = (
            lax.all_to_all(first_out[0], "tensor", split_axis=2, concat_axis=1, tiled=True),
            lax.all_to_all(first_out[1], "tensor", split_axis=2, concat_axis=1, tiled=True),
        )
        permuted = [
            permuted[member].reshape(
                permuted[member].shape[0], all_blocks, local_blocks, fold_ratio
            )
            for member in range(2)
        ]
        right_quads = [
            right_sets[member][layer_index].reshape(
                local_blocks, fold_ratio, all_blocks, block_size
            )
            for member in range(2)
        ]
        mixture = [
            jnp.einsum(
                "nkmp,mpkl->nml",
                permuted[member],
                right_quads[member],
                preferred_element_type=jnp.float32,
            )
            for member in range(2)
        ]
        stored.append((residuals, factors, normed, permuted, mixture, right_quads, gain_pair))
        residuals = [residuals[member] + gelu_value(mixture[member]) for member in range(2)]
    final_gains = [gain_sets[0][layer_count], gain_sets[1][layer_count]]
    factors, outputs = norm_pair(residuals, final_gains, model_width)
    gradients = norm_back_pair(
        residuals,
        factors,
        final_gains,
        [outputs[member] - targets[member] for member in range(2)],
        [jnp.zeros_like(residuals[member]) for member in range(2)],
        model_width,
    )
    left_terms = []
    right_terms = []
    for layer_index in range(layer_count - 1, -1, -1):
        inputs, factors, normed, permuted, mixture, right_quads, gain_pair = stored[layer_index]
        slopes = [
            (gradients[member] * gelu_slope(mixture[member])).astype(jnp.bfloat16)
            for member in range(2)
        ]
        right_grad = [
            jnp.einsum(
                "nkmp,nml->mpkl",
                permuted[member],
                slopes[member],
                preferred_element_type=jnp.float32,
            ).reshape(local_blocks, block_size, block_size)
            for member in range(2)
        ]
        back_moved = [
            jnp.einsum(
                "nml,mpkl->nkmp",
                slopes[member],
                right_quads[member],
                preferred_element_type=jnp.float32,
            )
            .astype(jnp.bfloat16)
            .reshape(slopes[member].shape[0], all_blocks, local_blocks * fold_ratio)
            for member in range(2)
        ]
        arrived = (
            lax.all_to_all(back_moved[0], "tensor", split_axis=1, concat_axis=2, tiled=True),
            lax.all_to_all(back_moved[1], "tensor", split_axis=1, concat_axis=2, tiled=True),
        )
        left_grad = [
            jnp.einsum(
                "nki,nkj->kij", normed[member], arrived[member], preferred_element_type=jnp.float32
            )
            for member in range(2)
        ]
        grad_normed = [
            jnp.einsum(
                "nkj,kij->nki",
                arrived[member],
                left_sets[member][layer_index],
                preferred_element_type=jnp.float32,
            )
            for member in range(2)
        ]
        gradients = norm_back_pair(inputs, factors, gain_pair, grad_normed, gradients, model_width)
        layer_left = jnp.stack(left_grad)
        layer_right = jnp.stack(right_grad)
        layer_left, layer_right = (
            lax.psum(layer_left.astype(jnp.bfloat16), "dp").astype(jnp.float32),
            lax.psum(layer_right.astype(jnp.bfloat16), "dp").astype(jnp.float32),
        )
        left_terms.insert(0, layer_left)
        right_terms.insert(0, layer_right)
    left_stack = jnp.stack(left_terms)
    right_stack = jnp.stack(right_terms)
    repaid = (
        shifted(left_stack[:, 1].astype(jnp.bfloat16), "section", -2).astype(jnp.float32),
        shifted(right_stack[:, 1].astype(jnp.bfloat16), "section", -2).astype(jnp.float32),
    )
    is_wide = lax.axis_index("section") < 2
    left_total = left_stack[:, 0] + jnp.where(is_wide, left_stack[:, 1] + repaid[0], 0.0)
    right_total = right_stack[:, 0] + jnp.where(is_wide, right_stack[:, 1] + repaid[1], 0.0)
    grad_factor = 1.0 / math.sqrt(2 * tok_rows * sections * replicas)
    returned = [
        gradients[member].astype(jnp.bfloat16).reshape(sections, -1, local_blocks, block_size)
        for member in range(2)
    ]
    back_lead, back_trail = (
        lax.all_to_all(returned[0], "section", split_axis=0, concat_axis=0, tiled=True),
        lax.all_to_all(returned[1], "section", split_axis=0, concat_axis=0, tiled=True),
    )
    gathered = jnp.concatenate((back_lead, back_trail), axis=1).reshape(
        slot_total, local_blocks, block_size
    )
    combined = (
        gathered[chosen[:, 0]].astype(jnp.float32) + gathered[chosen[:, 1]].astype(jnp.float32)
    ) * 0.5
    d_patches = combined.astype(jnp.bfloat16).reshape(tok_rows, feat_local)
    return (d_patches, (left_total * grad_factor)[None], (right_total * grad_factor)[None])


def solution(mesh):
    in_specs = (
        P(("section", "dp"), "tensor"),
        P(("section", "dp"), "tensor"),
        P(("section", "dp"), None),
        P("section", None, "tensor", None, None),
        P("section", None, "tensor", None, None),
        P("section", None, "tensor"),
    )
    out_specs = (
        P(("section", "dp"), "tensor"),
        P("section", None, "tensor", None, None),
        P("section", None, "tensor", None, None),
    )
    return jax.shard_map(shards, mesh=mesh, in_specs=in_specs, out_specs=out_specs, check_vma=False)
```

profile of v0, /device:TPU:5, one launch (start us, length us, event | category | flops | bytes accessed | tf_op | source)
XLA Modules:
  0.0 766.3 jit_solution(8685514338078486235)
XLA Ops:
  31.9 6.5 all-to-all-start
  49.0 7.6 all-to-all-done
  64.2 9.9 %all-reduce.10 = (f32[128]{0:T(128)S(1)}, f32[256]{0:T(256)S(1)}) all-reduce(f32[128]{0:T(128)S(1)} %reduce_sum.196, f32[256]{0:T(256)S(1)} %reduce_sum.185), channel_id=1, replica_groups=mesh['section'=4,'tensor'=4,'dp'=2] {'tensor'}, use_global_device_ids=true, to_apply=%region_24.25 | all-reduce | flops 384 | bytes 3072 | tf_op jit(solution)/shard_map/psum | solution.py:32
  86.8 13.9 %collective-permute-done.1 = bf16[1,4,16,128,128]{3,4,2,1,0:T(8,128)(2,1)} collective-permute-done((bf16[1,4,16,128,128]{3,4,2,1,0:T(8,128)(2,1)}, bf16[1,4,16,128,128]{3,4,2,1,0:T(8,128)(2,1)}, u32[]{:S(2)}, u32[]{:S(2)}) %collective-permute-start.1) | collective-permute-done | bytes 2097184 | tf_op jit(solution)/shard_map/ppermute | solution.py:16
  113.3 32.4 %collective-permute-done = bf16[1,4,16,128,128]{3,4,2,1,0:T(8,128)(2,1)} collective-permute-done((bf16[1,4,16,128,128]{3,4,2,1,0:T(8,128)(2,1)}, bf16[1,4,16,128,128]{3,4,2,1,0:T(8,128)(2,1)}, u32[]{:S(2)}, u32[]{:S(2)}) %collective-permute-start) | collective-permute-done | bytes 2097184 | tf_op jit(solution)/shard_map/ppermute | solution.py:16
  159.5 9.9 %all-reduce.9 = (f32[128]{0:T(128)S(1)}, f32[256]{0:T(256)S(1)}) all-reduce(f32[128]{0:T(128)S(1)} %get-tuple-element.49, f32[256]{0:T(256)S(1)} %get-tuple-element.47), channel_id=1, replica_groups=mesh['section'=4,'tensor'=4,'dp'=2] {'tensor'}, use_global_device_ids=true, to_apply=%region_26.27 | all-reduce | flops 384 | bytes 3072 | tf_op jit(solution)/shard_map/psum | solution.py:32
  181.3 5.6 all-to-all-done.12
  186.8 4.9 all-to-all-start.2
  198.3 18.1 %all-to-all-done.2 = bf16[256,16,128]{0,1,2:T(8,128)(2,1)} async-done(((bf16[256,16,128]{0,1,2:T(8,128)(2,1)}), bf16[256,16,128]{0,1,2:T(8,128)(2,1)}, u32[]{:S(2)}, u32[]{:S(2)}) %all-to-all-start.2) | async-done | bytes 1048608 | tf_op jit(solution)/shard_map/all_to_all | solution.py:147
  221.0 6.6 all-reduce.8
  249.5 20.5 %all-to-all-done.3 = bf16[256,16,128]{0,1,2:T(8,128)(2,1)} async-done(((bf16[256,16,128]{0,1,2:T(8,128)(2,1)}), bf16[256,16,128]{0,1,2:T(8,128)(2,1)}, u32[]{:S(2)}, u32[]{:S(2)}) %all-to-all-start.3) | async-done | bytes 1048608 | tf_op jit(solution)/shard_map/all_to_all | solution.py:147
  280.7 8.8 %all-reduce.7 = (f32[128]{0:T(128)S(1)}, f32[256]{0:T(256)S(1)}) all-reduce(f32[128]{0:T(128)S(1)} %get-tuple-element.41, f32[256]{0:T(256)S(1)} %get-tuple-element.39), channel_id=1, replica_groups=mesh['section'=4,'tensor'=4,'dp'=2] {'tensor'}, use_global_device_ids=true, to_apply=%region_30.31 | all-reduce | flops 384 | bytes 3072 | tf_op jit(solution)/shard_map/psum | solution.py:32
  320.4 11.6 %all-to-all-done.4 = bf16[256,16,128]{0,1,2:T(8,128)(2,1)} async-done(((bf16[256,16,128]{0,1,2:T(8,128)(2,1)}), bf16[256,16,128]{0,1,2:T(8,128)(2,1)}, u32[]{:S(2)}, u32[]{:S(2)}) %all-to-all-start.4) | async-done | bytes 1048608 | tf_op jit(solution)/shard_map/all_to_all | solution.py:147
  335.9 8.8 %all-reduce.6 = (f32[128]{0:T(128)S(1)}, f32[256]{0:T(256)S(1)}) all-reduce(f32[128]{0:T(128)S(1)} %get-tuple-element.81, f32[256]{0:T(256)S(1)} %get-tuple-element.83), channel_id=1, replica_groups=mesh['section'=4,'tensor'=4,'dp'=2] {'tensor'}, use_global_device_ids=true, to_apply=%region_32.33 | all-reduce | flops 384 | bytes 3072 | tf_op jit(solution)/shard_map/psum | solution.py:32
  350.3 6.6 all-reduce.5
  385.2 13.9 %all-to-all-done.6 = bf16[256,64,32]{0,2,1:T(8,128)(2,1)} async-done(((bf16[256,64,32]{0,2,1:T(8,128)(2,1)}), bf16[256,64,32]{0,2,1:T(8,128)(2,1)}, u32[]{:S(2)}, u32[]{:S(2)}) %all-to-all-start.6) | async-done | bytes 1048608 | tf_op jit(solution)/shard_map/all_to_all | solution.py:212
  403.8 10.7 %all-reduce.4 = (f32[128]{0:T(128)S(1)}, f32[256]{0:T(256)S(1)}) all-reduce(f32[128]{0:T(128)S(1)} %get-tuple-element.85, f32[256]{0:T(256)S(1)} %get-tuple-element.87), channel_id=1, replica_groups=mesh['section'=4,'tensor'=4,'dp'=2] {'tensor'}, use_global_device_ids=true, to_apply=%region_36.37 | all-reduce | flops 384 | bytes 3072 | tf_op jit(solution)/shard_map/psum | solution.py:49
  414.6 5.0 fusion.89
  425.3 5.3 fusion.25
  451.8 9.2 %all-to-all-done.7 = bf16[256,64,32]{0,2,1:T(8,128)(2,1)} async-done(((bf16[256,64,32]{0,2,1:T(8,128)(2,1)}), bf16[256,64,32]{0,2,1:T(8,128)(2,1)}, u32[]{:S(2)}, u32[]{:S(2)}) %all-to-all-start.7) | async-done | bytes 1048608 | tf_op jit(solution)/shard_map/all_to_all | solution.py:212
  465.8 8.7 %all-reduce.3 = (f32[128]{0:T(128)S(1)}, f32[256]{0:T(256)S(1)}) all-reduce(f32[128]{0:T(128)S(1)} %get-tuple-element.89, f32[256]{0:T(256)S(1)} %get-tuple-element.91), channel_id=1, replica_groups=mesh['section'=4,'tensor'=4,'dp'=2] {'tensor'}, use_global_device_ids=true, to_apply=%region_38.39 | all-reduce | flops 384 | bytes 3072 | tf_op jit(solution)/shard_map/psum | solution.py:49
  484.6 7.4 fusion.30
  495.2 4.6 all-to-all-start.8
  513.4 8.7 %all-to-all-done.8 = bf16[256,64,32]{0,2,1:T(8,128)(2,1)} async-done(((bf16[256,64,32]{0,2,1:T(8,128)(2,1)}), bf16[256,64,32]{0,2,1:T(8,128)(2,1)}, u32[]{:S(2)}, u32[]{:S(2)}) %all-to-all-start.8) | async-done | bytes 1048608 | tf_op jit(solution)/shard_map/all_to_all | solution.py:212
  526.6 8.8 %all-reduce.2 = (f32[128]{0:T(128)S(1)}, f32[256]{0:T(256)S(1)}) all-reduce(f32[128]{0:T(128)S(1)} %get-tuple-element.93, f32[256]{0:T(256)S(1)} %get-tuple-element.95), channel_id=1, replica_groups=mesh['section'=4,'tensor'=4,'dp'=2] {'tensor'}, use_global_device_ids=true, to_apply=%region_40.41 | all-reduce | flops 384 | bytes 3072 | tf_op jit(solution)/shard_map/psum | solution.py:49
  570.4 10.5 %all-to-all-done.9 = bf16[256,64,32]{0,2,1:T(8,128)(2,1)} async-done(((bf16[256,64,32]{0,2,1:T(8,128)(2,1)}), bf16[256,64,32]{0,2,1:T(8,128)(2,1)}, u32[]{:S(2)}, u32[]{:S(2)}) %all-to-all-start.9) | async-done | bytes 1048608 | tf_op jit(solution)/shard_map/all_to_all | solution.py:212
  591.5 8.8 %all-reduce.1 = (f32[128]{0:T(128)S(1)}, f32[256]{0:T(256)S(1)}) all-reduce(f32[128]{0:T(128)S(1)} %get-tuple-element.97, f32[256]{0:T(256)S(1)} %get-tuple-element.99), channel_id=1, replica_groups=mesh['section'=4,'tensor'=4,'dp'=2] {'tensor'}, use_global_device_ids=true, to_apply=%region_42.43 | all-reduce | flops 384 | bytes 3072 | tf_op jit(solution)/shard_map/psum | solution.py:49
  604.2 8.4 %all-to-all-start.19 = ((bf16[4,32,16,128]{3,1,2,0:T(8,128)(2,1)}), bf16[4,32,16,128]{3,1,2,0:T(8,128)(2,1)S(1)}, u32[]{:S(2)}, u32[]{:S(2)}) async-start(bf16[4,32,16,128]{3,1,2,0:T(8,128)(2,1)} %copy.345), calls=%async_computation.19 | async-start | bytes 1048576 | tf_op jit(solution)/shard_map/all_to_all | solution.py:255
  612.6 19.8 %all-reduce.14.cloned.1.call-done = (bf16[1,2,16,128,128]{4,3,2,1,0:T(8,128)(2,1)}, bf16[1,2,16,128,128]{4,3,2,1,0:T(8,128)(2,1)}, bf16[1,2,16,128,128]{4,3,2,1,...) async-done(((bf16[1,2,16,128,128]{4,3,2,1,0:T(8,128)(2,1)}, ...) | async-done | bytes 8388624 | tf_op jit(solution)/shard_map/psum | solution.py:234
  655.0 85.0 %all-to-all-done.10 = bf16[4,64,16,128]{3,1,2,0:T(8,128)(2,1)S(1)} async-done(((bf16[4,64,16,128]{3,1,2,0:T(8,128)(2,1)}), bf16[4,64,16,128]{3,1,2,0:T(8,128)(2,1)S(1)}, u32[]{:S(2)}, u32[]{:S(2)}) %all-to-all-start.10) | async-done | bytes 1048608 | tf_op jit(solution)/shard_map/all_to_all | solution.py:254
  745.7 8.0 %fusion.5 = f32[1,4,16,128,128]{4,3,2,1,0:T(8,128)} fusion(f32[4,2,16,128,128]{4,3,2,1,0:T(8,128)} %copy-done.13, bf16[4,16,128,128]{3,2,1,0:T(8,128)(2,1)} %collective-permute-done.3, pred[]{:T(512)S(6)} %lt.47), kind=kLoop, calls=%fused_computation.15 | loop fusion | flops 5242880 | bytes 14680065 | tf_op jit(solution)/shard_map/broadcast_in_dim | solution.py:264
  753.8 5.2 fusion.2
  (425 shorter events, 350.3 us)
Async XLA Ops:
  7.2 41.8 %collective-permute-start.2 = (bf16[1,5,2048]{2,1,0:T(8,128)(2,1)}, bf16[1,5,2048]{2,1,0:T(8,128)(2,1)S(1)}, u32[]{:S(2)}, u32[]{:S(2)}) collective-permute-start(bf16[1,5,2048]{2,1,0:T(8,128)(2,1)} %param.11), channel_id=1, source_target_pairs={{0,16},{8,24},{1,17},{9,25},{2,18},{10,26},{3,19},{11,27},{4,20},{... | collective-permute-start | bytes 61448 | tf_op jit(solution)/shard_map/ppermute | solution.py:16
  31.9 24.7 %all-to-all-start = ((bf16[4,96,16,128]{3,1,2,0:T(8,128)(2,1)}), bf16[4,96,16,128]{3,1,2,0:T(8,128)(2,1)}, u32[]{:S(2)}, u32[]{:S(2)}) async-start(bf16[4,96,16,128]{3,1,2,0:T(8,128)(2,1)} %get-tuple-element.74), calls=%async_computation | async-start | bytes 3145728 | tf_op jit(solution)/shard_map/all_to_all | solution.py:107
  41.0 59.7 %collective-permute-start.1 = (bf16[1,4,16,128,128]{3,4,2,1,0:T(8,128)(2,1)}, bf16[1,4,16,128,128]{3,4,2,1,0:T(8,128)(2,1)}, u32[]{:S(2)}, u32[]{:S(2)}) collective-permute-start(bf16[1,4,16,128,128]{3,4,2,1,0:T(8,128)(2,1)} %copy.316), channel_id=1, source_target_pairs={{0,16},{8,24},{1,17},{9,25},{2,18},{10,26},{3,19},{11,27},{4,20},{... | collective-permute-start | bytes 6291464 | tf_op jit(solution)/shard_map/ppermute | solution.py:16
  46.4 99.2 %collective-permute-start = (bf16[1,4,16,128,128]{3,4,2,1,0:T(8,128)(2,1)}, bf16[1,4,16,128,128]{3,4,2,1,0:T(8,128)(2,1)}, u32[]{:S(2)}, u32[]{:S(2)}) collective-permute-start(bf16[1,4,16,128,128]{3,4,2,1,0:T(8,128)(2,1)} %copy.313), channel_id=1, source_target_pairs={{0,16},{8,24},{1,17},{9,25},{2,18},{10,26},{3,19},{11,27},{4,20},{... | collective-permute-start | bytes 6291464 | tf_op jit(solution)/shard_map/ppermute | solution.py:16
  49.0 100.8 %copy-start.65 = (bf16[1,1,16,128,128]{4,3,2,1,0:T(8,128)(2,1)}, bf16[1,1,16,128,128]{4,3,2,1,0:T(8,128)(2,1)S(1)}, u32[]{:S(2)}) copy-start(bf16[1,1,16,128,128]{4,3,2,1,0:T(8,128)(2,1)S(1)} %get-tuple-element.54) | copy-start | bytes 1572868
  80.7 28.2 %all-to-all-start.1 = ((bf16[256,16,128]{0,1,2:T(8,128)(2,1)}), bf16[256,16,128]{0,1,2:T(8,128)(2,1)S(1)}, u32[]{:S(2)}, u32[]{:S(2)}) async-start(bf16[256,16,128]{0,1,2:T(8,128)(2,1)} %copy.284), calls=%async_computation.1 | async-start | bytes 2097152 | tf_op jit(solution)/shard_map/all_to_all | solution.py:147
  108.9 45.7 %all-to-all-start.11 = ((bf16[128,16,128]{0,1,2:T(8,128)(2,1)}), bf16[128,16,128]{0,1,2:T(8,128)(2,1)}, u32[]{:S(2)}, u32[]{:S(2)}) async-start(bf16[128,16,128]{0,1,2:T(8,128)(2,1)} %copy.317), calls=%async_computation.11 | async-start | bytes 1048576 | tf_op jit(solution)/shard_map/all_to_all | solution.py:148
  154.6 63.2 %copy-start.3 = (f32[256,16,128]{2,0,1:T(8,128)}, f32[256,16,128]{2,0,1:T(8,128)S(1)}, u32[]{:S(2)}) copy-start(f32[256,16,128]{2,0,1:T(8,128)S(1)} %get-tuple-element.48) | copy-start | bytes 6291460
  172.6 14.3 %all-to-all-start.12 = ((bf16[128,16,128]{0,1,2:T(8,128)(2,1)}), bf16[128,16,128]{0,1,2:T(8,128)(2,1)S(1)}, u32[]{:S(2)}, u32[]{:S(2)}) async-start(bf16[128,16,128]{0,1,2:T(8,128)(2,1)} %copy.320), calls=%async_computation.12 | async-start | bytes 1048576 | tf_op jit(solution)/shard_map/all_to_all | solution.py:148
  186.8 29.6 %all-to-all-start.2 = ((bf16[256,16,128]{0,1,2:T(8,128)(2,1)}), bf16[256,16,128]{0,1,2:T(8,128)(2,1)}, u32[]{:S(2)}, u32[]{:S(2)}) async-start(bf16[256,16,128]{0,1,2:T(8,128)(2,1)} %copy.287), calls=%async_computation.2 | async-start | bytes 2097152 | tf_op jit(solution)/shard_map/all_to_all | solution.py:147
  230.9 12.7 %all-to-all-start.13 = ((bf16[128,16,128]{0,1,2:T(8,128)(2,1)}), bf16[128,16,128]{0,1,2:T(8,128)(2,1)S(1)}, u32[]{:S(2)}, u32[]{:S(2)}) async-start(bf16[128,16,128]{0,1,2:T(8,128)(2,1)} %copy.323), calls=%async_computation.13 | async-start | bytes 1048576 | tf_op jit(solution)/shard_map/all_to_all | solution.py:148
  243.6 26.4 %all-to-all-start.3 = ((bf16[256,16,128]{0,1,2:T(8,128)(2,1)}), bf16[256,16,128]{0,1,2:T(8,128)(2,1)}, u32[]{:S(2)}, u32[]{:S(2)}) async-start(bf16[256,16,128]{0,1,2:T(8,128)(2,1)} %copy.290), calls=%async_computation.3 | async-start | bytes 2097152 | tf_op jit(solution)/shard_map/all_to_all | solution.py:147
  248.2 26.2 %copy-start.57 = (bf16[1,1,16,128,128]{4,3,2,1,0:T(8,128)(2,1)}, bf16[1,1,16,128,128]{4,3,2,1,0:T(8,128)(2,1)S(1)}, u32[]{:S(2)}) copy-start(bf16[1,1,16,128,128]{4,3,2,1,0:T(8,128)(2,1)S(1)} %copy.322) | copy-start | bytes 1572868
  248.2 26.2 %copy-start.16 = (f32[128,16,128]{2,0,1:T(8,128)S(1)}, f32[128,16,128]{2,0,1:T(8,128)}, u32[]{:S(2)}) copy-start(f32[128,16,128]{2,0,1:T(8,128)} %get-tuple-element.46) | copy-start | bytes 3145732
  249.5 26.9 %copy-start.55 = (bf16[128,16,4,32]{0,1,2,3:T(8,128)(2,1)}, bf16[128,16,4,32]{0,1,2,3:T(8,128)(2,1)S(1)}, u32[]{:S(2)}) copy-start(bf16[128,16,4,32]{0,1,2,3:T(8,128)(2,1)S(1)} %copy.324) | copy-start | bytes 1572868
  270.0 22.6 %all-to-all-start.5 = ((bf16[4,96,16,128]{3,1,2,0:T(8,128)(2,1)}), bf16[4,96,16,128]{3,1,2,0:T(8,128)(2,1)}, u32[]{:S(2)}, u32[]{:S(2)}) async-start(bf16[4,96,16,128]{3,1,2,0:T(8,128)(2,1)} %get-tuple-element.73), calls=%async_computation.5 | async-start | bytes 3145728 | tf_op jit(solution)/shard_map/all_to_all | solution.py:108
  292.6 13.1 %all-to-all-start.14 = ((bf16[128,16,128]{0,1,2:T(8,128)(2,1)}), bf16[128,16,128]{0,1,2:T(8,128)(2,1)S(1)}, u32[]{:S(2)}, u32[]{:S(2)}) async-start(bf16[128,16,128]{0,1,2:T(8,128)(2,1)} %copy.326), calls=%async_computation.14 | async-start | bytes 1048576 | tf_op jit(solution)/shard_map/all_to_all | solution.py:148
  305.7 26.4 %all-to-all-start.4 = ((bf16[256,16,128]{0,1,2:T(8,128)(2,1)}), bf16[256,16,128]{0,1,2:T(8,128)(2,1)}, u32[]{:S(2)}, u32[]{:S(2)}) async-start(bf16[256,16,128]{0,1,2:T(8,128)(2,1)} %copy.293), calls=%async_computation.4 | async-start | bytes 2097152 | tf_op jit(solution)/shard_map/all_to_all | solution.py:147
  361.5 13.3 %all-to-all-start.15 = ((bf16[128,64,32]{0,2,1:T(8,128)(2,1)}), bf16[128,64,32]{0,2,1:T(8,128)(2,1)}, u32[]{:S(2)}, u32[]{:S(2)}) async-start(bf16[128,64,32]{0,2,1:T(8,128)(2,1)} %copy.329), calls=%async_computation.15 | async-start | bytes 1048576 | tf_op jit(solution)/shard_map/all_to_all | solution.py:213
  374.8 24.3 %all-to-all-start.6 = ((bf16[256,64,32]{0,2,1:T(8,128)(2,1)}), bf16[256,64,32]{0,2,1:T(8,128)(2,1)}, u32[]{:S(2)}, u32[]{:S(2)}) async-start(bf16[256,64,32]{0,2,1:T(8,128)(2,1)} %copy.298), calls=%async_computation.6 | async-start | bytes 2097152 | tf_op jit(solution)/shard_map/all_to_all | solution.py:212
  382.3 18.1 %copy-start.61 = (bf16[128,16,4,32]{0,3,2,1:T(8,128)(2,1)}, bf16[128,16,4,32]{0,3,2,1:T(8,128)(2,1)S(1)}, u32[]{:S(2)}) copy-start(bf16[128,16,4,32]{0,3,2,1:T(8,128)(2,1)S(1)} %copy.330) | copy-start | bytes 1572868
  421.2 13.3 %all-to-all-start.16 = ((bf16[128,64,32]{0,2,1:T(8,128)(2,1)}), bf16[128,64,32]{0,2,1:T(8,128)(2,1)}, u32[]{:S(2)}, u32[]{:S(2)}) async-start(bf16[128,64,32]{0,2,1:T(8,128)(2,1)} %copy.333), calls=%async_computation.16 | async-start | bytes 1048576 | tf_op jit(solution)/shard_map/all_to_all | solution.py:213
  434.5 26.4 %all-to-all-start.7 = ((bf16[256,64,32]{0,2,1:T(8,128)(2,1)}), bf16[256,64,32]{0,2,1:T(8,128)(2,1)}, u32[]{:S(2)}, u32[]{:S(2)}) async-start(bf16[256,64,32]{0,2,1:T(8,128)(2,1)} %copy.301), calls=%async_computation.7 | async-start | bytes 2097152 | tf_op jit(solution)/shard_map/all_to_all | solution.py:212
  480.2 14.9 %all-to-all-start.17 = ((bf16[128,64,32]{0,2,1:T(8,128)(2,1)}), bf16[128,64,32]{0,2,1:T(8,128)(2,1)}, u32[]{:S(2)}, u32[]{:S(2)}) async-start(bf16[128,64,32]{0,2,1:T(8,128)(2,1)} %copy.337), calls=%async_computation.17 | async-start | bytes 1048576 | tf_op jit(solution)/shard_map/all_to_all | solution.py:213
  495.2 26.9 %all-to-all-start.8 = ((bf16[256,64,32]{0,2,1:T(8,128)(2,1)}), bf16[256,64,32]{0,2,1:T(8,128)(2,1)}, u32[]{:S(2)}, u32[]{:S(2)}) async-start(bf16[256,64,32]{0,2,1:T(8,128)(2,1)} %copy.304), calls=%async_computation.8 | async-start | bytes 2097152 | tf_op jit(solution)/shard_map/all_to_all | solution.py:212
  541.1 13.5 %all-to-all-start.18 = ((bf16[128,64,32]{0,2,1:T(8,128)(2,1)}), bf16[128,64,32]{0,2,1:T(8,128)(2,1)}, u32[]{:S(2)}, u32[]{:S(2)}) async-start(bf16[128,64,32]{0,2,1:T(8,128)(2,1)} %copy.341), calls=%async_computation.18 | async-start | bytes 1048576 | tf_op jit(solution)/shard_map/all_to_all | solution.py:213
  554.6 26.4 %all-to-all-start.9 = ((bf16[256,64,32]{0,2,1:T(8,128)(2,1)}), bf16[256,64,32]{0,2,1:T(8,128)(2,1)}, u32[]{:S(2)}, u32[]{:S(2)}) async-start(bf16[256,64,32]{0,2,1:T(8,128)(2,1)} %copy.307), calls=%async_computation.9 | async-start | bytes 2097152 | tf_op jit(solution)/shard_map/all_to_all | solution.py:212
  558.8 73.5 %all-reduce.14.cloned.1.call-start = ((), (), s32[]{:S(2)}) async-start(), calls=%async_computation.20 | async-start | bytes 16777216 | tf_op jit(solution)/shard_map/psum | solution.py:234
  604.2 47.0 %all-to-all-start.19 = ((bf16[4,32,16,128]{3,1,2,0:T(8,128)(2,1)}), bf16[4,32,16,128]{3,1,2,0:T(8,128)(2,1)S(1)}, u32[]{:S(2)}, u32[]{:S(2)}) async-start(bf16[4,32,16,128]{3,1,2,0:T(8,128)(2,1)} %copy.345), calls=%async_computation.19 | async-start | bytes 1048576 | tf_op jit(solution)/shard_map/all_to_all | solution.py:255
  636.6 109.1 %collective-permute-start.3 = (bf16[4,16,128,128]{3,2,1,0:T(8,128)(2,1)}, bf16[4,16,128,128]{3,2,1,0:T(8,128)(2,1)}, u32[]{:S(2)}, u32[]{:S(2)}) collective-permute-start(bf16[4,16,128,128]{3,2,1,0:T(8,128)(2,1)} %fusion.6), channel_id=1, source_target_pairs={{16,0},{24,8},{17,1},{25,9},{18,2},{26,10},{19,3},{27,11},{20,4},{... | collective-permute-start | bytes 6291464 | tf_op jit(solution)/shard_map/ppermute | solution.py:16
  642.8 110.9 %collective-permute-start.4 = (bf16[4,16,128,128]{3,2,1,0:T(8,128)(2,1)}, bf16[4,16,128,128]{3,2,1,0:T(8,128)(2,1)}, u32[]{:S(2)}, u32[]{:S(2)}) collective-permute-start(bf16[4,16,128,128]{3,2,1,0:T(8,128)(2,1)} %fusion.7), channel_id=1, source_target_pairs={{16,0},{24,8},{17,1},{25,9},{18,2},{26,10},{19,3},{27,11},{20,4},{... | collective-permute-start | bytes 6291464 | tf_op jit(solution)/shard_map/ppermute | solution.py:16
  651.2 88.9 %all-to-all-start.10 = ((bf16[4,64,16,128]{3,1,2,0:T(8,128)(2,1)}), bf16[4,64,16,128]{3,1,2,0:T(8,128)(2,1)S(1)}, u32[]{:S(2)}, u32[]{:S(2)}) async-start(bf16[4,64,16,128]{3,1,2,0:T(8,128)(2,1)} %copy.310), calls=%async_computation.10 | async-start | bytes 2097152 | tf_op jit(solution)/shard_map/all_to_all | solution.py:254
  (91 other events, 422.2 us)
Sparse Core Ops, SparseCore 0:
  585.8 46.5 all-reduce.13
where the time goes:
time: 782 us; the launch traced here: 766 us
  waiting for transfers between devices  273 us (35%)
  local copies, waits for them, and re-layouts  105 us (13%)
  starting transfers between devices  101 us (13%)
  other arithmetic  93.6 us (12%)
  matrix products  90.4 us (12%)
  blocking collectives  87.8 us (11%)
  between operations  16.1 us (2%)
    all_to_all x1, waiting for transfers between devices, shards(): lax.all_to_all(returned[0], 'section', split_axis=0, concat_axis=0, tiled...  85 us
    all_to_all x4, waiting for transfers between devices, shards(): lax.all_to_all(first_out[0], 'tensor', split_axis=2, concat_axis=1, tiled...  53.7 us
    ppermute x5, waiting for transfers between devices, shifted(): lax.ppermute(value, axis, [(source, source + steps) for source in range(f...  46.2 us
    psum x5, blocking collectives, norm_pair(): lax.psum((jnp.sum(residuals[0] * residuals[0], axis=(1, 2)), jnp.sum(resi...  44.1 us
    psum x5, blocking collectives, norm_back_pair(): lax.psum((jnp.sum(weighted[0] * residuals[0], axis=(1, 2)), jnp.sum(weigh...  43.7 us
    all_to_all x4, waiting for transfers between devices, shards(): lax.all_to_all(back_moved[0], 'tensor', split_axis=1, concat_axis=2, tile...  42.3 us
    convert_element_type x8, other arithmetic, shards(): (gradients[member] * gelu_slope(mixture[member])).astype(jnp.bfloat16)  37.1 us
    unnamed x200, local copies, waits for them, and re-layouts  24.5 us
  transfers between devices with their start and end apart: 26, of which 19 were waited for; matrix products, arithmetic and copies ran while one was open for 27% of the time, Pallas kernels for 0%

commit v1 on v0

--- a/solution.py
+++ b/solution.py
@@ -3,6 +3,8 @@
 import jax
 import jax.numpy as jnp
 from jax import lax
+from jax.experimental import pallas as pl
+from jax.experimental.pallas import tpu as pltpu
 from jax.sharding import PartitionSpec as P
 
 EPSILON = 1e-06
@@ -61,7 +63,7 @@
     ]
 
 
-def shards(patches, teacher, critic_pairs, left_factors, right_factors, norm_gains):
+def layered_shards(patches, teacher, critic_pairs, left_factors, right_factors, norm_gains):
     sections = lax.axis_size("section")
     tensor_width = lax.axis_size("tensor")
     replicas = lax.axis_size("dp")
@@ -264,6 +266,603 @@
     return (d_patches, (left_total * grad_factor)[None], (right_total * grad_factor)[None])
 
 
+VMEM_LIMIT = 60 * 1024 * 1024
+CHUNKS = 8
+AXES = ("section", "tensor", "dp")
+
+
+def planes_fit(mesh):
+    sections = mesh.shape["section"]
+    paired = mesh.shape["dp"] == 2 and sections & (sections - 1) == 0
+    return paired and mesh.shape["tensor"] == sections
+
+
+def inner_dot(left, right, left_dim, right_dim):
+    return lax.dot_general(
+        left,
+        right,
+        (((left_dim,), (right_dim,)), ((), ())),
+        preferred_element_type=jnp.float32,
+    )
+
+
+def fold_rows(values):
+    return jnp.sum(values.reshape(values.shape[0] // 8, 8, values.shape[1]), axis=0)
+
+
+def block_rows(block, size):
+    return pl.ds(pl.multiple_of(block * size, size), size)
+
+
+def column(gain_ref, block, slots):
+    blocks = gain_ref.shape[1]
+    picked = lax.broadcasted_iota(jnp.int32, (blocks, slots), 0) == block
+    return inner_dot(gain_ref[...], picked.astype(jnp.bfloat16), 1, 0)
+
+
+def chunk_copy(source, target, sems, chunk):
+    rows = target.shape[0] // CHUNKS
+    at = pl.ds(pl.multiple_of(chunk * rows, rows), rows)
+    return pltpu.make_async_copy(source.at[at], target.at[at], sems.at[chunk])
+
+
+def start_chunks(source, target, sems):
+    for chunk in range(CHUNKS):
+        chunk_copy(source, target, sems, chunk).start()
+
+
+def wait_chunks(source, target, sems):
+    for chunk in range(CHUNKS):
+        chunk_copy(source, target, sems, chunk).wait()
+
+
+def quarter_copies(pieces, whole, sems, me, outward=False):
+    rows = pieces[0].shape[0]
+    copies = []
+    for k, piece in enumerate(pieces):
+        part = whole.at[pl.ds(pl.multiple_of((me ^ k) * rows, rows), rows)]
+        ends = (part, piece) if outward else (piece, part)
+        copies.append(pltpu.make_async_copy(*ends, sems.at[k]))
+    return copies
+
+
+def factor_copies(own, peer, held, sems, side, outward=False):
+    half = own.shape[0]
+    copies = []
+    for part, ref in enumerate((own, peer)):
+        inside = held.at[pl.ds(part * half, half), side]
+        ends = (inside, ref.at[:, side]) if outward else (ref.at[:, side], inside)
+        copies.append(pltpu.make_async_copy(*ends, sems.at[2 * side + part]))
+    return copies
+
+
+def by_chunk(blocks, step, carry, before=None, after=None):
+    per_chunk = blocks // CHUNKS
+
+    def one(chunk, carry):
+        if before is not None:
+            before(chunk)
+        carry = lax.fori_loop(
+            0, per_chunk, lambda at, now: step(chunk * per_chunk + at, now), carry, unroll=True
+        )
+        if after is not None:
+            after(chunk)
+        return carry
+
+    return lax.fori_loop(0, CHUNKS, one, carry)
+
+
+def forward_kernel(first, inputs, table_ref, gain_ref, sums_ref, *refs):
+    sources, refs = refs[:inputs], refs[inputs:]
+    own, peer = sources[-2:]
+    out_ref, u_ref, z_ref, slope_ref, scale_ref, next_ref = refs[:6]
+    raw, h, w, u, z, slope, mid, in_sems, w_sems, out_sems = refs[6:]
+    features, slots = h.shape
+    size = w.shape[-1]
+    chunk_blocks = w.shape[2]
+    blocks = features // size
+    fold = size // blocks
+
+    left_in = factor_copies(own, peer, w, w_sems, 0)
+    right_in = factor_copies(own, peer, w, w_sems, 1)
+    if first:
+        pieces = quarter_copies(sources[:-2], raw, in_sems, table_ref[blocks])
+        for copy in pieces + left_in + right_in:
+            copy.start()
+        for copy in pieces:
+            copy.wait()
+
+        def squares(block, total):
+            rows = block_rows(block, size)
+            part = raw[rows, :].astype(jnp.float32)
+            h[rows, :] = part
+            return total + fold_rows(part * part)
+
+        total = by_chunk(blocks, squares, jnp.zeros((8, slots), jnp.float32))
+    else:
+        for copy in left_in:
+            copy.start()
+        start_chunks(sources[0], h, in_sems)
+        for copy in right_in:
+            copy.start()
+        total = sums_ref[...]
+    scale = lax.rsqrt(jnp.sum(total, axis=0, keepdims=True) / features + EPSILON)
+    scale_ref[...] = jnp.broadcast_to(scale, scale_ref.shape)
+    for copy in left_in:
+        copy.wait()
+
+    def arrive(chunk):
+        if not first:
+            chunk_copy(sources[0], h, in_sems, chunk).wait()
+
+    def left(block, carry):
+        rows = block_rows(block, size)
+        place = table_ref[block]
+        normed = (h[rows, :] * scale * column(gain_ref, block, slots)).astype(jnp.bfloat16)
+        u[rows, :] = normed
+        weight = w[place // chunk_blocks, 0, place % chunk_blocks]
+        mid[rows, :] = inner_dot(weight, normed, 0, 0)
+        return carry
+
+    def leave_left(chunk):
+        chunk_copy(u, u_ref, out_sems.at[0], chunk).start()
+
+    by_chunk(blocks, left, 0, arrive, leave_left)
+    for copy in right_in:
+        copy.wait()
+
+    def right(block, total):
+        rows = block_rows(block, size)
+        place = table_ref[block]
+        moved = [mid[pl.ds(block * fold + q, blocks, stride=size), :] for q in range(fold)]
+        moved = jnp.concatenate(moved, axis=0).astype(jnp.bfloat16)
+        z[rows, :] = moved
+        weight = w[place // chunk_blocks, 1, place % chunk_blocks]
+        mixture = inner_dot(weight, moved, 0, 0)
+        squared = mixture * mixture
+        tangent = jnp.tanh(mixture * (TANH_SLOPE + (TANH_SLOPE * CUBIC_TERM) * squared))
+        half = 0.5 + 0.5 * tangent
+        following = h[rows, :] + mixture * half
+        h[rows, :] = following
+        steep = half + mixture * (1.0 - tangent * tangent) * (
+            0.5 * TANH_SLOPE + (1.5 * TANH_SLOPE * CUBIC_TERM) * squared
+        )
+        slope[rows, :] = steep.astype(jnp.bfloat16)
+        return total + fold_rows(following * following)
+
+    leaving = ((h, out_ref, 1), (z, z_ref, 2), (slope, slope_ref, 3))
+
+    def leave_right(chunk):
+        for source, target, at in leaving:
+            chunk_copy(source, target, out_sems.at[at], chunk).start()
+
+    next_ref[...] = by_chunk(blocks, right, jnp.zeros((8, slots), jnp.float32), None, leave_right)
+    for source, target, at in ((u, u_ref, 0),) + leaving:
+        wait_chunks(source, target, out_sems.at[at])
+
+
+def backward_kernel(turning, last, inputs, table_ref, gain_ref, end_gain_ref, scale_ref, *refs):
+    sources, refs = refs[:inputs], refs[inputs:]
+    slope_ref, z_ref, u_ref, own, peer = sources[:5]
+    sources = sources[5:]
+    count = 4 if last else 1
+    outs, refs = refs[:count], refs[count:]
+    own_grad, peer_grad = refs[:2]
+    g, slope, z, u, h, w, gw, mid, turned, top, goal = refs[2:13]
+    in_sems, w_sems, out_sems, gw_sems = refs[13:]
+    features, slots = g.shape
+    size = w.shape[-1]
+    chunk_blocks = w.shape[2]
+    blocks = features // size
+    fold = size // blocks
+    me = table_ref[blocks]
+
+    left_in = factor_copies(own, peer, w, w_sems, 0)
+    right_in = factor_copies(own, peer, w, w_sems, 1)
+    if turning:
+        h_ref, top_ref = sources[:2]
+        goals = quarter_copies(sources[2:], goal, in_sems.at[5], me)
+        start_chunks(top_ref, top, in_sems.at[0])
+        for copy in goals:
+            copy.start()
+    elif last:
+        starts = quarter_copies(sources[1:], h, in_sems.at[5], me)
+        start_chunks(sources[0], g, in_sems.at[0])
+    else:
+        h_ref, g_ref = sources
+        start_chunks(g_ref, g, in_sems.at[0])
+    for copy in right_in:
+        copy.start()
+    start_chunks(slope_ref, slope, in_sems.at[1])
+    start_chunks(z_ref, z, in_sems.at[2])
+    for copy in left_in:
+        copy.start()
+    start_chunks(u_ref, u, in_sems.at[3])
+    if last:
+        for copy in starts:
+            copy.start()
+    else:
+        start_chunks(h_ref, h, in_sems.at[4])
+
+    if turning:
+        zero = jnp.zeros((8, slots), jnp.float32)
+
+        def sums(block, totals):
+            rows = block_rows(block, size)
+            part = top[rows, :]
+            scaled = part * column(end_gain_ref, block, slots)
+            return (
+                totals[0] + fold_rows(part * part),
+                totals[1] + fold_rows(scaled * scaled),
+                totals[2] + fold_rows(scaled * goal[rows, :].astype(jnp.float32)),
+            )
+
+        for copy in goals:
+            copy.wait()
+        totals = by_chunk(
+            blocks, sums, (zero, zero, zero), lambda chunk: chunk_copy(top_ref, top, in_sems.at[0], chunk).wait()
+        )
+        squares, gained, crossed = [jnp.sum(total, axis=0, keepdims=True) for total in totals]
+        end_scale = lax.rsqrt(squares / features + EPSILON)
+        end_back = end_scale * end_scale * end_scale * (end_scale * gained - crossed) / features
+
+    for copy in right_in:
+        copy.wait()
+
+    def arrive_right(chunk):
+        if not turning:
+            chunk_copy(sources[0] if last else g_ref, g, in_sems.at[0], chunk).wait()
+        chunk_copy(slope_ref, slope, in_sems.at[1], chunk).wait()
+        chunk_copy(z_ref, z, in_sems.at[2], chunk).wait()
+
+    def right(block, carry):
+        rows = block_rows(block, size)
+        place = table_ref[block]
+        at = (place // chunk_blocks, 1, place % chunk_blocks)
+        if turning:
+            part = top[rows, :]
+            gain = column(end_gain_ref, block, slots)
+            error = (part * end_scale * gain - goal[rows, :].astype(jnp.float32)) * gain
+            gradient = end_scale * error - part * end_back
+            g[rows, :] = gradient
+        else:
+            gradient = g[rows, :]
+        steep = (gradient * slope[rows, :].astype(jnp.float32)).astype(jnp.bfloat16)
+        gw[at] = inner_dot(z[rows, :], steep, 1, 1).astype(jnp.bfloat16)
+        mid[rows, :] = inner_dot(w[at], steep, 1, 0)
+        return carry
+
+    by_chunk(blocks, right, 0, arrive_right)
+    right_out = factor_copies(own_grad, peer_grad, gw, gw_sems, 1, outward=True)
+    for copy in right_out:
+        copy.start()
+    for copy in left_in:
+        copy.wait()
+    scale = scale_ref[0:1, :]
+    if last:
+        for copy in starts:
+            copy.wait()
+
+    def arrive_left(chunk):
+        chunk_copy(u_ref, u, in_sems.at[3], chunk).wait()
+        if not last:
+            chunk_copy(h_ref, h, in_sems.at[4], chunk).wait()
+
+    def left(block, total):
+        rows = block_rows(block, size)
+        place = table_ref[block]
+        at = (place // chunk_blocks, 0, place % chunk_blocks)
+        slot = block % turned.shape[0]
+        for q in range(fold):
+            turned[slot, pl.ds(q, blocks, stride=fold), :] = mid[
+                pl.ds(q * blocks + block, blocks, stride=size), :
+            ]
+        arrived = turned[slot].astype(jnp.bfloat16)
+        gw[at] = inner_dot(u[rows, :], arrived, 1, 1).astype(jnp.bfloat16)
+        weighted = inner_dot(w[at], arrived, 1, 0) * column(gain_ref, block, slots)
+        g[rows, :] = g[rows, :] + scale * weighted
+        return total + fold_rows(weighted * h[rows, :].astype(jnp.float32))
+
+    total = by_chunk(blocks, left, jnp.zeros((8, slots), jnp.float32), arrive_left)
+    left_out = factor_copies(own_grad, peer_grad, gw, gw_sems, 0, outward=True)
+    for copy in left_out:
+        copy.start()
+    back = scale * scale * scale * jnp.sum(total, axis=0, keepdims=True) / features
+
+    def finish(block, carry):
+        rows = block_rows(block, size)
+        ended = g[rows, :] - h[rows, :].astype(jnp.float32) * back
+        if last:
+            u[rows, :] = ended.astype(jnp.bfloat16)
+        else:
+            g[rows, :] = ended
+        return carry
+
+    if last:
+        by_chunk(blocks, finish, 0)
+        ends = quarter_copies(outs, u, out_sems, me, outward=True)
+        for copy in ends:
+            copy.start()
+        for copy in ends:
+            copy.wait()
+    else:
+        by_chunk(blocks, finish, 0, None, lambda chunk: chunk_copy(g, outs[0], out_sems, chunk).start())
+        wait_chunks(g, outs[0], out_sems)
+    for copy in right_out + left_out:
+        copy.wait()
+
+
+def shape_of(shape, dtype):
+    return jax.ShapeDtypeStruct(shape, dtype)
+
+
+SMEM = pl.BlockSpec(memory_space=pltpu.SMEM)
+INSIDE = pl.BlockSpec(memory_space=pltpu.VMEM)
+OUTSIDE = pl.BlockSpec(memory_space=pl.ANY)
+
+
+def run_forward(table, gain, sums, held, weights, whole, after=()):
+    first = len(held) > 1
+    sources = (*held, *weights)
+    half = weights[0].shape
+    out_shape = (
+        shape_of(whole, jnp.float32),
+        shape_of(whole, jnp.bfloat16),
+        shape_of(whole, jnp.bfloat16),
+        shape_of(whole, jnp.bfloat16),
+        shape_of((8, whole[1]), jnp.float32),
+        shape_of((8, whole[1]), jnp.float32),
+    )
+
+    def kernel(table_ref, gain_ref, sums_ref, *refs):
+        extra = len(sources) + len(after)
+        used = refs[: len(sources)] + refs[extra:]
+        forward_kernel(first, len(sources), table_ref, gain_ref, sums_ref, *used)
+
+    return pl.pallas_call(
+        kernel,
+        in_specs=[SMEM, INSIDE, INSIDE] + [OUTSIDE] * (len(sources) + len(after)),
+        out_specs=[OUTSIDE] * 4 + [INSIDE] * 2,
+        out_shape=out_shape,
+        scratch_shapes=[
+            pltpu.VMEM(whole if first else (16, 128), jnp.bfloat16),
+            pltpu.VMEM(whole, jnp.float32),
+            pltpu.VMEM((2 * half[0],) + half[1:], jnp.bfloat16),
+            pltpu.VMEM(whole, jnp.bfloat16),
+            pltpu.VMEM(whole, jnp.bfloat16),
+            pltpu.VMEM(whole, jnp.bfloat16),
+            pltpu.VMEM(whole, jnp.float32),
+            pltpu.SemaphoreType.DMA((CHUNKS,)),
+            pltpu.SemaphoreType.DMA((4,)),
+            pltpu.SemaphoreType.DMA((4, CHUNKS)),
+        ],
+        compiler_params=pltpu.CompilerParams(vmem_limit_bytes=VMEM_LIMIT),
+        cost_estimate=pl.CostEstimate(
+            flops=FORWARD_COST, bytes_accessed=20 * whole[0] * whole[1], transcendentals=0
+        ),
+        name="forward_layer",
+    )(table, gain, sums, *sources, *after)
+
+
+def run_backward(table, gain, end_gain, scale, kept, weights, sources, turning, last, after=()):
+    whole = kept[0].shape
+    sources = (*kept, *weights, *sources)
+    half = weights[0].shape
+    width = 4
+    ends = [shape_of((whole[0] // width, whole[1]), jnp.bfloat16)] * width if last else [
+        shape_of(whole, jnp.float32)
+    ]
+
+    def kernel(table_ref, gain_ref, end_gain_ref, scale_ref, *refs):
+        extra = len(sources) + len(after)
+        used = refs[: len(sources)] + refs[extra:]
+        backward_kernel(
+            turning, last, len(sources), table_ref, gain_ref, end_gain_ref, scale_ref, *used
+        )
+
+    small = (16, 128)
+    return pl.pallas_call(
+        kernel,
+        in_specs=[SMEM] + [INSIDE] * 3 + [OUTSIDE] * (len(sources) + len(after)),
+        out_specs=[OUTSIDE] * (len(ends) + 2),
+        out_shape=ends + [shape_of(half, jnp.bfloat16)] * 2,
+        scratch_shapes=[
+            pltpu.VMEM(whole, jnp.float32),
+            pltpu.VMEM(whole, jnp.bfloat16),
+            pltpu.VMEM(whole, jnp.bfloat16),
+            pltpu.VMEM(whole, jnp.bfloat16),
+            pltpu.VMEM(whole, jnp.bfloat16 if last else jnp.float32),
+            pltpu.VMEM((2 * half[0],) + half[1:], jnp.bfloat16),
+            pltpu.VMEM((2 * half[0],) + half[1:], jnp.bfloat16),
+            pltpu.VMEM(whole, jnp.float32),
+            pltpu.VMEM((8, half[-1], whole[1]), jnp.float32),
+            pltpu.VMEM(whole if turning else small, jnp.float32),
+            pltpu.VMEM(whole if turning else small, jnp.bfloat16),
+            pltpu.SemaphoreType.DMA((6, CHUNKS)),
+            pltpu.SemaphoreType.DMA((4,)),
+            pltpu.SemaphoreType.DMA((CHUNKS,)),
+            pltpu.SemaphoreType.DMA((4,)),
+        ],
+        compiler_params=pltpu.CompilerParams(vmem_limit_bytes=VMEM_LIMIT),
+        cost_estimate=pl.CostEstimate(
+            flops=BACKWARD_COST, bytes_accessed=30 * whole[0] * whole[1], transcendentals=0
+        ),
+        name="backward_layer",
+    )(table, gain, end_gain, scale, *sources, *after)
+
+
+FORWARD_COST = 15_000_000_000
+BACKWARD_COST = 18_000_000_000
+
+
+def plane_routes(width, replicas):
+    bits = width.bit_length() - 1
+    orders = [[(step + d) % bits for step in range(bits)] for d in range(replicas)]
+    every = [(s, t, d) for s in range(width) for t in range(width) for d in range(replicas)]
+
+    def route(move):
+        def index(s, t, d):
+            return (s * width + t) * replicas + d
+
+        return [(index(*place), index(*move(*place))) for place in every]
+
+    across = [route(lambda s, t, d, at=at: (s ^ (1 << orders[d][at]), t, d)) for at in range(bits)]
+    cores = route(lambda s, t, d: (s, t, 1 - d))
+    sections = [route(lambda s, t, d, k=k: (s ^ k, t, d)) for k in range(width)]
+    planes = [route(lambda s, t, d, k=k: (s, t ^ k, d)) for k in range(width)]
+    homes = [route(lambda s, t, d, k=k: (t, s ^ k, d)) for k in range(width)]
+    ranks = [[0] * width for d in range(replicas)]
+    for d in range(replicas):
+        for r in range(width):
+            ranks[d][sum(((r >> at) & 1) << orders[d][at] for at in range(bits))] = r
+    return across, cores, sections, planes, homes, ranks
+
+
+def plane_shards(patches, teacher, critic_pairs, left_factors, right_factors, norm_gains):
+    width = lax.axis_size("section")
+    replicas = lax.axis_size("dp")
+    tok_rows, feat_local = patches.shape
+    layer_count, local_blocks, size = left_factors.shape[1:4]
+    features = feat_local * width
+    blocks = features // size
+    wide = 2 * tok_rows // 3
+    whole = (features, wide)
+    chunk = local_blocks // (replicas * width)
+    across, cores, sections, planes, homes, ranks = plane_routes(width, replicas)
+    section = lax.axis_index("section")
+    tensor = lax.axis_index("tensor")
+    core = lax.axis_index("dp")
+
+    layer_rows = 2 * chunk * size
+
+    def piece_for(distance):
+        start = (core * width + (section ^ distance)) * chunk
+        parts = [
+            lax.dynamic_slice_in_dim(factors[0], start, chunk, axis=1)
+            for factors in (left_factors, right_factors)
+        ]
+        return jnp.stack(parts, axis=1).reshape(layer_count, layer_rows, size)
+
+    pieces = [piece_for(distance) for distance in range(width)]
+    gain_rows = norm_gains[0].reshape(-1, size)
+    groups = [(0,), (1,), tuple(range(2, layer_count))]
+    weights = []
+    arrived_gains = None
+    for group in groups:
+        sent = [piece[group[0] : group[-1] + 1].reshape(-1, size) for piece in pieces]
+        if group[0] == 0:
+            sent = [jnp.concatenate([value, gain_rows], axis=0) for value in sent]
+        sent = [sent[0]] + [
+            lax.ppermute(sent[distance], AXES, sections[distance]) for distance in range(1, width)
+        ]
+        spread = jnp.stack(sent)
+        sent = [
+            lax.dynamic_index_in_dim(spread, section ^ tensor ^ distance, 0, keepdims=False)
+            for distance in range(width)
+        ]
+        sent = [sent[0]] + [
+            lax.ppermute(sent[distance], AXES, planes[distance]) for distance in range(1, width)
+        ]
+        if group[0] == 0:
+            arrived_gains = jnp.stack([value[layer_rows:] for value in sent])
+        for at in range(len(group)):
+            rows = slice(at * layer_rows, (at + 1) * layer_rows)
+            mine = jnp.stack([value[rows] for value in sent])
+            for route in across:
+                mine = jnp.concatenate([mine, lax.ppermute(mine, AXES, route)], axis=0)
+            other = lax.ppermute(mine, AXES, cores)
+            weights.append([part.reshape(-1, 2, chunk, size, size) for part in (mine, other)])
+    gains = arrived_gains[jnp.arange(width) ^ tensor]
+    gains = gains.reshape(width, layer_count + 1, local_blocks, size).transpose(1, 3, 0, 2)
+    gains = gains.reshape(layer_count + 1, size, blocks)
+
+    block = jnp.arange(blocks, dtype=jnp.int32)
+    rest = block % local_blocks
+    replica = rest // (width * chunk)
+    rank = jnp.array(ranks, jnp.int32)[replica, section ^ ((rest // chunk) % width)]
+    part = (replica != core).astype(jnp.int32)
+    table = ((part * width + rank) * width + (tensor ^ (block // local_blocks))) * chunk + rest % chunk
+    table = jnp.concatenate([table, tensor[None]]).astype(jnp.int32)
+
+    critic_ids = jnp.arange(width, dtype=jnp.int32) ^ tensor
+    named = (critic_pairs[:, 0:1] == critic_ids) | (critic_pairs[:, 1:2] == critic_ids)
+    earlier = jnp.tril(jnp.ones((tok_rows, tok_rows), jnp.bfloat16), -1)
+    rank = jnp.dot(earlier, named.astype(jnp.bfloat16), preferred_element_type=jnp.float32)
+    rank = rank.astype(jnp.int32)
+    places = jnp.arange(wide, dtype=jnp.int32)
+    chosen = [
+        (named[:, k : k + 1] & (rank[:, k : k + 1] == places)).astype(jnp.bfloat16) for k in range(width)
+    ]
+
+    def dispatch(values):
+        sent = [inner_dot(values, chosen[k], 0, 0).astype(jnp.bfloat16) for k in range(width)]
+        return [sent[0]] + [lax.ppermute(sent[k], AXES, planes[k]) for k in range(1, width)]
+
+    start = dispatch(patches)
+    target = dispatch(teacher)
+
+    stored = []
+    residual = start
+    sums = jnp.zeros((8, wide), jnp.float32)
+    for layer in range(layer_count):
+        following, u, z, slope, scale, sums = run_forward(
+            table, gains[layer], sums, residual, weights[layer], whole
+        )
+        stored.append(((slope, z, u), scale, residual))
+        residual = (following,)
+
+    def added(one, two):
+        return (one.astype(jnp.float32) + two.astype(jnp.float32)).astype(jnp.bfloat16)
+
+    summed = []
+    gradient = None
+    for layer in range(layer_count - 1, -1, -1):
+        turning = layer == layer_count - 1
+        last = layer == 0
+        kept, scale, inputs = stored[layer]
+        if turning:
+            sources = (*inputs, *residual, *target)
+        elif last:
+            sources = (gradient, *inputs)
+        else:
+            sources = (*inputs, gradient)
+        *gradient, mine, other = run_backward(
+            table, gains[layer], gains[layer_count], scale, kept, weights[layer], sources, turning, last
+        )
+        gradient = gradient if last else gradient[0]
+        mine = added(mine, lax.ppermute(other, AXES, cores))
+        for route in across[::-1]:
+            half = mine.shape[0] // 2
+            mine = added(mine[:half], lax.ppermute(mine[half:], AXES, route))
+        summed.insert(0, mine.reshape(width, layer_rows, size))
+
+    def to_home(value):
+        sent = [
+            lax.dynamic_index_in_dim(value, section ^ tensor ^ k, 0, keepdims=False) for k in range(width)
+        ]
+        came = jnp.stack([lax.ppermute(sent[k], AXES, homes[k]) for k in range(width)])
+        return came, lax.ppermute(came, AXES, cores)
+
+    returned = [gradient[0]] + [lax.ppermute(gradient[k], AXES, planes[k]) for k in range(1, width)]
+    combined = sum(inner_dot(chosen[k], returned[k], 1, 1) for k in range(width))
+    d_patches = (0.5 * combined).astype(jnp.bfloat16)
+
+    grad_factor = 1.0 / math.sqrt(2 * tok_rows * width * replicas)
+    late = to_home(jnp.concatenate(summed[1:], axis=1))
+    early = to_home(summed[0])
+    pair = [jnp.concatenate([one, two], axis=1) for one, two in zip(early, late)]
+    order = jnp.arange(width) ^ tensor
+    pair = [
+        value[order].reshape(width, layer_count, 2, chunk, size, size).transpose(2, 1, 0, 3, 4, 5)
+        for value in pair
+    ]
+    pair = [value.reshape(2, layer_count, width * chunk, size, size) for value in pair]
+    low = jnp.where(core == 0, pair[0], pair[1])
+    high = jnp.where(core == 0, pair[1], pair[0])
+    grads = jnp.concatenate([low, high], axis=2).astype(jnp.float32) * grad_factor
+    return (d_patches, grads[0][None], grads[1][None])
+
+
 def solution(mesh):
     in_specs = (
         P(("section", "dp"), "tensor"),
@@ -278,4 +877,6 @@
         P("section", None, "tensor", None, None),
         P("section", None, "tensor", None, None),
     )
-    return jax.shard_map(shards, mesh=mesh, in_specs=in_specs, out_specs=out_specs, check_vma=False)
+    body = plane_shards if planes_fit(mesh) else layered_shards
+    return jax.shard_map(
+        body, mesh=mesh, in_specs=in_specs, out_specs=out_specs, check_vma=False)

time: 782 us -> 544 us (0.70)
  Pallas kernels: 0 us -> 141 us
  blocking collectives: 87.8 us -> 0 us
  matrix products: 90.4 us -> 15.6 us
  waiting for transfers between devices: 273 us -> 206 us
  other arithmetic: 93.6 us -> 33.7 us
  local copies, waits for them, and re-layouts: 105 us -> 52.8 us
  starting transfers between devices: 101 us -> 83.6 us
  between operations: 16.1 us -> 2.36 us
    all_to_all x20 -> x0, waiting for transfers between devices: 207 us -> none  [the longest x1 85 us: shards(): lax.all_to_all(returned[0], 'section', split_axis=0, concat_axis=0, tiled...]
    ppermute x5 -> x61, waiting for transfers between devices: 46.2 us -> 206 us  [the longest x8 53.7 us: plane_shards(): mine = jnp.concatenate([mine, lax.ppermute(mine, AXES, route)], axis=0)]
    pallas_call x0 -> x8, Pallas kernels: none -> 141 us  [the longest x4 85.2 us: run_backward(): pl.pallas_call(kernel, in_specs=[SMEM] + [INSIDE] * 3 + [OUTSIDE] * (len(...]
    all_to_all x20 -> x0, starting transfers between devices: 89.3 us -> none  [the longest x4 17.4 us: shards(): lax.all_to_all(back_moved[0], 'tensor', split_axis=1, concat_axis=2, tile...]
    psum x10 -> x0, blocking collectives: 87.8 us -> none  [the longest x5 44.1 us: norm_pair(): lax.psum((jnp.sum(residuals[0] * residuals[0], axis=(1, 2)), jnp.sum(resi...]
    dot_general x48 -> x13, matrix products: 90.4 us -> 15.6 us  [the longest x12 15.4 us: inner_dot(): lax.dot_general(left, right, (((left_dim,), (right_dim,)), ((), ())), pre...]
    ppermute x5 -> x61, starting transfers between devices: 11.1 us -> 83.6 us  [the longest x8 22.1 us: to_home(): lax.ppermute(sent[k], AXES, homes[k])]
    convert_element_type x18 -> x12, other arithmetic: 50.3 us -> 16.5 us  [added(): (one.astype(jnp.float32) + two.astype(jnp.float32)).astype(jnp.bfloat16)]
  transfers between devices with their start and end apart: 26 -> 61, of which waited for: 19 -> 21; matrix products, arithmetic and copies ran while one was open for 27% -> 15% of each run, Pallas kernels for 0% -> 14%
where the time goes in v1:
time: 544 us; the launch traced here: 535 us
  waiting for transfers between devices  206 us (38%)
  Pallas kernels  141 us (26%)
  starting transfers between devices  83.6 us (15%)
  local copies, waits for them, and re-layouts  52.8 us (10%)
  other arithmetic  33.7 us (6%)
  matrix products  15.6 us (3%)
    pallas_call x4, Pallas kernels, run_backward(): pl.pallas_call(kernel, in_specs=[SMEM] + [INSIDE] * 3 + [OUTSIDE] * (len(...  85.2 us
    pallas_call x4, Pallas kernels, run_forward(): pl.pallas_call(kernel, in_specs=[SMEM, INSIDE, INSIDE] + [OUTSIDE] * (len...  55.3 us
    ppermute x8, waiting for transfers between devices, plane_shards(): mine = jnp.concatenate([mine, lax.ppermute(mine, AXES, route)], axis=0)  53.7 us
    ppermute x8, waiting for transfers between devices, to_home(): lax.ppermute(sent[k], AXES, homes[k])  45.9 us
    ppermute x6, waiting for transfers between devices, dispatch(): lax.ppermute(sent[k], AXES, planes[k])  38.9 us
    ppermute x8, waiting for transfers between devices, plane_shards(): mine = added(mine[:half], lax.ppermute(mine[half:], AXES, route))  36.7 us
    unnamed x159, local copies, waits for them, and re-layouts  24.5 us
    ppermute x8, starting transfers between devices, to_home(): lax.ppermute(sent[k], AXES, homes[k])  22.1 us
  transfers between devices with their start and end apart: 61, of which 21 were waited for; matrix products, arithmetic and copies ran while one was open for 15% of the time, Pallas kernels for 14%

profile of v1, /device:TPU:5, one launch (start us, length us, event | category | flops | bytes accessed | tf_op | source)
XLA Modules:
  0.0 534.5 jit_solution(1903864615330353526)
XLA Ops:
  43.8 7.4 %collective-permute-done.22 = bf16[1024,128]{1,0:T(8,128)(2,1)S(1)} collective-permute-done((bf16[1024,128]{1,0:T(8,128)(2,1)S(1)}, bf16[1024,128]{1,0:T(8,128)(2,1)S(1)}, u32[]{:S(2)}, u32[]{:S(2)}) %collective-permute-start.22) | collective-permute-done | bytes 262176 | tf_op jit(solution)/shard_map/ppermute | solution.py:756
  70.8 14.9 %collective-permute-done.4 = bf16[592,128]{1,0:T(8,128)(2,1)S(1)} collective-permute-done((bf16[592,128]{1,0:T(8,128)(2,1)S(1)}, bf16[592,128]{1,0:T(8,128)(2,1)S(1)}, u32[]{:S(2)}, u32[]{:S(2)}) %collective-permute-start.4) | collective-permute-done | bytes 151584 | tf_op jit(solution)/shard_map/ppermute | solution.py:764
  99.1 3.3 collective-permute-done.9
  105.2 22.8 %collective-permute-done.10 = bf16[8,512,128]{2,1,0:T(8,128)(2,1)S(1)} collective-permute-done((bf16[8,512,128]{2,1,0:T(8,128)(2,1)S(1)}, bf16[8,512,128]{2,1,0:T(8,128)(2,1)S(1)}, u32[]{:S(2)}, u32[]{:S(2)}) %collective-permute-start.10) | collective-permute-done | bytes 1048608 | tf_op jit(solution)/shard_map/ppermute | solution.py:772
  132.8 10.3 %collective-permute-done.19 = bf16[8,512,128]{2,1,0:T(8,128)(2,1)S(1)} collective-permute-done((bf16[8,512,128]{2,1,0:T(8,128)(2,1)S(1)}, bf16[8,512,128]{2,1,0:T(8,128)(2,1)S(1)}, u32[]{:S(2)}, u32[]{:S(2)}) %collective-permute-start.19) | collective-permute-done | bytes 1048608 | tf_op jit(solution)/shard_map/ppermute | solution.py:772
  146.0 8.3 %collective-permute-done.31 = bf16[8,512,128]{2,1,0:T(8,128)(2,1)S(1)} collective-permute-done((bf16[8,512,128]{2,1,0:T(8,128)(2,1)S(1)}, bf16[8,512,128]{2,1,0:T(8,128)(2,1)S(1)}, u32[]{:S(2)}, u32[]{:S(2)}) %collective-permute-start.31) | collective-permute-done | bytes 1048608 | tf_op jit(solution)/shard_map/ppermute | solution.py:772
  156.7 8.9 %collective-permute-done.28 = bf16[8,512,128]{2,1,0:T(8,128)(2,1)S(1)} collective-permute-done((bf16[8,512,128]{2,1,0:T(8,128)(2,1)S(1)}, bf16[8,512,128]{2,1,0:T(8,128)(2,1)S(1)}, u32[]{:S(2)}, u32[]{:S(2)}) %collective-permute-start.28) | collective-permute-done | bytes 1048608 | tf_op jit(solution)/shard_map/ppermute | solution.py:772
  171.8 38.8 %collective-permute-done.7.refs_2_.refs_8_ = bf16[2048,128]{1,0:T(8,128)(2,1)S(1)} collective-permute-done((bf16[2048,128]{1,0:T(8,128)(2,1)S(1)}, bf16[2048,128]{1,0:T(8,128)(2,1)S(1)}, u32[]{:S(2)}, u32[]{:S(2)}) %collective-permute-start.7) | collective-permute-done | bytes 524320 | tf_op jit(solution)/shard_map/ppermute | solution.py:799
  210.6 9.8 %collective-permute-start.29 = (bf16[16,512,128]{2,1,0:T(8,128)(2,1)}, bf16[16,512,128]{2,1,0:T(8,128)(2,1)}, u32[]{:S(2)}, u32[]{:S(2)}) collective-permute-start(bf16[16,512,128]{2,1,0:T(8,128)(2,1)} %constant_dynamic-update-slice_fusion.45), channel_id=1, source_target_pairs={{0,1},{1,0},{2,3},{3,2},{4,5},{5,4},{6,7},{7,6},{8,9},{9,8},{10,11... | collective-permute-start | bytes 6291464 | tf_op jit(solution)/shard_map/ppermute | solution.py:773
  221.1 14.4 %forward_layer.4 = (f32[8192,128]{1,0:T(8,128)}, bf16[8192,128]{1,0:T(8,128)(2,1)}, bf16[8192,128]{1,0:T(8,128)(2,1)}, bf16[8192,128]{1,0:T(8,128)(2,1)}, f32[8,128]{1,0:T(8,128)}, /*index=5*/f32[8,128]{1,0:T(8,128)}) custom-call(s32[65]{0:T(128)} %pad_add_fusion.table_ref, bf16[128,64]{1,0:T(8,128)(2,1)} %copy.57.gain_ref, ...), custom_call_target="tpu_custom_call" | custom-call | flops 15000000512 | bytes 20971520 | tf_op jit(solution)/shard_map/forward_layer/pallas_call | solution.py:622
  236.9 13.6 %forward_layer.5 = (f32[8192,128]{1,0:T(8,128)}, bf16[8192,128]{1,0:T(8,128)(2,1)}, bf16[8192,128]{1,0:T(8,128)(2,1)}, bf16[8192,128]{1,0:T(8,128)(2,1)}, f32[8,128]{1,0:T(8,128)}, /*index=5*/f32[8,128]{1,0:T(8,128)}) custom-call(s32[65]{0:T(128)} %pad_add_fusion.table_ref, bf16[128,64]{1,0:T(8,128)(2,1)} %copy.55.gain_ref, ...), custom_call_target="tpu_custom_call" | custom-call | flops 15000000512 | bytes 20971520 | tf_op jit(solution)/shard_map/forward_layer/pallas_call | solution.py:622
  250.5 13.6 %forward_layer.6 = (f32[8192,128]{1,0:T(8,128)}, bf16[8192,128]{1,0:T(8,128)(2,1)}, bf16[8192,128]{1,0:T(8,128)(2,1)}, bf16[8192,128]{1,0:T(8,128)(2,1)}, f32[8,128]{1,0:T(8,128)}, /*index=5*/f32[8,128]{1,0:T(8,128)}) custom-call(s32[65]{0:T(128)} %pad_add_fusion.table_ref, bf16[128,64]{1,0:T(8,128)(2,1)} %copy.53.gain_ref, ...), custom_call_target="tpu_custom_call" | custom-call | flops 15000000512 | bytes 20971520 | tf_op jit(solution)/shard_map/forward_layer/pallas_call | solution.py:622
  264.2 13.6 %forward_layer.7 = (f32[8192,128]{1,0:T(8,128)}, bf16[8192,128]{1,0:T(8,128)(2,1)}, bf16[8192,128]{1,0:T(8,128)(2,1)}, bf16[8192,128]{1,0:T(8,128)(2,1)}, f32[8,128]{1,0:T(8,128)}, /*index=5*/f32[8,128]{1,0:T(8,128)}) custom-call(s32[65]{0:T(128)} %pad_add_fusion.table_ref, bf16[128,64]{1,0:T(8,128)(2,1)} %copy.51.gain_ref, ...), custom_call_target="tpu_custom_call" | custom-call | flops 15000000512 | bytes 20971520 | tf_op jit(solution)/shard_map/forward_layer/pallas_call | solution.py:622
  277.9 28.6 %backward_layer.4 = (f32[8192,128]{1,0:T(8,128)}, bf16[16,2,2,128,128]{4,3,2,1,0:T(8,128)(2,1)}, bf16[16,2,2,128,128]{4,3,2,1,0:T(8,128)(2,1)}) custom-call(s32[65]{0:T(128)} %pad_add_fusion.table_ref, bf16[128,64]{1,0:T(8,128)(2,1)} %copy.51.gain_ref, bf16[128,64]{1,0:T(8,128)(2,1)} %copy.58.end_gain_ref, f32[8,128]{1,0:T(8,128)} %get-tuple-element.59.scale_ref, ...), custom_call_target="tpu_custom_call" | custom-call | flops 17999998976 | bytes 31457280 | tf_op jit(solution)/shard_map/backward_layer/pallas_call | solution.py:664
  306.4 19.4 %backward_layer.5 = (f32[8192,128]{1,0:T(8,128)}, bf16[16,2,2,128,128]{4,3,2,1,0:T(8,128)(2,1)}, bf16[16,2,2,128,128]{4,3,2,1,0:T(8,128)(2,1)}) custom-call(s32[65]{0:T(128)} %pad_add_fusion.table_ref, bf16[128,64]{1,0:T(8,128)(2,1)} %copy.53.gain_ref, bf16[128,64]{1,0:T(8,128)(2,1)} %copy.58.end_gain_ref, f32[8,128]{1,0:T(8,128)} %get-tuple-element.53.scale_ref, ...), custom_call_target="tpu_custom_call" | custom-call | flops 17999998976 | bytes 31457280 | tf_op jit(solution)/shard_map/backward_layer/pallas_call | solution.py:664
  325.8 19.3 %backward_layer.6 = (f32[8192,128]{1,0:T(8,128)}, bf16[16,2,2,128,128]{4,3,2,1,0:T(8,128)(2,1)}, bf16[16,2,2,128,128]{4,3,2,1,0:T(8,128)(2,1)}) custom-call(s32[65]{0:T(128)} %pad_add_fusion.table_ref, bf16[128,64]{1,0:T(8,128)(2,1)} %copy.55.gain_ref, bf16[128,64]{1,0:T(8,128)(2,1)} %copy.58.end_gain_ref, f32[8,128]{1,0:T(8,128)} %get-tuple-element.47.scale_ref, ...), custom_call_target="tpu_custom_call" | custom-call | flops 17999998976 | bytes 31457280 | tf_op jit(solution)/shard_map/backward_layer/pallas_call | solution.py:664
  345.8 18.0 %backward_layer.7 = (bf16[2048,128]{1,0:T(8,128)(2,1)}, bf16[2048,128]{1,0:T(8,128)(2,1)}, bf16[2048,128]{1,0:T(8,128)(2,1)}, bf16[2048,128]{1,0:T(8,128)(2,1)},...) custom-call(s32[65]{0:T(128)} %pad_add_fusion.table_ref, bf16[128,64]{1,0:T(8,128)(2,1)} %copy.57.gain_ref, ...), custom_call_target="tpu_custom_call" | custom-call | flops 17999998976 | bytes 31457280 | tf_op jit(solution)/shard_map/backward_layer/pallas_call | solution.py:664
  381.6 3.0 add_convert_fusion.3
  388.7 9.3 %collective-permute-done.50 = bf16[8,2,2,128,128]{4,3,2,1,0:T(8,128)(2,1)} collective-permute-done((bf16[8,2,2,128,128]{4,3,2,1,0:T(8,128)(2,1)}, bf16[8,2,2,128,128]{4,3,2,1,0:T(8,128)(2,1)}, u32[]{:S(2)}, u32[]{:S(2)}) %collective-permute-start.50) | collective-permute-done | bytes 1048608 | tf_op jit(solution)/shard_map/ppermute | solution.py:836
  402.1 15.2 %collective-permute-done.53 = bf16[8,2,2,128,128]{4,3,2,1,0:T(8,128)(2,1)} collective-permute-done((bf16[8,2,2,128,128]{4,3,2,1,0:T(8,128)(2,1)}, bf16[8,2,2,128,128]{4,3,2,1,0:T(8,128)(2,1)}, u32[]{:S(2)}, u32[]{:S(2)}) %collective-permute-start.53) | collective-permute-done | bytes 1048608 | tf_op jit(solution)/shard_map/ppermute | solution.py:836
  420.8 12.2 %collective-permute-done.54 = bf16[4,2,2,128,128]{4,3,2,1,0:T(8,128)(2,1)S(1)} collective-permute-done((bf16[4,2,2,128,128]{4,3,2,1,0:T(8,128)(2,1)S(1)}, bf16[4,2,2,128,128]{4,3,2,1,0:T(8,128)(2,1)S(1)}, u32[]{:S(2)}, u32[]{:S(2)}) %collective-permute-start.54) | collective-permute-done | bytes 524320 | tf_op jit(solution)/shard_map/ppermute | solution.py:836
  433.5 5.7 %collective-permute-start.55 = (bf16[1536,128]{1,0:T(8,128)(2,1)S(1)}, bf16[1536,128]{1,0:T(8,128)(2,1)S(1)}, u32[]{:S(2)}, u32[]{:S(2)}) collective-permute-start(bf16[1536,128]{1,0:T(8,128)(2,1)S(1)} %get-tuple-element.103), channel_id=1, source_target_pairs={{0,0},{1,1},{2,8},{3,9},{4,16},{5,17},{6,24},{7,25},{8,2},{9,3},{1... | collective-permute-start | bytes 1179656 | tf_op jit(solution)/shard_map/ppermute | solution.py:843
  440.1 4.5 collective-permute-start.56
  445.6 11.1 %collective-permute-done.55 = bf16[1536,128]{1,0:T(8,128)(2,1)S(1)} collective-permute-done((bf16[1536,128]{1,0:T(8,128)(2,1)S(1)}, bf16[1536,128]{1,0:T(8,128)(2,1)S(1)}, u32[]{:S(2)}, u32[]{:S(2)}) %collective-permute-start.55) | collective-permute-done | bytes 393248 | tf_op jit(solution)/shard_map/ppermute | solution.py:843
  459.6 11.3 %collective-permute-done.58 = bf16[1536,128]{1,0:T(8,128)(2,1)S(1)} collective-permute-done((bf16[1536,128]{1,0:T(8,128)(2,1)S(1)}, bf16[1536,128]{1,0:T(8,128)(2,1)S(1)}, u32[]{:S(2)}, u32[]{:S(2)}) %collective-permute-start.58) | collective-permute-done | bytes 393248 | tf_op jit(solution)/shard_map/ppermute | solution.py:843
  470.9 13.2 %collective-permute-done.57 = bf16[1536,128]{1,0:T(8,128)(2,1)S(1)} collective-permute-done((bf16[1536,128]{1,0:T(8,128)(2,1)S(1)}, bf16[1536,128]{1,0:T(8,128)(2,1)S(1)}, u32[]{:S(2)}, u32[]{:S(2)}) %collective-permute-start.57) | collective-permute-done | bytes 393248 | tf_op jit(solution)/shard_map/ppermute | solution.py:843
  487.8 3.2 collective-permute-start.60
  491.0 4.3 collective-permute-done.37
  498.0 3.9 collective-permute-start.45
  502.0 5.1 collective-permute-start.44
  509.3 6.2 %collective-permute-done.43 = bf16[512,128]{1,0:T(8,128)(2,1)S(1)} collective-permute-done((bf16[512,128]{1,0:T(8,128)(2,1)S(1)}, bf16[512,128]{1,0:T(8,128)(2,1)S(1)}, u32[]{:S(2)}, u32[]{:S(2)}) %collective-permute-start.43) | collective-permute-done | bytes 131104 | tf_op jit(solution)/shard_map/ppermute | solution.py:843
  530.1 4.0 fusion.76
  (364 shorter events, 155.0 us)
Async XLA Ops:
  4.1 164.0 %collective-permute-start.6 = (bf16[2048,128]{1,0:T(8,128)(2,1)}, bf16[2048,128]{1,0:T(8,128)(2,1)}, u32[]{:S(2)}, u32[]{:S(2)}) collective-permute-start(bf16[2048,128]{1,0:T(8,128)(2,1)} %fusion.5), channel_id=1, source_target_pairs={{0,2},{1,3},{2,0},{3,1},{4,6},{5,7},{6,4},{7,5},{8,10},{9,11},{10,... | collective-permute-start | bytes 1572872 | tf_op jit(solution)/shard_map/ppermute | solution.py:799
  38.5 26.3 %collective-permute-start.17 = (bf16[512,128]{1,0:T(8,128)(2,1)S(1)}, bf16[512,128]{1,0:T(8,128)(2,1)S(1)}, u32[]{:S(2)}, u32[]{:S(2)}) collective-permute-start(bf16[512,128]{1,0:T(8,128)(2,1)S(1)} %get-tuple-element.125), channel_id=1, source_target_pairs={{0,6},{1,7},{2,4},{3,5},{4,2},{5,3},{6,0},{7,1},{8,14},{9,15},{10,... | collective-permute-start | bytes 393224 | tf_op jit(solution)/shard_map/ppermute | solution.py:764
  61.7 24.0 %collective-permute-start.4 = (bf16[592,128]{1,0:T(8,128)(2,1)S(1)}, bf16[592,128]{1,0:T(8,128)(2,1)S(1)}, u32[]{:S(2)}, u32[]{:S(2)}) collective-permute-start(bf16[592,128]{1,0:T(8,128)(2,1)S(1)} %get-tuple-element.114), channel_id=1, source_target_pairs={{0,4},{1,5},{2,6},{3,7},{4,0},{5,1},{6,2},{7,3},{8,12},{9,13},{10,... | collective-permute-start | bytes 454664 | tf_op jit(solution)/shard_map/ppermute | solution.py:764
  64.8 32.5 %collective-permute-start.26 = (bf16[1024,128]{1,0:T(8,128)(2,1)S(1)}, bf16[1024,128]{1,0:T(8,128)(2,1)S(1)}, u32[]{:S(2)}, u32[]{:S(2)}) collective-permute-start(bf16[1024,128]{1,0:T(8,128)(2,1)S(1)} %get-tuple-element.109), channel_id=1, source_target_pairs={{0,6},{1,7},{2,4},{3,5},{4,2},{5,3},{6,0},{7,1},{8,14},{9,15},{10,... | collective-permute-start | bytes 786440 | tf_op jit(solution)/shard_map/ppermute | solution.py:764
  69.2 27.9 %collective-permute-start.25 = (bf16[1024,128]{1,0:T(8,128)(2,1)}, bf16[1024,128]{1,0:T(8,128)(2,1)S(1)}, u32[]{:S(2)}, u32[]{:S(2)}) collective-permute-start(bf16[1024,128]{1,0:T(8,128)(2,1)} %get-tuple-element.110), channel_id=1, source_target_pairs={{0,4},{1,5},{2,6},{3,7},{4,0},{5,1},{6,2},{7,3},{8,12},{9,13},{10,... | collective-permute-start | bytes 786440 | tf_op jit(solution)/shard_map/ppermute | solution.py:764
  85.6 42.5 %collective-permute-start.18 = (bf16[4,512,128]{2,1,0:T(8,128)(2,1)S(1)}, bf16[4,512,128]{2,1,0:T(8,128)(2,1)S(1)}, u32[]{:S(2)}, u32[]{:S(2)}) collective-permute-start(bf16[4,512,128]{2,1,0:T(8,128)(2,1)S(1)} %pad_maximum_fusion.7), channel_id=1, source_target_pairs={{0,8},{1,17},{2,10},{3,19},{4,12},{5,21},{6,14},{7,23},{8,0},{9,25... | collective-permute-start | bytes 1572872 | tf_op jit(solution)/shard_map/ppermute | solution.py:772
  97.4 33.5 %collective-permute-start.27 = (bf16[4,512,128]{2,1,0:T(8,128)(2,1)S(1)}, bf16[4,512,128]{2,1,0:T(8,128)(2,1)S(1)}, u32[]{:S(2)}, u32[]{:S(2)}) collective-permute-start(bf16[4,512,128]{2,1,0:T(8,128)(2,1)S(1)} %pad_maximum_fusion.8), channel_id=1, source_target_pairs={{0,8},{1,17},{2,10},{3,19},{4,12},{5,21},{6,14},{7,23},{8,0},{9,25... | collective-permute-start | bytes 1572872 | tf_op jit(solution)/shard_map/ppermute | solution.py:772
  97.6 32.1 %collective-permute-start.30 = (bf16[4,512,128]{2,1,0:T(8,128)(2,1)S(1)}, bf16[4,512,128]{2,1,0:T(8,128)(2,1)S(1)}, u32[]{:S(2)}, u32[]{:S(2)}) collective-permute-start(bf16[4,512,128]{2,1,0:T(8,128)(2,1)S(1)} %pad_maximum_fusion.9), channel_id=1, source_target_pairs={{0,8},{1,17},{2,10},{3,19},{4,12},{5,21},{6,14},{7,23},{8,0},{9,25... | collective-permute-start | bytes 1572872 | tf_op jit(solution)/shard_map/ppermute | solution.py:772
  102.7 25.3 %collective-permute-start.10 = (bf16[8,512,128]{2,1,0:T(8,128)(2,1)S(1)}, bf16[8,512,128]{2,1,0:T(8,128)(2,1)S(1)}, u32[]{:S(2)}, u32[]{:S(2)}) collective-permute-start(bf16[8,512,128]{2,1,0:T(8,128)(2,1)S(1)} %get-tuple-element.139), channel_id=1, source_target_pairs={{0,16},{1,9},{2,18},{3,11},{4,20},{5,13},{6,22},{7,15},{8,24},{9,1... | collective-permute-start | bytes 3145736 | tf_op jit(solution)/shard_map/ppermute | solution.py:772
  128.1 82.5 %collective-permute-start.11 = (bf16[16,512,128]{2,1,0:T(8,128)(2,1)S(1)}, bf16[16,512,128]{2,1,0:T(8,128)(2,1)S(1)}, u32[]{:S(2)}, u32[]{:S(2)}) collective-permute-start(bf16[16,512,128]{2,1,0:T(8,128)(2,1)S(1)} %constant_dynamic-update-slice_fusion.11), channel_id=1, source_target_pairs={{0,1},{1,0},{2,3},{3,2},{4,5},{5,4},{6,7},{7,6},{8,9},{9,8},{10,11... | collective-permute-start | bytes 6291464 | tf_op jit(solution)/shard_map/ppermute | solution.py:773
  129.9 24.4 %collective-permute-start.31 = (bf16[8,512,128]{2,1,0:T(8,128)(2,1)S(1)}, bf16[8,512,128]{2,1,0:T(8,128)(2,1)S(1)}, u32[]{:S(2)}, u32[]{:S(2)}) collective-permute-start(bf16[8,512,128]{2,1,0:T(8,128)(2,1)S(1)} %get-tuple-element.120), channel_id=1, source_target_pairs={{0,16},{1,9},{2,18},{3,11},{4,20},{5,13},{6,22},{7,15},{8,24},{9,1... | collective-permute-start | bytes 3145736 | tf_op jit(solution)/shard_map/ppermute | solution.py:772
  131.9 33.7 %collective-permute-start.28 = (bf16[8,512,128]{2,1,0:T(8,128)(2,1)S(1)}, bf16[8,512,128]{2,1,0:T(8,128)(2,1)S(1)}, u32[]{:S(2)}, u32[]{:S(2)}) collective-permute-start(bf16[8,512,128]{2,1,0:T(8,128)(2,1)S(1)} %get-tuple-element.122), channel_id=1, source_target_pairs={{0,16},{1,9},{2,18},{3,11},{4,20},{5,13},{6,22},{7,15},{8,24},{9,1... | collective-permute-start | bytes 3145736 | tf_op jit(solution)/shard_map/ppermute | solution.py:772
  144.2 91.3 %collective-permute-start.20 = (bf16[16,512,128]{2,1,0:T(8,128)(2,1)}, bf16[16,512,128]{2,1,0:T(8,128)(2,1)}, u32[]{:S(2)}, u32[]{:S(2)}) collective-permute-start(bf16[16,512,128]{2,1,0:T(8,128)(2,1)} %constant_dynamic-update-slice_fusion.28), channel_id=1, source_target_pairs={{0,1},{1,0},{2,3},{3,2},{4,5},{5,4},{6,7},{7,6},{8,9},{9,8},{10,11... | collective-permute-start | bytes 6291464 | tf_op jit(solution)/shard_map/ppermute | solution.py:773
  165.6 45.0 %collective-permute-start.7 = (bf16[2048,128]{1,0:T(8,128)(2,1)S(1)}, bf16[2048,128]{1,0:T(8,128)(2,1)S(1)}, u32[]{:S(2)}, u32[]{:S(2)}) collective-permute-start(bf16[2048,128]{1,0:T(8,128)(2,1)S(1)} %copy-done.16), channel_id=1, source_target_pairs={{0,4},{1,5},{2,6},{3,7},{4,0},{5,1},{6,2},{7,3},{8,12},{9,13},{10,... | collective-permute-start | bytes 1572872 | tf_op jit(solution)/shard_map/ppermute | solution.py:799
  168.1 109.8 %collective-permute-start.33 = (bf16[2048,128]{1,0:T(8,128)(2,1)S(1)}, bf16[2048,128]{1,0:T(8,128)(2,1)}, u32[]{:S(2)}, u32[]{:S(2)}) collective-permute-start(bf16[2048,128]{1,0:T(8,128)(2,1)S(1)} %copy-done.15), channel_id=1, source_target_pairs={{0,2},{1,3},{2,0},{3,1},{4,6},{5,7},{6,4},{7,5},{8,10},{9,11},{10,... | collective-permute-start | bytes 1572872 | tf_op jit(solution)/shard_map/ppermute | solution.py:799
  170.8 107.1 %collective-permute-start.35 = (bf16[2048,128]{1,0:T(8,128)(2,1)S(1)}, bf16[2048,128]{1,0:T(8,128)(2,1)}, u32[]{:S(2)}, u32[]{:S(2)}) collective-permute-start(bf16[2048,128]{1,0:T(8,128)(2,1)S(1)} %copy-done.14), channel_id=1, source_target_pairs={{0,6},{1,7},{2,4},{3,5},{4,2},{5,3},{6,0},{7,1},{8,14},{9,15},{10,... | collective-permute-start | bytes 1572872 | tf_op jit(solution)/shard_map/ppermute | solution.py:799
  210.6 67.3 %collective-permute-start.34 = (bf16[2048,128]{1,0:T(8,128)(2,1)S(1)}, bf16[2048,128]{1,0:T(8,128)(2,1)}, u32[]{:S(2)}, u32[]{:S(2)}) collective-permute-start(bf16[2048,128]{1,0:T(8,128)(2,1)S(1)} %copy-done.13), channel_id=1, source_target_pairs={{0,4},{1,5},{2,6},{3,7},{4,0},{5,1},{6,2},{7,3},{8,12},{9,13},{10,... | collective-permute-start | bytes 1572872 | tf_op jit(solution)/shard_map/ppermute | solution.py:799
  210.6 39.9 %collective-permute-start.29 = (bf16[16,512,128]{2,1,0:T(8,128)(2,1)}, bf16[16,512,128]{2,1,0:T(8,128)(2,1)}, u32[]{:S(2)}, u32[]{:S(2)}) collective-permute-start(bf16[16,512,128]{2,1,0:T(8,128)(2,1)} %constant_dynamic-update-slice_fusion.45), channel_id=1, source_target_pairs={{0,1},{1,0},{2,3},{3,2},{4,5},{5,4},{6,7},{7,6},{8,9},{9,8},{10,11... | collective-permute-start | bytes 6291464 | tf_op jit(solution)/shard_map/ppermute | solution.py:773
  235.5 28.7 %collective-permute-start.32 = (bf16[16,512,128]{2,1,0:T(8,128)(2,1)S(1)}, bf16[16,512,128]{2,1,0:T(8,128)(2,1)}, u32[]{:S(2)}, u32[]{:S(2)}) collective-permute-start(bf16[16,512,128]{2,1,0:T(8,128)(2,1)S(1)} %copy-done.50), channel_id=1, source_target_pairs={{0,1},{1,0},{2,3},{3,2},{4,5},{5,4},{6,7},{7,6},{8,9},{9,8},{10,11... | collective-permute-start | bytes 6291464 | tf_op jit(solution)/shard_map/ppermute | solution.py:773
  345.3 24.5 %collective-permute-start.49 = (bf16[16,2,2,128,128]{4,3,2,1,0:T(8,128)(2,1)}, bf16[16,2,2,128,128]{4,3,2,1,0:T(8,128)(2,1)}, u32[]{:S(2)}, u32[]{:S(2)}) collective-permute-start(bf16[16,2,2,128,128]{4,3,2,1,0:T(8,128)(2,1)} %get-tuple-element.76), channel_id=1, source_target_pairs={{0,1},{1,0},{2,3},{3,2},{4,5},{5,4},{6,7},{7,6},{8,9},{9,8},{10,11... | collective-permute-start | bytes 6291464 | tf_op jit(solution)/shard_map/ppermute | solution.py:833
  345.7 29.0 %collective-permute-start.52 = (bf16[16,2,2,128,128]{4,3,2,1,0:T(8,128)(2,1)}, bf16[16,2,2,128,128]{4,3,2,1,0:T(8,128)(2,1)}, u32[]{:S(2)}, u32[]{:S(2)}) collective-permute-start(bf16[16,2,2,128,128]{4,3,2,1,0:T(8,128)(2,1)} %get-tuple-element.78), channel_id=1, source_target_pairs={{0,1},{1,0},{2,3},{3,2},{4,5},{5,4},{6,7},{7,6},{8,9},{9,8},{10,11... | collective-permute-start | bytes 6291464 | tf_op jit(solution)/shard_map/ppermute | solution.py:833
  379.8 37.5 %collective-permute-start.53 = (bf16[8,2,2,128,128]{4,3,2,1,0:T(8,128)(2,1)}, bf16[8,2,2,128,128]{4,3,2,1,0:T(8,128)(2,1)}, u32[]{:S(2)}, u32[]{:S(2)}) collective-permute-start(bf16[8,2,2,128,128]{4,3,2,1,0:T(8,128)(2,1)} %slice.321), channel_id=1, source_target_pairs={{0,16},{1,9},{2,18},{3,11},{4,20},{5,13},{6,22},{7,15},{8,24},{9,1... | collective-permute-start | bytes 3145736 | tf_op jit(solution)/shard_map/ppermute | solution.py:836
  380.5 59.6 %collective-permute-start.38 = (bf16[2048,128]{1,0:T(8,128)(2,1)S(1)}, bf16[2048,128]{1,0:T(8,128)(2,1)S(1)}, u32[]{:S(2)}, u32[]{:S(2)}) collective-permute-start(bf16[2048,128]{1,0:T(8,128)(2,1)S(1)} %copy-done.59), channel_id=1, source_target_pairs={{0,6},{1,7},{2,4},{3,5},{4,2},{5,3},{6,0},{7,1},{8,14},{9,15},{10,... | collective-permute-start | bytes 1572872 | tf_op jit(solution)/shard_map/ppermute | solution.py:846
  384.7 60.3 %collective-permute-start.40 = (bf16[8,2,2,128,128]{4,3,2,1,0:T(8,128)(2,1)S(1)}, bf16[8,2,2,128,128]{4,3,2,1,0:T(8,128)(2,1)S(1)}, u32[]{:S(2)}, u32[]{:S(2)}) collective-permute-start(bf16[8,2,2,128,128]{4,3,2,1,0:T(8,128)(2,1)S(1)} %slice.309), channel_id=1, source_target_pairs={{0,16},{1,9},{2,18},{3,11},{4,20},{5,13},{6,22},{7,15},{8,24},{9,1... | collective-permute-start | bytes 3145736 | tf_op jit(solution)/shard_map/ppermute | solution.py:836
  387.2 33.3 %collective-permute-start.48 = (bf16[4,2,2,128,128]{4,3,2,1,0:T(8,128)(2,1)S(1)}, bf16[4,2,2,128,128]{4,3,2,1,0:T(8,128)(2,1)S(1)}, u32[]{:S(2)}, u32[]{:S(2)}) collective-permute-start(bf16[4,2,2,128,128]{4,3,2,1,0:T(8,128)(2,1)S(1)} %slice.315), channel_id=1, source_target_pairs={{0,8},{1,17},{2,10},{3,19},{4,12},{5,21},{6,14},{7,23},{8,0},{9,25... | collective-permute-start | bytes 1572872 | tf_op jit(solution)/shard_map/ppermute | solution.py:836
  439.2 31.7 %collective-permute-start.58 = (bf16[1536,128]{1,0:T(8,128)(2,1)S(1)}, bf16[1536,128]{1,0:T(8,128)(2,1)S(1)}, u32[]{:S(2)}, u32[]{:S(2)}) collective-permute-start(bf16[1536,128]{1,0:T(8,128)(2,1)S(1)} %get-tuple-element.104), channel_id=1, source_target_pairs={{0,6},{1,7},{2,14},{3,15},{4,22},{5,23},{6,30},{7,31},{8,4},{9,5},... | collective-permute-start | bytes 1179656 | tf_op jit(solution)/shard_map/ppermute | solution.py:843
  439.3 44.8 %collective-permute-start.57 = (bf16[1536,128]{1,0:T(8,128)(2,1)S(1)}, bf16[1536,128]{1,0:T(8,128)(2,1)S(1)}, u32[]{:S(2)}, u32[]{:S(2)}) collective-permute-start(bf16[1536,128]{1,0:T(8,128)(2,1)S(1)} %get-tuple-element.105), channel_id=1, source_target_pairs={{0,4},{1,5},{2,12},{3,13},{4,20},{5,21},{6,28},{7,29},{8,6},{9,7},... | collective-permute-start | bytes 1179656 | tf_op jit(solution)/shard_map/ppermute | solution.py:843
  440.1 46.4 %collective-permute-start.56 = (bf16[1536,128]{1,0:T(8,128)(2,1)S(1)}, bf16[1536,128]{1,0:T(8,128)(2,1)S(1)}, u32[]{:S(2)}, u32[]{:S(2)}) collective-permute-start(bf16[1536,128]{1,0:T(8,128)(2,1)S(1)} %get-tuple-element.106), channel_id=1, source_target_pairs={{0,2},{1,3},{2,10},{3,11},{4,18},{5,19},{6,26},{7,27},{8,0},{9,1},... | collective-permute-start | bytes 1179656 | tf_op jit(solution)/shard_map/ppermute | solution.py:843
  445.0 50.3 %collective-permute-start.37 = (bf16[2048,128]{1,0:T(8,128)(2,1)S(1)}, bf16[2048,128]{1,0:T(8,128)(2,1)S(1)}, u32[]{:S(2)}, u32[]{:S(2)}) collective-permute-start(bf16[2048,128]{1,0:T(8,128)(2,1)S(1)} %copy-done.56), channel_id=1, source_target_pairs={{0,4},{1,5},{2,6},{3,7},{4,0},{5,1},{6,2},{7,3},{8,12},{9,13},{10,... | collective-permute-start | bytes 1572872 | tf_op jit(solution)/shard_map/ppermute | solution.py:846
  456.6 50.4 %collective-permute-start.36 = (bf16[2048,128]{1,0:T(8,128)(2,1)S(1)}, bf16[2048,128]{1,0:T(8,128)(2,1)S(1)}, u32[]{:S(2)}, u32[]{:S(2)}) collective-permute-start(bf16[2048,128]{1,0:T(8,128)(2,1)S(1)} %copy-done.55), channel_id=1, source_target_pairs={{0,2},{1,3},{2,0},{3,1},{4,6},{5,7},{6,4},{7,5},{8,10},{9,11},{10,... | collective-permute-start | bytes 1572872 | tf_op jit(solution)/shard_map/ppermute | solution.py:846
  470.9 24.8 %collective-permute-start.41 = (bf16[4,2,2,128,128]{4,3,2,1,0:T(8,128)(2,1)S(1)}, bf16[4,2,2,128,128]{4,3,2,1,0:T(8,128)(2,1)S(1)}, u32[]{:S(2)}, u32[]{:S(2)}) collective-permute-start(bf16[4,2,2,128,128]{4,3,2,1,0:T(8,128)(2,1)S(1)} %slice.311), channel_id=1, source_target_pairs={{0,8},{1,17},{2,10},{3,19},{4,12},{5,21},{6,14},{7,23},{8,0},{9,25... | collective-permute-start | bytes 1572872 | tf_op jit(solution)/shard_map/ppermute | solution.py:836
  487.8 34.2 %collective-permute-start.60 = (bf16[4,1536,128]{2,1,0:T(8,128)(2,1)}, bf16[4,1536,128]{2,1,0:T(8,128)(2,1)}, u32[]{:S(2)}, u32[]{:S(2)}) collective-permute-start(bf16[4,1536,128]{2,1,0:T(8,128)(2,1)} %pad_maximum_fusion.2), channel_id=1, source_target_pairs={{0,1},{1,0},{2,3},{3,2},{4,5},{5,4},{6,7},{7,6},{8,9},{9,8},{10,11... | collective-permute-start | bytes 4718600 | tf_op jit(solution)/shard_map/ppermute | solution.py:844
  (89 other events, 1374.3 us)

commit v2 on v1

--- a/solution.py
+++ b/solution.py
@@ -316,16 +316,6 @@
         chunk_copy(source, target, sems, chunk).wait()
 
 
-def quarter_copies(pieces, whole, sems, me, outward=False):
-    rows = pieces[0].shape[0]
-    copies = []
-    for k, piece in enumerate(pieces):
-        part = whole.at[pl.ds(pl.multiple_of((me ^ k) * rows, rows), rows)]
-        ends = (part, piece) if outward else (piece, part)
-        copies.append(pltpu.make_async_copy(*ends, sems.at[k]))
-    return copies
-
-
 def factor_copies(own, peer, held, sems, side, outward=False):
     half = own.shape[0]
     copies = []
@@ -366,11 +356,9 @@
     left_in = factor_copies(own, peer, w, w_sems, 0)
     right_in = factor_copies(own, peer, w, w_sems, 1)
     if first:
-        pieces = quarter_copies(sources[:-2], raw, in_sems, table_ref[blocks])
-        for copy in pieces + left_in + right_in:
+        start_chunks(sources[0], raw, in_sems)
+        for copy in left_in + right_in:
             copy.start()
-        for copy in pieces:
-            copy.wait()
 
         def squares(block, total):
             rows = block_rows(block, size)
@@ -378,7 +366,12 @@
             h[rows, :] = part
             return total + fold_rows(part * part)
 
-        total = by_chunk(blocks, squares, jnp.zeros((8, slots), jnp.float32))
+        total = by_chunk(
+            blocks,
+            squares,
+            jnp.zeros((8, slots), jnp.float32),
+            lambda chunk: chunk_copy(sources[0], raw, in_sems, chunk).wait(),
+        )
     else:
         for copy in left_in:
             copy.start()
@@ -445,31 +438,23 @@
     sources, refs = refs[:inputs], refs[inputs:]
     slope_ref, z_ref, u_ref, own, peer = sources[:5]
     sources = sources[5:]
-    count = 4 if last else 1
-    outs, refs = refs[:count], refs[count:]
-    own_grad, peer_grad = refs[:2]
-    g, slope, z, u, h, w, gw, mid, turned, top, goal = refs[2:13]
-    in_sems, w_sems, out_sems, gw_sems = refs[13:]
+    out_ref, own_grad, peer_grad = refs[:3]
+    g, slope, z, u, h, w, gw, mid, turned, top, goal = refs[3:14]
+    in_sems, w_sems, out_sems, gw_sems = refs[14:]
     features, slots = g.shape
     size = w.shape[-1]
     chunk_blocks = w.shape[2]
     blocks = features // size
     fold = size // blocks
-    me = table_ref[blocks]
 
     left_in = factor_copies(own, peer, w, w_sems, 0)
     right_in = factor_copies(own, peer, w, w_sems, 1)
+    h_ref, g_ref = sources[:2]
     if turning:
-        h_ref, top_ref = sources[:2]
-        goals = quarter_copies(sources[2:], goal, in_sems.at[5], me)
-        start_chunks(top_ref, top, in_sems.at[0])
-        for copy in goals:
-            copy.start()
-    elif last:
-        starts = quarter_copies(sources[1:], h, in_sems.at[5], me)
-        start_chunks(sources[0], g, in_sems.at[0])
+        goal_ref = sources[2]
+        start_chunks(g_ref, top, in_sems.at[0])
+        start_chunks(goal_ref, goal, in_sems.at[5])
     else:
-        h_ref, g_ref = sources
         start_chunks(g_ref, g, in_sems.at[0])
     for copy in right_in:
         copy.start()
@@ -478,11 +463,7 @@
     for copy in left_in:
         copy.start()
     start_chunks(u_ref, u, in_sems.at[3])
-    if last:
-        for copy in starts:
-            copy.start()
-    else:
-        start_chunks(h_ref, h, in_sems.at[4])
+    start_chunks(h_ref, h, in_sems.at[4])
 
     if turning:
         zero = jnp.zeros((8, slots), jnp.float32)
@@ -497,11 +478,11 @@
                 totals[2] + fold_rows(scaled * goal[rows, :].astype(jnp.float32)),
             )
 
-        for copy in goals:
-            copy.wait()
-        totals = by_chunk(
-            blocks, sums, (zero, zero, zero), lambda chunk: chunk_copy(top_ref, top, in_sems.at[0], chunk).wait()
-        )
+        def arrive_top(chunk):
+            chunk_copy(g_ref, top, in_sems.at[0], chunk).wait()
+            chunk_copy(goal_ref, goal, in_sems.at[5], chunk).wait()
+
+        totals = by_chunk(blocks, sums, (zero, zero, zero), arrive_top)
         squares, gained, crossed = [jnp.sum(total, axis=0, keepdims=True) for total in totals]
         end_scale = lax.rsqrt(squares / features + EPSILON)
         end_back = end_scale * end_scale * end_scale * (end_scale * gained - crossed) / features
@@ -511,7 +492,7 @@
 
     def arrive_right(chunk):
         if not turning:
-            chunk_copy(sources[0] if last else g_ref, g, in_sems.at[0], chunk).wait()
+            chunk_copy(g_ref, g, in_sems.at[0], chunk).wait()
         chunk_copy(slope_ref, slope, in_sems.at[1], chunk).wait()
         chunk_copy(z_ref, z, in_sems.at[2], chunk).wait()
 
@@ -539,14 +520,10 @@
     for copy in left_in:
         copy.wait()
     scale = scale_ref[0:1, :]
-    if last:
-        for copy in starts:
-            copy.wait()
 
     def arrive_left(chunk):
         chunk_copy(u_ref, u, in_sems.at[3], chunk).wait()
-        if not last:
-            chunk_copy(h_ref, h, in_sems.at[4], chunk).wait()
+        chunk_copy(h_ref, h, in_sems.at[4], chunk).wait()
 
     def left(block, total):
         rows = block_rows(block, size)
@@ -578,16 +555,9 @@
             g[rows, :] = ended
         return carry
 
-    if last:
-        by_chunk(blocks, finish, 0)
-        ends = quarter_copies(outs, u, out_sems, me, outward=True)
-        for copy in ends:
-            copy.start()
-        for copy in ends:
-            copy.wait()
-    else:
-        by_chunk(blocks, finish, 0, None, lambda chunk: chunk_copy(g, outs[0], out_sems, chunk).start())
-        wait_chunks(g, outs[0], out_sems)
+    ended = u if last else g
+    by_chunk(blocks, finish, 0, None, lambda chunk: chunk_copy(ended, out_ref, out_sems, chunk).start())
+    wait_chunks(ended, out_ref, out_sems)
     for copy in right_out + left_out:
         copy.wait()
 
@@ -601,9 +571,10 @@
 OUTSIDE = pl.BlockSpec(memory_space=pl.ANY)
 
 
-def run_forward(table, gain, sums, held, weights, whole, after=()):
-    first = len(held) > 1
-    sources = (*held, *weights)
+def run_forward(table, gain, sums, residual, weights, after=()):
+    whole = residual.shape
+    first = residual.dtype == jnp.bfloat16
+    sources = (residual, *weights)
     half = weights[0].shape
     out_shape = (
         shape_of(whole, jnp.float32),
@@ -648,10 +619,7 @@
     whole = kept[0].shape
     sources = (*kept, *weights, *sources)
     half = weights[0].shape
-    width = 4
-    ends = [shape_of((whole[0] // width, whole[1]), jnp.bfloat16)] * width if last else [
-        shape_of(whole, jnp.float32)
-    ]
+    ended = shape_of(whole, jnp.bfloat16 if last else jnp.float32)
 
     def kernel(table_ref, gain_ref, end_gain_ref, scale_ref, *refs):
         extra = len(sources) + len(after)
@@ -664,8 +632,8 @@
     return pl.pallas_call(
         kernel,
         in_specs=[SMEM] + [INSIDE] * 3 + [OUTSIDE] * (len(sources) + len(after)),
-        out_specs=[OUTSIDE] * (len(ends) + 2),
-        out_shape=ends + [shape_of(half, jnp.bfloat16)] * 2,
+        out_specs=[OUTSIDE] * 3,
+        out_shape=[ended] + [shape_of(half, jnp.bfloat16)] * 2,
         scratch_shapes=[
             pltpu.VMEM(whole, jnp.float32),
             pltpu.VMEM(whole, jnp.bfloat16),
@@ -695,9 +663,60 @@
 BACKWARD_COST = 18_000_000_000
 
 
+def assemble_kernel(layer_count, factor, place_ref, *refs):
+    sources, (left_ref, right_ref) = refs[: 2 * layer_count], refs[2 * layer_count : 2 * layer_count + 2]
+    held, wide, in_sems, out_sems = refs[2 * layer_count + 2 :]
+    width, chunk = held.shape[1], held.shape[3]
+    core, tensor = place_ref[0], place_ref[1]
+    arrivals = [
+        pltpu.make_async_copy(source, held.at[at], in_sems.at[at]) for at, source in enumerate(sources)
+    ]
+    for copy in arrivals:
+        copy.start()
+    leaving = []
+    for at in range(2 * layer_count):
+        arrivals[at].wait()
+        layer, side = at // 2, at % 2
+        half = core if side == 0 else 1 - core
+        wide[at] = held[at].astype(jnp.float32) * factor
+        for k in range(width):
+            start = (half * width + (tensor ^ k)) * chunk
+            for which, target in enumerate((left_ref, right_ref)):
+                copy = pltpu.make_async_copy(
+                    wide.at[at, k, which],
+                    target.at[layer, pl.ds(start, chunk)],
+                    out_sems.at[(at * width + k) * 2 + which],
+                )
+                copy.start()
+                leaving.append(copy)
+    for copy in leaving:
+        copy.wait()
+
+
+def run_assemble(places, pieces, layer_count, factor):
+    piece = pieces[0].shape
+    blocks = 2 * piece[0] * piece[2]
+    out = shape_of((layer_count, blocks) + piece[3:], jnp.float32)
+    return pl.pallas_call(
+        lambda *refs: assemble_kernel(layer_count, factor, *refs),
+        in_specs=[SMEM] + [OUTSIDE] * len(pieces),
+        out_specs=[OUTSIDE] * 2,
+        out_shape=[out] * 2,
+        scratch_shapes=[
+            pltpu.VMEM((2 * layer_count,) + piece, jnp.bfloat16),
+            pltpu.VMEM((2 * layer_count,) + piece, jnp.float32),
+            pltpu.SemaphoreType.DMA((2 * layer_count,)),
+            pltpu.SemaphoreType.DMA((4 * layer_count * piece[0],)),
+        ],
+        compiler_params=pltpu.CompilerParams(vmem_limit_bytes=VMEM_LIMIT),
+        cost_estimate=pl.CostEstimate(
+            flops=0, bytes_accessed=12 * layer_count * math.prod(piece), transcendentals=0
+        ),
+        name="assemble",
+    )(places, *pieces)
+
+
 def plane_routes(width, replicas):
-    bits = width.bit_length() - 1
-    orders = [[(step + d) % bits for step in range(bits)] for d in range(replicas)]
     every = [(s, t, d) for s in range(width) for t in range(width) for d in range(replicas)]
 
     def route(move):
@@ -706,16 +725,15 @@
 
         return [(index(*place), index(*move(*place))) for place in every]
 
-    across = [route(lambda s, t, d, at=at: (s ^ (1 << orders[d][at]), t, d)) for at in range(bits)]
     cores = route(lambda s, t, d: (s, t, 1 - d))
     sections = [route(lambda s, t, d, k=k: (s ^ k, t, d)) for k in range(width)]
     planes = [route(lambda s, t, d, k=k: (s, t ^ k, d)) for k in range(width)]
     homes = [route(lambda s, t, d, k=k: (t, s ^ k, d)) for k in range(width)]
-    ranks = [[0] * width for d in range(replicas)]
-    for d in range(replicas):
-        for r in range(width):
-            ranks[d][sum(((r >> at) & 1) << orders[d][at] for at in range(bits))] = r
-    return across, cores, sections, planes, homes, ranks
+    return cores, sections, planes, homes
+
+
+def added(*parts):
+    return sum(part.astype(jnp.float32) for part in parts).astype(jnp.bfloat16)
 
 
 def plane_shards(patches, teacher, critic_pairs, left_factors, right_factors, norm_gains):
@@ -726,63 +744,23 @@
     features = feat_local * width
     blocks = features // size
     wide = 2 * tok_rows // 3
-    whole = (features, wide)
     chunk = local_blocks // (replicas * width)
-    across, cores, sections, planes, homes, ranks = plane_routes(width, replicas)
+    layer_rows = 2 * chunk * size
+    cores, sections, planes, homes = plane_routes(width, replicas)
     section = lax.axis_index("section")
     tensor = lax.axis_index("tensor")
     core = lax.axis_index("dp")
-
-    layer_rows = 2 * chunk * size
-
-    def piece_for(distance):
-        start = (core * width + (section ^ distance)) * chunk
-        parts = [
-            lax.dynamic_slice_in_dim(factors[0], start, chunk, axis=1)
-            for factors in (left_factors, right_factors)
-        ]
-        return jnp.stack(parts, axis=1).reshape(layer_count, layer_rows, size)
-
-    pieces = [piece_for(distance) for distance in range(width)]
-    gain_rows = norm_gains[0].reshape(-1, size)
-    groups = [(0,), (1,), tuple(range(2, layer_count))]
-    weights = []
-    arrived_gains = None
-    for group in groups:
-        sent = [piece[group[0] : group[-1] + 1].reshape(-1, size) for piece in pieces]
-        if group[0] == 0:
-            sent = [jnp.concatenate([value, gain_rows], axis=0) for value in sent]
-        sent = [sent[0]] + [
-            lax.ppermute(sent[distance], AXES, sections[distance]) for distance in range(1, width)
-        ]
-        spread = jnp.stack(sent)
-        sent = [
-            lax.dynamic_index_in_dim(spread, section ^ tensor ^ distance, 0, keepdims=False)
-            for distance in range(width)
-        ]
-        sent = [sent[0]] + [
-            lax.ppermute(sent[distance], AXES, planes[distance]) for distance in range(1, width)
-        ]
-        if group[0] == 0:
-            arrived_gains = jnp.stack([value[layer_rows:] for value in sent])
-        for at in range(len(group)):
-            rows = slice(at * layer_rows, (at + 1) * layer_rows)
-            mine = jnp.stack([value[rows] for value in sent])
-            for route in across:
-                mine = jnp.concatenate([mine, lax.ppermute(mine, AXES, route)], axis=0)
-            other = lax.ppermute(mine, AXES, cores)
-            weights.append([part.reshape(-1, 2, chunk, size, size) for part in (mine, other)])
-    gains = arrived_gains[jnp.arange(width) ^ tensor]
-    gains = gains.reshape(width, layer_count + 1, local_blocks, size).transpose(1, 3, 0, 2)
-    gains = gains.reshape(layer_count + 1, size, blocks)
-
-    block = jnp.arange(blocks, dtype=jnp.int32)
-    rest = block % local_blocks
-    replica = rest // (width * chunk)
-    rank = jnp.array(ranks, jnp.int32)[replica, section ^ ((rest // chunk) % width)]
-    part = (replica != core).astype(jnp.int32)
-    table = ((part * width + rank) * width + (tensor ^ (block // local_blocks))) * chunk + rest % chunk
-    table = jnp.concatenate([table, tensor[None]]).astype(jnp.int32)
+    away = range(1, width)
+    tie = lax.optimization_barrier
+
+    def send(values, routes):
+        return [values[0]] + [lax.ppermute(values[k], AXES, routes[k]) for k in away]
+
+    def crossed(values):
+        spread = jnp.stack(values)
+        return [
+            lax.dynamic_index_in_dim(spread, section ^ tensor ^ k, 0, keepdims=False) for k in range(width)
+        ]
 
     critic_ids = jnp.arange(width, dtype=jnp.int32) ^ tensor
     named = (critic_pairs[:, 0:1] == critic_ids) | (critic_pairs[:, 1:2] == critic_ids)
@@ -794,73 +772,142 @@
         (named[:, k : k + 1] & (rank[:, k : k + 1] == places)).astype(jnp.bfloat16) for k in range(width)
     ]
 
-    def dispatch(values):
-        sent = [inner_dot(values, chosen[k], 0, 0).astype(jnp.bfloat16) for k in range(width)]
-        return [sent[0]] + [lax.ppermute(sent[k], AXES, planes[k]) for k in range(1, width)]
-
-    start = dispatch(patches)
-    target = dispatch(teacher)
-
+    def picked(values):
+        return [inner_dot(values, chosen[k], 0, 0).astype(jnp.bfloat16) for k in range(width)]
+
+    def in_order(values):
+        spread = jnp.stack(values)
+        return spread[jnp.arange(width) ^ tensor].reshape((features,) + spread.shape[2:])
+
+    def piece_for(distance):
+        start = (core * width + (section ^ distance)) * chunk
+        parts = [
+            lax.dynamic_slice_in_dim(factors[0], start, chunk, axis=1)
+            for factors in (left_factors, right_factors)
+        ]
+        return jnp.stack(parts, axis=1).reshape(layer_count, layer_rows, size)
+
+    pieces = [piece_for(distance) for distance in range(width)]
+    gain_rows = norm_gains[0].reshape(-1, size)
+    front = [jnp.concatenate([piece[0], gain_rows], axis=0) for piece in pieces]
+    rest = [piece[1:] for piece in pieces]
+    patch_sent = picked(patches)
+    front = send(front, sections)
+    patch_came = send(patch_sent, planes)
+    front, rest = tie((front, rest))
+    rest = send(rest, sections)
+    front = send(crossed(front), planes)
+    gains = jnp.stack([value[layer_rows:] for value in front])[jnp.arange(width) ^ tensor]
+    gains = gains.reshape(width, layer_count + 1, local_blocks, size).transpose(1, 3, 0, 2)
+    gains = gains.reshape(layer_count + 1, size, blocks)
+    arrived = [jnp.stack([value[:layer_rows] for value in front])]
+    for layer in range(1, layer_count):
+        arrived.append([value[layer - 1] for value in rest])
+
+    def to_plane(values, after):
+        values, _ = tie((crossed(values), after))
+        return send(values, planes)
+
+    def over_plane(mine):
+        return send([mine] * width, sections)
+
+    def both_cores(parts):
+        mine = jnp.concatenate(parts, axis=0)
+        return mine, lax.ppermute(mine, AXES, cores)
+
+    def as_weights(parts):
+        return [part.reshape(-1, 2, chunk, size, size) for part in parts]
+
+    spread = [over_plane(arrived[0])]
+    arrived[1] = jnp.stack(to_plane(arrived[1], front))
+    spread.append(over_plane(arrived[1]))
+    arrived[2] = to_plane(arrived[2], arrived[1])
+    weights = [as_weights(both_cores(spread[0]))]
+
+    block = jnp.arange(blocks, dtype=jnp.int32)
+    inside = block % local_blocks
+    part = (inside // (width * chunk) != core).astype(jnp.int32)
+    rank_of = section ^ ((inside // chunk) % width)
+    table = ((part * width + rank_of) * width + (tensor ^ (block // local_blocks))) * chunk + inside % chunk
+    table = table.astype(jnp.int32)
+
+    residual = in_order(patch_came)
+    sums = jnp.zeros((8, wide), jnp.float32)
+    target_sent = picked(teacher)
+    (residual, spread[1], arrived[2], target_sent) = tie((residual, spread[1], arrived[2], target_sent))
+    arrived[2] = jnp.stack(arrived[2])
     stored = []
-    residual = start
-    sums = jnp.zeros((8, wide), jnp.float32)
     for layer in range(layer_count):
+        flying = []
+        if layer + 1 < layer_count:
+            flying.append(both_cores(spread[layer + 1]))
+        if layer + 2 < layer_count:
+            flying.append(over_plane(arrived[layer + 2]))
+        if layer + 3 < layer_count:
+            flying.append(to_plane(arrived[layer + 3], arrived[layer + 2]))
         following, u, z, slope, scale, sums = run_forward(
-            table, gains[layer], sums, residual, weights[layer], whole
+            table, gains[layer], sums, residual, weights[layer]
         )
         stored.append(((slope, z, u), scale, residual))
-        residual = (following,)
-
-    def added(one, two):
-        return (one.astype(jnp.float32) + two.astype(jnp.float32)).astype(jnp.bfloat16)
-
-    summed = []
-    gradient = None
+        residual, flying = tie((following, flying))
+        if layer + 1 < layer_count:
+            weights.append(as_weights(flying[0]))
+        if layer + 2 < layer_count:
+            spread.append(flying[1])
+        if layer + 3 < layer_count:
+            arrived[layer + 3] = jnp.stack(flying[2])
+        if layer == 0:
+            target_sent, sums = tie((target_sent, sums))
+            target = in_order(send(target_sent, planes))
+
+    def core_sum(mine, other):
+        return (mine, lax.ppermute(other, AXES, cores))
+
+    def plane_sum(value):
+        value = value.reshape(width, width, layer_rows, size)
+        return send([value[k] for k in range(width)], sections)
+
+    def homeward(value):
+        sent = crossed([value[k] for k in range(width)])
+        return [lax.ppermute(sent[k], AXES, homes[k]) for k in range(width)]
+
+    steps = (
+        lambda state: core_sum(*state),
+        lambda state: plane_sum(added(*state)),
+        lambda state: homeward(added(*state)),
+        lambda state: (jnp.stack(state), lax.ppermute(jnp.stack(state), AXES, cores)),
+    )
+    gradient = residual
+    underway = []
     for layer in range(layer_count - 1, -1, -1):
         turning = layer == layer_count - 1
         last = layer == 0
         kept, scale, inputs = stored[layer]
-        if turning:
-            sources = (*inputs, *residual, *target)
-        elif last:
-            sources = (gradient, *inputs)
-        else:
-            sources = (*inputs, gradient)
-        *gradient, mine, other = run_backward(
+        sources = (inputs, gradient, target) if turning else (inputs, gradient)
+        underway = [(at + 1, steps[at](state)) for at, state in underway]
+        gradient, mine, other = run_backward(
             table, gains[layer], gains[layer_count], scale, kept, weights[layer], sources, turning, last
         )
-        gradient = gradient if last else gradient[0]
-        mine = added(mine, lax.ppermute(other, AXES, cores))
-        for route in across[::-1]:
-            half = mine.shape[0] // 2
-            mine = added(mine[:half], lax.ppermute(mine[half:], AXES, route))
-        summed.insert(0, mine.reshape(width, layer_rows, size))
-
-    def to_home(value):
-        sent = [
-            lax.dynamic_index_in_dim(value, section ^ tensor ^ k, 0, keepdims=False) for k in range(width)
-        ]
-        came = jnp.stack([lax.ppermute(sent[k], AXES, homes[k]) for k in range(width)])
-        return came, lax.ppermute(came, AXES, cores)
-
-    returned = [gradient[0]] + [lax.ppermute(gradient[k], AXES, planes[k]) for k in range(1, width)]
+        gradient, mine, other, states = tie((gradient, mine, other, [state for _, state in underway]))
+        underway = [(at, state) for (at, _), state in zip(underway, states)]
+        underway.append((0, (mine, other)))
+
+    returned = gradient.reshape(width, feat_local, wide)
+    returned = [lax.dynamic_index_in_dim(returned, tensor ^ k, 0, keepdims=False) for k in range(width)]
+    returned = send(returned, planes)
+    homes_of = []
+    for at, state in underway:
+        for step in steps[at:]:
+            state = step(state)
+        homes_of.append(state)
     combined = sum(inner_dot(chosen[k], returned[k], 1, 1) for k in range(width))
     d_patches = (0.5 * combined).astype(jnp.bfloat16)
-
     grad_factor = 1.0 / math.sqrt(2 * tok_rows * width * replicas)
-    late = to_home(jnp.concatenate(summed[1:], axis=1))
-    early = to_home(summed[0])
-    pair = [jnp.concatenate([one, two], axis=1) for one, two in zip(early, late)]
-    order = jnp.arange(width) ^ tensor
-    pair = [
-        value[order].reshape(width, layer_count, 2, chunk, size, size).transpose(2, 1, 0, 3, 4, 5)
-        for value in pair
-    ]
-    pair = [value.reshape(2, layer_count, width * chunk, size, size) for value in pair]
-    low = jnp.where(core == 0, pair[0], pair[1])
-    high = jnp.where(core == 0, pair[1], pair[0])
-    grads = jnp.concatenate([low, high], axis=2).astype(jnp.float32) * grad_factor
-    return (d_patches, grads[0][None], grads[1][None])
+    parts = [part.reshape(width, 2, chunk, size, size) for pair in homes_of[::-1] for part in pair]
+    grad_left, grad_right = run_assemble(
+        jnp.stack([core, tensor]).astype(jnp.int32), parts, layer_count, grad_factor
+    )
+    return (d_patches, grad_left[None], grad_right[None])
 
 
 def solution(mesh):

time: 544 us -> 519 us (0.954); the launches traced: 535 us -> 518 us
  waiting for transfers between devices: 206 us -> 166 us
  starting transfers between devices: 83.6 us -> 103 us
    ppermute x61 -> x79, waiting for transfers between devices: 206 us -> 166 us  [the longest x51 121 us: send(): lax.ppermute(values[k], AXES, routes[k])]
    ppermute x61 -> x79, starting transfers between devices: 83.6 us -> 103 us  [the longest x51 43 us: send(): lax.ppermute(values[k], AXES, routes[k])]
    another operation x11 -> x20, other arithmetic: 5.73 us -> 14.8 us  [the longest x8 5.7 us: plane_shards(): jnp.stack(state)]
    gather x4 -> x5, local copies, waits for them, and re-layouts: 5.96 us -> 13.4 us  [the longest x4 12.2 us: in_order(): spread[jnp.arange(width) ^ tensor].reshape((features,) + spread.shape[2:])]
    pallas_call x0 -> x1, Pallas kernels: none -> 5.65 us  [run_assemble(): pl.pallas_call(lambda *refs: assemble_kernel(layer_count, factor, *refs),...]
    convert_element_type x12 -> x8, other arithmetic: 16.5 us -> 11.7 us  [added(): sum((part.astype(jnp.float32) for part in parts)).astype(jnp.bfloat16)]
    unnamed x159 -> x147, local copies, waits for them, and re-layouts: 24.5 us -> 24 us
  transfers between devices with their start and end apart: 61 -> 79, of which waited for: 21 -> 26; matrix products, arithmetic and copies ran while one was open for 15% -> 16% of each run, Pallas kernels for 14% -> 19%
where the time goes in v2:
time: 519 us; the launch traced here: 518 us
  waiting for transfers between devices  166 us (32%)
  Pallas kernels  146 us (28%)
  starting transfers between devices  103 us (20%)
  local copies, waits for them, and re-layouts  55.8 us (11%)
  other arithmetic  32.1 us (6%)
  matrix products  12.7 us (2%)
    ppermute x51, waiting for transfers between devices, send(): lax.ppermute(values[k], AXES, routes[k])  121 us
    pallas_call x4, Pallas kernels, run_backward(): pl.pallas_call(kernel, in_specs=[SMEM] + [INSIDE] * 3 + [OUTSIDE] * (len(...  85.4 us
    pallas_call x4, Pallas kernels, run_forward(): pl.pallas_call(kernel, in_specs=[SMEM, INSIDE, INSIDE] + [OUTSIDE] * (len...  54.8 us
    ppermute x16, waiting for transfers between devices, homeward(): return [lax.ppermute(sent[k], AXES, homes[k]) for k in range(width)]  45.5 us
    ppermute x51, starting transfers between devices, send(): lax.ppermute(values[k], AXES, routes[k])  43 us
    ppermute x16, starting transfers between devices, homeward(): return [lax.ppermute(sent[k], AXES, homes[k]) for k in range(width)]  34.4 us
    unnamed x147, local copies, waits for them, and re-layouts  24 us
    dot_general x12, matrix products, inner_dot(): lax.dot_general(left, right, (((left_dim,), (right_dim,)), ((), ())), pre...  12.5 us
  transfers between devices with their start and end apart: 79, of which 26 were waited for; matrix products, arithmetic and copies ran while one was open for 16% of the time, Pallas kernels for 19%

profile of v2, /device:TPU:5, one launch (start us, length us, event | category | flops | bytes accessed | tf_op | source)
XLA Modules:
  0.0 518.1 jit_solution(606364949318886985)
XLA Ops:
  31.4 4.1 collective-permute-done.3
  58.5 5.4 %collective-permute-done.13 = bf16[512,128]{1,0:T(8,128)(2,1)S(1)} collective-permute-done((bf16[512,128]{1,0:T(8,128)(2,1)}, bf16[512,128]{1,0:T(8,128)(2,1)S(1)}, u32[]{:S(2)}, u32[]{:S(2)}) %collective-permute-start.13) | collective-permute-done | bytes 131104 | tf_op jit(solution)/shard_map/ppermute | solution.py:757
  71.2 6.0 %collective-permute-start.24 = (bf16[16,512,128]{2,1,0:T(8,128)(2,1)}, bf16[16,512,128]{2,1,0:T(8,128)(2,1)}, u32[]{:S(2)}, u32[]{:S(2)}) collective-permute-start(bf16[16,512,128]{2,1,0:T(8,128)(2,1)} %constant_dynamic-update-slice_fusion.7), channel_id=1, source_target_pairs={{0,1},{1,0},{2,3},{3,2},{4,5},{5,4},{6,7},{7,6},{8,9},{9,8},{10,11... | collective-permute-start | bytes 6291464 | tf_op jit(solution)/shard_map/ppermute | solution.py:816
  79.1 28.9 %collective-permute-done.7 = bf16[2048,128]{0,1:T(8,128)(2,1)S(1)} collective-permute-done((bf16[2048,128]{0,1:T(8,128)(2,1)}, bf16[2048,128]{0,1:T(8,128)(2,1)S(1)}, u32[]{:S(2)}, u32[]{:S(2)}) %collective-permute-start.7) | collective-permute-done | bytes 524320 | tf_op jit(solution)/shard_map/ppermute | solution.py:757
  120.4 3.9 copy.30
  124.3 8.1 %collective-permute-done.16 = bf16[4,512,128]{2,1,0:T(8,128)(2,1)} collective-permute-done((bf16[4,512,128]{2,1,0:T(8,128)(2,1)}, bf16[4,512,128]{2,1,0:T(8,128)(2,1)}, u32[]{:S(2)}, u32[]{:S(2)}) %collective-permute-start.16) | collective-permute-done | bytes 524320 | tf_op jit(solution)/shard_map/ppermute | solution.py:757
  145.1 4.2 collective-permute-done.29
  154.6 13.8 %forward_layer.4 = (f32[8192,128]{1,0:T(8,128)}, bf16[8192,128]{1,0:T(8,128)(2,1)}, bf16[8192,128]{1,0:T(8,128)(2,1)}, bf16[8192,128]{1,0:T(8,128)(2,1)}, f32[8,128]{1,0:T(8,128)}, /*index=5*/f32[8,128]{1,0:T(8,128)}) custom-call(s32[64]{0:T(128)} %fusion.67.table_ref, bf16[128,64]{1,0:T(8,128)(2,1)} %copy.42.gain_ref, f32[8,128]{1,0:T(8,128)} %broadcast_in_dim.14.sums_ref, ...), custom_call_target="tpu_custom_call" | custom-call | flops 15000000512 | bytes 20971520 | tf_op jit(solution)/shard_map/forward_layer/pallas_call | solution.py:593
  168.4 4.8 collective-permute-done.27
  183.6 13.7 %forward_layer.5 = (f32[8192,128]{1,0:T(8,128)}, bf16[8192,128]{1,0:T(8,128)(2,1)}, bf16[8192,128]{1,0:T(8,128)(2,1)}, bf16[8192,128]{1,0:T(8,128)(2,1)}, f32[8,128]{1,0:T(8,128)}, /*index=5*/f32[8,128]{1,0:T(8,128)}) custom-call(s32[64]{0:T(128)} %fusion.67.table_ref, bf16[128,64]{1,0:T(8,128)(2,1)} %copy.40.gain_ref, ...), custom_call_target="tpu_custom_call" | custom-call | flops 15000000512 | bytes 20971520 | tf_op jit(solution)/shard_map/forward_layer/pallas_call | solution.py:593
  199.1 6.8 %collective-permute-done.35 = bf16[4,512,128]{2,1,0:T(8,128)(2,1)S(1)} collective-permute-done((bf16[4,512,128]{2,1,0:T(8,128)(2,1)S(1)}, bf16[4,512,128]{2,1,0:T(8,128)(2,1)S(1)}, u32[]{:S(2)}, u32[]{:S(2)}) %collective-permute-start.35) | collective-permute-done | bytes 524320 | tf_op jit(solution)/shard_map/ppermute | solution.py:757
  213.8 11.5 %collective-permute-done.38 = bf16[2048,128]{0,1:T(8,128)(2,1)} collective-permute-done((bf16[2048,128]{0,1:T(8,128)(2,1)S(1)}, bf16[2048,128]{0,1:T(8,128)(2,1)}, u32[]{:S(2)}, u32[]{:S(2)}) %collective-permute-start.38) | collective-permute-done | bytes 524320 | tf_op jit(solution)/shard_map/ppermute | solution.py:757
  229.1 4.0 copy.35
  233.1 13.7 %forward_layer.6 = (f32[8192,128]{1,0:T(8,128)}, bf16[8192,128]{1,0:T(8,128)(2,1)}, bf16[8192,128]{1,0:T(8,128)(2,1)}, bf16[8192,128]{1,0:T(8,128)(2,1)}, f32[8,128]{1,0:T(8,128)}, /*index=5*/f32[8,128]{1,0:T(8,128)}) custom-call(s32[64]{0:T(128)} %fusion.67.table_ref, bf16[128,64]{1,0:T(8,128)(2,1)} %copy.38.gain_ref, ...), custom_call_target="tpu_custom_call" | custom-call | flops 15000000512 | bytes 20971520 | tf_op jit(solution)/shard_map/forward_layer/pallas_call | solution.py:593
  246.8 13.7 %forward_layer.7 = (f32[8192,128]{1,0:T(8,128)}, bf16[8192,128]{1,0:T(8,128)(2,1)}, bf16[8192,128]{1,0:T(8,128)(2,1)}, bf16[8192,128]{1,0:T(8,128)(2,1)}, f32[8,128]{1,0:T(8,128)}, /*index=5*/f32[8,128]{1,0:T(8,128)}) custom-call(s32[64]{0:T(128)} %fusion.67.table_ref, bf16[128,64]{1,0:T(8,128)(2,1)} %copy.36.gain_ref, ...), custom_call_target="tpu_custom_call" | custom-call | flops 15000000512 | bytes 20971520 | tf_op jit(solution)/shard_map/forward_layer/pallas_call | solution.py:593
  260.5 28.6 %backward_layer.4 = (f32[8192,128]{1,0:T(8,128)}, bf16[16,2,2,128,128]{4,3,2,1,0:T(8,128)(2,1)}, bf16[16,2,2,128,128]{4,3,2,1,0:T(8,128)(2,1)}) custom-call(s32[64]{0:T(128)} %fusion.67.table_ref, bf16[128,64]{1,0:T(8,128)(2,1)} %copy.36.gain_ref, bf16[128,64]{1,0:T(8,128)(2,1)} %copy.43.end_gain_ref, f32[8,128]{1,0:T(8,128)} %get-tuple-element.199.scale_ref, ...), custom_call_target="tpu_custom_call" | custom-call | flops 17999998976 | bytes 31457280 | tf_op jit(solution)/shard_map/backward_layer/pallas_call | solution.py:632
  292.3 19.4 %backward_layer.5 = (f32[8192,128]{1,0:T(8,128)}, bf16[16,2,2,128,128]{4,3,2,1,0:T(8,128)(2,1)}, bf16[16,2,2,128,128]{4,3,2,1,0:T(8,128)(2,1)}) custom-call(s32[64]{0:T(128)} %fusion.67.table_ref, bf16[128,64]{1,0:T(8,128)(2,1)} %copy.38.gain_ref, bf16[128,64]{1,0:T(8,128)(2,1)} %copy.43.end_gain_ref, f32[8,128]{1,0:T(8,128)} %get-tuple-element.186.scale_ref, ...), custom_call_target="tpu_custom_call" | custom-call | flops 17999998976 | bytes 31457280 | tf_op jit(solution)/shard_map/backward_layer/pallas_call | solution.py:632
  319.9 19.3 %backward_layer.6 = (f32[8192,128]{1,0:T(8,128)}, bf16[16,2,2,128,128]{4,3,2,1,0:T(8,128)(2,1)}, bf16[16,2,2,128,128]{4,3,2,1,0:T(8,128)(2,1)}) custom-call(s32[64]{0:T(128)} %fusion.67.table_ref, bf16[128,64]{1,0:T(8,128)(2,1)} %copy.40.gain_ref, bf16[128,64]{1,0:T(8,128)(2,1)} %copy.43.end_gain_ref, f32[8,128]{1,0:T(8,128)} %get-tuple-element.169.scale_ref, ...), custom_call_target="tpu_custom_call" | custom-call | flops 17999998976 | bytes 31457280 | tf_op jit(solution)/shard_map/backward_layer/pallas_call | solution.py:632
  347.1 4.2 collective-permute-start.46
  362.4 18.2 %backward_layer.7 = (bf16[8192,128]{1,0:T(8,128)(2,1)}, bf16[16,2,2,128,128]{4,3,2,1,0:T(8,128)(2,1)}, bf16[16,2,2,128,128]{4,3,2,1,0:T(8,128)(2,1)}) custom-call(s32[64]{0:T(128)} %fusion.67.table_ref, bf16[128,64]{1,0:T(8,128)(2,1)} %copy.42.gain_ref, bf16[128,64]{1,0:T(8,128)(2,1)} %copy.43.end_gain_ref, f32[8,128]{1,0:T(8,128)} %get-tuple-element.143.scale_ref, ...), custom_call_target="tpu_custom_call" | custom-call | flops 17999998976 | bytes 31457280 | tf_op jit(solution)/shard_map/backward_layer/pallas_call | solution.py:632
  380.6 4.5 collective-permute-done.50
  389.8 5.3 %collective-permute-start.74 = (bf16[512,128]{1,0:T(8,128)(2,1)S(1)}, bf16[512,128]{1,0:T(8,128)(2,1)S(1)}, u32[]{:S(2)}, u32[]{:S(2)}) collective-permute-start(bf16[512,128]{1,0:T(8,128)(2,1)S(1)} %get-tuple-element.288), channel_id=1, source_target_pairs={{0,2},{1,3},{2,10},{3,11},{4,18},{5,19},{6,26},{7,27},{8,0},{9,1},... | collective-permute-start | bytes 393224 | tf_op jit(solution)/shard_map/ppermute | solution.py:872
  405.6 13.7 %collective-permute-done.73 = bf16[512,128]{1,0:T(8,128)(2,1)S(1)} collective-permute-done((bf16[512,128]{1,0:T(8,128)(2,1)S(1)}, bf16[512,128]{1,0:T(8,128)(2,1)S(1)}, u32[]{:S(2)}, u32[]{:S(2)}) %collective-permute-start.73) | collective-permute-done | bytes 131104 | tf_op jit(solution)/shard_map/ppermute | solution.py:872
  424.4 7.4 %collective-permute-done.66 = bf16[4,512,128]{2,1,0:T(8,128)(2,1)S(1)} collective-permute-done((bf16[4,512,128]{2,1,0:T(8,128)(2,1)S(1)}, bf16[4,512,128]{2,1,0:T(8,128)(2,1)S(1)}, u32[]{:S(2)}, u32[]{:S(2)}) %collective-permute-start.66) | collective-permute-done | bytes 524320 | tf_op jit(solution)/shard_map/ppermute | solution.py:757
  434.3 10.7 %collective-permute-done.59 = bf16[4,512,128]{2,1,0:T(8,128)(2,1)S(1)} collective-permute-done((bf16[4,512,128]{2,1,0:T(8,128)(2,1)S(1)}, bf16[4,512,128]{2,1,0:T(8,128)(2,1)S(1)}, u32[]{:S(2)}, u32[]{:S(2)}) %collective-permute-start.59) | collective-permute-done | bytes 524320 | tf_op jit(solution)/shard_map/ppermute | solution.py:757
  448.1 7.2 %collective-permute-done.58 = bf16[4,512,128]{2,1,0:T(8,128)(2,1)S(1)} collective-permute-done((bf16[4,512,128]{2,1,0:T(8,128)(2,1)S(1)}, bf16[4,512,128]{2,1,0:T(8,128)(2,1)S(1)}, u32[]{:S(2)}, u32[]{:S(2)}) %collective-permute-start.58) | collective-permute-done | bytes 524320 | tf_op jit(solution)/shard_map/ppermute | solution.py:757
  455.3 5.1 collective-permute-start.69
  464.4 4.2 collective-permute-start.63
  473.1 23.1 %collective-permute-done.63 = bf16[512,128]{1,0:T(8,128)(2,1)S(1)} collective-permute-done((bf16[512,128]{1,0:T(8,128)(2,1)S(1)}, bf16[512,128]{1,0:T(8,128)(2,1)S(1)}, u32[]{:S(2)}, u32[]{:S(2)}) %collective-permute-start.63) | collective-permute-done | bytes 131104 | tf_op jit(solution)/shard_map/ppermute | solution.py:872
  496.3 4.2 collective-permute-start.78
  502.1 3.7 collective-permute-done.61
  512.2 5.7 %assemble.1 = (f32[4,16,128,128]{3,2,1,0:T(8,128)}, f32[4,16,128,128]{3,2,1,0:T(8,128)}) custom-call(s32[2]{0:T(128)} %pad_add_fusion.refs_0_, bf16[4,2,2,128,128]{4,3,2,1,0:T(8,128)(2,1)} %pad_maximum_fusion.10.refs_1_, bf16[4,2,2,128,128]{4,3,2,1,0:T(8,128)(2,1)} %bitcast.273, bf16[4,2,2,128,128]{4,3,2,1,0:T(8,128)(2,1)} %pad_maximum_fusion.12.refs_3_, ...), custom_call_target="tpu_custom_call" | custom-call | bytes 12582912 | tf_op jit(solution)/shard_map/assemble/pallas_call | solution.py:700
  (384 shorter events, 189.0 us)
Async XLA Ops:
  40.5 26.7 %collective-permute-start.21 = (bf16[4,512,128]{2,1,0:T(8,128)(2,1)}, bf16[4,512,128]{2,1,0:T(8,128)(2,1)S(1)}, u32[]{:S(2)}, u32[]{:S(2)}) collective-permute-start(bf16[4,512,128]{2,1,0:T(8,128)(2,1)} %pad_maximum_fusion.6), channel_id=1, source_target_pairs={{0,8},{1,9},{2,10},{3,11},{4,12},{5,13},{6,14},{7,15},{8,0},{9,1},... | collective-permute-start | bytes 1572872 | tf_op jit(solution)/shard_map/ppermute | solution.py:757
  41.7 27.4 %collective-permute-start.22 = (bf16[4,512,128]{2,1,0:T(8,128)(2,1)}, bf16[4,512,128]{2,1,0:T(8,128)(2,1)S(1)}, u32[]{:S(2)}, u32[]{:S(2)}) collective-permute-start(bf16[4,512,128]{2,1,0:T(8,128)(2,1)} %pad_maximum_fusion.6), channel_id=1, source_target_pairs={{0,16},{1,17},{2,18},{3,19},{4,20},{5,21},{6,22},{7,23},{8,24},{9,... | collective-permute-start | bytes 1572872 | tf_op jit(solution)/shard_map/ppermute | solution.py:757
  44.0 26.3 %collective-permute-start.23 = (bf16[4,512,128]{2,1,0:T(8,128)(2,1)}, bf16[4,512,128]{2,1,0:T(8,128)(2,1)S(1)}, u32[]{:S(2)}, u32[]{:S(2)}) collective-permute-start(bf16[4,512,128]{2,1,0:T(8,128)(2,1)} %pad_maximum_fusion.6), channel_id=1, source_target_pairs={{0,24},{1,25},{2,26},{3,27},{4,28},{5,29},{6,30},{7,31},{8,16},{9,... | collective-permute-start | bytes 1572872 | tf_op jit(solution)/shard_map/ppermute | solution.py:757
  66.3 41.8 %collective-permute-start.7 = (bf16[2048,128]{0,1:T(8,128)(2,1)}, bf16[2048,128]{0,1:T(8,128)(2,1)S(1)}, u32[]{:S(2)}, u32[]{:S(2)}) collective-permute-start(bf16[2048,128]{0,1:T(8,128)(2,1)} %fusion.5), channel_id=1, source_target_pairs={{0,4},{1,5},{2,6},{3,7},{4,0},{5,1},{6,2},{7,3},{8,12},{9,13},{10,... | collective-permute-start | bytes 1572872 | tf_op jit(solution)/shard_map/ppermute | solution.py:757
  67.2 40.9 %collective-permute-start.6 = (bf16[2048,128]{0,1:T(8,128)(2,1)}, bf16[2048,128]{0,1:T(8,128)(2,1)S(1)}, u32[]{:S(2)}, u32[]{:S(2)}) collective-permute-start(bf16[2048,128]{0,1:T(8,128)(2,1)} %fusion.4), channel_id=1, source_target_pairs={{0,2},{1,3},{2,0},{3,1},{4,6},{5,7},{6,4},{7,5},{8,10},{9,11},{10,... | collective-permute-start | bytes 1572872 | tf_op jit(solution)/shard_map/ppermute | solution.py:757
  69.2 40.3 %collective-permute-start.18 = (bf16[512,128]{1,0:T(8,128)(2,1)S(1)}, bf16[512,128]{1,0:T(8,128)(2,1)S(1)}, u32[]{:S(2)}, u32[]{:S(2)}) collective-permute-start(bf16[512,128]{1,0:T(8,128)(2,1)S(1)} %get-tuple-element.139), channel_id=1, source_target_pairs={{0,2},{1,3},{2,0},{3,1},{4,6},{5,7},{6,4},{7,5},{8,10},{9,11},{10,... | collective-permute-start | bytes 393224 | tf_op jit(solution)/shard_map/ppermute | solution.py:757
  71.2 81.4 %collective-permute-start.24 = (bf16[16,512,128]{2,1,0:T(8,128)(2,1)}, bf16[16,512,128]{2,1,0:T(8,128)(2,1)}, u32[]{:S(2)}, u32[]{:S(2)}) collective-permute-start(bf16[16,512,128]{2,1,0:T(8,128)(2,1)} %constant_dynamic-update-slice_fusion.7), channel_id=1, source_target_pairs={{0,1},{1,0},{2,3},{3,2},{4,5},{5,4},{6,7},{7,6},{8,9},{9,8},{10,11... | collective-permute-start | bytes 6291464 | tf_op jit(solution)/shard_map/ppermute | solution.py:816
  78.8 45.5 %collective-permute-start.15 = (bf16[4,512,128]{2,1,0:T(8,128)(2,1)}, bf16[4,512,128]{2,1,0:T(8,128)(2,1)}, u32[]{:S(2)}, u32[]{:S(2)}) collective-permute-start(bf16[4,512,128]{2,1,0:T(8,128)(2,1)} %pad_maximum_fusion.4), channel_id=1, source_target_pairs={{0,8},{1,9},{2,10},{3,11},{4,12},{5,13},{6,14},{7,15},{8,0},{9,1},... | collective-permute-start | bytes 1572872 | tf_op jit(solution)/shard_map/ppermute | solution.py:757
  108.0 24.3 %collective-permute-start.16 = (bf16[4,512,128]{2,1,0:T(8,128)(2,1)}, bf16[4,512,128]{2,1,0:T(8,128)(2,1)}, u32[]{:S(2)}, u32[]{:S(2)}) collective-permute-start(bf16[4,512,128]{2,1,0:T(8,128)(2,1)} %pad_maximum_fusion.4), channel_id=1, source_target_pairs={{0,16},{1,17},{2,18},{3,19},{4,20},{5,21},{6,22},{7,23},{8,24},{9,... | collective-permute-start | bytes 1572872 | tf_op jit(solution)/shard_map/ppermute | solution.py:757
  108.1 24.3 %collective-permute-start.17 = (bf16[4,512,128]{2,1,0:T(8,128)(2,1)}, bf16[4,512,128]{2,1,0:T(8,128)(2,1)}, u32[]{:S(2)}, u32[]{:S(2)}) collective-permute-start(bf16[4,512,128]{2,1,0:T(8,128)(2,1)} %pad_maximum_fusion.4), channel_id=1, source_target_pairs={{0,24},{1,25},{2,26},{3,27},{4,28},{5,29},{6,30},{7,31},{8,16},{9,... | collective-permute-start | bytes 1572872 | tf_op jit(solution)/shard_map/ppermute | solution.py:757
  140.2 33.0 %collective-permute-start.25 = (bf16[16,512,128]{2,1,0:T(8,128)(2,1)}, bf16[16,512,128]{2,1,0:T(8,128)(2,1)}, u32[]{:S(2)}, u32[]{:S(2)}) collective-permute-start(bf16[16,512,128]{2,1,0:T(8,128)(2,1)} %constant_dynamic-update-slice_fusion.14), channel_id=1, source_target_pairs={{0,1},{1,0},{2,3},{3,2},{4,5},{5,4},{6,7},{7,6},{8,9},{9,8},{10,11... | collective-permute-start | bytes 6291464 | tf_op jit(solution)/shard_map/ppermute | solution.py:816
  144.0 24.4 %collective-permute-start.26 = (bf16[4,512,128]{2,1,0:T(8,128)(2,1)S(1)}, bf16[4,512,128]{2,1,0:T(8,128)(2,1)S(1)}, u32[]{:S(2)}, u32[]{:S(2)}) collective-permute-start(bf16[4,512,128]{2,1,0:T(8,128)(2,1)S(1)} %pad_maximum_fusion.7), channel_id=1, source_target_pairs={{0,8},{1,9},{2,10},{3,11},{4,12},{5,13},{6,14},{7,15},{8,0},{9,1},... | collective-permute-start | bytes 1572872 | tf_op jit(solution)/shard_map/ppermute | solution.py:757
  176.5 29.3 %collective-permute-start.32 = (bf16[16,512,128]{2,1,0:T(8,128)(2,1)}, bf16[16,512,128]{2,1,0:T(8,128)(2,1)}, u32[]{:S(2)}, u32[]{:S(2)}) collective-permute-start(bf16[16,512,128]{2,1,0:T(8,128)(2,1)} %constant_dynamic-update-slice_fusion.18), channel_id=1, source_target_pairs={{0,1},{1,0},{2,3},{3,2},{4,5},{5,4},{6,7},{7,6},{8,9},{9,8},{10,11... | collective-permute-start | bytes 6291464 | tf_op jit(solution)/shard_map/ppermute | solution.py:816
  178.9 34.9 %collective-permute-start.39 = (bf16[2048,128]{0,1:T(8,128)(2,1)S(1)}, bf16[2048,128]{0,1:T(8,128)(2,1)}, u32[]{:S(2)}, u32[]{:S(2)}) collective-permute-start(bf16[2048,128]{0,1:T(8,128)(2,1)S(1)} %copy-done.23), channel_id=1, source_target_pairs={{0,6},{1,7},{2,4},{3,5},{4,2},{5,3},{6,0},{7,1},{8,14},{9,15},{10,... | collective-permute-start | bytes 1572872 | tf_op jit(solution)/shard_map/ppermute | solution.py:757
  197.3 28.0 %collective-permute-start.38 = (bf16[2048,128]{0,1:T(8,128)(2,1)S(1)}, bf16[2048,128]{0,1:T(8,128)(2,1)}, u32[]{:S(2)}, u32[]{:S(2)}) collective-permute-start(bf16[2048,128]{0,1:T(8,128)(2,1)S(1)} %copy-done.22), channel_id=1, source_target_pairs={{0,4},{1,5},{2,6},{3,7},{4,0},{5,1},{6,2},{7,3},{8,12},{9,13},{10,... | collective-permute-start | bytes 1572872 | tf_op jit(solution)/shard_map/ppermute | solution.py:757
  197.4 27.9 %collective-permute-start.37 = (bf16[2048,128]{0,1:T(8,128)(2,1)S(1)}, bf16[2048,128]{0,1:T(8,128)(2,1)}, u32[]{:S(2)}, u32[]{:S(2)}) collective-permute-start(bf16[2048,128]{0,1:T(8,128)(2,1)S(1)} %copy-done.21), channel_id=1, source_target_pairs={{0,2},{1,3},{2,0},{3,1},{4,6},{5,7},{6,4},{7,5},{8,10},{9,11},{10,... | collective-permute-start | bytes 1572872 | tf_op jit(solution)/shard_map/ppermute | solution.py:757
  210.0 36.7 %collective-permute-start.36 = (bf16[16,512,128]{2,1,0:T(8,128)(2,1)}, bf16[16,512,128]{2,1,0:T(8,128)(2,1)}, u32[]{:S(2)}, u32[]{:S(2)}) collective-permute-start(bf16[16,512,128]{2,1,0:T(8,128)(2,1)} %constant_dynamic-update-slice_fusion.22), channel_id=1, source_target_pairs={{0,1},{1,0},{2,3},{3,2},{4,5},{5,4},{6,7},{7,6},{8,9},{9,8},{10,11... | collective-permute-start | bytes 6291464 | tf_op jit(solution)/shard_map/ppermute | solution.py:816
  313.0 29.2 %collective-permute-start.44 = (bf16[16,2,2,128,128]{4,3,2,1,0:T(8,128)(2,1)}, bf16[16,2,2,128,128]{4,3,2,1,0:T(8,128)(2,1)S(1)}, u32[]{:S(2)}, u32[]{:S(2)}) collective-permute-start(bf16[16,2,2,128,128]{4,3,2,1,0:T(8,128)(2,1)} %get-tuple-element.221), channel_id=1, source_target_pairs={{0,1},{1,0},{2,3},{3,2},{4,5},{5,4},{6,7},{7,6},{8,9},{9,8},{10,11... | collective-permute-start | bytes 6291464 | tf_op jit(solution)/shard_map/ppermute | solution.py:864
  317.9 24.3 %collective-permute-start.43 = (bf16[4,512,128]{2,1,0:T(8,128)(2,1)}, bf16[4,512,128]{2,1,0:T(8,128)(2,1)}, u32[]{:S(2)}, u32[]{:S(2)}) collective-permute-start(bf16[4,512,128]{2,1,0:T(8,128)(2,1)} %bitcast.103), channel_id=1, source_target_pairs={{0,24},{1,25},{2,26},{3,27},{4,28},{5,29},{6,30},{7,31},{8,16},{9,... | collective-permute-start | bytes 1572872 | tf_op jit(solution)/shard_map/ppermute | solution.py:757
  351.4 29.2 %collective-permute-start.48 = (bf16[512,128]{1,0:T(8,128)(2,1)}, bf16[512,128]{1,0:T(8,128)(2,1)}, u32[]{:S(2)}, u32[]{:S(2)}) collective-permute-start(bf16[512,128]{1,0:T(8,128)(2,1)} %get-tuple-element.297), channel_id=1, source_target_pairs={{0,6},{1,7},{2,14},{3,15},{4,22},{5,23},{6,30},{7,31},{8,4},{9,5},... | collective-permute-start | bytes 393224 | tf_op jit(solution)/shard_map/ppermute | solution.py:872
  351.6 33.5 %collective-permute-start.52 = (bf16[16,2,2,128,128]{4,3,2,1,0:T(8,128)(2,1)}, bf16[16,2,2,128,128]{4,3,2,1,0:T(8,128)(2,1)S(1)}, u32[]{:S(2)}, u32[]{:S(2)}) collective-permute-start(bf16[16,2,2,128,128]{4,3,2,1,0:T(8,128)(2,1)} %get-tuple-element.233), channel_id=1, source_target_pairs={{0,1},{1,0},{2,3},{3,2},{4,5},{5,4},{6,7},{7,6},{8,9},{9,8},{10,11... | collective-permute-start | bytes 6291464 | tf_op jit(solution)/shard_map/ppermute | solution.py:864
  385.9 34.3 %collective-permute-start.56 = (bf16[16,2,2,128,128]{4,3,2,1,0:T(8,128)(2,1)}, bf16[16,2,2,128,128]{4,3,2,1,0:T(8,128)(2,1)S(1)}, u32[]{:S(2)}, u32[]{:S(2)}) collective-permute-start(bf16[16,2,2,128,128]{4,3,2,1,0:T(8,128)(2,1)} %get-tuple-element.236), channel_id=1, source_target_pairs={{0,1},{1,0},{2,3},{3,2},{4,5},{5,4},{6,7},{7,6},{8,9},{9,8},{10,11... | collective-permute-start | bytes 6291464 | tf_op jit(solution)/shard_map/ppermute | solution.py:864
  395.1 24.2 %collective-permute-start.73 = (bf16[512,128]{1,0:T(8,128)(2,1)S(1)}, bf16[512,128]{1,0:T(8,128)(2,1)S(1)}, u32[]{:S(2)}, u32[]{:S(2)}) collective-permute-start(bf16[512,128]{1,0:T(8,128)(2,1)S(1)} %get-tuple-element.285), channel_id=1, source_target_pairs={{0,0},{1,1},{2,8},{3,9},{4,16},{5,17},{6,24},{7,25},{8,2},{9,3},{1... | collective-permute-start | bytes 393224 | tf_op jit(solution)/shard_map/ppermute | solution.py:872
  403.0 61.2 %collective-permute-start.55 = (bf16[2048,128]{1,0:T(8,128)(2,1)S(1)}, bf16[2048,128]{1,0:T(8,128)(2,1)S(1)}, u32[]{:S(2)}, u32[]{:S(2)}) collective-permute-start(bf16[2048,128]{1,0:T(8,128)(2,1)S(1)} %get-tuple-element.264), channel_id=1, source_target_pairs={{0,6},{1,7},{2,4},{3,5},{4,2},{5,3},{6,0},{7,1},{8,14},{9,15},{10,... | collective-permute-start | bytes 1572872 | tf_op jit(solution)/shard_map/ppermute | solution.py:757
  403.5 30.0 %collective-permute-start.53 = (bf16[2048,128]{1,0:T(8,128)(2,1)S(1)}, bf16[2048,128]{1,0:T(8,128)(2,1)S(1)}, u32[]{:S(2)}, u32[]{:S(2)}) collective-permute-start(bf16[2048,128]{1,0:T(8,128)(2,1)S(1)} %get-tuple-element.265), channel_id=1, source_target_pairs={{0,2},{1,3},{2,0},{3,1},{4,6},{5,7},{6,4},{7,5},{8,10},{9,11},{10,... | collective-permute-start | bytes 1572872 | tf_op jit(solution)/shard_map/ppermute | solution.py:757
  432.8 27.6 %collective-permute-start.57 = (bf16[4,512,128]{2,1,0:T(8,128)(2,1)S(1)}, bf16[4,512,128]{2,1,0:T(8,128)(2,1)S(1)}, u32[]{:S(2)}, u32[]{:S(2)}) collective-permute-start(bf16[4,512,128]{2,1,0:T(8,128)(2,1)S(1)} %bitcast.286), channel_id=1, source_target_pairs={{0,8},{1,9},{2,10},{3,11},{4,12},{5,13},{6,14},{7,15},{8,0},{9,1},... | collective-permute-start | bytes 1572872 | tf_op jit(solution)/shard_map/ppermute | solution.py:757
  433.5 30.9 %collective-permute-start.71 = (bf16[512,128]{1,0:T(8,128)(2,1)S(1)}, bf16[512,128]{1,0:T(8,128)(2,1)S(1)}, u32[]{:S(2)}, u32[]{:S(2)}) collective-permute-start(bf16[512,128]{1,0:T(8,128)(2,1)S(1)} %get-tuple-element.290), channel_id=1, source_target_pairs={{0,6},{1,7},{2,14},{3,15},{4,22},{5,23},{6,30},{7,31},{8,4},{9,5},... | collective-permute-start | bytes 393224 | tf_op jit(solution)/shard_map/ppermute | solution.py:872
  464.3 43.6 %collective-permute-start.54 = (bf16[2048,128]{1,0:T(8,128)(2,1)S(1)}, bf16[2048,128]{1,0:T(8,128)(2,1)S(1)}, u32[]{:S(2)}, u32[]{:S(2)}) collective-permute-start(bf16[2048,128]{1,0:T(8,128)(2,1)S(1)} %get-tuple-element.263), channel_id=1, source_target_pairs={{0,4},{1,5},{2,6},{3,7},{4,0},{5,1},{6,2},{7,3},{8,12},{9,13},{10,... | collective-permute-start | bytes 1572872 | tf_op jit(solution)/shard_map/ppermute | solution.py:757
  464.4 31.9 %collective-permute-start.63 = (bf16[512,128]{1,0:T(8,128)(2,1)S(1)}, bf16[512,128]{1,0:T(8,128)(2,1)S(1)}, u32[]{:S(2)}, u32[]{:S(2)}) collective-permute-start(bf16[512,128]{1,0:T(8,128)(2,1)S(1)} %get-tuple-element.294), channel_id=1, source_target_pairs={{0,6},{1,7},{2,14},{3,15},{4,22},{5,23},{6,30},{7,31},{8,4},{9,5},... | collective-permute-start | bytes 393224 | tf_op jit(solution)/shard_map/ppermute | solution.py:872
  468.6 31.9 %collective-permute-start.62 = (bf16[512,128]{1,0:T(8,128)(2,1)S(1)}, bf16[512,128]{1,0:T(8,128)(2,1)S(1)}, u32[]{:S(2)}, u32[]{:S(2)}) collective-permute-start(bf16[512,128]{1,0:T(8,128)(2,1)S(1)} %get-tuple-element.295), channel_id=1, source_target_pairs={{0,4},{1,5},{2,12},{3,13},{4,20},{5,21},{6,28},{7,29},{8,6},{9,7},... | collective-permute-start | bytes 393224 | tf_op jit(solution)/shard_map/ppermute | solution.py:872
  468.7 37.0 %collective-permute-start.61 = (bf16[512,128]{1,0:T(8,128)(2,1)S(1)}, bf16[512,128]{1,0:T(8,128)(2,1)S(1)}, u32[]{:S(2)}, u32[]{:S(2)}) collective-permute-start(bf16[512,128]{1,0:T(8,128)(2,1)S(1)} %get-tuple-element.296), channel_id=1, source_target_pairs={{0,2},{1,3},{2,10},{3,11},{4,18},{5,19},{6,26},{7,27},{8,0},{9,1},... | collective-permute-start | bytes 393224 | tf_op jit(solution)/shard_map/ppermute | solution.py:872
  469.8 36.7 %collective-permute-start.60 = (bf16[512,128]{1,0:T(8,128)(2,1)S(1)}, bf16[512,128]{1,0:T(8,128)(2,1)S(1)}, u32[]{:S(2)}, u32[]{:S(2)}) collective-permute-start(bf16[512,128]{1,0:T(8,128)(2,1)S(1)} %get-tuple-element.293), channel_id=1, source_target_pairs={{0,0},{1,1},{2,8},{3,9},{4,16},{5,17},{6,24},{7,25},{8,2},{9,3},{1... | collective-permute-start | bytes 393224 | tf_op jit(solution)/shard_map/ppermute | solution.py:872
  (110 other events, 1360.3 us)

commit v3 on v2

--- a/solution.py
+++ b/solution.py
@@ -268,6 +268,8 @@
 
 VMEM_LIMIT = 60 * 1024 * 1024
 CHUNKS = 8
+PARTS = 4
+SMALL = (16, 128)
 AXES = ("section", "tensor", "dp")
 
 
@@ -316,13 +318,23 @@
         chunk_copy(source, target, sems, chunk).wait()
 
 
-def factor_copies(own, peer, held, sems, side, outward=False):
-    half = own.shape[0]
+def quarter_copies(pieces, whole, sems, me, outward=False):
+    rows = pieces[0].shape[0]
     copies = []
-    for part, ref in enumerate((own, peer)):
-        inside = held.at[pl.ds(part * half, half), side]
+    for k, piece in enumerate(pieces):
+        part = whole.at[pl.ds(pl.multiple_of((me ^ k) * rows, rows), rows)]
+        ends = (part, piece) if outward else (piece, part)
+        copies.append(pltpu.make_async_copy(*ends, sems.at[k]))
+    return copies
+
+
+def factor_copies(parts, held, sems, side, outward=False):
+    count = parts[0].shape[0]
+    copies = []
+    for at, ref in enumerate(parts):
+        inside = held.at[pl.ds(at * count, count), side]
         ends = (inside, ref.at[:, side]) if outward else (ref.at[:, side], inside)
-        copies.append(pltpu.make_async_copy(*ends, sems.at[2 * side + part]))
+        copies.append(pltpu.make_async_copy(*ends, sems.at[side, at]))
     return copies
 
 
@@ -344,7 +356,7 @@
 
 def forward_kernel(first, inputs, table_ref, gain_ref, sums_ref, *refs):
     sources, refs = refs[:inputs], refs[inputs:]
-    own, peer = sources[-2:]
+    parts, sources = sources[:PARTS], sources[PARTS:]
     out_ref, u_ref, z_ref, slope_ref, scale_ref, next_ref = refs[:6]
     raw, h, w, u, z, slope, mid, in_sems, w_sems, out_sems = refs[6:]
     features, slots = h.shape
@@ -353,12 +365,14 @@
     blocks = features // size
     fold = size // blocks
 
-    left_in = factor_copies(own, peer, w, w_sems, 0)
-    right_in = factor_copies(own, peer, w, w_sems, 1)
+    left_in = factor_copies(parts, w, w_sems, 0)
+    right_in = factor_copies(parts, w, w_sems, 1)
     if first:
-        start_chunks(sources[0], raw, in_sems)
-        for copy in left_in + right_in:
+        pieces = quarter_copies(sources, raw, in_sems, table_ref[2, 0])
+        for copy in pieces + left_in + right_in:
             copy.start()
+        for copy in pieces:
+            copy.wait()
 
         def squares(block, total):
             rows = block_rows(block, size)
@@ -366,12 +380,7 @@
             h[rows, :] = part
             return total + fold_rows(part * part)
 
-        total = by_chunk(
-            blocks,
-            squares,
-            jnp.zeros((8, slots), jnp.float32),
-            lambda chunk: chunk_copy(sources[0], raw, in_sems, chunk).wait(),
-        )
+        total = by_chunk(blocks, squares, jnp.zeros((8, slots), jnp.float32))
     else:
         for copy in left_in:
             copy.start()
@@ -390,7 +399,7 @@
 
     def left(block, carry):
         rows = block_rows(block, size)
-        place = table_ref[block]
+        place = table_ref[0, block]
         normed = (h[rows, :] * scale * column(gain_ref, block, slots)).astype(jnp.bfloat16)
         u[rows, :] = normed
         weight = w[place // chunk_blocks, 0, place % chunk_blocks]
@@ -406,7 +415,7 @@
 
     def right(block, total):
         rows = block_rows(block, size)
-        place = table_ref[block]
+        place = table_ref[0, block]
         moved = [mid[pl.ds(block * fold + q, blocks, stride=size), :] for q in range(fold)]
         moved = jnp.concatenate(moved, axis=0).astype(jnp.bfloat16)
         z[rows, :] = moved
@@ -436,24 +445,28 @@
 
 def backward_kernel(turning, last, inputs, table_ref, gain_ref, end_gain_ref, scale_ref, *refs):
     sources, refs = refs[:inputs], refs[inputs:]
-    slope_ref, z_ref, u_ref, own, peer = sources[:5]
-    sources = sources[5:]
-    out_ref, own_grad, peer_grad = refs[:3]
-    g, slope, z, u, h, w, gw, mid, turned, top, goal = refs[3:14]
-    in_sems, w_sems, out_sems, gw_sems = refs[14:]
+    slope_ref, z_ref, u_ref = sources[:3]
+    parts, sources = sources[3 : 3 + PARTS], sources[3 + PARTS :]
+    count = len(refs) - 17
+    outs, refs = refs[:count], refs[count:]
+    own_grad, peer_grad = refs[:2]
+    g, slope, z, u, h, w, gw, mid, turned, top, goal = refs[2:13]
+    in_sems, w_sems, out_sems, gw_sems = refs[13:]
+    me = table_ref[2, 0]
     features, slots = g.shape
     size = w.shape[-1]
     chunk_blocks = w.shape[2]
     blocks = features // size
     fold = size // blocks
 
-    left_in = factor_copies(own, peer, w, w_sems, 0)
-    right_in = factor_copies(own, peer, w, w_sems, 1)
-    h_ref, g_ref = sources[:2]
+    left_in = factor_copies(parts, w, w_sems, 0)
+    right_in = factor_copies(parts, w, w_sems, 1)
+    g_ref, sources = sources[0], sources[1:]
     if turning:
-        goal_ref = sources[2]
+        goals = quarter_copies(sources[1:], goal, in_sems.at[5], me)
         start_chunks(g_ref, top, in_sems.at[0])
-        start_chunks(goal_ref, goal, in_sems.at[5])
+        for copy in goals:
+            copy.start()
     else:
         start_chunks(g_ref, g, in_sems.at[0])
     for copy in right_in:
@@ -463,7 +476,12 @@
     for copy in left_in:
         copy.start()
     start_chunks(u_ref, u, in_sems.at[3])
-    start_chunks(h_ref, h, in_sems.at[4])
+    if last:
+        starts = quarter_copies(sources, h, in_sems.at[5], me)
+        for copy in starts:
+            copy.start()
+    else:
+        start_chunks(sources[0], h, in_sems.at[4])
 
     if turning:
         zero = jnp.zeros((8, slots), jnp.float32)
@@ -480,8 +498,9 @@
 
         def arrive_top(chunk):
             chunk_copy(g_ref, top, in_sems.at[0], chunk).wait()
-            chunk_copy(goal_ref, goal, in_sems.at[5], chunk).wait()
-
+
+        for copy in goals:
+            copy.wait()
         totals = by_chunk(blocks, sums, (zero, zero, zero), arrive_top)
         squares, gained, crossed = [jnp.sum(total, axis=0, keepdims=True) for total in totals]
         end_scale = lax.rsqrt(squares / features + EPSILON)
@@ -498,8 +517,9 @@
 
     def right(block, carry):
         rows = block_rows(block, size)
-        place = table_ref[block]
+        place, home = table_ref[0, block], table_ref[1, block]
         at = (place // chunk_blocks, 1, place % chunk_blocks)
+        to = (home // chunk_blocks, 1, home % chunk_blocks)
         if turning:
             part = top[rows, :]
             gain = column(end_gain_ref, block, slots)
@@ -509,39 +529,45 @@
         else:
             gradient = g[rows, :]
         steep = (gradient * slope[rows, :].astype(jnp.float32)).astype(jnp.bfloat16)
-        gw[at] = inner_dot(z[rows, :], steep, 1, 1).astype(jnp.bfloat16)
+        gw[to] = inner_dot(z[rows, :], steep, 1, 1).astype(jnp.bfloat16)
         mid[rows, :] = inner_dot(w[at], steep, 1, 0)
         return carry
 
     by_chunk(blocks, right, 0, arrive_right)
-    right_out = factor_copies(own_grad, peer_grad, gw, gw_sems, 1, outward=True)
+    right_out = factor_copies((own_grad, peer_grad), gw, gw_sems, 1, outward=True)
     for copy in right_out:
         copy.start()
     for copy in left_in:
         copy.wait()
     scale = scale_ref[0:1, :]
 
+    if last:
+        for copy in starts:
+            copy.wait()
+
     def arrive_left(chunk):
         chunk_copy(u_ref, u, in_sems.at[3], chunk).wait()
-        chunk_copy(h_ref, h, in_sems.at[4], chunk).wait()
+        if not last:
+            chunk_copy(sources[0], h, in_sems.at[4], chunk).wait()
 
     def left(block, total):
         rows = block_rows(block, size)
-        place = table_ref[block]
+        place, home = table_ref[0, block], table_ref[1, block]
         at = (place // chunk_blocks, 0, place % chunk_blocks)
+        to = (home // chunk_blocks, 0, home % chunk_blocks)
         slot = block % turned.shape[0]
         for q in range(fold):
             turned[slot, pl.ds(q, blocks, stride=fold), :] = mid[
                 pl.ds(q * blocks + block, blocks, stride=size), :
             ]
         arrived = turned[slot].astype(jnp.bfloat16)
-        gw[at] = inner_dot(u[rows, :], arrived, 1, 1).astype(jnp.bfloat16)
+        gw[to] = inner_dot(u[rows, :], arrived, 1, 1).astype(jnp.bfloat16)
         weighted = inner_dot(w[at], arrived, 1, 0) * column(gain_ref, block, slots)
         g[rows, :] = g[rows, :] + scale * weighted
         return total + fold_rows(weighted * h[rows, :].astype(jnp.float32))
 
     total = by_chunk(blocks, left, jnp.zeros((8, slots), jnp.float32), arrive_left)
-    left_out = factor_copies(own_grad, peer_grad, gw, gw_sems, 0, outward=True)
+    left_out = factor_copies((own_grad, peer_grad), gw, gw_sems, 0, outward=True)
     for copy in left_out:
         copy.start()
     back = scale * scale * scale * jnp.sum(total, axis=0, keepdims=True) / features
@@ -555,9 +581,16 @@
             g[rows, :] = ended
         return carry
 
-    ended = u if last else g
-    by_chunk(blocks, finish, 0, None, lambda chunk: chunk_copy(ended, out_ref, out_sems, chunk).start())
-    wait_chunks(ended, out_ref, out_sems)
+    if last:
+        by_chunk(blocks, finish, 0)
+        ends = quarter_copies(outs, u, out_sems, me, outward=True)
+        for copy in ends:
+            copy.start()
+        for copy in ends:
+            copy.wait()
+    else:
+        by_chunk(blocks, finish, 0, None, lambda chunk: chunk_copy(g, outs[0], out_sems, chunk).start())
+        wait_chunks(g, outs[0], out_sems)
     for copy in right_out + left_out:
         copy.wait()
 
@@ -571,11 +604,11 @@
 OUTSIDE = pl.BlockSpec(memory_space=pl.ANY)
 
 
-def run_forward(table, gain, sums, residual, weights, after=()):
-    whole = residual.shape
-    first = residual.dtype == jnp.bfloat16
-    sources = (residual, *weights)
-    half = weights[0].shape
+def run_forward(table, gain, sums, residual, weights):
+    first = len(residual) > 1
+    whole = (residual[0].shape[0] * len(residual), residual[0].shape[1])
+    sources = (*weights, *residual)
+    held = (PARTS * weights[0].shape[0],) + weights[0].shape[1:]
     out_shape = (
         shape_of(whole, jnp.float32),
         shape_of(whole, jnp.bfloat16),
@@ -584,27 +617,21 @@
         shape_of((8, whole[1]), jnp.float32),
         shape_of((8, whole[1]), jnp.float32),
     )
-
-    def kernel(table_ref, gain_ref, sums_ref, *refs):
-        extra = len(sources) + len(after)
-        used = refs[: len(sources)] + refs[extra:]
-        forward_kernel(first, len(sources), table_ref, gain_ref, sums_ref, *used)
-
     return pl.pallas_call(
-        kernel,
-        in_specs=[SMEM, INSIDE, INSIDE] + [OUTSIDE] * (len(sources) + len(after)),
+        lambda *refs: forward_kernel(first, len(sources), *refs),
+        in_specs=[SMEM, INSIDE, INSIDE] + [OUTSIDE] * len(sources),
         out_specs=[OUTSIDE] * 4 + [INSIDE] * 2,
         out_shape=out_shape,
         scratch_shapes=[
-            pltpu.VMEM(whole if first else (16, 128), jnp.bfloat16),
+            pltpu.VMEM(whole if first else SMALL, jnp.bfloat16),
             pltpu.VMEM(whole, jnp.float32),
-            pltpu.VMEM((2 * half[0],) + half[1:], jnp.bfloat16),
+            pltpu.VMEM(held, jnp.bfloat16),
             pltpu.VMEM(whole, jnp.bfloat16),
             pltpu.VMEM(whole, jnp.bfloat16),
             pltpu.VMEM(whole, jnp.bfloat16),
             pltpu.VMEM(whole, jnp.float32),
             pltpu.SemaphoreType.DMA((CHUNKS,)),
-            pltpu.SemaphoreType.DMA((4,)),
+            pltpu.SemaphoreType.DMA((2, PARTS)),
             pltpu.SemaphoreType.DMA((4, CHUNKS)),
         ],
         compiler_params=pltpu.CompilerParams(vmem_limit_bytes=VMEM_LIMIT),
@@ -612,51 +639,178 @@
             flops=FORWARD_COST, bytes_accessed=20 * whole[0] * whole[1], transcendentals=0
         ),
         name="forward_layer",
-    )(table, gain, sums, *sources, *after)
-
-
-def run_backward(table, gain, end_gain, scale, kept, weights, sources, turning, last, after=()):
+    )(table, gain, sums, *sources)
+
+
+def run_backward(table, gain, end_gain, scale, kept, weights, sources, turning, last):
     whole = kept[0].shape
+    width = len(sources) - 1
     sources = (*kept, *weights, *sources)
-    half = weights[0].shape
-    ended = shape_of(whole, jnp.bfloat16 if last else jnp.float32)
-
-    def kernel(table_ref, gain_ref, end_gain_ref, scale_ref, *refs):
-        extra = len(sources) + len(after)
-        used = refs[: len(sources)] + refs[extra:]
-        backward_kernel(
-            turning, last, len(sources), table_ref, gain_ref, end_gain_ref, scale_ref, *used
-        )
-
-    small = (16, 128)
+    held = (PARTS * weights[0].shape[0],) + weights[0].shape[1:]
+    half = (held[0] // 2,) + held[1:]
+    ends = [shape_of(whole, jnp.float32)]
+    if last:
+        ends = [shape_of((whole[0] // width, whole[1]), jnp.bfloat16)] * width
+    out_shape = ends + [shape_of(half, jnp.bfloat16)] * 2
     return pl.pallas_call(
-        kernel,
-        in_specs=[SMEM] + [INSIDE] * 3 + [OUTSIDE] * (len(sources) + len(after)),
-        out_specs=[OUTSIDE] * 3,
-        out_shape=[ended] + [shape_of(half, jnp.bfloat16)] * 2,
+        lambda *refs: backward_kernel(turning, last, len(sources), *refs),
+        in_specs=[SMEM] + [INSIDE] * 3 + [OUTSIDE] * len(sources),
+        out_specs=[OUTSIDE] * len(out_shape),
+        out_shape=out_shape,
         scratch_shapes=[
             pltpu.VMEM(whole, jnp.float32),
             pltpu.VMEM(whole, jnp.bfloat16),
             pltpu.VMEM(whole, jnp.bfloat16),
             pltpu.VMEM(whole, jnp.bfloat16),
             pltpu.VMEM(whole, jnp.bfloat16 if last else jnp.float32),
-            pltpu.VMEM((2 * half[0],) + half[1:], jnp.bfloat16),
-            pltpu.VMEM((2 * half[0],) + half[1:], jnp.bfloat16),
+            pltpu.VMEM(held, jnp.bfloat16),
+            pltpu.VMEM(held, jnp.bfloat16),
             pltpu.VMEM(whole, jnp.float32),
-            pltpu.VMEM((8, half[-1], whole[1]), jnp.float32),
-            pltpu.VMEM(whole if turning else small, jnp.float32),
-            pltpu.VMEM(whole if turning else small, jnp.bfloat16),
+            pltpu.VMEM((8, held[-1], whole[1]), jnp.float32),
+            pltpu.VMEM(whole if turning else SMALL, jnp.float32),
+            pltpu.VMEM(whole if turning else SMALL, jnp.bfloat16),
             pltpu.SemaphoreType.DMA((6, CHUNKS)),
-            pltpu.SemaphoreType.DMA((4,)),
+            pltpu.SemaphoreType.DMA((2, PARTS)),
             pltpu.SemaphoreType.DMA((CHUNKS,)),
-            pltpu.SemaphoreType.DMA((4,)),
+            pltpu.SemaphoreType.DMA((2, PARTS)),
         ],
         compiler_params=pltpu.CompilerParams(vmem_limit_bytes=VMEM_LIMIT),
         cost_estimate=pl.CostEstimate(
             flops=BACKWARD_COST, bytes_accessed=30 * whole[0] * whole[1], transcendentals=0
         ),
         name="backward_layer",
-    )(table, gain, end_gain, scale, *sources, *after)
+    )(table, gain, end_gain, scale, *sources)
+
+
+def copies_kernel(plan, inputs, outputs, *refs):
+    sems = refs[-1]
+    copies = [
+        pltpu.make_async_copy(source, target, sems.at[at])
+        for at, (source, target) in enumerate(plan(refs[:inputs], refs[inputs : inputs + outputs]))
+    ]
+    for copy in copies:
+        copy.start()
+    for copy in copies:
+        copy.wait()
+
+
+def run_copies(plan, scalars, inputs, out_shape, most, name):
+    extra = [] if scalars is None else [scalars]
+    size = sum(math.prod(out.shape) for out in out_shape)
+    return pl.pallas_call(
+        lambda *refs: copies_kernel(plan, len(extra) + len(inputs), len(out_shape), *refs),
+        in_specs=[SMEM] * len(extra) + [OUTSIDE] * len(inputs),
+        out_specs=[OUTSIDE] * len(out_shape),
+        out_shape=out_shape,
+        scratch_shapes=[pltpu.SemaphoreType.DMA((most,))],
+        cost_estimate=pl.CostEstimate(flops=0, bytes_accessed=4 * size, transcendentals=0),
+        name=name,
+    )(*extra, *inputs)
+
+
+def joined(parts):
+    rows = parts[0].shape[0]
+    whole = shape_of((rows * len(parts),) + parts[0].shape[1:], parts[0].dtype)
+
+    def plan(sources, targets):
+        return [(source, targets[0].at[pl.ds(at * rows, rows)]) for at, source in enumerate(sources)]
+
+    return run_copies(plan, None, parts, [whole], len(parts), "join")[0]
+
+
+def factor_pieces(place, left, right, gain_rows, groups, chunk):
+    width = 4
+    size = left.shape[-1]
+    shapes = []
+    for group in groups:
+        rows = len(group) * 2 * chunk * size + (gain_rows.shape[0] if group[0] == 0 else 0)
+        shapes += [shape_of((rows, size), jnp.bfloat16)] * width
+
+    def plan(sources, targets):
+        place_ref, left_ref, right_ref, gain_ref = sources
+        copies = []
+        for at, group in enumerate(groups):
+            for j in range(width):
+                target = targets[at * width + j]
+                start = (place_ref[2] * width + (place_ref[0] ^ place_ref[1] ^ j)) * chunk
+                row = 0
+                for layer in group:
+                    for ref in (left_ref, right_ref):
+                        for inside in range(chunk):
+                            copies.append((ref.at[layer, start + inside], target.at[pl.ds(row, size)]))
+                            row += size
+                if group[0] == 0:
+                    copies.append((gain_ref, target.at[pl.ds(row, gain_rows.shape[0])]))
+        return copies
+
+    most = width * (sum(len(group) for group in groups) * 2 * chunk + 1)
+    flat = run_copies(plan, place, (left, right, gain_rows), shapes, most, "pieces")
+    return [flat[at * width : (at + 1) * width] for at in range(len(groups))]
+
+
+def choice(pairs, critic, slots):
+    rows = pairs.shape[0]
+    named = (pairs[:, 0:1] == critic) | (pairs[:, 1:2] == critic)
+    named = jnp.broadcast_to(named.astype(jnp.float32), (rows, slots))
+    before = lax.broadcasted_iota(jnp.int32, (rows, rows), 1) < lax.broadcasted_iota(jnp.int32, (rows, rows), 0)
+    rank = inner_dot(before.astype(jnp.bfloat16), named.astype(jnp.bfloat16), 1, 0)
+    at = lax.broadcasted_iota(jnp.int32, (rows, slots), 1).astype(jnp.float32)
+    return jnp.where(rank == at, named, 0.0).astype(jnp.bfloat16)
+
+
+def pick_kernel(place_ref, pairs_ref, values_ref, *out_refs):
+    width = len(out_refs)
+    features, slots = out_refs[0].shape
+    pairs = pairs_ref[...]
+    chosen = [choice(pairs, place_ref[1] ^ k, slots) for k in range(width)]
+    step = 512
+    for start in range(0, features, step):
+        part = values_ref[:, pl.ds(start, step)]
+        for k in range(width):
+            out_refs[k][pl.ds(start, step), :] = inner_dot(part, chosen[k], 0, 0).astype(jnp.bfloat16)
+
+
+def run_pick(place, pairs, values, width, slots):
+    rows, features = values.shape
+    return pl.pallas_call(
+        pick_kernel,
+        in_specs=[SMEM] + [INSIDE] * 2,
+        out_specs=[INSIDE] * width,
+        out_shape=[shape_of((features, slots), jnp.bfloat16)] * width,
+        compiler_params=pltpu.CompilerParams(vmem_limit_bytes=VMEM_LIMIT),
+        cost_estimate=pl.CostEstimate(
+            flops=2 * rows * features * slots * width, bytes_accessed=8 * rows * features, transcendentals=0
+        ),
+        name="pick",
+    )(place, pairs, values)
+
+
+def combine_kernel(place_ref, pairs_ref, *refs):
+    came, out_ref = refs[:-1], refs[-1]
+    width = len(came)
+    features, slots = came[0].shape
+    pairs = pairs_ref[...]
+    chosen = [choice(pairs, place_ref[1] ^ k, slots) for k in range(width)]
+    step = 512
+    for start in range(0, features, step):
+        total = sum(inner_dot(chosen[k], came[k][pl.ds(start, step), :], 1, 1) for k in range(width))
+        out_ref[:, pl.ds(start, step)] = (0.5 * total).astype(jnp.bfloat16)
+
+
+def run_combine(place, pairs, came):
+    rows = pairs.shape[0]
+    features = came[0].shape[0]
+    return pl.pallas_call(
+        combine_kernel,
+        in_specs=[SMEM] + [INSIDE] * (1 + len(came)),
+        out_specs=INSIDE,
+        out_shape=shape_of((rows, features), jnp.bfloat16),
+        compiler_params=pltpu.CompilerParams(vmem_limit_bytes=VMEM_LIMIT),
+        cost_estimate=pl.CostEstimate(
+            flops=2 * rows * came[0].size * len(came), bytes_accessed=4 * came[0].size * len(came), transcendentals=0
+        ),
+        name="combine",
+    )(place, pairs, *came)
 
 
 FORWARD_COST = 15_000_000_000
@@ -667,7 +821,7 @@
     sources, (left_ref, right_ref) = refs[: 2 * layer_count], refs[2 * layer_count : 2 * layer_count + 2]
     held, wide, in_sems, out_sems = refs[2 * layer_count + 2 :]
     width, chunk = held.shape[1], held.shape[3]
-    core, tensor = place_ref[0], place_ref[1]
+    origin, core = place_ref[0] ^ place_ref[1], place_ref[2]
     arrivals = [
         pltpu.make_async_copy(source, held.at[at], in_sems.at[at]) for at, source in enumerate(sources)
     ]
@@ -680,7 +834,7 @@
         half = core if side == 0 else 1 - core
         wide[at] = held[at].astype(jnp.float32) * factor
         for k in range(width):
-            start = (half * width + (tensor ^ k)) * chunk
+            start = (half * width + (origin ^ k)) * chunk
             for which, target in enumerate((left_ref, right_ref)):
                 copy = pltpu.make_async_copy(
                     wide.at[at, k, which],
@@ -717,6 +871,8 @@
 
 
 def plane_routes(width, replicas):
+    bits = width.bit_length() - 1
+    orders = [[(step + d) % bits for step in range(bits)] for d in range(replicas)]
     every = [(s, t, d) for s in range(width) for t in range(width) for d in range(replicas)]
 
     def route(move):
@@ -725,11 +881,19 @@
 
         return [(index(*place), index(*move(*place))) for place in every]
 
-    cores = route(lambda s, t, d: (s, t, 1 - d))
-    sections = [route(lambda s, t, d, k=k: (s ^ k, t, d)) for k in range(width)]
-    planes = [route(lambda s, t, d, k=k: (s, t ^ k, d)) for k in range(width)]
-    homes = [route(lambda s, t, d, k=k: (t, s ^ k, d)) for k in range(width)]
-    return cores, sections, planes, homes
+    ranks = [[0] * width for _ in range(replicas)]
+    for d in range(replicas):
+        for r in range(width):
+            ranks[d][sum(((r >> at) & 1) << orders[d][at] for at in range(bits))] = r
+    return {
+        "spread": [route(lambda s, t, d, j=j: (s ^ t ^ j, t, d)) for j in range(width)],
+        "lift": [route(lambda s, t, d, j=j: (s, t ^ s ^ j, d)) for j in range(width)],
+        "across": [route(lambda s, t, d, at=at: (s ^ (1 << orders[d][at]), t, d)) for at in range(bits)],
+        "cores": route(lambda s, t, d: (s, t, 1 - d)),
+        "sections": [route(lambda s, t, d, k=k: (s ^ k, t, d)) for k in range(width)],
+        "planes": [route(lambda s, t, d, k=k: (s, t ^ k, d)) for k in range(width)],
+        "homes": [route(lambda s, t, d, j=j: (t, t ^ s ^ j, d)) for j in range(width)],
+    }, ranks
 
 
 def added(*parts):
@@ -741,172 +905,164 @@
     replicas = lax.axis_size("dp")
     tok_rows, feat_local = patches.shape
     layer_count, local_blocks, size = left_factors.shape[1:4]
-    features = feat_local * width
-    blocks = features // size
+    blocks = feat_local * width // size
     wide = 2 * tok_rows // 3
     chunk = local_blocks // (replicas * width)
     layer_rows = 2 * chunk * size
-    cores, sections, planes, homes = plane_routes(width, replicas)
+    routes, ranks = plane_routes(width, replicas)
     section = lax.axis_index("section")
     tensor = lax.axis_index("tensor")
     core = lax.axis_index("dp")
-    away = range(1, width)
+    place = jnp.stack([section, tensor, core]).astype(jnp.int32)
     tie = lax.optimization_barrier
 
-    def send(values, routes):
-        return [values[0]] + [lax.ppermute(values[k], AXES, routes[k]) for k in away]
-
-    def crossed(values):
-        spread = jnp.stack(values)
-        return [
-            lax.dynamic_index_in_dim(spread, section ^ tensor ^ k, 0, keepdims=False) for k in range(width)
+    def move(value, route):
+        return lax.ppermute(value, AXES, route)
+
+    def move_all(values, name):
+        return [move(value, route) for value, route in zip(values, routes[name])]
+
+    def send(values, name):
+        return [values[0]] + [move(values[k], routes[name][k]) for k in range(1, width)]
+
+    def gather_one(mine):
+        return joined([mine, move(mine, routes["across"][0])])
+
+    def gather_two(pair):
+        return pair, move(pair, routes["across"][1]), move(pair, routes["cores"])
+
+    def gather_three(pair, other, peer):
+        return [pair, other, peer, move(other, routes["cores"])]
+
+    def as_weights(parts):
+        return [part.reshape(-1, 2, chunk, size, size) for part in parts]
+
+    block = jnp.arange(blocks, dtype=jnp.int32)
+    inside = block % local_blocks
+    replica = inside // (width * chunk)
+    part = (replica != core).astype(jnp.int32)
+    distance = section ^ ((inside // chunk) % width)
+    piece = tensor ^ (section ^ distance) ^ (block // local_blocks)
+    rank = jnp.array(ranks, jnp.int32)[replica, distance]
+    table = jnp.stack(
+        [
+            ((part * width + rank) * width + piece) * chunk + inside % chunk,
+            ((part * width + distance) * width + piece) * chunk + inside % chunk,
+            jnp.broadcast_to(tensor, block.shape),
         ]
-
-    critic_ids = jnp.arange(width, dtype=jnp.int32) ^ tensor
-    named = (critic_pairs[:, 0:1] == critic_ids) | (critic_pairs[:, 1:2] == critic_ids)
-    earlier = jnp.tril(jnp.ones((tok_rows, tok_rows), jnp.bfloat16), -1)
-    rank = jnp.dot(earlier, named.astype(jnp.bfloat16), preferred_element_type=jnp.float32)
-    rank = rank.astype(jnp.int32)
-    places = jnp.arange(wide, dtype=jnp.int32)
-    chosen = [
-        (named[:, k : k + 1] & (rank[:, k : k + 1] == places)).astype(jnp.bfloat16) for k in range(width)
-    ]
-
-    def picked(values):
-        return [inner_dot(values, chosen[k], 0, 0).astype(jnp.bfloat16) for k in range(width)]
-
-    def in_order(values):
-        spread = jnp.stack(values)
-        return spread[jnp.arange(width) ^ tensor].reshape((features,) + spread.shape[2:])
-
-    def piece_for(distance):
-        start = (core * width + (section ^ distance)) * chunk
-        parts = [
-            lax.dynamic_slice_in_dim(factors[0], start, chunk, axis=1)
-            for factors in (left_factors, right_factors)
-        ]
-        return jnp.stack(parts, axis=1).reshape(layer_count, layer_rows, size)
-
-    pieces = [piece_for(distance) for distance in range(width)]
+    ).astype(jnp.int32)
+
+    patch_sent = run_pick(place, critic_pairs, patches, width, wide)
+    patch_sent, factors = tie((patch_sent, (left_factors[0], right_factors[0])))
+    groups = [(0,), (1,), tuple(range(2, layer_count))]
     gain_rows = norm_gains[0].reshape(-1, size)
-    front = [jnp.concatenate([piece[0], gain_rows], axis=0) for piece in pieces]
-    rest = [piece[1:] for piece in pieces]
-    patch_sent = picked(patches)
-    front = send(front, sections)
-    patch_came = send(patch_sent, planes)
-    front, rest = tie((front, rest))
-    rest = send(rest, sections)
-    front = send(crossed(front), planes)
-    gains = jnp.stack([value[layer_rows:] for value in front])[jnp.arange(width) ^ tensor]
+    pieces = factor_pieces(place, *factors, gain_rows, groups, chunk)
+
+    patch_came = send(patch_sent, "planes")
+    near = [move_all(pieces[0], "spread")]
+    near[0], pieces[1] = tie((near[0], pieces[1]))
+    near.append(move_all(pieces[1], "spread"))
+    front = move_all(near[0], "lift")
+    near[1], pieces[2] = tie((near[1], pieces[2]))
+    near.append(move_all(pieces[2], "spread"))
+    front, near[1] = tie((front, near[1]))
+    second = move_all(near[1], "lift")
+    gains = jnp.stack([value[layer_rows:] for value in front])[jnp.arange(width) ^ section ^ tensor]
     gains = gains.reshape(width, layer_count + 1, local_blocks, size).transpose(1, 3, 0, 2)
     gains = gains.reshape(layer_count + 1, size, blocks)
-    arrived = [jnp.stack([value[:layer_rows] for value in front])]
-    for layer in range(1, layer_count):
-        arrived.append([value[layer - 1] for value in rest])
-
-    def to_plane(values, after):
-        values, _ = tie((crossed(values), after))
-        return send(values, planes)
-
-    def over_plane(mine):
-        return send([mine] * width, sections)
-
-    def both_cores(parts):
-        mine = jnp.concatenate(parts, axis=0)
-        return mine, lax.ppermute(mine, AXES, cores)
-
-    def as_weights(parts):
-        return [part.reshape(-1, 2, chunk, size, size) for part in parts]
-
-    spread = [over_plane(arrived[0])]
-    arrived[1] = jnp.stack(to_plane(arrived[1], front))
-    spread.append(over_plane(arrived[1]))
-    arrived[2] = to_plane(arrived[2], arrived[1])
-    weights = [as_weights(both_cores(spread[0]))]
-
-    block = jnp.arange(blocks, dtype=jnp.int32)
-    inside = block % local_blocks
-    part = (inside // (width * chunk) != core).astype(jnp.int32)
-    rank_of = section ^ ((inside // chunk) % width)
-    table = ((part * width + rank_of) * width + (tensor ^ (block // local_blocks))) * chunk + inside % chunk
-    table = table.astype(jnp.int32)
-
-    residual = in_order(patch_came)
+    lowest = [joined([value[:layer_rows].reshape(1, layer_rows, size) for value in front])]
+    pair = gather_one(lowest[0])
+    gathered = gather_two(pair)
+    weights = [as_weights(gather_three(*gathered))]
+    lowest.append(joined([value.reshape(1, layer_rows, size) for value in second]))
+    pair = gather_one(lowest[1])
+    patch_came, second, near[2] = tie((patch_came, second, near[2]))
+    later = move_all(near[2], "lift")
+    pairs = [None, pair] + [None] * (layer_count - 2)
+    pairs[1], later, teacher = tie((pairs[1], later, teacher))
+    for layer in range(2, layer_count):
+        at = (layer - 2) * layer_rows
+        lowest.append(joined([value[at : at + layer_rows].reshape(1, layer_rows, size) for value in later]))
+    target_sent = run_pick(place, critic_pairs, teacher, width, wide)
+
+    residual = patch_came
     sums = jnp.zeros((8, wide), jnp.float32)
-    target_sent = picked(teacher)
-    (residual, spread[1], arrived[2], target_sent) = tie((residual, spread[1], arrived[2], target_sent))
-    arrived[2] = jnp.stack(arrived[2])
+    flying = {1: gather_two(pairs[1])}
+    if layer_count > 2:
+        pairs[2] = gather_one(lowest[2])
+    residual, flying, pairs, target_sent = tie((residual, flying, pairs, target_sent))
     stored = []
     for layer in range(layer_count):
-        flying = []
+        ahead = {}
         if layer + 1 < layer_count:
-            flying.append(both_cores(spread[layer + 1]))
+            ahead["weights"] = gather_three(*flying.pop(layer + 1))
         if layer + 2 < layer_count:
-            flying.append(over_plane(arrived[layer + 2]))
+            ahead["two"] = gather_two(pairs[layer + 2])
         if layer + 3 < layer_count:
-            flying.append(to_plane(arrived[layer + 3], arrived[layer + 2]))
+            ahead["one"] = (lowest[layer + 3], move(lowest[layer + 3], routes["across"][0]))
         following, u, z, slope, scale, sums = run_forward(
             table, gains[layer], sums, residual, weights[layer]
         )
         stored.append(((slope, z, u), scale, residual))
-        residual, flying = tie((following, flying))
+        following, ahead = tie((following, ahead))
+        residual = (following,)
         if layer + 1 < layer_count:
-            weights.append(as_weights(flying[0]))
+            weights.append(as_weights(ahead["weights"]))
         if layer + 2 < layer_count:
-            spread.append(flying[1])
+            flying[layer + 2] = ahead["two"]
         if layer + 3 < layer_count:
-            arrived[layer + 3] = jnp.stack(flying[2])
+            pairs[layer + 3] = joined(list(ahead["one"]))
         if layer == 0:
             target_sent, sums = tie((target_sent, sums))
-            target = in_order(send(target_sent, planes))
+            target = send(target_sent, "planes")
 
     def core_sum(mine, other):
-        return (mine, lax.ppermute(other, AXES, cores))
+        return (mine, move(other, routes["cores"]))
 
     def plane_sum(value):
         value = value.reshape(width, width, layer_rows, size)
-        return send([value[k] for k in range(width)], sections)
+        return send([value[k] for k in range(width)], "sections")
 
     def homeward(value):
-        sent = crossed([value[k] for k in range(width)])
-        return [lax.ppermute(sent[k], AXES, homes[k]) for k in range(width)]
+        return move_all([value[j] for j in range(width)], "homes")
+
+    def both_halves(parts):
+        whole = joined([part.reshape(1, layer_rows, size) for part in parts])
+        return whole, move(whole, routes["cores"])
 
     steps = (
         lambda state: core_sum(*state),
         lambda state: plane_sum(added(*state)),
         lambda state: homeward(added(*state)),
-        lambda state: (jnp.stack(state), lax.ppermute(jnp.stack(state), AXES, cores)),
-    )
-    gradient = residual
+        both_halves,
+    )
+    gradient = residual[0]
     underway = []
     for layer in range(layer_count - 1, -1, -1):
         turning = layer == layer_count - 1
         last = layer == 0
         kept, scale, inputs = stored[layer]
-        sources = (inputs, gradient, target) if turning else (inputs, gradient)
+        sources = (gradient, *inputs, *target) if turning else (gradient, *inputs)
         underway = [(at + 1, steps[at](state)) for at, state in underway]
-        gradient, mine, other = run_backward(
+        *gradient, mine, other = run_backward(
             table, gains[layer], gains[layer_count], scale, kept, weights[layer], sources, turning, last
         )
         gradient, mine, other, states = tie((gradient, mine, other, [state for _, state in underway]))
         underway = [(at, state) for (at, _), state in zip(underway, states)]
         underway.append((0, (mine, other)))
-
-    returned = gradient.reshape(width, feat_local, wide)
-    returned = [lax.dynamic_index_in_dim(returned, tensor ^ k, 0, keepdims=False) for k in range(width)]
-    returned = send(returned, planes)
+        if not last:
+            gradient = gradient[0]
+
+    returned = send(gradient, "planes")
     homes_of = []
     for at, state in underway:
         for step in steps[at:]:
             state = step(state)
         homes_of.append(state)
-    combined = sum(inner_dot(chosen[k], returned[k], 1, 1) for k in range(width))
-    d_patches = (0.5 * combined).astype(jnp.bfloat16)
+    d_patches = run_combine(place, critic_pairs, returned)
     grad_factor = 1.0 / math.sqrt(2 * tok_rows * width * replicas)
     parts = [part.reshape(width, 2, chunk, size, size) for pair in homes_of[::-1] for part in pair]
-    grad_left, grad_right = run_assemble(
-        jnp.stack([core, tensor]).astype(jnp.int32), parts, layer_count, grad_factor
-    )
+    grad_left, grad_right = run_assemble(place, parts, layer_count, grad_factor)
     return (d_patches, grad_left[None], grad_right[None])
 
 

time: 519 us -> 816 us (1.57); the launches traced: 518 us -> 802 us
  Pallas kernels: 146 us -> 492 us
  starting transfers between devices: 103 us -> 176 us
  waiting for transfers between devices: 166 us -> 98.7 us
  local copies, waits for them, and re-layouts: 55.8 us -> 20.5 us
  other arithmetic: 32.1 us -> 12.2 us
  matrix products: 12.7 us -> 0 us
    pallas_call x8 -> x24, Pallas kernels: 140 us -> 487 us  [the longest x13 336 us: run_copies(): pl.pallas_call(lambda *refs: copies_kernel(plan, len(extra) + len(inputs)...]
    ppermute x79 -> x85, starting transfers between devices: 103 us -> 176 us  [move(): return lax.ppermute(value, AXES, route)]
    ppermute x79 -> x85, waiting for transfers between devices: 166 us -> 98.7 us  [move(): return lax.ppermute(value, AXES, route)]
    another operation x23 -> x2, other arithmetic: 18.9 us -> 1.19 us  [the longest x1 0.64 us: plane_shards(): place = jnp.stack([section, tensor, core]).astype(jnp.int32)]
    unnamed x147 -> x87, local copies, waits for them, and re-layouts: 24 us -> 6.81 us
    dot_general x13 -> x0, matrix products: 12.7 us -> none  [the longest x12 12.5 us: inner_dot(): lax.dot_general(left, right, (((left_dim,), (right_dim,)), ((), ())), pre...]
    gather x4 -> x1, local copies, waits for them, and re-layouts: 12.2 us -> 0.88 us  [plane_shards(): rank = jnp.array(ranks, jnp.int32)[replica, distance]]
  transfers between devices with their start and end apart: 79 -> 85, of which waited for: 26 -> 19; matrix products, arithmetic and copies ran while one was open for 16% -> 3% of each run, Pallas kernels for 19% -> 46%
where the time goes in v3:
time: 816 us; the launch traced here: 802 us
  Pallas kernels  492 us (60%)
  starting transfers between devices  176 us (22%)
  waiting for transfers between devices  98.7 us (12%)
  local copies, waits for them, and re-layouts  20.5 us (3%)
  other arithmetic  12.2 us (1%)
    pallas_call x13, Pallas kernels, run_copies(): pl.pallas_call(lambda *refs: copies_kernel(plan, len(extra) + len(inputs)...  336 us
    ppermute x85, starting transfers between devices, move(): return lax.ppermute(value, AXES, route)  176 us
    ppermute x85, waiting for transfers between devices, move(): return lax.ppermute(value, AXES, route)  98.7 us
    pallas_call x4, Pallas kernels, run_backward(): pl.pallas_call(lambda *refs: backward_kernel(turning, last, len(sources),...  84.2 us
    pallas_call x4, Pallas kernels, run_forward(): pl.pallas_call(lambda *refs: forward_kernel(first, len(sources), *refs),...  54.5 us
  transfers between devices with their start and end apart: 85, of which 19 were waited for; matrix products, arithmetic and copies ran while one was open for 3% of the time, Pallas kernels for 46%

profile of v3, /device:TPU:5, one launch (start us, length us, event | category | flops | bytes accessed | tf_op | source)
XLA Modules:
  0.0 801.5 jit_solution(4865305010681087783)
XLA Ops:
  8.1 68.4 %pieces.1 = (bf16[592,128]{1,0:T(8,128)(2,1)}, bf16[592,128]{1,0:T(8,128)(2,1)}, bf16[592,128]{1,0:T(8,128)(2,1)}, bf16[592,128]{1,0:T(8,128)(2,1)}, bf16[512,12...) custom-call(s32[3]{0:T(128)} %pad_add_fusion.1.place_ref.refs_0_, ...), custom_call_target="tpu_custom_call" | custom-call | bytes 4358144 | tf_op jit(solution)/shard_map/pieces/pallas_call | solution.py:700
  118.6 17.0 %join.12.refs_0_ = bf16[4,512,128]{2,1,0:T(8,128)(2,1)} custom-call(bf16[1,512,128]{2,1,0:T(8,128)(2,1)} %get-tuple-element.401.refs_0_, bf16[1,512,128]{2,1,0:T(8,128)(2,1)} %get-tuple-element.400.refs_1_, bf16[1,512,128]{2,1,0:T(8,128)(2,1)} %get-tuple-element.399.refs_2_, bf16[1,512,128]{2,1,0:T(8,128)(2,1)} %get-tuple-element.398.refs_3_), custom_call_target="tpu_custom_call" | custom-call | bytes 1048576 | tf_op jit(solution)/shard_map/join/pallas_call | solution.py:700
  148.4 8.6 %collective-permute-done.19 = bf16[512,128]{1,0:T(8,128)(2,1)S(1)} collective-permute-done((bf16[512,128]{1,0:T(8,128)(2,1)S(1)}, bf16[512,128]{1,0:T(8,128)(2,1)S(1)}, u32[]{:S(2)}, u32[]{:S(2)}) %collective-permute-start.19) | collective-permute-done | bytes 131104 | tf_op jit(solution)/shard_map/ppermute | solution.py:920
  164.0 32.9 %join.13 = bf16[8,512,128]{2,1,0:T(8,128)(2,1)} custom-call(bf16[4,512,128]{2,1,0:T(8,128)(2,1)} %join.12.refs_0_, bf16[4,512,128]{2,1,0:T(8,128)(2,1)} %copy-done.17), custom_call_target="tpu_custom_call" | custom-call | bytes 2097152 | tf_op jit(solution)/shard_map/join/pallas_call | solution.py:700
  200.8 17.0 %join.14.refs_0_ = bf16[4,512,128]{2,1,0:T(8,128)(2,1)} custom-call(bf16[1,512,128]{2,1,0:T(8,128)(2,1)} %bitcast.196, bf16[1,512,128]{2,1,0:T(8,128)(2,1)} %bitcast.197, bf16[1,512,128]{2,1,0:T(8,128)(2,1)} %bitcast.198, bf16[1,512,128]{2,1,0:T(8,128)(2,1)} %bitcast.199), custom_call_target="tpu_custom_call" | custom-call | bytes 1048576 | tf_op jit(solution)/shard_map/join/pallas_call | solution.py:700
  217.8 6.5 collective-permute-start.27
  235.3 5.2 collective-permute-done.26
  251.1 32.9 %join.15 = bf16[8,512,128]{2,1,0:T(8,128)(2,1)} custom-call(bf16[4,512,128]{2,1,0:T(8,128)(2,1)} %join.14.refs_0_, bf16[4,512,128]{2,1,0:T(8,128)(2,1)} %copy-done.14), custom_call_target="tpu_custom_call" | custom-call | bytes 2097152 | tf_op jit(solution)/shard_map/join/pallas_call | solution.py:700
  284.0 6.6 collective-permute-start.14
  295.5 17.0 %join.16.refs_0_ = bf16[4,512,128]{2,1,0:T(8,128)(2,1)} custom-call(bf16[1,512,128]{2,1,0:T(8,128)(2,1)} %get-tuple-element.408.refs_0_, bf16[1,512,128]{2,1,0:T(8,128)(2,1)} %get-tuple-element.388.refs_1_, bf16[1,512,128]{2,1,0:T(8,128)(2,1)} %get-tuple-element.406.refs_2_, bf16[1,512,128]{2,1,0:T(8,128)(2,1)} %get-tuple-element.384.refs_3_), custom_call_target="tpu_custom_call" | custom-call | bytes 1048576 | tf_op jit(solution)/shard_map/join/pallas_call | solution.py:700
  316.8 17.0 %join.18.refs_0_ = bf16[4,512,128]{2,1,0:T(8,128)(2,1)} custom-call(bf16[1,512,128]{2,1,0:T(8,128)(2,1)} %get-tuple-element.409.refs_0_, bf16[1,512,128]{2,1,0:T(8,128)(2,1)} %get-tuple-element.387.refs_1_, bf16[1,512,128]{2,1,0:T(8,128)(2,1)} %get-tuple-element.407.refs_2_, bf16[1,512,128]{2,1,0:T(8,128)(2,1)} %get-tuple-element.383.refs_3_), custom_call_target="tpu_custom_call" | custom-call | bytes 1048576 | tf_op jit(solution)/shard_map/join/pallas_call | solution.py:700
  339.3 32.9 %join.17 = bf16[8,512,128]{2,1,0:T(8,128)(2,1)} custom-call(bf16[4,512,128]{2,1,0:T(8,128)(2,1)} %join.16.refs_0_, bf16[4,512,128]{2,1,0:T(8,128)(2,1)} %copy-done.16), custom_call_target="tpu_custom_call" | custom-call | bytes 2097152 | tf_op jit(solution)/shard_map/join/pallas_call | solution.py:700
  374.4 14.5 %forward_layer.4 = (f32[8192,128]{1,0:T(8,128)}, bf16[8192,128]{1,0:T(8,128)(2,1)}, bf16[8192,128]{1,0:T(8,128)(2,1)}, bf16[8192,128]{1,0:T(8,128)(2,1)}, f32[8,128]{1,0:T(8,128)}, /*index=5*/f32[8,128]{1,0:T(8,128)}) custom-call(s32[3,64]{1,0:T(4,128)} %pad_add_fusion.refs_0_, bf16[128,64]{1,0:T(8,128)(2,1)} %copy.27.refs_1_, ...), custom_call_target="tpu_custom_call" | custom-call | flops 15000000512 | bytes 20971520 | tf_op jit(solution)/shard_map/forward_layer/pallas_call | solution.py:620
  390.5 32.9 %join.19 = bf16[8,512,128]{2,1,0:T(8,128)(2,1)} custom-call(bf16[4,512,128]{2,1,0:T(8,128)(2,1)} %join.18.refs_0_, bf16[4,512,128]{2,1,0:T(8,128)(2,1)} %copy-done.15), custom_call_target="tpu_custom_call" | custom-call | bytes 2097152 | tf_op jit(solution)/shard_map/join/pallas_call | solution.py:700
  424.8 13.4 %forward_layer.5 = (f32[8192,128]{1,0:T(8,128)}, bf16[8192,128]{1,0:T(8,128)(2,1)}, bf16[8192,128]{1,0:T(8,128)(2,1)}, bf16[8192,128]{1,0:T(8,128)(2,1)}, f32[8,128]{1,0:T(8,128)}, /*index=5*/f32[8,128]{1,0:T(8,128)}) custom-call(s32[3,64]{1,0:T(4,128)} %pad_add_fusion.refs_0_, bf16[128,64]{1,0:T(8,128)(2,1)} %copy.25.refs_1_, ...), custom_call_target="tpu_custom_call" | custom-call | flops 15000000512 | bytes 20971520 | tf_op jit(solution)/shard_map/forward_layer/pallas_call | solution.py:620
  441.7 13.3 %forward_layer.6 = (f32[8192,128]{1,0:T(8,128)}, bf16[8192,128]{1,0:T(8,128)(2,1)}, bf16[8192,128]{1,0:T(8,128)(2,1)}, bf16[8192,128]{1,0:T(8,128)(2,1)}, f32[8,128]{1,0:T(8,128)}, /*index=5*/f32[8,128]{1,0:T(8,128)}) custom-call(s32[3,64]{1,0:T(4,128)} %pad_add_fusion.refs_0_, bf16[128,64]{1,0:T(8,128)(2,1)} %copy.23.refs_1_, ...), custom_call_target="tpu_custom_call" | custom-call | flops 15000000512 | bytes 20971520 | tf_op jit(solution)/shard_map/forward_layer/pallas_call | solution.py:620
  456.1 13.3 %forward_layer.7 = (f32[8192,128]{1,0:T(8,128)}, bf16[8192,128]{1,0:T(8,128)(2,1)}, bf16[8192,128]{1,0:T(8,128)(2,1)}, bf16[8192,128]{1,0:T(8,128)(2,1)}, f32[8,128]{1,0:T(8,128)}, /*index=5*/f32[8,128]{1,0:T(8,128)}) custom-call(s32[3,64]{1,0:T(4,128)} %pad_add_fusion.refs_0_, bf16[128,64]{1,0:T(8,128)(2,1)} %copy.21.refs_1_, ...), custom_call_target="tpu_custom_call" | custom-call | flops 15000000512 | bytes 20971520 | tf_op jit(solution)/shard_map/forward_layer/pallas_call | solution.py:620
  469.5 28.4 %backward_layer.4 = (f32[8192,128]{1,0:T(8,128)}, bf16[16,2,2,128,128]{4,3,2,1,0:T(8,128)(2,1)}, bf16[16,2,2,128,128]{4,3,2,1,0:T(8,128)(2,1)}) custom-call(s32[3,64]{1,0:T(4,128)} %pad_add_fusion.refs_0_, bf16[128,64]{1,0:T(8,128)(2,1)} %copy.21.refs_1_, bf16[128,64]{1,0:T(8,128)(2,1)} %copy.28.refs_2_, f32[8,128]{1,0:T(8,128)} %get-tuple-element.295.refs_3_, ...), custom_call_target="tpu_custom_call" | custom-call | flops 17999998976 | bytes 31457280 | tf_op jit(solution)/shard_map/backward_layer/pallas_call | solution.py:655
  498.5 19.0 %backward_layer.5 = (f32[8192,128]{1,0:T(8,128)}, bf16[16,2,2,128,128]{4,3,2,1,0:T(8,128)(2,1)}, bf16[16,2,2,128,128]{4,3,2,1,0:T(8,128)(2,1)}) custom-call(s32[3,64]{1,0:T(4,128)} %pad_add_fusion.refs_0_, bf16[128,64]{1,0:T(8,128)(2,1)} %copy.23.refs_1_, bf16[128,64]{1,0:T(8,128)(2,1)} %copy.28.refs_2_, f32[8,128]{1,0:T(8,128)} %get-tuple-element.281.refs_3_, ...), custom_call_target="tpu_custom_call" | custom-call | flops 17999998976 | bytes 31457280 | tf_op jit(solution)/shard_map/backward_layer/pallas_call | solution.py:655
  525.8 19.0 %backward_layer.6 = (f32[8192,128]{1,0:T(8,128)}, bf16[16,2,2,128,128]{4,3,2,1,0:T(8,128)(2,1)}, bf16[16,2,2,128,128]{4,3,2,1,0:T(8,128)(2,1)}) custom-call(s32[3,64]{1,0:T(4,128)} %pad_add_fusion.refs_0_, bf16[128,64]{1,0:T(8,128)(2,1)} %copy.25.refs_1_, bf16[128,64]{1,0:T(8,128)(2,1)} %copy.28.refs_2_, f32[8,128]{1,0:T(8,128)} %get-tuple-element.265.refs_3_, ...), custom_call_target="tpu_custom_call" | custom-call | flops 17999998976 | bytes 31457280 | tf_op jit(solution)/shard_map/backward_layer/pallas_call | solution.py:655
  573.3 17.8 %backward_layer.7 = (bf16[2048,128]{1,0:T(8,128)(2,1)}, bf16[2048,128]{1,0:T(8,128)(2,1)}, bf16[2048,128]{1,0:T(8,128)(2,1)}, bf16[2048,128]{1,0:T(8,128)(2,1)},...) custom-call(s32[3,64]{1,0:T(4,128)} %pad_add_fusion.refs_0_, bf16[128,64]{1,0:T(8,128)(2,1)} %copy.27.refs_1_, ...), custom_call_target="tpu_custom_call" | custom-call | flops 17999998976 | bytes 31457280 | tf_op jit(solution)/shard_map/backward_layer/pallas_call | solution.py:655
  612.1 14.4 %collective-permute-done.73 = bf16[4,512,128]{2,1,0:T(8,128)(2,1)S(1)} collective-permute-done((bf16[4,512,128]{2,1,0:T(8,128)(2,1)S(1)}, bf16[4,512,128]{2,1,0:T(8,128)(2,1)S(1)}, u32[]{:S(2)}, u32[]{:S(2)}) %collective-permute-start.73) | collective-permute-done | bytes 524320 | tf_op jit(solution)/shard_map/ppermute | solution.py:920
  626.5 12.4 %collective-permute-done.72 = bf16[4,512,128]{2,1,0:T(8,128)(2,1)S(1)} collective-permute-done((bf16[4,512,128]{2,1,0:T(8,128)(2,1)S(1)}, bf16[4,512,128]{2,1,0:T(8,128)(2,1)S(1)}, u32[]{:S(2)}, u32[]{:S(2)}) %collective-permute-start.72) | collective-permute-done | bytes 524320 | tf_op jit(solution)/shard_map/ppermute | solution.py:920
  638.9 5.3 collective-permute-start.64
  651.0 9.9 %collective-permute-done.64 = bf16[4,512,128]{2,1,0:T(8,128)(2,1)S(1)} collective-permute-done((bf16[4,512,128]{2,1,0:T(8,128)(2,1)S(1)}, bf16[4,512,128]{2,1,0:T(8,128)(2,1)S(1)}, u32[]{:S(2)}, u32[]{:S(2)}) %collective-permute-start.64) | collective-permute-done | bytes 524320 | tf_op jit(solution)/shard_map/ppermute | solution.py:920
  668.9 6.6 collective-permute-start.75
  675.5 20.8 %collective-permute-done.77 = bf16[512,128]{1,0:T(8,128)(2,1)S(1)} collective-permute-done((bf16[512,128]{1,0:T(8,128)(2,1)S(1)}, bf16[512,128]{1,0:T(8,128)(2,1)S(1)}, u32[]{:S(2)}, u32[]{:S(2)}) %collective-permute-start.77) | collective-permute-done | bytes 131104 | tf_op jit(solution)/shard_map/ppermute | solution.py:920
  715.6 17.0 %join.23 = bf16[4,512,128]{2,1,0:T(8,128)(2,1)} custom-call(bf16[1,512,128]{2,1,0:T(8,128)(2,1)} %bitcast.101.refs_0_, bf16[1,512,128]{2,1,0:T(8,128)(2,1)} %bitcast.185, bf16[1,512,128]{2,1,0:T(8,128)(2,1)} %bitcast.184, bf16[1,512,128]{2,1,0:T(8,128)(2,1)} %bitcast.183), custom_call_target="tpu_custom_call" | custom-call | bytes 1048576 | tf_op jit(solution)/shard_map/join/pallas_call | solution.py:700
  732.6 17.0 %join.22 = bf16[4,512,128]{2,1,0:T(8,128)(2,1)} custom-call(bf16[1,512,128]{2,1,0:T(8,128)(2,1)} %bitcast.189, bf16[1,512,128]{2,1,0:T(8,128)(2,1)} %bitcast.188, bf16[1,512,128]{2,1,0:T(8,128)(2,1)} %bitcast.187, bf16[1,512,128]{2,1,0:T(8,128)(2,1)} %bitcast.186), custom_call_target="tpu_custom_call" | custom-call | bytes 1048576 | tf_op jit(solution)/shard_map/join/pallas_call | solution.py:700
  749.7 17.0 %join.21 = bf16[4,512,128]{2,1,0:T(8,128)(2,1)} custom-call(bf16[1,512,128]{2,1,0:T(8,128)(2,1)} %bitcast.195, bf16[1,512,128]{2,1,0:T(8,128)(2,1)} %bitcast.192, bf16[1,512,128]{2,1,0:T(8,128)(2,1)} %bitcast.191, bf16[1,512,128]{2,1,0:T(8,128)(2,1)} %bitcast.190), custom_call_target="tpu_custom_call" | custom-call | bytes 1048576 | tf_op jit(solution)/shard_map/join/pallas_call | solution.py:700
  771.6 17.0 %join.20 = bf16[4,512,128]{2,1,0:T(8,128)(2,1)} custom-call(bf16[1,512,128]{2,1,0:T(8,128)(2,1)} %bitcast.68.refs_0_, bf16[1,512,128]{2,1,0:T(8,128)(2,1)} %bitcast.70.refs_1_, bf16[1,512,128]{2,1,0:T(8,128)(2,1)} %bitcast.194, bf16[1,512,128]{2,1,0:T(8,128)(2,1)} %bitcast.193), custom_call_target="tpu_custom_call" | custom-call | bytes 1048576 | tf_op jit(solution)/shard_map/join/pallas_call | solution.py:700
  795.7 5.7 assemble.1
  (291 shorter events, 222.5 us)
Async XLA Ops:
  138.7 79.1 %collective-permute-start.16 = (bf16[2048,128]{1,0:T(8,128)(2,1)}, bf16[2048,128]{1,0:T(8,128)(2,1)S(1)}, u32[]{:S(2)}, u32[]{:S(2)}) collective-permute-start(bf16[2048,128]{1,0:T(8,128)(2,1)} %get-tuple-element.212), channel_id=1, source_target_pairs={{0,2},{1,3},{2,0},{3,1},{4,6},{5,7},{6,4},{7,5},{8,10},{9,11},{10,... | collective-permute-start | bytes 1572872 | tf_op jit(solution)/shard_map/ppermute | solution.py:920
  148.1 76.3 %collective-permute-start.17 = (bf16[2048,128]{1,0:T(8,128)(2,1)}, bf16[2048,128]{1,0:T(8,128)(2,1)}, u32[]{:S(2)}, u32[]{:S(2)}) collective-permute-start(bf16[2048,128]{1,0:T(8,128)(2,1)} %get-tuple-element.213), channel_id=1, source_target_pairs={{0,4},{1,5},{2,6},{3,7},{4,0},{5,1},{6,2},{7,3},{8,12},{9,13},{10,... | collective-permute-start | bytes 1572872 | tf_op jit(solution)/shard_map/ppermute | solution.py:920
  157.0 70.5 %collective-permute-start.18 = (bf16[2048,128]{1,0:T(8,128)(2,1)}, bf16[2048,128]{1,0:T(8,128)(2,1)}, u32[]{:S(2)}, u32[]{:S(2)}) collective-permute-start(bf16[2048,128]{1,0:T(8,128)(2,1)} %get-tuple-element.214), channel_id=1, source_target_pairs={{0,6},{1,7},{2,4},{3,5},{4,2},{5,3},{6,0},{7,1},{8,14},{9,15},{10,... | collective-permute-start | bytes 1572872 | tf_op jit(solution)/shard_map/ppermute | solution.py:920
  160.4 36.5 %collective-permute-start.21 = (bf16[512,128]{1,0:T(8,128)(2,1)}, bf16[512,128]{1,0:T(8,128)(2,1)S(1)}, u32[]{:S(2)}, u32[]{:S(2)}) collective-permute-start(bf16[512,128]{1,0:T(8,128)(2,1)} %collective-permute-done.10), channel_id=1, source_target_pairs={{0,4},{1,5},{2,6},{3,7},{4,0},{5,1},{6,2},{7,3},{8,14},{9,15},{10,... | collective-permute-start | bytes 393224 | tf_op jit(solution)/shard_map/ppermute | solution.py:920
  162.0 35.1 %collective-permute-start.22 = (bf16[512,128]{1,0:T(8,128)(2,1)}, bf16[512,128]{1,0:T(8,128)(2,1)S(1)}, u32[]{:S(2)}, u32[]{:S(2)}) collective-permute-start(bf16[512,128]{1,0:T(8,128)(2,1)} %collective-permute-done.11), channel_id=1, source_target_pairs={{0,6},{1,7},{2,4},{3,5},{4,2},{5,3},{6,0},{7,1},{8,12},{9,13},{10,... | collective-permute-start | bytes 393224 | tf_op jit(solution)/shard_map/ppermute | solution.py:920
  196.9 96.1 %collective-permute-start.13 = (bf16[8,512,128]{2,1,0:T(8,128)(2,1)}, bf16[8,512,128]{2,1,0:T(8,128)(2,1)}, u32[]{:S(2)}, u32[]{:S(2)}) collective-permute-start(bf16[8,512,128]{2,1,0:T(8,128)(2,1)} %join.13), channel_id=1, source_target_pairs={{0,16},{1,9},{2,18},{3,11},{4,20},{5,13},{6,22},{7,15},{8,24},{9,1... | collective-permute-start | bytes 3145736 | tf_op jit(solution)/shard_map/ppermute | solution.py:920
  197.0 32.5 %collective-permute-start.23 = (bf16[1024,128]{1,0:T(8,128)(2,1)}, bf16[1024,128]{1,0:T(8,128)(2,1)}, u32[]{:S(2)}, u32[]{:S(2)}) collective-permute-start(bf16[1024,128]{1,0:T(8,128)(2,1)} %get-tuple-element.219), channel_id=1, source_target_pairs={{0,0},{1,1},{2,10},{3,11},{4,20},{5,21},{6,30},{7,31},{8,8},{9,9},... | collective-permute-start | bytes 786440 | tf_op jit(solution)/shard_map/ppermute | solution.py:920
  240.5 43.5 %collective-permute-start.28 = (bf16[1024,128]{1,0:T(8,128)(2,1)}, bf16[1024,128]{1,0:T(8,128)(2,1)S(1)}, u32[]{:S(2)}, u32[]{:S(2)}) collective-permute-start(bf16[1024,128]{1,0:T(8,128)(2,1)} %collective-permute-done.23), channel_id=1, source_target_pairs={{0,0},{1,1},{2,2},{3,3},{4,4},{5,5},{6,6},{7,7},{8,10},{9,11},{10,... | collective-permute-start | bytes 786440 | tf_op jit(solution)/shard_map/ppermute | solution.py:920
  244.2 46.5 %collective-permute-start.29 = (bf16[1024,128]{1,0:T(8,128)(2,1)}, bf16[1024,128]{1,0:T(8,128)(2,1)S(1)}, u32[]{:S(2)}, u32[]{:S(2)}) collective-permute-start(bf16[1024,128]{1,0:T(8,128)(2,1)} %copy-done.42), channel_id=1, source_target_pairs={{0,2},{1,3},{2,0},{3,1},{4,6},{5,7},{6,4},{7,5},{8,8},{9,9},{10,10... | collective-permute-start | bytes 786440 | tf_op jit(solution)/shard_map/ppermute | solution.py:920
  246.1 44.6 %collective-permute-start.30 = (bf16[1024,128]{1,0:T(8,128)(2,1)}, bf16[1024,128]{1,0:T(8,128)(2,1)S(1)}, u32[]{:S(2)}, u32[]{:S(2)}) collective-permute-start(bf16[1024,128]{1,0:T(8,128)(2,1)} %collective-permute-done.25), channel_id=1, source_target_pairs={{0,4},{1,5},{2,6},{3,7},{4,0},{5,1},{6,2},{7,3},{8,14},{9,15},{10,... | collective-permute-start | bytes 786440 | tf_op jit(solution)/shard_map/ppermute | solution.py:920
  247.7 43.0 %collective-permute-start.31 = (bf16[1024,128]{1,0:T(8,128)(2,1)}, bf16[1024,128]{1,0:T(8,128)(2,1)S(1)}, u32[]{:S(2)}, u32[]{:S(2)}) collective-permute-start(bf16[1024,128]{1,0:T(8,128)(2,1)} %collective-permute-done.26), channel_id=1, source_target_pairs={{0,6},{1,7},{2,4},{3,5},{4,2},{5,3},{6,0},{7,1},{8,12},{9,13},{10,... | collective-permute-start | bytes 786440 | tf_op jit(solution)/shard_map/ppermute | solution.py:920
  284.0 89.3 %collective-permute-start.14 = (bf16[8,512,128]{2,1,0:T(8,128)(2,1)S(1)}, bf16[8,512,128]{2,1,0:T(8,128)(2,1)}, u32[]{:S(2)}, u32[]{:S(2)}) collective-permute-start(bf16[8,512,128]{2,1,0:T(8,128)(2,1)S(1)} %copy-done.7), channel_id=1, source_target_pairs={{0,1},{1,0},{2,3},{3,2},{4,5},{5,4},{6,7},{7,6},{8,9},{9,8},{10,11... | collective-permute-start | bytes 3145736 | tf_op jit(solution)/shard_map/ppermute | solution.py:920
  290.7 81.5 %collective-permute-start.33 = (bf16[8,512,128]{2,1,0:T(8,128)(2,1)}, bf16[8,512,128]{2,1,0:T(8,128)(2,1)}, u32[]{:S(2)}, u32[]{:S(2)}) collective-permute-start(bf16[8,512,128]{2,1,0:T(8,128)(2,1)} %join.15), channel_id=1, source_target_pairs={{0,1},{1,0},{2,3},{3,2},{4,5},{5,4},{6,7},{7,6},{8,9},{9,8},{10,11... | collective-permute-start | bytes 3145736 | tf_op jit(solution)/shard_map/ppermute | solution.py:920
  290.8 81.4 %collective-permute-start.32 = (bf16[8,512,128]{2,1,0:T(8,128)(2,1)}, bf16[8,512,128]{2,1,0:T(8,128)(2,1)}, u32[]{:S(2)}, u32[]{:S(2)}) collective-permute-start(bf16[8,512,128]{2,1,0:T(8,128)(2,1)} %join.15), channel_id=1, source_target_pairs={{0,16},{1,9},{2,18},{3,11},{4,20},{5,13},{6,22},{7,15},{8,24},{9,1... | collective-permute-start | bytes 3145736 | tf_op jit(solution)/shard_map/ppermute | solution.py:920
  293.0 80.8 %collective-permute-start.15 = (bf16[8,512,128]{2,1,0:T(8,128)(2,1)}, bf16[8,512,128]{2,1,0:T(8,128)(2,1)}, u32[]{:S(2)}, u32[]{:S(2)}) collective-permute-start(bf16[8,512,128]{2,1,0:T(8,128)(2,1)} %collective-permute-done.13), channel_id=1, source_target_pairs={{0,1},{1,0},{2,3},{3,2},{4,5},{5,4},{6,7},{7,6},{8,9},{9,8},{10,11... | collective-permute-start | bytes 3145736 | tf_op jit(solution)/shard_map/ppermute | solution.py:920
  337.8 51.4 %collective-permute-start.35 = (bf16[4,512,128]{2,1,0:T(8,128)(2,1)}, bf16[4,512,128]{2,1,0:T(8,128)(2,1)S(1)}, u32[]{:S(2)}, u32[]{:S(2)}) collective-permute-start(bf16[4,512,128]{2,1,0:T(8,128)(2,1)} %join.18.refs_0_), channel_id=1, source_target_pairs={{0,8},{1,17},{2,10},{3,19},{4,12},{5,21},{6,14},{7,23},{8,0},{9,25... | collective-permute-start | bytes 1572872 | tf_op jit(solution)/shard_map/ppermute | solution.py:920
  388.9 80.6 %collective-permute-start.43 = (bf16[2048,128]{1,0:T(8,128)(2,1)}, bf16[2048,128]{1,0:T(8,128)(2,1)}, u32[]{:S(2)}, u32[]{:S(2)}) collective-permute-start(bf16[2048,128]{1,0:T(8,128)(2,1)} %get-tuple-element.301), channel_id=1, source_target_pairs={{0,2},{1,3},{2,0},{3,1},{4,6},{5,7},{6,4},{7,5},{8,10},{9,11},{10,... | collective-permute-start | bytes 1572872 | tf_op jit(solution)/shard_map/ppermute | solution.py:920
  389.2 80.3 %collective-permute-start.44 = (bf16[2048,128]{1,0:T(8,128)(2,1)}, bf16[2048,128]{1,0:T(8,128)(2,1)}, u32[]{:S(2)}, u32[]{:S(2)}) collective-permute-start(bf16[2048,128]{1,0:T(8,128)(2,1)} %get-tuple-element.302), channel_id=1, source_target_pairs={{0,4},{1,5},{2,6},{3,7},{4,0},{5,1},{6,2},{7,3},{8,12},{9,13},{10,... | collective-permute-start | bytes 1572872 | tf_op jit(solution)/shard_map/ppermute | solution.py:920
  438.2 31.2 %collective-permute-start.45 = (bf16[2048,128]{1,0:T(8,128)(2,1)S(1)}, bf16[2048,128]{1,0:T(8,128)(2,1)}, u32[]{:S(2)}, u32[]{:S(2)}) collective-permute-start(bf16[2048,128]{1,0:T(8,128)(2,1)S(1)} %copy-done.40), channel_id=1, source_target_pairs={{0,6},{1,7},{2,4},{3,5},{4,2},{5,3},{6,0},{7,1},{8,14},{9,15},{10,... | collective-permute-start | bytes 1572872 | tf_op jit(solution)/shard_map/ppermute | solution.py:920
  561.1 30.1 %collective-permute-start.51 = (bf16[512,128]{1,0:T(8,128)(2,1)}, bf16[512,128]{1,0:T(8,128)(2,1)}, u32[]{:S(2)}, u32[]{:S(2)}) collective-permute-start(bf16[512,128]{1,0:T(8,128)(2,1)} %get-tuple-element.382), channel_id=1, source_target_pairs={{0,0},{1,1},{2,10},{3,11},{4,20},{5,21},{6,30},{7,31},{8,2},{9,3},... | collective-permute-start | bytes 393224 | tf_op jit(solution)/shard_map/ppermute | solution.py:920
  563.0 33.9 %collective-permute-start.58 = (bf16[16,2,2,128,128]{4,3,2,1,0:T(8,128)(2,1)}, bf16[16,2,2,128,128]{4,3,2,1,0:T(8,128)(2,1)S(1)}, u32[]{:S(2)}, u32[]{:S(2)}) collective-permute-start(bf16[16,2,2,128,128]{4,3,2,1,0:T(8,128)(2,1)} %get-tuple-element.332), channel_id=1, source_target_pairs={{0,1},{1,0},{2,3},{3,2},{4,5},{5,4},{6,7},{7,6},{8,9},{9,8},{10,11... | collective-permute-start | bytes 6291464 | tf_op jit(solution)/shard_map/ppermute | solution.py:920
  599.1 45.5 %collective-permute-start.82 = (bf16[512,128]{1,0:T(8,128)(2,1)S(1)}, bf16[512,128]{1,0:T(8,128)(2,1)S(1)}, u32[]{:S(2)}, u32[]{:S(2)}) collective-permute-start(bf16[512,128]{1,0:T(8,128)(2,1)S(1)} %get-tuple-element.367), channel_id=1, source_target_pairs={{0,6},{1,7},{2,12},{3,13},{4,18},{5,19},{6,24},{7,25},{8,4},{9,5},... | collective-permute-start | bytes 393224 | tf_op jit(solution)/shard_map/ppermute | solution.py:920
  601.9 62.0 %collective-permute-start.81 = (bf16[512,128]{1,0:T(8,128)(2,1)S(1)}, bf16[512,128]{1,0:T(8,128)(2,1)S(1)}, u32[]{:S(2)}, u32[]{:S(2)}) collective-permute-start(bf16[512,128]{1,0:T(8,128)(2,1)S(1)} %get-tuple-element.368), channel_id=1, source_target_pairs={{0,4},{1,5},{2,14},{3,15},{4,16},{5,17},{6,26},{7,27},{8,6},{9,7},... | collective-permute-start | bytes 393224 | tf_op jit(solution)/shard_map/ppermute | solution.py:920
  610.4 33.8 %collective-permute-start.71 = (bf16[4,512,128]{2,1,0:T(8,128)(2,1)S(1)}, bf16[4,512,128]{2,1,0:T(8,128)(2,1)S(1)}, u32[]{:S(2)}, u32[]{:S(2)}) collective-permute-start(bf16[4,512,128]{2,1,0:T(8,128)(2,1)S(1)} %bitcast.178), channel_id=1, source_target_pairs={{0,8},{1,9},{2,10},{3,11},{4,12},{5,13},{6,14},{7,15},{8,0},{9,1},... | collective-permute-start | bytes 1572872 | tf_op jit(solution)/shard_map/ppermute | solution.py:920
  660.9 127.8 %collective-permute-start.59 = (bf16[2048,128]{1,0:T(8,128)(2,1)}, bf16[2048,128]{1,0:T(8,128)(2,1)S(1)}, u32[]{:S(2)}, u32[]{:S(2)}) collective-permute-start(bf16[2048,128]{1,0:T(8,128)(2,1)} %get-tuple-element.334), channel_id=1, source_target_pairs={{0,2},{1,3},{2,0},{3,1},{4,6},{5,7},{6,4},{7,5},{8,10},{9,11},{10,... | collective-permute-start | bytes 1572872 | tf_op jit(solution)/shard_map/ppermute | solution.py:920
  660.9 128.3 %collective-permute-start.60 = (bf16[2048,128]{1,0:T(8,128)(2,1)}, bf16[2048,128]{1,0:T(8,128)(2,1)S(1)}, u32[]{:S(2)}, u32[]{:S(2)}) collective-permute-start(bf16[2048,128]{1,0:T(8,128)(2,1)} %get-tuple-element.335), channel_id=1, source_target_pairs={{0,4},{1,5},{2,6},{3,7},{4,0},{5,1},{6,2},{7,3},{8,12},{9,13},{10,... | collective-permute-start | bytes 1572872 | tf_op jit(solution)/shard_map/ppermute | solution.py:920
  663.9 32.5 %collective-permute-start.77 = (bf16[512,128]{1,0:T(8,128)(2,1)S(1)}, bf16[512,128]{1,0:T(8,128)(2,1)S(1)}, u32[]{:S(2)}, u32[]{:S(2)}) collective-permute-start(bf16[512,128]{1,0:T(8,128)(2,1)S(1)} %get-tuple-element.371), channel_id=1, source_target_pairs={{0,6},{1,7},{2,12},{3,13},{4,18},{5,19},{6,24},{7,25},{8,4},{9,5},... | collective-permute-start | bytes 393224 | tf_op jit(solution)/shard_map/ppermute | solution.py:920
  666.7 32.0 %collective-permute-start.76 = (bf16[512,128]{1,0:T(8,128)(2,1)S(1)}, bf16[512,128]{1,0:T(8,128)(2,1)S(1)}, u32[]{:S(2)}, u32[]{:S(2)}) collective-permute-start(bf16[512,128]{1,0:T(8,128)(2,1)S(1)} %get-tuple-element.372), channel_id=1, source_target_pairs={{0,4},{1,5},{2,14},{3,15},{4,16},{5,17},{6,26},{7,27},{8,6},{9,7},... | collective-permute-start | bytes 393224 | tf_op jit(solution)/shard_map/ppermute | solution.py:920
  668.9 33.4 %collective-permute-start.75 = (bf16[512,128]{1,0:T(8,128)(2,1)S(1)}, bf16[512,128]{1,0:T(8,128)(2,1)S(1)}, u32[]{:S(2)}, u32[]{:S(2)}) collective-permute-start(bf16[512,128]{1,0:T(8,128)(2,1)S(1)} %get-tuple-element.373), channel_id=1, source_target_pairs={{0,2},{1,3},{2,8},{3,9},{4,22},{5,23},{6,28},{7,29},{8,0},{9,1},{1... | collective-permute-start | bytes 393224 | tf_op jit(solution)/shard_map/ppermute | solution.py:920
  704.3 62.4 %collective-permute-start.67 = (bf16[512,128]{1,0:T(8,128)(2,1)S(1)}, bf16[512,128]{1,0:T(8,128)(2,1)}, u32[]{:S(2)}, u32[]{:S(2)}) collective-permute-start(bf16[512,128]{1,0:T(8,128)(2,1)S(1)} %get-tuple-element.377), channel_id=1, source_target_pairs={{0,2},{1,3},{2,8},{3,9},{4,22},{5,23},{6,28},{7,29},{8,0},{9,1},{1... | collective-permute-start | bytes 393224 | tf_op jit(solution)/shard_map/ppermute | solution.py:920
  709.2 62.3 %collective-permute-start.66 = (bf16[512,128]{1,0:T(8,128)(2,1)S(1)}, bf16[512,128]{1,0:T(8,128)(2,1)}, u32[]{:S(2)}, u32[]{:S(2)}) collective-permute-start(bf16[512,128]{1,0:T(8,128)(2,1)S(1)} %get-tuple-element.378), channel_id=1, source_target_pairs={{0,0},{1,1},{2,10},{3,11},{4,20},{5,21},{6,30},{7,31},{8,2},{9,3},... | collective-permute-start | bytes 393224 | tf_op jit(solution)/shard_map/ppermute | solution.py:920
  712.1 77.1 %collective-permute-start.61 = (bf16[2048,128]{1,0:T(8,128)(2,1)}, bf16[2048,128]{1,0:T(8,128)(2,1)S(1)}, u32[]{:S(2)}, u32[]{:S(2)}) collective-permute-start(bf16[2048,128]{1,0:T(8,128)(2,1)} %get-tuple-element.336), channel_id=1, source_target_pairs={{0,6},{1,7},{2,4},{3,5},{4,2},{5,3},{6,0},{7,1},{8,14},{9,15},{10,... | collective-permute-start | bytes 1572872 | tf_op jit(solution)/shard_map/ppermute | solution.py:920
  (96 other events, 2120.9 us)

commit v4 on v3

--- a/solution.py
+++ b/solution.py
@@ -318,16 +318,6 @@
         chunk_copy(source, target, sems, chunk).wait()
 
 
-def quarter_copies(pieces, whole, sems, me, outward=False):
-    rows = pieces[0].shape[0]
-    copies = []
-    for k, piece in enumerate(pieces):
-        part = whole.at[pl.ds(pl.multiple_of((me ^ k) * rows, rows), rows)]
-        ends = (part, piece) if outward else (piece, part)
-        copies.append(pltpu.make_async_copy(*ends, sems.at[k]))
-    return copies
-
-
 def factor_copies(parts, held, sems, side, outward=False):
     count = parts[0].shape[0]
     copies = []
@@ -368,11 +358,9 @@
     left_in = factor_copies(parts, w, w_sems, 0)
     right_in = factor_copies(parts, w, w_sems, 1)
     if first:
-        pieces = quarter_copies(sources, raw, in_sems, table_ref[2, 0])
-        for copy in pieces + left_in + right_in:
+        start_chunks(sources[0], raw, in_sems)
+        for copy in left_in + right_in:
             copy.start()
-        for copy in pieces:
-            copy.wait()
 
         def squares(block, total):
             rows = block_rows(block, size)
@@ -380,7 +368,12 @@
             h[rows, :] = part
             return total + fold_rows(part * part)
 
-        total = by_chunk(blocks, squares, jnp.zeros((8, slots), jnp.float32))
+        total = by_chunk(
+            blocks,
+            squares,
+            jnp.zeros((8, slots), jnp.float32),
+            lambda chunk: chunk_copy(sources[0], raw, in_sems, chunk).wait(),
+        )
     else:
         for copy in left_in:
             copy.start()
@@ -447,12 +440,9 @@
     sources, refs = refs[:inputs], refs[inputs:]
     slope_ref, z_ref, u_ref = sources[:3]
     parts, sources = sources[3 : 3 + PARTS], sources[3 + PARTS :]
-    count = len(refs) - 17
-    outs, refs = refs[:count], refs[count:]
-    own_grad, peer_grad = refs[:2]
-    g, slope, z, u, h, w, gw, mid, turned, top, goal = refs[2:13]
-    in_sems, w_sems, out_sems, gw_sems = refs[13:]
-    me = table_ref[2, 0]
+    out_ref, own_grad, peer_grad = refs[:3]
+    g, slope, z, u, h, w, gw, mid, turned, top, goal = refs[3:14]
+    in_sems, w_sems, out_sems, gw_sems = refs[14:]
     features, slots = g.shape
     size = w.shape[-1]
     chunk_blocks = w.shape[2]
@@ -461,12 +451,10 @@
 
     left_in = factor_copies(parts, w, w_sems, 0)
     right_in = factor_copies(parts, w, w_sems, 1)
-    g_ref, sources = sources[0], sources[1:]
+    g_ref, h_ref = sources[:2]
     if turning:
-        goals = quarter_copies(sources[1:], goal, in_sems.at[5], me)
         start_chunks(g_ref, top, in_sems.at[0])
-        for copy in goals:
-            copy.start()
+        start_chunks(sources[2], goal, in_sems.at[5])
     else:
         start_chunks(g_ref, g, in_sems.at[0])
     for copy in right_in:
@@ -476,12 +464,7 @@
     for copy in left_in:
         copy.start()
     start_chunks(u_ref, u, in_sems.at[3])
-    if last:
-        starts = quarter_copies(sources, h, in_sems.at[5], me)
-        for copy in starts:
-            copy.start()
-    else:
-        start_chunks(sources[0], h, in_sems.at[4])
+    start_chunks(h_ref, h, in_sems.at[4])
 
     if turning:
         zero = jnp.zeros((8, slots), jnp.float32)
@@ -498,9 +481,8 @@
 
         def arrive_top(chunk):
             chunk_copy(g_ref, top, in_sems.at[0], chunk).wait()
-
-        for copy in goals:
-            copy.wait()
+            chunk_copy(sources[2], goal, in_sems.at[5], chunk).wait()
+
         totals = by_chunk(blocks, sums, (zero, zero, zero), arrive_top)
         squares, gained, crossed = [jnp.sum(total, axis=0, keepdims=True) for total in totals]
         end_scale = lax.rsqrt(squares / features + EPSILON)
@@ -541,14 +523,9 @@
         copy.wait()
     scale = scale_ref[0:1, :]
 
-    if last:
-        for copy in starts:
-            copy.wait()
-
     def arrive_left(chunk):
         chunk_copy(u_ref, u, in_sems.at[3], chunk).wait()
-        if not last:
-            chunk_copy(sources[0], h, in_sems.at[4], chunk).wait()
+        chunk_copy(h_ref, h, in_sems.at[4], chunk).wait()
 
     def left(block, total):
         rows = block_rows(block, size)
@@ -581,16 +558,9 @@
             g[rows, :] = ended
         return carry
 
-    if last:
-        by_chunk(blocks, finish, 0)
-        ends = quarter_copies(outs, u, out_sems, me, outward=True)
-        for copy in ends:
-            copy.start()
-        for copy in ends:
-            copy.wait()
-    else:
-        by_chunk(blocks, finish, 0, None, lambda chunk: chunk_copy(g, outs[0], out_sems, chunk).start())
-        wait_chunks(g, outs[0], out_sems)
+    ended = u if last else g
+    by_chunk(blocks, finish, 0, None, lambda chunk: chunk_copy(ended, out_ref, out_sems, chunk).start())
+    wait_chunks(ended, out_ref, out_sems)
     for copy in right_out + left_out:
         copy.wait()
 
@@ -605,9 +575,9 @@
 
 
 def run_forward(table, gain, sums, residual, weights):
-    first = len(residual) > 1
-    whole = (residual[0].shape[0] * len(residual), residual[0].shape[1])
-    sources = (*weights, *residual)
+    first = residual.dtype == jnp.bfloat16
+    whole = residual.shape
+    sources = (*weights, residual)
     held = (PARTS * weights[0].shape[0],) + weights[0].shape[1:]
     out_shape = (
         shape_of(whole, jnp.float32),
@@ -644,14 +614,10 @@
 
 def run_backward(table, gain, end_gain, scale, kept, weights, sources, turning, last):
     whole = kept[0].shape
-    width = len(sources) - 1
     sources = (*kept, *weights, *sources)
     held = (PARTS * weights[0].shape[0],) + weights[0].shape[1:]
     half = (held[0] // 2,) + held[1:]
-    ends = [shape_of(whole, jnp.float32)]
-    if last:
-        ends = [shape_of((whole[0] // width, whole[1]), jnp.bfloat16)] * width
-    out_shape = ends + [shape_of(half, jnp.bfloat16)] * 2
+    out_shape = [shape_of(whole, jnp.bfloat16 if last else jnp.float32)] + [shape_of(half, jnp.bfloat16)] * 2
     return pl.pallas_call(
         lambda *refs: backward_kernel(turning, last, len(sources), *refs),
         in_specs=[SMEM] + [INSIDE] * 3 + [OUTSIDE] * len(sources),
@@ -700,9 +666,10 @@
     return pl.pallas_call(
         lambda *refs: copies_kernel(plan, len(extra) + len(inputs), len(out_shape), *refs),
         in_specs=[SMEM] * len(extra) + [OUTSIDE] * len(inputs),
-        out_specs=[OUTSIDE] * len(out_shape),
+        out_specs=[INSIDE] * len(out_shape),
         out_shape=out_shape,
         scratch_shapes=[pltpu.SemaphoreType.DMA((most,))],
+        compiler_params=pltpu.CompilerParams(vmem_limit_bytes=VMEM_LIMIT),
         cost_estimate=pl.CostEstimate(flops=0, bytes_accessed=4 * size, transcendentals=0),
         name=name,
     )(*extra, *inputs)
@@ -758,59 +725,55 @@
     return jnp.where(rank == at, named, 0.0).astype(jnp.bfloat16)
 
 
-def pick_kernel(place_ref, pairs_ref, values_ref, *out_refs):
-    width = len(out_refs)
-    features, slots = out_refs[0].shape
+def pick_kernel(pairs_ref, values_ref, out_ref):
+    width, features, slots = out_ref.shape
     pairs = pairs_ref[...]
-    chosen = [choice(pairs, place_ref[1] ^ k, slots) for k in range(width)]
+    chosen = [choice(pairs, critic, slots) for critic in range(width)]
     step = 512
     for start in range(0, features, step):
         part = values_ref[:, pl.ds(start, step)]
         for k in range(width):
-            out_refs[k][pl.ds(start, step), :] = inner_dot(part, chosen[k], 0, 0).astype(jnp.bfloat16)
-
-
-def run_pick(place, pairs, values, width, slots):
+            out_ref[k, pl.ds(start, step), :] = inner_dot(part, chosen[k], 0, 0).astype(jnp.bfloat16)
+
+
+def run_pick(pairs, values, width, slots):
     rows, features = values.shape
     return pl.pallas_call(
         pick_kernel,
-        in_specs=[SMEM] + [INSIDE] * 2,
-        out_specs=[INSIDE] * width,
-        out_shape=[shape_of((features, slots), jnp.bfloat16)] * width,
+        in_specs=[INSIDE] * 2,
+        out_specs=INSIDE,
+        out_shape=shape_of((width, features, slots), jnp.bfloat16),
         compiler_params=pltpu.CompilerParams(vmem_limit_bytes=VMEM_LIMIT),
         cost_estimate=pl.CostEstimate(
             flops=2 * rows * features * slots * width, bytes_accessed=8 * rows * features, transcendentals=0
         ),
         name="pick",
-    )(place, pairs, values)
-
-
-def combine_kernel(place_ref, pairs_ref, *refs):
-    came, out_ref = refs[:-1], refs[-1]
-    width = len(came)
-    features, slots = came[0].shape
+    )(pairs, values)
+
+
+def combine_kernel(pairs_ref, came_ref, out_ref):
+    width, features, slots = came_ref.shape
     pairs = pairs_ref[...]
-    chosen = [choice(pairs, place_ref[1] ^ k, slots) for k in range(width)]
+    chosen = [choice(pairs, critic, slots) for critic in range(width)]
     step = 512
     for start in range(0, features, step):
-        total = sum(inner_dot(chosen[k], came[k][pl.ds(start, step), :], 1, 1) for k in range(width))
+        total = sum(inner_dot(chosen[k], came_ref[k, pl.ds(start, step), :], 1, 1) for k in range(width))
         out_ref[:, pl.ds(start, step)] = (0.5 * total).astype(jnp.bfloat16)
 
 
-def run_combine(place, pairs, came):
+def run_combine(pairs, came):
     rows = pairs.shape[0]
-    features = came[0].shape[0]
     return pl.pallas_call(
         combine_kernel,
-        in_specs=[SMEM] + [INSIDE] * (1 + len(came)),
+        in_specs=[INSIDE] * 2,
         out_specs=INSIDE,
-        out_shape=shape_of((rows, features), jnp.bfloat16),
+        out_shape=shape_of((rows, came.shape[1]), jnp.bfloat16),
         compiler_params=pltpu.CompilerParams(vmem_limit_bytes=VMEM_LIMIT),
         cost_estimate=pl.CostEstimate(
-            flops=2 * rows * came[0].size * len(came), bytes_accessed=4 * came[0].size * len(came), transcendentals=0
+            flops=2 * rows * came.size, bytes_accessed=4 * came.size, transcendentals=0
         ),
         name="combine",
-    )(place, pairs, *came)
+    )(pairs, came)
 
 
 FORWARD_COST = 15_000_000_000
@@ -948,42 +911,40 @@
         [
             ((part * width + rank) * width + piece) * chunk + inside % chunk,
             ((part * width + distance) * width + piece) * chunk + inside % chunk,
-            jnp.broadcast_to(tensor, block.shape),
         ]
     ).astype(jnp.int32)
 
-    patch_sent = run_pick(place, critic_pairs, patches, width, wide)
-    patch_sent, factors = tie((patch_sent, (left_factors[0], right_factors[0])))
-    groups = [(0,), (1,), tuple(range(2, layer_count))]
+    def to_planes(value):
+        return lax.all_to_all(value, "tensor", split_axis=0, concat_axis=0, tiled=True)
+
+    patch_sent = run_pick(critic_pairs, patches, width, wide)
+    factors = (left_factors[0], right_factors[0])
+    groups = [tuple(range(0, 2)), tuple(range(2, layer_count))]
     gain_rows = norm_gains[0].reshape(-1, size)
     pieces = factor_pieces(place, *factors, gain_rows, groups, chunk)
 
-    patch_came = send(patch_sent, "planes")
+    patch_came = to_planes(patch_sent).reshape(-1, wide)
     near = [move_all(pieces[0], "spread")]
     near[0], pieces[1] = tie((near[0], pieces[1]))
+    front = move_all(near[0], "lift")
     near.append(move_all(pieces[1], "spread"))
-    front = move_all(near[0], "lift")
-    near[1], pieces[2] = tie((near[1], pieces[2]))
-    near.append(move_all(pieces[2], "spread"))
-    front, near[1] = tie((front, near[1]))
-    second = move_all(near[1], "lift")
-    gains = jnp.stack([value[layer_rows:] for value in front])[jnp.arange(width) ^ section ^ tensor]
+
+    def lowest_of(values, at):
+        at = at * layer_rows
+        return joined([value[at : at + layer_rows].reshape(1, layer_rows, size) for value in values])
+
+    gains = jnp.stack([value[2 * layer_rows :] for value in front])[jnp.arange(width) ^ section ^ tensor]
     gains = gains.reshape(width, layer_count + 1, local_blocks, size).transpose(1, 3, 0, 2)
     gains = gains.reshape(layer_count + 1, size, blocks)
-    lowest = [joined([value[:layer_rows].reshape(1, layer_rows, size) for value in front])]
-    pair = gather_one(lowest[0])
-    gathered = gather_two(pair)
-    weights = [as_weights(gather_three(*gathered))]
-    lowest.append(joined([value.reshape(1, layer_rows, size) for value in second]))
-    pair = gather_one(lowest[1])
-    patch_came, second, near[2] = tie((patch_came, second, near[2]))
-    later = move_all(near[2], "lift")
-    pairs = [None, pair] + [None] * (layer_count - 2)
+    lowest = [lowest_of(front, 0), lowest_of(front, 1)]
+    pairs = [gather_one(lowest[0]), gather_one(lowest[1])] + [None] * (layer_count - 2)
+    weights = [as_weights(gather_three(*gather_two(pairs[0])))]
+    patch_came, near[1] = tie((patch_came, near[1]))
+    later = move_all(near[1], "lift")
     pairs[1], later, teacher = tie((pairs[1], later, teacher))
     for layer in range(2, layer_count):
-        at = (layer - 2) * layer_rows
-        lowest.append(joined([value[at : at + layer_rows].reshape(1, layer_rows, size) for value in later]))
-    target_sent = run_pick(place, critic_pairs, teacher, width, wide)
+        lowest.append(lowest_of(later, layer - 2))
+    target_sent = run_pick(critic_pairs, teacher, width, wide)
 
     residual = patch_came
     sums = jnp.zeros((8, wide), jnp.float32)
@@ -1005,7 +966,7 @@
         )
         stored.append(((slope, z, u), scale, residual))
         following, ahead = tie((following, ahead))
-        residual = (following,)
+        residual = following
         if layer + 1 < layer_count:
             weights.append(as_weights(ahead["weights"]))
         if layer + 2 < layer_count:
@@ -1014,7 +975,7 @@
             pairs[layer + 3] = joined(list(ahead["one"]))
         if layer == 0:
             target_sent, sums = tie((target_sent, sums))
-            target = send(target_sent, "planes")
+            target = to_planes(target_sent).reshape(-1, wide)
 
     def core_sum(mine, other):
         return (mine, move(other, routes["cores"]))
@@ -1036,30 +997,28 @@
         lambda state: homeward(added(*state)),
         both_halves,
     )
-    gradient = residual[0]
+    gradient = residual
     underway = []
     for layer in range(layer_count - 1, -1, -1):
         turning = layer == layer_count - 1
         last = layer == 0
         kept, scale, inputs = stored[layer]
-        sources = (gradient, *inputs, *target) if turning else (gradient, *inputs)
+        sources = (gradient, inputs, target) if turning else (gradient, inputs)
         underway = [(at + 1, steps[at](state)) for at, state in underway]
-        *gradient, mine, other = run_backward(
+        gradient, mine, other = run_backward(
             table, gains[layer], gains[layer_count], scale, kept, weights[layer], sources, turning, last
         )
         gradient, mine, other, states = tie((gradient, mine, other, [state for _, state in underway]))
         underway = [(at, state) for (at, _), state in zip(underway, states)]
         underway.append((0, (mine, other)))
-        if not last:
-            gradient = gradient[0]
-
-    returned = send(gradient, "planes")
+
+    returned = to_planes(gradient.reshape(width, feat_local, wide))
     homes_of = []
     for at, state in underway:
         for step in steps[at:]:
             state = step(state)
         homes_of.append(state)
-    d_patches = run_combine(place, critic_pairs, returned)
+    d_patches = run_combine(critic_pairs, returned)
     grad_factor = 1.0 / math.sqrt(2 * tok_rows * width * replicas)
     parts = [part.reshape(width, 2, chunk, size, size) for pair in homes_of[::-1] for part in pair]
     grad_left, grad_right = run_assemble(place, parts, layer_count, grad_factor)

time: 816 us -> 518 us (0.63); the launches traced: 802 us -> 512 us
  Pallas kernels: 492 us -> 185 us
  waiting for transfers between devices: 98.7 us -> 108 us
    pallas_call x13, Pallas kernels: 336 us -> 28.3 us  [run_copies(): pl.pallas_call(lambda *refs: copies_kernel(plan, len(extra) + len(inputs)...]
    all_to_all x0 -> x3, starting transfers between devices: none -> 12.6 us  [to_planes(): lax.all_to_all(value, 'tensor', split_axis=0, concat_axis=0, tiled=True)]
    ppermute x85 -> x68, starting transfers between devices: 176 us -> 165 us  [move(): return lax.ppermute(value, AXES, route)]
    ppermute x85 -> x68, waiting for transfers between devices: 98.7 us -> 105 us  [move(): return lax.ppermute(value, AXES, route)]
  transfers between devices with their start and end apart: 85 -> 71, of which waited for: 19 -> 16; matrix products, arithmetic and copies ran while one was open for 3% -> 6% of each run, Pallas kernels for 46% -> 29%
where the time goes in v4:
time: 518 us; the launch traced here: 512 us
  Pallas kernels  185 us (36%)
  starting transfers between devices  178 us (34%)
  waiting for transfers between devices  108 us (21%)
  local copies, waits for them, and re-layouts  26.4 us (5%)
  other arithmetic  13.5 us (3%)
    ppermute x68, starting transfers between devices, move(): return lax.ppermute(value, AXES, route)  165 us
    ppermute x68, waiting for transfers between devices, move(): return lax.ppermute(value, AXES, route)  105 us
    pallas_call x4, Pallas kernels, run_backward(): pl.pallas_call(lambda *refs: backward_kernel(turning, last, len(sources),...  84.4 us
    pallas_call x4, Pallas kernels, run_forward(): pl.pallas_call(lambda *refs: forward_kernel(first, len(sources), *refs),...  54 us
    pallas_call x13, Pallas kernels, run_copies(): pl.pallas_call(lambda *refs: copies_kernel(plan, len(extra) + len(inputs)...  28.3 us
    all_to_all x3, starting transfers between devices, to_planes(): lax.all_to_all(value, 'tensor', split_axis=0, concat_axis=0, tiled=True)  12.6 us
    convert_element_type x8, other arithmetic, added(): sum((part.astype(jnp.float32) for part in parts)).astype(jnp.bfloat16)  12.2 us
  transfers between devices with their start and end apart: 71, of which 16 were waited for; matrix products, arithmetic and copies ran while one was open for 6% of the time, Pallas kernels for 29%

profile of v4, /device:TPU:5, one launch (start us, length us, event | category | flops | bytes accessed | tf_op | source)
XLA Modules:
  0.0 512.0 jit_solution(2014800875857684711)
XLA Ops:
  2.1 4.1 pick.2
  6.2 4.7 all-to-all-start
  12.2 4.1 pieces.1
  27.3 8.9 %collective-permute-done.2 = bf16[1104,128]{1,0:T(8,128)(2,1)S(1)} collective-permute-done((bf16[1104,128]{1,0:T(8,128)(2,1)}, bf16[1104,128]{1,0:T(8,128)(2,1)S(1)}, u32[]{:S(2)}, u32[]{:S(2)}) %collective-permute-start.2) | collective-permute-done | bytes 282656 | tf_op jit(solution)/shard_map/ppermute | solution.py:883
  39.3 7.2 %collective-permute-start.5 = (bf16[1104,128]{1,0:T(8,128)(2,1)S(1)}, bf16[1104,128]{1,0:T(8,128)(2,1)S(1)}, u32[]{:S(2)}, u32[]{:S(2)}) collective-permute-start(bf16[1104,128]{1,0:T(8,128)(2,1)S(1)} %collective-permute-done.1), channel_id=1, source_target_pairs={{0,2},{1,3},{2,0},{3,1},{4,6},{5,7},{6,4},{7,5},{8,8},{9,9},{10,10... | collective-permute-start | bytes 847880 | tf_op jit(solution)/shard_map/ppermute | solution.py:883
  49.1 27.8 %collective-permute-done.4 = bf16[1104,128]{1,0:T(8,128)(2,1)S(1)} collective-permute-done((bf16[1104,128]{1,0:T(8,128)(2,1)S(1)}, bf16[1104,128]{1,0:T(8,128)(2,1)S(1)}, u32[]{:S(2)}, u32[]{:S(2)}) %collective-permute-start.4) | collective-permute-done | bytes 282656 | tf_op jit(solution)/shard_map/ppermute | solution.py:883
  85.4 4.6 collective-permute-done.8.refs_1_
  93.1 6.9 %collective-permute-start.9 = (bf16[8,512,128]{2,1,0:T(8,128)(2,1)}, bf16[8,512,128]{2,1,0:T(8,128)(2,1)}, u32[]{:S(2)}, u32[]{:S(2)}) collective-permute-start(bf16[8,512,128]{2,1,0:T(8,128)(2,1)} %join.13), channel_id=1, source_target_pairs={{0,16},{1,9},{2,18},{3,11},{4,20},{5,13},{6,22},{7,15},{8,24},{9,1... | collective-permute-start | bytes 3145736 | tf_op jit(solution)/shard_map/ppermute | solution.py:883
  112.6 11.5 %collective-permute-done.13 = bf16[1024,128]{1,0:T(8,128)(2,1)S(1)} collective-permute-done((bf16[1024,128]{1,0:T(8,128)(2,1)}, bf16[1024,128]{1,0:T(8,128)(2,1)S(1)}, u32[]{:S(2)}, u32[]{:S(2)}) %collective-permute-start.13) | collective-permute-done | bytes 262176 | tf_op jit(solution)/shard_map/ppermute | solution.py:883
  141.0 5.2 %collective-permute-start.10 = (bf16[8,512,128]{2,1,0:T(8,128)(2,1)}, bf16[8,512,128]{2,1,0:T(8,128)(2,1)}, u32[]{:S(2)}, u32[]{:S(2)}) collective-permute-start(bf16[8,512,128]{2,1,0:T(8,128)(2,1)} %join.13), channel_id=1, source_target_pairs={{0,1},{1,0},{2,3},{3,2},{4,5},{5,4},{6,7},{7,6},{8,9},{9,8},{10,11... | collective-permute-start | bytes 3145736 | tf_op jit(solution)/shard_map/ppermute | solution.py:883
  146.2 5.5 %collective-permute-start.11 = (bf16[8,512,128]{2,1,0:T(8,128)(2,1)}, bf16[8,512,128]{2,1,0:T(8,128)(2,1)}, u32[]{:S(2)}, u32[]{:S(2)}) collective-permute-start(bf16[8,512,128]{2,1,0:T(8,128)(2,1)} %collective-permute-done.9), channel_id=1, source_target_pairs={{0,1},{1,0},{2,3},{3,2},{4,5},{5,4},{6,7},{7,6},{8,9},{9,8},{10,11... | collective-permute-start | bytes 3145736 | tf_op jit(solution)/shard_map/ppermute | solution.py:883
  162.3 9.8 %collective-permute-start.23 = (bf16[4,512,128]{2,1,0:T(8,128)(2,1)}, bf16[4,512,128]{2,1,0:T(8,128)(2,1)S(1)}, u32[]{:S(2)}, u32[]{:S(2)}) collective-permute-start(bf16[4,512,128]{2,1,0:T(8,128)(2,1)} %join.16.refs_0_), channel_id=1, source_target_pairs={{0,8},{1,17},{2,10},{3,19},{4,12},{5,21},{6,14},{7,23},{8,0},{9,25... | collective-permute-start | bytes 1572872 | tf_op jit(solution)/shard_map/ppermute | solution.py:883
  178.3 4.2 pick.3
  190.3 14.0 %forward_layer.4 = (f32[8192,128]{1,0:T(8,128)}, bf16[8192,128]{1,0:T(8,128)(2,1)}, bf16[8192,128]{1,0:T(8,128)(2,1)}, bf16[8192,128]{1,0:T(8,128)(2,1)}, f32[8,128]{1,0:T(8,128)}, /*index=5*/f32[8,128]{1,0:T(8,128)}) custom-call(s32[2,64]{1,0:T(2,128)} %pad_add_fusion.refs_0_, bf16[128,64]{1,0:T(8,128)(2,1)} %copy.27.refs_1_, ...), custom_call_target="tpu_custom_call" | custom-call | flops 15000000512 | bytes 20971520 | tf_op jit(solution)/shard_map/forward_layer/pallas_call | solution.py:590
  212.2 13.3 %forward_layer.5 = (f32[8192,128]{1,0:T(8,128)}, bf16[8192,128]{1,0:T(8,128)(2,1)}, bf16[8192,128]{1,0:T(8,128)(2,1)}, bf16[8192,128]{1,0:T(8,128)(2,1)}, f32[8,128]{1,0:T(8,128)}, /*index=5*/f32[8,128]{1,0:T(8,128)}) custom-call(s32[2,64]{1,0:T(2,128)} %pad_add_fusion.refs_0_, bf16[128,64]{1,0:T(8,128)(2,1)} %copy.25.refs_1_, ...), custom_call_target="tpu_custom_call" | custom-call | flops 15000000512 | bytes 20971520 | tf_op jit(solution)/shard_map/forward_layer/pallas_call | solution.py:590
  226.8 13.3 %forward_layer.6 = (f32[8192,128]{1,0:T(8,128)}, bf16[8192,128]{1,0:T(8,128)(2,1)}, bf16[8192,128]{1,0:T(8,128)(2,1)}, bf16[8192,128]{1,0:T(8,128)(2,1)}, f32[8,128]{1,0:T(8,128)}, /*index=5*/f32[8,128]{1,0:T(8,128)}) custom-call(s32[2,64]{1,0:T(2,128)} %pad_add_fusion.refs_0_, bf16[128,64]{1,0:T(8,128)(2,1)} %copy.23.refs_1_, ...), custom_call_target="tpu_custom_call" | custom-call | flops 15000000512 | bytes 20971520 | tf_op jit(solution)/shard_map/forward_layer/pallas_call | solution.py:590
  240.2 13.4 %forward_layer.7 = (f32[8192,128]{1,0:T(8,128)}, bf16[8192,128]{1,0:T(8,128)(2,1)}, bf16[8192,128]{1,0:T(8,128)(2,1)}, bf16[8192,128]{1,0:T(8,128)(2,1)}, f32[8,128]{1,0:T(8,128)}, /*index=5*/f32[8,128]{1,0:T(8,128)}) custom-call(s32[2,64]{1,0:T(2,128)} %pad_add_fusion.refs_0_, bf16[128,64]{1,0:T(8,128)(2,1)} %copy.21.refs_1_, ...), custom_call_target="tpu_custom_call" | custom-call | flops 15000000512 | bytes 20971520 | tf_op jit(solution)/shard_map/forward_layer/pallas_call | solution.py:590
  257.6 28.3 %backward_layer.4 = (f32[8192,128]{1,0:T(8,128)}, bf16[16,2,2,128,128]{4,3,2,1,0:T(8,128)(2,1)}, bf16[16,2,2,128,128]{4,3,2,1,0:T(8,128)(2,1)}) custom-call(s32[2,64]{1,0:T(2,128)} %pad_add_fusion.refs_0_, bf16[128,64]{1,0:T(8,128)(2,1)} %copy.21.refs_1_, bf16[128,64]{1,0:T(8,128)(2,1)} %copy.28.refs_2_, f32[8,128]{1,0:T(8,128)} %get-tuple-element.200.refs_3_, ...), custom_call_target="tpu_custom_call" | custom-call | flops 17999998976 | bytes 31457280 | tf_op jit(solution)/shard_map/backward_layer/pallas_call | solution.py:621
  286.8 19.0 %backward_layer.5 = (f32[8192,128]{1,0:T(8,128)}, bf16[16,2,2,128,128]{4,3,2,1,0:T(8,128)(2,1)}, bf16[16,2,2,128,128]{4,3,2,1,0:T(8,128)(2,1)}) custom-call(s32[2,64]{1,0:T(2,128)} %pad_add_fusion.refs_0_, bf16[128,64]{1,0:T(8,128)(2,1)} %copy.23.refs_1_, bf16[128,64]{1,0:T(8,128)(2,1)} %copy.28.refs_2_, f32[8,128]{1,0:T(8,128)} %get-tuple-element.186.refs_3_, ...), custom_call_target="tpu_custom_call" | custom-call | flops 17999998976 | bytes 31457280 | tf_op jit(solution)/shard_map/backward_layer/pallas_call | solution.py:621
  314.0 19.1 %backward_layer.6 = (f32[8192,128]{1,0:T(8,128)}, bf16[16,2,2,128,128]{4,3,2,1,0:T(8,128)(2,1)}, bf16[16,2,2,128,128]{4,3,2,1,0:T(8,128)(2,1)}) custom-call(s32[2,64]{1,0:T(2,128)} %pad_add_fusion.refs_0_, bf16[128,64]{1,0:T(8,128)(2,1)} %copy.25.refs_1_, bf16[128,64]{1,0:T(8,128)(2,1)} %copy.28.refs_2_, f32[8,128]{1,0:T(8,128)} %get-tuple-element.170.refs_3_, ...), custom_call_target="tpu_custom_call" | custom-call | flops 17999998976 | bytes 31457280 | tf_op jit(solution)/shard_map/backward_layer/pallas_call | solution.py:621
  343.3 5.1 collective-permute-start.38
  354.0 4.1 collective-permute-start.43
  358.4 18.1 %backward_layer.7 = (bf16[8192,128]{1,0:T(8,128)(2,1)}, bf16[16,2,2,128,128]{4,3,2,1,0:T(8,128)(2,1)}, bf16[16,2,2,128,128]{4,3,2,1,0:T(8,128)(2,1)}) custom-call(s32[2,64]{1,0:T(2,128)} %pad_add_fusion.refs_0_, bf16[128,64]{1,0:T(8,128)(2,1)} %copy.27.refs_1_, bf16[128,64]{1,0:T(8,128)(2,1)} %copy.28.refs_2_, f32[8,128]{1,0:T(8,128)} %get-tuple-element.153.refs_3_, ...), custom_call_target="tpu_custom_call" | custom-call | flops 17999998976 | bytes 31457280 | tf_op jit(solution)/shard_map/backward_layer/pallas_call | solution.py:621
  398.0 4.3 collective-permute-start.56
  405.3 12.5 %collective-permute-done.56 = bf16[4,512,128]{2,1,0:T(8,128)(2,1)S(1)} collective-permute-done((bf16[4,512,128]{2,1,0:T(8,128)(2,1)S(1)}, bf16[4,512,128]{2,1,0:T(8,128)(2,1)S(1)}, u32[]{:S(2)}, u32[]{:S(2)}) %collective-permute-start.56) | collective-permute-done | bytes 524320 | tf_op jit(solution)/shard_map/ppermute | solution.py:883
  421.2 5.6 %collective-permute-done.55 = bf16[4,512,128]{2,1,0:T(8,128)(2,1)S(1)} collective-permute-done((bf16[4,512,128]{2,1,0:T(8,128)(2,1)S(1)}, bf16[4,512,128]{2,1,0:T(8,128)(2,1)S(1)}, u32[]{:S(2)}, u32[]{:S(2)}) %collective-permute-start.55) | collective-permute-done | bytes 524320 | tf_op jit(solution)/shard_map/ppermute | solution.py:883
  432.8 7.5 %collective-permute-done.48 = bf16[4,512,128]{2,1,0:T(8,128)(2,1)S(1)} collective-permute-done((bf16[4,512,128]{2,1,0:T(8,128)(2,1)S(1)}, bf16[4,512,128]{2,1,0:T(8,128)(2,1)S(1)}, u32[]{:S(2)}, u32[]{:S(2)}) %collective-permute-start.48) | collective-permute-done | bytes 524320 | tf_op jit(solution)/shard_map/ppermute | solution.py:883
  442.3 11.7 %collective-permute-done.47 = bf16[4,512,128]{2,1,0:T(8,128)(2,1)S(1)} collective-permute-done((bf16[4,512,128]{2,1,0:T(8,128)(2,1)S(1)}, bf16[4,512,128]{2,1,0:T(8,128)(2,1)S(1)}, u32[]{:S(2)}, u32[]{:S(2)}) %collective-permute-start.47) | collective-permute-done | bytes 524320 | tf_op jit(solution)/shard_map/ppermute | solution.py:883
  456.0 5.0 collective-permute-start.60
  463.2 5.1 collective-permute-start.58
  478.1 6.7 %collective-permute-start.50 = (bf16[512,128]{1,0:T(8,128)(2,1)S(1)}, bf16[512,128]{1,0:T(8,128)(2,1)}, u32[]{:S(2)}, u32[]{:S(2)}) collective-permute-start(bf16[512,128]{1,0:T(8,128)(2,1)S(1)} %get-tuple-element.273), channel_id=1, source_target_pairs={{0,2},{1,3},{2,8},{3,9},{4,22},{5,23},{6,28},{7,29},{8,0},{9,1},{1... | collective-permute-start | bytes 393224 | tf_op jit(solution)/shard_map/ppermute | solution.py:883
  506.2 5.7 %assemble.1 = (f32[4,16,128,128]{3,2,1,0:T(8,128)}, f32[4,16,128,128]{3,2,1,0:T(8,128)}) custom-call(s32[3]{0:T(128)} %pad_add_fusion.1.refs_0_, bf16[4,2,2,128,128]{4,3,2,1,0:T(8,128)(2,1)} %bitcast.168, bf16[4,2,2,128,128]{4,3,2,1,0:T(8,128)(2,1)} %bitcast.79.refs_2_, bf16[4,2,2,128,128]{4,3,2,1,0:T(8,128)(2,1)} %bitcast.167, ...), custom_call_target="tpu_custom_call" | custom-call | bytes 12582912 | tf_op jit(solution)/shard_map/assemble/pallas_call | solution.py:817
  (246 shorter events, 193.9 us)
Async XLA Ops:
  6.2 122.5 %all-to-all-start = ((bf16[4,2048,128]{2,1,0:T(8,128)(2,1)}), bf16[4,2048,128]{2,1,0:T(8,128)(2,1)S(1)}, u32[]{:S(2)}, u32[]{:S(2)}) async-start(bf16[4,2048,128]{2,1,0:T(8,128)(2,1)} %pick.2), calls=%async_computation | async-start | bytes 4194304 | tf_op jit(solution)/shard_map/all_to_all | solution.py:918
  36.2 40.7 %collective-permute-start.4 = (bf16[1104,128]{1,0:T(8,128)(2,1)S(1)}, bf16[1104,128]{1,0:T(8,128)(2,1)S(1)}, u32[]{:S(2)}, u32[]{:S(2)}) collective-permute-start(bf16[1104,128]{1,0:T(8,128)(2,1)S(1)} %collective-permute-done), channel_id=1, source_target_pairs={{0,0},{1,1},{2,2},{3,3},{4,4},{5,5},{6,6},{7,7},{8,10},{9,11},{10,... | collective-permute-start | bytes 847880 | tf_op jit(solution)/shard_map/ppermute | solution.py:883
  39.3 38.3 %collective-permute-start.5 = (bf16[1104,128]{1,0:T(8,128)(2,1)S(1)}, bf16[1104,128]{1,0:T(8,128)(2,1)S(1)}, u32[]{:S(2)}, u32[]{:S(2)}) collective-permute-start(bf16[1104,128]{1,0:T(8,128)(2,1)S(1)} %collective-permute-done.1), channel_id=1, source_target_pairs={{0,2},{1,3},{2,0},{3,1},{4,6},{5,7},{6,4},{7,5},{8,8},{9,9},{10,10... | collective-permute-start | bytes 847880 | tf_op jit(solution)/shard_map/ppermute | solution.py:883
  46.5 31.9 %collective-permute-start.6 = (bf16[1104,128]{1,0:T(8,128)(2,1)S(1)}, bf16[1104,128]{1,0:T(8,128)(2,1)S(1)}, u32[]{:S(2)}, u32[]{:S(2)}) collective-permute-start(bf16[1104,128]{1,0:T(8,128)(2,1)S(1)} %collective-permute-done.2), channel_id=1, source_target_pairs={{0,4},{1,5},{2,6},{3,7},{4,0},{5,1},{6,2},{7,3},{8,14},{9,15},{10,... | collective-permute-start | bytes 847880 | tf_op jit(solution)/shard_map/ppermute | solution.py:883
  47.2 31.9 %collective-permute-start.7 = (bf16[1104,128]{1,0:T(8,128)(2,1)S(1)}, bf16[1104,128]{1,0:T(8,128)(2,1)S(1)}, u32[]{:S(2)}, u32[]{:S(2)}) collective-permute-start(bf16[1104,128]{1,0:T(8,128)(2,1)S(1)} %collective-permute-done.3), channel_id=1, source_target_pairs={{0,6},{1,7},{2,4},{3,5},{4,2},{5,3},{6,0},{7,1},{8,12},{9,13},{10,... | collective-permute-start | bytes 847880 | tf_op jit(solution)/shard_map/ppermute | solution.py:883
  81.8 26.3 %collective-permute-start.12 = (bf16[1024,128]{1,0:T(8,128)(2,1)}, bf16[1024,128]{1,0:T(8,128)(2,1)}, u32[]{:S(2)}, u32[]{:S(2)}) collective-permute-start(bf16[1024,128]{1,0:T(8,128)(2,1)} %get-tuple-element.137), channel_id=1, source_target_pairs={{0,0},{1,1},{2,10},{3,11},{4,20},{5,21},{6,30},{7,31},{8,8},{9,9},... | collective-permute-start | bytes 786440 | tf_op jit(solution)/shard_map/ppermute | solution.py:883
  93.1 47.9 %collective-permute-start.9 = (bf16[8,512,128]{2,1,0:T(8,128)(2,1)}, bf16[8,512,128]{2,1,0:T(8,128)(2,1)}, u32[]{:S(2)}, u32[]{:S(2)}) collective-permute-start(bf16[8,512,128]{2,1,0:T(8,128)(2,1)} %join.13), channel_id=1, source_target_pairs={{0,16},{1,9},{2,18},{3,11},{4,20},{5,13},{6,22},{7,15},{8,24},{9,1... | collective-permute-start | bytes 3145736 | tf_op jit(solution)/shard_map/ppermute | solution.py:883
  102.8 33.1 %collective-permute-start.16 = (bf16[4,512,128]{2,1,0:T(8,128)(2,1)}, bf16[4,512,128]{2,1,0:T(8,128)(2,1)S(1)}, u32[]{:S(2)}, u32[]{:S(2)}) collective-permute-start(bf16[4,512,128]{2,1,0:T(8,128)(2,1)} %join.14.refs_0_), channel_id=1, source_target_pairs={{0,8},{1,17},{2,10},{3,19},{4,12},{5,21},{6,14},{7,23},{8,0},{9,25... | collective-permute-start | bytes 1572872 | tf_op jit(solution)/shard_map/ppermute | solution.py:883
  141.0 47.9 %collective-permute-start.10 = (bf16[8,512,128]{2,1,0:T(8,128)(2,1)}, bf16[8,512,128]{2,1,0:T(8,128)(2,1)}, u32[]{:S(2)}, u32[]{:S(2)}) collective-permute-start(bf16[8,512,128]{2,1,0:T(8,128)(2,1)} %join.13), channel_id=1, source_target_pairs={{0,1},{1,0},{2,3},{3,2},{4,5},{5,4},{6,7},{7,6},{8,9},{9,8},{10,11... | collective-permute-start | bytes 3145736 | tf_op jit(solution)/shard_map/ppermute | solution.py:883
  146.2 43.5 %collective-permute-start.11 = (bf16[8,512,128]{2,1,0:T(8,128)(2,1)}, bf16[8,512,128]{2,1,0:T(8,128)(2,1)}, u32[]{:S(2)}, u32[]{:S(2)}) collective-permute-start(bf16[8,512,128]{2,1,0:T(8,128)(2,1)} %collective-permute-done.9), channel_id=1, source_target_pairs={{0,1},{1,0},{2,3},{3,2},{4,5},{5,4},{6,7},{7,6},{8,9},{9,8},{10,11... | collective-permute-start | bytes 3145736 | tf_op jit(solution)/shard_map/ppermute | solution.py:883
  151.8 33.7 %collective-permute-start.22 = (bf16[8,512,128]{2,1,0:T(8,128)(2,1)}, bf16[8,512,128]{2,1,0:T(8,128)(2,1)}, u32[]{:S(2)}, u32[]{:S(2)}) collective-permute-start(bf16[8,512,128]{2,1,0:T(8,128)(2,1)} %join.15), channel_id=1, source_target_pairs={{0,1},{1,0},{2,3},{3,2},{4,5},{5,4},{6,7},{7,6},{8,9},{9,8},{10,11... | collective-permute-start | bytes 3145736 | tf_op jit(solution)/shard_map/ppermute | solution.py:883
  154.2 31.3 %collective-permute-start.21 = (bf16[8,512,128]{2,1,0:T(8,128)(2,1)}, bf16[8,512,128]{2,1,0:T(8,128)(2,1)}, u32[]{:S(2)}, u32[]{:S(2)}) collective-permute-start(bf16[8,512,128]{2,1,0:T(8,128)(2,1)} %join.15), channel_id=1, source_target_pairs={{0,16},{1,9},{2,18},{3,11},{4,20},{5,13},{6,22},{7,15},{8,24},{9,1... | collective-permute-start | bytes 3145736 | tf_op jit(solution)/shard_map/ppermute | solution.py:883
  182.5 25.7 %collective-permute-start.24 = (bf16[4,512,128]{2,1,0:T(8,128)(2,1)S(1)}, bf16[4,512,128]{2,1,0:T(8,128)(2,1)S(1)}, u32[]{:S(2)}, u32[]{:S(2)}) collective-permute-start(bf16[4,512,128]{2,1,0:T(8,128)(2,1)S(1)} %copy-done.8), channel_id=1, source_target_pairs={{0,8},{1,17},{2,10},{3,19},{4,12},{5,21},{6,14},{7,23},{8,0},{9,25... | collective-permute-start | bytes 1572872 | tf_op jit(solution)/shard_map/ppermute | solution.py:883
  204.3 52.0 %all-to-all-start.1 = ((bf16[4,2048,128]{2,1,0:T(8,128)(2,1)}), bf16[4,2048,128]{2,1,0:T(8,128)(2,1)S(1)}, u32[]{:S(2)}, u32[]{:S(2)}) async-start(bf16[4,2048,128]{2,1,0:T(8,128)(2,1)} %pick.3), calls=%async_computation.1 | async-start | bytes 4194304 | tf_op jit(solution)/shard_map/all_to_all | solution.py:918
  307.1 29.7 %collective-permute-start.36 = (bf16[16,2,2,128,128]{4,3,2,1,0:T(8,128)(2,1)}, bf16[16,2,2,128,128]{4,3,2,1,0:T(8,128)(2,1)S(1)}, u32[]{:S(2)}, u32[]{:S(2)}) collective-permute-start(bf16[16,2,2,128,128]{4,3,2,1,0:T(8,128)(2,1)} %get-tuple-element.219), channel_id=1, source_target_pairs={{0,1},{1,0},{2,3},{3,2},{4,5},{5,4},{6,7},{7,6},{8,9},{9,8},{10,11... | collective-permute-start | bytes 6291464 | tf_op jit(solution)/shard_map/ppermute | solution.py:883
  311.3 24.6 %collective-permute-start.34 = (bf16[4,512,128]{2,1,0:T(8,128)(2,1)}, bf16[4,512,128]{2,1,0:T(8,128)(2,1)S(1)}, u32[]{:S(2)}, u32[]{:S(2)}) collective-permute-start(bf16[4,512,128]{2,1,0:T(8,128)(2,1)} %bitcast.55), channel_id=1, source_target_pairs={{0,16},{1,17},{2,18},{3,19},{4,20},{5,21},{6,22},{7,23},{8,24},{9,... | collective-permute-start | bytes 1572872 | tf_op jit(solution)/shard_map/ppermute | solution.py:883
  311.5 24.4 %collective-permute-start.35 = (bf16[4,512,128]{2,1,0:T(8,128)(2,1)}, bf16[4,512,128]{2,1,0:T(8,128)(2,1)S(1)}, u32[]{:S(2)}, u32[]{:S(2)}) collective-permute-start(bf16[4,512,128]{2,1,0:T(8,128)(2,1)} %bitcast.56), channel_id=1, source_target_pairs={{0,24},{1,25},{2,26},{3,27},{4,28},{5,29},{6,30},{7,31},{8,16},{9,... | collective-permute-start | bytes 1572872 | tf_op jit(solution)/shard_map/ppermute | solution.py:883
  313.1 23.7 %collective-permute-start.33 = (bf16[4,512,128]{2,1,0:T(8,128)(2,1)}, bf16[4,512,128]{2,1,0:T(8,128)(2,1)}, u32[]{:S(2)}, u32[]{:S(2)}) collective-permute-start(bf16[4,512,128]{2,1,0:T(8,128)(2,1)} %bitcast.54), channel_id=1, source_target_pairs={{0,8},{1,9},{2,10},{3,11},{4,12},{5,13},{6,14},{7,15},{8,0},{9,1},... | collective-permute-start | bytes 1572872 | tf_op jit(solution)/shard_map/ppermute | solution.py:883
  348.5 28.1 %collective-permute-start.37 = (bf16[512,128]{1,0:T(8,128)(2,1)S(1)}, bf16[512,128]{1,0:T(8,128)(2,1)S(1)}, u32[]{:S(2)}, u32[]{:S(2)}) collective-permute-start(bf16[512,128]{1,0:T(8,128)(2,1)S(1)} %get-tuple-element.278), channel_id=1, source_target_pairs={{0,0},{1,1},{2,10},{3,11},{4,20},{5,21},{6,30},{7,31},{8,2},{9,3},... | collective-permute-start | bytes 393224 | tf_op jit(solution)/shard_map/ppermute | solution.py:883
  350.6 31.2 %collective-permute-start.44 = (bf16[16,2,2,128,128]{4,3,2,1,0:T(8,128)(2,1)}, bf16[16,2,2,128,128]{4,3,2,1,0:T(8,128)(2,1)}, u32[]{:S(2)}, u32[]{:S(2)}) collective-permute-start(bf16[16,2,2,128,128]{4,3,2,1,0:T(8,128)(2,1)} %get-tuple-element.231), channel_id=1, source_target_pairs={{0,1},{1,0},{2,3},{3,2},{4,5},{5,4},{6,7},{7,6},{8,9},{9,8},{10,11... | collective-permute-start | bytes 6291464 | tf_op jit(solution)/shard_map/ppermute | solution.py:883
  353.9 24.9 %collective-permute-start.42 = (bf16[4,512,128]{2,1,0:T(8,128)(2,1)S(1)}, bf16[4,512,128]{2,1,0:T(8,128)(2,1)S(1)}, u32[]{:S(2)}, u32[]{:S(2)}) collective-permute-start(bf16[4,512,128]{2,1,0:T(8,128)(2,1)S(1)} %bitcast.186), channel_id=1, source_target_pairs={{0,16},{1,17},{2,18},{3,19},{4,20},{5,21},{6,22},{7,23},{8,24},{9,... | collective-permute-start | bytes 1572872 | tf_op jit(solution)/shard_map/ppermute | solution.py:883
  354.0 24.8 %collective-permute-start.43 = (bf16[4,512,128]{2,1,0:T(8,128)(2,1)S(1)}, bf16[4,512,128]{2,1,0:T(8,128)(2,1)}, u32[]{:S(2)}, u32[]{:S(2)}) collective-permute-start(bf16[4,512,128]{2,1,0:T(8,128)(2,1)S(1)} %bitcast.185), channel_id=1, source_target_pairs={{0,24},{1,25},{2,26},{3,27},{4,28},{5,29},{6,30},{7,31},{8,16},{9,... | collective-permute-start | bytes 1572872 | tf_op jit(solution)/shard_map/ppermute | solution.py:883
  358.1 23.6 %collective-permute-start.41 = (bf16[4,512,128]{2,1,0:T(8,128)(2,1)S(1)}, bf16[4,512,128]{2,1,0:T(8,128)(2,1)}, u32[]{:S(2)}, u32[]{:S(2)}) collective-permute-start(bf16[4,512,128]{2,1,0:T(8,128)(2,1)S(1)} %bitcast.183), channel_id=1, source_target_pairs={{0,8},{1,9},{2,10},{3,11},{4,12},{5,13},{6,14},{7,15},{8,0},{9,1},... | collective-permute-start | bytes 1572872 | tf_op jit(solution)/shard_map/ppermute | solution.py:883
  382.6 117.5 %all-to-all-start.2 = ((bf16[4,2048,128]{2,1,0:T(8,128)(2,1)}), bf16[4,2048,128]{2,1,0:T(8,128)(2,1)S(1)}, u32[]{:S(2)}, u32[]{:S(2)}) async-start(bf16[4,2048,128]{2,1,0:T(8,128)(2,1)} %bitcast.171), calls=%async_computation.2 | async-start | bytes 4194304 | tf_op jit(solution)/shard_map/all_to_all | solution.py:918
  388.3 72.9 %collective-permute-start.65 = (bf16[512,128]{1,0:T(8,128)(2,1)S(1)}, bf16[512,128]{1,0:T(8,128)(2,1)S(1)}, u32[]{:S(2)}, u32[]{:S(2)}) collective-permute-start(bf16[512,128]{1,0:T(8,128)(2,1)S(1)} %get-tuple-element.263), channel_id=1, source_target_pairs={{0,6},{1,7},{2,12},{3,13},{4,18},{5,19},{6,24},{7,25},{8,4},{9,5},... | collective-permute-start | bytes 393224 | tf_op jit(solution)/shard_map/ppermute | solution.py:883
  391.3 71.9 %collective-permute-start.64 = (bf16[512,128]{1,0:T(8,128)(2,1)S(1)}, bf16[512,128]{1,0:T(8,128)(2,1)S(1)}, u32[]{:S(2)}, u32[]{:S(2)}) collective-permute-start(bf16[512,128]{1,0:T(8,128)(2,1)S(1)} %get-tuple-element.264), channel_id=1, source_target_pairs={{0,4},{1,5},{2,14},{3,15},{4,16},{5,17},{6,26},{7,27},{8,6},{9,7},... | collective-permute-start | bytes 393224 | tf_op jit(solution)/shard_map/ppermute | solution.py:883
  402.3 24.5 %collective-permute-start.55 = (bf16[4,512,128]{2,1,0:T(8,128)(2,1)S(1)}, bf16[4,512,128]{2,1,0:T(8,128)(2,1)S(1)}, u32[]{:S(2)}, u32[]{:S(2)}) collective-permute-start(bf16[4,512,128]{2,1,0:T(8,128)(2,1)S(1)} %bitcast.190), channel_id=1, source_target_pairs={{0,16},{1,17},{2,18},{3,19},{4,20},{5,21},{6,22},{7,23},{8,24},{9,... | collective-permute-start | bytes 1572872 | tf_op jit(solution)/shard_map/ppermute | solution.py:883
  402.3 26.8 %collective-permute-start.54 = (bf16[4,512,128]{2,1,0:T(8,128)(2,1)S(1)}, bf16[4,512,128]{2,1,0:T(8,128)(2,1)S(1)}, u32[]{:S(2)}, u32[]{:S(2)}) collective-permute-start(bf16[4,512,128]{2,1,0:T(8,128)(2,1)S(1)} %bitcast.188), channel_id=1, source_target_pairs={{0,8},{1,9},{2,10},{3,11},{4,12},{5,13},{6,14},{7,15},{8,0},{9,1},... | collective-permute-start | bytes 1572872 | tf_op jit(solution)/shard_map/ppermute | solution.py:883
  426.8 27.2 %collective-permute-start.47 = (bf16[4,512,128]{2,1,0:T(8,128)(2,1)S(1)}, bf16[4,512,128]{2,1,0:T(8,128)(2,1)S(1)}, u32[]{:S(2)}, u32[]{:S(2)}) collective-permute-start(bf16[4,512,128]{2,1,0:T(8,128)(2,1)S(1)} %bitcast.187), channel_id=1, source_target_pairs={{0,16},{1,17},{2,18},{3,19},{4,20},{5,21},{6,22},{7,23},{8,24},{9,... | collective-permute-start | bytes 1572872 | tf_op jit(solution)/shard_map/ppermute | solution.py:883
  429.1 26.9 %collective-permute-start.46 = (bf16[4,512,128]{2,1,0:T(8,128)(2,1)S(1)}, bf16[4,512,128]{2,1,0:T(8,128)(2,1)S(1)}, u32[]{:S(2)}, u32[]{:S(2)}) collective-permute-start(bf16[4,512,128]{2,1,0:T(8,128)(2,1)S(1)} %bitcast.184), channel_id=1, source_target_pairs={{0,8},{1,9},{2,10},{3,11},{4,12},{5,13},{6,14},{7,15},{8,0},{9,1},... | collective-permute-start | bytes 1572872 | tf_op jit(solution)/shard_map/ppermute | solution.py:883
  440.4 28.7 %collective-permute-start.63 = (bf16[512,128]{1,0:T(8,128)(2,1)S(1)}, bf16[512,128]{1,0:T(8,128)(2,1)S(1)}, u32[]{:S(2)}, u32[]{:S(2)}) collective-permute-start(bf16[512,128]{1,0:T(8,128)(2,1)S(1)} %get-tuple-element.265), channel_id=1, source_target_pairs={{0,2},{1,3},{2,8},{3,9},{4,22},{5,23},{6,28},{7,29},{8,0},{9,1},{1... | collective-permute-start | bytes 393224 | tf_op jit(solution)/shard_map/ppermute | solution.py:883
  471.8 24.8 %collective-permute-start.52 = (bf16[512,128]{1,0:T(8,128)(2,1)}, bf16[512,128]{1,0:T(8,128)(2,1)S(1)}, u32[]{:S(2)}, u32[]{:S(2)}) collective-permute-start(bf16[512,128]{1,0:T(8,128)(2,1)} %get-tuple-element.271), channel_id=1, source_target_pairs={{0,6},{1,7},{2,12},{3,13},{4,18},{5,19},{6,24},{7,25},{8,4},{9,5},... | collective-permute-start | bytes 393224 | tf_op jit(solution)/shard_map/ppermute | solution.py:883
  (72 other events, 967.7 us)

commit v5 on v4

--- a/solution.py
+++ b/solution.py
@@ -318,14 +318,24 @@
         chunk_copy(source, target, sems, chunk).wait()
 
 
-def factor_copies(parts, held, sems, side, outward=False):
+def factor_copies(parts, layer, held, sems, side):
     count = parts[0].shape[0]
-    copies = []
-    for at, ref in enumerate(parts):
-        inside = held.at[pl.ds(at * count, count), side]
-        ends = (inside, ref.at[:, side]) if outward else (ref.at[:, side], inside)
-        copies.append(pltpu.make_async_copy(*ends, sems.at[side, at]))
-    return copies
+    return [
+        pltpu.make_async_copy(
+            ref.at[:, layer, side], held.at[pl.ds(at * count, count), side], sems.at[side, at]
+        )
+        for at, ref in enumerate(parts)
+    ]
+
+
+def gradient_copies(held, parts, sems, side):
+    count = parts[0].shape[0]
+    return [
+        pltpu.make_async_copy(
+            held.at[pl.ds(at * count, count), side], ref.at[:, side], sems.at[side, at]
+        )
+        for at, ref in enumerate(parts)
+    ]
 
 
 def by_chunk(blocks, step, carry, before=None, after=None):
@@ -344,7 +354,7 @@
     return lax.fori_loop(0, CHUNKS, one, carry)
 
 
-def forward_kernel(first, inputs, table_ref, gain_ref, sums_ref, *refs):
+def forward_kernel(first, layer, inputs, table_ref, gain_ref, sums_ref, *refs):
     sources, refs = refs[:inputs], refs[inputs:]
     parts, sources = sources[:PARTS], sources[PARTS:]
     out_ref, u_ref, z_ref, slope_ref, scale_ref, next_ref = refs[:6]
@@ -355,8 +365,8 @@
     blocks = features // size
     fold = size // blocks
 
-    left_in = factor_copies(parts, w, w_sems, 0)
-    right_in = factor_copies(parts, w, w_sems, 1)
+    left_in = factor_copies(parts, layer, w, w_sems, 0)
+    right_in = factor_copies(parts, layer, w, w_sems, 1)
     if first:
         start_chunks(sources[0], raw, in_sems)
         for copy in left_in + right_in:
@@ -436,7 +446,7 @@
         wait_chunks(source, target, out_sems.at[at])
 
 
-def backward_kernel(turning, last, inputs, table_ref, gain_ref, end_gain_ref, scale_ref, *refs):
+def backward_kernel(turning, last, layer, inputs, table_ref, gain_ref, end_gain_ref, scale_ref, *refs):
     sources, refs = refs[:inputs], refs[inputs:]
     slope_ref, z_ref, u_ref = sources[:3]
     parts, sources = sources[3 : 3 + PARTS], sources[3 + PARTS :]
@@ -449,8 +459,8 @@
     blocks = features // size
     fold = size // blocks
 
-    left_in = factor_copies(parts, w, w_sems, 0)
-    right_in = factor_copies(parts, w, w_sems, 1)
+    left_in = factor_copies(parts, layer, w, w_sems, 0)
+    right_in = factor_copies(parts, layer, w, w_sems, 1)
     g_ref, h_ref = sources[:2]
     if turning:
         start_chunks(g_ref, top, in_sems.at[0])
@@ -516,7 +526,7 @@
         return carry
 
     by_chunk(blocks, right, 0, arrive_right)
-    right_out = factor_copies((own_grad, peer_grad), gw, gw_sems, 1, outward=True)
+    right_out = gradient_copies(gw, (own_grad, peer_grad), gw_sems, 1)
     for copy in right_out:
         copy.start()
     for copy in left_in:
@@ -544,7 +554,7 @@
         return total + fold_rows(weighted * h[rows, :].astype(jnp.float32))
 
     total = by_chunk(blocks, left, jnp.zeros((8, slots), jnp.float32), arrive_left)
-    left_out = factor_copies((own_grad, peer_grad), gw, gw_sems, 0, outward=True)
+    left_out = gradient_copies(gw, (own_grad, peer_grad), gw_sems, 0)
     for copy in left_out:
         copy.start()
     back = scale * scale * scale * jnp.sum(total, axis=0, keepdims=True) / features
@@ -574,11 +584,11 @@
 OUTSIDE = pl.BlockSpec(memory_space=pl.ANY)
 
 
-def run_forward(table, gain, sums, residual, weights):
+def run_forward(table, gain, sums, residual, weights, layer):
     first = residual.dtype == jnp.bfloat16
     whole = residual.shape
     sources = (*weights, residual)
-    held = (PARTS * weights[0].shape[0],) + weights[0].shape[1:]
+    held = (PARTS * weights[0].shape[0],) + weights[0].shape[2:]
     out_shape = (
         shape_of(whole, jnp.float32),
         shape_of(whole, jnp.bfloat16),
@@ -588,7 +598,7 @@
         shape_of((8, whole[1]), jnp.float32),
     )
     return pl.pallas_call(
-        lambda *refs: forward_kernel(first, len(sources), *refs),
+        lambda *refs: forward_kernel(first, layer, len(sources), *refs),
         in_specs=[SMEM, INSIDE, INSIDE] + [OUTSIDE] * len(sources),
         out_specs=[OUTSIDE] * 4 + [INSIDE] * 2,
         out_shape=out_shape,
@@ -612,14 +622,14 @@
     )(table, gain, sums, *sources)
 
 
-def run_backward(table, gain, end_gain, scale, kept, weights, sources, turning, last):
+def run_backward(table, gain, end_gain, scale, kept, weights, layer, sources, turning, last):
     whole = kept[0].shape
     sources = (*kept, *weights, *sources)
-    held = (PARTS * weights[0].shape[0],) + weights[0].shape[1:]
+    held = (PARTS * weights[0].shape[0],) + weights[0].shape[2:]
     half = (held[0] // 2,) + held[1:]
     out_shape = [shape_of(whole, jnp.bfloat16 if last else jnp.float32)] + [shape_of(half, jnp.bfloat16)] * 2
     return pl.pallas_call(
-        lambda *refs: backward_kernel(turning, last, len(sources), *refs),
+        lambda *refs: backward_kernel(turning, last, layer, len(sources), *refs),
         in_specs=[SMEM] + [INSIDE] * 3 + [OUTSIDE] * len(sources),
         out_specs=[OUTSIDE] * len(out_shape),
         out_shape=out_shape,
@@ -675,14 +685,45 @@
     )(*extra, *inputs)
 
 
-def joined(parts):
-    rows = parts[0].shape[0]
+def joined(parts, rows=None):
+    rows = parts[0].shape[0] if rows is None else rows
     whole = shape_of((rows * len(parts),) + parts[0].shape[1:], parts[0].dtype)
 
     def plan(sources, targets):
-        return [(source, targets[0].at[pl.ds(at * rows, rows)]) for at, source in enumerate(sources)]
+        return [
+            (source.at[pl.ds(0, rows)], targets[0].at[pl.ds(at * rows, rows)])
+            for at, source in enumerate(sources)
+        ]
 
     return run_copies(plan, None, parts, [whole], len(parts), "join")[0]
+
+
+def sum_kernel(terms, refs_in, *refs):
+    sources, outs = refs[:refs_in], refs[refs_in:]
+    groups = refs_in // terms
+    count = len(outs)
+    for group in range(groups):
+        mine = sources[group * terms : (group + 1) * terms]
+        rows = mine[0].shape[0] // count
+        for at, out in enumerate(outs):
+            total = sum(ref[pl.ds(at * rows, rows), :].astype(jnp.float32) for ref in mine)
+            out[pl.ds(group * rows, rows), :] = total.astype(jnp.bfloat16)
+
+
+def run_sum(groups, outputs):
+    flat = [term.reshape(-1, term.shape[-1]) for terms in groups for term in terms]
+    rows, lanes = flat[0].shape
+    return pl.pallas_call(
+        lambda *refs: sum_kernel(len(groups[0]), len(flat), *refs),
+        in_specs=[INSIDE] * len(flat),
+        out_specs=[INSIDE] * outputs,
+        out_shape=[shape_of((len(groups) * rows // outputs, lanes), jnp.bfloat16)] * outputs,
+        compiler_params=pltpu.CompilerParams(vmem_limit_bytes=VMEM_LIMIT),
+        cost_estimate=pl.CostEstimate(
+            flops=rows * lanes * len(flat), bytes_accessed=2 * rows * lanes * (len(flat) + 1), transcendentals=0
+        ),
+        name="sum",
+    )(*flat)
 
 
 def factor_pieces(place, left, right, gain_rows, groups, chunk):
@@ -780,10 +821,11 @@
 BACKWARD_COST = 18_000_000_000
 
 
-def assemble_kernel(layer_count, factor, place_ref, *refs):
-    sources, (left_ref, right_ref) = refs[: 2 * layer_count], refs[2 * layer_count : 2 * layer_count + 2]
-    held, wide, in_sems, out_sems = refs[2 * layer_count + 2 :]
-    width, chunk = held.shape[1], held.shape[3]
+def assemble_kernel(layers, factor, place_ref, *refs):
+    count = 2 * len(layers)
+    sources, (left_ref, right_ref) = refs[:count], refs[count : count + 2]
+    held, wide, in_sems, out_sems = refs[count + 2 :]
+    width, chunk = held.shape[1], held.shape[4]
     origin, core = place_ref[0] ^ place_ref[1], place_ref[2]
     arrivals = [
         pltpu.make_async_copy(source, held.at[at], in_sems.at[at]) for at, source in enumerate(sources)
@@ -791,46 +833,46 @@
     for copy in arrivals:
         copy.start()
     leaving = []
-    for at in range(2 * layer_count):
+    for at in range(count):
         arrivals[at].wait()
-        layer, side = at // 2, at % 2
-        half = core if side == 0 else 1 - core
-        wide[at] = held[at].astype(jnp.float32) * factor
+        half = core if at % 2 == 0 else 1 - core
         for k in range(width):
+            wide[at, k] = held[at, k].astype(jnp.float32) * factor
             start = (half * width + (origin ^ k)) * chunk
-            for which, target in enumerate((left_ref, right_ref)):
-                copy = pltpu.make_async_copy(
-                    wide.at[at, k, which],
-                    target.at[layer, pl.ds(start, chunk)],
-                    out_sems.at[(at * width + k) * 2 + which],
-                )
-                copy.start()
-                leaving.append(copy)
+            for inside, layer in enumerate(layers[at // 2]):
+                for which, target in enumerate((left_ref, right_ref)):
+                    copy = pltpu.make_async_copy(
+                        wide.at[at, k, inside, which],
+                        target.at[layer, pl.ds(start, chunk)],
+                        out_sems.at[len(leaving)],
+                    )
+                    copy.start()
+                    leaving.append(copy)
     for copy in leaving:
         copy.wait()
 
 
-def run_assemble(places, pieces, layer_count, factor):
+def run_assemble(place, pieces, layers, factor):
     piece = pieces[0].shape
-    blocks = 2 * piece[0] * piece[2]
-    out = shape_of((layer_count, blocks) + piece[3:], jnp.float32)
+    layer_count = sum(len(group) for group in layers)
+    out = shape_of((layer_count, 2 * piece[0] * piece[3]) + piece[4:], jnp.float32)
     return pl.pallas_call(
-        lambda *refs: assemble_kernel(layer_count, factor, *refs),
+        lambda *refs: assemble_kernel(layers, factor, *refs),
         in_specs=[SMEM] + [OUTSIDE] * len(pieces),
         out_specs=[OUTSIDE] * 2,
         out_shape=[out] * 2,
         scratch_shapes=[
-            pltpu.VMEM((2 * layer_count,) + piece, jnp.bfloat16),
-            pltpu.VMEM((2 * layer_count,) + piece, jnp.float32),
-            pltpu.SemaphoreType.DMA((2 * layer_count,)),
+            pltpu.VMEM((len(pieces),) + piece, jnp.bfloat16),
+            pltpu.VMEM((len(pieces),) + piece, jnp.float32),
+            pltpu.SemaphoreType.DMA((len(pieces),)),
             pltpu.SemaphoreType.DMA((4 * layer_count * piece[0],)),
         ],
         compiler_params=pltpu.CompilerParams(vmem_limit_bytes=VMEM_LIMIT),
         cost_estimate=pl.CostEstimate(
-            flops=0, bytes_accessed=12 * layer_count * math.prod(piece), transcendentals=0
+            flops=0, bytes_accessed=6 * len(pieces) * math.prod(piece), transcendentals=0
         ),
         name="assemble",
-    )(places, *pieces)
+    )(place, *pieces)
 
 
 def plane_routes(width, replicas):
@@ -857,10 +899,6 @@
         "planes": [route(lambda s, t, d, k=k: (s, t ^ k, d)) for k in range(width)],
         "homes": [route(lambda s, t, d, j=j: (t, t ^ s ^ j, d)) for j in range(width)],
     }, ranks
-
-
-def added(*parts):
-    return sum(part.astype(jnp.float32) for part in parts).astype(jnp.bfloat16)
 
 
 def plane_shards(patches, teacher, critic_pairs, left_factors, right_factors, norm_gains):
@@ -898,7 +936,7 @@
         return [pair, other, peer, move(other, routes["cores"])]
 
     def as_weights(parts):
-        return [part.reshape(-1, 2, chunk, size, size) for part in parts]
+        return [part.reshape(2 * width, -1, 2, chunk, size, size) for part in parts]
 
     block = jnp.arange(blocks, dtype=jnp.int32)
     inside = block % local_blocks
@@ -926,102 +964,96 @@
     patch_came = to_planes(patch_sent).reshape(-1, wide)
     near = [move_all(pieces[0], "spread")]
     near[0], pieces[1] = tie((near[0], pieces[1]))
-    front = move_all(near[0], "lift")
+    came = [move_all(near[0], "lift")]
     near.append(move_all(pieces[1], "spread"))
-
-    def lowest_of(values, at):
-        at = at * layer_rows
-        return joined([value[at : at + layer_rows].reshape(1, layer_rows, size) for value in values])
-
-    gains = jnp.stack([value[2 * layer_rows :] for value in front])[jnp.arange(width) ^ section ^ tensor]
+    group_rows = [len(group) * layer_rows for group in groups]
+
+    def lowest_of(at):
+        mine = joined(came[at], group_rows[at])
+        return mine.reshape(width, group_rows[at], size)
+
+    gains = jnp.stack([value[group_rows[0] :] for value in came[0]])[jnp.arange(width) ^ section ^ tensor]
     gains = gains.reshape(width, layer_count + 1, local_blocks, size).transpose(1, 3, 0, 2)
     gains = gains.reshape(layer_count + 1, size, blocks)
-    lowest = [lowest_of(front, 0), lowest_of(front, 1)]
-    pairs = [gather_one(lowest[0]), gather_one(lowest[1])] + [None] * (layer_count - 2)
-    weights = [as_weights(gather_three(*gather_two(pairs[0])))]
-    patch_came, near[1] = tie((patch_came, near[1]))
-    later = move_all(near[1], "lift")
-    pairs[1], later, teacher = tie((pairs[1], later, teacher))
-    for layer in range(2, layer_count):
-        lowest.append(lowest_of(later, layer - 2))
+    pair = gather_one(lowest_of(0))
+    came.append(move_all(near[1], "lift"))
+    weights = [as_weights(gather_three(*gather_two(pair)))]
+    later = gather_one(lowest_of(1))
     target_sent = run_pick(critic_pairs, teacher, width, wide)
 
     residual = patch_came
+    residual, weights, later, target_sent = tie((residual, weights, later, target_sent))
+    flying = gather_two(later)
     sums = jnp.zeros((8, wide), jnp.float32)
-    flying = {1: gather_two(pairs[1])}
-    if layer_count > 2:
-        pairs[2] = gather_one(lowest[2])
-    residual, flying, pairs, target_sent = tie((residual, flying, pairs, target_sent))
     stored = []
     for layer in range(layer_count):
-        ahead = {}
-        if layer + 1 < layer_count:
-            ahead["weights"] = gather_three(*flying.pop(layer + 1))
-        if layer + 2 < layer_count:
-            ahead["two"] = gather_two(pairs[layer + 2])
-        if layer + 3 < layer_count:
-            ahead["one"] = (lowest[layer + 3], move(lowest[layer + 3], routes["across"][0]))
+        group = 0 if layer in groups[0] else 1
         following, u, z, slope, scale, sums = run_forward(
-            table, gains[layer], sums, residual, weights[layer]
+            table, gains[layer], sums, residual, weights[group], layer - groups[group][0]
         )
         stored.append(((slope, z, u), scale, residual))
-        following, ahead = tie((following, ahead))
         residual = following
-        if layer + 1 < layer_count:
-            weights.append(as_weights(ahead["weights"]))
-        if layer + 2 < layer_count:
-            flying[layer + 2] = ahead["two"]
-        if layer + 3 < layer_count:
-            pairs[layer + 3] = joined(list(ahead["one"]))
         if layer == 0:
-            target_sent, sums = tie((target_sent, sums))
+            residual, sums, flying, target_sent = tie((residual, sums, flying, target_sent))
+            weights.append(as_weights(gather_three(*flying)))
             target = to_planes(target_sent).reshape(-1, wide)
+        if layer == groups[0][-1]:
+            residual, sums, weights[1] = tie((residual, sums, weights[1]))
 
     def core_sum(mine, other):
         return (mine, move(other, routes["cores"]))
 
-    def plane_sum(value):
-        value = value.reshape(width, width, layer_rows, size)
-        return send([value[k] for k in range(width)], "sections")
-
-    def homeward(value):
-        return move_all([value[j] for j in range(width)], "homes")
+    def plane_sum(mine, other):
+        return send(run_sum([(mine, other)], width), "sections")
+
+    def homeward(parts):
+        return move_all(run_sum(parts, width), "homes")
 
     def both_halves(parts):
-        whole = joined([part.reshape(1, layer_rows, size) for part in parts])
-        return whole, move(whole, routes["cores"])
-
-    steps = (
-        lambda state: core_sum(*state),
-        lambda state: plane_sum(added(*state)),
-        lambda state: homeward(added(*state)),
-        both_halves,
-    )
+        whole = joined(parts)
+        return [part.reshape(width, -1, 2, chunk, size, size) for part in (whole, move(whole, routes["cores"]))]
+
+    steps = (core_sum, plane_sum)
     gradient = residual
     underway = []
     for layer in range(layer_count - 1, -1, -1):
         turning = layer == layer_count - 1
         last = layer == 0
         kept, scale, inputs = stored[layer]
+        group = 0 if layer in groups[0] else 1
         sources = (gradient, inputs, target) if turning else (gradient, inputs)
-        underway = [(at + 1, steps[at](state)) for at, state in underway]
+        underway = [(at + 1, steps[at](*state)) if at < len(steps) else (at, state) for at, state in underway]
         gradient, mine, other = run_backward(
-            table, gains[layer], gains[layer_count], scale, kept, weights[layer], sources, turning, last
+            table,
+            gains[layer],
+            gains[layer_count],
+            scale,
+            kept,
+            weights[group],
+            layer - groups[group][0],
+            sources,
+            turning,
+            last,
         )
         gradient, mine, other, states = tie((gradient, mine, other, [state for _, state in underway]))
         underway = [(at, state) for (at, _), state in zip(underway, states)]
         underway.append((0, (mine, other)))
 
     returned = to_planes(gradient.reshape(width, feat_local, wide))
-    homes_of = []
+    homes_of = [None, None]
+    ended = []
     for at, state in underway:
         for step in steps[at:]:
-            state = step(state)
-        homes_of.append(state)
+            state = step(*state)
+        ended.insert(0, state)
+    ended[1:] = tie(ended[1:])
+    homes_of[1] = both_halves(homeward(ended[groups[1][0] :]))
+    home = homeward(ended[: groups[1][0]])
     d_patches = run_combine(critic_pairs, returned)
+    d_patches, home, homes_of[1] = tie((d_patches, home, homes_of[1]))
+    homes_of[0] = both_halves(home)
     grad_factor = 1.0 / math.sqrt(2 * tok_rows * width * replicas)
-    parts = [part.reshape(width, 2, chunk, size, size) for pair in homes_of[::-1] for part in pair]
-    grad_left, grad_right = run_assemble(place, parts, layer_count, grad_factor)
+    grad_left, grad_right = run_assemble(place, homes_of[0] + homes_of[1], groups, grad_factor)
     return (d_patches, grad_left[None], grad_right[None])
 
 

time: 518 us -> 545 us (1.052)
  waiting for transfers between devices: 108 us -> 195 us
  starting transfers between devices: 178 us -> 125 us
  other arithmetic: 13.5 us -> 1.29 us
  Pallas kernels: 185 us -> 196 us
    ppermute x68 -> x50, waiting for transfers between devices: 105 us -> 187 us  [move(): return lax.ppermute(value, AXES, route)]
    ppermute x68 -> x50, starting transfers between devices: 165 us -> 112 us  [move(): return lax.ppermute(value, AXES, route)]
    pallas_call x9 -> x15, Pallas kernels: 144 us -> 166 us  [the longest x4 84.5 us: run_backward(): pl.pallas_call(lambda *refs: backward_kernel(turning, last, layer, len(so...]
    convert_element_type x8 -> x0, other arithmetic: 12.2 us -> none  [added(): sum((part.astype(jnp.float32) for part in parts)).astype(jnp.bfloat16)]
    pallas_call x13 -> x7, Pallas kernels: 28.3 us -> 18.6 us  [run_copies(): pl.pallas_call(lambda *refs: copies_kernel(plan, len(extra) + len(inputs)...]
    reshape x6 -> x0, local copies, waits for them, and re-layouts: 6.47 us -> none  [lowest_of(): value[at:at + layer_rows].reshape(1, layer_rows, size)]
    unnamed x67 -> x75, local copies, waits for them, and re-layouts: 10.3 us -> 12.8 us
  transfers between devices with their start and end apart: 71 -> 53, of which waited for: 16 -> 26; matrix products, arithmetic and copies ran while one was open for 6% -> 2% of each run, Pallas kernels for 29% -> 28%
where the time goes in v5:
time: 545 us; the launch traced here: 542 us
  Pallas kernels  196 us (36%)
  waiting for transfers between devices  195 us (36%)
  starting transfers between devices  125 us (23%)
  local copies, waits for them, and re-layouts  22.8 us (4%)
    ppermute x50, waiting for transfers between devices, move(): return lax.ppermute(value, AXES, route)  187 us
    ppermute x50, starting transfers between devices, move(): return lax.ppermute(value, AXES, route)  112 us
    pallas_call x4, Pallas kernels, run_backward(): pl.pallas_call(lambda *refs: backward_kernel(turning, last, layer, len(so...  84.5 us
    pallas_call x4, Pallas kernels, run_forward(): pl.pallas_call(lambda *refs: forward_kernel(first, layer, len(sources), *...  54 us
    pallas_call x6, Pallas kernels, run_sum(): pl.pallas_call(lambda *refs: sum_kernel(len(groups[0]), len(flat), *refs)...  21.5 us
    pallas_call x7, Pallas kernels, run_copies(): pl.pallas_call(lambda *refs: copies_kernel(plan, len(extra) + len(inputs)...  18.6 us
    all_to_all x3, starting transfers between devices, to_planes(): lax.all_to_all(value, 'tensor', split_axis=0, concat_axis=0, tiled=True)  12.8 us
    unnamed x75, local copies, waits for them, and re-layouts  12.8 us
  transfers between devices with their start and end apart: 53, of which 26 were waited for; matrix products, arithmetic and copies ran while one was open for 2% of the time, Pallas kernels for 28%

profile of v5, /device:TPU:5, one launch (start us, length us, event | category | flops | bytes accessed | tf_op | source)
XLA Modules:
  0.0 542.5 jit_solution(2878750204333647045)
XLA Ops:
  18.0 8.9 %collective-permute-done.2 = bf16[1104,128]{1,0:T(8,128)(2,1)S(1)} collective-permute-done((bf16[1104,128]{1,0:T(8,128)(2,1)}, bf16[1104,128]{1,0:T(8,128)(2,1)S(1)}, u32[]{:S(2)}, u32[]{:S(2)}) %collective-permute-start.2) | collective-permute-done | bytes 282656 | tf_op jit(solution)/shard_map/ppermute | solution.py:921
  29.7 7.0 %collective-permute-start.5 = (bf16[1104,128]{1,0:T(8,128)(2,1)S(1)}, bf16[1104,128]{1,0:T(8,128)(2,1)S(1)}, u32[]{:S(2)}, u32[]{:S(2)}) collective-permute-start(bf16[1104,128]{1,0:T(8,128)(2,1)S(1)} %collective-permute-done.1), channel_id=1, source_target_pairs={{0,2},{1,3},{2,0},{3,1},{4,6},{5,7},{6,4},{7,5},{8,8},{9,9},{10,10... | collective-permute-start | bytes 847880 | tf_op jit(solution)/shard_map/ppermute | solution.py:921
  39.4 7.9 %collective-permute-done.5.refs_1_ = bf16[1104,128]{1,0:T(8,128)(2,1)S(1)} collective-permute-done((bf16[1104,128]{1,0:T(8,128)(2,1)S(1)}, bf16[1104,128]{1,0:T(8,128)(2,1)S(1)}, u32[]{:S(2)}, u32[]{:S(2)}) %collective-permute-start.5) | collective-permute-done | bytes 282656 | tf_op jit(solution)/shard_map/ppermute | solution.py:921
  47.4 8.0 %collective-permute-done.7.refs_3_ = bf16[1104,128]{1,0:T(8,128)(2,1)S(1)} collective-permute-done((bf16[1104,128]{1,0:T(8,128)(2,1)S(1)}, bf16[1104,128]{1,0:T(8,128)(2,1)S(1)}, u32[]{:S(2)}, u32[]{:S(2)}) %collective-permute-start.7) | collective-permute-done | bytes 282656 | tf_op jit(solution)/shard_map/ppermute | solution.py:921
  61.4 12.7 %collective-permute-done.8.refs_1_ = bf16[4,1024,128]{2,1,0:T(8,128)(2,1)S(1)} collective-permute-done((bf16[4,1024,128]{2,1,0:T(8,128)(2,1)}, bf16[4,1024,128]{2,1,0:T(8,128)(2,1)S(1)}, u32[]{:S(2)}, u32[]{:S(2)}) %collective-permute-start.8) | collective-permute-done | bytes 1048608 | tf_op jit(solution)/shard_map/ppermute | solution.py:921
  87.2 4.7 all-to-all-start
  94.7 11.6 %collective-permute-done.9 = bf16[8,1024,128]{2,1,0:T(8,128)(2,1)} collective-permute-done((bf16[8,1024,128]{2,1,0:T(8,128)(2,1)}, bf16[8,1024,128]{2,1,0:T(8,128)(2,1)}, u32[]{:S(2)}, u32[]{:S(2)}) %collective-permute-start.9) | collective-permute-done | bytes 2097184 | tf_op jit(solution)/shard_map/ppermute | solution.py:921
  120.3 9.9 %collective-permute-start.13 = (bf16[1024,128]{1,0:T(8,128)(2,1)S(1)}, bf16[1024,128]{1,0:T(8,128)(2,1)S(1)}, u32[]{:S(2)}, u32[]{:S(2)}) collective-permute-start(bf16[1024,128]{1,0:T(8,128)(2,1)S(1)} %collective-permute-done.12), channel_id=1, source_target_pairs={{0,0},{1,1},{2,2},{3,3},{4,4},{5,5},{6,6},{7,7},{8,10},{9,11},{10,... | collective-permute-start | bytes 786440 | tf_op jit(solution)/shard_map/ppermute | solution.py:921
  132.8 23.6 %collective-permute-done.13.refs_0_ = bf16[1024,128]{1,0:T(8,128)(2,1)S(1)} collective-permute-done((bf16[1024,128]{1,0:T(8,128)(2,1)S(1)}, bf16[1024,128]{1,0:T(8,128)(2,1)S(1)}, u32[]{:S(2)}, u32[]{:S(2)}) %collective-permute-start.13) | collective-permute-done | bytes 262176 | tf_op jit(solution)/shard_map/ppermute | solution.py:921
  158.4 5.1 collective-permute-done.19.refs_3_
  173.7 7.0 %collective-permute-done.20.refs_1_ = bf16[4,1024,128]{2,1,0:T(8,128)(2,1)S(1)} collective-permute-done((bf16[4,1024,128]{2,1,0:T(8,128)(2,1)}, bf16[4,1024,128]{2,1,0:T(8,128)(2,1)S(1)}, u32[]{:S(2)}, u32[]{:S(2)}) %collective-permute-start.20) | collective-permute-done | bytes 1048608 | tf_op jit(solution)/shard_map/ppermute | solution.py:921
  184.5 4.6 collective-permute-start.22
  192.5 14.0 %forward_layer.4 = (f32[8192,128]{1,0:T(8,128)}, bf16[8192,128]{1,0:T(8,128)(2,1)}, bf16[8192,128]{1,0:T(8,128)(2,1)}, bf16[8192,128]{1,0:T(8,128)(2,1)}, f32[8,128]{1,0:T(8,128)}, /*index=5*/f32[8,128]{1,0:T(8,128)}) custom-call(s32[2,64]{1,0:T(2,128)} %pad_add_fusion.refs_0_, bf16[128,64]{1,0:T(8,128)(2,1)} %copy.27.refs_1_, ...), custom_call_target="tpu_custom_call" | custom-call | flops 15000000512 | bytes 20971520 | tf_op jit(solution)/shard_map/forward_layer/pallas_call | solution.py:600
  206.6 8.1 %collective-permute-done.21 = bf16[8,1024,128]{2,1,0:T(8,128)(2,1)} collective-permute-done((bf16[8,1024,128]{2,1,0:T(8,128)(2,1)}, bf16[8,1024,128]{2,1,0:T(8,128)(2,1)}, u32[]{:S(2)}, u32[]{:S(2)}) %collective-permute-start.21) | collective-permute-done | bytes 2097184 | tf_op jit(solution)/shard_map/ppermute | solution.py:921
  222.8 13.3 %forward_layer.5 = (f32[8192,128]{1,0:T(8,128)}, bf16[8192,128]{1,0:T(8,128)(2,1)}, bf16[8192,128]{1,0:T(8,128)(2,1)}, bf16[8192,128]{1,0:T(8,128)(2,1)}, f32[8,128]{1,0:T(8,128)}, /*index=5*/f32[8,128]{1,0:T(8,128)}) custom-call(s32[2,64]{1,0:T(2,128)} %pad_add_fusion.refs_0_, bf16[128,64]{1,0:T(8,128)(2,1)} %copy.25.refs_1_, ...), custom_call_target="tpu_custom_call" | custom-call | flops 15000000512 | bytes 20971520 | tf_op jit(solution)/shard_map/forward_layer/pallas_call | solution.py:600
  236.1 13.4 %forward_layer.6 = (f32[8192,128]{1,0:T(8,128)}, bf16[8192,128]{1,0:T(8,128)(2,1)}, bf16[8192,128]{1,0:T(8,128)(2,1)}, bf16[8192,128]{1,0:T(8,128)(2,1)}, f32[8,128]{1,0:T(8,128)}, /*index=5*/f32[8,128]{1,0:T(8,128)}) custom-call(s32[2,64]{1,0:T(2,128)} %pad_add_fusion.refs_0_, bf16[128,64]{1,0:T(8,128)(2,1)} %copy.23.refs_1_, ...), custom_call_target="tpu_custom_call" | custom-call | flops 15000000512 | bytes 20971520 | tf_op jit(solution)/shard_map/forward_layer/pallas_call | solution.py:600
  249.5 13.3 %forward_layer.7 = (f32[8192,128]{1,0:T(8,128)}, bf16[8192,128]{1,0:T(8,128)(2,1)}, bf16[8192,128]{1,0:T(8,128)(2,1)}, bf16[8192,128]{1,0:T(8,128)(2,1)}, f32[8,128]{1,0:T(8,128)}, /*index=5*/f32[8,128]{1,0:T(8,128)}) custom-call(s32[2,64]{1,0:T(2,128)} %pad_add_fusion.refs_0_, bf16[128,64]{1,0:T(8,128)(2,1)} %copy.21.refs_1_, ...), custom_call_target="tpu_custom_call" | custom-call | flops 15000000512 | bytes 20971520 | tf_op jit(solution)/shard_map/forward_layer/pallas_call | solution.py:600
  262.8 8.0 %all-to-all-done.1 = bf16[4,2048,128]{2,1,0:T(8,128)(2,1)S(1)} async-done(((bf16[4,2048,128]{2,1,0:T(8,128)(2,1)}), bf16[4,2048,128]{2,1,0:T(8,128)(2,1)S(1)}, u32[]{:S(2)}, u32[]{:S(2)}) %all-to-all-start.1) | async-done | bytes 2097184 | tf_op jit(solution)/shard_map/all_to_all | solution.py:956
  272.2 28.4 %backward_layer.4 = (f32[8192,128]{1,0:T(8,128)}, bf16[16,2,2,128,128]{4,3,2,1,0:T(8,128)(2,1)}, bf16[16,2,2,128,128]{4,3,2,1,0:T(8,128)(2,1)}) custom-call(s32[2,64]{1,0:T(2,128)} %pad_add_fusion.refs_0_, bf16[128,64]{1,0:T(8,128)(2,1)} %copy.21.refs_1_, bf16[128,64]{1,0:T(8,128)(2,1)} %copy.28.refs_2_, f32[8,128]{1,0:T(8,128)} %get-tuple-element.197.refs_3_, ...), custom_call_target="tpu_custom_call" | custom-call | flops 17999998976 | bytes 31457280 | tf_op jit(solution)/shard_map/backward_layer/pallas_call | solution.py:631
  301.7 19.0 %backward_layer.5 = (f32[8192,128]{1,0:T(8,128)}, bf16[16,2,2,128,128]{4,3,2,1,0:T(8,128)(2,1)}, bf16[16,2,2,128,128]{4,3,2,1,0:T(8,128)(2,1)}) custom-call(s32[2,64]{1,0:T(2,128)} %pad_add_fusion.refs_0_, bf16[128,64]{1,0:T(8,128)(2,1)} %copy.23.refs_1_, bf16[128,64]{1,0:T(8,128)(2,1)} %copy.28.refs_2_, f32[8,128]{1,0:T(8,128)} %get-tuple-element.191.refs_3_, ...), custom_call_target="tpu_custom_call" | custom-call | flops 17999998976 | bytes 31457280 | tf_op jit(solution)/shard_map/backward_layer/pallas_call | solution.py:631
  328.4 19.1 %backward_layer.6 = (f32[8192,128]{1,0:T(8,128)}, bf16[16,2,2,128,128]{4,3,2,1,0:T(8,128)(2,1)}, bf16[16,2,2,128,128]{4,3,2,1,0:T(8,128)(2,1)}) custom-call(s32[2,64]{1,0:T(2,128)} %pad_add_fusion.refs_0_, bf16[128,64]{1,0:T(8,128)(2,1)} %copy.25.refs_1_, bf16[128,64]{1,0:T(8,128)(2,1)} %copy.28.refs_2_, f32[8,128]{1,0:T(8,128)} %get-tuple-element.176.refs_3_, ...), custom_call_target="tpu_custom_call" | custom-call | flops 17999998976 | bytes 31457280 | tf_op jit(solution)/shard_map/backward_layer/pallas_call | solution.py:631
  357.9 18.1 %backward_layer.7 = (bf16[8192,128]{1,0:T(8,128)(2,1)}, bf16[16,2,2,128,128]{4,3,2,1,0:T(8,128)(2,1)}, bf16[16,2,2,128,128]{4,3,2,1,0:T(8,128)(2,1)}) custom-call(s32[2,64]{1,0:T(2,128)} %pad_add_fusion.refs_0_, bf16[128,64]{1,0:T(8,128)(2,1)} %copy.27.refs_1_, bf16[128,64]{1,0:T(8,128)(2,1)} %copy.28.refs_2_, f32[8,128]{1,0:T(8,128)} %get-tuple-element.166.refs_3_, ...), custom_call_target="tpu_custom_call" | custom-call | flops 17999998976 | bytes 31457280 | tf_op jit(solution)/shard_map/backward_layer/pallas_call | solution.py:631
  394.3 11.2 %collective-permute-done.37.refs_5_ = bf16[2048,128]{1,0:T(8,128)(2,1)S(1)} collective-permute-done((bf16[2048,128]{1,0:T(8,128)(2,1)}, bf16[2048,128]{1,0:T(8,128)(2,1)S(1)}, u32[]{:S(2)}, u32[]{:S(2)}) %collective-permute-start.37) | collective-permute-done | bytes 524320 | tf_op jit(solution)/shard_map/ppermute | solution.py:921
  405.5 11.0 %collective-permute-done.39.refs_7_ = bf16[2048,128]{1,0:T(8,128)(2,1)} collective-permute-done((bf16[2048,128]{1,0:T(8,128)(2,1)}, bf16[2048,128]{1,0:T(8,128)(2,1)}, u32[]{:S(2)}, u32[]{:S(2)}) %collective-permute-start.39) | collective-permute-done | bytes 524320 | tf_op jit(solution)/shard_map/ppermute | solution.py:921
  420.0 5.4 collective-permute-start.44
  433.4 15.5 %collective-permute-done.44.refs_0_ = bf16[1024,128]{1,0:T(8,128)(2,1)S(1)} collective-permute-done((bf16[1024,128]{1,0:T(8,128)(2,1)}, bf16[1024,128]{1,0:T(8,128)(2,1)S(1)}, u32[]{:S(2)}, u32[]{:S(2)}) %collective-permute-start.44) | collective-permute-done | bytes 262176 | tf_op jit(solution)/shard_map/ppermute | solution.py:921
  448.9 8.0 %collective-permute-done.45.refs_1_ = bf16[1024,128]{1,0:T(8,128)(2,1)S(1)} collective-permute-done((bf16[1024,128]{1,0:T(8,128)(2,1)}, bf16[1024,128]{1,0:T(8,128)(2,1)S(1)}, u32[]{:S(2)}, u32[]{:S(2)}) %collective-permute-start.45) | collective-permute-done | bytes 262176 | tf_op jit(solution)/shard_map/ppermute | solution.py:921
  468.5 11.2 %collective-permute-done.34.refs_1_ = bf16[2048,128]{1,0:T(8,128)(2,1)S(1)} collective-permute-done((bf16[2048,128]{1,0:T(8,128)(2,1)}, bf16[2048,128]{1,0:T(8,128)(2,1)S(1)}, u32[]{:S(2)}, u32[]{:S(2)}) %collective-permute-start.34) | collective-permute-done | bytes 524320 | tf_op jit(solution)/shard_map/ppermute | solution.py:921
  479.7 11.2 %collective-permute-done.35.refs_2_ = bf16[2048,128]{1,0:T(8,128)(2,1)} collective-permute-done((bf16[2048,128]{1,0:T(8,128)(2,1)}, bf16[2048,128]{1,0:T(8,128)(2,1)}, u32[]{:S(2)}, u32[]{:S(2)}) %collective-permute-start.35) | collective-permute-done | bytes 524320 | tf_op jit(solution)/shard_map/ppermute | solution.py:921
  502.7 4.9 collective-permute-start.43
  522.6 6.6 %collective-permute-done.43.refs_3_ = bf16[1024,128]{1,0:T(8,128)(2,1)} collective-permute-done((bf16[1024,128]{1,0:T(8,128)(2,1)}, bf16[1024,128]{1,0:T(8,128)(2,1)}, u32[]{:S(2)}, u32[]{:S(2)}) %collective-permute-start.43) | collective-permute-done | bytes 262176 | tf_op jit(solution)/shard_map/ppermute | solution.py:921
  536.5 5.8 %assemble.1 = (f32[4,16,128,128]{3,2,1,0:T(8,128)}, f32[4,16,128,128]{3,2,1,0:T(8,128)}) custom-call(s32[3]{0:T(128)} %pad_add_fusion.1.refs_0_, bf16[4,2,2,2,128,128]{5,4,3,2,1,0:T(8,128)(2,1)} %bitcast.62, bf16[4,2,2,2,128,128]{5,4,3,2,1,0:T(8,128)(2,1)} %bitcast.86, bf16[4,2,2,2,128,128]{5,4,3,2,1,0:T(8,128)(2,1)} %bitcast.61, ...), custom_call_target="tpu_custom_call" | custom-call | bytes 12582912 | tf_op jit(solution)/shard_map/assemble/pallas_call | solution.py:859
  (196 shorter events, 184.5 us)
Async XLA Ops:
  77.9 28.4 %collective-permute-start.9 = (bf16[8,1024,128]{2,1,0:T(8,128)(2,1)}, bf16[8,1024,128]{2,1,0:T(8,128)(2,1)}, u32[]{:S(2)}, u32[]{:S(2)}) collective-permute-start(bf16[8,1024,128]{2,1,0:T(8,128)(2,1)} %join.7), channel_id=1, source_target_pairs={{0,16},{1,9},{2,18},{3,11},{4,20},{5,13},{6,22},{7,15},{8,24},{9,1... | collective-permute-start | bytes 6291464 | tf_op jit(solution)/shard_map/ppermute | solution.py:921
  87.2 97.3 %all-to-all-start = ((bf16[4,2048,128]{2,1,0:T(8,128)(2,1)}), bf16[4,2048,128]{2,1,0:T(8,128)(2,1)}, u32[]{:S(2)}, u32[]{:S(2)}) async-start(bf16[4,2048,128]{2,1,0:T(8,128)(2,1)} %pick.2), calls=%async_computation | async-start | bytes 4194304 | tf_op jit(solution)/shard_map/all_to_all | solution.py:956
  92.0 92.6 %collective-permute-start.10 = (bf16[8,1024,128]{2,1,0:T(8,128)(2,1)S(1)}, bf16[8,1024,128]{2,1,0:T(8,128)(2,1)}, u32[]{:S(2)}, u32[]{:S(2)}) collective-permute-start(bf16[8,1024,128]{2,1,0:T(8,128)(2,1)S(1)} %copy-done.2), channel_id=1, source_target_pairs={{0,1},{1,0},{2,3},{3,2},{4,5},{5,4},{6,7},{7,6},{8,9},{9,8},{10,11... | collective-permute-start | bytes 6291464 | tf_op jit(solution)/shard_map/ppermute | solution.py:921
  106.3 78.2 %collective-permute-start.11 = (bf16[8,1024,128]{2,1,0:T(8,128)(2,1)}, bf16[8,1024,128]{2,1,0:T(8,128)(2,1)}, u32[]{:S(2)}, u32[]{:S(2)}) collective-permute-start(bf16[8,1024,128]{2,1,0:T(8,128)(2,1)} %collective-permute-done.9), channel_id=1, source_target_pairs={{0,1},{1,0},{2,3},{3,2},{4,5},{5,4},{6,7},{7,6},{8,9},{9,8},{10,11... | collective-permute-start | bytes 6291464 | tf_op jit(solution)/shard_map/ppermute | solution.py:921
  120.3 36.1 %collective-permute-start.13 = (bf16[1024,128]{1,0:T(8,128)(2,1)S(1)}, bf16[1024,128]{1,0:T(8,128)(2,1)S(1)}, u32[]{:S(2)}, u32[]{:S(2)}) collective-permute-start(bf16[1024,128]{1,0:T(8,128)(2,1)S(1)} %collective-permute-done.12), channel_id=1, source_target_pairs={{0,0},{1,1},{2,2},{3,3},{4,4},{5,5},{6,6},{7,7},{8,10},{9,11},{10,... | collective-permute-start | bytes 786440 | tf_op jit(solution)/shard_map/ppermute | solution.py:921
  130.2 28.2 %collective-permute-start.15 = (bf16[1024,128]{1,0:T(8,128)(2,1)S(1)}, bf16[1024,128]{1,0:T(8,128)(2,1)S(1)}, u32[]{:S(2)}, u32[]{:S(2)}) collective-permute-start(bf16[1024,128]{1,0:T(8,128)(2,1)S(1)} %collective-permute-done.14), channel_id=1, source_target_pairs={{0,2},{1,3},{2,0},{3,1},{4,6},{5,7},{6,4},{7,5},{8,8},{9,9},{10,10... | collective-permute-start | bytes 786440 | tf_op jit(solution)/shard_map/ppermute | solution.py:921
  132.1 26.2 %collective-permute-start.17 = (bf16[1024,128]{1,0:T(8,128)(2,1)S(1)}, bf16[1024,128]{1,0:T(8,128)(2,1)S(1)}, u32[]{:S(2)}, u32[]{:S(2)}) collective-permute-start(bf16[1024,128]{1,0:T(8,128)(2,1)S(1)} %collective-permute-done.16), channel_id=1, source_target_pairs={{0,4},{1,5},{2,6},{3,7},{4,0},{5,1},{6,2},{7,3},{8,14},{9,15},{10,... | collective-permute-start | bytes 786440 | tf_op jit(solution)/shard_map/ppermute | solution.py:921
  184.5 22.0 %collective-permute-start.22 = (bf16[8,1024,128]{2,1,0:T(8,128)(2,1)}, bf16[8,1024,128]{2,1,0:T(8,128)(2,1)S(1)}, u32[]{:S(2)}, u32[]{:S(2)}) collective-permute-start(bf16[8,1024,128]{2,1,0:T(8,128)(2,1)} %join.9), channel_id=1, source_target_pairs={{0,1},{1,0},{2,3},{3,2},{4,5},{5,4},{6,7},{7,6},{8,9},{9,8},{10,11... | collective-permute-start | bytes 6291464 | tf_op jit(solution)/shard_map/ppermute | solution.py:921
  189.1 25.5 %collective-permute-start.21 = (bf16[8,1024,128]{2,1,0:T(8,128)(2,1)}, bf16[8,1024,128]{2,1,0:T(8,128)(2,1)}, u32[]{:S(2)}, u32[]{:S(2)}) collective-permute-start(bf16[8,1024,128]{2,1,0:T(8,128)(2,1)} %join.9), channel_id=1, source_target_pairs={{0,16},{1,9},{2,18},{3,11},{4,20},{5,13},{6,22},{7,15},{8,24},{9,1... | collective-permute-start | bytes 6291464 | tf_op jit(solution)/shard_map/ppermute | solution.py:921
  214.6 21.4 %collective-permute-start.23 = (bf16[8,1024,128]{2,1,0:T(8,128)(2,1)}, bf16[8,1024,128]{2,1,0:T(8,128)(2,1)}, u32[]{:S(2)}, u32[]{:S(2)}) collective-permute-start(bf16[8,1024,128]{2,1,0:T(8,128)(2,1)} %collective-permute-done.21), channel_id=1, source_target_pairs={{0,1},{1,0},{2,3},{3,2},{4,5},{5,4},{6,7},{7,6},{8,9},{9,8},{10,11... | collective-permute-start | bytes 6291464 | tf_op jit(solution)/shard_map/ppermute | solution.py:921
  218.5 52.3 %all-to-all-start.1 = ((bf16[4,2048,128]{2,1,0:T(8,128)(2,1)}), bf16[4,2048,128]{2,1,0:T(8,128)(2,1)S(1)}, u32[]{:S(2)}, u32[]{:S(2)}) async-start(bf16[4,2048,128]{2,1,0:T(8,128)(2,1)} %pick.3), calls=%async_computation.1 | async-start | bytes 4194304 | tf_op jit(solution)/shard_map/all_to_all | solution.py:956
  322.0 27.9 %collective-permute-start.28 = (bf16[16,2,2,128,128]{4,3,2,1,0:T(8,128)(2,1)}, bf16[16,2,2,128,128]{4,3,2,1,0:T(8,128)(2,1)S(1)}, u32[]{:S(2)}, u32[]{:S(2)}) collective-permute-start(bf16[16,2,2,128,128]{4,3,2,1,0:T(8,128)(2,1)} %get-tuple-element.220), channel_id=1, source_target_pairs={{0,1},{1,0},{2,3},{3,2},{4,5},{5,4},{6,7},{7,6},{8,9},{9,8},{10,11... | collective-permute-start | bytes 6291464 | tf_op jit(solution)/shard_map/ppermute | solution.py:921
  325.7 21.7 %collective-permute-start.25 = (bf16[2048,128]{1,0:T(8,128)(2,1)}, bf16[2048,128]{1,0:T(8,128)(2,1)S(1)}, u32[]{:S(2)}, u32[]{:S(2)}) collective-permute-start(bf16[2048,128]{1,0:T(8,128)(2,1)} %get-tuple-element.216), channel_id=1, source_target_pairs={{0,8},{1,9},{2,10},{3,11},{4,12},{5,13},{6,14},{7,15},{8,0},{9,1},... | collective-permute-start | bytes 1572872 | tf_op jit(solution)/shard_map/ppermute | solution.py:921
  325.7 21.7 %collective-permute-start.26 = (bf16[2048,128]{1,0:T(8,128)(2,1)}, bf16[2048,128]{1,0:T(8,128)(2,1)S(1)}, u32[]{:S(2)}, u32[]{:S(2)}) collective-permute-start(bf16[2048,128]{1,0:T(8,128)(2,1)} %get-tuple-element.217), channel_id=1, source_target_pairs={{0,16},{1,17},{2,18},{3,19},{4,20},{5,21},{6,22},{7,23},{8,24},{9,... | collective-permute-start | bytes 1572872 | tf_op jit(solution)/shard_map/ppermute | solution.py:921
  327.0 22.9 %collective-permute-start.27 = (bf16[2048,128]{1,0:T(8,128)(2,1)}, bf16[2048,128]{1,0:T(8,128)(2,1)S(1)}, u32[]{:S(2)}, u32[]{:S(2)}) collective-permute-start(bf16[2048,128]{1,0:T(8,128)(2,1)} %get-tuple-element.218), channel_id=1, source_target_pairs={{0,24},{1,25},{2,26},{3,27},{4,28},{5,29},{6,30},{7,31},{8,16},{9,... | collective-permute-start | bytes 1572872 | tf_op jit(solution)/shard_map/ppermute | solution.py:921
  350.0 30.0 %collective-permute-start.32 = (bf16[16,2,2,128,128]{4,3,2,1,0:T(8,128)(2,1)}, bf16[16,2,2,128,128]{4,3,2,1,0:T(8,128)(2,1)}, u32[]{:S(2)}, u32[]{:S(2)}) collective-permute-start(bf16[16,2,2,128,128]{4,3,2,1,0:T(8,128)(2,1)} %get-tuple-element.236), channel_id=1, source_target_pairs={{0,1},{1,0},{2,3},{3,2},{4,5},{5,4},{6,7},{7,6},{8,9},{9,8},{10,11... | collective-permute-start | bytes 6291464 | tf_op jit(solution)/shard_map/ppermute | solution.py:921
  355.3 20.8 %collective-permute-start.29 = (bf16[2048,128]{1,0:T(8,128)(2,1)}, bf16[2048,128]{1,0:T(8,128)(2,1)S(1)}, u32[]{:S(2)}, u32[]{:S(2)}) collective-permute-start(bf16[2048,128]{1,0:T(8,128)(2,1)} %get-tuple-element.232), channel_id=1, source_target_pairs={{0,8},{1,9},{2,10},{3,11},{4,12},{5,13},{6,14},{7,15},{8,0},{9,1},... | collective-permute-start | bytes 1572872 | tf_op jit(solution)/shard_map/ppermute | solution.py:921
  356.7 23.2 %collective-permute-start.31 = (bf16[2048,128]{1,0:T(8,128)(2,1)}, bf16[2048,128]{1,0:T(8,128)(2,1)S(1)}, u32[]{:S(2)}, u32[]{:S(2)}) collective-permute-start(bf16[2048,128]{1,0:T(8,128)(2,1)} %get-tuple-element.234), channel_id=1, source_target_pairs={{0,24},{1,25},{2,26},{3,27},{4,28},{5,29},{6,30},{7,31},{8,16},{9,... | collective-permute-start | bytes 1572872 | tf_op jit(solution)/shard_map/ppermute | solution.py:921
  380.8 126.9 %all-to-all-start.2 = ((bf16[4,2048,128]{2,1,0:T(8,128)(2,1)}), bf16[4,2048,128]{2,1,0:T(8,128)(2,1)S(1)}, u32[]{:S(2)}, u32[]{:S(2)}) async-start(bf16[4,2048,128]{2,1,0:T(8,128)(2,1)} %bitcast.73), calls=%async_computation.2 | async-start | bytes 4194304 | tf_op jit(solution)/shard_map/all_to_all | solution.py:956
  384.6 77.6 %collective-permute-start.33 = (bf16[16,2,2,128,128]{4,3,2,1,0:T(8,128)(2,1)}, bf16[16,2,2,128,128]{4,3,2,1,0:T(8,128)(2,1)}, u32[]{:S(2)}, u32[]{:S(2)}) collective-permute-start(bf16[16,2,2,128,128]{4,3,2,1,0:T(8,128)(2,1)} %get-tuple-element.239), channel_id=1, source_target_pairs={{0,1},{1,0},{2,3},{3,2},{4,5},{5,4},{6,7},{7,6},{8,9},{9,8},{10,11... | collective-permute-start | bytes 6291464 | tf_op jit(solution)/shard_map/ppermute | solution.py:921
  393.0 23.5 %collective-permute-start.39 = (bf16[2048,128]{1,0:T(8,128)(2,1)}, bf16[2048,128]{1,0:T(8,128)(2,1)}, u32[]{:S(2)}, u32[]{:S(2)}) collective-permute-start(bf16[2048,128]{1,0:T(8,128)(2,1)} %get-tuple-element.249), channel_id=1, source_target_pairs={{0,24},{1,25},{2,26},{3,27},{4,28},{5,29},{6,30},{7,31},{8,16},{9,... | collective-permute-start | bytes 1572872 | tf_op jit(solution)/shard_map/ppermute | solution.py:921
  420.0 29.0 %collective-permute-start.44 = (bf16[1024,128]{1,0:T(8,128)(2,1)}, bf16[1024,128]{1,0:T(8,128)(2,1)S(1)}, u32[]{:S(2)}, u32[]{:S(2)}) collective-permute-start(bf16[1024,128]{1,0:T(8,128)(2,1)} %get-tuple-element.274), channel_id=1, source_target_pairs={{0,0},{1,1},{2,10},{3,11},{4,20},{5,21},{6,30},{7,31},{8,2},{9,3},... | collective-permute-start | bytes 786440 | tf_op jit(solution)/shard_map/ppermute | solution.py:921
  425.4 31.5 %collective-permute-start.45 = (bf16[1024,128]{1,0:T(8,128)(2,1)}, bf16[1024,128]{1,0:T(8,128)(2,1)S(1)}, u32[]{:S(2)}, u32[]{:S(2)}) collective-permute-start(bf16[1024,128]{1,0:T(8,128)(2,1)} %get-tuple-element.275), channel_id=1, source_target_pairs={{0,2},{1,3},{2,8},{3,9},{4,22},{5,23},{6,28},{7,29},{8,0},{9,1},{1... | collective-permute-start | bytes 786440 | tf_op jit(solution)/shard_map/ppermute | solution.py:921
  429.2 27.7 %collective-permute-start.46 = (bf16[1024,128]{1,0:T(8,128)(2,1)}, bf16[1024,128]{1,0:T(8,128)(2,1)S(1)}, u32[]{:S(2)}, u32[]{:S(2)}) collective-permute-start(bf16[1024,128]{1,0:T(8,128)(2,1)} %get-tuple-element.276), channel_id=1, source_target_pairs={{0,4},{1,5},{2,14},{3,15},{4,16},{5,17},{6,26},{7,27},{8,6},{9,7},... | collective-permute-start | bytes 786440 | tf_op jit(solution)/shard_map/ppermute | solution.py:921
  431.2 26.0 %collective-permute-start.47 = (bf16[1024,128]{1,0:T(8,128)(2,1)}, bf16[1024,128]{1,0:T(8,128)(2,1)S(1)}, u32[]{:S(2)}, u32[]{:S(2)}) collective-permute-start(bf16[1024,128]{1,0:T(8,128)(2,1)} %get-tuple-element.277), channel_id=1, source_target_pairs={{0,6},{1,7},{2,12},{3,13},{4,18},{5,19},{6,24},{7,25},{8,4},{9,5},... | collective-permute-start | bytes 786440 | tf_op jit(solution)/shard_map/ppermute | solution.py:921
  460.6 52.2 %collective-permute-start.48 = (bf16[4096,128]{1,0:T(8,128)(2,1)}, bf16[4096,128]{1,0:T(8,128)(2,1)S(1)}, u32[]{:S(2)}, u32[]{:S(2)}) collective-permute-start(bf16[4096,128]{1,0:T(8,128)(2,1)} %join.10), channel_id=1, source_target_pairs={{0,1},{1,0},{2,3},{3,2},{4,5},{5,4},{6,7},{7,6},{8,9},{9,8},{10,11... | collective-permute-start | bytes 3145736 | tf_op jit(solution)/shard_map/ppermute | solution.py:921
  465.8 25.1 %collective-permute-start.35 = (bf16[2048,128]{1,0:T(8,128)(2,1)}, bf16[2048,128]{1,0:T(8,128)(2,1)}, u32[]{:S(2)}, u32[]{:S(2)}) collective-permute-start(bf16[2048,128]{1,0:T(8,128)(2,1)} %get-tuple-element.242), channel_id=1, source_target_pairs={{0,16},{1,17},{2,18},{3,19},{4,20},{5,21},{6,22},{7,23},{8,24},{9,... | collective-permute-start | bytes 1572872 | tf_op jit(solution)/shard_map/ppermute | solution.py:921
  465.8 25.1 %collective-permute-start.36 = (bf16[2048,128]{1,0:T(8,128)(2,1)}, bf16[2048,128]{1,0:T(8,128)(2,1)}, u32[]{:S(2)}, u32[]{:S(2)}) collective-permute-start(bf16[2048,128]{1,0:T(8,128)(2,1)} %get-tuple-element.243), channel_id=1, source_target_pairs={{0,24},{1,25},{2,26},{3,27},{4,28},{5,29},{6,30},{7,31},{8,16},{9,... | collective-permute-start | bytes 1572872 | tf_op jit(solution)/shard_map/ppermute | solution.py:921
  494.4 22.2 %collective-permute-start.40 = (bf16[1024,128]{1,0:T(8,128)(2,1)}, bf16[1024,128]{1,0:T(8,128)(2,1)S(1)}, u32[]{:S(2)}, u32[]{:S(2)}) collective-permute-start(bf16[1024,128]{1,0:T(8,128)(2,1)} %get-tuple-element.262), channel_id=1, source_target_pairs={{0,0},{1,1},{2,10},{3,11},{4,20},{5,21},{6,30},{7,31},{8,2},{9,3},... | collective-permute-start | bytes 786440 | tf_op jit(solution)/shard_map/ppermute | solution.py:921
  497.6 23.3 %collective-permute-start.41 = (bf16[1024,128]{1,0:T(8,128)(2,1)}, bf16[1024,128]{1,0:T(8,128)(2,1)}, u32[]{:S(2)}, u32[]{:S(2)}) collective-permute-start(bf16[1024,128]{1,0:T(8,128)(2,1)} %get-tuple-element.263), channel_id=1, source_target_pairs={{0,2},{1,3},{2,8},{3,9},{4,22},{5,23},{6,28},{7,29},{8,0},{9,1},{1... | collective-permute-start | bytes 786440 | tf_op jit(solution)/shard_map/ppermute | solution.py:921
  500.8 21.8 %collective-permute-start.42 = (bf16[1024,128]{1,0:T(8,128)(2,1)}, bf16[1024,128]{1,0:T(8,128)(2,1)}, u32[]{:S(2)}, u32[]{:S(2)}) collective-permute-start(bf16[1024,128]{1,0:T(8,128)(2,1)} %get-tuple-element.264), channel_id=1, source_target_pairs={{0,4},{1,5},{2,14},{3,15},{4,16},{5,17},{6,26},{7,27},{8,6},{9,7},... | collective-permute-start | bytes 786440 | tf_op jit(solution)/shard_map/ppermute | solution.py:921
  502.7 26.4 %collective-permute-start.43 = (bf16[1024,128]{1,0:T(8,128)(2,1)}, bf16[1024,128]{1,0:T(8,128)(2,1)}, u32[]{:S(2)}, u32[]{:S(2)}) collective-permute-start(bf16[1024,128]{1,0:T(8,128)(2,1)} %get-tuple-element.265), channel_id=1, source_target_pairs={{0,6},{1,7},{2,12},{3,13},{4,18},{5,19},{6,24},{7,25},{8,4},{9,5},... | collective-permute-start | bytes 786440 | tf_op jit(solution)/shard_map/ppermute | solution.py:921
  (58 other events, 712.8 us)

commit v6 on v5

--- a/solution.py
+++ b/solution.py
@@ -296,12 +296,6 @@
     return pl.ds(pl.multiple_of(block * size, size), size)
 
 
-def column(gain_ref, block, slots):
-    blocks = gain_ref.shape[1]
-    picked = lax.broadcasted_iota(jnp.int32, (blocks, slots), 0) == block
-    return inner_dot(gain_ref[...], picked.astype(jnp.bfloat16), 1, 0)
-
-
 def chunk_copy(source, target, sems, chunk):
     rows = target.shape[0] // CHUNKS
     at = pl.ds(pl.multiple_of(chunk * rows, rows), rows)
@@ -354,11 +348,11 @@
     return lax.fori_loop(0, CHUNKS, one, carry)
 
 
-def forward_kernel(first, layer, inputs, table_ref, gain_ref, sums_ref, *refs):
+def forward_kernel(first, layer, inputs, table_ref, sums_ref, gain_ref, *refs):
     sources, refs = refs[:inputs], refs[inputs:]
     parts, sources = sources[:PARTS], sources[PARTS:]
     out_ref, u_ref, z_ref, slope_ref, scale_ref, next_ref = refs[:6]
-    raw, h, w, u, z, slope, mid, in_sems, w_sems, out_sems = refs[6:]
+    raw, h, w, u, z, slope, mid, gain, in_sems, gain_sems, w_sems, out_sems = refs[6:]
     features, slots = h.shape
     size = w.shape[-1]
     chunk_blocks = w.shape[2]
@@ -369,7 +363,10 @@
     right_in = factor_copies(parts, layer, w, w_sems, 1)
     if first:
         start_chunks(sources[0], raw, in_sems)
-        for copy in left_in + right_in:
+        for copy in left_in:
+            copy.start()
+        start_chunks(gain_ref, gain, gain_sems)
+        for copy in right_in:
             copy.start()
 
         def squares(block, total):
@@ -388,6 +385,7 @@
         for copy in left_in:
             copy.start()
         start_chunks(sources[0], h, in_sems)
+        start_chunks(gain_ref, gain, gain_sems)
         for copy in right_in:
             copy.start()
         total = sums_ref[...]
@@ -397,13 +395,14 @@
         copy.wait()
 
     def arrive(chunk):
+        chunk_copy(gain_ref, gain, gain_sems, chunk).wait()
         if not first:
             chunk_copy(sources[0], h, in_sems, chunk).wait()
 
     def left(block, carry):
         rows = block_rows(block, size)
         place = table_ref[0, block]
-        normed = (h[rows, :] * scale * column(gain_ref, block, slots)).astype(jnp.bfloat16)
+        normed = (h[rows, :] * scale * gain[rows, :].astype(jnp.float32)).astype(jnp.bfloat16)
         u[rows, :] = normed
         weight = w[place // chunk_blocks, 0, place % chunk_blocks]
         mid[rows, :] = inner_dot(weight, normed, 0, 0)
@@ -446,13 +445,13 @@
         wait_chunks(source, target, out_sems.at[at])
 
 
-def backward_kernel(turning, last, layer, inputs, table_ref, gain_ref, end_gain_ref, scale_ref, *refs):
+def backward_kernel(turning, last, layer, inputs, table_ref, scale_ref, gain_ref, end_gain_ref, *refs):
     sources, refs = refs[:inputs], refs[inputs:]
     slope_ref, z_ref, u_ref = sources[:3]
     parts, sources = sources[3 : 3 + PARTS], sources[3 + PARTS :]
     out_ref, own_grad, peer_grad = refs[:3]
-    g, slope, z, u, h, w, gw, mid, turned, top, goal = refs[3:14]
-    in_sems, w_sems, out_sems, gw_sems = refs[14:]
+    g, slope, z, u, h, w, gw, mid, turned, gain, top, goal, end_gain = refs[3:16]
+    in_sems, w_sems, out_sems, gw_sems = refs[16:]
     features, slots = g.shape
     size = w.shape[-1]
     chunk_blocks = w.shape[2]
@@ -464,6 +463,7 @@
     g_ref, h_ref = sources[:2]
     if turning:
         start_chunks(g_ref, top, in_sems.at[0])
+        start_chunks(end_gain_ref, end_gain, in_sems.at[6])
         start_chunks(sources[2], goal, in_sems.at[5])
     else:
         start_chunks(g_ref, g, in_sems.at[0])
@@ -474,6 +474,7 @@
     for copy in left_in:
         copy.start()
     start_chunks(u_ref, u, in_sems.at[3])
+    start_chunks(gain_ref, gain, in_sems.at[7])
     start_chunks(h_ref, h, in_sems.at[4])
 
     if turning:
@@ -482,7 +483,7 @@
         def sums(block, totals):
             rows = block_rows(block, size)
             part = top[rows, :]
-            scaled = part * column(end_gain_ref, block, slots)
+            scaled = part * end_gain[rows, :].astype(jnp.float32)
             return (
                 totals[0] + fold_rows(part * part),
                 totals[1] + fold_rows(scaled * scaled),
@@ -491,6 +492,7 @@
 
         def arrive_top(chunk):
             chunk_copy(g_ref, top, in_sems.at[0], chunk).wait()
+            chunk_copy(end_gain_ref, end_gain, in_sems.at[6], chunk).wait()
             chunk_copy(sources[2], goal, in_sems.at[5], chunk).wait()
 
         totals = by_chunk(blocks, sums, (zero, zero, zero), arrive_top)
@@ -514,8 +516,8 @@
         to = (home // chunk_blocks, 1, home % chunk_blocks)
         if turning:
             part = top[rows, :]
-            gain = column(end_gain_ref, block, slots)
-            error = (part * end_scale * gain - goal[rows, :].astype(jnp.float32)) * gain
+            factor = end_gain[rows, :].astype(jnp.float32)
+            error = (part * end_scale * factor - goal[rows, :].astype(jnp.float32)) * factor
             gradient = end_scale * error - part * end_back
             g[rows, :] = gradient
         else:
@@ -535,6 +537,7 @@
 
     def arrive_left(chunk):
         chunk_copy(u_ref, u, in_sems.at[3], chunk).wait()
+        chunk_copy(gain_ref, gain, in_sems.at[7], chunk).wait()
         chunk_copy(h_ref, h, in_sems.at[4], chunk).wait()
 
     def left(block, total):
@@ -549,7 +552,7 @@
             ]
         arrived = turned[slot].astype(jnp.bfloat16)
         gw[to] = inner_dot(u[rows, :], arrived, 1, 1).astype(jnp.bfloat16)
-        weighted = inner_dot(w[at], arrived, 1, 0) * column(gain_ref, block, slots)
+        weighted = inner_dot(w[at], arrived, 1, 0) * gain[rows, :].astype(jnp.float32)
         g[rows, :] = g[rows, :] + scale * weighted
         return total + fold_rows(weighted * h[rows, :].astype(jnp.float32))
 
@@ -599,7 +602,7 @@
     )
     return pl.pallas_call(
         lambda *refs: forward_kernel(first, layer, len(sources), *refs),
-        in_specs=[SMEM, INSIDE, INSIDE] + [OUTSIDE] * len(sources),
+        in_specs=[SMEM, INSIDE, OUTSIDE] + [OUTSIDE] * len(sources),
         out_specs=[OUTSIDE] * 4 + [INSIDE] * 2,
         out_shape=out_shape,
         scratch_shapes=[
@@ -610,6 +613,8 @@
             pltpu.VMEM(whole, jnp.bfloat16),
             pltpu.VMEM(whole, jnp.bfloat16),
             pltpu.VMEM(whole, jnp.float32),
+            pltpu.VMEM(whole, jnp.bfloat16),
+            pltpu.SemaphoreType.DMA((CHUNKS,)),
             pltpu.SemaphoreType.DMA((CHUNKS,)),
             pltpu.SemaphoreType.DMA((2, PARTS)),
             pltpu.SemaphoreType.DMA((4, CHUNKS)),
@@ -619,7 +624,7 @@
             flops=FORWARD_COST, bytes_accessed=20 * whole[0] * whole[1], transcendentals=0
         ),
         name="forward_layer",
-    )(table, gain, sums, *sources)
+    )(table, sums, gain, *sources)
 
 
 def run_backward(table, gain, end_gain, scale, kept, weights, layer, sources, turning, last):
@@ -630,7 +635,7 @@
     out_shape = [shape_of(whole, jnp.bfloat16 if last else jnp.float32)] + [shape_of(half, jnp.bfloat16)] * 2
     return pl.pallas_call(
         lambda *refs: backward_kernel(turning, last, layer, len(sources), *refs),
-        in_specs=[SMEM] + [INSIDE] * 3 + [OUTSIDE] * len(sources),
+        in_specs=[SMEM, INSIDE] + [OUTSIDE] * (2 + len(sources)),
         out_specs=[OUTSIDE] * len(out_shape),
         out_shape=out_shape,
         scratch_shapes=[
@@ -643,9 +648,11 @@
             pltpu.VMEM(held, jnp.bfloat16),
             pltpu.VMEM(whole, jnp.float32),
             pltpu.VMEM((8, held[-1], whole[1]), jnp.float32),
+            pltpu.VMEM(whole, jnp.bfloat16),
             pltpu.VMEM(whole if turning else SMALL, jnp.float32),
             pltpu.VMEM(whole if turning else SMALL, jnp.bfloat16),
-            pltpu.SemaphoreType.DMA((6, CHUNKS)),
+            pltpu.VMEM(whole if turning else SMALL, jnp.bfloat16),
+            pltpu.SemaphoreType.DMA((8, CHUNKS)),
             pltpu.SemaphoreType.DMA((2, PARTS)),
             pltpu.SemaphoreType.DMA((CHUNKS,)),
             pltpu.SemaphoreType.DMA((2, PARTS)),
@@ -655,7 +662,7 @@
             flops=BACKWARD_COST, bytes_accessed=30 * whole[0] * whole[1], transcendentals=0
         ),
         name="backward_layer",
-    )(table, gain, end_gain, scale, *sources)
+    )(table, scale, gain, end_gain, *sources)
 
 
 def copies_kernel(plan, inputs, outputs, *refs):
@@ -955,41 +962,45 @@
     def to_planes(value):
         return lax.all_to_all(value, "tensor", split_axis=0, concat_axis=0, tiled=True)
 
-    patch_sent = run_pick(critic_pairs, patches, width, wide)
     factors = (left_factors[0], right_factors[0])
     groups = [tuple(range(0, 2)), tuple(range(2, layer_count))]
     gain_rows = norm_gains[0].reshape(-1, size)
     pieces = factor_pieces(place, *factors, gain_rows, groups, chunk)
 
+    group_rows = [len(group) * layer_rows for group in groups]
+
+    def lowest_of(came, at):
+        return joined(came, group_rows[at]).reshape(width, group_rows[at], size)
+
+    near = move_all(pieces[0], "spread")
+    patch_sent = run_pick(critic_pairs, patches, width, wide)
+    near, patch_sent, pieces[1] = tie((near, patch_sent, pieces[1]))
     patch_came = to_planes(patch_sent).reshape(-1, wide)
-    near = [move_all(pieces[0], "spread")]
-    near[0], pieces[1] = tie((near[0], pieces[1]))
-    came = [move_all(near[0], "lift")]
-    near.append(move_all(pieces[1], "spread"))
-    group_rows = [len(group) * layer_rows for group in groups]
-
-    def lowest_of(at):
-        mine = joined(came[at], group_rows[at])
-        return mine.reshape(width, group_rows[at], size)
-
-    gains = jnp.stack([value[group_rows[0] :] for value in came[0]])[jnp.arange(width) ^ section ^ tensor]
-    gains = gains.reshape(width, layer_count + 1, local_blocks, size).transpose(1, 3, 0, 2)
-    gains = gains.reshape(layer_count + 1, size, blocks)
-    pair = gather_one(lowest_of(0))
-    came.append(move_all(near[1], "lift"))
-    weights = [as_weights(gather_three(*gather_two(pair)))]
-    later = gather_one(lowest_of(1))
+    came = move_all(near, "lift")
+    far = move_all(pieces[1], "spread")
+    came, far = tie((came, far))
+    lowest = lowest_of(came, 0)
+    beside = move(lowest, routes["across"][0])
+    late = move_all(far, "lift")
+    gains = jnp.stack([value[group_rows[0] :] for value in came])[jnp.arange(width) ^ section ^ tensor]
+    gains = gains.reshape(width, layer_count + 1, feat_local).transpose(1, 0, 2).reshape(layer_count + 1, -1)
+    lowest, beside, late, patch_came = tie((lowest, beside, late, patch_came))
+    first_two = gather_two(joined([lowest, beside]))
+    columns = [jnp.broadcast_to(gain[:, None], (gain.shape[0], wide)) for gain in gains]
     target_sent = run_pick(critic_pairs, teacher, width, wide)
+    first_two, late, columns, target_sent = tie((first_two, late, columns, target_sent))
+    weights = [as_weights(gather_three(*first_two))]
+    later = gather_one(lowest_of(late, 1))
 
     residual = patch_came
-    residual, weights, later, target_sent = tie((residual, weights, later, target_sent))
+    residual, weights, later = tie((residual, weights, later))
     flying = gather_two(later)
     sums = jnp.zeros((8, wide), jnp.float32)
     stored = []
     for layer in range(layer_count):
         group = 0 if layer in groups[0] else 1
         following, u, z, slope, scale, sums = run_forward(
-            table, gains[layer], sums, residual, weights[group], layer - groups[group][0]
+            table, columns[layer], sums, residual, weights[group], layer - groups[group][0]
         )
         stored.append(((slope, z, u), scale, residual))
         residual = following
@@ -1025,8 +1036,8 @@
         underway = [(at + 1, steps[at](*state)) if at < len(steps) else (at, state) for at, state in underway]
         gradient, mine, other = run_backward(
             table,
-            gains[layer],
-            gains[layer_count],
+            columns[layer],
+            columns[layer_count],
             scale,
             kept,
             weights[group],
@@ -1040,15 +1051,13 @@
         underway.append((0, (mine, other)))
 
     returned = to_planes(gradient.reshape(width, feat_local, wide))
-    homes_of = [None, None]
-    ended = []
-    for at, state in underway:
-        for step in steps[at:]:
-            state = step(*state)
-        ended.insert(0, state)
-    ended[1:] = tie(ended[1:])
-    homes_of[1] = both_halves(homeward(ended[groups[1][0] :]))
+    ended = [steps[at](*state) if at < len(steps) else state for at, state in underway][::-1]
+    ended = tie(ended)
+    ended[0] = plane_sum(*ended[0])
+    homes_of = [None, homeward(ended[groups[1][0] :])]
+    returned, ended[: groups[1][0]], homes_of[1] = tie((returned, ended[: groups[1][0]], homes_of[1]))
     home = homeward(ended[: groups[1][0]])
+    homes_of[1] = both_halves(homes_of[1])
     d_patches = run_combine(critic_pairs, returned)
     d_patches, home, homes_of[1] = tie((d_patches, home, homes_of[1]))
     homes_of[0] = both_halves(home)

time: 545 us -> 540 us (level)
  starting transfers between devices: 125 us -> 113 us
  Pallas kernels: 196 us -> 188 us
  waiting for transfers between devices: 195 us -> 203 us
  local copies, waits for them, and re-layouts: 22.8 us -> 30.5 us
    ppermute x50, starting transfers between devices: 112 us -> 100 us  [move(): return lax.ppermute(value, AXES, route)]
    broadcast_in_dim x0 -> x5, local copies, waits for them, and re-layouts: none -> 11 us  [plane_shards(): jnp.broadcast_to(gain[:, None], (gain.shape[0], wide))]
    pallas_call x4, Pallas kernels: 84.5 us -> 77.7 us  [run_backward(): pl.pallas_call(lambda *refs: backward_kernel(turning, last, layer, len(so...]
    unnamed x75 -> x92, local copies, waits for them, and re-layouts: 12.8 us -> 14.1 us
  transfers between devices with their start and end apart: 53 -> 53, of which waited for: 26 -> 24; matrix products, arithmetic and copies ran while one was open for 2% -> 1% of each run, Pallas kernels for 28% -> 28%
where the time goes in v6:
time: 540 us; the launch traced here: 537 us
  waiting for transfers between devices  203 us (38%)
  Pallas kernels  188 us (35%)
  starting transfers between devices  113 us (21%)
  local copies, waits for them, and re-layouts  30.5 us (6%)
    ppermute x50, waiting for transfers between devices, move(): return lax.ppermute(value, AXES, route)  192 us
    ppermute x50, starting transfers between devices, move(): return lax.ppermute(value, AXES, route)  100 us
    pallas_call x4, Pallas kernels, run_backward(): pl.pallas_call(lambda *refs: backward_kernel(turning, last, layer, len(so...  77.7 us
    pallas_call x4, Pallas kernels, run_forward(): pl.pallas_call(lambda *refs: forward_kernel(first, layer, len(sources), *...  51.6 us
    pallas_call x6, Pallas kernels, run_sum(): pl.pallas_call(lambda *refs: sum_kernel(len(groups[0]), len(flat), *refs)...  21.6 us
    pallas_call x7, Pallas kernels, run_copies(): pl.pallas_call(lambda *refs: copies_kernel(plan, len(extra) + len(inputs)...  19.6 us
    unnamed x92, local copies, waits for them, and re-layouts  14.1 us
    all_to_all x3, starting transfers between devices, to_planes(): lax.all_to_all(value, 'tensor', split_axis=0, concat_axis=0, tiled=True)  12.7 us
  transfers between devices with their start and end apart: 53, of which 24 were waited for; matrix products, arithmetic and copies ran while one was open for 1% of the time, Pallas kernels for 28%

profile of v6, /device:TPU:5, one launch (start us, length us, event | category | flops | bytes accessed | tf_op | source)
XLA Modules:
  0.0 537.4 jit_solution(5930665712765209655)
XLA Ops:
  2.6 4.2 pieces.1
  21.8 5.4 %collective-permute-done.2 = bf16[1104,128]{1,0:T(8,128)(2,1)} collective-permute-done((bf16[1104,128]{1,0:T(8,128)(2,1)}, bf16[1104,128]{1,0:T(8,128)(2,1)}, u32[]{:S(2)}, u32[]{:S(2)}) %collective-permute-start.2) | collective-permute-done | bytes 282656 | tf_op jit(solution)/shard_map/ppermute | solution.py:928
  27.9 5.1 all-to-all-start
  40.6 4.2 collective-permute-start.4
  52.4 4.9 collective-permute-start.11
  57.3 4.4 collective-permute-done.11
  61.7 37.2 %collective-permute-done.4.refs_0_ = bf16[1104,128]{1,0:T(8,128)(2,1)S(1)} collective-permute-done((bf16[1104,128]{1,0:T(8,128)(2,1)S(1)}, bf16[1104,128]{1,0:T(8,128)(2,1)S(1)}, u32[]{:S(2)}, u32[]{:S(2)}) %collective-permute-start.4) | collective-permute-done | bytes 282656 | tf_op jit(solution)/shard_map/ppermute | solution.py:928
  103.5 8.7 %collective-permute-start.13 = (bf16[1024,128]{1,0:T(8,128)(2,1)}, bf16[1024,128]{1,0:T(8,128)(2,1)S(1)}, u32[]{:S(2)}, u32[]{:S(2)}) collective-permute-start(bf16[1024,128]{1,0:T(8,128)(2,1)} %copy-done.37), channel_id=1, source_target_pairs={{0,0},{1,1},{2,2},{3,3},{4,4},{5,5},{6,6},{7,7},{8,10},{9,11},{10,... | collective-permute-start | bytes 786440 | tf_op jit(solution)/shard_map/ppermute | solution.py:928
  118.6 10.9 %collective-permute-done.13.refs_0_ = bf16[1024,128]{1,0:T(8,128)(2,1)S(1)} collective-permute-done((bf16[1024,128]{1,0:T(8,128)(2,1)}, bf16[1024,128]{1,0:T(8,128)(2,1)S(1)}, u32[]{:S(2)}, u32[]{:S(2)}) %collective-permute-start.13) | collective-permute-done | bytes 262176 | tf_op jit(solution)/shard_map/ppermute | solution.py:928
  129.5 6.4 %collective-permute-done.16.refs_3_ = bf16[1024,128]{1,0:T(8,128)(2,1)S(1)} collective-permute-done((bf16[1024,128]{1,0:T(8,128)(2,1)}, bf16[1024,128]{1,0:T(8,128)(2,1)S(1)}, u32[]{:S(2)}, u32[]{:S(2)}) %collective-permute-start.16) | collective-permute-done | bytes 262176 | tf_op jit(solution)/shard_map/ppermute | solution.py:928
  149.3 17.3 %collective-permute-done.17 = bf16[8,1024,128]{2,1,0:T(8,128)(2,1)} collective-permute-done((bf16[8,1024,128]{2,1,0:T(8,128)(2,1)}, bf16[8,1024,128]{2,1,0:T(8,128)(2,1)}, u32[]{:S(2)}, u32[]{:S(2)}) %collective-permute-start.17) | collective-permute-done | bytes 2097184 | tf_op jit(solution)/shard_map/ppermute | solution.py:928
  185.2 12.7 %collective-permute-done.20.refs_1_ = bf16[4,1024,128]{2,1,0:T(8,128)(2,1)S(1)} collective-permute-done((bf16[4,1024,128]{2,1,0:T(8,128)(2,1)}, bf16[4,1024,128]{2,1,0:T(8,128)(2,1)S(1)}, u32[]{:S(2)}, u32[]{:S(2)}) %collective-permute-start.20) | collective-permute-done | bytes 1048608 | tf_op jit(solution)/shard_map/ppermute | solution.py:928
  207.2 13.6 %forward_layer.4 = (f32[8192,128]{1,0:T(8,128)}, bf16[8192,128]{1,0:T(8,128)(2,1)}, bf16[8192,128]{1,0:T(8,128)(2,1)}, bf16[8192,128]{1,0:T(8,128)(2,1)}, f32[8,128]{1,0:T(8,128)}, /*index=5*/f32[8,128]{1,0:T(8,128)}) custom-call(s32[2,64]{1,0:T(2,128)} %pad_add_fusion.refs_0_, f32[8,128]{1,0:T(8,128)} %broadcast_in_dim.47.refs_1_, ...), custom_call_target="tpu_custom_call" | custom-call | flops 15000000512 | bytes 20971520 | tf_op jit(solution)/shard_map/forward_layer/pallas_call | solution.py:603
  220.8 8.3 %collective-permute-done.21 = bf16[8,1024,128]{2,1,0:T(8,128)(2,1)} collective-permute-done((bf16[8,1024,128]{2,1,0:T(8,128)(2,1)}, bf16[8,1024,128]{2,1,0:T(8,128)(2,1)}, u32[]{:S(2)}, u32[]{:S(2)}) %collective-permute-start.21) | collective-permute-done | bytes 2097184 | tf_op jit(solution)/shard_map/ppermute | solution.py:928
  233.6 12.6 %forward_layer.5 = (f32[8192,128]{1,0:T(8,128)}, bf16[8192,128]{1,0:T(8,128)(2,1)}, bf16[8192,128]{1,0:T(8,128)(2,1)}, bf16[8192,128]{1,0:T(8,128)(2,1)}, f32[8,128]{1,0:T(8,128)}, /*index=5*/f32[8,128]{1,0:T(8,128)}) custom-call(s32[2,64]{1,0:T(2,128)} %pad_add_fusion.refs_0_, f32[8,128]{1,0:T(8,128)} %get-tuple-element.242.refs_1_, ...), custom_call_target="tpu_custom_call" | custom-call | flops 15000000512 | bytes 20971520 | tf_op jit(solution)/shard_map/forward_layer/pallas_call | solution.py:603
  246.2 12.7 %forward_layer.6 = (f32[8192,128]{1,0:T(8,128)}, bf16[8192,128]{1,0:T(8,128)(2,1)}, bf16[8192,128]{1,0:T(8,128)(2,1)}, bf16[8192,128]{1,0:T(8,128)(2,1)}, f32[8,128]{1,0:T(8,128)}, /*index=5*/f32[8,128]{1,0:T(8,128)}) custom-call(s32[2,64]{1,0:T(2,128)} %pad_add_fusion.refs_0_, f32[8,128]{1,0:T(8,128)} %get-tuple-element.254.refs_1_, ...), custom_call_target="tpu_custom_call" | custom-call | flops 15000000512 | bytes 20971520 | tf_op jit(solution)/shard_map/forward_layer/pallas_call | solution.py:603
  258.9 12.7 %forward_layer.7 = (f32[8192,128]{1,0:T(8,128)}, bf16[8192,128]{1,0:T(8,128)(2,1)}, bf16[8192,128]{1,0:T(8,128)(2,1)}, bf16[8192,128]{1,0:T(8,128)(2,1)}, f32[8,128]{1,0:T(8,128)}, /*index=5*/f32[8,128]{1,0:T(8,128)}) custom-call(s32[2,64]{1,0:T(2,128)} %pad_add_fusion.refs_0_, f32[8,128]{1,0:T(8,128)} %get-tuple-element.265.refs_1_, ...), custom_call_target="tpu_custom_call" | custom-call | flops 15000000512 | bytes 20971520 | tf_op jit(solution)/shard_map/forward_layer/pallas_call | solution.py:603
  271.6 10.2 %all-to-all-done.1 = bf16[4,2048,128]{2,1,0:T(8,128)(2,1)S(1)} async-done(((bf16[4,2048,128]{2,1,0:T(8,128)(2,1)}), bf16[4,2048,128]{2,1,0:T(8,128)(2,1)S(1)}, u32[]{:S(2)}, u32[]{:S(2)}) %all-to-all-start.1) | async-done | bytes 2097184 | tf_op jit(solution)/shard_map/all_to_all | solution.py:963
  283.1 20.7 %backward_layer.4 = (f32[8192,128]{1,0:T(8,128)}, bf16[16,2,2,128,128]{4,3,2,1,0:T(8,128)(2,1)}, bf16[16,2,2,128,128]{4,3,2,1,0:T(8,128)(2,1)}) custom-call(s32[2,64]{1,0:T(2,128)} %pad_add_fusion.refs_0_, f32[8,128]{1,0:T(8,128)} %get-tuple-element.268.refs_1_, bf16[8192,128]{1,0:T(8,128)(2,1)} %broadcast_in_dim.55.refs_2_, ...), custom_call_target="tpu_custom_call" | custom-call | flops 17999998976 | bytes 31457280 | tf_op jit(solution)/shard_map/backward_layer/pallas_call | solution.py:636
  304.8 19.3 %backward_layer.5 = (f32[8192,128]{1,0:T(8,128)}, bf16[16,2,2,128,128]{4,3,2,1,0:T(8,128)(2,1)}, bf16[16,2,2,128,128]{4,3,2,1,0:T(8,128)(2,1)}) custom-call(s32[2,64]{1,0:T(2,128)} %pad_add_fusion.refs_0_, f32[8,128]{1,0:T(8,128)} %get-tuple-element.261.refs_1_, bf16[8192,128]{1,0:T(8,128)(2,1)} %broadcast_in_dim.53.refs_2_, ...), custom_call_target="tpu_custom_call" | custom-call | flops 17999998976 | bytes 31457280 | tf_op jit(solution)/shard_map/backward_layer/pallas_call | solution.py:636
  332.4 19.3 %backward_layer.6 = (f32[8192,128]{1,0:T(8,128)}, bf16[16,2,2,128,128]{4,3,2,1,0:T(8,128)(2,1)}, bf16[16,2,2,128,128]{4,3,2,1,0:T(8,128)(2,1)}) custom-call(s32[2,64]{1,0:T(2,128)} %pad_add_fusion.refs_0_, f32[8,128]{1,0:T(8,128)} %get-tuple-element.245.refs_1_, bf16[8192,128]{1,0:T(8,128)(2,1)} %broadcast_in_dim.51.refs_2_, ...), custom_call_target="tpu_custom_call" | custom-call | flops 17999998976 | bytes 31457280 | tf_op jit(solution)/shard_map/backward_layer/pallas_call | solution.py:636
  363.2 18.5 %backward_layer.7 = (bf16[8192,128]{1,0:T(8,128)(2,1)}, bf16[16,2,2,128,128]{4,3,2,1,0:T(8,128)(2,1)}, bf16[16,2,2,128,128]{4,3,2,1,0:T(8,128)(2,1)}) custom-call(s32[2,64]{1,0:T(2,128)} %pad_add_fusion.refs_0_, f32[8,128]{1,0:T(8,128)} %get-tuple-element.233.refs_1_, bf16[8192,128]{1,0:T(8,128)(2,1)} %broadcast_in_dim.49.refs_2_, ...), custom_call_target="tpu_custom_call" | custom-call | flops 17999998976 | bytes 31457280 | tf_op jit(solution)/shard_map/backward_layer/pallas_call | solution.py:636
  398.5 11.2 %collective-permute-done.34.refs_5_ = bf16[2048,128]{1,0:T(8,128)(2,1)} collective-permute-done((bf16[2048,128]{1,0:T(8,128)(2,1)}, bf16[2048,128]{1,0:T(8,128)(2,1)}, u32[]{:S(2)}, u32[]{:S(2)}) %collective-permute-start.34) | collective-permute-done | bytes 524320 | tf_op jit(solution)/shard_map/ppermute | solution.py:928
  409.7 11.1 %collective-permute-done.35.refs_6_ = bf16[2048,128]{1,0:T(8,128)(2,1)} collective-permute-done((bf16[2048,128]{1,0:T(8,128)(2,1)}, bf16[2048,128]{1,0:T(8,128)(2,1)}, u32[]{:S(2)}, u32[]{:S(2)}) %collective-permute-start.35) | collective-permute-done | bytes 524320 | tf_op jit(solution)/shard_map/ppermute | solution.py:928
  425.2 5.3 collective-permute-start.40
  441.0 13.3 %collective-permute-done.40.refs_0_ = bf16[1024,128]{1,0:T(8,128)(2,1)S(1)} collective-permute-done((bf16[1024,128]{1,0:T(8,128)(2,1)}, bf16[1024,128]{1,0:T(8,128)(2,1)S(1)}, u32[]{:S(2)}, u32[]{:S(2)}) %collective-permute-start.40) | collective-permute-done | bytes 262176 | tf_op jit(solution)/shard_map/ppermute | solution.py:928
  456.2 5.9 %collective-permute-done.41.refs_1_ = bf16[1024,128]{1,0:T(8,128)(2,1)S(1)} collective-permute-done((bf16[1024,128]{1,0:T(8,128)(2,1)}, bf16[1024,128]{1,0:T(8,128)(2,1)S(1)}, u32[]{:S(2)}, u32[]{:S(2)}) %collective-permute-start.41) | collective-permute-done | bytes 262176 | tf_op jit(solution)/shard_map/ppermute | solution.py:928
  467.8 14.6 %collective-permute-done.43.refs_3_ = bf16[1024,128]{1,0:T(8,128)(2,1)S(1)} collective-permute-done((bf16[1024,128]{1,0:T(8,128)(2,1)S(1)}, bf16[1024,128]{1,0:T(8,128)(2,1)S(1)}, u32[]{:S(2)}, u32[]{:S(2)}) %collective-permute-start.43) | collective-permute-done | bytes 262176 | tf_op jit(solution)/shard_map/ppermute | solution.py:928
  503.3 5.5 %collective-permute-done.44.refs_0_ = bf16[1024,128]{1,0:T(8,128)(2,1)S(1)} collective-permute-done((bf16[1024,128]{1,0:T(8,128)(2,1)}, bf16[1024,128]{1,0:T(8,128)(2,1)S(1)}, u32[]{:S(2)}, u32[]{:S(2)}) %collective-permute-start.44) | collective-permute-done | bytes 262176 | tf_op jit(solution)/shard_map/ppermute | solution.py:928
  508.8 8.5 %collective-permute-done.45.refs_1_ = bf16[1024,128]{1,0:T(8,128)(2,1)S(1)} collective-permute-done((bf16[1024,128]{1,0:T(8,128)(2,1)}, bf16[1024,128]{1,0:T(8,128)(2,1)S(1)}, u32[]{:S(2)}, u32[]{:S(2)}) %collective-permute-start.45) | collective-permute-done | bytes 262176 | tf_op jit(solution)/shard_map/ppermute | solution.py:928
  518.9 5.4 %collective-permute-done.47.refs_3_ = bf16[1024,128]{1,0:T(8,128)(2,1)S(1)} collective-permute-done((bf16[1024,128]{1,0:T(8,128)(2,1)}, bf16[1024,128]{1,0:T(8,128)(2,1)S(1)}, u32[]{:S(2)}, u32[]{:S(2)}) %collective-permute-start.47) | collective-permute-done | bytes 262176 | tf_op jit(solution)/shard_map/ppermute | solution.py:928
  531.4 5.8 %assemble.1 = (f32[4,16,128,128]{3,2,1,0:T(8,128)}, f32[4,16,128,128]{3,2,1,0:T(8,128)}) custom-call(s32[3]{0:T(128)} %pad_add_fusion.1.refs_0_, bf16[4,2,2,2,128,128]{5,4,3,2,1,0:T(8,128)(2,1)} %bitcast.64, bf16[4,2,2,2,128,128]{5,4,3,2,1,0:T(8,128)(2,1)} %bitcast.90, bf16[4,2,2,2,128,128]{5,4,3,2,1,0:T(8,128)(2,1)} %bitcast.63, ...), custom_call_target="tpu_custom_call" | custom-call | bytes 12582912 | tf_op jit(solution)/shard_map/assemble/pallas_call | solution.py:866
  (211 shorter events, 179.9 us)
Async XLA Ops:
  27.9 108.7 %all-to-all-start = ((bf16[4,2048,128]{2,1,0:T(8,128)(2,1)}), bf16[4,2048,128]{2,1,0:T(8,128)(2,1)S(1)}, u32[]{:S(2)}, u32[]{:S(2)}) async-start(bf16[4,2048,128]{2,1,0:T(8,128)(2,1)} %pick.2), calls=%async_computation | async-start | bytes 4194304 | tf_op jit(solution)/shard_map/all_to_all | solution.py:963
  40.6 58.3 %collective-permute-start.4 = (bf16[1104,128]{1,0:T(8,128)(2,1)S(1)}, bf16[1104,128]{1,0:T(8,128)(2,1)S(1)}, u32[]{:S(2)}, u32[]{:S(2)}) collective-permute-start(bf16[1104,128]{1,0:T(8,128)(2,1)S(1)} %collective-permute-done), channel_id=1, source_target_pairs={{0,0},{1,1},{2,2},{3,3},{4,4},{5,5},{6,6},{7,7},{8,10},{9,11},{10,... | collective-permute-start | bytes 847880 | tf_op jit(solution)/shard_map/ppermute | solution.py:928
  44.8 54.1 %collective-permute-start.5 = (bf16[1104,128]{1,0:T(8,128)(2,1)S(1)}, bf16[1104,128]{1,0:T(8,128)(2,1)S(1)}, u32[]{:S(2)}, u32[]{:S(2)}) collective-permute-start(bf16[1104,128]{1,0:T(8,128)(2,1)S(1)} %collective-permute-done.1), channel_id=1, source_target_pairs={{0,2},{1,3},{2,0},{3,1},{4,6},{5,7},{6,4},{7,5},{8,8},{9,9},{10,10... | collective-permute-start | bytes 847880 | tf_op jit(solution)/shard_map/ppermute | solution.py:928
  48.8 50.1 %collective-permute-start.6 = (bf16[1104,128]{1,0:T(8,128)(2,1)}, bf16[1104,128]{1,0:T(8,128)(2,1)S(1)}, u32[]{:S(2)}, u32[]{:S(2)}) collective-permute-start(bf16[1104,128]{1,0:T(8,128)(2,1)} %collective-permute-done.2), channel_id=1, source_target_pairs={{0,4},{1,5},{2,6},{3,7},{4,0},{5,1},{6,2},{7,3},{8,14},{9,15},{10,... | collective-permute-start | bytes 847880 | tf_op jit(solution)/shard_map/ppermute | solution.py:928
  50.4 48.5 %collective-permute-start.7 = (bf16[1104,128]{1,0:T(8,128)(2,1)}, bf16[1104,128]{1,0:T(8,128)(2,1)S(1)}, u32[]{:S(2)}, u32[]{:S(2)}) collective-permute-start(bf16[1104,128]{1,0:T(8,128)(2,1)} %copy-done.36), channel_id=1, source_target_pairs={{0,6},{1,7},{2,4},{3,5},{4,2},{5,3},{6,0},{7,1},{8,12},{9,13},{10,... | collective-permute-start | bytes 847880 | tf_op jit(solution)/shard_map/ppermute | solution.py:928
  102.7 33.9 %collective-permute-start.12 = (bf16[4,1024,128]{2,1,0:T(8,128)(2,1)}, bf16[4,1024,128]{2,1,0:T(8,128)(2,1)S(1)}, u32[]{:S(2)}, u32[]{:S(2)}) collective-permute-start(bf16[4,1024,128]{2,1,0:T(8,128)(2,1)} %bitcast.65), channel_id=1, source_target_pairs={{0,8},{1,17},{2,10},{3,19},{4,12},{5,21},{6,14},{7,23},{8,0},{9,25... | collective-permute-start | bytes 3145736 | tf_op jit(solution)/shard_map/ppermute | solution.py:928
  103.5 26.0 %collective-permute-start.13 = (bf16[1024,128]{1,0:T(8,128)(2,1)}, bf16[1024,128]{1,0:T(8,128)(2,1)S(1)}, u32[]{:S(2)}, u32[]{:S(2)}) collective-permute-start(bf16[1024,128]{1,0:T(8,128)(2,1)} %copy-done.37), channel_id=1, source_target_pairs={{0,0},{1,1},{2,2},{3,3},{4,4},{5,5},{6,6},{7,7},{8,10},{9,11},{10,... | collective-permute-start | bytes 786440 | tf_op jit(solution)/shard_map/ppermute | solution.py:928
  141.2 25.5 %collective-permute-start.17 = (bf16[8,1024,128]{2,1,0:T(8,128)(2,1)}, bf16[8,1024,128]{2,1,0:T(8,128)(2,1)}, u32[]{:S(2)}, u32[]{:S(2)}) collective-permute-start(bf16[8,1024,128]{2,1,0:T(8,128)(2,1)} %join.7), channel_id=1, source_target_pairs={{0,16},{1,9},{2,18},{3,11},{4,20},{5,13},{6,22},{7,15},{8,24},{9,1... | collective-permute-start | bytes 6291464 | tf_op jit(solution)/shard_map/ppermute | solution.py:928
  177.6 24.1 %collective-permute-start.19 = (bf16[8,1024,128]{2,1,0:T(8,128)(2,1)}, bf16[8,1024,128]{2,1,0:T(8,128)(2,1)S(1)}, u32[]{:S(2)}, u32[]{:S(2)}) collective-permute-start(bf16[8,1024,128]{2,1,0:T(8,128)(2,1)} %collective-permute-done.17), channel_id=1, source_target_pairs={{0,1},{1,0},{2,3},{3,2},{4,5},{5,4},{6,7},{7,6},{8,9},{9,8},{10,11... | collective-permute-start | bytes 6291464 | tf_op jit(solution)/shard_map/ppermute | solution.py:928
  203.4 25.8 %collective-permute-start.21 = (bf16[8,1024,128]{2,1,0:T(8,128)(2,1)}, bf16[8,1024,128]{2,1,0:T(8,128)(2,1)}, u32[]{:S(2)}, u32[]{:S(2)}) collective-permute-start(bf16[8,1024,128]{2,1,0:T(8,128)(2,1)} %join.9), channel_id=1, source_target_pairs={{0,16},{1,9},{2,18},{3,11},{4,20},{5,13},{6,22},{7,15},{8,24},{9,1... | collective-permute-start | bytes 6291464 | tf_op jit(solution)/shard_map/ppermute | solution.py:928
  229.8 52.0 %all-to-all-start.1 = ((bf16[4,2048,128]{2,1,0:T(8,128)(2,1)}), bf16[4,2048,128]{2,1,0:T(8,128)(2,1)S(1)}, u32[]{:S(2)}, u32[]{:S(2)}) async-start(bf16[4,2048,128]{2,1,0:T(8,128)(2,1)} %pick.3), calls=%async_computation.1 | async-start | bytes 4194304 | tf_op jit(solution)/shard_map/all_to_all | solution.py:963
  325.4 29.8 %collective-permute-start.28 = (bf16[16,2,2,128,128]{4,3,2,1,0:T(8,128)(2,1)}, bf16[16,2,2,128,128]{4,3,2,1,0:T(8,128)(2,1)S(1)}, u32[]{:S(2)}, u32[]{:S(2)}) collective-permute-start(bf16[16,2,2,128,128]{4,3,2,1,0:T(8,128)(2,1)} %get-tuple-element.291), channel_id=1, source_target_pairs={{0,1},{1,0},{2,3},{3,2},{4,5},{5,4},{6,7},{7,6},{8,9},{9,8},{10,11... | collective-permute-start | bytes 6291464 | tf_op jit(solution)/shard_map/ppermute | solution.py:928
  329.1 22.6 %collective-permute-start.25 = (bf16[2048,128]{1,0:T(8,128)(2,1)}, bf16[2048,128]{1,0:T(8,128)(2,1)S(1)}, u32[]{:S(2)}, u32[]{:S(2)}) collective-permute-start(bf16[2048,128]{1,0:T(8,128)(2,1)} %get-tuple-element.287), channel_id=1, source_target_pairs={{0,8},{1,9},{2,10},{3,11},{4,12},{5,13},{6,14},{7,15},{8,0},{9,1},... | collective-permute-start | bytes 1572872 | tf_op jit(solution)/shard_map/ppermute | solution.py:928
  330.7 23.6 %collective-permute-start.26 = (bf16[2048,128]{1,0:T(8,128)(2,1)}, bf16[2048,128]{1,0:T(8,128)(2,1)S(1)}, u32[]{:S(2)}, u32[]{:S(2)}) collective-permute-start(bf16[2048,128]{1,0:T(8,128)(2,1)} %get-tuple-element.288), channel_id=1, source_target_pairs={{0,16},{1,17},{2,18},{3,19},{4,20},{5,21},{6,22},{7,23},{8,24},{9,... | collective-permute-start | bytes 1572872 | tf_op jit(solution)/shard_map/ppermute | solution.py:928
  332.4 22.8 %collective-permute-start.27 = (bf16[2048,128]{1,0:T(8,128)(2,1)}, bf16[2048,128]{1,0:T(8,128)(2,1)S(1)}, u32[]{:S(2)}, u32[]{:S(2)}) collective-permute-start(bf16[2048,128]{1,0:T(8,128)(2,1)} %get-tuple-element.289), channel_id=1, source_target_pairs={{0,24},{1,25},{2,26},{3,27},{4,28},{5,29},{6,30},{7,31},{8,16},{9,... | collective-permute-start | bytes 1572872 | tf_op jit(solution)/shard_map/ppermute | solution.py:928
  355.2 30.1 %collective-permute-start.32 = (bf16[16,2,2,128,128]{4,3,2,1,0:T(8,128)(2,1)}, bf16[16,2,2,128,128]{4,3,2,1,0:T(8,128)(2,1)}, u32[]{:S(2)}, u32[]{:S(2)}) collective-permute-start(bf16[16,2,2,128,128]{4,3,2,1,0:T(8,128)(2,1)} %get-tuple-element.307), channel_id=1, source_target_pairs={{0,1},{1,0},{2,3},{3,2},{4,5},{5,4},{6,7},{7,6},{8,9},{9,8},{10,11... | collective-permute-start | bytes 6291464 | tf_op jit(solution)/shard_map/ppermute | solution.py:928
  360.5 21.1 %collective-permute-start.29 = (bf16[2048,128]{1,0:T(8,128)(2,1)}, bf16[2048,128]{1,0:T(8,128)(2,1)S(1)}, u32[]{:S(2)}, u32[]{:S(2)}) collective-permute-start(bf16[2048,128]{1,0:T(8,128)(2,1)} %get-tuple-element.303), channel_id=1, source_target_pairs={{0,8},{1,9},{2,10},{3,11},{4,12},{5,13},{6,14},{7,15},{8,0},{9,1},... | collective-permute-start | bytes 1572872 | tf_op jit(solution)/shard_map/ppermute | solution.py:928
  361.7 20.8 %collective-permute-start.30 = (bf16[2048,128]{1,0:T(8,128)(2,1)}, bf16[2048,128]{1,0:T(8,128)(2,1)S(1)}, u32[]{:S(2)}, u32[]{:S(2)}) collective-permute-start(bf16[2048,128]{1,0:T(8,128)(2,1)} %get-tuple-element.304), channel_id=1, source_target_pairs={{0,16},{1,17},{2,18},{3,19},{4,20},{5,21},{6,22},{7,23},{8,24},{9,... | collective-permute-start | bytes 1572872 | tf_op jit(solution)/shard_map/ppermute | solution.py:928
  362.0 23.3 %collective-permute-start.31 = (bf16[2048,128]{1,0:T(8,128)(2,1)}, bf16[2048,128]{1,0:T(8,128)(2,1)S(1)}, u32[]{:S(2)}, u32[]{:S(2)}) collective-permute-start(bf16[2048,128]{1,0:T(8,128)(2,1)} %get-tuple-element.305), channel_id=1, source_target_pairs={{0,24},{1,25},{2,26},{3,27},{4,28},{5,29},{6,30},{7,31},{8,16},{9,... | collective-permute-start | bytes 1572872 | tf_op jit(solution)/shard_map/ppermute | solution.py:928
  386.1 97.9 %all-to-all-start.2 = ((bf16[4,2048,128]{2,1,0:T(8,128)(2,1)}), bf16[4,2048,128]{2,1,0:T(8,128)(2,1)S(1)}, u32[]{:S(2)}, u32[]{:S(2)}) async-start(bf16[4,2048,128]{2,1,0:T(8,128)(2,1)} %bitcast.77), calls=%async_computation.2 | async-start | bytes 4194304 | tf_op jit(solution)/shard_map/all_to_all | solution.py:963
  389.9 31.9 %collective-permute-start.33 = (bf16[16,2,2,128,128]{4,3,2,1,0:T(8,128)(2,1)}, bf16[16,2,2,128,128]{4,3,2,1,0:T(8,128)(2,1)}, u32[]{:S(2)}, u32[]{:S(2)}) collective-permute-start(bf16[16,2,2,128,128]{4,3,2,1,0:T(8,128)(2,1)} %get-tuple-element.310), channel_id=1, source_target_pairs={{0,1},{1,0},{2,3},{3,2},{4,5},{5,4},{6,7},{7,6},{8,9},{9,8},{10,11... | collective-permute-start | bytes 6291464 | tf_op jit(solution)/shard_map/ppermute | solution.py:928
  396.9 23.9 %collective-permute-start.35 = (bf16[2048,128]{1,0:T(8,128)(2,1)}, bf16[2048,128]{1,0:T(8,128)(2,1)}, u32[]{:S(2)}, u32[]{:S(2)}) collective-permute-start(bf16[2048,128]{1,0:T(8,128)(2,1)} %get-tuple-element.315), channel_id=1, source_target_pairs={{0,16},{1,17},{2,18},{3,19},{4,20},{5,21},{6,22},{7,23},{8,24},{9,... | collective-permute-start | bytes 1572872 | tf_op jit(solution)/shard_map/ppermute | solution.py:928
  398.4 23.4 %collective-permute-start.36 = (bf16[2048,128]{1,0:T(8,128)(2,1)}, bf16[2048,128]{1,0:T(8,128)(2,1)}, u32[]{:S(2)}, u32[]{:S(2)}) collective-permute-start(bf16[2048,128]{1,0:T(8,128)(2,1)} %get-tuple-element.316), channel_id=1, source_target_pairs={{0,24},{1,25},{2,26},{3,27},{4,28},{5,29},{6,30},{7,31},{8,16},{9,... | collective-permute-start | bytes 1572872 | tf_op jit(solution)/shard_map/ppermute | solution.py:928
  425.2 29.1 %collective-permute-start.40 = (bf16[1024,128]{1,0:T(8,128)(2,1)}, bf16[1024,128]{1,0:T(8,128)(2,1)S(1)}, u32[]{:S(2)}, u32[]{:S(2)}) collective-permute-start(bf16[1024,128]{1,0:T(8,128)(2,1)} %get-tuple-element.343), channel_id=1, source_target_pairs={{0,0},{1,1},{2,10},{3,11},{4,20},{5,21},{6,30},{7,31},{8,2},{9,3},... | collective-permute-start | bytes 786440 | tf_op jit(solution)/shard_map/ppermute | solution.py:928
  430.5 31.6 %collective-permute-start.41 = (bf16[1024,128]{1,0:T(8,128)(2,1)}, bf16[1024,128]{1,0:T(8,128)(2,1)S(1)}, u32[]{:S(2)}, u32[]{:S(2)}) collective-permute-start(bf16[1024,128]{1,0:T(8,128)(2,1)} %get-tuple-element.344), channel_id=1, source_target_pairs={{0,2},{1,3},{2,8},{3,9},{4,22},{5,23},{6,28},{7,29},{8,0},{9,1},{1... | collective-permute-start | bytes 786440 | tf_op jit(solution)/shard_map/ppermute | solution.py:928
  438.4 44.0 %collective-permute-start.37 = (bf16[2048,128]{1,0:T(8,128)(2,1)}, bf16[2048,128]{1,0:T(8,128)(2,1)S(1)}, u32[]{:S(2)}, u32[]{:S(2)}) collective-permute-start(bf16[2048,128]{1,0:T(8,128)(2,1)} %get-tuple-element.328), channel_id=1, source_target_pairs={{0,8},{1,9},{2,10},{3,11},{4,12},{5,13},{6,14},{7,15},{8,0},{9,1},... | collective-permute-start | bytes 1572872 | tf_op jit(solution)/shard_map/ppermute | solution.py:928
  438.4 44.0 %collective-permute-start.38 = (bf16[2048,128]{1,0:T(8,128)(2,1)}, bf16[2048,128]{1,0:T(8,128)(2,1)S(1)}, u32[]{:S(2)}, u32[]{:S(2)}) collective-permute-start(bf16[2048,128]{1,0:T(8,128)(2,1)} %get-tuple-element.329), channel_id=1, source_target_pairs={{0,16},{1,17},{2,18},{3,19},{4,20},{5,21},{6,22},{7,23},{8,24},{9,... | collective-permute-start | bytes 1572872 | tf_op jit(solution)/shard_map/ppermute | solution.py:928
  438.4 45.7 %collective-permute-start.39 = (bf16[2048,128]{1,0:T(8,128)(2,1)}, bf16[2048,128]{1,0:T(8,128)(2,1)}, u32[]{:S(2)}, u32[]{:S(2)}) collective-permute-start(bf16[2048,128]{1,0:T(8,128)(2,1)} %get-tuple-element.330), channel_id=1, source_target_pairs={{0,24},{1,25},{2,26},{3,27},{4,28},{5,29},{6,30},{7,31},{8,16},{9,... | collective-permute-start | bytes 1572872 | tf_op jit(solution)/shard_map/ppermute | solution.py:928
  487.0 37.3 %collective-permute-start.48 = (bf16[4096,128]{1,0:T(8,128)(2,1)}, bf16[4096,128]{1,0:T(8,128)(2,1)S(1)}, u32[]{:S(2)}, u32[]{:S(2)}) collective-permute-start(bf16[4096,128]{1,0:T(8,128)(2,1)} %join.10), channel_id=1, source_target_pairs={{0,1},{1,0},{2,3},{3,2},{4,5},{5,4},{6,7},{7,6},{8,9},{9,8},{10,11... | collective-permute-start | bytes 3145736 | tf_op jit(solution)/shard_map/ppermute | solution.py:928
  493.7 23.6 %collective-permute-start.45 = (bf16[1024,128]{1,0:T(8,128)(2,1)}, bf16[1024,128]{1,0:T(8,128)(2,1)S(1)}, u32[]{:S(2)}, u32[]{:S(2)}) collective-permute-start(bf16[1024,128]{1,0:T(8,128)(2,1)} %get-tuple-element.357), channel_id=1, source_target_pairs={{0,2},{1,3},{2,8},{3,9},{4,22},{5,23},{6,28},{7,29},{8,0},{9,1},{1... | collective-permute-start | bytes 786440 | tf_op jit(solution)/shard_map/ppermute | solution.py:928
  495.6 23.3 %collective-permute-start.46 = (bf16[1024,128]{1,0:T(8,128)(2,1)}, bf16[1024,128]{1,0:T(8,128)(2,1)S(1)}, u32[]{:S(2)}, u32[]{:S(2)}) collective-permute-start(bf16[1024,128]{1,0:T(8,128)(2,1)} %get-tuple-element.358), channel_id=1, source_target_pairs={{0,4},{1,5},{2,14},{3,15},{4,16},{5,17},{6,26},{7,27},{8,6},{9,7},... | collective-permute-start | bytes 786440 | tf_op jit(solution)/shard_map/ppermute | solution.py:928
  497.6 26.8 %collective-permute-start.47 = (bf16[1024,128]{1,0:T(8,128)(2,1)}, bf16[1024,128]{1,0:T(8,128)(2,1)S(1)}, u32[]{:S(2)}, u32[]{:S(2)}) collective-permute-start(bf16[1024,128]{1,0:T(8,128)(2,1)} %get-tuple-element.359), channel_id=1, source_target_pairs={{0,6},{1,7},{2,12},{3,13},{4,18},{5,19},{6,24},{7,25},{8,4},{9,5},... | collective-permute-start | bytes 786440 | tf_op jit(solution)/shard_map/ppermute | solution.py:928
  (64 other events, 808.8 us)

commit v7 on v6

--- a/solution.py
+++ b/solution.py
@@ -418,7 +418,7 @@
     def right(block, total):
         rows = block_rows(block, size)
         place = table_ref[0, block]
-        moved = [mid[pl.ds(block * fold + q, blocks, stride=size), :] for q in range(fold)]
+        moved = [mid[pl.ds(q * blocks + block, blocks, stride=size), :] for q in range(fold)]
         moved = jnp.concatenate(moved, axis=0).astype(jnp.bfloat16)
         z[rows, :] = moved
         weight = w[place // chunk_blocks, 1, place % chunk_blocks]
@@ -450,8 +450,8 @@
     slope_ref, z_ref, u_ref = sources[:3]
     parts, sources = sources[3 : 3 + PARTS], sources[3 + PARTS :]
     out_ref, own_grad, peer_grad = refs[:3]
-    g, slope, z, u, h, w, gw, mid, turned, gain, top, goal, end_gain = refs[3:16]
-    in_sems, w_sems, out_sems, gw_sems = refs[16:]
+    g, slope, z, u, h, w, gw, mid, gain, top, goal, end_gain = refs[3:15]
+    in_sems, w_sems, out_sems, gw_sems = refs[15:]
     features, slots = g.shape
     size = w.shape[-1]
     chunk_blocks = w.shape[2]
@@ -545,12 +545,8 @@
         place, home = table_ref[0, block], table_ref[1, block]
         at = (place // chunk_blocks, 0, place % chunk_blocks)
         to = (home // chunk_blocks, 0, home % chunk_blocks)
-        slot = block % turned.shape[0]
-        for q in range(fold):
-            turned[slot, pl.ds(q, blocks, stride=fold), :] = mid[
-                pl.ds(q * blocks + block, blocks, stride=size), :
-            ]
-        arrived = turned[slot].astype(jnp.bfloat16)
+        arrived = [mid[pl.ds(q * blocks + block, blocks, stride=size), :] for q in range(fold)]
+        arrived = jnp.concatenate(arrived, axis=0).astype(jnp.bfloat16)
         gw[to] = inner_dot(u[rows, :], arrived, 1, 1).astype(jnp.bfloat16)
         weighted = inner_dot(w[at], arrived, 1, 0) * gain[rows, :].astype(jnp.float32)
         g[rows, :] = g[rows, :] + scale * weighted
@@ -647,7 +643,6 @@
             pltpu.VMEM(held, jnp.bfloat16),
             pltpu.VMEM(held, jnp.bfloat16),
             pltpu.VMEM(whole, jnp.float32),
-            pltpu.VMEM((8, held[-1], whole[1]), jnp.float32),
             pltpu.VMEM(whole, jnp.bfloat16),
             pltpu.VMEM(whole if turning else SMALL, jnp.float32),
             pltpu.VMEM(whole if turning else SMALL, jnp.bfloat16),
@@ -665,11 +660,11 @@
     )(table, scale, gain, end_gain, *sources)
 
 
-def copies_kernel(plan, inputs, outputs, *refs):
-    sems = refs[-1]
+def join_kernel(rows, *refs):
+    sources, whole, sems = refs[:-2], refs[-2], refs[-1]
     copies = [
-        pltpu.make_async_copy(source, target, sems.at[at])
-        for at, (source, target) in enumerate(plan(refs[:inputs], refs[inputs : inputs + outputs]))
+        pltpu.make_async_copy(source.at[pl.ds(0, rows)], whole.at[pl.ds(at * rows, rows)], sems.at[at])
+        for at, source in enumerate(sources)
     ]
     for copy in copies:
         copy.start()
@@ -677,89 +672,110 @@
         copy.wait()
 
 
-def run_copies(plan, scalars, inputs, out_shape, most, name):
-    extra = [] if scalars is None else [scalars]
-    size = sum(math.prod(out.shape) for out in out_shape)
-    return pl.pallas_call(
-        lambda *refs: copies_kernel(plan, len(extra) + len(inputs), len(out_shape), *refs),
-        in_specs=[SMEM] * len(extra) + [OUTSIDE] * len(inputs),
-        out_specs=[INSIDE] * len(out_shape),
-        out_shape=out_shape,
-        scratch_shapes=[pltpu.SemaphoreType.DMA((most,))],
-        compiler_params=pltpu.CompilerParams(vmem_limit_bytes=VMEM_LIMIT),
-        cost_estimate=pl.CostEstimate(flops=0, bytes_accessed=4 * size, transcendentals=0),
-        name=name,
-    )(*extra, *inputs)
-
-
 def joined(parts, rows=None):
     rows = parts[0].shape[0] if rows is None else rows
     whole = shape_of((rows * len(parts),) + parts[0].shape[1:], parts[0].dtype)
-
-    def plan(sources, targets):
-        return [
-            (source.at[pl.ds(0, rows)], targets[0].at[pl.ds(at * rows, rows)])
-            for at, source in enumerate(sources)
-        ]
-
-    return run_copies(plan, None, parts, [whole], len(parts), "join")[0]
-
-
-def sum_kernel(terms, refs_in, *refs):
-    sources, outs = refs[:refs_in], refs[refs_in:]
-    groups = refs_in // terms
-    count = len(outs)
-    for group in range(groups):
-        mine = sources[group * terms : (group + 1) * terms]
-        rows = mine[0].shape[0] // count
-        for at, out in enumerate(outs):
-            total = sum(ref[pl.ds(at * rows, rows), :].astype(jnp.float32) for ref in mine)
-            out[pl.ds(group * rows, rows), :] = total.astype(jnp.bfloat16)
-
-
-def run_sum(groups, outputs):
-    flat = [term.reshape(-1, term.shape[-1]) for terms in groups for term in terms]
-    rows, lanes = flat[0].shape
     return pl.pallas_call(
-        lambda *refs: sum_kernel(len(groups[0]), len(flat), *refs),
-        in_specs=[INSIDE] * len(flat),
-        out_specs=[INSIDE] * outputs,
-        out_shape=[shape_of((len(groups) * rows // outputs, lanes), jnp.bfloat16)] * outputs,
+        lambda *refs: join_kernel(rows, *refs),
+        in_specs=[OUTSIDE] * len(parts),
+        out_specs=INSIDE,
+        out_shape=whole,
+        scratch_shapes=[pltpu.SemaphoreType.DMA((len(parts),))],
         compiler_params=pltpu.CompilerParams(vmem_limit_bytes=VMEM_LIMIT),
         cost_estimate=pl.CostEstimate(
-            flops=rows * lanes * len(flat), bytes_accessed=2 * rows * lanes * (len(flat) + 1), transcendentals=0
+            flops=0, bytes_accessed=4 * math.prod(whole.shape), transcendentals=0
+        ),
+        name="join",
+    )(*parts)
+
+
+def sum_kernel(terms, inputs, *refs):
+    sources, outs = refs[:inputs], refs[inputs:]
+    for group in range(inputs // terms):
+        mine = sources[group * terms : (group + 1) * terms]
+        for at, out in enumerate(outs):
+            total = sum(ref[at].astype(jnp.float32) for ref in mine)
+            out[group] = total.astype(jnp.bfloat16)
+
+
+def run_sum(groups, outputs):
+    flat = [term.reshape(outputs, -1, term.shape[-1]) for terms in groups for term in terms]
+    _, rows, lanes = flat[0].shape
+    steps = 4
+    out_shape = [shape_of((len(groups), rows, lanes), jnp.bfloat16)] * outputs
+    sums = pl.pallas_call(
+        lambda *refs: sum_kernel(len(groups[0]), len(flat), *refs),
+        grid=(steps,),
+        in_specs=[pl.BlockSpec((outputs, rows // steps, lanes), lambda i: (0, i, 0))] * len(flat),
+        out_specs=[pl.BlockSpec((len(groups), rows // steps, lanes), lambda i: (0, i, 0))] * outputs,
+        out_shape=out_shape,
+        compiler_params=pltpu.CompilerParams(vmem_limit_bytes=VMEM_LIMIT),
+        cost_estimate=pl.CostEstimate(
+            flops=flat[0].size * len(flat), bytes_accessed=2 * flat[0].size * (len(flat) + 1), transcendentals=0
         ),
         name="sum",
     )(*flat)
-
-
-def factor_pieces(place, left, right, gain_rows, groups, chunk):
-    width = 4
-    size = left.shape[-1]
+    return [out.reshape(-1, lanes) for out in sums]
+
+
+def pieces_kernel(groups, chunk, place_ref, order_ref, left_ref, right_ref, gain_ref, *refs):
+    outs, (held, left_sem, sems) = refs[:-3], refs[-3:]
+    size = held.shape[-1]
+    width = len(outs) // len(groups)
+    half = held.shape[1]
+    origin = place_ref[0] ^ place_ref[1]
+    lefts = pltpu.make_async_copy(left_ref.at[:, pl.ds(place_ref[2] * half, half)], held, left_sem.at[0])
+    lefts.start()
+    copies = []
+    turns = []
+    for at, group in enumerate(groups):
+        for j in range(width):
+            out = outs[at * width + j]
+            start = (origin ^ j) * chunk
+            row = 0
+            for layer in group:
+                for inside in range(chunk):
+                    turns.append((layer, start + inside, out, row))
+                    row += size
+                for inside in range(chunk):
+                    source = right_ref.at[layer, place_ref[2] * half + start + inside]
+                    copies.append((source, out.at[pl.ds(row, size)]))
+                    row += size
+            if group[0] == 0:
+                copies.append((gain_ref, out.at[pl.ds(row, gain_ref.shape[0])]))
+    copies = [
+        pltpu.make_async_copy(source, target, sems.at[at]) for at, (source, target) in enumerate(copies)
+    ]
+    for copy in copies:
+        copy.start()
+    lefts.wait()
+    for layer, block, out, row in turns:
+        turned = inner_dot(held[layer, block], order_ref[...], 1, 0)
+        out[pl.ds(row, size), :] = turned.astype(jnp.bfloat16)
+    for copy in copies:
+        copy.wait()
+
+
+def factor_pieces(place, order, left, right, gain_rows, groups, chunk, width):
+    layer_count, blocks, size = left.shape[:3]
     shapes = []
     for group in groups:
         rows = len(group) * 2 * chunk * size + (gain_rows.shape[0] if group[0] == 0 else 0)
         shapes += [shape_of((rows, size), jnp.bfloat16)] * width
-
-    def plan(sources, targets):
-        place_ref, left_ref, right_ref, gain_ref = sources
-        copies = []
-        for at, group in enumerate(groups):
-            for j in range(width):
-                target = targets[at * width + j]
-                start = (place_ref[2] * width + (place_ref[0] ^ place_ref[1] ^ j)) * chunk
-                row = 0
-                for layer in group:
-                    for ref in (left_ref, right_ref):
-                        for inside in range(chunk):
-                            copies.append((ref.at[layer, start + inside], target.at[pl.ds(row, size)]))
-                            row += size
-                if group[0] == 0:
-                    copies.append((gain_ref, target.at[pl.ds(row, gain_rows.shape[0])]))
-        return copies
-
-    most = width * (sum(len(group) for group in groups) * 2 * chunk + 1)
-    flat = run_copies(plan, place, (left, right, gain_rows), shapes, most, "pieces")
+    flat = pl.pallas_call(
+        lambda *refs: pieces_kernel(groups, chunk, *refs),
+        in_specs=[SMEM, INSIDE] + [OUTSIDE] * 3,
+        out_specs=[INSIDE] * len(shapes),
+        out_shape=shapes,
+        scratch_shapes=[
+            pltpu.VMEM((layer_count, blocks // 2, size, size), jnp.bfloat16),
+            pltpu.SemaphoreType.DMA((1,)),
+            pltpu.SemaphoreType.DMA((width * (layer_count * chunk + 1),)),
+        ],
+        compiler_params=pltpu.CompilerParams(vmem_limit_bytes=VMEM_LIMIT),
+        cost_estimate=pl.CostEstimate(flops=left.size * size, bytes_accessed=4 * left.size, transcendentals=0),
+        name="pieces",
+    )(place, order, left, right, gain_rows)
     return [flat[at * width : (at + 1) * width] for at in range(len(groups))]
 
 
@@ -828,14 +844,15 @@
 BACKWARD_COST = 18_000_000_000
 
 
-def assemble_kernel(layers, factor, place_ref, *refs):
+def assemble_kernel(layers, factor, place_ref, order_ref, *refs):
     count = 2 * len(layers)
     sources, (left_ref, right_ref) = refs[:count], refs[count : count + 2]
-    held, wide, in_sems, out_sems = refs[count + 2 :]
-    width, chunk = held.shape[1], held.shape[4]
+    held, wide = refs[count + 2 : 2 * count + 2], refs[2 * count + 2 : 3 * count + 2]
+    in_sems, out_sems = refs[3 * count + 2 :]
     origin, core = place_ref[0] ^ place_ref[1], place_ref[2]
+    order = order_ref[...]
     arrivals = [
-        pltpu.make_async_copy(source, held.at[at], in_sems.at[at]) for at, source in enumerate(sources)
+        pltpu.make_async_copy(source, held[at], in_sems.at[at]) for at, source in enumerate(sources)
     ]
     for copy in arrivals:
         copy.start()
@@ -843,13 +860,17 @@
     for at in range(count):
         arrivals[at].wait()
         half = core if at % 2 == 0 else 1 - core
+        width, _, _, chunk = held[at].shape[:4]
         for k in range(width):
-            wide[at, k] = held[at, k].astype(jnp.float32) * factor
             start = (half * width + (origin ^ k)) * chunk
             for inside, layer in enumerate(layers[at // 2]):
+                for block in range(chunk):
+                    left = inner_dot(held[at][k, inside, 0, block], order, 1, 1)
+                    wide[at][k, inside, 0, block] = left * factor
+                wide[at][k, inside, 1] = held[at][k, inside, 1].astype(jnp.float32) * factor
                 for which, target in enumerate((left_ref, right_ref)):
                     copy = pltpu.make_async_copy(
-                        wide.at[at, k, inside, which],
+                        wide[at].at[k, inside, which],
                         target.at[layer, pl.ds(start, chunk)],
                         out_sems.at[len(leaving)],
                     )
@@ -859,27 +880,25 @@
         copy.wait()
 
 
-def run_assemble(place, pieces, layers, factor):
+def run_assemble(place, order, pieces, layers, factor):
     piece = pieces[0].shape
     layer_count = sum(len(group) for group in layers)
     out = shape_of((layer_count, 2 * piece[0] * piece[3]) + piece[4:], jnp.float32)
     return pl.pallas_call(
         lambda *refs: assemble_kernel(layers, factor, *refs),
-        in_specs=[SMEM] + [OUTSIDE] * len(pieces),
+        in_specs=[SMEM, INSIDE] + [OUTSIDE] * len(pieces),
         out_specs=[OUTSIDE] * 2,
         out_shape=[out] * 2,
-        scratch_shapes=[
-            pltpu.VMEM((len(pieces),) + piece, jnp.bfloat16),
-            pltpu.VMEM((len(pieces),) + piece, jnp.float32),
+        scratch_shapes=[pltpu.VMEM(part.shape, jnp.bfloat16) for part in pieces]
+        + [pltpu.VMEM(part.shape, jnp.float32) for part in pieces]
+        + [
             pltpu.SemaphoreType.DMA((len(pieces),)),
             pltpu.SemaphoreType.DMA((4 * layer_count * piece[0],)),
         ],
         compiler_params=pltpu.CompilerParams(vmem_limit_bytes=VMEM_LIMIT),
-        cost_estimate=pl.CostEstimate(
-            flops=0, bytes_accessed=6 * len(pieces) * math.prod(piece), transcendentals=0
-        ),
+        cost_estimate=pl.CostEstimate(flops=0, bytes_accessed=4 * math.prod(out.shape) * 3, transcendentals=0),
         name="assemble",
-    )(place, *pieces)
+    )(place, order, *pieces)
 
 
 def plane_routes(width, replicas):
@@ -965,7 +984,10 @@
     factors = (left_factors[0], right_factors[0])
     groups = [tuple(range(0, 2)), tuple(range(2, layer_count))]
     gain_rows = norm_gains[0].reshape(-1, size)
-    pieces = factor_pieces(place, *factors, gain_rows, groups, chunk)
+    fold = size // blocks
+    columns = jnp.arange(size)
+    order = (columns[:, None] == (columns % blocks) * fold + columns // blocks).astype(jnp.bfloat16)
+    pieces = factor_pieces(place, order, *factors, gain_rows, groups, chunk, width)
 
     group_rows = [len(group) * layer_rows for group in groups]
 
@@ -975,26 +997,27 @@
     near = move_all(pieces[0], "spread")
     patch_sent = run_pick(critic_pairs, patches, width, wide)
     near, patch_sent, pieces[1] = tie((near, patch_sent, pieces[1]))
-    patch_came = to_planes(patch_sent).reshape(-1, wide)
     came = move_all(near, "lift")
     far = move_all(pieces[1], "spread")
-    came, far = tie((came, far))
+    came, far, patch_sent = tie((came, far, patch_sent))
     lowest = lowest_of(came, 0)
     beside = move(lowest, routes["across"][0])
     late = move_all(far, "lift")
     gains = jnp.stack([value[group_rows[0] :] for value in came])[jnp.arange(width) ^ section ^ tensor]
     gains = gains.reshape(width, layer_count + 1, feat_local).transpose(1, 0, 2).reshape(layer_count + 1, -1)
-    lowest, beside, late, patch_came = tie((lowest, beside, late, patch_came))
+    columns = [jnp.broadcast_to(gain[:, None], (gain.shape[0], wide)) for gain in gains]
+    lowest, beside, late, columns, patch_sent = tie((lowest, beside, late, columns, patch_sent))
+    patch_came = to_planes(patch_sent).reshape(-1, wide)
     first_two = gather_two(joined([lowest, beside]))
-    columns = [jnp.broadcast_to(gain[:, None], (gain.shape[0], wide)) for gain in gains]
     target_sent = run_pick(critic_pairs, teacher, width, wide)
-    first_two, late, columns, target_sent = tie((first_two, late, columns, target_sent))
+    first_two, late, target_sent = tie((first_two, late, target_sent))
     weights = [as_weights(gather_three(*first_two))]
-    later = gather_one(lowest_of(late, 1))
+    later = lowest_of(late, 1)
+    later = (later, move(later, routes["across"][0]))
+    weights, later, patch_came = tie((weights, later, patch_came))
 
     residual = patch_came
-    residual, weights, later = tie((residual, weights, later))
-    flying = gather_two(later)
+    flying = gather_two(joined(list(later)))
     sums = jnp.zeros((8, wide), jnp.float32)
     stored = []
     for layer in range(layer_count):
@@ -1054,15 +1077,17 @@
     ended = [steps[at](*state) if at < len(steps) else state for at, state in underway][::-1]
     ended = tie(ended)
     ended[0] = plane_sum(*ended[0])
-    homes_of = [None, homeward(ended[groups[1][0] :])]
-    returned, ended[: groups[1][0]], homes_of[1] = tie((returned, ended[: groups[1][0]], homes_of[1]))
-    home = homeward(ended[: groups[1][0]])
+    homes_of = [None, homeward(ended[1:])]
+    ended[0], homes_of[1], returned = tie((ended[0], homes_of[1], returned))
+    home = homeward(ended[:1])
     homes_of[1] = both_halves(homes_of[1])
     d_patches = run_combine(critic_pairs, returned)
     d_patches, home, homes_of[1] = tie((d_patches, home, homes_of[1]))
     homes_of[0] = both_halves(home)
     grad_factor = 1.0 / math.sqrt(2 * tok_rows * width * replicas)
-    grad_left, grad_right = run_assemble(place, homes_of[0] + homes_of[1], groups, grad_factor)
+    grad_left, grad_right = run_assemble(
+        place, order, homes_of[0] + homes_of[1], [(0,), tuple(range(1, layer_count))], grad_factor
+    )
     return (d_patches, grad_left[None], grad_right[None])
 
 

time: 540 us -> 518 us (0.959)
  waiting for transfers between devices: 203 us -> 172 us
  starting transfers between devices: 113 us -> 123 us
    ppermute x50, waiting for transfers between devices: 192 us -> 145 us  [move(): return lax.ppermute(value, AXES, route)]
    all_to_all x3, waiting for transfers between devices: 10.2 us -> 27.1 us  [to_planes(): lax.all_to_all(value, 'tensor', split_axis=0, concat_axis=0, tiled=True)]
    ppermute x50, starting transfers between devices: 100 us -> 112 us  [move(): return lax.ppermute(value, AXES, route)]
    unnamed x92 -> x90, local copies, waits for them, and re-layouts: 14.1 us -> 10.6 us
  transfers between devices with their start and end apart: 53 -> 53, of which waited for: 24 -> 21; matrix products, arithmetic and copies ran while one was open for 1% -> 1% of each run, Pallas kernels for 28% -> 28%
where the time goes in v7:
time: 518 us; the launch traced here: 516 us
  Pallas kernels  190 us (37%)
  waiting for transfers between devices  172 us (33%)
  starting transfers between devices  123 us (24%)
  local copies, waits for them, and re-layouts  27.1 us (5%)
    ppermute x50, waiting for transfers between devices, move(): return lax.ppermute(value, AXES, route)  145 us
    ppermute x50, starting transfers between devices, move(): return lax.ppermute(value, AXES, route)  112 us
    pallas_call x4, Pallas kernels, run_backward(): pl.pallas_call(lambda *refs: backward_kernel(turning, last, layer, len(so...  73.6 us
    pallas_call x4, Pallas kernels, run_forward(): pl.pallas_call(lambda *refs: forward_kernel(first, layer, len(sources), *...  53.1 us
    all_to_all x3, waiting for transfers between devices, to_planes(): lax.all_to_all(value, 'tensor', split_axis=0, concat_axis=0, tiled=True)  27.1 us
    pallas_call x6, Pallas kernels, run_sum(): pl.pallas_call(lambda *refs: sum_kernel(len(groups[0]), len(flat), *refs)...  24.9 us
    pallas_call x6, Pallas kernels, joined(): pl.pallas_call(lambda *refs: join_kernel(rows, *refs), in_specs=[OUTSIDE]...  15.6 us
    broadcast_in_dim x5, local copies, waits for them, and re-layouts, plane_shards(): jnp.broadcast_to(gain[:, None], (gain.shape[0], wide))  11.1 us
  transfers between devices with their start and end apart: 53, of which 21 were waited for; matrix products, arithmetic and copies ran while one was open for 1% of the time, Pallas kernels for 28%

profile of v7, /device:TPU:5, one launch (start us, length us, event | category | flops | bytes accessed | tf_op | source)
XLA Modules:
  0.0 515.6 jit_solution(7602463001278715902)
XLA Ops:
  23.0 5.3 %collective-permute-done.2 = bf16[1104,128]{1,0:T(8,128)(2,1)S(1)} collective-permute-done((bf16[1104,128]{1,0:T(8,128)(2,1)}, bf16[1104,128]{1,0:T(8,128)(2,1)S(1)}, u32[]{:S(2)}, u32[]{:S(2)}) %collective-permute-start.2) | collective-permute-done | bytes 282656 | tf_op jit(solution)/shard_map/ppermute | solution.py:947
  33.1 5.5 %collective-permute-start.4 = (bf16[1104,128]{1,0:T(8,128)(2,1)S(1)}, bf16[1104,128]{1,0:T(8,128)(2,1)S(1)}, u32[]{:S(2)}, u32[]{:S(2)}) collective-permute-start(bf16[1104,128]{1,0:T(8,128)(2,1)S(1)} %collective-permute-done), channel_id=1, source_target_pairs={{0,0},{1,1},{2,2},{3,3},{4,4},{5,5},{6,6},{7,7},{8,10},{9,11},{10,... | collective-permute-start | bytes 847880 | tf_op jit(solution)/shard_map/ppermute | solution.py:947
  38.5 6.9 %collective-permute-start.5 = (bf16[1104,128]{1,0:T(8,128)(2,1)S(1)}, bf16[1104,128]{1,0:T(8,128)(2,1)S(1)}, u32[]{:S(2)}, u32[]{:S(2)}) collective-permute-start(bf16[1104,128]{1,0:T(8,128)(2,1)S(1)} %collective-permute-done.1), channel_id=1, source_target_pairs={{0,2},{1,3},{2,0},{3,1},{4,6},{5,7},{6,4},{7,5},{8,8},{9,9},{10,10... | collective-permute-start | bytes 847880 | tf_op jit(solution)/shard_map/ppermute | solution.py:947
  50.2 6.7 %collective-permute-done.11 = bf16[1024,128]{1,0:T(8,128)(2,1)S(1)} collective-permute-done((bf16[1024,128]{1,0:T(8,128)(2,1)S(1)}, bf16[1024,128]{1,0:T(8,128)(2,1)S(1)}, u32[]{:S(2)}, u32[]{:S(2)}) %collective-permute-start.11) | collective-permute-done | bytes 262176 | tf_op jit(solution)/shard_map/ppermute | solution.py:947
  56.9 5.1 collective-permute-done.7.refs_3_
  64.9 4.7 collective-permute-start.12
  69.7 6.5 %collective-permute-start.13 = (bf16[1024,128]{1,0:T(8,128)(2,1)S(1)}, bf16[1024,128]{1,0:T(8,128)(2,1)S(1)}, u32[]{:S(2)}, u32[]{:S(2)}) collective-permute-start(bf16[1024,128]{1,0:T(8,128)(2,1)S(1)} %collective-permute-done.8), channel_id=1, source_target_pairs={{0,0},{1,1},{2,2},{3,3},{4,4},{5,5},{6,6},{7,7},{8,10},{9,11},{10,... | collective-permute-start | bytes 786440 | tf_op jit(solution)/shard_map/ppermute | solution.py:947
  76.2 5.0 collective-permute-start.14
  87.4 6.5 %collective-permute-done.13.refs_0_ = bf16[1024,128]{1,0:T(8,128)(2,1)S(1)} collective-permute-done((bf16[1024,128]{1,0:T(8,128)(2,1)S(1)}, bf16[1024,128]{1,0:T(8,128)(2,1)S(1)}, u32[]{:S(2)}, u32[]{:S(2)}) %collective-permute-start.13) | collective-permute-done | bytes 262176 | tf_op jit(solution)/shard_map/ppermute | solution.py:947
  120.4 17.3 %collective-permute-done.17 = bf16[8,1024,128]{2,1,0:T(8,128)(2,1)} collective-permute-done((bf16[8,1024,128]{2,1,0:T(8,128)(2,1)}, bf16[8,1024,128]{2,1,0:T(8,128)(2,1)}, u32[]{:S(2)}, u32[]{:S(2)}) %collective-permute-start.17) | collective-permute-done | bytes 2097184 | tf_op jit(solution)/shard_map/ppermute | solution.py:947
  145.5 18.1 %all-to-all-done = bf16[4,2048,128]{2,1,0:T(8,128)(2,1)S(1)} async-done(((bf16[4,2048,128]{2,1,0:T(8,128)(2,1)}), bf16[4,2048,128]{2,1,0:T(8,128)(2,1)S(1)}, u32[]{:S(2)}, u32[]{:S(2)}) %all-to-all-start) | async-done | bytes 2097184 | tf_op jit(solution)/shard_map/all_to_all | solution.py:982
  172.5 14.0 %forward_layer.4 = (f32[8192,128]{1,0:T(8,128)}, bf16[8192,128]{1,0:T(8,128)(2,1)}, bf16[8192,128]{1,0:T(8,128)(2,1)}, bf16[8192,128]{1,0:T(8,128)(2,1)}, f32[8,128]{1,0:T(8,128)}, /*index=5*/f32[8,128]{1,0:T(8,128)}) custom-call(s32[2,64]{1,0:T(2,128)} %pad_add_fusion.refs_0_, f32[8,128]{1,0:T(8,128)} %broadcast_in_dim.49.refs_1_, ...), custom_call_target="tpu_custom_call" | custom-call | flops 15000000512 | bytes 20971520 | tf_op jit(solution)/shard_map/forward_layer/pallas_call | solution.py:599
  186.4 8.4 %collective-permute-done.21 = bf16[8,1024,128]{2,1,0:T(8,128)(2,1)} collective-permute-done((bf16[8,1024,128]{2,1,0:T(8,128)(2,1)}, bf16[8,1024,128]{2,1,0:T(8,128)(2,1)}, u32[]{:S(2)}, u32[]{:S(2)}) %collective-permute-start.21) | collective-permute-done | bytes 2097184 | tf_op jit(solution)/shard_map/ppermute | solution.py:947
  194.9 5.8 %collective-permute-start.23 = (bf16[8,1024,128]{2,1,0:T(8,128)(2,1)}, bf16[8,1024,128]{2,1,0:T(8,128)(2,1)}, u32[]{:S(2)}, u32[]{:S(2)}) collective-permute-start(bf16[8,1024,128]{2,1,0:T(8,128)(2,1)} %collective-permute-done.21), channel_id=1, source_target_pairs={{0,1},{1,0},{2,3},{3,2},{4,5},{5,4},{6,7},{7,6},{8,9},{9,8},{10,11... | collective-permute-start | bytes 6291464 | tf_op jit(solution)/shard_map/ppermute | solution.py:947
  204.5 13.0 %forward_layer.5 = (f32[8192,128]{1,0:T(8,128)}, bf16[8192,128]{1,0:T(8,128)(2,1)}, bf16[8192,128]{1,0:T(8,128)(2,1)}, bf16[8192,128]{1,0:T(8,128)(2,1)}, f32[8,128]{1,0:T(8,128)}, /*index=5*/f32[8,128]{1,0:T(8,128)}) custom-call(s32[2,64]{1,0:T(2,128)} %pad_add_fusion.refs_0_, f32[8,128]{1,0:T(8,128)} %get-tuple-element.242.refs_1_, ...), custom_call_target="tpu_custom_call" | custom-call | flops 15000000512 | bytes 20971520 | tf_op jit(solution)/shard_map/forward_layer/pallas_call | solution.py:599
  217.5 13.1 %forward_layer.6 = (f32[8192,128]{1,0:T(8,128)}, bf16[8192,128]{1,0:T(8,128)(2,1)}, bf16[8192,128]{1,0:T(8,128)(2,1)}, bf16[8192,128]{1,0:T(8,128)(2,1)}, f32[8,128]{1,0:T(8,128)}, /*index=5*/f32[8,128]{1,0:T(8,128)}) custom-call(s32[2,64]{1,0:T(2,128)} %pad_add_fusion.refs_0_, f32[8,128]{1,0:T(8,128)} %get-tuple-element.254.refs_1_, ...), custom_call_target="tpu_custom_call" | custom-call | flops 15000000512 | bytes 20971520 | tf_op jit(solution)/shard_map/forward_layer/pallas_call | solution.py:599
  230.6 13.1 %forward_layer.7 = (f32[8192,128]{1,0:T(8,128)}, bf16[8192,128]{1,0:T(8,128)(2,1)}, bf16[8192,128]{1,0:T(8,128)(2,1)}, bf16[8192,128]{1,0:T(8,128)(2,1)}, f32[8,128]{1,0:T(8,128)}, /*index=5*/f32[8,128]{1,0:T(8,128)}) custom-call(s32[2,64]{1,0:T(2,128)} %pad_add_fusion.refs_0_, f32[8,128]{1,0:T(8,128)} %get-tuple-element.265.refs_1_, ...), custom_call_target="tpu_custom_call" | custom-call | flops 15000000512 | bytes 20971520 | tf_op jit(solution)/shard_map/forward_layer/pallas_call | solution.py:599
  243.6 9.0 %all-to-all-done.1 = bf16[4,2048,128]{2,1,0:T(8,128)(2,1)S(1)} async-done(((bf16[4,2048,128]{2,1,0:T(8,128)(2,1)}), bf16[4,2048,128]{2,1,0:T(8,128)(2,1)S(1)}, u32[]{:S(2)}, u32[]{:S(2)}) %all-to-all-start.1) | async-done | bytes 2097184 | tf_op jit(solution)/shard_map/all_to_all | solution.py:982
  253.9 19.7 %backward_layer.4 = (f32[8192,128]{1,0:T(8,128)}, bf16[16,2,2,128,128]{4,3,2,1,0:T(8,128)(2,1)}, bf16[16,2,2,128,128]{4,3,2,1,0:T(8,128)(2,1)}) custom-call(s32[2,64]{1,0:T(2,128)} %pad_add_fusion.refs_0_, f32[8,128]{1,0:T(8,128)} %get-tuple-element.268.refs_1_, bf16[8192,128]{1,0:T(8,128)(2,1)} %broadcast_in_dim.57.refs_2_, ...), custom_call_target="tpu_custom_call" | custom-call | flops 17999998976 | bytes 31457280 | tf_op jit(solution)/shard_map/backward_layer/pallas_call | solution.py:632
  274.5 18.3 %backward_layer.5 = (f32[8192,128]{1,0:T(8,128)}, bf16[16,2,2,128,128]{4,3,2,1,0:T(8,128)(2,1)}, bf16[16,2,2,128,128]{4,3,2,1,0:T(8,128)(2,1)}) custom-call(s32[2,64]{1,0:T(2,128)} %pad_add_fusion.refs_0_, f32[8,128]{1,0:T(8,128)} %get-tuple-element.261.refs_1_, bf16[8192,128]{1,0:T(8,128)(2,1)} %broadcast_in_dim.55.refs_2_, ...), custom_call_target="tpu_custom_call" | custom-call | flops 17999998976 | bytes 31457280 | tf_op jit(solution)/shard_map/backward_layer/pallas_call | solution.py:632
  301.1 18.2 %backward_layer.6 = (f32[8192,128]{1,0:T(8,128)}, bf16[16,2,2,128,128]{4,3,2,1,0:T(8,128)(2,1)}, bf16[16,2,2,128,128]{4,3,2,1,0:T(8,128)(2,1)}) custom-call(s32[2,64]{1,0:T(2,128)} %pad_add_fusion.refs_0_, f32[8,128]{1,0:T(8,128)} %get-tuple-element.245.refs_1_, bf16[8192,128]{1,0:T(8,128)(2,1)} %broadcast_in_dim.53.refs_2_, ...), custom_call_target="tpu_custom_call" | custom-call | flops 17999998976 | bytes 31457280 | tf_op jit(solution)/shard_map/backward_layer/pallas_call | solution.py:632
  319.4 4.7 collective-permute-done.27
  332.3 17.4 %backward_layer.7 = (bf16[8192,128]{1,0:T(8,128)(2,1)}, bf16[16,2,2,128,128]{4,3,2,1,0:T(8,128)(2,1)}, bf16[16,2,2,128,128]{4,3,2,1,0:T(8,128)(2,1)}) custom-call(s32[2,64]{1,0:T(2,128)} %pad_add_fusion.refs_0_, f32[8,128]{1,0:T(8,128)} %get-tuple-element.232.refs_1_, bf16[8192,128]{1,0:T(8,128)(2,1)} %broadcast_in_dim.51.refs_2_, ...), custom_call_target="tpu_custom_call" | custom-call | flops 17999998976 | bytes 31457280 | tf_op jit(solution)/shard_map/backward_layer/pallas_call | solution.py:632
  367.8 10.7 %collective-permute-done.34 = bf16[2048,128]{1,0:T(8,128)(2,1)S(1)} collective-permute-done((bf16[2048,128]{1,0:T(8,128)(2,1)}, bf16[2048,128]{1,0:T(8,128)(2,1)S(1)}, u32[]{:S(2)}, u32[]{:S(2)}) %collective-permute-start.34) | collective-permute-done | bytes 524320 | tf_op jit(solution)/shard_map/ppermute | solution.py:947
  378.5 11.2 %collective-permute-done.35 = bf16[2048,128]{1,0:T(8,128)(2,1)S(1)} collective-permute-done((bf16[2048,128]{1,0:T(8,128)(2,1)}, bf16[2048,128]{1,0:T(8,128)(2,1)S(1)}, u32[]{:S(2)}, u32[]{:S(2)}) %collective-permute-start.35) | collective-permute-done | bytes 524320 | tf_op jit(solution)/shard_map/ppermute | solution.py:947
  392.1 4.8 sum.10
  397.0 5.9 %collective-permute-start.41 = (bf16[1536,128]{1,0:T(8,128)(2,1)}, bf16[1536,128]{1,0:T(8,128)(2,1)S(1)}, u32[]{:S(2)}, u32[]{:S(2)}) collective-permute-start(bf16[1536,128]{1,0:T(8,128)(2,1)} %bitcast.173), channel_id=1, source_target_pairs={{0,2},{1,3},{2,8},{3,9},{4,22},{5,23},{6,28},{7,29},{8,0},{9,1},{1... | collective-permute-start | bytes 1179656 | tf_op jit(solution)/shard_map/ppermute | solution.py:947
  412.4 19.4 %collective-permute-done.41.refs_1_ = bf16[1536,128]{1,0:T(8,128)(2,1)S(1)} collective-permute-done((bf16[1536,128]{1,0:T(8,128)(2,1)}, bf16[1536,128]{1,0:T(8,128)(2,1)S(1)}, u32[]{:S(2)}, u32[]{:S(2)}) %collective-permute-start.41) | collective-permute-done | bytes 393248 | tf_op jit(solution)/shard_map/ppermute | solution.py:947
  433.7 6.0 %collective-permute-done.40.refs_0_ = bf16[1536,128]{1,0:T(8,128)(2,1)S(1)} collective-permute-done((bf16[1536,128]{1,0:T(8,128)(2,1)}, bf16[1536,128]{1,0:T(8,128)(2,1)S(1)}, u32[]{:S(2)}, u32[]{:S(2)}) %collective-permute-start.40) | collective-permute-done | bytes 393248 | tf_op jit(solution)/shard_map/ppermute | solution.py:947
  441.9 24.4 %collective-permute-done.42.refs_2_ = bf16[1536,128]{1,0:T(8,128)(2,1)S(1)} collective-permute-done((bf16[1536,128]{1,0:T(8,128)(2,1)}, bf16[1536,128]{1,0:T(8,128)(2,1)S(1)}, u32[]{:S(2)}, u32[]{:S(2)}) %collective-permute-start.42) | collective-permute-done | bytes 393248 | tf_op jit(solution)/shard_map/ppermute | solution.py:947
  487.3 7.4 %collective-permute-start.47 = (bf16[512,128]{1,0:T(8,128)(2,1)}, bf16[512,128]{1,0:T(8,128)(2,1)S(1)}, u32[]{:S(2)}, u32[]{:S(2)}) collective-permute-start(bf16[512,128]{1,0:T(8,128)(2,1)} %bitcast.174), channel_id=1, source_target_pairs={{0,6},{1,7},{2,12},{3,13},{4,18},{5,19},{6,24},{7,25},{8,4},{9,5},... | collective-permute-start | bytes 393224 | tf_op jit(solution)/shard_map/ppermute | solution.py:947
  509.5 5.9 %assemble.1 = (f32[4,16,128,128]{3,2,1,0:T(8,128)}, f32[4,16,128,128]{3,2,1,0:T(8,128)}) custom-call(s32[3]{0:T(128)} %pad_add_fusion.1.refs_0_, bf16[128,128]{1,0:T(8,128)(2,1)} %fusion.refs_1_, bf16[4,1,2,2,128,128]{5,4,3,2,1,0:T(8,128)(2,1)} %bitcast.110, bf16[4,1,2,2,128,128]{5,4,3,2,1,0:T(8,128)(2,1)} %bitcast.142, ...), custom_call_target="tpu_custom_call" | custom-call | bytes 12582912 | tf_op jit(solution)/shard_map/assemble/pallas_call | solution.py:887
  (211 shorter events, 176.2 us)
Async XLA Ops:
  33.1 23.8 %collective-permute-start.4 = (bf16[1104,128]{1,0:T(8,128)(2,1)S(1)}, bf16[1104,128]{1,0:T(8,128)(2,1)S(1)}, u32[]{:S(2)}, u32[]{:S(2)}) collective-permute-start(bf16[1104,128]{1,0:T(8,128)(2,1)S(1)} %collective-permute-done), channel_id=1, source_target_pairs={{0,0},{1,1},{2,2},{3,3},{4,4},{5,5},{6,6},{7,7},{8,10},{9,11},{10,... | collective-permute-start | bytes 847880 | tf_op jit(solution)/shard_map/ppermute | solution.py:947
  64.9 33.1 %collective-permute-start.12 = (bf16[4,1024,128]{2,1,0:T(8,128)(2,1)}, bf16[4,1024,128]{2,1,0:T(8,128)(2,1)S(1)}, u32[]{:S(2)}, u32[]{:S(2)}) collective-permute-start(bf16[4,1024,128]{2,1,0:T(8,128)(2,1)} %bitcast.104), channel_id=1, source_target_pairs={{0,8},{1,17},{2,10},{3,19},{4,12},{5,21},{6,14},{7,23},{8,0},{9,25... | collective-permute-start | bytes 3145736 | tf_op jit(solution)/shard_map/ppermute | solution.py:947
  69.7 24.2 %collective-permute-start.13 = (bf16[1024,128]{1,0:T(8,128)(2,1)S(1)}, bf16[1024,128]{1,0:T(8,128)(2,1)S(1)}, u32[]{:S(2)}, u32[]{:S(2)}) collective-permute-start(bf16[1024,128]{1,0:T(8,128)(2,1)S(1)} %collective-permute-done.8), channel_id=1, source_target_pairs={{0,0},{1,1},{2,2},{3,3},{4,4},{5,5},{6,6},{7,7},{8,10},{9,11},{10,... | collective-permute-start | bytes 786440 | tf_op jit(solution)/shard_map/ppermute | solution.py:947
  112.1 25.6 %collective-permute-start.17 = (bf16[8,1024,128]{2,1,0:T(8,128)(2,1)}, bf16[8,1024,128]{2,1,0:T(8,128)(2,1)}, u32[]{:S(2)}, u32[]{:S(2)}) collective-permute-start(bf16[8,1024,128]{2,1,0:T(8,128)(2,1)} %join.7), channel_id=1, source_target_pairs={{0,16},{1,9},{2,18},{3,11},{4,20},{5,13},{6,22},{7,15},{8,24},{9,1... | collective-permute-start | bytes 6291464 | tf_op jit(solution)/shard_map/ppermute | solution.py:947
  112.6 51.0 %all-to-all-start = ((bf16[4,2048,128]{2,1,0:T(8,128)(2,1)}), bf16[4,2048,128]{2,1,0:T(8,128)(2,1)S(1)}, u32[]{:S(2)}, u32[]{:S(2)}) async-start(bf16[4,2048,128]{2,1,0:T(8,128)(2,1)} %pick.2), calls=%async_computation | async-start | bytes 4194304 | tf_op jit(solution)/shard_map/all_to_all | solution.py:982
  137.7 25.9 %collective-permute-start.19 = (bf16[8,1024,128]{2,1,0:T(8,128)(2,1)}, bf16[8,1024,128]{2,1,0:T(8,128)(2,1)}, u32[]{:S(2)}, u32[]{:S(2)}) collective-permute-start(bf16[8,1024,128]{2,1,0:T(8,128)(2,1)} %collective-permute-done.17), channel_id=1, source_target_pairs={{0,1},{1,0},{2,3},{3,2},{4,5},{5,4},{6,7},{7,6},{8,9},{9,8},{10,11... | collective-permute-start | bytes 6291464 | tf_op jit(solution)/shard_map/ppermute | solution.py:947
  142.4 21.2 %collective-permute-start.20 = (bf16[4,1024,128]{2,1,0:T(8,128)(2,1)}, bf16[4,1024,128]{2,1,0:T(8,128)(2,1)S(1)}, u32[]{:S(2)}, u32[]{:S(2)}) collective-permute-start(bf16[4,1024,128]{2,1,0:T(8,128)(2,1)} %bitcast.106), channel_id=1, source_target_pairs={{0,8},{1,17},{2,10},{3,19},{4,12},{5,21},{6,14},{7,23},{8,0},{9,25... | collective-permute-start | bytes 3145736 | tf_op jit(solution)/shard_map/ppermute | solution.py:947
  167.5 18.9 %collective-permute-start.22 = (bf16[8,1024,128]{2,1,0:T(8,128)(2,1)}, bf16[8,1024,128]{2,1,0:T(8,128)(2,1)}, u32[]{:S(2)}, u32[]{:S(2)}) collective-permute-start(bf16[8,1024,128]{2,1,0:T(8,128)(2,1)} %join.9), channel_id=1, source_target_pairs={{0,1},{1,0},{2,3},{3,2},{4,5},{5,4},{6,7},{7,6},{8,9},{9,8},{10,11... | collective-permute-start | bytes 6291464 | tf_op jit(solution)/shard_map/ppermute | solution.py:947
  169.4 25.5 %collective-permute-start.21 = (bf16[8,1024,128]{2,1,0:T(8,128)(2,1)}, bf16[8,1024,128]{2,1,0:T(8,128)(2,1)}, u32[]{:S(2)}, u32[]{:S(2)}) collective-permute-start(bf16[8,1024,128]{2,1,0:T(8,128)(2,1)} %join.9), channel_id=1, source_target_pairs={{0,16},{1,9},{2,18},{3,11},{4,20},{5,13},{6,22},{7,15},{8,24},{9,1... | collective-permute-start | bytes 6291464 | tf_op jit(solution)/shard_map/ppermute | solution.py:947
  194.9 22.6 %collective-permute-start.23 = (bf16[8,1024,128]{2,1,0:T(8,128)(2,1)}, bf16[8,1024,128]{2,1,0:T(8,128)(2,1)}, u32[]{:S(2)}, u32[]{:S(2)}) collective-permute-start(bf16[8,1024,128]{2,1,0:T(8,128)(2,1)} %collective-permute-done.21), channel_id=1, source_target_pairs={{0,1},{1,0},{2,3},{3,2},{4,5},{5,4},{6,7},{7,6},{8,9},{9,8},{10,11... | collective-permute-start | bytes 6291464 | tf_op jit(solution)/shard_map/ppermute | solution.py:947
  200.7 51.9 %all-to-all-start.1 = ((bf16[4,2048,128]{2,1,0:T(8,128)(2,1)}), bf16[4,2048,128]{2,1,0:T(8,128)(2,1)S(1)}, u32[]{:S(2)}, u32[]{:S(2)}) async-start(bf16[4,2048,128]{2,1,0:T(8,128)(2,1)} %pick.3), calls=%async_computation.1 | async-start | bytes 4194304 | tf_op jit(solution)/shard_map/all_to_all | solution.py:982
  273.6 19.1 %collective-permute-start.24 = (bf16[16,2,2,128,128]{4,3,2,1,0:T(8,128)(2,1)}, bf16[16,2,2,128,128]{4,3,2,1,0:T(8,128)(2,1)S(1)}, u32[]{:S(2)}, u32[]{:S(2)}) collective-permute-start(bf16[16,2,2,128,128]{4,3,2,1,0:T(8,128)(2,1)} %get-tuple-element.279), channel_id=1, source_target_pairs={{0,1},{1,0},{2,3},{3,2},{4,5},{5,4},{6,7},{7,6},{8,9},{9,8},{10,11... | collective-permute-start | bytes 6291464 | tf_op jit(solution)/shard_map/ppermute | solution.py:947
  294.1 30.1 %collective-permute-start.28 = (bf16[16,2,2,128,128]{4,3,2,1,0:T(8,128)(2,1)}, bf16[16,2,2,128,128]{4,3,2,1,0:T(8,128)(2,1)S(1)}, u32[]{:S(2)}, u32[]{:S(2)}) collective-permute-start(bf16[16,2,2,128,128]{4,3,2,1,0:T(8,128)(2,1)} %get-tuple-element.291), channel_id=1, source_target_pairs={{0,1},{1,0},{2,3},{3,2},{4,5},{5,4},{6,7},{7,6},{8,9},{9,8},{10,11... | collective-permute-start | bytes 6291464 | tf_op jit(solution)/shard_map/ppermute | solution.py:947
  298.2 21.2 %collective-permute-start.25 = (bf16[2048,128]{1,0:T(8,128)(2,1)}, bf16[2048,128]{1,0:T(8,128)(2,1)S(1)}, u32[]{:S(2)}, u32[]{:S(2)}) collective-permute-start(bf16[2048,128]{1,0:T(8,128)(2,1)} %bitcast.166), channel_id=1, source_target_pairs={{0,8},{1,9},{2,10},{3,11},{4,12},{5,13},{6,14},{7,15},{8,0},{9,1},... | collective-permute-start | bytes 1572872 | tf_op jit(solution)/shard_map/ppermute | solution.py:947
  298.9 20.5 %collective-permute-start.26 = (bf16[2048,128]{1,0:T(8,128)(2,1)}, bf16[2048,128]{1,0:T(8,128)(2,1)S(1)}, u32[]{:S(2)}, u32[]{:S(2)}) collective-permute-start(bf16[2048,128]{1,0:T(8,128)(2,1)} %bitcast.165), channel_id=1, source_target_pairs={{0,16},{1,17},{2,18},{3,19},{4,20},{5,21},{6,22},{7,23},{8,24},{9,... | collective-permute-start | bytes 1572872 | tf_op jit(solution)/shard_map/ppermute | solution.py:947
  300.6 23.5 %collective-permute-start.27 = (bf16[2048,128]{1,0:T(8,128)(2,1)}, bf16[2048,128]{1,0:T(8,128)(2,1)S(1)}, u32[]{:S(2)}, u32[]{:S(2)}) collective-permute-start(bf16[2048,128]{1,0:T(8,128)(2,1)} %bitcast.163), channel_id=1, source_target_pairs={{0,24},{1,25},{2,26},{3,27},{4,28},{5,29},{6,30},{7,31},{8,16},{9,... | collective-permute-start | bytes 1572872 | tf_op jit(solution)/shard_map/ppermute | solution.py:947
  324.1 29.8 %collective-permute-start.32 = (bf16[16,2,2,128,128]{4,3,2,1,0:T(8,128)(2,1)}, bf16[16,2,2,128,128]{4,3,2,1,0:T(8,128)(2,1)}, u32[]{:S(2)}, u32[]{:S(2)}) collective-permute-start(bf16[16,2,2,128,128]{4,3,2,1,0:T(8,128)(2,1)} %get-tuple-element.307), channel_id=1, source_target_pairs={{0,1},{1,0},{2,3},{3,2},{4,5},{5,4},{6,7},{7,6},{8,9},{9,8},{10,11... | collective-permute-start | bytes 6291464 | tf_op jit(solution)/shard_map/ppermute | solution.py:947
  329.7 20.1 %collective-permute-start.29 = (bf16[2048,128]{1,0:T(8,128)(2,1)}, bf16[2048,128]{1,0:T(8,128)(2,1)S(1)}, u32[]{:S(2)}, u32[]{:S(2)}) collective-permute-start(bf16[2048,128]{1,0:T(8,128)(2,1)} %bitcast.164), channel_id=1, source_target_pairs={{0,8},{1,9},{2,10},{3,11},{4,12},{5,13},{6,14},{7,15},{8,0},{9,1},... | collective-permute-start | bytes 1572872 | tf_op jit(solution)/shard_map/ppermute | solution.py:947
  330.3 20.3 %collective-permute-start.30 = (bf16[2048,128]{1,0:T(8,128)(2,1)}, bf16[2048,128]{1,0:T(8,128)(2,1)S(1)}, u32[]{:S(2)}, u32[]{:S(2)}) collective-permute-start(bf16[2048,128]{1,0:T(8,128)(2,1)} %bitcast.162), channel_id=1, source_target_pairs={{0,16},{1,17},{2,18},{3,19},{4,20},{5,21},{6,22},{7,23},{8,24},{9,... | collective-permute-start | bytes 1572872 | tf_op jit(solution)/shard_map/ppermute | solution.py:947
  331.4 22.5 %collective-permute-start.31 = (bf16[2048,128]{1,0:T(8,128)(2,1)}, bf16[2048,128]{1,0:T(8,128)(2,1)S(1)}, u32[]{:S(2)}, u32[]{:S(2)}) collective-permute-start(bf16[2048,128]{1,0:T(8,128)(2,1)} %bitcast.161), channel_id=1, source_target_pairs={{0,24},{1,25},{2,26},{3,27},{4,28},{5,29},{6,30},{7,31},{8,16},{9,... | collective-permute-start | bytes 1572872 | tf_op jit(solution)/shard_map/ppermute | solution.py:947
  354.7 116.5 %all-to-all-start.2 = ((bf16[4,2048,128]{2,1,0:T(8,128)(2,1)}), bf16[4,2048,128]{2,1,0:T(8,128)(2,1)S(1)}, u32[]{:S(2)}, u32[]{:S(2)}) async-start(bf16[4,2048,128]{2,1,0:T(8,128)(2,1)} %bitcast.117), calls=%async_computation.2 | async-start | bytes 4194304 | tf_op jit(solution)/shard_map/all_to_all | solution.py:982
  358.4 33.0 %collective-permute-start.33 = (bf16[16,2,2,128,128]{4,3,2,1,0:T(8,128)(2,1)}, bf16[16,2,2,128,128]{4,3,2,1,0:T(8,128)(2,1)}, u32[]{:S(2)}, u32[]{:S(2)}) collective-permute-start(bf16[16,2,2,128,128]{4,3,2,1,0:T(8,128)(2,1)} %get-tuple-element.309), channel_id=1, source_target_pairs={{0,1},{1,0},{2,3},{3,2},{4,5},{5,4},{6,7},{7,6},{8,9},{9,8},{10,11... | collective-permute-start | bytes 6291464 | tf_op jit(solution)/shard_map/ppermute | solution.py:947
  365.5 24.2 %collective-permute-start.35 = (bf16[2048,128]{1,0:T(8,128)(2,1)}, bf16[2048,128]{1,0:T(8,128)(2,1)S(1)}, u32[]{:S(2)}, u32[]{:S(2)}) collective-permute-start(bf16[2048,128]{1,0:T(8,128)(2,1)} %bitcast.168), channel_id=1, source_target_pairs={{0,16},{1,17},{2,18},{3,19},{4,20},{5,21},{6,22},{7,23},{8,24},{9,... | collective-permute-start | bytes 1572872 | tf_op jit(solution)/shard_map/ppermute | solution.py:947
  367.3 24.0 %collective-permute-start.36 = (bf16[2048,128]{1,0:T(8,128)(2,1)}, bf16[2048,128]{1,0:T(8,128)(2,1)S(1)}, u32[]{:S(2)}, u32[]{:S(2)}) collective-permute-start(bf16[2048,128]{1,0:T(8,128)(2,1)} %bitcast.167), channel_id=1, source_target_pairs={{0,24},{1,25},{2,26},{3,27},{4,28},{5,29},{6,30},{7,31},{8,16},{9,... | collective-permute-start | bytes 1572872 | tf_op jit(solution)/shard_map/ppermute | solution.py:947
  397.0 34.8 %collective-permute-start.41 = (bf16[1536,128]{1,0:T(8,128)(2,1)}, bf16[1536,128]{1,0:T(8,128)(2,1)S(1)}, u32[]{:S(2)}, u32[]{:S(2)}) collective-permute-start(bf16[1536,128]{1,0:T(8,128)(2,1)} %bitcast.173), channel_id=1, source_target_pairs={{0,2},{1,3},{2,8},{3,9},{4,22},{5,23},{6,28},{7,29},{8,0},{9,1},{1... | collective-permute-start | bytes 1179656 | tf_op jit(solution)/shard_map/ppermute | solution.py:947
  402.9 36.8 %collective-permute-start.40 = (bf16[1536,128]{1,0:T(8,128)(2,1)}, bf16[1536,128]{1,0:T(8,128)(2,1)S(1)}, u32[]{:S(2)}, u32[]{:S(2)}) collective-permute-start(bf16[1536,128]{1,0:T(8,128)(2,1)} %bitcast.172), channel_id=1, source_target_pairs={{0,0},{1,1},{2,10},{3,11},{4,20},{5,21},{6,30},{7,31},{8,2},{9,3},... | collective-permute-start | bytes 1179656 | tf_op jit(solution)/shard_map/ppermute | solution.py:947
  409.6 60.9 %collective-permute-start.37 = (bf16[2048,128]{1,0:T(8,128)(2,1)}, bf16[2048,128]{1,0:T(8,128)(2,1)S(1)}, u32[]{:S(2)}, u32[]{:S(2)}) collective-permute-start(bf16[2048,128]{1,0:T(8,128)(2,1)} %bitcast.160), channel_id=1, source_target_pairs={{0,8},{1,9},{2,10},{3,11},{4,12},{5,13},{6,14},{7,15},{8,0},{9,1},... | collective-permute-start | bytes 1572872 | tf_op jit(solution)/shard_map/ppermute | solution.py:947
  411.2 59.3 %collective-permute-start.38 = (bf16[2048,128]{1,0:T(8,128)(2,1)}, bf16[2048,128]{1,0:T(8,128)(2,1)S(1)}, u32[]{:S(2)}, u32[]{:S(2)}) collective-permute-start(bf16[2048,128]{1,0:T(8,128)(2,1)} %bitcast.159), channel_id=1, source_target_pairs={{0,16},{1,17},{2,18},{3,19},{4,20},{5,21},{6,22},{7,23},{8,24},{9,... | collective-permute-start | bytes 1572872 | tf_op jit(solution)/shard_map/ppermute | solution.py:947
  411.2 60.1 %collective-permute-start.39 = (bf16[2048,128]{1,0:T(8,128)(2,1)}, bf16[2048,128]{1,0:T(8,128)(2,1)}, u32[]{:S(2)}, u32[]{:S(2)}) collective-permute-start(bf16[2048,128]{1,0:T(8,128)(2,1)} %bitcast.158), channel_id=1, source_target_pairs={{0,24},{1,25},{2,26},{3,27},{4,28},{5,29},{6,30},{7,31},{8,16},{9,... | collective-permute-start | bytes 1572872 | tf_op jit(solution)/shard_map/ppermute | solution.py:947
  431.8 34.5 %collective-permute-start.42 = (bf16[1536,128]{1,0:T(8,128)(2,1)}, bf16[1536,128]{1,0:T(8,128)(2,1)S(1)}, u32[]{:S(2)}, u32[]{:S(2)}) collective-permute-start(bf16[1536,128]{1,0:T(8,128)(2,1)} %bitcast.171), channel_id=1, source_target_pairs={{0,4},{1,5},{2,14},{3,15},{4,16},{5,17},{6,26},{7,27},{8,6},{9,7},... | collective-permute-start | bytes 1179656 | tf_op jit(solution)/shard_map/ppermute | solution.py:947
  439.7 30.8 %collective-permute-start.43 = (bf16[1536,128]{1,0:T(8,128)(2,1)}, bf16[1536,128]{1,0:T(8,128)(2,1)S(1)}, u32[]{:S(2)}, u32[]{:S(2)}) collective-permute-start(bf16[1536,128]{1,0:T(8,128)(2,1)} %bitcast.170), channel_id=1, source_target_pairs={{0,6},{1,7},{2,12},{3,13},{4,18},{5,19},{6,24},{7,25},{8,4},{9,5},... | collective-permute-start | bytes 1179656 | tf_op jit(solution)/shard_map/ppermute | solution.py:947
  474.8 28.7 %collective-permute-start.48 = (bf16[6144,128]{1,0:T(8,128)(2,1)}, bf16[6144,128]{1,0:T(8,128)(2,1)}, u32[]{:S(2)}, u32[]{:S(2)}) collective-permute-start(bf16[6144,128]{1,0:T(8,128)(2,1)} %join.10), channel_id=1, source_target_pairs={{0,1},{1,0},{2,3},{3,2},{4,5},{5,4},{6,7},{7,6},{8,9},{9,8},{10,11... | collective-permute-start | bytes 4718600 | tf_op jit(solution)/shard_map/ppermute | solution.py:947
  (63 other events, 712.0 us)

commit v8 on v7

--- a/solution.py
+++ b/solution.py
@@ -511,7 +511,7 @@
 
     def right(block, carry):
         rows = block_rows(block, size)
-        place, home = table_ref[0, block], table_ref[1, block]
+        place, home = table_ref[0, block], table_ref[2 if last else 1, block]
         at = (place // chunk_blocks, 1, place % chunk_blocks)
         to = (home // chunk_blocks, 1, home % chunk_blocks)
         if turning:
@@ -542,7 +542,7 @@
 
     def left(block, total):
         rows = block_rows(block, size)
-        place, home = table_ref[0, block], table_ref[1, block]
+        place, home = table_ref[0, block], table_ref[2 if last else 1, block]
         at = (place // chunk_blocks, 0, place % chunk_blocks)
         to = (home // chunk_blocks, 0, home % chunk_blocks)
         arrived = [mid[pl.ds(q * blocks + block, blocks, stride=size), :] for q in range(fold)]
@@ -693,21 +693,29 @@
     sources, outs = refs[:inputs], refs[inputs:]
     for group in range(inputs // terms):
         mine = sources[group * terms : (group + 1) * terms]
-        for at, out in enumerate(outs):
-            total = sum(ref[at].astype(jnp.float32) for ref in mine)
-            out[group] = total.astype(jnp.bfloat16)
-
-
-def run_sum(groups, outputs):
-    flat = [term.reshape(outputs, -1, term.shape[-1]) for terms in groups for term in terms]
+        for at in range(mine[0].shape[0]):
+            total = sum(ref[at].astype(jnp.float32) for ref in mine).astype(jnp.bfloat16)
+            if len(outs) > 1:
+                outs[at][group] = total
+            else:
+                outs[0][at, group] = total
+
+
+def run_sum(groups, parts, apart=True):
+    flat = [term.reshape(parts, -1, term.shape[-1]) for terms in groups for term in terms]
     _, rows, lanes = flat[0].shape
     steps = 4
-    out_shape = [shape_of((len(groups), rows, lanes), jnp.bfloat16)] * outputs
+    if apart:
+        out_shape = [shape_of((len(groups), rows, lanes), jnp.bfloat16)] * parts
+        out_specs = [pl.BlockSpec((len(groups), rows // steps, lanes), lambda i: (0, i, 0))] * parts
+    else:
+        out_shape = [shape_of((parts, len(groups), rows, lanes), jnp.bfloat16)]
+        out_specs = [pl.BlockSpec((parts, len(groups), rows // steps, lanes), lambda i: (0, 0, i, 0))]
     sums = pl.pallas_call(
         lambda *refs: sum_kernel(len(groups[0]), len(flat), *refs),
         grid=(steps,),
-        in_specs=[pl.BlockSpec((outputs, rows // steps, lanes), lambda i: (0, i, 0))] * len(flat),
-        out_specs=[pl.BlockSpec((len(groups), rows // steps, lanes), lambda i: (0, i, 0))] * outputs,
+        in_specs=[pl.BlockSpec((parts, rows // steps, lanes), lambda i: (0, i, 0))] * len(flat),
+        out_specs=out_specs,
         out_shape=out_shape,
         compiler_params=pltpu.CompilerParams(vmem_limit_bytes=VMEM_LIMIT),
         cost_estimate=pl.CostEstimate(
@@ -715,58 +723,48 @@
         ),
         name="sum",
     )(*flat)
-    return [out.reshape(-1, lanes) for out in sums]
-
-
-def pieces_kernel(groups, chunk, place_ref, order_ref, left_ref, right_ref, gain_ref, *refs):
-    outs, (held, left_sem, sems) = refs[:-3], refs[-3:]
-    size = held.shape[-1]
-    width = len(outs) // len(groups)
-    half = held.shape[1]
-    origin = place_ref[0] ^ place_ref[1]
-    lefts = pltpu.make_async_copy(left_ref.at[:, pl.ds(place_ref[2] * half, half)], held, left_sem.at[0])
+    return [out.reshape(-1, lanes) for out in sums] if apart else sums[0].reshape(parts, -1, lanes)
+
+
+def pieces_kernel(chunk, place_ref, order_ref, left_ref, right_ref, gain_ref, out_ref, held, left_sem, sems):
+    layer_count, half, size = held.shape[:3]
+    first = place_ref[2] * half
+    lefts = pltpu.make_async_copy(left_ref.at[:, pl.ds(first, half)], held, left_sem.at[0])
     lefts.start()
     copies = []
     turns = []
-    for at, group in enumerate(groups):
-        for j in range(width):
-            out = outs[at * width + j]
-            start = (origin ^ j) * chunk
-            row = 0
-            for layer in group:
-                for inside in range(chunk):
-                    turns.append((layer, start + inside, out, row))
-                    row += size
-                for inside in range(chunk):
-                    source = right_ref.at[layer, place_ref[2] * half + start + inside]
-                    copies.append((source, out.at[pl.ds(row, size)]))
-                    row += size
-            if group[0] == 0:
-                copies.append((gain_ref, out.at[pl.ds(row, gain_ref.shape[0])]))
+    for section in range(out_ref.shape[0]):
+        row = 0
+        for layer in range(layer_count):
+            for inside in range(chunk):
+                turns.append((layer, section * chunk + inside, section, row))
+                row += size
+            for inside in range(chunk):
+                source = right_ref.at[layer, first + section * chunk + inside]
+                copies.append((source, out_ref.at[section, pl.ds(row, size)]))
+                row += size
+        copies.append((gain_ref, out_ref.at[section, pl.ds(row, gain_ref.shape[0])]))
     copies = [
         pltpu.make_async_copy(source, target, sems.at[at]) for at, (source, target) in enumerate(copies)
     ]
     for copy in copies:
         copy.start()
     lefts.wait()
-    for layer, block, out, row in turns:
+    for layer, block, section, row in turns:
         turned = inner_dot(held[layer, block], order_ref[...], 1, 0)
-        out[pl.ds(row, size), :] = turned.astype(jnp.bfloat16)
+        out_ref[section, pl.ds(row, size), :] = turned.astype(jnp.bfloat16)
     for copy in copies:
         copy.wait()
 
 
-def factor_pieces(place, order, left, right, gain_rows, groups, chunk, width):
+def factor_pieces(place, order, left, right, gain_rows, chunk, width):
     layer_count, blocks, size = left.shape[:3]
-    shapes = []
-    for group in groups:
-        rows = len(group) * 2 * chunk * size + (gain_rows.shape[0] if group[0] == 0 else 0)
-        shapes += [shape_of((rows, size), jnp.bfloat16)] * width
-    flat = pl.pallas_call(
-        lambda *refs: pieces_kernel(groups, chunk, *refs),
+    rows = layer_count * 2 * chunk * size + gain_rows.shape[0]
+    return pl.pallas_call(
+        lambda *refs: pieces_kernel(chunk, *refs),
         in_specs=[SMEM, INSIDE] + [OUTSIDE] * 3,
-        out_specs=[INSIDE] * len(shapes),
-        out_shape=shapes,
+        out_specs=INSIDE,
+        out_shape=shape_of((width, rows, size), jnp.bfloat16),
         scratch_shapes=[
             pltpu.VMEM((layer_count, blocks // 2, size, size), jnp.bfloat16),
             pltpu.SemaphoreType.DMA((1,)),
@@ -776,7 +774,6 @@
         cost_estimate=pl.CostEstimate(flops=left.size * size, bytes_accessed=4 * left.size, transcendentals=0),
         name="pieces",
     )(place, order, left, right, gain_rows)
-    return [flat[at * width : (at + 1) * width] for at in range(len(groups))]
 
 
 def choice(pairs, critic, slots):
@@ -862,7 +859,7 @@
         half = core if at % 2 == 0 else 1 - core
         width, _, _, chunk = held[at].shape[:4]
         for k in range(width):
-            start = (half * width + (origin ^ k)) * chunk
+            start = (half * width + (origin ^ k if at < 2 else k)) * chunk
             for inside, layer in enumerate(layers[at // 2]):
                 for block in range(chunk):
                     left = inner_dot(held[at][k, inside, 0, block], order, 1, 1)
@@ -917,12 +914,9 @@
         for r in range(width):
             ranks[d][sum(((r >> at) & 1) << orders[d][at] for at in range(bits))] = r
     return {
-        "spread": [route(lambda s, t, d, j=j: (s ^ t ^ j, t, d)) for j in range(width)],
-        "lift": [route(lambda s, t, d, j=j: (s, t ^ s ^ j, d)) for j in range(width)],
         "across": [route(lambda s, t, d, at=at: (s ^ (1 << orders[d][at]), t, d)) for at in range(bits)],
         "cores": route(lambda s, t, d: (s, t, 1 - d)),
         "sections": [route(lambda s, t, d, k=k: (s ^ k, t, d)) for k in range(width)],
-        "planes": [route(lambda s, t, d, k=k: (s, t ^ k, d)) for k in range(width)],
         "homes": [route(lambda s, t, d, j=j: (t, t ^ s ^ j, d)) for j in range(width)],
     }, ranks
 
@@ -969,51 +963,50 @@
     replica = inside // (width * chunk)
     part = (replica != core).astype(jnp.int32)
     distance = section ^ ((inside // chunk) % width)
-    piece = tensor ^ (section ^ distance) ^ (block // local_blocks)
+    quarter = block // local_blocks
     rank = jnp.array(ranks, jnp.int32)[replica, distance]
     table = jnp.stack(
         [
-            ((part * width + rank) * width + piece) * chunk + inside % chunk,
-            ((part * width + distance) * width + piece) * chunk + inside % chunk,
+            ((part * width + index) * width + piece) * chunk + inside % chunk
+            for index, piece in (
+                (rank, quarter),
+                (distance, quarter),
+                (distance, tensor ^ section ^ distance ^ quarter),
+            )
         ]
     ).astype(jnp.int32)
 
     def to_planes(value):
         return lax.all_to_all(value, "tensor", split_axis=0, concat_axis=0, tiled=True)
 
-    factors = (left_factors[0], right_factors[0])
-    groups = [tuple(range(0, 2)), tuple(range(2, layer_count))]
-    gain_rows = norm_gains[0].reshape(-1, size)
+    def to_sections(value):
+        return lax.all_to_all(value, "section", split_axis=0, concat_axis=0, tiled=True)
+
+    half_layers = layer_count // 2
+    groups = [tuple(range(half_layers)), tuple(range(half_layers, layer_count))]
     fold = size // blocks
     columns = jnp.arange(size)
     order = (columns[:, None] == (columns % blocks) * fold + columns // blocks).astype(jnp.bfloat16)
-    pieces = factor_pieces(place, order, *factors, gain_rows, groups, chunk, width)
-
-    group_rows = [len(group) * layer_rows for group in groups]
-
-    def lowest_of(came, at):
-        return joined(came, group_rows[at]).reshape(width, group_rows[at], size)
-
-    near = move_all(pieces[0], "spread")
+    gain_rows = norm_gains[0].reshape(-1, size)
+    pieces = factor_pieces(place, order, left_factors[0], right_factors[0], gain_rows, chunk, width)
+    pieces, patches, teacher = tie((pieces, patches, teacher))
+    spread = to_sections(pieces)
     patch_sent = run_pick(critic_pairs, patches, width, wide)
-    near, patch_sent, pieces[1] = tie((near, patch_sent, pieces[1]))
-    came = move_all(near, "lift")
-    far = move_all(pieces[1], "spread")
-    came, far, patch_sent = tie((came, far, patch_sent))
-    lowest = lowest_of(came, 0)
-    beside = move(lowest, routes["across"][0])
-    late = move_all(far, "lift")
-    gains = jnp.stack([value[group_rows[0] :] for value in came])[jnp.arange(width) ^ section ^ tensor]
-    gains = gains.reshape(width, layer_count + 1, feat_local).transpose(1, 0, 2).reshape(layer_count + 1, -1)
+    target_sent = run_pick(critic_pairs, teacher, width, wide)
+    spread, patch_sent, target_sent = tie((spread, patch_sent, target_sent))
+    lifted = to_planes(spread)
+    lifted, patch_sent = tie((lifted, patch_sent))
+    patch_came = to_planes(patch_sent).reshape(-1, wide)
+    lowest = [lifted[:, group[0] * layer_rows : (group[-1] + 1) * layer_rows] for group in groups]
+    beside = move(lowest[0], routes["across"][0])
+    gains = lifted[:, layer_count * layer_rows :].reshape(width, layer_count + 1, feat_local)
+    gains = gains.transpose(1, 0, 2).reshape(layer_count + 1, -1)
     columns = [jnp.broadcast_to(gain[:, None], (gain.shape[0], wide)) for gain in gains]
-    lowest, beside, late, columns, patch_sent = tie((lowest, beside, late, columns, patch_sent))
-    patch_came = to_planes(patch_sent).reshape(-1, wide)
-    first_two = gather_two(joined([lowest, beside]))
-    target_sent = run_pick(critic_pairs, teacher, width, wide)
-    first_two, late, target_sent = tie((first_two, late, target_sent))
+    lowest, beside, columns = tie((lowest, beside, columns))
+    first_two = gather_two(joined([lowest[0], beside]))
+    first_two, lowest[1] = tie((first_two, lowest[1]))
     weights = [as_weights(gather_three(*first_two))]
-    later = lowest_of(late, 1)
-    later = (later, move(later, routes["across"][0]))
+    later = (lowest[1], move(lowest[1], routes["across"][0]))
     weights, later, patch_came = tie((weights, later, patch_came))
 
     residual = patch_came
@@ -1043,9 +1036,9 @@
     def homeward(parts):
         return move_all(run_sum(parts, width), "homes")
 
-    def both_halves(parts):
-        whole = joined(parts)
-        return [part.reshape(width, -1, 2, chunk, size, size) for part in (whole, move(whole, routes["cores"]))]
+    def both_halves(whole):
+        pair = (whole, move(whole, routes["cores"]))
+        return [part.reshape(width, -1, 2, chunk, size, size) for part in pair]
 
     steps = (core_sum, plane_sum)
     gradient = residual
@@ -1077,16 +1070,16 @@
     ended = [steps[at](*state) if at < len(steps) else state for at, state in underway][::-1]
     ended = tie(ended)
     ended[0] = plane_sum(*ended[0])
-    homes_of = [None, homeward(ended[1:])]
-    ended[0], homes_of[1], returned = tie((ended[0], homes_of[1], returned))
+    others = to_planes(run_sum(ended[1:], width, apart=False))
+    ended[0], returned = tie((ended[0], returned))
     home = homeward(ended[:1])
-    homes_of[1] = both_halves(homes_of[1])
     d_patches = run_combine(critic_pairs, returned)
-    d_patches, home, homes_of[1] = tie((d_patches, home, homes_of[1]))
-    homes_of[0] = both_halves(home)
+    others = to_sections(others)
+    d_patches, home, others = tie((d_patches, home, others))
+    homes_of = both_halves(joined(home)) + both_halves(others)
     grad_factor = 1.0 / math.sqrt(2 * tok_rows * width * replicas)
     grad_left, grad_right = run_assemble(
-        place, order, homes_of[0] + homes_of[1], [(0,), tuple(range(1, layer_count))], grad_factor
+        place, order, homes_of, [(0,), tuple(range(1, layer_count))], grad_factor
     )
     return (d_patches, grad_left[None], grad_right[None])
 

time: 518 us -> 538 us (1.039)
  blocking collectives: 0 us -> 94.3 us
  starting transfers between devices: 123 us -> 60.6 us
  Pallas kernels: 190 us -> 183 us
    all_to_all x0 -> x2, blocking collectives: none -> 94.3 us  [to_planes(): lax.all_to_all(value, 'tensor', split_axis=0, concat_axis=0, tiled=True)]
    ppermute x50 -> x30, starting transfers between devices: 112 us -> 40.6 us  [move(): return lax.ppermute(value, AXES, route)]
    ppermute x50 -> x30, waiting for transfers between devices: 145 us -> 114 us  [move(): return lax.ppermute(value, AXES, route)]
    all_to_all x3, waiting for transfers between devices: 27.1 us -> 42.7 us  [to_planes(): lax.all_to_all(value, 'tensor', split_axis=0, concat_axis=0, tiled=True)]
    all_to_all x0 -> x2, waiting for transfers between devices: none -> 15.5 us  [to_sections(): lax.all_to_all(value, 'section', split_axis=0, concat_axis=0, tiled=True)]
    all_to_all x0 -> x2, starting transfers between devices: none -> 8.98 us  [to_sections(): lax.all_to_all(value, 'section', split_axis=0, concat_axis=0, tiled=True)]
    pallas_call x6 -> x3, Pallas kernels: 15.6 us -> 8.44 us  [joined(): pl.pallas_call(lambda *refs: join_kernel(rows, *refs), in_specs=[OUTSIDE]...]
  transfers between devices with their start and end apart: 53 -> 35, of which waited for: 21 -> 18; matrix products, arithmetic and copies ran while one was open for 1% -> 1% of each run, Pallas kernels for 28% -> 27%
where the time goes in v8:
time: 538 us; the launch traced here: 537 us
  Pallas kernels  183 us (34%)
  waiting for transfers between devices  172 us (32%)
  blocking collectives  94.3 us (18%)
  starting transfers between devices  60.6 us (11%)
  local copies, waits for them, and re-layouts  23.4 us (4%)
    ppermute x30, waiting for transfers between devices, move(): return lax.ppermute(value, AXES, route)  114 us
    all_to_all x2, blocking collectives, to_planes(): lax.all_to_all(value, 'tensor', split_axis=0, concat_axis=0, tiled=True)  94.3 us
    pallas_call x4, Pallas kernels, run_backward(): pl.pallas_call(lambda *refs: backward_kernel(turning, last, layer, len(so...  73.8 us
    pallas_call x4, Pallas kernels, run_forward(): pl.pallas_call(lambda *refs: forward_kernel(first, layer, len(sources), *...  53 us
    all_to_all x3, waiting for transfers between devices, to_planes(): lax.all_to_all(value, 'tensor', split_axis=0, concat_axis=0, tiled=True)  42.7 us
    ppermute x30, starting transfers between devices, move(): return lax.ppermute(value, AXES, route)  40.6 us
    pallas_call x6, Pallas kernels, run_sum(): pl.pallas_call(lambda *refs: sum_kernel(len(groups[0]), len(flat), *refs)...  25 us
    all_to_all x2, waiting for transfers between devices, to_sections(): lax.all_to_all(value, 'section', split_axis=0, concat_axis=0, tiled=True)  15.5 us
  transfers between devices with their start and end apart: 35, of which 18 were waited for; matrix products, arithmetic and copies ran while one was open for 1% of the time, Pallas kernels for 27%

profile of v8, /device:TPU:5, one launch (start us, length us, event | category | flops | bytes accessed | tf_op | source)
XLA Modules:
  0.0 536.6 jit_solution(3235653114460084802)
XLA Ops:
  3.3 4.6 pieces.1
  16.5 4.2 pick.3
  20.7 15.5 %all-to-all-done = bf16[4,2128,128]{2,1,0:T(8,128)(2,1)S(1)} async-done(((bf16[4,2128,128]{2,1,0:T(8,128)(2,1)}), bf16[4,2128,128]{2,1,0:T(8,128)(2,1)S(1)}, u32[]{:S(2)}, u32[]{:S(2)}) %all-to-all-start) | async-done | bytes 2179104 | tf_op jit(solution)/shard_map/all_to_all | solution.py:983
  36.2 53.8 %all_to_all.35 = bf16[4,2128,128]{2,1,0:T(8,128)(2,1)S(1)} all-to-all(bf16[4,2128,128]{2,1,0:T(8,128)(2,1)S(1)} %all-to-all-done), channel_id=1, replica_groups=mesh['section'=4,'tensor'=4,'dp'=2] {'tensor'}, dimensions={0} | all-to-all | bytes 4358144 | tf_op jit(solution)/shard_map/all_to_all | solution.py:980
  91.4 12.9 %collective-permute-done.refs_1_ = bf16[4,1024,128]{2,1,0:T(8,128)(2,1)S(1)} collective-permute-done((bf16[4,1024,128]{2,1,0:T(8,128)(2,1)S(1)}, bf16[4,1024,128]{2,1,0:T(8,128)(2,1)S(1)}, u32[]{:S(2)}, u32[]{:S(2)}) %collective-permute-start) | collective-permute-done | bytes 1048608 | tf_op jit(solution)/shard_map/ppermute | solution.py:941
  125.0 21.4 %collective-permute-done.1 = bf16[8,1024,128]{2,1,0:T(8,128)(2,1)} collective-permute-done((bf16[8,1024,128]{2,1,0:T(8,128)(2,1)}, bf16[8,1024,128]{2,1,0:T(8,128)(2,1)}, u32[]{:S(2)}, u32[]{:S(2)}) %collective-permute-start.1) | collective-permute-done | bytes 2097184 | tf_op jit(solution)/shard_map/ppermute | solution.py:941
  147.8 24.8 %all-to-all-done.2 = bf16[4,2048,128]{2,1,0:T(8,128)(2,1)S(1)} async-done(((bf16[4,2048,128]{2,1,0:T(8,128)(2,1)}), bf16[4,2048,128]{2,1,0:T(8,128)(2,1)S(1)}, u32[]{:S(2)}, u32[]{:S(2)}) %all-to-all-start.2) | async-done | bytes 2097184 | tf_op jit(solution)/shard_map/all_to_all | solution.py:980
  181.0 14.0 %forward_layer.4 = (f32[8192,128]{1,0:T(8,128)}, bf16[8192,128]{1,0:T(8,128)(2,1)}, bf16[8192,128]{1,0:T(8,128)(2,1)}, bf16[8192,128]{1,0:T(8,128)(2,1)}, f32[8,128]{1,0:T(8,128)}, /*index=5*/f32[8,128]{1,0:T(8,128)}) custom-call(s32[3,64]{1,0:T(4,128)} %pad_add_fusion.refs_0_, f32[8,128]{1,0:T(8,128)} %broadcast_in_dim.48.refs_1_, ...), custom_call_target="tpu_custom_call" | custom-call | flops 15000000512 | bytes 20971520 | tf_op jit(solution)/shard_map/forward_layer/pallas_call | solution.py:599
  195.0 8.2 %collective-permute-done.5 = bf16[8,1024,128]{2,1,0:T(8,128)(2,1)} collective-permute-done((bf16[8,1024,128]{2,1,0:T(8,128)(2,1)}, bf16[8,1024,128]{2,1,0:T(8,128)(2,1)}, u32[]{:S(2)}, u32[]{:S(2)}) %collective-permute-start.5) | collective-permute-done | bytes 2097184 | tf_op jit(solution)/shard_map/ppermute | solution.py:941
  207.9 13.0 %forward_layer.5 = (f32[8192,128]{1,0:T(8,128)}, bf16[8192,128]{1,0:T(8,128)(2,1)}, bf16[8192,128]{1,0:T(8,128)(2,1)}, bf16[8192,128]{1,0:T(8,128)(2,1)}, f32[8,128]{1,0:T(8,128)}, /*index=5*/f32[8,128]{1,0:T(8,128)}) custom-call(s32[3,64]{1,0:T(4,128)} %pad_add_fusion.refs_0_, f32[8,128]{1,0:T(8,128)} %get-tuple-element.181.refs_1_, ...), custom_call_target="tpu_custom_call" | custom-call | flops 15000000512 | bytes 20971520 | tf_op jit(solution)/shard_map/forward_layer/pallas_call | solution.py:599
  220.9 13.0 %forward_layer.6 = (f32[8192,128]{1,0:T(8,128)}, bf16[8192,128]{1,0:T(8,128)(2,1)}, bf16[8192,128]{1,0:T(8,128)(2,1)}, bf16[8192,128]{1,0:T(8,128)(2,1)}, f32[8,128]{1,0:T(8,128)}, /*index=5*/f32[8,128]{1,0:T(8,128)}) custom-call(s32[3,64]{1,0:T(4,128)} %pad_add_fusion.refs_0_, f32[8,128]{1,0:T(8,128)} %get-tuple-element.193.refs_1_, ...), custom_call_target="tpu_custom_call" | custom-call | flops 15000000512 | bytes 20971520 | tf_op jit(solution)/shard_map/forward_layer/pallas_call | solution.py:599
  233.9 13.1 %forward_layer.7 = (f32[8192,128]{1,0:T(8,128)}, bf16[8192,128]{1,0:T(8,128)(2,1)}, bf16[8192,128]{1,0:T(8,128)(2,1)}, bf16[8192,128]{1,0:T(8,128)(2,1)}, f32[8,128]{1,0:T(8,128)}, /*index=5*/f32[8,128]{1,0:T(8,128)}) custom-call(s32[3,64]{1,0:T(4,128)} %pad_add_fusion.refs_0_, f32[8,128]{1,0:T(8,128)} %get-tuple-element.204.refs_1_, ...), custom_call_target="tpu_custom_call" | custom-call | flops 15000000512 | bytes 20971520 | tf_op jit(solution)/shard_map/forward_layer/pallas_call | solution.py:599
  247.0 9.1 %all-to-all-done.3 = bf16[4,2048,128]{2,1,0:T(8,128)(2,1)S(1)} async-done(((bf16[4,2048,128]{2,1,0:T(8,128)(2,1)}), bf16[4,2048,128]{2,1,0:T(8,128)(2,1)S(1)}, u32[]{:S(2)}, u32[]{:S(2)}) %all-to-all-start.3) | async-done | bytes 2097184 | tf_op jit(solution)/shard_map/all_to_all | solution.py:980
  257.4 19.7 %backward_layer.4 = (f32[8192,128]{1,0:T(8,128)}, bf16[16,2,2,128,128]{4,3,2,1,0:T(8,128)(2,1)}, bf16[16,2,2,128,128]{4,3,2,1,0:T(8,128)(2,1)}) custom-call(s32[3,64]{1,0:T(4,128)} %pad_add_fusion.refs_0_, f32[8,128]{1,0:T(8,128)} %get-tuple-element.207.refs_1_, bf16[8192,128]{1,0:T(8,128)(2,1)} %broadcast_in_dim.56.refs_2_, ...), custom_call_target="tpu_custom_call" | custom-call | flops 17999998976 | bytes 31457280 | tf_op jit(solution)/shard_map/backward_layer/pallas_call | solution.py:632
  277.9 18.4 %backward_layer.5 = (f32[8192,128]{1,0:T(8,128)}, bf16[16,2,2,128,128]{4,3,2,1,0:T(8,128)(2,1)}, bf16[16,2,2,128,128]{4,3,2,1,0:T(8,128)(2,1)}) custom-call(s32[3,64]{1,0:T(4,128)} %pad_add_fusion.refs_0_, f32[8,128]{1,0:T(8,128)} %get-tuple-element.200.refs_1_, bf16[8192,128]{1,0:T(8,128)(2,1)} %broadcast_in_dim.54.refs_2_, ...), custom_call_target="tpu_custom_call" | custom-call | flops 17999998976 | bytes 31457280 | tf_op jit(solution)/shard_map/backward_layer/pallas_call | solution.py:632
  297.6 4.2 sum.6
  304.4 18.3 %backward_layer.6 = (f32[8192,128]{1,0:T(8,128)}, bf16[16,2,2,128,128]{4,3,2,1,0:T(8,128)(2,1)}, bf16[16,2,2,128,128]{4,3,2,1,0:T(8,128)(2,1)}) custom-call(s32[3,64]{1,0:T(4,128)} %pad_add_fusion.refs_0_, f32[8,128]{1,0:T(8,128)} %get-tuple-element.184.refs_1_, bf16[8192,128]{1,0:T(8,128)(2,1)} %broadcast_in_dim.52.refs_2_, ...), custom_call_target="tpu_custom_call" | custom-call | flops 17999998976 | bytes 31457280 | tf_op jit(solution)/shard_map/backward_layer/pallas_call | solution.py:632
  322.7 4.3 collective-permute-done.11
  328.8 4.2 sum.7
  335.6 17.5 %backward_layer.7 = (bf16[8192,128]{1,0:T(8,128)(2,1)}, bf16[16,2,2,128,128]{4,3,2,1,0:T(8,128)(2,1)}, bf16[16,2,2,128,128]{4,3,2,1,0:T(8,128)(2,1)}) custom-call(s32[3,64]{1,0:T(4,128)} %pad_add_fusion.refs_0_, f32[8,128]{1,0:T(8,128)} %get-tuple-element.171.refs_1_, bf16[8192,128]{1,0:T(8,128)(2,1)} %broadcast_in_dim.50.refs_2_, ...), custom_call_target="tpu_custom_call" | custom-call | flops 17999998976 | bytes 31457280 | tf_op jit(solution)/shard_map/backward_layer/pallas_call | solution.py:632
  371.2 11.1 %collective-permute-done.18 = bf16[2048,128]{1,0:T(8,128)(2,1)S(1)} collective-permute-done((bf16[2048,128]{1,0:T(8,128)(2,1)}, bf16[2048,128]{1,0:T(8,128)(2,1)S(1)}, u32[]{:S(2)}, u32[]{:S(2)}) %collective-permute-start.18) | collective-permute-done | bytes 524320 | tf_op jit(solution)/shard_map/ppermute | solution.py:941
  383.2 11.2 %collective-permute-done.20 = bf16[2048,128]{1,0:T(8,128)(2,1)S(1)} collective-permute-done((bf16[2048,128]{1,0:T(8,128)(2,1)}, bf16[2048,128]{1,0:T(8,128)(2,1)S(1)}, u32[]{:S(2)}, u32[]{:S(2)}) %collective-permute-start.20) | collective-permute-done | bytes 524320 | tf_op jit(solution)/shard_map/ppermute | solution.py:941
  395.1 4.8 sum.11
  400.0 8.9 %all-to-all-done.4.came_ref = bf16[4,2048,128]{2,1,0:T(8,128)(2,1)S(1)} async-done(((bf16[4,2048,128]{2,1,0:T(8,128)(2,1)}), bf16[4,2048,128]{2,1,0:T(8,128)(2,1)S(1)}, u32[]{:S(2)}, u32[]{:S(2)}) %all-to-all-start.4) | async-done | bytes 2097184 | tf_op jit(solution)/shard_map/all_to_all | solution.py:980
  408.9 40.4 %all_to_all.36 = bf16[4,1536,128]{2,1,0:T(8,128)(2,1)} all-to-all(bf16[4,1536,128]{2,1,0:T(8,128)(2,1)} %bitcast.88), channel_id=1, replica_groups=mesh['section'=4,'tensor'=4,'dp'=2] {'tensor'}, dimensions={0} | all-to-all | bytes 3145728 | tf_op jit(solution)/shard_map/all_to_all | solution.py:980
  449.3 5.3 all-to-all-start.6
  454.6 4.2 sum.9
  461.4 21.6 %collective-permute-done.21 = bf16[2048,128]{1,0:T(8,128)(2,1)S(1)} collective-permute-done((bf16[2048,128]{1,0:T(8,128)(2,1)}, bf16[2048,128]{1,0:T(8,128)(2,1)S(1)}, u32[]{:S(2)}, u32[]{:S(2)}) %collective-permute-start.21) | collective-permute-done | bytes 524320 | tf_op jit(solution)/shard_map/ppermute | solution.py:941
  483.6 10.6 %collective-permute-done.23 = bf16[2048,128]{1,0:T(8,128)(2,1)S(1)} collective-permute-done((bf16[2048,128]{1,0:T(8,128)(2,1)}, bf16[2048,128]{1,0:T(8,128)(2,1)S(1)}, u32[]{:S(2)}, u32[]{:S(2)}) %collective-permute-start.23) | collective-permute-done | bytes 524320 | tf_op jit(solution)/shard_map/ppermute | solution.py:941
  498.6 5.5 %collective-permute-start.25 = (bf16[512,128]{1,0:T(8,128)(2,1)}, bf16[512,128]{1,0:T(8,128)(2,1)S(1)}, u32[]{:S(2)}, u32[]{:S(2)}) collective-permute-start(bf16[512,128]{1,0:T(8,128)(2,1)} %bitcast.156), channel_id=1, source_target_pairs={{0,2},{1,3},{2,8},{3,9},{4,22},{5,23},{6,28},{7,29},{8,0},{9,1},{1... | collective-permute-start | bytes 393224 | tf_op jit(solution)/shard_map/ppermute | solution.py:941
  515.8 7.2 %collective-permute-done.27.refs_3_ = bf16[512,128]{1,0:T(8,128)(2,1)S(1)} collective-permute-done((bf16[512,128]{1,0:T(8,128)(2,1)}, bf16[512,128]{1,0:T(8,128)(2,1)S(1)}, u32[]{:S(2)}, u32[]{:S(2)}) %collective-permute-start.27) | collective-permute-done | bytes 131104 | tf_op jit(solution)/shard_map/ppermute | solution.py:941
  530.6 5.9 %assemble.1 = (f32[4,16,128,128]{3,2,1,0:T(8,128)}, f32[4,16,128,128]{3,2,1,0:T(8,128)}) custom-call(s32[3]{0:T(128)} %pad_add_fusion.1.refs_0_, bf16[128,128]{1,0:T(8,128)(2,1)} %fusion.refs_1_, bf16[4,1,2,2,128,128]{5,4,3,2,1,0:T(8,128)(2,1)} %bitcast.91, bf16[4,1,2,2,128,128]{5,4,3,2,1,0:T(8,128)(2,1)} %bitcast.112, ...), custom_call_target="tpu_custom_call" | custom-call | bytes 12582912 | tf_op jit(solution)/shard_map/assemble/pallas_call | solution.py:884
  (143 shorter events, 104.8 us)
Async XLA Ops:
  8.0 28.3 %all-to-all-start = ((bf16[4,2128,128]{2,1,0:T(8,128)(2,1)}), bf16[4,2128,128]{2,1,0:T(8,128)(2,1)S(1)}, u32[]{:S(2)}, u32[]{:S(2)}) async-start(bf16[4,2128,128]{2,1,0:T(8,128)(2,1)} %pieces.1), calls=%async_computation | async-start | bytes 4358144 | tf_op jit(solution)/shard_map/all_to_all | solution.py:983
  90.2 14.0 %collective-permute-start = (bf16[4,1024,128]{2,1,0:T(8,128)(2,1)S(1)}, bf16[4,1024,128]{2,1,0:T(8,128)(2,1)S(1)}, u32[]{:S(2)}, u32[]{:S(2)}) collective-permute-start(bf16[4,1024,128]{2,1,0:T(8,128)(2,1)S(1)} %get-tuple-element.158.refs_0_), channel_id=1, source_target_pairs={{0,8},{1,17},{2,10},{3,19},{4,12},{5,21},{6,14},{7,23},{8,0},{9,25... | collective-permute-start | bytes 3145736 | tf_op jit(solution)/shard_map/ppermute | solution.py:941
  120.9 25.5 %collective-permute-start.1 = (bf16[8,1024,128]{2,1,0:T(8,128)(2,1)}, bf16[8,1024,128]{2,1,0:T(8,128)(2,1)}, u32[]{:S(2)}, u32[]{:S(2)}) collective-permute-start(bf16[8,1024,128]{2,1,0:T(8,128)(2,1)} %join.3), channel_id=1, source_target_pairs={{0,16},{1,9},{2,18},{3,11},{4,20},{5,13},{6,22},{7,15},{8,24},{9,1... | collective-permute-start | bytes 6291464 | tf_op jit(solution)/shard_map/ppermute | solution.py:941
  121.2 51.4 %all-to-all-start.2 = ((bf16[4,2048,128]{2,1,0:T(8,128)(2,1)}), bf16[4,2048,128]{2,1,0:T(8,128)(2,1)S(1)}, u32[]{:S(2)}, u32[]{:S(2)}) async-start(bf16[4,2048,128]{2,1,0:T(8,128)(2,1)} %pick.2), calls=%async_computation.2 | async-start | bytes 4194304 | tf_op jit(solution)/shard_map/all_to_all | solution.py:980
  146.4 26.2 %collective-permute-start.3 = (bf16[8,1024,128]{2,1,0:T(8,128)(2,1)}, bf16[8,1024,128]{2,1,0:T(8,128)(2,1)}, u32[]{:S(2)}, u32[]{:S(2)}) collective-permute-start(bf16[8,1024,128]{2,1,0:T(8,128)(2,1)} %collective-permute-done.1), channel_id=1, source_target_pairs={{0,1},{1,0},{2,3},{3,2},{4,5},{5,4},{6,7},{7,6},{8,9},{9,8},{10,11... | collective-permute-start | bytes 6291464 | tf_op jit(solution)/shard_map/ppermute | solution.py:941
  147.3 25.2 %collective-permute-start.4 = (bf16[4,1024,128]{2,1,0:T(8,128)(2,1)S(1)}, bf16[4,1024,128]{2,1,0:T(8,128)(2,1)}, u32[]{:S(2)}, u32[]{:S(2)}) collective-permute-start(bf16[4,1024,128]{2,1,0:T(8,128)(2,1)S(1)} %get-tuple-element.178.refs_0_), channel_id=1, source_target_pairs={{0,8},{1,17},{2,10},{3,19},{4,12},{5,21},{6,14},{7,23},{8,0},{9,25... | collective-permute-start | bytes 3145736 | tf_op jit(solution)/shard_map/ppermute | solution.py:941
  176.2 18.7 %collective-permute-start.6 = (bf16[8,1024,128]{2,1,0:T(8,128)(2,1)}, bf16[8,1024,128]{2,1,0:T(8,128)(2,1)}, u32[]{:S(2)}, u32[]{:S(2)}) collective-permute-start(bf16[8,1024,128]{2,1,0:T(8,128)(2,1)} %join.4), channel_id=1, source_target_pairs={{0,1},{1,0},{2,3},{3,2},{4,5},{5,4},{6,7},{7,6},{8,9},{9,8},{10,11... | collective-permute-start | bytes 6291464 | tf_op jit(solution)/shard_map/ppermute | solution.py:941
  177.7 25.5 %collective-permute-start.5 = (bf16[8,1024,128]{2,1,0:T(8,128)(2,1)}, bf16[8,1024,128]{2,1,0:T(8,128)(2,1)}, u32[]{:S(2)}, u32[]{:S(2)}) collective-permute-start(bf16[8,1024,128]{2,1,0:T(8,128)(2,1)} %join.4), channel_id=1, source_target_pairs={{0,16},{1,9},{2,18},{3,11},{4,20},{5,13},{6,22},{7,15},{8,24},{9,1... | collective-permute-start | bytes 6291464 | tf_op jit(solution)/shard_map/ppermute | solution.py:941
  203.2 17.7 %collective-permute-start.7 = (bf16[8,1024,128]{2,1,0:T(8,128)(2,1)}, bf16[8,1024,128]{2,1,0:T(8,128)(2,1)}, u32[]{:S(2)}, u32[]{:S(2)}) collective-permute-start(bf16[8,1024,128]{2,1,0:T(8,128)(2,1)} %collective-permute-done.5), channel_id=1, source_target_pairs={{0,1},{1,0},{2,3},{3,2},{4,5},{5,4},{6,7},{7,6},{8,9},{9,8},{10,11... | collective-permute-start | bytes 6291464 | tf_op jit(solution)/shard_map/ppermute | solution.py:941
  204.1 51.9 %all-to-all-start.3 = ((bf16[4,2048,128]{2,1,0:T(8,128)(2,1)}), bf16[4,2048,128]{2,1,0:T(8,128)(2,1)S(1)}, u32[]{:S(2)}, u32[]{:S(2)}) async-start(bf16[4,2048,128]{2,1,0:T(8,128)(2,1)} %pick.3), calls=%async_computation.3 | async-start | bytes 4194304 | tf_op jit(solution)/shard_map/all_to_all | solution.py:980
  277.1 19.2 %collective-permute-start.8 = (bf16[16,2,2,128,128]{4,3,2,1,0:T(8,128)(2,1)}, bf16[16,2,2,128,128]{4,3,2,1,0:T(8,128)(2,1)S(1)}, u32[]{:S(2)}, u32[]{:S(2)}) collective-permute-start(bf16[16,2,2,128,128]{4,3,2,1,0:T(8,128)(2,1)} %get-tuple-element.218), channel_id=1, source_target_pairs={{0,1},{1,0},{2,3},{3,2},{4,5},{5,4},{6,7},{7,6},{8,9},{9,8},{10,11... | collective-permute-start | bytes 6291464 | tf_op jit(solution)/shard_map/ppermute | solution.py:941
  297.6 29.5 %collective-permute-start.12 = (bf16[16,2,2,128,128]{4,3,2,1,0:T(8,128)(2,1)}, bf16[16,2,2,128,128]{4,3,2,1,0:T(8,128)(2,1)S(1)}, u32[]{:S(2)}, u32[]{:S(2)}) collective-permute-start(bf16[16,2,2,128,128]{4,3,2,1,0:T(8,128)(2,1)} %get-tuple-element.230), channel_id=1, source_target_pairs={{0,1},{1,0},{2,3},{3,2},{4,5},{5,4},{6,7},{7,6},{8,9},{9,8},{10,11... | collective-permute-start | bytes 6291464 | tf_op jit(solution)/shard_map/ppermute | solution.py:941
  301.8 20.9 %collective-permute-start.9 = (bf16[2048,128]{1,0:T(8,128)(2,1)}, bf16[2048,128]{1,0:T(8,128)(2,1)S(1)}, u32[]{:S(2)}, u32[]{:S(2)}) collective-permute-start(bf16[2048,128]{1,0:T(8,128)(2,1)} %bitcast.146), channel_id=1, source_target_pairs={{0,8},{1,9},{2,10},{3,11},{4,12},{5,13},{6,14},{7,15},{8,0},{9,1},... | collective-permute-start | bytes 1572872 | tf_op jit(solution)/shard_map/ppermute | solution.py:941
  302.9 19.8 %collective-permute-start.10 = (bf16[2048,128]{1,0:T(8,128)(2,1)}, bf16[2048,128]{1,0:T(8,128)(2,1)S(1)}, u32[]{:S(2)}, u32[]{:S(2)}) collective-permute-start(bf16[2048,128]{1,0:T(8,128)(2,1)} %bitcast.145), channel_id=1, source_target_pairs={{0,16},{1,17},{2,18},{3,19},{4,20},{5,21},{6,22},{7,23},{8,24},{9,... | collective-permute-start | bytes 1572872 | tf_op jit(solution)/shard_map/ppermute | solution.py:941
  303.4 23.7 %collective-permute-start.11 = (bf16[2048,128]{1,0:T(8,128)(2,1)}, bf16[2048,128]{1,0:T(8,128)(2,1)S(1)}, u32[]{:S(2)}, u32[]{:S(2)}) collective-permute-start(bf16[2048,128]{1,0:T(8,128)(2,1)} %bitcast.143), channel_id=1, source_target_pairs={{0,24},{1,25},{2,26},{3,27},{4,28},{5,29},{6,30},{7,31},{8,16},{9,... | collective-permute-start | bytes 1572872 | tf_op jit(solution)/shard_map/ppermute | solution.py:941
  327.1 29.7 %collective-permute-start.16 = (bf16[16,2,2,128,128]{4,3,2,1,0:T(8,128)(2,1)}, bf16[16,2,2,128,128]{4,3,2,1,0:T(8,128)(2,1)}, u32[]{:S(2)}, u32[]{:S(2)}) collective-permute-start(bf16[16,2,2,128,128]{4,3,2,1,0:T(8,128)(2,1)} %get-tuple-element.246), channel_id=1, source_target_pairs={{0,1},{1,0},{2,3},{3,2},{4,5},{5,4},{6,7},{7,6},{8,9},{9,8},{10,11... | collective-permute-start | bytes 6291464 | tf_op jit(solution)/shard_map/ppermute | solution.py:941
  333.0 20.2 %collective-permute-start.13 = (bf16[2048,128]{1,0:T(8,128)(2,1)}, bf16[2048,128]{1,0:T(8,128)(2,1)S(1)}, u32[]{:S(2)}, u32[]{:S(2)}) collective-permute-start(bf16[2048,128]{1,0:T(8,128)(2,1)} %bitcast.144), channel_id=1, source_target_pairs={{0,8},{1,9},{2,10},{3,11},{4,12},{5,13},{6,14},{7,15},{8,0},{9,1},... | collective-permute-start | bytes 1572872 | tf_op jit(solution)/shard_map/ppermute | solution.py:941
  333.3 20.7 %collective-permute-start.14 = (bf16[2048,128]{1,0:T(8,128)(2,1)}, bf16[2048,128]{1,0:T(8,128)(2,1)S(1)}, u32[]{:S(2)}, u32[]{:S(2)}) collective-permute-start(bf16[2048,128]{1,0:T(8,128)(2,1)} %bitcast.142), channel_id=1, source_target_pairs={{0,16},{1,17},{2,18},{3,19},{4,20},{5,21},{6,22},{7,23},{8,24},{9,... | collective-permute-start | bytes 1572872 | tf_op jit(solution)/shard_map/ppermute | solution.py:941
  334.4 22.4 %collective-permute-start.15 = (bf16[2048,128]{1,0:T(8,128)(2,1)}, bf16[2048,128]{1,0:T(8,128)(2,1)S(1)}, u32[]{:S(2)}, u32[]{:S(2)}) collective-permute-start(bf16[2048,128]{1,0:T(8,128)(2,1)} %bitcast.141), channel_id=1, source_target_pairs={{0,24},{1,25},{2,26},{3,27},{4,28},{5,29},{6,30},{7,31},{8,16},{9,... | collective-permute-start | bytes 1572872 | tf_op jit(solution)/shard_map/ppermute | solution.py:941
  357.6 51.3 %all-to-all-start.4 = ((bf16[4,2048,128]{2,1,0:T(8,128)(2,1)}), bf16[4,2048,128]{2,1,0:T(8,128)(2,1)S(1)}, u32[]{:S(2)}, u32[]{:S(2)}) async-start(bf16[4,2048,128]{2,1,0:T(8,128)(2,1)} %bitcast.104), calls=%async_computation.4 | async-start | bytes 4194304 | tf_op jit(solution)/shard_map/all_to_all | solution.py:980
  361.2 33.1 %collective-permute-start.17 = (bf16[16,2,2,128,128]{4,3,2,1,0:T(8,128)(2,1)}, bf16[16,2,2,128,128]{4,3,2,1,0:T(8,128)(2,1)}, u32[]{:S(2)}, u32[]{:S(2)}) collective-permute-start(bf16[16,2,2,128,128]{4,3,2,1,0:T(8,128)(2,1)} %get-tuple-element.248), channel_id=1, source_target_pairs={{0,1},{1,0},{2,3},{3,2},{4,5},{5,4},{6,7},{7,6},{8,9},{9,8},{10,11... | collective-permute-start | bytes 6291464 | tf_op jit(solution)/shard_map/ppermute | solution.py:941
  368.5 13.7 %collective-permute-start.18 = (bf16[2048,128]{1,0:T(8,128)(2,1)}, bf16[2048,128]{1,0:T(8,128)(2,1)S(1)}, u32[]{:S(2)}, u32[]{:S(2)}) collective-permute-start(bf16[2048,128]{1,0:T(8,128)(2,1)} %bitcast.151), channel_id=1, source_target_pairs={{0,8},{1,9},{2,10},{3,11},{4,12},{5,13},{6,14},{7,15},{8,0},{9,1},... | collective-permute-start | bytes 1572872 | tf_op jit(solution)/shard_map/ppermute | solution.py:941
  369.7 13.5 %collective-permute-start.19 = (bf16[2048,128]{1,0:T(8,128)(2,1)}, bf16[2048,128]{1,0:T(8,128)(2,1)S(1)}, u32[]{:S(2)}, u32[]{:S(2)}) collective-permute-start(bf16[2048,128]{1,0:T(8,128)(2,1)} %bitcast.149), channel_id=1, source_target_pairs={{0,16},{1,17},{2,18},{3,19},{4,20},{5,21},{6,22},{7,23},{8,24},{9,... | collective-permute-start | bytes 1572872 | tf_op jit(solution)/shard_map/ppermute | solution.py:941
  370.1 24.2 %collective-permute-start.20 = (bf16[2048,128]{1,0:T(8,128)(2,1)}, bf16[2048,128]{1,0:T(8,128)(2,1)S(1)}, u32[]{:S(2)}, u32[]{:S(2)}) collective-permute-start(bf16[2048,128]{1,0:T(8,128)(2,1)} %bitcast.147), channel_id=1, source_target_pairs={{0,24},{1,25},{2,26},{3,27},{4,28},{5,29},{6,30},{7,31},{8,16},{9,... | collective-permute-start | bytes 1572872 | tf_op jit(solution)/shard_map/ppermute | solution.py:941
  449.3 73.7 %all-to-all-start.6 = ((bf16[4,1536,128]{2,1,0:T(8,128)(2,1)}), bf16[4,1536,128]{2,1,0:T(8,128)(2,1)}, u32[]{:S(2)}, u32[]{:S(2)}) async-start(bf16[4,1536,128]{2,1,0:T(8,128)(2,1)} %all_to_all.36), calls=%async_computation.6 | async-start | bytes 3145728 | tf_op jit(solution)/shard_map/all_to_all | solution.py:983
  458.8 24.3 %collective-permute-start.21 = (bf16[2048,128]{1,0:T(8,128)(2,1)}, bf16[2048,128]{1,0:T(8,128)(2,1)S(1)}, u32[]{:S(2)}, u32[]{:S(2)}) collective-permute-start(bf16[2048,128]{1,0:T(8,128)(2,1)} %bitcast.152), channel_id=1, source_target_pairs={{0,8},{1,9},{2,10},{3,11},{4,12},{5,13},{6,14},{7,15},{8,0},{9,1},... | collective-permute-start | bytes 1572872 | tf_op jit(solution)/shard_map/ppermute | solution.py:941
  459.9 23.7 %collective-permute-start.22 = (bf16[2048,128]{1,0:T(8,128)(2,1)}, bf16[2048,128]{1,0:T(8,128)(2,1)S(1)}, u32[]{:S(2)}, u32[]{:S(2)}) collective-permute-start(bf16[2048,128]{1,0:T(8,128)(2,1)} %bitcast.150), channel_id=1, source_target_pairs={{0,16},{1,17},{2,18},{3,19},{4,20},{5,21},{6,22},{7,23},{8,24},{9,... | collective-permute-start | bytes 1572872 | tf_op jit(solution)/shard_map/ppermute | solution.py:941
  460.2 34.0 %collective-permute-start.23 = (bf16[2048,128]{1,0:T(8,128)(2,1)}, bf16[2048,128]{1,0:T(8,128)(2,1)S(1)}, u32[]{:S(2)}, u32[]{:S(2)}) collective-permute-start(bf16[2048,128]{1,0:T(8,128)(2,1)} %bitcast.148), channel_id=1, source_target_pairs={{0,24},{1,25},{2,26},{3,27},{4,28},{5,29},{6,30},{7,31},{8,16},{9,... | collective-permute-start | bytes 1572872 | tf_op jit(solution)/shard_map/ppermute | solution.py:941
  498.6 17.1 %collective-permute-start.25 = (bf16[512,128]{1,0:T(8,128)(2,1)}, bf16[512,128]{1,0:T(8,128)(2,1)S(1)}, u32[]{:S(2)}, u32[]{:S(2)}) collective-permute-start(bf16[512,128]{1,0:T(8,128)(2,1)} %bitcast.156), channel_id=1, source_target_pairs={{0,2},{1,3},{2,8},{3,9},{4,22},{5,23},{6,28},{7,29},{8,0},{9,1},{1... | collective-permute-start | bytes 393224 | tf_op jit(solution)/shard_map/ppermute | solution.py:941
  504.1 11.7 %collective-permute-start.24 = (bf16[512,128]{1,0:T(8,128)(2,1)}, bf16[512,128]{1,0:T(8,128)(2,1)S(1)}, u32[]{:S(2)}, u32[]{:S(2)}) collective-permute-start(bf16[512,128]{1,0:T(8,128)(2,1)} %bitcast.155), channel_id=1, source_target_pairs={{0,0},{1,1},{2,10},{3,11},{4,20},{5,21},{6,30},{7,31},{8,2},{9,3},... | collective-permute-start | bytes 393224 | tf_op jit(solution)/shard_map/ppermute | solution.py:941
  506.3 9.5 %collective-permute-start.26 = (bf16[512,128]{1,0:T(8,128)(2,1)}, bf16[512,128]{1,0:T(8,128)(2,1)S(1)}, u32[]{:S(2)}, u32[]{:S(2)}) collective-permute-start(bf16[512,128]{1,0:T(8,128)(2,1)} %bitcast.154), channel_id=1, source_target_pairs={{0,4},{1,5},{2,14},{3,15},{4,16},{5,17},{6,26},{7,27},{8,6},{9,7},... | collective-permute-start | bytes 393224 | tf_op jit(solution)/shard_map/ppermute | solution.py:941
  508.2 14.8 %collective-permute-start.27 = (bf16[512,128]{1,0:T(8,128)(2,1)}, bf16[512,128]{1,0:T(8,128)(2,1)S(1)}, u32[]{:S(2)}, u32[]{:S(2)}) collective-permute-start(bf16[512,128]{1,0:T(8,128)(2,1)} %bitcast.153), channel_id=1, source_target_pairs={{0,6},{1,7},{2,12},{3,13},{4,18},{5,19},{6,24},{7,25},{8,4},{9,5},... | collective-permute-start | bytes 393224 | tf_op jit(solution)/shard_map/ppermute | solution.py:941
  (31 other events, 321.4 us)

commit v9 on v8

--- a/solution.py
+++ b/solution.py
@@ -296,6 +296,12 @@
     return pl.ds(pl.multiple_of(block * size, size), size)
 
 
+def column(gain_ref, block, slots):
+    blocks = gain_ref.shape[1]
+    picked = lax.broadcasted_iota(jnp.int32, (blocks, slots), 0) == block
+    return inner_dot(gain_ref[...], picked.astype(jnp.bfloat16), 1, 0)
+
+
 def chunk_copy(source, target, sems, chunk):
     rows = target.shape[0] // CHUNKS
     at = pl.ds(pl.multiple_of(chunk * rows, rows), rows)
@@ -352,7 +358,7 @@
     sources, refs = refs[:inputs], refs[inputs:]
     parts, sources = sources[:PARTS], sources[PARTS:]
     out_ref, u_ref, z_ref, slope_ref, scale_ref, next_ref = refs[:6]
-    raw, h, w, u, z, slope, mid, gain, in_sems, gain_sems, w_sems, out_sems = refs[6:]
+    raw, h, w, u, z, slope, mid, in_sems, w_sems, out_sems = refs[6:]
     features, slots = h.shape
     size = w.shape[-1]
     chunk_blocks = w.shape[2]
@@ -363,10 +369,7 @@
     right_in = factor_copies(parts, layer, w, w_sems, 1)
     if first:
         start_chunks(sources[0], raw, in_sems)
-        for copy in left_in:
-            copy.start()
-        start_chunks(gain_ref, gain, gain_sems)
-        for copy in right_in:
+        for copy in left_in + right_in:
             copy.start()
 
         def squares(block, total):
@@ -385,7 +388,6 @@
         for copy in left_in:
             copy.start()
         start_chunks(sources[0], h, in_sems)
-        start_chunks(gain_ref, gain, gain_sems)
         for copy in right_in:
             copy.start()
         total = sums_ref[...]
@@ -395,14 +397,13 @@
         copy.wait()
 
     def arrive(chunk):
-        chunk_copy(gain_ref, gain, gain_sems, chunk).wait()
         if not first:
             chunk_copy(sources[0], h, in_sems, chunk).wait()
 
     def left(block, carry):
         rows = block_rows(block, size)
         place = table_ref[0, block]
-        normed = (h[rows, :] * scale * gain[rows, :].astype(jnp.float32)).astype(jnp.bfloat16)
+        normed = (h[rows, :] * scale * column(gain_ref, block, slots)).astype(jnp.bfloat16)
         u[rows, :] = normed
         weight = w[place // chunk_blocks, 0, place % chunk_blocks]
         mid[rows, :] = inner_dot(weight, normed, 0, 0)
@@ -450,8 +451,8 @@
     slope_ref, z_ref, u_ref = sources[:3]
     parts, sources = sources[3 : 3 + PARTS], sources[3 + PARTS :]
     out_ref, own_grad, peer_grad = refs[:3]
-    g, slope, z, u, h, w, gw, mid, gain, top, goal, end_gain = refs[3:15]
-    in_sems, w_sems, out_sems, gw_sems = refs[15:]
+    g, slope, z, u, h, w, gw, mid, top, goal, end_gain = refs[3:14]
+    in_sems, w_sems, out_sems, gw_sems = refs[14:]
     features, slots = g.shape
     size = w.shape[-1]
     chunk_blocks = w.shape[2]
@@ -474,7 +475,6 @@
     for copy in left_in:
         copy.start()
     start_chunks(u_ref, u, in_sems.at[3])
-    start_chunks(gain_ref, gain, in_sems.at[7])
     start_chunks(h_ref, h, in_sems.at[4])
 
     if turning:
@@ -537,7 +537,6 @@
 
     def arrive_left(chunk):
         chunk_copy(u_ref, u, in_sems.at[3], chunk).wait()
-        chunk_copy(gain_ref, gain, in_sems.at[7], chunk).wait()
         chunk_copy(h_ref, h, in_sems.at[4], chunk).wait()
 
     def left(block, total):
@@ -548,7 +547,7 @@
         arrived = [mid[pl.ds(q * blocks + block, blocks, stride=size), :] for q in range(fold)]
         arrived = jnp.concatenate(arrived, axis=0).astype(jnp.bfloat16)
         gw[to] = inner_dot(u[rows, :], arrived, 1, 1).astype(jnp.bfloat16)
-        weighted = inner_dot(w[at], arrived, 1, 0) * gain[rows, :].astype(jnp.float32)
+        weighted = inner_dot(w[at], arrived, 1, 0) * column(gain_ref, block, slots)
         g[rows, :] = g[rows, :] + scale * weighted
         return total + fold_rows(weighted * h[rows, :].astype(jnp.float32))
 
@@ -598,7 +597,7 @@
     )
     return pl.pallas_call(
         lambda *refs: forward_kernel(first, layer, len(sources), *refs),
-        in_specs=[SMEM, INSIDE, OUTSIDE] + [OUTSIDE] * len(sources),
+        in_specs=[SMEM, INSIDE, INSIDE] + [OUTSIDE] * len(sources),
         out_specs=[OUTSIDE] * 4 + [INSIDE] * 2,
         out_shape=out_shape,
         scratch_shapes=[
@@ -609,8 +608,6 @@
             pltpu.VMEM(whole, jnp.bfloat16),
             pltpu.VMEM(whole, jnp.bfloat16),
             pltpu.VMEM(whole, jnp.float32),
-            pltpu.VMEM(whole, jnp.bfloat16),
-            pltpu.SemaphoreType.DMA((CHUNKS,)),
             pltpu.SemaphoreType.DMA((CHUNKS,)),
             pltpu.SemaphoreType.DMA((2, PARTS)),
             pltpu.SemaphoreType.DMA((4, CHUNKS)),
@@ -631,7 +628,7 @@
     out_shape = [shape_of(whole, jnp.bfloat16 if last else jnp.float32)] + [shape_of(half, jnp.bfloat16)] * 2
     return pl.pallas_call(
         lambda *refs: backward_kernel(turning, last, layer, len(sources), *refs),
-        in_specs=[SMEM, INSIDE] + [OUTSIDE] * (2 + len(sources)),
+        in_specs=[SMEM, INSIDE, INSIDE] + [OUTSIDE] * (1 + len(sources)),
         out_specs=[OUTSIDE] * len(out_shape),
         out_shape=out_shape,
         scratch_shapes=[
@@ -643,11 +640,10 @@
             pltpu.VMEM(held, jnp.bfloat16),
             pltpu.VMEM(held, jnp.bfloat16),
             pltpu.VMEM(whole, jnp.float32),
-            pltpu.VMEM(whole, jnp.bfloat16),
             pltpu.VMEM(whole if turning else SMALL, jnp.float32),
             pltpu.VMEM(whole if turning else SMALL, jnp.bfloat16),
             pltpu.VMEM(whole if turning else SMALL, jnp.bfloat16),
-            pltpu.SemaphoreType.DMA((8, CHUNKS)),
+            pltpu.SemaphoreType.DMA((7, CHUNKS)),
             pltpu.SemaphoreType.DMA((2, PARTS)),
             pltpu.SemaphoreType.DMA((CHUNKS,)),
             pltpu.SemaphoreType.DMA((2, PARTS)),
@@ -704,7 +700,7 @@
 def run_sum(groups, parts, apart=True):
     flat = [term.reshape(parts, -1, term.shape[-1]) for terms in groups for term in terms]
     _, rows, lanes = flat[0].shape
-    steps = 4
+    steps = 8
     if apart:
         out_shape = [shape_of((len(groups), rows, lanes), jnp.bfloat16)] * parts
         out_specs = [pl.BlockSpec((len(groups), rows // steps, lanes), lambda i: (0, i, 0))] * parts
@@ -999,33 +995,35 @@
     patch_came = to_planes(patch_sent).reshape(-1, wide)
     lowest = [lifted[:, group[0] * layer_rows : (group[-1] + 1) * layer_rows] for group in groups]
     beside = move(lowest[0], routes["across"][0])
-    gains = lifted[:, layer_count * layer_rows :].reshape(width, layer_count + 1, feat_local)
-    gains = gains.transpose(1, 0, 2).reshape(layer_count + 1, -1)
-    columns = [jnp.broadcast_to(gain[:, None], (gain.shape[0], wide)) for gain in gains]
-    lowest, beside, columns = tie((lowest, beside, columns))
+    gains = lifted[:, layer_count * layer_rows :].reshape(width, layer_count + 1, local_blocks, size)
+    gains = gains.transpose(1, 3, 0, 2).reshape(layer_count + 1, size, blocks)
+    end_column = jnp.broadcast_to(gains[layer_count].T[:, :, None], (blocks, size, wide)).reshape(-1, wide)
+    lowest, beside = tie((lowest, beside))
     first_two = gather_two(joined([lowest[0], beside]))
-    first_two, lowest[1] = tie((first_two, lowest[1]))
+    first_two, lowest[1], patch_came = tie((first_two, lowest[1], patch_came))
     weights = [as_weights(gather_three(*first_two))]
     later = (lowest[1], move(lowest[1], routes["across"][0]))
-    weights, later, patch_came = tie((weights, later, patch_came))
-
-    residual = patch_came
+    weights, later, end_column = tie((weights, later, end_column))
+
+    residual, target_sent = tie((patch_came, target_sent))
+    target = to_planes(target_sent).reshape(-1, wide)
     flying = gather_two(joined(list(later)))
     sums = jnp.zeros((8, wide), jnp.float32)
     stored = []
     for layer in range(layer_count):
         group = 0 if layer in groups[0] else 1
         following, u, z, slope, scale, sums = run_forward(
-            table, columns[layer], sums, residual, weights[group], layer - groups[group][0]
+            table, gains[layer], sums, residual, weights[group], layer - groups[group][0]
         )
         stored.append(((slope, z, u), scale, residual))
         residual = following
         if layer == 0:
-            residual, sums, flying, target_sent = tie((residual, sums, flying, target_sent))
+            residual, sums, flying = tie((residual, sums, flying))
             weights.append(as_weights(gather_three(*flying)))
-            target = to_planes(target_sent).reshape(-1, wide)
         if layer == groups[0][-1]:
             residual, sums, weights[1] = tie((residual, sums, weights[1]))
+        if layer == layer_count - 2:
+            residual, sums, target = tie((residual, sums, target))
 
     def core_sum(mine, other):
         return (mine, move(other, routes["cores"]))
@@ -1052,8 +1050,8 @@
         underway = [(at + 1, steps[at](*state)) if at < len(steps) else (at, state) for at, state in underway]
         gradient, mine, other = run_backward(
             table,
-            columns[layer],
-            columns[layer_count],
+            gains[layer],
+            end_column,
             scale,
             kept,
             weights[group],
@@ -1071,7 +1069,7 @@
     ended = tie(ended)
     ended[0] = plane_sum(*ended[0])
     others = to_planes(run_sum(ended[1:], width, apart=False))
-    ended[0], returned = tie((ended[0], returned))
+    ended[0], returned, others = tie((ended[0], returned, others))
     home = homeward(ended[:1])
     d_patches = run_combine(critic_pairs, returned)
     others = to_sections(others)

time: 538 us -> 505 us (0.939)
  blocking collectives: 94.3 us -> 53.7 us
  Pallas kernels: 183 us -> 195 us
  local copies, waits for them, and re-layouts: 23.4 us -> 16.8 us
  starting transfers between devices: 60.6 us -> 67 us
    all_to_all x2 -> x1, blocking collectives: 94.3 us -> 53.7 us  [to_planes(): lax.all_to_all(value, 'tensor', split_axis=0, concat_axis=0, tiled=True)]
    ppermute x30, waiting for transfers between devices: 114 us -> 88.8 us  [move(): return lax.ppermute(value, AXES, route)]
    all_to_all x3 -> x4, waiting for transfers between devices: 42.7 us -> 62 us  [to_planes(): lax.all_to_all(value, 'tensor', split_axis=0, concat_axis=0, tiled=True)]
    pallas_call x6, Pallas kernels: 25 us -> 35.7 us  [run_sum(): pl.pallas_call(lambda *refs: sum_kernel(len(groups[0]), len(flat), *refs)...]
    broadcast_in_dim x5 -> x1, local copies, waits for them, and re-layouts: 11.1 us -> 2.29 us  [plane_shards(): jnp.broadcast_to(gains[layer_count].T[:, :, None], (blocks, size, wide))]
    all_to_all x3 -> x4, starting transfers between devices: 11 us -> 16.4 us  [to_planes(): lax.all_to_all(value, 'tensor', split_axis=0, concat_axis=0, tiled=True)]
  transfers between devices with their start and end apart: 35 -> 36, of which waited for: 18 -> 18; matrix products, arithmetic and copies ran while one was open for 1% -> 1% of each run, Pallas kernels for 27% -> 29%
where the time goes in v9:
time: 505 us; the launch traced here: 502 us
  Pallas kernels  195 us (39%)
  waiting for transfers between devices  167 us (33%)
  starting transfers between devices  67 us (13%)
  blocking collectives  53.7 us (11%)
  local copies, waits for them, and re-layouts  16.8 us (3%)
    ppermute x30, waiting for transfers between devices, move(): return lax.ppermute(value, AXES, route)  88.8 us
    pallas_call x4, Pallas kernels, run_backward(): pl.pallas_call(lambda *refs: backward_kernel(turning, last, layer, len(so...  73 us
    all_to_all x4, waiting for transfers between devices, to_planes(): lax.all_to_all(value, 'tensor', split_axis=0, concat_axis=0, tiled=True)  62 us
    pallas_call x4, Pallas kernels, run_forward(): pl.pallas_call(lambda *refs: forward_kernel(first, layer, len(sources), *...  55.5 us
    all_to_all x1, blocking collectives, to_planes(): lax.all_to_all(value, 'tensor', split_axis=0, concat_axis=0, tiled=True)  53.7 us
    ppermute x30, starting transfers between devices, move(): return lax.ppermute(value, AXES, route)  41.5 us
    pallas_call x6, Pallas kernels, run_sum(): pl.pallas_call(lambda *refs: sum_kernel(len(groups[0]), len(flat), *refs)...  35.7 us
    all_to_all x4, starting transfers between devices, to_planes(): lax.all_to_all(value, 'tensor', split_axis=0, concat_axis=0, tiled=True)  16.4 us
  transfers between devices with their start and end apart: 36, of which 18 were waited for; matrix products, arithmetic and copies ran while one was open for 1% of the time, Pallas kernels for 29%

profile of v9, /device:TPU:5, one launch (start us, length us, event | category | flops | bytes accessed | tf_op | source)
XLA Modules:
  0.0 502.3 jit_solution(10601539219915644341)
XLA Ops:
  3.3 4.6 pieces.1
  21.5 16.2 %all-to-all-done = bf16[4,2128,128]{2,1,0:T(8,128)(2,1)} async-done(((bf16[4,2128,128]{2,1,0:T(8,128)(2,1)}), bf16[4,2128,128]{2,1,0:T(8,128)(2,1)}, u32[]{:S(2)}, u32[]{:S(2)}) %all-to-all-start) | async-done | bytes 2179104 | tf_op jit(solution)/shard_map/all_to_all | solution.py:979
  37.7 53.7 %all_to_all.35 = bf16[4,2128,128]{2,1,0:T(8,128)(2,1)S(1)} all-to-all(bf16[4,2128,128]{2,1,0:T(8,128)(2,1)} %all-to-all-done), channel_id=1, replica_groups=mesh['section'=4,'tensor'=4,'dp'=2] {'tensor'}, dimensions={0} | all-to-all | bytes 4358144 | tf_op jit(solution)/shard_map/all_to_all | solution.py:976
  97.4 9.5 %collective-permute-done.refs_1_ = bf16[4,1024,128]{2,1,0:T(8,128)(2,1)} collective-permute-done((bf16[4,1024,128]{2,1,0:T(8,128)(2,1)}, bf16[4,1024,128]{2,1,0:T(8,128)(2,1)}, u32[]{:S(2)}, u32[]{:S(2)}) %collective-permute-start) | collective-permute-done | bytes 1048608 | tf_op jit(solution)/shard_map/ppermute | solution.py:937
  112.7 32.5 %all-to-all-done.2 = bf16[4,2048,128]{2,1,0:T(8,128)(2,1)} async-done(((bf16[4,2048,128]{2,1,0:T(8,128)(2,1)}), bf16[4,2048,128]{2,1,0:T(8,128)(2,1)}, u32[]{:S(2)}, u32[]{:S(2)}) %all-to-all-start.2) | async-done | bytes 2097184 | tf_op jit(solution)/shard_map/all_to_all | solution.py:976
  147.8 12.8 %collective-permute-done.4.refs_1_ = bf16[4,1024,128]{2,1,0:T(8,128)(2,1)S(1)} collective-permute-done((bf16[4,1024,128]{2,1,0:T(8,128)(2,1)S(1)}, bf16[4,1024,128]{2,1,0:T(8,128)(2,1)S(1)}, u32[]{:S(2)}, u32[]{:S(2)}) %collective-permute-start.4) | collective-permute-done | bytes 1048608 | tf_op jit(solution)/shard_map/ppermute | solution.py:937
  171.6 14.4 %forward_layer.4 = (f32[8192,128]{1,0:T(8,128)}, bf16[8192,128]{1,0:T(8,128)(2,1)}, bf16[8192,128]{1,0:T(8,128)(2,1)}, bf16[8192,128]{1,0:T(8,128)(2,1)}, f32[8,128]{1,0:T(8,128)}, /*index=5*/f32[8,128]{1,0:T(8,128)}) custom-call(s32[3,64]{1,0:T(4,128)} %pad_add_fusion.refs_0_, f32[8,128]{1,0:T(8,128)} %broadcast_in_dim.10.refs_1_, ...), custom_call_target="tpu_custom_call" | custom-call | flops 15000000512 | bytes 20971520 | tf_op jit(solution)/shard_map/forward_layer/pallas_call | solution.py:598
  186.0 7.2 %collective-permute-done.5 = bf16[8,1024,128]{2,1,0:T(8,128)(2,1)} collective-permute-done((bf16[8,1024,128]{2,1,0:T(8,128)(2,1)}, bf16[8,1024,128]{2,1,0:T(8,128)(2,1)}, u32[]{:S(2)}, u32[]{:S(2)}) %collective-permute-start.5) | collective-permute-done | bytes 2097184 | tf_op jit(solution)/shard_map/ppermute | solution.py:937
  200.1 13.7 %forward_layer.5 = (f32[8192,128]{1,0:T(8,128)}, bf16[8192,128]{1,0:T(8,128)(2,1)}, bf16[8192,128]{1,0:T(8,128)(2,1)}, bf16[8192,128]{1,0:T(8,128)(2,1)}, f32[8,128]{1,0:T(8,128)}, /*index=5*/f32[8,128]{1,0:T(8,128)}) custom-call(s32[3,64]{1,0:T(4,128)} %pad_add_fusion.refs_0_, f32[8,128]{1,0:T(8,128)} %get-tuple-element.182.refs_1_, ...), custom_call_target="tpu_custom_call" | custom-call | flops 15000000512 | bytes 20971520 | tf_op jit(solution)/shard_map/forward_layer/pallas_call | solution.py:598
  213.8 13.7 %forward_layer.6 = (f32[8192,128]{1,0:T(8,128)}, bf16[8192,128]{1,0:T(8,128)(2,1)}, bf16[8192,128]{1,0:T(8,128)(2,1)}, bf16[8192,128]{1,0:T(8,128)(2,1)}, f32[8,128]{1,0:T(8,128)}, /*index=5*/f32[8,128]{1,0:T(8,128)}) custom-call(s32[3,64]{1,0:T(4,128)} %pad_add_fusion.refs_0_, f32[8,128]{1,0:T(8,128)} %get-tuple-element.193.refs_1_, ...), custom_call_target="tpu_custom_call" | custom-call | flops 15000000512 | bytes 20971520 | tf_op jit(solution)/shard_map/forward_layer/pallas_call | solution.py:598
  227.5 18.6 %all-to-all-done.3 = bf16[4,2048,128]{2,1,0:T(8,128)(2,1)S(1)} async-done(((bf16[4,2048,128]{2,1,0:T(8,128)(2,1)}), bf16[4,2048,128]{2,1,0:T(8,128)(2,1)S(1)}, u32[]{:S(2)}, u32[]{:S(2)}) %all-to-all-start.3) | async-done | bytes 2097184 | tf_op jit(solution)/shard_map/all_to_all | solution.py:976
  246.1 13.8 %forward_layer.7 = (f32[8192,128]{1,0:T(8,128)}, bf16[8192,128]{1,0:T(8,128)(2,1)}, bf16[8192,128]{1,0:T(8,128)(2,1)}, bf16[8192,128]{1,0:T(8,128)(2,1)}, f32[8,128]{1,0:T(8,128)}, /*index=5*/f32[8,128]{1,0:T(8,128)}) custom-call(s32[3,64]{1,0:T(4,128)} %pad_add_fusion.refs_0_, f32[8,128]{1,0:T(8,128)} %get-tuple-element.206.refs_1_, ...), custom_call_target="tpu_custom_call" | custom-call | flops 15000000512 | bytes 20971520 | tf_op jit(solution)/shard_map/forward_layer/pallas_call | solution.py:598
  259.8 19.5 %backward_layer.4 = (f32[8192,128]{1,0:T(8,128)}, bf16[16,2,2,128,128]{4,3,2,1,0:T(8,128)(2,1)}, bf16[16,2,2,128,128]{4,3,2,1,0:T(8,128)(2,1)}) custom-call(s32[3,64]{1,0:T(4,128)} %pad_add_fusion.refs_0_, f32[8,128]{1,0:T(8,128)} %get-tuple-element.208.refs_1_, bf16[128,64]{1,0:T(8,128)(2,1)} %copy.20.refs_2_, bf16[8192,128]{1,0:T(8,128)(2,1)} %broadcast_in_dim.23.refs_3_, ...), custom_call_target="tpu_custom_call" | custom-call | flops 17999998976 | bytes 31457280 | tf_op jit(solution)/shard_map/backward_layer/pallas_call | solution.py:629
  280.2 18.1 %backward_layer.5 = (f32[8192,128]{1,0:T(8,128)}, bf16[16,2,2,128,128]{4,3,2,1,0:T(8,128)(2,1)}, bf16[16,2,2,128,128]{4,3,2,1,0:T(8,128)(2,1)}) custom-call(s32[3,64]{1,0:T(4,128)} %pad_add_fusion.refs_0_, f32[8,128]{1,0:T(8,128)} %get-tuple-element.199.refs_1_, bf16[128,64]{1,0:T(8,128)(2,1)} %copy.19.refs_2_, bf16[8192,128]{1,0:T(8,128)(2,1)} %broadcast_in_dim.23.refs_3_, ...), custom_call_target="tpu_custom_call" | custom-call | flops 17999998976 | bytes 31457280 | tf_op jit(solution)/shard_map/backward_layer/pallas_call | solution.py:629
  299.7 6.0 %sum.6 = (bf16[1,2048,128]{2,1,0:T(8,128)(2,1)}, bf16[1,2048,128]{2,1,0:T(8,128)(2,1)}, bf16[1,2048,128]{2,1,0:T(8,128)(2,1)}, bf16[1,2048,128]{2,1,0:T(8,128)(2,1)}) custom-call(bf16[4,2048,128]{2,1,0:T(8,128)(2,1)} %bitcast.109, bf16[4,2048,128]{2,1,0:T(8,128)(2,1)} %bitcast.110), custom_call_target="tpu_custom_call" | custom-call | flops 2097152 | bytes 6291456 | tf_op jit(solution)/shard_map/sum/pallas_call | solution.py:710
  308.4 18.1 %backward_layer.6 = (f32[8192,128]{1,0:T(8,128)}, bf16[16,2,2,128,128]{4,3,2,1,0:T(8,128)(2,1)}, bf16[16,2,2,128,128]{4,3,2,1,0:T(8,128)(2,1)}) custom-call(s32[3,64]{1,0:T(4,128)} %pad_add_fusion.refs_0_, f32[8,128]{1,0:T(8,128)} %get-tuple-element.184.refs_1_, bf16[128,64]{1,0:T(8,128)(2,1)} %copy.18.refs_2_, bf16[8192,128]{1,0:T(8,128)(2,1)} %broadcast_in_dim.23.refs_3_, ...), custom_call_target="tpu_custom_call" | custom-call | flops 17999998976 | bytes 31457280 | tf_op jit(solution)/shard_map/backward_layer/pallas_call | solution.py:629
  332.7 6.0 %sum.7 = (bf16[1,2048,128]{2,1,0:T(8,128)(2,1)}, bf16[1,2048,128]{2,1,0:T(8,128)(2,1)}, bf16[1,2048,128]{2,1,0:T(8,128)(2,1)}, bf16[1,2048,128]{2,1,0:T(8,128)(2,1)}) custom-call(bf16[4,2048,128]{2,1,0:T(8,128)(2,1)} %bitcast.106, bf16[4,2048,128]{2,1,0:T(8,128)(2,1)} %bitcast.107), custom_call_target="tpu_custom_call" | custom-call | flops 2097152 | bytes 6291456 | tf_op jit(solution)/shard_map/sum/pallas_call | solution.py:710
  341.3 17.2 %backward_layer.7 = (bf16[8192,128]{1,0:T(8,128)(2,1)}, bf16[16,2,2,128,128]{4,3,2,1,0:T(8,128)(2,1)}, bf16[16,2,2,128,128]{4,3,2,1,0:T(8,128)(2,1)}) custom-call(s32[3,64]{1,0:T(4,128)} %pad_add_fusion.refs_0_, f32[8,128]{1,0:T(8,128)} %get-tuple-element.173.refs_1_, bf16[128,64]{1,0:T(8,128)(2,1)} %copy.17.refs_2_, ...), custom_call_target="tpu_custom_call" | custom-call | flops 17999998976 | bytes 31457280 | tf_op jit(solution)/shard_map/backward_layer/pallas_call | solution.py:629
  370.1 6.0 %sum.8 = (bf16[1,2048,128]{2,1,0:T(8,128)(2,1)}, bf16[1,2048,128]{2,1,0:T(8,128)(2,1)}, bf16[1,2048,128]{2,1,0:T(8,128)(2,1)}, bf16[1,2048,128]{2,1,0:T(8,128)(2,1)}) custom-call(bf16[4,2048,128]{2,1,0:T(8,128)(2,1)} %bitcast.104, bf16[4,2048,128]{2,1,0:T(8,128)(2,1)} %bitcast.39.refs_1_), custom_call_target="tpu_custom_call" | custom-call | flops 2097152 | bytes 6291456 | tf_op jit(solution)/shard_map/sum/pallas_call | solution.py:710
  378.8 11.1 %collective-permute-done.18 = bf16[2048,128]{1,0:T(8,128)(2,1)S(1)} collective-permute-done((bf16[2048,128]{1,0:T(8,128)(2,1)}, bf16[2048,128]{1,0:T(8,128)(2,1)S(1)}, u32[]{:S(2)}, u32[]{:S(2)}) %collective-permute-start.18) | collective-permute-done | bytes 524320 | tf_op jit(solution)/shard_map/ppermute | solution.py:937
  390.6 11.4 %collective-permute-done.20 = bf16[2048,128]{1,0:T(8,128)(2,1)S(1)} collective-permute-done((bf16[2048,128]{1,0:T(8,128)(2,1)}, bf16[2048,128]{1,0:T(8,128)(2,1)S(1)}, u32[]{:S(2)}, u32[]{:S(2)}) %collective-permute-start.20) | collective-permute-done | bytes 524320 | tf_op jit(solution)/shard_map/ppermute | solution.py:937
  402.9 6.5 %sum.10 = bf16[4,3,512,128]{3,2,1,0:T(8,128)(2,1)} custom-call(bf16[4,512,128]{2,1,0:T(8,128)(2,1)} %bitcast.125, bf16[4,512,128]{2,1,0:T(8,128)(2,1)} %bitcast.126, bf16[4,512,128]{2,1,0:T(8,128)(2,1)} %bitcast.127, bf16[4,512,128]{2,1,0:T(8,128)(2,1)} %bitcast.128, bf16[4,512,128]{2,1,0:T(8,128)(2,1)} %bitcast.121, bf16[4,512,128]{2,1,0:T(8,128)(2,1)} %bitcast.122, ...), custom_call_target="tpu_custom_call" | custom-call | flops 3145728 | bytes 6815744 | tf_op jit(solution)/shard_map/sum/pallas_call | solution.py:710
  409.4 5.1 %all-to-all-done.4.came_ref = bf16[4,2048,128]{2,1,0:T(8,128)(2,1)S(1)} async-done(((bf16[4,2048,128]{2,1,0:T(8,128)(2,1)}), bf16[4,2048,128]{2,1,0:T(8,128)(2,1)S(1)}, u32[]{:S(2)}, u32[]{:S(2)}) %all-to-all-start.4) | async-done | bytes 2097184 | tf_op jit(solution)/shard_map/all_to_all | solution.py:976
  419.1 6.0 %sum.9 = (bf16[1,2048,128]{2,1,0:T(8,128)(2,1)}, bf16[1,2048,128]{2,1,0:T(8,128)(2,1)}, bf16[1,2048,128]{2,1,0:T(8,128)(2,1)}, bf16[1,2048,128]{2,1,0:T(8,128)(2,1)}) custom-call(bf16[4,2048,128]{2,1,0:T(8,128)(2,1)} %bitcast.103, bf16[4,2048,128]{2,1,0:T(8,128)(2,1)} %bitcast.45.refs_1_), custom_call_target="tpu_custom_call" | custom-call | flops 2097152 | bytes 6291456 | tf_op jit(solution)/shard_map/sum/pallas_call | solution.py:710
  427.8 9.6 %collective-permute-done.21 = bf16[2048,128]{1,0:T(8,128)(2,1)S(1)} collective-permute-done((bf16[2048,128]{1,0:T(8,128)(2,1)}, bf16[2048,128]{1,0:T(8,128)(2,1)S(1)}, u32[]{:S(2)}, u32[]{:S(2)}) %collective-permute-start.21) | collective-permute-done | bytes 524320 | tf_op jit(solution)/shard_map/ppermute | solution.py:937
  438.4 11.1 %collective-permute-done.23 = bf16[2048,128]{1,0:T(8,128)(2,1)S(1)} collective-permute-done((bf16[2048,128]{1,0:T(8,128)(2,1)}, bf16[2048,128]{1,0:T(8,128)(2,1)S(1)}, u32[]{:S(2)}, u32[]{:S(2)}) %collective-permute-start.23) | collective-permute-done | bytes 524320 | tf_op jit(solution)/shard_map/ppermute | solution.py:937
  449.5 5.9 %all-to-all-done.5 = bf16[4,1536,128]{2,1,0:T(8,128)(2,1)} async-done(((bf16[4,1536,128]{2,1,0:T(8,128)(2,1)}), bf16[4,1536,128]{2,1,0:T(8,128)(2,1)}, u32[]{:S(2)}, u32[]{:S(2)}) %all-to-all-start.5) | async-done | bytes 1572896 | tf_op jit(solution)/shard_map/all_to_all | solution.py:976
  455.4 4.6 all-to-all-start.6
  460.0 5.3 %sum.11 = (bf16[1,512,128]{2,1,0:T(8,128)(2,1)}, bf16[1,512,128]{2,1,0:T(8,128)(2,1)}, bf16[1,512,128]{2,1,0:T(8,128)(2,1)}, bf16[1,512,128]{2,1,0:T(8,128)(2,1)}) custom-call(bf16[4,512,128]{2,1,0:T(8,128)(2,1)} %bitcast.113, bf16[4,512,128]{2,1,0:T(8,128)(2,1)} %bitcast.114, bf16[4,512,128]{2,1,0:T(8,128)(2,1)} %bitcast.115, bf16[4,512,128]{2,1,0:T(8,128)(2,1)} %bitcast.116), custom_call_target="tpu_custom_call" | custom-call | flops 1048576 | bytes 2621440 | tf_op jit(solution)/shard_map/sum/pallas_call | solution.py:710
  472.4 6.1 %collective-permute-start.27 = (bf16[512,128]{1,0:T(8,128)(2,1)}, bf16[512,128]{1,0:T(8,128)(2,1)}, u32[]{:S(2)}, u32[]{:S(2)}) collective-permute-start(bf16[512,128]{1,0:T(8,128)(2,1)} %bitcast.154), channel_id=1, source_target_pairs={{0,6},{1,7},{2,12},{3,13},{4,18},{5,19},{6,24},{7,25},{8,4},{9,5},... | collective-permute-start | bytes 393224 | tf_op jit(solution)/shard_map/ppermute | solution.py:937
  482.4 5.9 %collective-permute-done.27.refs_3_ = bf16[512,128]{1,0:T(8,128)(2,1)} collective-permute-done((bf16[512,128]{1,0:T(8,128)(2,1)}, bf16[512,128]{1,0:T(8,128)(2,1)}, u32[]{:S(2)}, u32[]{:S(2)}) %collective-permute-start.27) | collective-permute-done | bytes 131104 | tf_op jit(solution)/shard_map/ppermute | solution.py:937
  496.3 5.9 %assemble.1 = (f32[4,16,128,128]{3,2,1,0:T(8,128)}, f32[4,16,128,128]{3,2,1,0:T(8,128)}) custom-call(s32[3]{0:T(128)} %pad_add_fusion.1.refs_0_, bf16[128,128]{1,0:T(8,128)(2,1)} %fusion.refs_1_, bf16[4,1,2,2,128,128]{5,4,3,2,1,0:T(8,128)(2,1)} %bitcast.94, bf16[4,1,2,2,128,128]{5,4,3,2,1,0:T(8,128)(2,1)} %bitcast.112, ...), custom_call_target="tpu_custom_call" | custom-call | bytes 12582912 | tf_op jit(solution)/shard_map/assemble/pallas_call | solution.py:880
  (137 shorter events, 105.1 us)
Async XLA Ops:
  8.0 29.8 %all-to-all-start = ((bf16[4,2128,128]{2,1,0:T(8,128)(2,1)}), bf16[4,2128,128]{2,1,0:T(8,128)(2,1)}, u32[]{:S(2)}, u32[]{:S(2)}) async-start(bf16[4,2128,128]{2,1,0:T(8,128)(2,1)} %pieces.1), calls=%async_computation | async-start | bytes 4358144 | tf_op jit(solution)/shard_map/all_to_all | solution.py:979
  92.6 14.3 %collective-permute-start = (bf16[4,1024,128]{2,1,0:T(8,128)(2,1)}, bf16[4,1024,128]{2,1,0:T(8,128)(2,1)}, u32[]{:S(2)}, u32[]{:S(2)}) collective-permute-start(bf16[4,1024,128]{2,1,0:T(8,128)(2,1)} %get-tuple-element.158.refs_0_), channel_id=1, source_target_pairs={{0,8},{1,17},{2,10},{3,19},{4,12},{5,21},{6,14},{7,23},{8,0},{9,25... | collective-permute-start | bytes 3145736 | tf_op jit(solution)/shard_map/ppermute | solution.py:937
  92.9 52.2 %all-to-all-start.2 = ((bf16[4,2048,128]{2,1,0:T(8,128)(2,1)}), bf16[4,2048,128]{2,1,0:T(8,128)(2,1)}, u32[]{:S(2)}, u32[]{:S(2)}) async-start(bf16[4,2048,128]{2,1,0:T(8,128)(2,1)} %pick.2), calls=%async_computation.2 | async-start | bytes 4194304 | tf_op jit(solution)/shard_map/all_to_all | solution.py:976
  109.7 35.4 %collective-permute-start.2 = (bf16[8,1024,128]{2,1,0:T(8,128)(2,1)}, bf16[8,1024,128]{2,1,0:T(8,128)(2,1)}, u32[]{:S(2)}, u32[]{:S(2)}) collective-permute-start(bf16[8,1024,128]{2,1,0:T(8,128)(2,1)} %join.3), channel_id=1, source_target_pairs={{0,1},{1,0},{2,3},{3,2},{4,5},{5,4},{6,7},{7,6},{8,9},{9,8},{10,11... | collective-permute-start | bytes 6291464 | tf_op jit(solution)/shard_map/ppermute | solution.py:937
  112.4 32.8 %collective-permute-start.1 = (bf16[8,1024,128]{2,1,0:T(8,128)(2,1)}, bf16[8,1024,128]{2,1,0:T(8,128)(2,1)}, u32[]{:S(2)}, u32[]{:S(2)}) collective-permute-start(bf16[8,1024,128]{2,1,0:T(8,128)(2,1)} %join.3), channel_id=1, source_target_pairs={{0,16},{1,9},{2,18},{3,11},{4,20},{5,13},{6,22},{7,15},{8,24},{9,1... | collective-permute-start | bytes 6291464 | tf_op jit(solution)/shard_map/ppermute | solution.py:937
  145.1 16.4 %collective-permute-start.3 = (bf16[8,1024,128]{2,1,0:T(8,128)(2,1)}, bf16[8,1024,128]{2,1,0:T(8,128)(2,1)S(1)}, u32[]{:S(2)}, u32[]{:S(2)}) collective-permute-start(bf16[8,1024,128]{2,1,0:T(8,128)(2,1)} %collective-permute-done.1), channel_id=1, source_target_pairs={{0,1},{1,0},{2,3},{3,2},{4,5},{5,4},{6,7},{7,6},{8,9},{9,8},{10,11... | collective-permute-start | bytes 6291464 | tf_op jit(solution)/shard_map/ppermute | solution.py:937
  146.6 13.9 %collective-permute-start.4 = (bf16[4,1024,128]{2,1,0:T(8,128)(2,1)S(1)}, bf16[4,1024,128]{2,1,0:T(8,128)(2,1)S(1)}, u32[]{:S(2)}, u32[]{:S(2)}) collective-permute-start(bf16[4,1024,128]{2,1,0:T(8,128)(2,1)S(1)} %get-tuple-element.180.refs_0_), channel_id=1, source_target_pairs={{0,8},{1,17},{2,10},{3,19},{4,12},{5,21},{6,14},{7,23},{8,0},{9,25... | collective-permute-start | bytes 3145736 | tf_op jit(solution)/shard_map/ppermute | solution.py:937
  166.7 19.3 %collective-permute-start.6 = (bf16[8,1024,128]{2,1,0:T(8,128)(2,1)}, bf16[8,1024,128]{2,1,0:T(8,128)(2,1)}, u32[]{:S(2)}, u32[]{:S(2)}) collective-permute-start(bf16[8,1024,128]{2,1,0:T(8,128)(2,1)} %join.4), channel_id=1, source_target_pairs={{0,1},{1,0},{2,3},{3,2},{4,5},{5,4},{6,7},{7,6},{8,9},{9,8},{10,11... | collective-permute-start | bytes 6291464 | tf_op jit(solution)/shard_map/ppermute | solution.py:937
  167.7 25.5 %collective-permute-start.5 = (bf16[8,1024,128]{2,1,0:T(8,128)(2,1)}, bf16[8,1024,128]{2,1,0:T(8,128)(2,1)}, u32[]{:S(2)}, u32[]{:S(2)}) collective-permute-start(bf16[8,1024,128]{2,1,0:T(8,128)(2,1)} %join.4), channel_id=1, source_target_pairs={{0,16},{1,9},{2,18},{3,11},{4,20},{5,13},{6,22},{7,15},{8,24},{9,1... | collective-permute-start | bytes 6291464 | tf_op jit(solution)/shard_map/ppermute | solution.py:937
  193.2 20.6 %collective-permute-start.7 = (bf16[8,1024,128]{2,1,0:T(8,128)(2,1)}, bf16[8,1024,128]{2,1,0:T(8,128)(2,1)}, u32[]{:S(2)}, u32[]{:S(2)}) collective-permute-start(bf16[8,1024,128]{2,1,0:T(8,128)(2,1)} %collective-permute-done.5), channel_id=1, source_target_pairs={{0,1},{1,0},{2,3},{3,2},{4,5},{5,4},{6,7},{7,6},{8,9},{9,8},{10,11... | collective-permute-start | bytes 6291464 | tf_op jit(solution)/shard_map/ppermute | solution.py:937
  194.1 51.9 %all-to-all-start.3 = ((bf16[4,2048,128]{2,1,0:T(8,128)(2,1)}), bf16[4,2048,128]{2,1,0:T(8,128)(2,1)S(1)}, u32[]{:S(2)}, u32[]{:S(2)}) async-start(bf16[4,2048,128]{2,1,0:T(8,128)(2,1)} %pick.3), calls=%async_computation.3 | async-start | bytes 4194304 | tf_op jit(solution)/shard_map/all_to_all | solution.py:976
  279.4 19.0 %collective-permute-start.8 = (bf16[16,2,2,128,128]{4,3,2,1,0:T(8,128)(2,1)}, bf16[16,2,2,128,128]{4,3,2,1,0:T(8,128)(2,1)S(1)}, u32[]{:S(2)}, u32[]{:S(2)}) collective-permute-start(bf16[16,2,2,128,128]{4,3,2,1,0:T(8,128)(2,1)} %get-tuple-element.219), channel_id=1, source_target_pairs={{0,1},{1,0},{2,3},{3,2},{4,5},{5,4},{6,7},{7,6},{8,9},{9,8},{10,11... | collective-permute-start | bytes 6291464 | tf_op jit(solution)/shard_map/ppermute | solution.py:937
  299.7 31.4 %collective-permute-start.12 = (bf16[16,2,2,128,128]{4,3,2,1,0:T(8,128)(2,1)}, bf16[16,2,2,128,128]{4,3,2,1,0:T(8,128)(2,1)S(1)}, u32[]{:S(2)}, u32[]{:S(2)}) collective-permute-start(bf16[16,2,2,128,128]{4,3,2,1,0:T(8,128)(2,1)} %get-tuple-element.231), channel_id=1, source_target_pairs={{0,1},{1,0},{2,3},{3,2},{4,5},{5,4},{6,7},{7,6},{8,9},{9,8},{10,11... | collective-permute-start | bytes 6291464 | tf_op jit(solution)/shard_map/ppermute | solution.py:937
  305.7 20.8 %collective-permute-start.9 = (bf16[2048,128]{1,0:T(8,128)(2,1)}, bf16[2048,128]{1,0:T(8,128)(2,1)S(1)}, u32[]{:S(2)}, u32[]{:S(2)}) collective-permute-start(bf16[2048,128]{1,0:T(8,128)(2,1)} %bitcast.147), channel_id=1, source_target_pairs={{0,8},{1,9},{2,10},{3,11},{4,12},{5,13},{6,14},{7,15},{8,0},{9,1},... | collective-permute-start | bytes 1572872 | tf_op jit(solution)/shard_map/ppermute | solution.py:937
  306.8 19.8 %collective-permute-start.10 = (bf16[2048,128]{1,0:T(8,128)(2,1)}, bf16[2048,128]{1,0:T(8,128)(2,1)S(1)}, u32[]{:S(2)}, u32[]{:S(2)}) collective-permute-start(bf16[2048,128]{1,0:T(8,128)(2,1)} %bitcast.146), channel_id=1, source_target_pairs={{0,16},{1,17},{2,18},{3,19},{4,20},{5,21},{6,22},{7,23},{8,24},{9,... | collective-permute-start | bytes 1572872 | tf_op jit(solution)/shard_map/ppermute | solution.py:937
  307.2 23.9 %collective-permute-start.11 = (bf16[2048,128]{1,0:T(8,128)(2,1)}, bf16[2048,128]{1,0:T(8,128)(2,1)S(1)}, u32[]{:S(2)}, u32[]{:S(2)}) collective-permute-start(bf16[2048,128]{1,0:T(8,128)(2,1)} %bitcast.144), channel_id=1, source_target_pairs={{0,24},{1,25},{2,26},{3,27},{4,28},{5,29},{6,30},{7,31},{8,16},{9,... | collective-permute-start | bytes 1572872 | tf_op jit(solution)/shard_map/ppermute | solution.py:937
  331.1 31.3 %collective-permute-start.16 = (bf16[16,2,2,128,128]{4,3,2,1,0:T(8,128)(2,1)}, bf16[16,2,2,128,128]{4,3,2,1,0:T(8,128)(2,1)}, u32[]{:S(2)}, u32[]{:S(2)}) collective-permute-start(bf16[16,2,2,128,128]{4,3,2,1,0:T(8,128)(2,1)} %get-tuple-element.247), channel_id=1, source_target_pairs={{0,1},{1,0},{2,3},{3,2},{4,5},{5,4},{6,7},{7,6},{8,9},{9,8},{10,11... | collective-permute-start | bytes 6291464 | tf_op jit(solution)/shard_map/ppermute | solution.py:937
  338.6 19.9 %collective-permute-start.13 = (bf16[2048,128]{1,0:T(8,128)(2,1)}, bf16[2048,128]{1,0:T(8,128)(2,1)S(1)}, u32[]{:S(2)}, u32[]{:S(2)}) collective-permute-start(bf16[2048,128]{1,0:T(8,128)(2,1)} %bitcast.145), channel_id=1, source_target_pairs={{0,8},{1,9},{2,10},{3,11},{4,12},{5,13},{6,14},{7,15},{8,0},{9,1},... | collective-permute-start | bytes 1572872 | tf_op jit(solution)/shard_map/ppermute | solution.py:937
  339.1 20.3 %collective-permute-start.14 = (bf16[2048,128]{1,0:T(8,128)(2,1)}, bf16[2048,128]{1,0:T(8,128)(2,1)S(1)}, u32[]{:S(2)}, u32[]{:S(2)}) collective-permute-start(bf16[2048,128]{1,0:T(8,128)(2,1)} %bitcast.143), channel_id=1, source_target_pairs={{0,16},{1,17},{2,18},{3,19},{4,20},{5,21},{6,22},{7,23},{8,24},{9,... | collective-permute-start | bytes 1572872 | tf_op jit(solution)/shard_map/ppermute | solution.py:937
  340.2 22.2 %collective-permute-start.15 = (bf16[2048,128]{1,0:T(8,128)(2,1)}, bf16[2048,128]{1,0:T(8,128)(2,1)S(1)}, u32[]{:S(2)}, u32[]{:S(2)}) collective-permute-start(bf16[2048,128]{1,0:T(8,128)(2,1)} %bitcast.142), channel_id=1, source_target_pairs={{0,24},{1,25},{2,26},{3,27},{4,28},{5,29},{6,30},{7,31},{8,16},{9,... | collective-permute-start | bytes 1572872 | tf_op jit(solution)/shard_map/ppermute | solution.py:937
  363.2 51.3 %all-to-all-start.4 = ((bf16[4,2048,128]{2,1,0:T(8,128)(2,1)}), bf16[4,2048,128]{2,1,0:T(8,128)(2,1)S(1)}, u32[]{:S(2)}, u32[]{:S(2)}) async-start(bf16[4,2048,128]{2,1,0:T(8,128)(2,1)} %bitcast.105), calls=%async_computation.4 | async-start | bytes 4194304 | tf_op jit(solution)/shard_map/all_to_all | solution.py:976
  366.8 35.2 %collective-permute-start.17 = (bf16[16,2,2,128,128]{4,3,2,1,0:T(8,128)(2,1)}, bf16[16,2,2,128,128]{4,3,2,1,0:T(8,128)(2,1)}, u32[]{:S(2)}, u32[]{:S(2)}) collective-permute-start(bf16[16,2,2,128,128]{4,3,2,1,0:T(8,128)(2,1)} %get-tuple-element.249), channel_id=1, source_target_pairs={{0,1},{1,0},{2,3},{3,2},{4,5},{5,4},{6,7},{7,6},{8,9},{9,8},{10,11... | collective-permute-start | bytes 6291464 | tf_op jit(solution)/shard_map/ppermute | solution.py:937
  376.1 13.8 %collective-permute-start.18 = (bf16[2048,128]{1,0:T(8,128)(2,1)}, bf16[2048,128]{1,0:T(8,128)(2,1)S(1)}, u32[]{:S(2)}, u32[]{:S(2)}) collective-permute-start(bf16[2048,128]{1,0:T(8,128)(2,1)} %bitcast.152), channel_id=1, source_target_pairs={{0,8},{1,9},{2,10},{3,11},{4,12},{5,13},{6,14},{7,15},{8,0},{9,1},... | collective-permute-start | bytes 1572872 | tf_op jit(solution)/shard_map/ppermute | solution.py:937
  377.2 13.4 %collective-permute-start.19 = (bf16[2048,128]{1,0:T(8,128)(2,1)}, bf16[2048,128]{1,0:T(8,128)(2,1)S(1)}, u32[]{:S(2)}, u32[]{:S(2)}) collective-permute-start(bf16[2048,128]{1,0:T(8,128)(2,1)} %bitcast.150), channel_id=1, source_target_pairs={{0,16},{1,17},{2,18},{3,19},{4,20},{5,21},{6,22},{7,23},{8,24},{9,... | collective-permute-start | bytes 1572872 | tf_op jit(solution)/shard_map/ppermute | solution.py:937
  377.6 24.4 %collective-permute-start.20 = (bf16[2048,128]{1,0:T(8,128)(2,1)}, bf16[2048,128]{1,0:T(8,128)(2,1)S(1)}, u32[]{:S(2)}, u32[]{:S(2)}) collective-permute-start(bf16[2048,128]{1,0:T(8,128)(2,1)} %bitcast.148), channel_id=1, source_target_pairs={{0,24},{1,25},{2,26},{3,27},{4,28},{5,29},{6,30},{7,31},{8,16},{9,... | collective-permute-start | bytes 1572872 | tf_op jit(solution)/shard_map/ppermute | solution.py:937
  414.5 40.9 %all-to-all-start.5 = ((bf16[4,1536,128]{2,1,0:T(8,128)(2,1)}), bf16[4,1536,128]{2,1,0:T(8,128)(2,1)}, u32[]{:S(2)}, u32[]{:S(2)}) async-start(bf16[4,1536,128]{2,1,0:T(8,128)(2,1)} %bitcast.91), calls=%async_computation.5 | async-start | bytes 3145728 | tf_op jit(solution)/shard_map/all_to_all | solution.py:976
  425.1 12.3 %collective-permute-start.21 = (bf16[2048,128]{1,0:T(8,128)(2,1)}, bf16[2048,128]{1,0:T(8,128)(2,1)S(1)}, u32[]{:S(2)}, u32[]{:S(2)}) collective-permute-start(bf16[2048,128]{1,0:T(8,128)(2,1)} %bitcast.153), channel_id=1, source_target_pairs={{0,8},{1,9},{2,10},{3,11},{4,12},{5,13},{6,14},{7,15},{8,0},{9,1},... | collective-permute-start | bytes 1572872 | tf_op jit(solution)/shard_map/ppermute | solution.py:937
  426.6 22.9 %collective-permute-start.23 = (bf16[2048,128]{1,0:T(8,128)(2,1)}, bf16[2048,128]{1,0:T(8,128)(2,1)S(1)}, u32[]{:S(2)}, u32[]{:S(2)}) collective-permute-start(bf16[2048,128]{1,0:T(8,128)(2,1)} %bitcast.149), channel_id=1, source_target_pairs={{0,24},{1,25},{2,26},{3,27},{4,28},{5,29},{6,30},{7,31},{8,16},{9,... | collective-permute-start | bytes 1572872 | tf_op jit(solution)/shard_map/ppermute | solution.py:937
  455.4 33.0 %all-to-all-start.6 = ((bf16[4,1536,128]{2,1,0:T(8,128)(2,1)}), bf16[4,1536,128]{2,1,0:T(8,128)(2,1)S(1)}, u32[]{:S(2)}, u32[]{:S(2)}) async-start(bf16[4,1536,128]{2,1,0:T(8,128)(2,1)} %all-to-all-done.5), calls=%async_computation.6 | async-start | bytes 3145728 | tf_op jit(solution)/shard_map/all_to_all | solution.py:979
  465.2 17.1 %collective-permute-start.25 = (bf16[512,128]{1,0:T(8,128)(2,1)}, bf16[512,128]{1,0:T(8,128)(2,1)S(1)}, u32[]{:S(2)}, u32[]{:S(2)}) collective-permute-start(bf16[512,128]{1,0:T(8,128)(2,1)} %bitcast.157), channel_id=1, source_target_pairs={{0,2},{1,3},{2,8},{3,9},{4,22},{5,23},{6,28},{7,29},{8,0},{9,1},{1... | collective-permute-start | bytes 393224 | tf_op jit(solution)/shard_map/ppermute | solution.py:937
  467.2 15.2 %collective-permute-start.24 = (bf16[512,128]{1,0:T(8,128)(2,1)}, bf16[512,128]{1,0:T(8,128)(2,1)S(1)}, u32[]{:S(2)}, u32[]{:S(2)}) collective-permute-start(bf16[512,128]{1,0:T(8,128)(2,1)} %bitcast.156), channel_id=1, source_target_pairs={{0,0},{1,1},{2,10},{3,11},{4,20},{5,21},{6,30},{7,31},{8,2},{9,3},... | collective-permute-start | bytes 393224 | tf_op jit(solution)/shard_map/ppermute | solution.py:937
  472.4 15.9 %collective-permute-start.27 = (bf16[512,128]{1,0:T(8,128)(2,1)}, bf16[512,128]{1,0:T(8,128)(2,1)}, u32[]{:S(2)}, u32[]{:S(2)}) collective-permute-start(bf16[512,128]{1,0:T(8,128)(2,1)} %bitcast.154), channel_id=1, source_target_pairs={{0,6},{1,7},{2,12},{3,13},{4,18},{5,19},{6,24},{7,25},{8,4},{9,5},... | collective-permute-start | bytes 393224 | tf_op jit(solution)/shard_map/ppermute | solution.py:937
  (31 other events, 333.4 us)

commit v10 on v9

--- a/solution.py
+++ b/solution.py
@@ -268,6 +268,7 @@
 
 VMEM_LIMIT = 60 * 1024 * 1024
 CHUNKS = 8
+TOGETHER = 4
 PARTS = 4
 SMALL = (16, 128)
 AXES = ("section", "tensor", "dp")
@@ -341,12 +342,20 @@
 def by_chunk(blocks, step, carry, before=None, after=None):
     per_chunk = blocks // CHUNKS
 
+    def few(start, carry):
+        stores = []
+        for at in range(TOGETHER):
+            made, carry = step(start + at, carry)
+            stores += made
+        for ref, index, value in stores:
+            ref[index] = value
+        return carry
+
     def one(chunk, carry):
         if before is not None:
             before(chunk)
-        carry = lax.fori_loop(
-            0, per_chunk, lambda at, now: step(chunk * per_chunk + at, now), carry, unroll=True
-        )
+        for at in range(0, per_chunk, TOGETHER):
+            carry = few(chunk * per_chunk + at, carry)
         if after is not None:
             after(chunk)
         return carry
@@ -375,8 +384,7 @@
         def squares(block, total):
             rows = block_rows(block, size)
             part = raw[rows, :].astype(jnp.float32)
-            h[rows, :] = part
-            return total + fold_rows(part * part)
+            return [(h, (rows, slice(None)), part)], total + fold_rows(part * part)
 
         total = by_chunk(
             blocks,
@@ -404,10 +412,10 @@
         rows = block_rows(block, size)
         place = table_ref[0, block]
         normed = (h[rows, :] * scale * column(gain_ref, block, slots)).astype(jnp.bfloat16)
-        u[rows, :] = normed
         weight = w[place // chunk_blocks, 0, place % chunk_blocks]
-        mid[rows, :] = inner_dot(weight, normed, 0, 0)
-        return carry
+        first_out = inner_dot(weight, normed, 0, 0)
+        at = (rows, slice(None))
+        return [(u, at, normed), (mid, at, first_out)], carry
 
     def leave_left(chunk):
         chunk_copy(u, u_ref, out_sems.at[0], chunk).start()
@@ -421,19 +429,18 @@
         place = table_ref[0, block]
         moved = [mid[pl.ds(q * blocks + block, blocks, stride=size), :] for q in range(fold)]
         moved = jnp.concatenate(moved, axis=0).astype(jnp.bfloat16)
-        z[rows, :] = moved
         weight = w[place // chunk_blocks, 1, place % chunk_blocks]
         mixture = inner_dot(weight, moved, 0, 0)
         squared = mixture * mixture
         tangent = jnp.tanh(mixture * (TANH_SLOPE + (TANH_SLOPE * CUBIC_TERM) * squared))
         half = 0.5 + 0.5 * tangent
         following = h[rows, :] + mixture * half
-        h[rows, :] = following
         steep = half + mixture * (1.0 - tangent * tangent) * (
             0.5 * TANH_SLOPE + (1.5 * TANH_SLOPE * CUBIC_TERM) * squared
         )
-        slope[rows, :] = steep.astype(jnp.bfloat16)
-        return total + fold_rows(following * following)
+        at = (rows, slice(None))
+        stores = [(z, at, moved), (h, at, following), (slope, at, steep.astype(jnp.bfloat16))]
+        return stores, total + fold_rows(following * following)
 
     leaving = ((h, out_ref, 1), (z, z_ref, 2), (slope, slope_ref, 3))
 
@@ -484,7 +491,7 @@
             rows = block_rows(block, size)
             part = top[rows, :]
             scaled = part * end_gain[rows, :].astype(jnp.float32)
-            return (
+            return [], (
                 totals[0] + fold_rows(part * part),
                 totals[1] + fold_rows(scaled * scaled),
                 totals[2] + fold_rows(scaled * goal[rows, :].astype(jnp.float32)),
@@ -519,13 +526,14 @@
             factor = end_gain[rows, :].astype(jnp.float32)
             error = (part * end_scale * factor - goal[rows, :].astype(jnp.float32)) * factor
             gradient = end_scale * error - part * end_back
-            g[rows, :] = gradient
+            stores = [(g, (rows, slice(None)), gradient)]
         else:
             gradient = g[rows, :]
+            stores = []
         steep = (gradient * slope[rows, :].astype(jnp.float32)).astype(jnp.bfloat16)
-        gw[to] = inner_dot(z[rows, :], steep, 1, 1).astype(jnp.bfloat16)
-        mid[rows, :] = inner_dot(w[at], steep, 1, 0)
-        return carry
+        stores.append((gw, to, inner_dot(z[rows, :], steep, 1, 1).astype(jnp.bfloat16)))
+        stores.append((mid, (rows, slice(None)), inner_dot(w[at], steep, 1, 0)))
+        return stores, carry
 
     by_chunk(blocks, right, 0, arrive_right)
     right_out = gradient_copies(gw, (own_grad, peer_grad), gw_sems, 1)
@@ -546,10 +554,11 @@
         to = (home // chunk_blocks, 0, home % chunk_blocks)
         arrived = [mid[pl.ds(q * blocks + block, blocks, stride=size), :] for q in range(fold)]
         arrived = jnp.concatenate(arrived, axis=0).astype(jnp.bfloat16)
-        gw[to] = inner_dot(u[rows, :], arrived, 1, 1).astype(jnp.bfloat16)
+        factor_grad = inner_dot(u[rows, :], arrived, 1, 1).astype(jnp.bfloat16)
         weighted = inner_dot(w[at], arrived, 1, 0) * column(gain_ref, block, slots)
-        g[rows, :] = g[rows, :] + scale * weighted
-        return total + fold_rows(weighted * h[rows, :].astype(jnp.float32))
+        carried = g[rows, :] + scale * weighted
+        stores = [(gw, to, factor_grad), (g, (rows, slice(None)), carried)]
+        return stores, total + fold_rows(weighted * h[rows, :].astype(jnp.float32))
 
     total = by_chunk(blocks, left, jnp.zeros((8, slots), jnp.float32), arrive_left)
     left_out = gradient_copies(gw, (own_grad, peer_grad), gw_sems, 0)
@@ -560,11 +569,8 @@
     def finish(block, carry):
         rows = block_rows(block, size)
         ended = g[rows, :] - h[rows, :].astype(jnp.float32) * back
-        if last:
-            u[rows, :] = ended.astype(jnp.bfloat16)
-        else:
-            g[rows, :] = ended
-        return carry
+        at = (rows, slice(None))
+        return [(u, at, ended.astype(jnp.bfloat16)) if last else (g, at, ended)], carry
 
     ended = u if last else g
     by_chunk(blocks, finish, 0, None, lambda chunk: chunk_copy(ended, out_ref, out_sems, chunk).start())
@@ -700,7 +706,7 @@
 def run_sum(groups, parts, apart=True):
     flat = [term.reshape(parts, -1, term.shape[-1]) for terms in groups for term in terms]
     _, rows, lanes = flat[0].shape
-    steps = 8
+    steps = 2
     if apart:
         out_shape = [shape_of((len(groups), rows, lanes), jnp.bfloat16)] * parts
         out_specs = [pl.BlockSpec((len(groups), rows // steps, lanes), lambda i: (0, i, 0))] * parts
@@ -1000,9 +1006,9 @@
     end_column = jnp.broadcast_to(gains[layer_count].T[:, :, None], (blocks, size, wide)).reshape(-1, wide)
     lowest, beside = tie((lowest, beside))
     first_two = gather_two(joined([lowest[0], beside]))
-    first_two, lowest[1], patch_came = tie((first_two, lowest[1], patch_came))
+    later = (lowest[1], move(lowest[1], routes["across"][0]))
+    first_two, later, patch_came = tie((first_two, later, patch_came))
     weights = [as_weights(gather_three(*first_two))]
-    later = (lowest[1], move(lowest[1], routes["across"][0]))
     weights, later, end_column = tie((weights, later, end_column))
 
     residual, target_sent = tie((patch_came, target_sent))
@@ -1021,9 +1027,7 @@
             residual, sums, flying = tie((residual, sums, flying))
             weights.append(as_weights(gather_three(*flying)))
         if layer == groups[0][-1]:
-            residual, sums, weights[1] = tie((residual, sums, weights[1]))
-        if layer == layer_count - 2:
-            residual, sums, target = tie((residual, sums, target))
+            residual, sums, weights[1], target = tie((residual, sums, weights[1], target))
 
     def core_sum(mine, other):
         return (mine, move(other, routes["cores"]))

time: 505 us -> 477 us (0.945)
  Pallas kernels: 195 us -> 179 us
  waiting for transfers between devices: 167 us -> 159 us
    all_to_all x4, waiting for transfers between devices: 62 us -> 39.7 us  [to_planes(): lax.all_to_all(value, 'tensor', split_axis=0, concat_axis=0, tiled=True)]
    pallas_call x6, Pallas kernels: 35.7 us -> 19.7 us  [run_sum(): pl.pallas_call(lambda *refs: sum_kernel(len(groups[0]), len(flat), *refs)...]
    ppermute x30, waiting for transfers between devices: 88.8 us -> 103 us  [move(): return lax.ppermute(value, AXES, route)]
  transfers between devices with their start and end apart: 36 -> 36, of which waited for: 18 -> 20; matrix products, arithmetic and copies ran while one was open for 1% -> 1% of each run, Pallas kernels for 29% -> 25%
where the time goes in v10:
time: 477 us; the launch traced here: 475 us
  Pallas kernels  179 us (38%)
  waiting for transfers between devices  159 us (33%)
  starting transfers between devices  64.9 us (14%)
  blocking collectives  53.7 us (11%)
  local copies, waits for them, and re-layouts  15.9 us (3%)
    ppermute x30, waiting for transfers between devices, move(): return lax.ppermute(value, AXES, route)  103 us
    pallas_call x4, Pallas kernels, run_backward(): pl.pallas_call(lambda *refs: backward_kernel(turning, last, layer, len(so...  73.1 us
    pallas_call x4, Pallas kernels, run_forward(): pl.pallas_call(lambda *refs: forward_kernel(first, layer, len(sources), *...  55.5 us
    all_to_all x1, blocking collectives, to_planes(): lax.all_to_all(value, 'tensor', split_axis=0, concat_axis=0, tiled=True)  53.7 us
    ppermute x30, starting transfers between devices, move(): return lax.ppermute(value, AXES, route)  40 us
    all_to_all x4, waiting for transfers between devices, to_planes(): lax.all_to_all(value, 'tensor', split_axis=0, concat_axis=0, tiled=True)  39.7 us
    pallas_call x6, Pallas kernels, run_sum(): pl.pallas_call(lambda *refs: sum_kernel(len(groups[0]), len(flat), *refs)...  19.7 us
    all_to_all x4, starting transfers between devices, to_planes(): lax.all_to_all(value, 'tensor', split_axis=0, concat_axis=0, tiled=True)  16.2 us
  transfers between devices with their start and end apart: 36, of which 20 were waited for; matrix products, arithmetic and copies ran while one was open for 1% of the time, Pallas kernels for 25%

profile of v10, /device:TPU:5, one launch (start us, length us, event | category | flops | bytes accessed | tf_op | source)
XLA Modules:
  0.0 475.2 jit_solution(8148361265603904553)
XLA Ops:
  3.3 4.6 pieces.1
  7.9 4.5 all-to-all-start
  13.2 4.1 pick.2
  17.3 4.2 pick.3
  21.5 16.2 %all-to-all-done = bf16[4,2128,128]{2,1,0:T(8,128)(2,1)} async-done(((bf16[4,2128,128]{2,1,0:T(8,128)(2,1)}), bf16[4,2128,128]{2,1,0:T(8,128)(2,1)}, u32[]{:S(2)}, u32[]{:S(2)}) %all-to-all-start) | async-done | bytes 2179104 | tf_op jit(solution)/shard_map/all_to_all | solution.py:985
  37.7 53.7 %all_to_all.35 = bf16[4,2128,128]{2,1,0:T(8,128)(2,1)S(1)} all-to-all(bf16[4,2128,128]{2,1,0:T(8,128)(2,1)} %all-to-all-done), channel_id=1, replica_groups=mesh['section'=4,'tensor'=4,'dp'=2] {'tensor'}, dimensions={0} | all-to-all | bytes 4358144 | tf_op jit(solution)/shard_map/all_to_all | solution.py:982
  92.8 4.5 all-to-all-start.2
  97.3 9.5 %collective-permute-done.refs_1_ = bf16[4,1024,128]{2,1,0:T(8,128)(2,1)} collective-permute-done((bf16[4,1024,128]{2,1,0:T(8,128)(2,1)}, bf16[4,1024,128]{2,1,0:T(8,128)(2,1)}, u32[]{:S(2)}, u32[]{:S(2)}) %collective-permute-start) | collective-permute-done | bytes 1048608 | tf_op jit(solution)/shard_map/ppermute | solution.py:943
  113.7 23.8 %collective-permute-done.3.refs_1_ = bf16[4,1024,128]{2,1,0:T(8,128)(2,1)} collective-permute-done((bf16[4,1024,128]{2,1,0:T(8,128)(2,1)S(1)}, bf16[4,1024,128]{2,1,0:T(8,128)(2,1)}, u32[]{:S(2)}, u32[]{:S(2)}) %collective-permute-start.3) | collective-permute-done | bytes 1048608 | tf_op jit(solution)/shard_map/ppermute | solution.py:943
  137.5 7.6 %all-to-all-done.2 = bf16[4,2048,128]{2,1,0:T(8,128)(2,1)} async-done(((bf16[4,2048,128]{2,1,0:T(8,128)(2,1)}), bf16[4,2048,128]{2,1,0:T(8,128)(2,1)}, u32[]{:S(2)}, u32[]{:S(2)}) %all-to-all-start.2) | async-done | bytes 2097184 | tf_op jit(solution)/shard_map/all_to_all | solution.py:982
  166.5 14.4 %forward_layer.4 = (f32[8192,128]{1,0:T(8,128)}, bf16[8192,128]{1,0:T(8,128)(2,1)}, bf16[8192,128]{1,0:T(8,128)(2,1)}, bf16[8192,128]{1,0:T(8,128)(2,1)}, f32[8,128]{1,0:T(8,128)}, /*index=5*/f32[8,128]{1,0:T(8,128)}) custom-call(s32[3,64]{1,0:T(4,128)} %pad_add_fusion.refs_0_, f32[8,128]{1,0:T(8,128)} %broadcast_in_dim.10.refs_1_, ...), custom_call_target="tpu_custom_call" | custom-call | flops 15000000512 | bytes 20971520 | tf_op jit(solution)/shard_map/forward_layer/pallas_call | solution.py:604
  187.8 13.7 %forward_layer.5 = (f32[8192,128]{1,0:T(8,128)}, bf16[8192,128]{1,0:T(8,128)(2,1)}, bf16[8192,128]{1,0:T(8,128)(2,1)}, bf16[8192,128]{1,0:T(8,128)(2,1)}, f32[8,128]{1,0:T(8,128)}, /*index=5*/f32[8,128]{1,0:T(8,128)}) custom-call(s32[3,64]{1,0:T(4,128)} %pad_add_fusion.refs_0_, f32[8,128]{1,0:T(8,128)} %get-tuple-element.182.refs_1_, ...), custom_call_target="tpu_custom_call" | custom-call | flops 15000000512 | bytes 20971520 | tf_op jit(solution)/shard_map/forward_layer/pallas_call | solution.py:604
  201.5 12.1 %all-to-all-done.3 = bf16[4,2048,128]{2,1,0:T(8,128)(2,1)S(1)} async-done(((bf16[4,2048,128]{2,1,0:T(8,128)(2,1)}), bf16[4,2048,128]{2,1,0:T(8,128)(2,1)S(1)}, u32[]{:S(2)}, u32[]{:S(2)}) %all-to-all-start.3) | async-done | bytes 2097184 | tf_op jit(solution)/shard_map/all_to_all | solution.py:982
  213.6 13.7 %forward_layer.6 = (f32[8192,128]{1,0:T(8,128)}, bf16[8192,128]{1,0:T(8,128)(2,1)}, bf16[8192,128]{1,0:T(8,128)(2,1)}, bf16[8192,128]{1,0:T(8,128)(2,1)}, f32[8,128]{1,0:T(8,128)}, /*index=5*/f32[8,128]{1,0:T(8,128)}) custom-call(s32[3,64]{1,0:T(4,128)} %pad_add_fusion.refs_0_, f32[8,128]{1,0:T(8,128)} %get-tuple-element.194.refs_1_, ...), custom_call_target="tpu_custom_call" | custom-call | flops 15000000512 | bytes 20971520 | tf_op jit(solution)/shard_map/forward_layer/pallas_call | solution.py:604
  227.3 13.7 %forward_layer.7 = (f32[8192,128]{1,0:T(8,128)}, bf16[8192,128]{1,0:T(8,128)(2,1)}, bf16[8192,128]{1,0:T(8,128)(2,1)}, bf16[8192,128]{1,0:T(8,128)(2,1)}, f32[8,128]{1,0:T(8,128)}, /*index=5*/f32[8,128]{1,0:T(8,128)}) custom-call(s32[3,64]{1,0:T(4,128)} %pad_add_fusion.refs_0_, f32[8,128]{1,0:T(8,128)} %get-tuple-element.204.refs_1_, ...), custom_call_target="tpu_custom_call" | custom-call | flops 15000000512 | bytes 20971520 | tf_op jit(solution)/shard_map/forward_layer/pallas_call | solution.py:604
  241.1 19.5 %backward_layer.4 = (f32[8192,128]{1,0:T(8,128)}, bf16[16,2,2,128,128]{4,3,2,1,0:T(8,128)(2,1)}, bf16[16,2,2,128,128]{4,3,2,1,0:T(8,128)(2,1)}) custom-call(s32[3,64]{1,0:T(4,128)} %pad_add_fusion.refs_0_, f32[8,128]{1,0:T(8,128)} %get-tuple-element.206.refs_1_, bf16[128,64]{1,0:T(8,128)(2,1)} %copy.20.refs_2_, bf16[8192,128]{1,0:T(8,128)(2,1)} %broadcast_in_dim.23.refs_3_, ...), custom_call_target="tpu_custom_call" | custom-call | flops 17999998976 | bytes 31457280 | tf_op jit(solution)/shard_map/backward_layer/pallas_call | solution.py:635
  261.9 18.1 %backward_layer.5 = (f32[8192,128]{1,0:T(8,128)}, bf16[16,2,2,128,128]{4,3,2,1,0:T(8,128)(2,1)}, bf16[16,2,2,128,128]{4,3,2,1,0:T(8,128)(2,1)}) custom-call(s32[3,64]{1,0:T(4,128)} %pad_add_fusion.refs_0_, f32[8,128]{1,0:T(8,128)} %get-tuple-element.200.refs_1_, bf16[128,64]{1,0:T(8,128)(2,1)} %copy.19.refs_2_, bf16[8192,128]{1,0:T(8,128)(2,1)} %broadcast_in_dim.23.refs_3_, ...), custom_call_target="tpu_custom_call" | custom-call | flops 17999998976 | bytes 31457280 | tf_op jit(solution)/shard_map/backward_layer/pallas_call | solution.py:635
  287.4 18.1 %backward_layer.6 = (f32[8192,128]{1,0:T(8,128)}, bf16[16,2,2,128,128]{4,3,2,1,0:T(8,128)(2,1)}, bf16[16,2,2,128,128]{4,3,2,1,0:T(8,128)(2,1)}) custom-call(s32[3,64]{1,0:T(4,128)} %pad_add_fusion.refs_0_, f32[8,128]{1,0:T(8,128)} %get-tuple-element.184.refs_1_, bf16[128,64]{1,0:T(8,128)(2,1)} %copy.18.refs_2_, bf16[8192,128]{1,0:T(8,128)(2,1)} %broadcast_in_dim.23.refs_3_, ...), custom_call_target="tpu_custom_call" | custom-call | flops 17999998976 | bytes 31457280 | tf_op jit(solution)/shard_map/backward_layer/pallas_call | solution.py:635
  305.5 4.2 collective-permute-done.11
  317.3 17.4 %backward_layer.7 = (bf16[8192,128]{1,0:T(8,128)(2,1)}, bf16[16,2,2,128,128]{4,3,2,1,0:T(8,128)(2,1)}, bf16[16,2,2,128,128]{4,3,2,1,0:T(8,128)(2,1)}) custom-call(s32[3,64]{1,0:T(4,128)} %pad_add_fusion.refs_0_, f32[8,128]{1,0:T(8,128)} %get-tuple-element.173.refs_1_, bf16[128,64]{1,0:T(8,128)(2,1)} %copy.17.refs_2_, ...), custom_call_target="tpu_custom_call" | custom-call | flops 17999998976 | bytes 31457280 | tf_op jit(solution)/shard_map/backward_layer/pallas_call | solution.py:635
  352.4 11.1 %collective-permute-done.18 = bf16[2048,128]{1,0:T(8,128)(2,1)S(1)} collective-permute-done((bf16[2048,128]{1,0:T(8,128)(2,1)}, bf16[2048,128]{1,0:T(8,128)(2,1)S(1)}, u32[]{:S(2)}, u32[]{:S(2)}) %collective-permute-start.18) | collective-permute-done | bytes 524320 | tf_op jit(solution)/shard_map/ppermute | solution.py:943
  363.9 11.3 %collective-permute-done.20 = bf16[2048,128]{1,0:T(8,128)(2,1)S(1)} collective-permute-done((bf16[2048,128]{1,0:T(8,128)(2,1)}, bf16[2048,128]{1,0:T(8,128)(2,1)S(1)}, u32[]{:S(2)}, u32[]{:S(2)}) %collective-permute-start.20) | collective-permute-done | bytes 524320 | tf_op jit(solution)/shard_map/ppermute | solution.py:943
  376.1 4.1 sum.10
  380.2 10.7 %all-to-all-done.4.came_ref = bf16[4,2048,128]{2,1,0:T(8,128)(2,1)S(1)} async-done(((bf16[4,2048,128]{2,1,0:T(8,128)(2,1)}), bf16[4,2048,128]{2,1,0:T(8,128)(2,1)S(1)}, u32[]{:S(2)}, u32[]{:S(2)}) %all-to-all-start.4) | async-done | bytes 2097184 | tf_op jit(solution)/shard_map/all_to_all | solution.py:982
  390.9 4.4 all-to-all-start.5
  401.3 9.6 %collective-permute-done.21 = bf16[2048,128]{1,0:T(8,128)(2,1)S(1)} collective-permute-done((bf16[2048,128]{1,0:T(8,128)(2,1)}, bf16[2048,128]{1,0:T(8,128)(2,1)S(1)}, u32[]{:S(2)}, u32[]{:S(2)}) %collective-permute-start.21) | collective-permute-done | bytes 524320 | tf_op jit(solution)/shard_map/ppermute | solution.py:943
  411.3 11.1 %collective-permute-done.23 = bf16[2048,128]{1,0:T(8,128)(2,1)S(1)} collective-permute-done((bf16[2048,128]{1,0:T(8,128)(2,1)}, bf16[2048,128]{1,0:T(8,128)(2,1)S(1)}, u32[]{:S(2)}, u32[]{:S(2)}) %collective-permute-start.23) | collective-permute-done | bytes 524320 | tf_op jit(solution)/shard_map/ppermute | solution.py:943
  422.5 9.3 %all-to-all-done.5 = bf16[4,1536,128]{2,1,0:T(8,128)(2,1)} async-done(((bf16[4,1536,128]{2,1,0:T(8,128)(2,1)}), bf16[4,1536,128]{2,1,0:T(8,128)(2,1)}, u32[]{:S(2)}, u32[]{:S(2)}) %all-to-all-start.5) | async-done | bytes 1572896 | tf_op jit(solution)/shard_map/all_to_all | solution.py:982
  431.8 4.2 all-to-all-start.6
  445.5 6.1 %collective-permute-start.27 = (bf16[512,128]{1,0:T(8,128)(2,1)}, bf16[512,128]{1,0:T(8,128)(2,1)}, u32[]{:S(2)}, u32[]{:S(2)}) collective-permute-start(bf16[512,128]{1,0:T(8,128)(2,1)} %bitcast.154), channel_id=1, source_target_pairs={{0,6},{1,7},{2,12},{3,13},{4,18},{5,19},{6,24},{7,25},{8,4},{9,5},... | collective-permute-start | bytes 393224 | tf_op jit(solution)/shard_map/ppermute | solution.py:943
  455.5 5.8 %collective-permute-done.27.refs_3_ = bf16[512,128]{1,0:T(8,128)(2,1)} collective-permute-done((bf16[512,128]{1,0:T(8,128)(2,1)}, bf16[512,128]{1,0:T(8,128)(2,1)}, u32[]{:S(2)}, u32[]{:S(2)}) %collective-permute-start.27) | collective-permute-done | bytes 131104 | tf_op jit(solution)/shard_map/ppermute | solution.py:943
  469.2 5.9 %assemble.1 = (f32[4,16,128,128]{3,2,1,0:T(8,128)}, f32[4,16,128,128]{3,2,1,0:T(8,128)}) custom-call(s32[3]{0:T(128)} %pad_add_fusion.1.refs_0_, bf16[128,128]{1,0:T(8,128)(2,1)} %fusion.refs_1_, bf16[4,1,2,2,128,128]{5,4,3,2,1,0:T(8,128)(2,1)} %bitcast.94, bf16[4,1,2,2,128,128]{5,4,3,2,1,0:T(8,128)(2,1)} %bitcast.112, ...), custom_call_target="tpu_custom_call" | custom-call | bytes 12582912 | tf_op jit(solution)/shard_map/assemble/pallas_call | solution.py:886
  (135 shorter events, 102.9 us)
Async XLA Ops:
  7.9 29.8 %all-to-all-start = ((bf16[4,2128,128]{2,1,0:T(8,128)(2,1)}), bf16[4,2128,128]{2,1,0:T(8,128)(2,1)}, u32[]{:S(2)}, u32[]{:S(2)}) async-start(bf16[4,2128,128]{2,1,0:T(8,128)(2,1)} %pieces.1), calls=%async_computation | async-start | bytes 4358144 | tf_op jit(solution)/shard_map/all_to_all | solution.py:985
  92.5 14.3 %collective-permute-start = (bf16[4,1024,128]{2,1,0:T(8,128)(2,1)}, bf16[4,1024,128]{2,1,0:T(8,128)(2,1)}, u32[]{:S(2)}, u32[]{:S(2)}) collective-permute-start(bf16[4,1024,128]{2,1,0:T(8,128)(2,1)} %get-tuple-element.157.refs_0_), channel_id=1, source_target_pairs={{0,8},{1,17},{2,10},{3,19},{4,12},{5,21},{6,14},{7,23},{8,0},{9,25... | collective-permute-start | bytes 3145736 | tf_op jit(solution)/shard_map/ppermute | solution.py:943
  92.8 52.2 %all-to-all-start.2 = ((bf16[4,2048,128]{2,1,0:T(8,128)(2,1)}), bf16[4,2048,128]{2,1,0:T(8,128)(2,1)}, u32[]{:S(2)}, u32[]{:S(2)}) async-start(bf16[4,2048,128]{2,1,0:T(8,128)(2,1)} %pick.2), calls=%async_computation.2 | async-start | bytes 4194304 | tf_op jit(solution)/shard_map/all_to_all | solution.py:982
  109.6 35.4 %collective-permute-start.2 = (bf16[8,1024,128]{2,1,0:T(8,128)(2,1)}, bf16[8,1024,128]{2,1,0:T(8,128)(2,1)}, u32[]{:S(2)}, u32[]{:S(2)}) collective-permute-start(bf16[8,1024,128]{2,1,0:T(8,128)(2,1)} %join.3), channel_id=1, source_target_pairs={{0,1},{1,0},{2,3},{3,2},{4,5},{5,4},{6,7},{7,6},{8,9},{9,8},{10,11... | collective-permute-start | bytes 6291464 | tf_op jit(solution)/shard_map/ppermute | solution.py:943
  112.3 36.7 %collective-permute-start.1 = (bf16[8,1024,128]{2,1,0:T(8,128)(2,1)}, bf16[8,1024,128]{2,1,0:T(8,128)(2,1)}, u32[]{:S(2)}, u32[]{:S(2)}) collective-permute-start(bf16[8,1024,128]{2,1,0:T(8,128)(2,1)} %join.3), channel_id=1, source_target_pairs={{0,16},{1,9},{2,18},{3,11},{4,20},{5,13},{6,22},{7,15},{8,24},{9,1... | collective-permute-start | bytes 6291464 | tf_op jit(solution)/shard_map/ppermute | solution.py:943
  112.6 24.9 %collective-permute-start.3 = (bf16[4,1024,128]{2,1,0:T(8,128)(2,1)S(1)}, bf16[4,1024,128]{2,1,0:T(8,128)(2,1)}, u32[]{:S(2)}, u32[]{:S(2)}) collective-permute-start(bf16[4,1024,128]{2,1,0:T(8,128)(2,1)S(1)} %get-tuple-element.180.refs_0_), channel_id=1, source_target_pairs={{0,8},{1,17},{2,10},{3,19},{4,12},{5,21},{6,14},{7,23},{8,0},{9,25... | collective-permute-start | bytes 3145736 | tf_op jit(solution)/shard_map/ppermute | solution.py:943
  158.7 22.2 %collective-permute-start.6 = (bf16[8,1024,128]{2,1,0:T(8,128)(2,1)}, bf16[8,1024,128]{2,1,0:T(8,128)(2,1)}, u32[]{:S(2)}, u32[]{:S(2)}) collective-permute-start(bf16[8,1024,128]{2,1,0:T(8,128)(2,1)} %join.4), channel_id=1, source_target_pairs={{0,1},{1,0},{2,3},{3,2},{4,5},{5,4},{6,7},{7,6},{8,9},{9,8},{10,11... | collective-permute-start | bytes 6291464 | tf_op jit(solution)/shard_map/ppermute | solution.py:943
  159.1 25.5 %collective-permute-start.5 = (bf16[8,1024,128]{2,1,0:T(8,128)(2,1)}, bf16[8,1024,128]{2,1,0:T(8,128)(2,1)}, u32[]{:S(2)}, u32[]{:S(2)}) collective-permute-start(bf16[8,1024,128]{2,1,0:T(8,128)(2,1)} %join.4), channel_id=1, source_target_pairs={{0,16},{1,9},{2,18},{3,11},{4,20},{5,13},{6,22},{7,15},{8,24},{9,1... | collective-permute-start | bytes 6291464 | tf_op jit(solution)/shard_map/ppermute | solution.py:943
  162.1 51.4 %all-to-all-start.3 = ((bf16[4,2048,128]{2,1,0:T(8,128)(2,1)}), bf16[4,2048,128]{2,1,0:T(8,128)(2,1)S(1)}, u32[]{:S(2)}, u32[]{:S(2)}) async-start(bf16[4,2048,128]{2,1,0:T(8,128)(2,1)} %pick.3), calls=%async_computation.3 | async-start | bytes 4194304 | tf_op jit(solution)/shard_map/all_to_all | solution.py:982
  184.6 29.0 %collective-permute-start.7 = (bf16[8,1024,128]{2,1,0:T(8,128)(2,1)}, bf16[8,1024,128]{2,1,0:T(8,128)(2,1)}, u32[]{:S(2)}, u32[]{:S(2)}) collective-permute-start(bf16[8,1024,128]{2,1,0:T(8,128)(2,1)} %collective-permute-done.5), channel_id=1, source_target_pairs={{0,1},{1,0},{2,3},{3,2},{4,5},{5,4},{6,7},{7,6},{8,9},{9,8},{10,11... | collective-permute-start | bytes 6291464 | tf_op jit(solution)/shard_map/ppermute | solution.py:943
  260.6 19.5 %collective-permute-start.8 = (bf16[16,2,2,128,128]{4,3,2,1,0:T(8,128)(2,1)}, bf16[16,2,2,128,128]{4,3,2,1,0:T(8,128)(2,1)S(1)}, u32[]{:S(2)}, u32[]{:S(2)}) collective-permute-start(bf16[16,2,2,128,128]{4,3,2,1,0:T(8,128)(2,1)} %get-tuple-element.217), channel_id=1, source_target_pairs={{0,1},{1,0},{2,3},{3,2},{4,5},{5,4},{6,7},{7,6},{8,9},{9,8},{10,11... | collective-permute-start | bytes 6291464 | tf_op jit(solution)/shard_map/ppermute | solution.py:943
  281.4 28.3 %collective-permute-start.12 = (bf16[16,2,2,128,128]{4,3,2,1,0:T(8,128)(2,1)}, bf16[16,2,2,128,128]{4,3,2,1,0:T(8,128)(2,1)S(1)}, u32[]{:S(2)}, u32[]{:S(2)}) collective-permute-start(bf16[16,2,2,128,128]{4,3,2,1,0:T(8,128)(2,1)} %get-tuple-element.229), channel_id=1, source_target_pairs={{0,1},{1,0},{2,3},{3,2},{4,5},{5,4},{6,7},{7,6},{8,9},{9,8},{10,11... | collective-permute-start | bytes 6291464 | tf_op jit(solution)/shard_map/ppermute | solution.py:943
  284.7 20.7 %collective-permute-start.9 = (bf16[2048,128]{1,0:T(8,128)(2,1)}, bf16[2048,128]{1,0:T(8,128)(2,1)S(1)}, u32[]{:S(2)}, u32[]{:S(2)}) collective-permute-start(bf16[2048,128]{1,0:T(8,128)(2,1)} %bitcast.147), channel_id=1, source_target_pairs={{0,8},{1,9},{2,10},{3,11},{4,12},{5,13},{6,14},{7,15},{8,0},{9,1},... | collective-permute-start | bytes 1572872 | tf_op jit(solution)/shard_map/ppermute | solution.py:943
  285.4 20.0 %collective-permute-start.10 = (bf16[2048,128]{1,0:T(8,128)(2,1)}, bf16[2048,128]{1,0:T(8,128)(2,1)S(1)}, u32[]{:S(2)}, u32[]{:S(2)}) collective-permute-start(bf16[2048,128]{1,0:T(8,128)(2,1)} %bitcast.146), channel_id=1, source_target_pairs={{0,16},{1,17},{2,18},{3,19},{4,20},{5,21},{6,22},{7,23},{8,24},{9,... | collective-permute-start | bytes 1572872 | tf_op jit(solution)/shard_map/ppermute | solution.py:943
  286.2 23.5 %collective-permute-start.11 = (bf16[2048,128]{1,0:T(8,128)(2,1)}, bf16[2048,128]{1,0:T(8,128)(2,1)S(1)}, u32[]{:S(2)}, u32[]{:S(2)}) collective-permute-start(bf16[2048,128]{1,0:T(8,128)(2,1)} %bitcast.144), channel_id=1, source_target_pairs={{0,24},{1,25},{2,26},{3,27},{4,28},{5,29},{6,30},{7,31},{8,16},{9,... | collective-permute-start | bytes 1572872 | tf_op jit(solution)/shard_map/ppermute | solution.py:943
  309.7 29.1 %collective-permute-start.16 = (bf16[16,2,2,128,128]{4,3,2,1,0:T(8,128)(2,1)}, bf16[16,2,2,128,128]{4,3,2,1,0:T(8,128)(2,1)}, u32[]{:S(2)}, u32[]{:S(2)}) collective-permute-start(bf16[16,2,2,128,128]{4,3,2,1,0:T(8,128)(2,1)} %get-tuple-element.245), channel_id=1, source_target_pairs={{0,1},{1,0},{2,3},{3,2},{4,5},{5,4},{6,7},{7,6},{8,9},{9,8},{10,11... | collective-permute-start | bytes 6291464 | tf_op jit(solution)/shard_map/ppermute | solution.py:943
  314.6 20.1 %collective-permute-start.13 = (bf16[2048,128]{1,0:T(8,128)(2,1)}, bf16[2048,128]{1,0:T(8,128)(2,1)S(1)}, u32[]{:S(2)}, u32[]{:S(2)}) collective-permute-start(bf16[2048,128]{1,0:T(8,128)(2,1)} %bitcast.145), channel_id=1, source_target_pairs={{0,8},{1,9},{2,10},{3,11},{4,12},{5,13},{6,14},{7,15},{8,0},{9,1},... | collective-permute-start | bytes 1572872 | tf_op jit(solution)/shard_map/ppermute | solution.py:943
  315.4 20.1 %collective-permute-start.14 = (bf16[2048,128]{1,0:T(8,128)(2,1)}, bf16[2048,128]{1,0:T(8,128)(2,1)S(1)}, u32[]{:S(2)}, u32[]{:S(2)}) collective-permute-start(bf16[2048,128]{1,0:T(8,128)(2,1)} %bitcast.143), channel_id=1, source_target_pairs={{0,16},{1,17},{2,18},{3,19},{4,20},{5,21},{6,22},{7,23},{8,24},{9,... | collective-permute-start | bytes 1572872 | tf_op jit(solution)/shard_map/ppermute | solution.py:943
  316.1 22.7 %collective-permute-start.15 = (bf16[2048,128]{1,0:T(8,128)(2,1)}, bf16[2048,128]{1,0:T(8,128)(2,1)S(1)}, u32[]{:S(2)}, u32[]{:S(2)}) collective-permute-start(bf16[2048,128]{1,0:T(8,128)(2,1)} %bitcast.142), channel_id=1, source_target_pairs={{0,24},{1,25},{2,26},{3,27},{4,28},{5,29},{6,30},{7,31},{8,16},{9,... | collective-permute-start | bytes 1572872 | tf_op jit(solution)/shard_map/ppermute | solution.py:943
  339.6 51.3 %all-to-all-start.4 = ((bf16[4,2048,128]{2,1,0:T(8,128)(2,1)}), bf16[4,2048,128]{2,1,0:T(8,128)(2,1)S(1)}, u32[]{:S(2)}, u32[]{:S(2)}) async-start(bf16[4,2048,128]{2,1,0:T(8,128)(2,1)} %bitcast.105), calls=%async_computation.4 | async-start | bytes 4194304 | tf_op jit(solution)/shard_map/all_to_all | solution.py:982
  343.2 32.0 %collective-permute-start.17 = (bf16[16,2,2,128,128]{4,3,2,1,0:T(8,128)(2,1)}, bf16[16,2,2,128,128]{4,3,2,1,0:T(8,128)(2,1)}, u32[]{:S(2)}, u32[]{:S(2)}) collective-permute-start(bf16[16,2,2,128,128]{4,3,2,1,0:T(8,128)(2,1)} %get-tuple-element.247), channel_id=1, source_target_pairs={{0,1},{1,0},{2,3},{3,2},{4,5},{5,4},{6,7},{7,6},{8,9},{9,8},{10,11... | collective-permute-start | bytes 6291464 | tf_op jit(solution)/shard_map/ppermute | solution.py:943
  349.8 13.7 %collective-permute-start.18 = (bf16[2048,128]{1,0:T(8,128)(2,1)}, bf16[2048,128]{1,0:T(8,128)(2,1)S(1)}, u32[]{:S(2)}, u32[]{:S(2)}) collective-permute-start(bf16[2048,128]{1,0:T(8,128)(2,1)} %bitcast.152), channel_id=1, source_target_pairs={{0,8},{1,9},{2,10},{3,11},{4,12},{5,13},{6,14},{7,15},{8,0},{9,1},... | collective-permute-start | bytes 1572872 | tf_op jit(solution)/shard_map/ppermute | solution.py:943
  350.5 13.4 %collective-permute-start.19 = (bf16[2048,128]{1,0:T(8,128)(2,1)}, bf16[2048,128]{1,0:T(8,128)(2,1)S(1)}, u32[]{:S(2)}, u32[]{:S(2)}) collective-permute-start(bf16[2048,128]{1,0:T(8,128)(2,1)} %bitcast.150), channel_id=1, source_target_pairs={{0,16},{1,17},{2,18},{3,19},{4,20},{5,21},{6,22},{7,23},{8,24},{9,... | collective-permute-start | bytes 1572872 | tf_op jit(solution)/shard_map/ppermute | solution.py:943
  351.3 24.0 %collective-permute-start.20 = (bf16[2048,128]{1,0:T(8,128)(2,1)}, bf16[2048,128]{1,0:T(8,128)(2,1)S(1)}, u32[]{:S(2)}, u32[]{:S(2)}) collective-permute-start(bf16[2048,128]{1,0:T(8,128)(2,1)} %bitcast.148), channel_id=1, source_target_pairs={{0,24},{1,25},{2,26},{3,27},{4,28},{5,29},{6,30},{7,31},{8,16},{9,... | collective-permute-start | bytes 1572872 | tf_op jit(solution)/shard_map/ppermute | solution.py:943
  390.9 40.9 %all-to-all-start.5 = ((bf16[4,1536,128]{2,1,0:T(8,128)(2,1)}), bf16[4,1536,128]{2,1,0:T(8,128)(2,1)}, u32[]{:S(2)}, u32[]{:S(2)}) async-start(bf16[4,1536,128]{2,1,0:T(8,128)(2,1)} %bitcast.91), calls=%async_computation.5 | async-start | bytes 3145728 | tf_op jit(solution)/shard_map/all_to_all | solution.py:982
  398.6 12.3 %collective-permute-start.21 = (bf16[2048,128]{1,0:T(8,128)(2,1)}, bf16[2048,128]{1,0:T(8,128)(2,1)S(1)}, u32[]{:S(2)}, u32[]{:S(2)}) collective-permute-start(bf16[2048,128]{1,0:T(8,128)(2,1)} %bitcast.153), channel_id=1, source_target_pairs={{0,8},{1,9},{2,10},{3,11},{4,12},{5,13},{6,14},{7,15},{8,0},{9,1},... | collective-permute-start | bytes 1572872 | tf_op jit(solution)/shard_map/ppermute | solution.py:943
  399.3 12.0 %collective-permute-start.22 = (bf16[2048,128]{1,0:T(8,128)(2,1)}, bf16[2048,128]{1,0:T(8,128)(2,1)S(1)}, u32[]{:S(2)}, u32[]{:S(2)}) collective-permute-start(bf16[2048,128]{1,0:T(8,128)(2,1)} %bitcast.151), channel_id=1, source_target_pairs={{0,16},{1,17},{2,18},{3,19},{4,20},{5,21},{6,22},{7,23},{8,24},{9,... | collective-permute-start | bytes 1572872 | tf_op jit(solution)/shard_map/ppermute | solution.py:943
  400.0 22.4 %collective-permute-start.23 = (bf16[2048,128]{1,0:T(8,128)(2,1)}, bf16[2048,128]{1,0:T(8,128)(2,1)S(1)}, u32[]{:S(2)}, u32[]{:S(2)}) collective-permute-start(bf16[2048,128]{1,0:T(8,128)(2,1)} %bitcast.149), channel_id=1, source_target_pairs={{0,24},{1,25},{2,26},{3,27},{4,28},{5,29},{6,30},{7,31},{8,16},{9,... | collective-permute-start | bytes 1572872 | tf_op jit(solution)/shard_map/ppermute | solution.py:943
  431.8 29.5 %all-to-all-start.6 = ((bf16[4,1536,128]{2,1,0:T(8,128)(2,1)}), bf16[4,1536,128]{2,1,0:T(8,128)(2,1)S(1)}, u32[]{:S(2)}, u32[]{:S(2)}) async-start(bf16[4,1536,128]{2,1,0:T(8,128)(2,1)} %all-to-all-done.5), calls=%async_computation.6 | async-start | bytes 3145728 | tf_op jit(solution)/shard_map/all_to_all | solution.py:985
  438.3 17.1 %collective-permute-start.25 = (bf16[512,128]{1,0:T(8,128)(2,1)}, bf16[512,128]{1,0:T(8,128)(2,1)S(1)}, u32[]{:S(2)}, u32[]{:S(2)}) collective-permute-start(bf16[512,128]{1,0:T(8,128)(2,1)} %bitcast.157), channel_id=1, source_target_pairs={{0,2},{1,3},{2,8},{3,9},{4,22},{5,23},{6,28},{7,29},{8,0},{9,1},{1... | collective-permute-start | bytes 393224 | tf_op jit(solution)/shard_map/ppermute | solution.py:943
  440.2 15.2 %collective-permute-start.24 = (bf16[512,128]{1,0:T(8,128)(2,1)}, bf16[512,128]{1,0:T(8,128)(2,1)S(1)}, u32[]{:S(2)}, u32[]{:S(2)}) collective-permute-start(bf16[512,128]{1,0:T(8,128)(2,1)} %bitcast.156), channel_id=1, source_target_pairs={{0,0},{1,1},{2,10},{3,11},{4,20},{5,21},{6,30},{7,31},{8,2},{9,3},... | collective-permute-start | bytes 393224 | tf_op jit(solution)/shard_map/ppermute | solution.py:943
  445.5 15.8 %collective-permute-start.27 = (bf16[512,128]{1,0:T(8,128)(2,1)}, bf16[512,128]{1,0:T(8,128)(2,1)}, u32[]{:S(2)}, u32[]{:S(2)}) collective-permute-start(bf16[512,128]{1,0:T(8,128)(2,1)} %bitcast.154), channel_id=1, source_target_pairs={{0,6},{1,7},{2,12},{3,13},{4,18},{5,19},{6,24},{7,25},{8,4},{9,5},... | collective-permute-start | bytes 393224 | tf_op jit(solution)/shard_map/ppermute | solution.py:943
  (30 other events, 286.9 us)

commit v11 on v10

--- a/solution.py
+++ b/solution.py
@@ -470,19 +470,22 @@
     right_in = factor_copies(parts, layer, w, w_sems, 1)
     g_ref, h_ref = sources[:2]
     if turning:
-        start_chunks(g_ref, top, in_sems.at[0])
-        start_chunks(end_gain_ref, end_gain, in_sems.at[6])
-        start_chunks(sources[2], goal, in_sems.at[5])
-    else:
-        start_chunks(g_ref, g, in_sems.at[0])
+        for chunk in range(CHUNKS):
+            chunk_copy(g_ref, top, in_sems.at[0], chunk).start()
+            chunk_copy(end_gain_ref, end_gain, in_sems.at[6], chunk).start()
+            chunk_copy(sources[2], goal, in_sems.at[5], chunk).start()
     for copy in right_in:
         copy.start()
-    start_chunks(slope_ref, slope, in_sems.at[1])
-    start_chunks(z_ref, z, in_sems.at[2])
+    for chunk in range(CHUNKS):
+        if not turning:
+            chunk_copy(g_ref, g, in_sems.at[0], chunk).start()
+        chunk_copy(slope_ref, slope, in_sems.at[1], chunk).start()
+        chunk_copy(z_ref, z, in_sems.at[2], chunk).start()
     for copy in left_in:
         copy.start()
-    start_chunks(u_ref, u, in_sems.at[3])
-    start_chunks(h_ref, h, in_sems.at[4])
+    for chunk in range(CHUNKS):
+        chunk_copy(u_ref, u, in_sems.at[3], chunk).start()
+        chunk_copy(h_ref, h, in_sems.at[4], chunk).start()
 
     if turning:
         zero = jnp.zeros((8, slots), jnp.float32)
@@ -516,7 +519,7 @@
         chunk_copy(slope_ref, slope, in_sems.at[1], chunk).wait()
         chunk_copy(z_ref, z, in_sems.at[2], chunk).wait()
 
-    def right(block, carry):
+    def right(block, total):
         rows = block_rows(block, size)
         place, home = table_ref[0, block], table_ref[2 if last else 1, block]
         at = (place // chunk_blocks, 1, place % chunk_blocks)
@@ -531,23 +534,26 @@
             gradient = g[rows, :]
             stores = []
         steep = (gradient * slope[rows, :].astype(jnp.float32)).astype(jnp.bfloat16)
-        stores.append((gw, to, inner_dot(z[rows, :], steep, 1, 1).astype(jnp.bfloat16)))
-        stores.append((mid, (rows, slice(None)), inner_dot(w[at], steep, 1, 0)))
-        return stores, carry
-
-    by_chunk(blocks, right, 0, arrive_right)
+        taken = z[rows, :]
+        back = inner_dot(w[at], steep, 1, 0)
+        stores.append((gw, to, inner_dot(taken, steep, 1, 1).astype(jnp.bfloat16)))
+        stores.append((mid, (rows, slice(None)), back))
+        return stores, total + fold_rows(taken.astype(jnp.float32) * back)
+
+    total = by_chunk(blocks, right, jnp.zeros((8, slots), jnp.float32), arrive_right)
     right_out = gradient_copies(gw, (own_grad, peer_grad), gw_sems, 1)
     for copy in right_out:
         copy.start()
     for copy in left_in:
         copy.wait()
     scale = scale_ref[0:1, :]
+    back = scale * scale * jnp.sum(total, axis=0, keepdims=True) / features
 
     def arrive_left(chunk):
         chunk_copy(u_ref, u, in_sems.at[3], chunk).wait()
         chunk_copy(h_ref, h, in_sems.at[4], chunk).wait()
 
-    def left(block, total):
+    def left(block, carry):
         rows = block_rows(block, size)
         place, home = table_ref[0, block], table_ref[2 if last else 1, block]
         at = (place // chunk_blocks, 0, place % chunk_blocks)
@@ -556,24 +562,19 @@
         arrived = jnp.concatenate(arrived, axis=0).astype(jnp.bfloat16)
         factor_grad = inner_dot(u[rows, :], arrived, 1, 1).astype(jnp.bfloat16)
         weighted = inner_dot(w[at], arrived, 1, 0) * column(gain_ref, block, slots)
-        carried = g[rows, :] + scale * weighted
-        stores = [(gw, to, factor_grad), (g, (rows, slice(None)), carried)]
-        return stores, total + fold_rows(weighted * h[rows, :].astype(jnp.float32))
-
-    total = by_chunk(blocks, left, jnp.zeros((8, slots), jnp.float32), arrive_left)
+        ended = g[rows, :] + scale * weighted - h[rows, :].astype(jnp.float32) * back
+        index = (rows, slice(None))
+        stores = [(gw, to, factor_grad)]
+        stores.append((u, index, ended.astype(jnp.bfloat16)) if last else (g, index, ended))
+        return stores, carry
+
+    ended = u if last else g
+    by_chunk(
+        blocks, left, 0, arrive_left, lambda chunk: chunk_copy(ended, out_ref, out_sems, chunk).start()
+    )
     left_out = gradient_copies(gw, (own_grad, peer_grad), gw_sems, 0)
     for copy in left_out:
         copy.start()
-    back = scale * scale * scale * jnp.sum(total, axis=0, keepdims=True) / features
-
-    def finish(block, carry):
-        rows = block_rows(block, size)
-        ended = g[rows, :] - h[rows, :].astype(jnp.float32) * back
-        at = (rows, slice(None))
-        return [(u, at, ended.astype(jnp.bfloat16)) if last else (g, at, ended)], carry
-
-    ended = u if last else g
-    by_chunk(blocks, finish, 0, None, lambda chunk: chunk_copy(ended, out_ref, out_sems, chunk).start())
     wait_chunks(ended, out_ref, out_sems)
     for copy in right_out + left_out:
         copy.wait()
@@ -839,8 +840,8 @@
     )(pairs, came)
 
 
-FORWARD_COST = 15_000_000_000
-BACKWARD_COST = 18_000_000_000
+FORWARD_COST = 4_000_000_000
+BACKWARD_COST = 5_000_000_000
 
 
 def assemble_kernel(layers, factor, place_ref, order_ref, *refs):
@@ -1004,12 +1005,12 @@
     gains = lifted[:, layer_count * layer_rows :].reshape(width, layer_count + 1, local_blocks, size)
     gains = gains.transpose(1, 3, 0, 2).reshape(layer_count + 1, size, blocks)
     end_column = jnp.broadcast_to(gains[layer_count].T[:, :, None], (blocks, size, wide)).reshape(-1, wide)
-    lowest, beside = tie((lowest, beside))
+    lowest, beside, end_column = tie((lowest, beside, end_column))
     first_two = gather_two(joined([lowest[0], beside]))
     later = (lowest[1], move(lowest[1], routes["across"][0]))
     first_two, later, patch_came = tie((first_two, later, patch_came))
     weights = [as_weights(gather_three(*first_two))]
-    weights, later, end_column = tie((weights, later, end_column))
+    weights, later = tie((weights, later))
 
     residual, target_sent = tie((patch_came, target_sent))
     target = to_planes(target_sent).reshape(-1, wide)
@@ -1027,7 +1028,9 @@
             residual, sums, flying = tie((residual, sums, flying))
             weights.append(as_weights(gather_three(*flying)))
         if layer == groups[0][-1]:
-            residual, sums, weights[1], target = tie((residual, sums, weights[1], target))
+            residual, sums, weights[1] = tie((residual, sums, weights[1]))
+        if layer == layer_count - 2:
+            residual, sums, target = tie((residual, sums, target))
 
     def core_sum(mine, other):
         return (mine, move(other, routes["cores"]))

time: 477 us -> 466 us (0.977)
  waiting for transfers between devices: 159 us -> 148 us
    all_to_all x4, waiting for transfers between devices: 39.7 us -> 25.3 us  [to_planes(): lax.all_to_all(value, 'tensor', split_axis=0, concat_axis=0, tiled=True)]
  transfers between devices with their start and end apart: 36 -> 36, of which waited for: 20 -> 19; matrix products, arithmetic and copies ran while one was open for 1% -> 2% of each run, Pallas kernels for 25% -> 28%
where the time goes in v11:
time: 466 us; the launch traced here: 463 us
  Pallas kernels  178 us (38%)
  waiting for transfers between devices  148 us (32%)
  starting transfers between devices  63.6 us (14%)
  blocking collectives  53.7 us (12%)
  local copies, waits for them, and re-layouts  17.4 us (4%)
    ppermute x30, waiting for transfers between devices, move(): return lax.ppermute(value, AXES, route)  106 us
    pallas_call x4, Pallas kernels, run_backward(): pl.pallas_call(lambda *refs: backward_kernel(turning, last, layer, len(so...  72 us
    pallas_call x4, Pallas kernels, run_forward(): pl.pallas_call(lambda *refs: forward_kernel(first, layer, len(sources), *...  55.6 us
    all_to_all x1, blocking collectives, to_planes(): lax.all_to_all(value, 'tensor', split_axis=0, concat_axis=0, tiled=True)  53.7 us
    ppermute x30, starting transfers between devices, move(): return lax.ppermute(value, AXES, route)  38.6 us
    all_to_all x4, waiting for transfers between devices, to_planes(): lax.all_to_all(value, 'tensor', split_axis=0, concat_axis=0, tiled=True)  25.3 us
    pallas_call x6, Pallas kernels, run_sum(): pl.pallas_call(lambda *refs: sum_kernel(len(groups[0]), len(flat), *refs)...  19.7 us
    all_to_all x2, waiting for transfers between devices, to_sections(): lax.all_to_all(value, 'section', split_axis=0, concat_axis=0, tiled=True)  16.2 us
  transfers between devices with their start and end apart: 36, of which 19 were waited for; matrix products, arithmetic and copies ran while one was open for 2% of the time, Pallas kernels for 28%

profile of v11, /device:TPU:5, one launch (start us, length us, event | category | flops | bytes accessed | tf_op | source)
XLA Modules:
  0.0 463.4 jit_solution(16940190244246086247)
XLA Ops:
  3.3 4.6 pieces.1
  8.0 4.5 all-to-all-start
  13.2 4.1 pick.2
  17.3 4.2 pick.3
  21.5 16.2 %all-to-all-done = bf16[4,2128,128]{2,1,0:T(8,128)(2,1)} async-done(((bf16[4,2128,128]{2,1,0:T(8,128)(2,1)}), bf16[4,2128,128]{2,1,0:T(8,128)(2,1)}, u32[]{:S(2)}, u32[]{:S(2)}) %all-to-all-start) | async-done | bytes 2179104 | tf_op jit(solution)/shard_map/all_to_all | solution.py:986
  37.7 53.7 %all_to_all.35 = bf16[4,2128,128]{2,1,0:T(8,128)(2,1)S(1)} all-to-all(bf16[4,2128,128]{2,1,0:T(8,128)(2,1)} %all-to-all-done), channel_id=1, replica_groups=mesh['section'=4,'tensor'=4,'dp'=2] {'tensor'}, dimensions={0} | all-to-all | bytes 4358144 | tf_op jit(solution)/shard_map/all_to_all | solution.py:983
  92.9 4.5 all-to-all-start.2
  97.4 9.4 %collective-permute-done.refs_1_ = bf16[4,1024,128]{2,1,0:T(8,128)(2,1)} collective-permute-done((bf16[4,1024,128]{2,1,0:T(8,128)(2,1)}, bf16[4,1024,128]{2,1,0:T(8,128)(2,1)}, u32[]{:S(2)}, u32[]{:S(2)}) %collective-permute-start) | collective-permute-done | bytes 1048608 | tf_op jit(solution)/shard_map/ppermute | solution.py:944
  115.9 23.8 %collective-permute-done.3.refs_1_ = bf16[4,1024,128]{2,1,0:T(8,128)(2,1)} collective-permute-done((bf16[4,1024,128]{2,1,0:T(8,128)(2,1)S(1)}, bf16[4,1024,128]{2,1,0:T(8,128)(2,1)}, u32[]{:S(2)}, u32[]{:S(2)}) %collective-permute-start.3) | collective-permute-done | bytes 1048608 | tf_op jit(solution)/shard_map/ppermute | solution.py:944
  139.7 5.4 %all-to-all-done.2 = bf16[4,2048,128]{2,1,0:T(8,128)(2,1)} async-done(((bf16[4,2048,128]{2,1,0:T(8,128)(2,1)}), bf16[4,2048,128]{2,1,0:T(8,128)(2,1)}, u32[]{:S(2)}, u32[]{:S(2)}) %all-to-all-start.2) | async-done | bytes 2097184 | tf_op jit(solution)/shard_map/all_to_all | solution.py:983
  145.1 6.2 %collective-permute-done.1 = bf16[8,1024,128]{2,1,0:T(8,128)(2,1)} collective-permute-done((bf16[8,1024,128]{2,1,0:T(8,128)(2,1)}, bf16[8,1024,128]{2,1,0:T(8,128)(2,1)}, u32[]{:S(2)}, u32[]{:S(2)}) %collective-permute-start.1) | collective-permute-done | bytes 2097184 | tf_op jit(solution)/shard_map/ppermute | solution.py:944
  167.9 14.4 %forward_layer.4 = (f32[8192,128]{1,0:T(8,128)}, bf16[8192,128]{1,0:T(8,128)(2,1)}, bf16[8192,128]{1,0:T(8,128)(2,1)}, bf16[8192,128]{1,0:T(8,128)(2,1)}, f32[8,128]{1,0:T(8,128)}, /*index=5*/f32[8,128]{1,0:T(8,128)}) custom-call(s32[3,64]{1,0:T(4,128)} %pad_add_fusion.refs_0_, f32[8,128]{1,0:T(8,128)} %broadcast_in_dim.10.refs_1_, ...), custom_call_target="tpu_custom_call" | custom-call | flops 4000000000 | bytes 20971520 | tf_op jit(solution)/shard_map/forward_layer/pallas_call | solution.py:605
  189.1 13.7 %forward_layer.5 = (f32[8192,128]{1,0:T(8,128)}, bf16[8192,128]{1,0:T(8,128)(2,1)}, bf16[8192,128]{1,0:T(8,128)(2,1)}, bf16[8192,128]{1,0:T(8,128)(2,1)}, f32[8,128]{1,0:T(8,128)}, /*index=5*/f32[8,128]{1,0:T(8,128)}) custom-call(s32[3,64]{1,0:T(4,128)} %pad_add_fusion.refs_0_, f32[8,128]{1,0:T(8,128)} %get-tuple-element.184.refs_1_, ...), custom_call_target="tpu_custom_call" | custom-call | flops 4000000000 | bytes 20971520 | tf_op jit(solution)/shard_map/forward_layer/pallas_call | solution.py:605
  202.8 13.7 %forward_layer.6 = (f32[8192,128]{1,0:T(8,128)}, bf16[8192,128]{1,0:T(8,128)(2,1)}, bf16[8192,128]{1,0:T(8,128)(2,1)}, bf16[8192,128]{1,0:T(8,128)(2,1)}, f32[8,128]{1,0:T(8,128)}, /*index=5*/f32[8,128]{1,0:T(8,128)}) custom-call(s32[3,64]{1,0:T(4,128)} %pad_add_fusion.refs_0_, f32[8,128]{1,0:T(8,128)} %get-tuple-element.195.refs_1_, ...), custom_call_target="tpu_custom_call" | custom-call | flops 4000000000 | bytes 20971520 | tf_op jit(solution)/shard_map/forward_layer/pallas_call | solution.py:605
  216.6 13.8 %forward_layer.7 = (f32[8192,128]{1,0:T(8,128)}, bf16[8192,128]{1,0:T(8,128)(2,1)}, bf16[8192,128]{1,0:T(8,128)(2,1)}, bf16[8192,128]{1,0:T(8,128)(2,1)}, f32[8,128]{1,0:T(8,128)}, /*index=5*/f32[8,128]{1,0:T(8,128)}) custom-call(s32[3,64]{1,0:T(4,128)} %pad_add_fusion.refs_0_, f32[8,128]{1,0:T(8,128)} %get-tuple-element.208.refs_1_, ...), custom_call_target="tpu_custom_call" | custom-call | flops 4000000000 | bytes 20971520 | tf_op jit(solution)/shard_map/forward_layer/pallas_call | solution.py:605
  230.4 19.3 %backward_layer.4 = (f32[8192,128]{1,0:T(8,128)}, bf16[16,2,2,128,128]{4,3,2,1,0:T(8,128)(2,1)}, bf16[16,2,2,128,128]{4,3,2,1,0:T(8,128)(2,1)}) custom-call(s32[3,64]{1,0:T(4,128)} %pad_add_fusion.refs_0_, f32[8,128]{1,0:T(8,128)} %get-tuple-element.210.refs_1_, bf16[128,64]{1,0:T(8,128)(2,1)} %copy.20.refs_2_, bf16[8192,128]{1,0:T(8,128)(2,1)} %broadcast_in_dim.23.refs_3_, ...), custom_call_target="tpu_custom_call" | custom-call | flops 5000000000 | bytes 31457280 | tf_op jit(solution)/shard_map/backward_layer/pallas_call | solution.py:636
  249.7 17.6 %backward_layer.5 = (f32[8192,128]{1,0:T(8,128)}, bf16[16,2,2,128,128]{4,3,2,1,0:T(8,128)(2,1)}, bf16[16,2,2,128,128]{4,3,2,1,0:T(8,128)(2,1)}) custom-call(s32[3,64]{1,0:T(4,128)} %pad_add_fusion.refs_0_, f32[8,128]{1,0:T(8,128)} %get-tuple-element.201.refs_1_, bf16[128,64]{1,0:T(8,128)(2,1)} %copy.19.refs_2_, bf16[8192,128]{1,0:T(8,128)(2,1)} %broadcast_in_dim.23.refs_3_, ...), custom_call_target="tpu_custom_call" | custom-call | flops 5000000000 | bytes 31457280 | tf_op jit(solution)/shard_map/backward_layer/pallas_call | solution.py:636
  275.1 17.6 %backward_layer.6 = (f32[8192,128]{1,0:T(8,128)}, bf16[16,2,2,128,128]{4,3,2,1,0:T(8,128)(2,1)}, bf16[16,2,2,128,128]{4,3,2,1,0:T(8,128)(2,1)}) custom-call(s32[3,64]{1,0:T(4,128)} %pad_add_fusion.refs_0_, f32[8,128]{1,0:T(8,128)} %get-tuple-element.186.refs_1_, bf16[128,64]{1,0:T(8,128)(2,1)} %copy.18.refs_2_, bf16[8192,128]{1,0:T(8,128)(2,1)} %broadcast_in_dim.23.refs_3_, ...), custom_call_target="tpu_custom_call" | custom-call | flops 5000000000 | bytes 31457280 | tf_op jit(solution)/shard_map/backward_layer/pallas_call | solution.py:636
  292.8 5.2 %collective-permute-done.11 = bf16[2048,128]{1,0:T(8,128)(2,1)S(1)} collective-permute-done((bf16[2048,128]{1,0:T(8,128)(2,1)}, bf16[2048,128]{1,0:T(8,128)(2,1)S(1)}, u32[]{:S(2)}, u32[]{:S(2)}) %collective-permute-start.11) | collective-permute-done | bytes 524320 | tf_op jit(solution)/shard_map/ppermute | solution.py:944
  305.3 17.6 %backward_layer.7 = (bf16[8192,128]{1,0:T(8,128)(2,1)}, bf16[16,2,2,128,128]{4,3,2,1,0:T(8,128)(2,1)}, bf16[16,2,2,128,128]{4,3,2,1,0:T(8,128)(2,1)}) custom-call(s32[3,64]{1,0:T(4,128)} %pad_add_fusion.refs_0_, f32[8,128]{1,0:T(8,128)} %get-tuple-element.175.refs_1_, bf16[128,64]{1,0:T(8,128)(2,1)} %copy.17.refs_2_, ...), custom_call_target="tpu_custom_call" | custom-call | flops 5000000000 | bytes 31457280 | tf_op jit(solution)/shard_map/backward_layer/pallas_call | solution.py:636
  340.4 11.1 %collective-permute-done.18 = bf16[2048,128]{1,0:T(8,128)(2,1)S(1)} collective-permute-done((bf16[2048,128]{1,0:T(8,128)(2,1)}, bf16[2048,128]{1,0:T(8,128)(2,1)S(1)}, u32[]{:S(2)}, u32[]{:S(2)}) %collective-permute-start.18) | collective-permute-done | bytes 524320 | tf_op jit(solution)/shard_map/ppermute | solution.py:944
  351.9 11.3 %collective-permute-done.20 = bf16[2048,128]{1,0:T(8,128)(2,1)S(1)} collective-permute-done((bf16[2048,128]{1,0:T(8,128)(2,1)}, bf16[2048,128]{1,0:T(8,128)(2,1)S(1)}, u32[]{:S(2)}, u32[]{:S(2)}) %collective-permute-start.20) | collective-permute-done | bytes 524320 | tf_op jit(solution)/shard_map/ppermute | solution.py:944
  364.1 4.1 sum.10
  368.2 10.8 %all-to-all-done.4.came_ref = bf16[4,2048,128]{2,1,0:T(8,128)(2,1)S(1)} async-done(((bf16[4,2048,128]{2,1,0:T(8,128)(2,1)}), bf16[4,2048,128]{2,1,0:T(8,128)(2,1)S(1)}, u32[]{:S(2)}, u32[]{:S(2)}) %all-to-all-start.4) | async-done | bytes 2097184 | tf_op jit(solution)/shard_map/all_to_all | solution.py:983
  379.0 4.4 all-to-all-start.5
  389.4 9.6 %collective-permute-done.21 = bf16[2048,128]{1,0:T(8,128)(2,1)S(1)} collective-permute-done((bf16[2048,128]{1,0:T(8,128)(2,1)}, bf16[2048,128]{1,0:T(8,128)(2,1)S(1)}, u32[]{:S(2)}, u32[]{:S(2)}) %collective-permute-start.21) | collective-permute-done | bytes 524320 | tf_op jit(solution)/shard_map/ppermute | solution.py:944
  399.5 11.2 %collective-permute-done.23 = bf16[2048,128]{1,0:T(8,128)(2,1)S(1)} collective-permute-done((bf16[2048,128]{1,0:T(8,128)(2,1)}, bf16[2048,128]{1,0:T(8,128)(2,1)S(1)}, u32[]{:S(2)}, u32[]{:S(2)}) %collective-permute-start.23) | collective-permute-done | bytes 524320 | tf_op jit(solution)/shard_map/ppermute | solution.py:944
  410.7 9.2 %all-to-all-done.5 = bf16[4,1536,128]{2,1,0:T(8,128)(2,1)} async-done(((bf16[4,1536,128]{2,1,0:T(8,128)(2,1)}), bf16[4,1536,128]{2,1,0:T(8,128)(2,1)}, u32[]{:S(2)}, u32[]{:S(2)}) %all-to-all-start.5) | async-done | bytes 1572896 | tf_op jit(solution)/shard_map/all_to_all | solution.py:983
  419.9 4.3 all-to-all-start.6
  433.7 6.1 %collective-permute-start.27 = (bf16[512,128]{1,0:T(8,128)(2,1)}, bf16[512,128]{1,0:T(8,128)(2,1)}, u32[]{:S(2)}, u32[]{:S(2)}) collective-permute-start(bf16[512,128]{1,0:T(8,128)(2,1)} %bitcast.158), channel_id=1, source_target_pairs={{0,6},{1,7},{2,12},{3,13},{4,18},{5,19},{6,24},{7,25},{8,4},{9,5},... | collective-permute-start | bytes 393224 | tf_op jit(solution)/shard_map/ppermute | solution.py:944
  443.7 5.8 %collective-permute-done.27.refs_3_ = bf16[512,128]{1,0:T(8,128)(2,1)} collective-permute-done((bf16[512,128]{1,0:T(8,128)(2,1)}, bf16[512,128]{1,0:T(8,128)(2,1)}, u32[]{:S(2)}, u32[]{:S(2)}) %collective-permute-start.27) | collective-permute-done | bytes 131104 | tf_op jit(solution)/shard_map/ppermute | solution.py:944
  457.4 5.9 %assemble.1 = (f32[4,16,128,128]{3,2,1,0:T(8,128)}, f32[4,16,128,128]{3,2,1,0:T(8,128)}) custom-call(s32[3]{0:T(128)} %pad_add_fusion.1.refs_0_, bf16[128,128]{1,0:T(8,128)(2,1)} %fusion.refs_1_, bf16[4,1,2,2,128,128]{5,4,3,2,1,0:T(8,128)(2,1)} %bitcast.111, bf16[4,1,2,2,128,128]{5,4,3,2,1,0:T(8,128)(2,1)} %bitcast.120, ...), custom_call_target="tpu_custom_call" | custom-call | bytes 12582912 | tf_op jit(solution)/shard_map/assemble/pallas_call | solution.py:887
  (137 shorter events, 99.0 us)
Async XLA Ops:
  8.0 29.8 %all-to-all-start = ((bf16[4,2128,128]{2,1,0:T(8,128)(2,1)}), bf16[4,2128,128]{2,1,0:T(8,128)(2,1)}, u32[]{:S(2)}, u32[]{:S(2)}) async-start(bf16[4,2128,128]{2,1,0:T(8,128)(2,1)} %pieces.1), calls=%async_computation | async-start | bytes 4358144 | tf_op jit(solution)/shard_map/all_to_all | solution.py:986
  92.6 14.3 %collective-permute-start = (bf16[4,1024,128]{2,1,0:T(8,128)(2,1)}, bf16[4,1024,128]{2,1,0:T(8,128)(2,1)}, u32[]{:S(2)}, u32[]{:S(2)}) collective-permute-start(bf16[4,1024,128]{2,1,0:T(8,128)(2,1)} %get-tuple-element.159.refs_0_), channel_id=1, source_target_pairs={{0,8},{1,17},{2,10},{3,19},{4,12},{5,21},{6,14},{7,23},{8,0},{9,25... | collective-permute-start | bytes 3145736 | tf_op jit(solution)/shard_map/ppermute | solution.py:944
  92.9 52.2 %all-to-all-start.2 = ((bf16[4,2048,128]{2,1,0:T(8,128)(2,1)}), bf16[4,2048,128]{2,1,0:T(8,128)(2,1)}, u32[]{:S(2)}, u32[]{:S(2)}) async-start(bf16[4,2048,128]{2,1,0:T(8,128)(2,1)} %pick.2), calls=%async_computation.2 | async-start | bytes 4194304 | tf_op jit(solution)/shard_map/all_to_all | solution.py:983
  111.9 33.2 %collective-permute-start.2 = (bf16[8,1024,128]{2,1,0:T(8,128)(2,1)}, bf16[8,1024,128]{2,1,0:T(8,128)(2,1)S(1)}, u32[]{:S(2)}, u32[]{:S(2)}) collective-permute-start(bf16[8,1024,128]{2,1,0:T(8,128)(2,1)} %join.3), channel_id=1, source_target_pairs={{0,1},{1,0},{2,3},{3,2},{4,5},{5,4},{6,7},{7,6},{8,9},{9,8},{10,11... | collective-permute-start | bytes 6291464 | tf_op jit(solution)/shard_map/ppermute | solution.py:944
  114.6 36.7 %collective-permute-start.1 = (bf16[8,1024,128]{2,1,0:T(8,128)(2,1)}, bf16[8,1024,128]{2,1,0:T(8,128)(2,1)}, u32[]{:S(2)}, u32[]{:S(2)}) collective-permute-start(bf16[8,1024,128]{2,1,0:T(8,128)(2,1)} %join.3), channel_id=1, source_target_pairs={{0,16},{1,9},{2,18},{3,11},{4,20},{5,13},{6,22},{7,15},{8,24},{9,1... | collective-permute-start | bytes 6291464 | tf_op jit(solution)/shard_map/ppermute | solution.py:944
  114.8 24.9 %collective-permute-start.3 = (bf16[4,1024,128]{2,1,0:T(8,128)(2,1)S(1)}, bf16[4,1024,128]{2,1,0:T(8,128)(2,1)}, u32[]{:S(2)}, u32[]{:S(2)}) collective-permute-start(bf16[4,1024,128]{2,1,0:T(8,128)(2,1)S(1)} %get-tuple-element.182.refs_0_), channel_id=1, source_target_pairs={{0,8},{1,17},{2,10},{3,19},{4,12},{5,21},{6,14},{7,23},{8,0},{9,25... | collective-permute-start | bytes 3145736 | tf_op jit(solution)/shard_map/ppermute | solution.py:944
  160.1 22.2 %collective-permute-start.6 = (bf16[8,1024,128]{2,1,0:T(8,128)(2,1)}, bf16[8,1024,128]{2,1,0:T(8,128)(2,1)}, u32[]{:S(2)}, u32[]{:S(2)}) collective-permute-start(bf16[8,1024,128]{2,1,0:T(8,128)(2,1)} %join.4), channel_id=1, source_target_pairs={{0,1},{1,0},{2,3},{3,2},{4,5},{5,4},{6,7},{7,6},{8,9},{9,8},{10,11... | collective-permute-start | bytes 6291464 | tf_op jit(solution)/shard_map/ppermute | solution.py:944
  160.5 25.5 %collective-permute-start.5 = (bf16[8,1024,128]{2,1,0:T(8,128)(2,1)}, bf16[8,1024,128]{2,1,0:T(8,128)(2,1)}, u32[]{:S(2)}, u32[]{:S(2)}) collective-permute-start(bf16[8,1024,128]{2,1,0:T(8,128)(2,1)} %join.4), channel_id=1, source_target_pairs={{0,16},{1,9},{2,18},{3,11},{4,20},{5,13},{6,22},{7,15},{8,24},{9,1... | collective-permute-start | bytes 6291464 | tf_op jit(solution)/shard_map/ppermute | solution.py:944
  162.2 54.4 %all-to-all-start.3 = ((bf16[4,2048,128]{2,1,0:T(8,128)(2,1)}), bf16[4,2048,128]{2,1,0:T(8,128)(2,1)S(1)}, u32[]{:S(2)}, u32[]{:S(2)}) async-start(bf16[4,2048,128]{2,1,0:T(8,128)(2,1)} %pick.3), calls=%async_computation.3 | async-start | bytes 4194304 | tf_op jit(solution)/shard_map/all_to_all | solution.py:983
  186.0 16.8 %collective-permute-start.7 = (bf16[8,1024,128]{2,1,0:T(8,128)(2,1)}, bf16[8,1024,128]{2,1,0:T(8,128)(2,1)}, u32[]{:S(2)}, u32[]{:S(2)}) collective-permute-start(bf16[8,1024,128]{2,1,0:T(8,128)(2,1)} %collective-permute-done.5), channel_id=1, source_target_pairs={{0,1},{1,0},{2,3},{3,2},{4,5},{5,4},{6,7},{7,6},{8,9},{9,8},{10,11... | collective-permute-start | bytes 6291464 | tf_op jit(solution)/shard_map/ppermute | solution.py:944
  249.6 17.7 %collective-permute-start.8 = (bf16[16,2,2,128,128]{4,3,2,1,0:T(8,128)(2,1)}, bf16[16,2,2,128,128]{4,3,2,1,0:T(8,128)(2,1)S(1)}, u32[]{:S(2)}, u32[]{:S(2)}) collective-permute-start(bf16[16,2,2,128,128]{4,3,2,1,0:T(8,128)(2,1)} %get-tuple-element.221), channel_id=1, source_target_pairs={{0,1},{1,0},{2,3},{3,2},{4,5},{5,4},{6,7},{7,6},{8,9},{9,8},{10,11... | collective-permute-start | bytes 6291464 | tf_op jit(solution)/shard_map/ppermute | solution.py:944
  268.7 29.3 %collective-permute-start.12 = (bf16[16,2,2,128,128]{4,3,2,1,0:T(8,128)(2,1)}, bf16[16,2,2,128,128]{4,3,2,1,0:T(8,128)(2,1)S(1)}, u32[]{:S(2)}, u32[]{:S(2)}) collective-permute-start(bf16[16,2,2,128,128]{4,3,2,1,0:T(8,128)(2,1)} %get-tuple-element.233), channel_id=1, source_target_pairs={{0,1},{1,0},{2,3},{3,2},{4,5},{5,4},{6,7},{7,6},{8,9},{9,8},{10,11... | collective-permute-start | bytes 6291464 | tf_op jit(solution)/shard_map/ppermute | solution.py:944
  272.5 20.2 %collective-permute-start.9 = (bf16[2048,128]{1,0:T(8,128)(2,1)}, bf16[2048,128]{1,0:T(8,128)(2,1)S(1)}, u32[]{:S(2)}, u32[]{:S(2)}) collective-permute-start(bf16[2048,128]{1,0:T(8,128)(2,1)} %bitcast.151), channel_id=1, source_target_pairs={{0,8},{1,9},{2,10},{3,11},{4,12},{5,13},{6,14},{7,15},{8,0},{9,1},... | collective-permute-start | bytes 1572872 | tf_op jit(solution)/shard_map/ppermute | solution.py:944
  273.2 19.5 %collective-permute-start.10 = (bf16[2048,128]{1,0:T(8,128)(2,1)}, bf16[2048,128]{1,0:T(8,128)(2,1)S(1)}, u32[]{:S(2)}, u32[]{:S(2)}) collective-permute-start(bf16[2048,128]{1,0:T(8,128)(2,1)} %bitcast.150), channel_id=1, source_target_pairs={{0,16},{1,17},{2,18},{3,19},{4,20},{5,21},{6,22},{7,23},{8,24},{9,... | collective-permute-start | bytes 1572872 | tf_op jit(solution)/shard_map/ppermute | solution.py:944
  274.0 24.0 %collective-permute-start.11 = (bf16[2048,128]{1,0:T(8,128)(2,1)}, bf16[2048,128]{1,0:T(8,128)(2,1)S(1)}, u32[]{:S(2)}, u32[]{:S(2)}) collective-permute-start(bf16[2048,128]{1,0:T(8,128)(2,1)} %bitcast.148), channel_id=1, source_target_pairs={{0,24},{1,25},{2,26},{3,27},{4,28},{5,29},{6,30},{7,31},{8,16},{9,... | collective-permute-start | bytes 1572872 | tf_op jit(solution)/shard_map/ppermute | solution.py:944
  298.0 28.9 %collective-permute-start.16 = (bf16[16,2,2,128,128]{4,3,2,1,0:T(8,128)(2,1)}, bf16[16,2,2,128,128]{4,3,2,1,0:T(8,128)(2,1)}, u32[]{:S(2)}, u32[]{:S(2)}) collective-permute-start(bf16[16,2,2,128,128]{4,3,2,1,0:T(8,128)(2,1)} %get-tuple-element.249), channel_id=1, source_target_pairs={{0,1},{1,0},{2,3},{3,2},{4,5},{5,4},{6,7},{7,6},{8,9},{9,8},{10,11... | collective-permute-start | bytes 6291464 | tf_op jit(solution)/shard_map/ppermute | solution.py:944
  302.7 20.2 %collective-permute-start.13 = (bf16[2048,128]{1,0:T(8,128)(2,1)}, bf16[2048,128]{1,0:T(8,128)(2,1)S(1)}, u32[]{:S(2)}, u32[]{:S(2)}) collective-permute-start(bf16[2048,128]{1,0:T(8,128)(2,1)} %bitcast.149), channel_id=1, source_target_pairs={{0,8},{1,9},{2,10},{3,11},{4,12},{5,13},{6,14},{7,15},{8,0},{9,1},... | collective-permute-start | bytes 1572872 | tf_op jit(solution)/shard_map/ppermute | solution.py:944
  303.4 20.3 %collective-permute-start.14 = (bf16[2048,128]{1,0:T(8,128)(2,1)}, bf16[2048,128]{1,0:T(8,128)(2,1)S(1)}, u32[]{:S(2)}, u32[]{:S(2)}) collective-permute-start(bf16[2048,128]{1,0:T(8,128)(2,1)} %bitcast.147), channel_id=1, source_target_pairs={{0,16},{1,17},{2,18},{3,19},{4,20},{5,21},{6,22},{7,23},{8,24},{9,... | collective-permute-start | bytes 1572872 | tf_op jit(solution)/shard_map/ppermute | solution.py:944
  304.1 22.8 %collective-permute-start.15 = (bf16[2048,128]{1,0:T(8,128)(2,1)}, bf16[2048,128]{1,0:T(8,128)(2,1)S(1)}, u32[]{:S(2)}, u32[]{:S(2)}) collective-permute-start(bf16[2048,128]{1,0:T(8,128)(2,1)} %bitcast.146), channel_id=1, source_target_pairs={{0,24},{1,25},{2,26},{3,27},{4,28},{5,29},{6,30},{7,31},{8,16},{9,... | collective-permute-start | bytes 1572872 | tf_op jit(solution)/shard_map/ppermute | solution.py:944
  327.7 51.3 %all-to-all-start.4 = ((bf16[4,2048,128]{2,1,0:T(8,128)(2,1)}), bf16[4,2048,128]{2,1,0:T(8,128)(2,1)S(1)}, u32[]{:S(2)}, u32[]{:S(2)}) async-start(bf16[4,2048,128]{2,1,0:T(8,128)(2,1)} %bitcast.114), calls=%async_computation.4 | async-start | bytes 4194304 | tf_op jit(solution)/shard_map/all_to_all | solution.py:983
  331.3 31.9 %collective-permute-start.17 = (bf16[16,2,2,128,128]{4,3,2,1,0:T(8,128)(2,1)}, bf16[16,2,2,128,128]{4,3,2,1,0:T(8,128)(2,1)}, u32[]{:S(2)}, u32[]{:S(2)}) collective-permute-start(bf16[16,2,2,128,128]{4,3,2,1,0:T(8,128)(2,1)} %get-tuple-element.251), channel_id=1, source_target_pairs={{0,1},{1,0},{2,3},{3,2},{4,5},{5,4},{6,7},{7,6},{8,9},{9,8},{10,11... | collective-permute-start | bytes 6291464 | tf_op jit(solution)/shard_map/ppermute | solution.py:944
  337.8 13.7 %collective-permute-start.18 = (bf16[2048,128]{1,0:T(8,128)(2,1)}, bf16[2048,128]{1,0:T(8,128)(2,1)S(1)}, u32[]{:S(2)}, u32[]{:S(2)}) collective-permute-start(bf16[2048,128]{1,0:T(8,128)(2,1)} %bitcast.156), channel_id=1, source_target_pairs={{0,8},{1,9},{2,10},{3,11},{4,12},{5,13},{6,14},{7,15},{8,0},{9,1},... | collective-permute-start | bytes 1572872 | tf_op jit(solution)/shard_map/ppermute | solution.py:944
  338.5 13.4 %collective-permute-start.19 = (bf16[2048,128]{1,0:T(8,128)(2,1)}, bf16[2048,128]{1,0:T(8,128)(2,1)S(1)}, u32[]{:S(2)}, u32[]{:S(2)}) collective-permute-start(bf16[2048,128]{1,0:T(8,128)(2,1)} %bitcast.154), channel_id=1, source_target_pairs={{0,16},{1,17},{2,18},{3,19},{4,20},{5,21},{6,22},{7,23},{8,24},{9,... | collective-permute-start | bytes 1572872 | tf_op jit(solution)/shard_map/ppermute | solution.py:944
  339.2 24.0 %collective-permute-start.20 = (bf16[2048,128]{1,0:T(8,128)(2,1)}, bf16[2048,128]{1,0:T(8,128)(2,1)S(1)}, u32[]{:S(2)}, u32[]{:S(2)}) collective-permute-start(bf16[2048,128]{1,0:T(8,128)(2,1)} %bitcast.152), channel_id=1, source_target_pairs={{0,24},{1,25},{2,26},{3,27},{4,28},{5,29},{6,30},{7,31},{8,16},{9,... | collective-permute-start | bytes 1572872 | tf_op jit(solution)/shard_map/ppermute | solution.py:944
  379.0 40.9 %all-to-all-start.5 = ((bf16[4,1536,128]{2,1,0:T(8,128)(2,1)}), bf16[4,1536,128]{2,1,0:T(8,128)(2,1)}, u32[]{:S(2)}, u32[]{:S(2)}) async-start(bf16[4,1536,128]{2,1,0:T(8,128)(2,1)} %bitcast.108), calls=%async_computation.5 | async-start | bytes 3145728 | tf_op jit(solution)/shard_map/all_to_all | solution.py:983
  386.7 12.3 %collective-permute-start.21 = (bf16[2048,128]{1,0:T(8,128)(2,1)}, bf16[2048,128]{1,0:T(8,128)(2,1)S(1)}, u32[]{:S(2)}, u32[]{:S(2)}) collective-permute-start(bf16[2048,128]{1,0:T(8,128)(2,1)} %bitcast.157), channel_id=1, source_target_pairs={{0,8},{1,9},{2,10},{3,11},{4,12},{5,13},{6,14},{7,15},{8,0},{9,1},... | collective-permute-start | bytes 1572872 | tf_op jit(solution)/shard_map/ppermute | solution.py:944
  387.5 12.0 %collective-permute-start.22 = (bf16[2048,128]{1,0:T(8,128)(2,1)}, bf16[2048,128]{1,0:T(8,128)(2,1)S(1)}, u32[]{:S(2)}, u32[]{:S(2)}) collective-permute-start(bf16[2048,128]{1,0:T(8,128)(2,1)} %bitcast.155), channel_id=1, source_target_pairs={{0,16},{1,17},{2,18},{3,19},{4,20},{5,21},{6,22},{7,23},{8,24},{9,... | collective-permute-start | bytes 1572872 | tf_op jit(solution)/shard_map/ppermute | solution.py:944
  388.3 22.4 %collective-permute-start.23 = (bf16[2048,128]{1,0:T(8,128)(2,1)}, bf16[2048,128]{1,0:T(8,128)(2,1)S(1)}, u32[]{:S(2)}, u32[]{:S(2)}) collective-permute-start(bf16[2048,128]{1,0:T(8,128)(2,1)} %bitcast.153), channel_id=1, source_target_pairs={{0,24},{1,25},{2,26},{3,27},{4,28},{5,29},{6,30},{7,31},{8,16},{9,... | collective-permute-start | bytes 1572872 | tf_op jit(solution)/shard_map/ppermute | solution.py:944
  419.9 29.6 %all-to-all-start.6 = ((bf16[4,1536,128]{2,1,0:T(8,128)(2,1)}), bf16[4,1536,128]{2,1,0:T(8,128)(2,1)S(1)}, u32[]{:S(2)}, u32[]{:S(2)}) async-start(bf16[4,1536,128]{2,1,0:T(8,128)(2,1)} %all-to-all-done.5), calls=%async_computation.6 | async-start | bytes 3145728 | tf_op jit(solution)/shard_map/all_to_all | solution.py:986
  426.5 17.1 %collective-permute-start.25 = (bf16[512,128]{1,0:T(8,128)(2,1)}, bf16[512,128]{1,0:T(8,128)(2,1)S(1)}, u32[]{:S(2)}, u32[]{:S(2)}) collective-permute-start(bf16[512,128]{1,0:T(8,128)(2,1)} %bitcast.161), channel_id=1, source_target_pairs={{0,2},{1,3},{2,8},{3,9},{4,22},{5,23},{6,28},{7,29},{8,0},{9,1},{1... | collective-permute-start | bytes 393224 | tf_op jit(solution)/shard_map/ppermute | solution.py:944
  428.4 15.2 %collective-permute-start.24 = (bf16[512,128]{1,0:T(8,128)(2,1)}, bf16[512,128]{1,0:T(8,128)(2,1)S(1)}, u32[]{:S(2)}, u32[]{:S(2)}) collective-permute-start(bf16[512,128]{1,0:T(8,128)(2,1)} %bitcast.160), channel_id=1, source_target_pairs={{0,0},{1,1},{2,10},{3,11},{4,20},{5,21},{6,30},{7,31},{8,2},{9,3},... | collective-permute-start | bytes 393224 | tf_op jit(solution)/shard_map/ppermute | solution.py:944
  433.7 15.8 %collective-permute-start.27 = (bf16[512,128]{1,0:T(8,128)(2,1)}, bf16[512,128]{1,0:T(8,128)(2,1)}, u32[]{:S(2)}, u32[]{:S(2)}) collective-permute-start(bf16[512,128]{1,0:T(8,128)(2,1)} %bitcast.158), channel_id=1, source_target_pairs={{0,6},{1,7},{2,12},{3,13},{4,18},{5,19},{6,24},{7,25},{8,4},{9,5},... | collective-permute-start | bytes 393224 | tf_op jit(solution)/shard_map/ppermute | solution.py:944
  (31 other events, 300.4 us)

commit v12 on v11

--- a/solution.py
+++ b/solution.py
@@ -297,10 +297,9 @@
     return pl.ds(pl.multiple_of(block * size, size), size)
 
 
-def column(gain_ref, block, slots):
-    blocks = gain_ref.shape[1]
-    picked = lax.broadcasted_iota(jnp.int32, (blocks, slots), 0) == block
-    return inner_dot(gain_ref[...], picked.astype(jnp.bfloat16), 1, 0)
+def column(gain_ref, block, at, slots):
+    gains = gain_ref[block // gain_ref.shape[2]]
+    return jnp.broadcast_to(gains[:, at : at + 1], (gains.shape[0], slots))
 
 
 def chunk_copy(source, target, sems, chunk):
@@ -342,10 +341,10 @@
 def by_chunk(blocks, step, carry, before=None, after=None):
     per_chunk = blocks // CHUNKS
 
-    def few(start, carry):
+    def few(start, first, carry):
         stores = []
         for at in range(TOGETHER):
-            made, carry = step(start + at, carry)
+            made, carry = step(start + at, first + at, carry)
             stores += made
         for ref, index, value in stores:
             ref[index] = value
@@ -355,7 +354,7 @@
         if before is not None:
             before(chunk)
         for at in range(0, per_chunk, TOGETHER):
-            carry = few(chunk * per_chunk + at, carry)
+            carry = few(chunk * per_chunk + at, at, carry)
         if after is not None:
             after(chunk)
         return carry
@@ -381,7 +380,7 @@
         for copy in left_in + right_in:
             copy.start()
 
-        def squares(block, total):
+        def squares(block, _, total):
             rows = block_rows(block, size)
             part = raw[rows, :].astype(jnp.float32)
             return [(h, (rows, slice(None)), part)], total + fold_rows(part * part)
@@ -408,10 +407,10 @@
         if not first:
             chunk_copy(sources[0], h, in_sems, chunk).wait()
 
-    def left(block, carry):
+    def left(block, nth, carry):
         rows = block_rows(block, size)
         place = table_ref[0, block]
-        normed = (h[rows, :] * scale * column(gain_ref, block, slots)).astype(jnp.bfloat16)
+        normed = (h[rows, :] * scale * column(gain_ref, block, nth, slots)).astype(jnp.bfloat16)
         weight = w[place // chunk_blocks, 0, place % chunk_blocks]
         first_out = inner_dot(weight, normed, 0, 0)
         at = (rows, slice(None))
@@ -424,7 +423,7 @@
     for copy in right_in:
         copy.wait()
 
-    def right(block, total):
+    def right(block, nth, total):
         rows = block_rows(block, size)
         place = table_ref[0, block]
         moved = [mid[pl.ds(q * blocks + block, blocks, stride=size), :] for q in range(fold)]
@@ -458,8 +457,8 @@
     slope_ref, z_ref, u_ref = sources[:3]
     parts, sources = sources[3 : 3 + PARTS], sources[3 + PARTS :]
     out_ref, own_grad, peer_grad = refs[:3]
-    g, slope, z, u, h, w, gw, mid, top, goal, end_gain = refs[3:14]
-    in_sems, w_sems, out_sems, gw_sems = refs[14:]
+    g, slope, z, u, h, w, gw, mid, top, goal = refs[3:13]
+    in_sems, w_sems, out_sems, gw_sems = refs[13:]
     features, slots = g.shape
     size = w.shape[-1]
     chunk_blocks = w.shape[2]
@@ -472,7 +471,6 @@
     if turning:
         for chunk in range(CHUNKS):
             chunk_copy(g_ref, top, in_sems.at[0], chunk).start()
-            chunk_copy(end_gain_ref, end_gain, in_sems.at[6], chunk).start()
             chunk_copy(sources[2], goal, in_sems.at[5], chunk).start()
     for copy in right_in:
         copy.start()
@@ -490,10 +488,10 @@
     if turning:
         zero = jnp.zeros((8, slots), jnp.float32)
 
-        def sums(block, totals):
+        def sums(block, nth, totals):
             rows = block_rows(block, size)
             part = top[rows, :]
-            scaled = part * end_gain[rows, :].astype(jnp.float32)
+            scaled = part * column(end_gain_ref, block, nth, slots)
             return [], (
                 totals[0] + fold_rows(part * part),
                 totals[1] + fold_rows(scaled * scaled),
@@ -502,7 +500,6 @@
 
         def arrive_top(chunk):
             chunk_copy(g_ref, top, in_sems.at[0], chunk).wait()
-            chunk_copy(end_gain_ref, end_gain, in_sems.at[6], chunk).wait()
             chunk_copy(sources[2], goal, in_sems.at[5], chunk).wait()
 
         totals = by_chunk(blocks, sums, (zero, zero, zero), arrive_top)
@@ -519,14 +516,14 @@
         chunk_copy(slope_ref, slope, in_sems.at[1], chunk).wait()
         chunk_copy(z_ref, z, in_sems.at[2], chunk).wait()
 
-    def right(block, total):
+    def right(block, nth, total):
         rows = block_rows(block, size)
         place, home = table_ref[0, block], table_ref[2 if last else 1, block]
         at = (place // chunk_blocks, 1, place % chunk_blocks)
         to = (home // chunk_blocks, 1, home % chunk_blocks)
         if turning:
             part = top[rows, :]
-            factor = end_gain[rows, :].astype(jnp.float32)
+            factor = column(end_gain_ref, block, nth, slots)
             error = (part * end_scale * factor - goal[rows, :].astype(jnp.float32)) * factor
             gradient = end_scale * error - part * end_back
             stores = [(g, (rows, slice(None)), gradient)]
@@ -553,7 +550,7 @@
         chunk_copy(u_ref, u, in_sems.at[3], chunk).wait()
         chunk_copy(h_ref, h, in_sems.at[4], chunk).wait()
 
-    def left(block, carry):
+    def left(block, nth, carry):
         rows = block_rows(block, size)
         place, home = table_ref[0, block], table_ref[2 if last else 1, block]
         at = (place // chunk_blocks, 0, place % chunk_blocks)
@@ -561,7 +558,7 @@
         arrived = [mid[pl.ds(q * blocks + block, blocks, stride=size), :] for q in range(fold)]
         arrived = jnp.concatenate(arrived, axis=0).astype(jnp.bfloat16)
         factor_grad = inner_dot(u[rows, :], arrived, 1, 1).astype(jnp.bfloat16)
-        weighted = inner_dot(w[at], arrived, 1, 0) * column(gain_ref, block, slots)
+        weighted = inner_dot(w[at], arrived, 1, 0) * column(gain_ref, block, nth, slots)
         ended = g[rows, :] + scale * weighted - h[rows, :].astype(jnp.float32) * back
         index = (rows, slice(None))
         stores = [(gw, to, factor_grad)]
@@ -635,7 +632,7 @@
     out_shape = [shape_of(whole, jnp.bfloat16 if last else jnp.float32)] + [shape_of(half, jnp.bfloat16)] * 2
     return pl.pallas_call(
         lambda *refs: backward_kernel(turning, last, layer, len(sources), *refs),
-        in_specs=[SMEM, INSIDE, INSIDE] + [OUTSIDE] * (1 + len(sources)),
+        in_specs=[SMEM] + [INSIDE] * 3 + [OUTSIDE] * len(sources),
         out_specs=[OUTSIDE] * len(out_shape),
         out_shape=out_shape,
         scratch_shapes=[
@@ -649,8 +646,7 @@
             pltpu.VMEM(whole, jnp.float32),
             pltpu.VMEM(whole if turning else SMALL, jnp.float32),
             pltpu.VMEM(whole if turning else SMALL, jnp.bfloat16),
-            pltpu.VMEM(whole if turning else SMALL, jnp.bfloat16),
-            pltpu.SemaphoreType.DMA((7, CHUNKS)),
+            pltpu.SemaphoreType.DMA((6, CHUNKS)),
             pltpu.SemaphoreType.DMA((2, PARTS)),
             pltpu.SemaphoreType.DMA((CHUNKS,)),
             pltpu.SemaphoreType.DMA((2, PARTS)),
@@ -1003,18 +999,19 @@
     lowest = [lifted[:, group[0] * layer_rows : (group[-1] + 1) * layer_rows] for group in groups]
     beside = move(lowest[0], routes["across"][0])
     gains = lifted[:, layer_count * layer_rows :].reshape(width, layer_count + 1, local_blocks, size)
-    gains = gains.transpose(1, 3, 0, 2).reshape(layer_count + 1, size, blocks)
-    end_column = jnp.broadcast_to(gains[layer_count].T[:, :, None], (blocks, size, wide)).reshape(-1, wide)
-    lowest, beside, end_column = tie((lowest, beside, end_column))
+    gains = gains.transpose(1, 3, 0, 2).reshape(layer_count + 1, size, CHUNKS, blocks // CHUNKS)
+    gains = gains.transpose(0, 2, 1, 3).astype(jnp.float32)
+    later = (lowest[1], move(lowest[1], routes["across"][0]))
+    lowest[0], beside, later, gains = tie((lowest[0], beside, later, gains))
     first_two = gather_two(joined([lowest[0], beside]))
-    later = (lowest[1], move(lowest[1], routes["across"][0]))
+    later = joined(list(later))
     first_two, later, patch_came = tie((first_two, later, patch_came))
     weights = [as_weights(gather_three(*first_two))]
     weights, later = tie((weights, later))
 
     residual, target_sent = tie((patch_came, target_sent))
     target = to_planes(target_sent).reshape(-1, wide)
-    flying = gather_two(joined(list(later)))
+    flying = gather_two(later)
     sums = jnp.zeros((8, wide), jnp.float32)
     stored = []
     for layer in range(layer_count):
@@ -1058,7 +1055,7 @@
         gradient, mine, other = run_backward(
             table,
             gains[layer],
-            end_column,
+            gains[layer_count],
             scale,
             kept,
             weights[group],

time: 466 us -> 461 us (0.989)
  waiting for transfers between devices: 148 us -> 142 us
    ppermute x30, waiting for transfers between devices: 106 us -> 85.5 us  [move(): return lax.ppermute(value, AXES, route)]
    all_to_all x4, waiting for transfers between devices: 25.3 us -> 40.7 us  [to_planes(): lax.all_to_all(value, 'tensor', split_axis=0, concat_axis=0, tiled=True)]
  transfers between devices with their start and end apart: 36 -> 36, of which waited for: 19 -> 18; matrix products, arithmetic and copies ran while one was open for 2% -> 1% of each run, Pallas kernels for 28% -> 30%
where the time goes in v12:
time: 461 us; the launch traced here: 459 us
  Pallas kernels  181 us (39%)
  waiting for transfers between devices  142 us (31%)
  starting transfers between devices  63.7 us (14%)
  blocking collectives  53.8 us (12%)
  local copies, waits for them, and re-layouts  14.9 us (3%)
    ppermute x30, waiting for transfers between devices, move(): return lax.ppermute(value, AXES, route)  85.5 us
    pallas_call x4, Pallas kernels, run_backward(): pl.pallas_call(lambda *refs: backward_kernel(turning, last, layer, len(so...  72.9 us
    pallas_call x4, Pallas kernels, run_forward(): pl.pallas_call(lambda *refs: forward_kernel(first, layer, len(sources), *...  58.4 us
    all_to_all x1, blocking collectives, to_planes(): lax.all_to_all(value, 'tensor', split_axis=0, concat_axis=0, tiled=True)  53.8 us
    all_to_all x4, waiting for transfers between devices, to_planes(): lax.all_to_all(value, 'tensor', split_axis=0, concat_axis=0, tiled=True)  40.7 us
    ppermute x30, starting transfers between devices, move(): return lax.ppermute(value, AXES, route)  38.3 us
    pallas_call x6, Pallas kernels, run_sum(): pl.pallas_call(lambda *refs: sum_kernel(len(groups[0]), len(flat), *refs)...  19.6 us
    all_to_all x4, starting transfers between devices, to_planes(): lax.all_to_all(value, 'tensor', split_axis=0, concat_axis=0, tiled=True)  17.1 us
  transfers between devices with their start and end apart: 36, of which 18 were waited for; matrix products, arithmetic and copies ran while one was open for 1% of the time, Pallas kernels for 30%

profile of v12, /device:TPU:5, one launch (start us, length us, event | category | flops | bytes accessed | tf_op | source)
XLA Modules:
  0.0 459.1 jit_solution(4624398295552217728)
XLA Ops:
  3.3 4.6 %pieces.1 = bf16[4,2128,128]{2,1,0:T(8,128)(2,1)} custom-call(s32[3]{0:T(128)} %pad_add_fusion.1.refs_0_, bf16[128,128]{1,0:T(8,128)(2,1)} %fusion.refs_1_, bf16[4,16,128,128]{3,2,1,0:T(8,128)(2,1)} %bitcast.108, bf16[4,16,128,128]{3,2,1,0:T(8,128)(2,1)} %bitcast.109, bf16[80,128]{1,0:T(8,128)(2,1)} %reshape_squeeze.3.refs_4_), custom_call_target="tpu_custom_call" | custom-call | flops 134217728 | bytes 4194304 | tf_op jit(solution)/shard_map/pieces/pallas_call | solution.py:762
  8.0 4.5 all-to-all-start
  13.2 4.1 pick.2
  17.3 4.2 pick.3
  21.5 16.2 %all-to-all-done = bf16[4,2128,128]{2,1,0:T(8,128)(2,1)} async-done(((bf16[4,2128,128]{2,1,0:T(8,128)(2,1)}), bf16[4,2128,128]{2,1,0:T(8,128)(2,1)}, u32[]{:S(2)}, u32[]{:S(2)}) %all-to-all-start) | async-done | bytes 2179104 | tf_op jit(solution)/shard_map/all_to_all | solution.py:982
  37.7 53.8 %all_to_all.35 = bf16[4,2128,128]{2,1,0:T(8,128)(2,1)S(1)} all-to-all(bf16[4,2128,128]{2,1,0:T(8,128)(2,1)} %all-to-all-done), channel_id=1, replica_groups=mesh['section'=4,'tensor'=4,'dp'=2] {'tensor'}, dimensions={0} | all-to-all | bytes 4358144 | tf_op jit(solution)/shard_map/all_to_all | solution.py:979
  94.4 4.5 all-to-all-start.2
  99.7 7.5 %collective-permute-done.1.refs_1_ = bf16[4,1024,128]{2,1,0:T(8,128)(2,1)} collective-permute-done((bf16[4,1024,128]{2,1,0:T(8,128)(2,1)}, bf16[4,1024,128]{2,1,0:T(8,128)(2,1)}, u32[]{:S(2)}, u32[]{:S(2)}) %collective-permute-start.1) | collective-permute-done | bytes 1048608 | tf_op jit(solution)/shard_map/ppermute | solution.py:940
  107.2 11.2 %collective-permute-done.refs_1_ = bf16[4,1024,128]{2,1,0:T(8,128)(2,1)} collective-permute-done((bf16[4,1024,128]{2,1,0:T(8,128)(2,1)}, bf16[4,1024,128]{2,1,0:T(8,128)(2,1)}, u32[]{:S(2)}, u32[]{:S(2)}) %collective-permute-start) | collective-permute-done | bytes 1048608 | tf_op jit(solution)/shard_map/ppermute | solution.py:940
  127.2 19.5 %all-to-all-done.2 = bf16[4,2048,128]{2,1,0:T(8,128)(2,1)} async-done(((bf16[4,2048,128]{2,1,0:T(8,128)(2,1)}), bf16[4,2048,128]{2,1,0:T(8,128)(2,1)}, u32[]{:S(2)}, u32[]{:S(2)}) %all-to-all-start.2) | async-done | bytes 2097184 | tf_op jit(solution)/shard_map/all_to_all | solution.py:979
  150.4 4.1 collective-permute-done.4
  156.7 4.7 %all-to-all-start.3 = ((bf16[4,2048,128]{2,1,0:T(8,128)(2,1)}), bf16[4,2048,128]{2,1,0:T(8,128)(2,1)}, u32[]{:S(2)}, u32[]{:S(2)}) async-start(bf16[4,2048,128]{2,1,0:T(8,128)(2,1)} %pick.3), calls=%async_computation.3 | async-start | bytes 4194304 | tf_op jit(solution)/shard_map/all_to_all | solution.py:979
  163.5 15.1 %forward_layer.4 = (f32[8192,128]{1,0:T(8,128)}, bf16[8192,128]{1,0:T(8,128)(2,1)}, bf16[8192,128]{1,0:T(8,128)(2,1)}, bf16[8192,128]{1,0:T(8,128)(2,1)}, f32[8,128]{1,0:T(8,128)}, /*index=5*/f32[8,128]{1,0:T(8,128)}) custom-call(s32[3,64]{1,0:T(4,128)} %pad_add_fusion.refs_0_, f32[8,128]{1,0:T(8,128)} %broadcast_in_dim.6.refs_1_, ...), custom_call_target="tpu_custom_call" | custom-call | flops 4000000000 | bytes 20971520 | tf_op jit(solution)/shard_map/forward_layer/pallas_call | solution.py:602
  181.4 14.4 %forward_layer.5 = (f32[8192,128]{1,0:T(8,128)}, bf16[8192,128]{1,0:T(8,128)(2,1)}, bf16[8192,128]{1,0:T(8,128)(2,1)}, bf16[8192,128]{1,0:T(8,128)(2,1)}, f32[8,128]{1,0:T(8,128)}, /*index=5*/f32[8,128]{1,0:T(8,128)}) custom-call(s32[3,64]{1,0:T(4,128)} %pad_add_fusion.refs_0_, f32[8,128]{1,0:T(8,128)} %get-tuple-element.182.refs_1_, ...), custom_call_target="tpu_custom_call" | custom-call | flops 4000000000 | bytes 20971520 | tf_op jit(solution)/shard_map/forward_layer/pallas_call | solution.py:602
  197.2 14.4 %forward_layer.6 = (f32[8192,128]{1,0:T(8,128)}, bf16[8192,128]{1,0:T(8,128)(2,1)}, bf16[8192,128]{1,0:T(8,128)(2,1)}, bf16[8192,128]{1,0:T(8,128)(2,1)}, f32[8,128]{1,0:T(8,128)}, /*index=5*/f32[8,128]{1,0:T(8,128)}) custom-call(s32[3,64]{1,0:T(4,128)} %pad_add_fusion.refs_0_, f32[8,128]{1,0:T(8,128)} %get-tuple-element.193.refs_1_, ...), custom_call_target="tpu_custom_call" | custom-call | flops 4000000000 | bytes 20971520 | tf_op jit(solution)/shard_map/forward_layer/pallas_call | solution.py:602
  211.7 14.5 %forward_layer.7 = (f32[8192,128]{1,0:T(8,128)}, bf16[8192,128]{1,0:T(8,128)(2,1)}, bf16[8192,128]{1,0:T(8,128)(2,1)}, bf16[8192,128]{1,0:T(8,128)(2,1)}, f32[8,128]{1,0:T(8,128)}, /*index=5*/f32[8,128]{1,0:T(8,128)}) custom-call(s32[3,64]{1,0:T(4,128)} %pad_add_fusion.refs_0_, f32[8,128]{1,0:T(8,128)} %get-tuple-element.206.refs_1_, ...), custom_call_target="tpu_custom_call" | custom-call | flops 4000000000 | bytes 20971520 | tf_op jit(solution)/shard_map/forward_layer/pallas_call | solution.py:602
  226.2 19.6 %backward_layer.4 = (f32[8192,128]{1,0:T(8,128)}, bf16[16,2,2,128,128]{4,3,2,1,0:T(8,128)(2,1)}, bf16[16,2,2,128,128]{4,3,2,1,0:T(8,128)(2,1)}) custom-call(s32[3,64]{1,0:T(4,128)} %pad_add_fusion.refs_0_, f32[8,128]{1,0:T(8,128)} %get-tuple-element.208.refs_1_, f32[8,128,8]{2,1,0:T(8,128)} %get-tuple-element.301.refs_2_, ...), custom_call_target="tpu_custom_call" | custom-call | flops 5000000000 | bytes 31457280 | tf_op jit(solution)/shard_map/backward_layer/pallas_call | solution.py:633
  245.8 17.7 %backward_layer.5 = (f32[8192,128]{1,0:T(8,128)}, bf16[16,2,2,128,128]{4,3,2,1,0:T(8,128)(2,1)}, bf16[16,2,2,128,128]{4,3,2,1,0:T(8,128)(2,1)}) custom-call(s32[3,64]{1,0:T(4,128)} %pad_add_fusion.refs_0_, f32[8,128]{1,0:T(8,128)} %get-tuple-element.199.refs_1_, f32[8,128,8]{2,1,0:T(8,128)} %get-tuple-element.302.refs_2_, ...), custom_call_target="tpu_custom_call" | custom-call | flops 5000000000 | bytes 31457280 | tf_op jit(solution)/shard_map/backward_layer/pallas_call | solution.py:633
  271.3 17.8 %backward_layer.6 = (f32[8192,128]{1,0:T(8,128)}, bf16[16,2,2,128,128]{4,3,2,1,0:T(8,128)(2,1)}, bf16[16,2,2,128,128]{4,3,2,1,0:T(8,128)(2,1)}) custom-call(s32[3,64]{1,0:T(4,128)} %pad_add_fusion.refs_0_, f32[8,128]{1,0:T(8,128)} %get-tuple-element.184.refs_1_, f32[8,128,8]{2,1,0:T(8,128)} %get-tuple-element.303.refs_2_, ...), custom_call_target="tpu_custom_call" | custom-call | flops 5000000000 | bytes 31457280 | tf_op jit(solution)/shard_map/backward_layer/pallas_call | solution.py:633
  289.1 4.5 collective-permute-done.11
  301.0 17.8 %backward_layer.7 = (bf16[8192,128]{1,0:T(8,128)(2,1)}, bf16[16,2,2,128,128]{4,3,2,1,0:T(8,128)(2,1)}, bf16[16,2,2,128,128]{4,3,2,1,0:T(8,128)(2,1)}) custom-call(s32[3,64]{1,0:T(4,128)} %pad_add_fusion.refs_0_, f32[8,128]{1,0:T(8,128)} %get-tuple-element.175.refs_1_, f32[8,128,8]{2,1,0:T(8,128)} %get-tuple-element.305.refs_2_, ...), custom_call_target="tpu_custom_call" | custom-call | flops 5000000000 | bytes 31457280 | tf_op jit(solution)/shard_map/backward_layer/pallas_call | solution.py:633
  336.4 11.1 %collective-permute-done.18 = bf16[2048,128]{1,0:T(8,128)(2,1)S(1)} collective-permute-done((bf16[2048,128]{1,0:T(8,128)(2,1)}, bf16[2048,128]{1,0:T(8,128)(2,1)S(1)}, u32[]{:S(2)}, u32[]{:S(2)}) %collective-permute-start.18) | collective-permute-done | bytes 524320 | tf_op jit(solution)/shard_map/ppermute | solution.py:940
  347.6 11.3 %collective-permute-done.20 = bf16[2048,128]{1,0:T(8,128)(2,1)S(1)} collective-permute-done((bf16[2048,128]{1,0:T(8,128)(2,1)}, bf16[2048,128]{1,0:T(8,128)(2,1)S(1)}, u32[]{:S(2)}, u32[]{:S(2)}) %collective-permute-start.20) | collective-permute-done | bytes 524320 | tf_op jit(solution)/shard_map/ppermute | solution.py:940
  359.7 4.1 sum.10
  363.8 11.4 %all-to-all-done.4.came_ref = bf16[4,2048,128]{2,1,0:T(8,128)(2,1)S(1)} async-done(((bf16[4,2048,128]{2,1,0:T(8,128)(2,1)}), bf16[4,2048,128]{2,1,0:T(8,128)(2,1)S(1)}, u32[]{:S(2)}, u32[]{:S(2)}) %all-to-all-start.4) | async-done | bytes 2097184 | tf_op jit(solution)/shard_map/all_to_all | solution.py:979
  375.2 4.4 all-to-all-start.5
  385.6 9.6 %collective-permute-done.21 = bf16[2048,128]{1,0:T(8,128)(2,1)S(1)} collective-permute-done((bf16[2048,128]{1,0:T(8,128)(2,1)}, bf16[2048,128]{1,0:T(8,128)(2,1)S(1)}, u32[]{:S(2)}, u32[]{:S(2)}) %collective-permute-start.21) | collective-permute-done | bytes 524320 | tf_op jit(solution)/shard_map/ppermute | solution.py:940
  395.2 11.1 %collective-permute-done.23 = bf16[2048,128]{1,0:T(8,128)(2,1)S(1)} collective-permute-done((bf16[2048,128]{1,0:T(8,128)(2,1)}, bf16[2048,128]{1,0:T(8,128)(2,1)S(1)}, u32[]{:S(2)}, u32[]{:S(2)}) %collective-permute-start.23) | collective-permute-done | bytes 524320 | tf_op jit(solution)/shard_map/ppermute | solution.py:940
  406.3 9.7 %all-to-all-done.5 = bf16[4,1536,128]{2,1,0:T(8,128)(2,1)} async-done(((bf16[4,1536,128]{2,1,0:T(8,128)(2,1)}), bf16[4,1536,128]{2,1,0:T(8,128)(2,1)}, u32[]{:S(2)}, u32[]{:S(2)}) %all-to-all-start.5) | async-done | bytes 1572896 | tf_op jit(solution)/shard_map/all_to_all | solution.py:979
  429.4 6.1 %collective-permute-start.27 = (bf16[512,128]{1,0:T(8,128)(2,1)}, bf16[512,128]{1,0:T(8,128)(2,1)}, u32[]{:S(2)}, u32[]{:S(2)}) collective-permute-start(bf16[512,128]{1,0:T(8,128)(2,1)} %bitcast.152), channel_id=1, source_target_pairs={{0,6},{1,7},{2,12},{3,13},{4,18},{5,19},{6,24},{7,25},{8,4},{9,5},... | collective-permute-start | bytes 393224 | tf_op jit(solution)/shard_map/ppermute | solution.py:940
  439.3 5.8 %collective-permute-done.27.refs_3_ = bf16[512,128]{1,0:T(8,128)(2,1)} collective-permute-done((bf16[512,128]{1,0:T(8,128)(2,1)}, bf16[512,128]{1,0:T(8,128)(2,1)}, u32[]{:S(2)}, u32[]{:S(2)}) %collective-permute-start.27) | collective-permute-done | bytes 131104 | tf_op jit(solution)/shard_map/ppermute | solution.py:940
  453.1 5.9 %assemble.1 = (f32[4,16,128,128]{3,2,1,0:T(8,128)}, f32[4,16,128,128]{3,2,1,0:T(8,128)}) custom-call(s32[3]{0:T(128)} %pad_add_fusion.1.refs_0_, bf16[128,128]{1,0:T(8,128)(2,1)} %fusion.refs_1_, bf16[4,1,2,2,128,128]{5,4,3,2,1,0:T(8,128)(2,1)} %bitcast.110, bf16[4,1,2,2,128,128]{5,4,3,2,1,0:T(8,128)(2,1)} %bitcast.120, ...), custom_call_target="tpu_custom_call" | custom-call | bytes 12582912 | tf_op jit(solution)/shard_map/assemble/pallas_call | solution.py:883
  (127 shorter events, 92.7 us)
Async XLA Ops:
  8.0 29.8 %all-to-all-start = ((bf16[4,2128,128]{2,1,0:T(8,128)(2,1)}), bf16[4,2128,128]{2,1,0:T(8,128)(2,1)}, u32[]{:S(2)}, u32[]{:S(2)}) async-start(bf16[4,2128,128]{2,1,0:T(8,128)(2,1)} %pieces.1), calls=%async_computation | async-start | bytes 4358144 | tf_op jit(solution)/shard_map/all_to_all | solution.py:982
  93.0 14.3 %collective-permute-start.1 = (bf16[4,1024,128]{2,1,0:T(8,128)(2,1)}, bf16[4,1024,128]{2,1,0:T(8,128)(2,1)}, u32[]{:S(2)}, u32[]{:S(2)}) collective-permute-start(bf16[4,1024,128]{2,1,0:T(8,128)(2,1)} %get-tuple-element.161.refs_0_), channel_id=1, source_target_pairs={{0,8},{1,17},{2,10},{3,19},{4,12},{5,21},{6,14},{7,23},{8,0},{9,25... | collective-permute-start | bytes 3145736 | tf_op jit(solution)/shard_map/ppermute | solution.py:940
  93.3 25.2 %collective-permute-start = (bf16[4,1024,128]{2,1,0:T(8,128)(2,1)}, bf16[4,1024,128]{2,1,0:T(8,128)(2,1)}, u32[]{:S(2)}, u32[]{:S(2)}) collective-permute-start(bf16[4,1024,128]{2,1,0:T(8,128)(2,1)} %get-tuple-element.159.refs_0_), channel_id=1, source_target_pairs={{0,8},{1,17},{2,10},{3,19},{4,12},{5,21},{6,14},{7,23},{8,0},{9,25... | collective-permute-start | bytes 3145736 | tf_op jit(solution)/shard_map/ppermute | solution.py:940
  94.4 52.2 %all-to-all-start.2 = ((bf16[4,2048,128]{2,1,0:T(8,128)(2,1)}), bf16[4,2048,128]{2,1,0:T(8,128)(2,1)}, u32[]{:S(2)}, u32[]{:S(2)}) async-start(bf16[4,2048,128]{2,1,0:T(8,128)(2,1)} %pick.2), calls=%async_computation.2 | async-start | bytes 4194304 | tf_op jit(solution)/shard_map/all_to_all | solution.py:979
  121.4 25.3 %collective-permute-start.3 = (bf16[8,1024,128]{2,1,0:T(8,128)(2,1)}, bf16[8,1024,128]{2,1,0:T(8,128)(2,1)}, u32[]{:S(2)}, u32[]{:S(2)}) collective-permute-start(bf16[8,1024,128]{2,1,0:T(8,128)(2,1)} %join.3), channel_id=1, source_target_pairs={{0,1},{1,0},{2,3},{3,2},{4,5},{5,4},{6,7},{7,6},{8,9},{9,8},{10,11... | collective-permute-start | bytes 6291464 | tf_op jit(solution)/shard_map/ppermute | solution.py:940
  124.0 25.5 %collective-permute-start.2 = (bf16[8,1024,128]{2,1,0:T(8,128)(2,1)}, bf16[8,1024,128]{2,1,0:T(8,128)(2,1)}, u32[]{:S(2)}, u32[]{:S(2)}) collective-permute-start(bf16[8,1024,128]{2,1,0:T(8,128)(2,1)} %join.3), channel_id=1, source_target_pairs={{0,16},{1,9},{2,18},{3,11},{4,20},{5,13},{6,22},{7,15},{8,24},{9,1... | collective-permute-start | bytes 6291464 | tf_op jit(solution)/shard_map/ppermute | solution.py:940
  154.6 24.1 %collective-permute-start.6 = (bf16[8,1024,128]{2,1,0:T(8,128)(2,1)}, bf16[8,1024,128]{2,1,0:T(8,128)(2,1)}, u32[]{:S(2)}, u32[]{:S(2)}) collective-permute-start(bf16[8,1024,128]{2,1,0:T(8,128)(2,1)} %join.4), channel_id=1, source_target_pairs={{0,1},{1,0},{2,3},{3,2},{4,5},{5,4},{6,7},{7,6},{8,9},{9,8},{10,11... | collective-permute-start | bytes 6291464 | tf_op jit(solution)/shard_map/ppermute | solution.py:940
  154.9 25.5 %collective-permute-start.5 = (bf16[8,1024,128]{2,1,0:T(8,128)(2,1)}, bf16[8,1024,128]{2,1,0:T(8,128)(2,1)}, u32[]{:S(2)}, u32[]{:S(2)}) collective-permute-start(bf16[8,1024,128]{2,1,0:T(8,128)(2,1)} %join.4), channel_id=1, source_target_pairs={{0,16},{1,9},{2,18},{3,11},{4,20},{5,13},{6,22},{7,15},{8,24},{9,1... | collective-permute-start | bytes 6291464 | tf_op jit(solution)/shard_map/ppermute | solution.py:940
  156.7 54.9 %all-to-all-start.3 = ((bf16[4,2048,128]{2,1,0:T(8,128)(2,1)}), bf16[4,2048,128]{2,1,0:T(8,128)(2,1)}, u32[]{:S(2)}, u32[]{:S(2)}) async-start(bf16[4,2048,128]{2,1,0:T(8,128)(2,1)} %pick.3), calls=%async_computation.3 | async-start | bytes 4194304 | tf_op jit(solution)/shard_map/all_to_all | solution.py:979
  180.4 15.4 %collective-permute-start.7 = (bf16[8,1024,128]{2,1,0:T(8,128)(2,1)}, bf16[8,1024,128]{2,1,0:T(8,128)(2,1)S(1)}, u32[]{:S(2)}, u32[]{:S(2)}) collective-permute-start(bf16[8,1024,128]{2,1,0:T(8,128)(2,1)} %collective-permute-done.5), channel_id=1, source_target_pairs={{0,1},{1,0},{2,3},{3,2},{4,5},{5,4},{6,7},{7,6},{8,9},{9,8},{10,11... | collective-permute-start | bytes 6291464 | tf_op jit(solution)/shard_map/ppermute | solution.py:940
  245.8 17.8 %collective-permute-start.8 = (bf16[16,2,2,128,128]{4,3,2,1,0:T(8,128)(2,1)}, bf16[16,2,2,128,128]{4,3,2,1,0:T(8,128)(2,1)S(1)}, u32[]{:S(2)}, u32[]{:S(2)}) collective-permute-start(bf16[16,2,2,128,128]{4,3,2,1,0:T(8,128)(2,1)} %get-tuple-element.219), channel_id=1, source_target_pairs={{0,1},{1,0},{2,3},{3,2},{4,5},{5,4},{6,7},{7,6},{8,9},{9,8},{10,11... | collective-permute-start | bytes 6291464 | tf_op jit(solution)/shard_map/ppermute | solution.py:940
  264.9 28.8 %collective-permute-start.12 = (bf16[16,2,2,128,128]{4,3,2,1,0:T(8,128)(2,1)}, bf16[16,2,2,128,128]{4,3,2,1,0:T(8,128)(2,1)S(1)}, u32[]{:S(2)}, u32[]{:S(2)}) collective-permute-start(bf16[16,2,2,128,128]{4,3,2,1,0:T(8,128)(2,1)} %get-tuple-element.231), channel_id=1, source_target_pairs={{0,1},{1,0},{2,3},{3,2},{4,5},{5,4},{6,7},{7,6},{8,9},{9,8},{10,11... | collective-permute-start | bytes 6291464 | tf_op jit(solution)/shard_map/ppermute | solution.py:940
  268.6 20.5 %collective-permute-start.9 = (bf16[2048,128]{1,0:T(8,128)(2,1)}, bf16[2048,128]{1,0:T(8,128)(2,1)S(1)}, u32[]{:S(2)}, u32[]{:S(2)}) collective-permute-start(bf16[2048,128]{1,0:T(8,128)(2,1)} %bitcast.145), channel_id=1, source_target_pairs={{0,8},{1,9},{2,10},{3,11},{4,12},{5,13},{6,14},{7,15},{8,0},{9,1},... | collective-permute-start | bytes 1572872 | tf_op jit(solution)/shard_map/ppermute | solution.py:940
  268.9 20.2 %collective-permute-start.10 = (bf16[2048,128]{1,0:T(8,128)(2,1)}, bf16[2048,128]{1,0:T(8,128)(2,1)S(1)}, u32[]{:S(2)}, u32[]{:S(2)}) collective-permute-start(bf16[2048,128]{1,0:T(8,128)(2,1)} %bitcast.144), channel_id=1, source_target_pairs={{0,16},{1,17},{2,18},{3,19},{4,20},{5,21},{6,22},{7,23},{8,24},{9,... | collective-permute-start | bytes 1572872 | tf_op jit(solution)/shard_map/ppermute | solution.py:940
  270.0 23.7 %collective-permute-start.11 = (bf16[2048,128]{1,0:T(8,128)(2,1)}, bf16[2048,128]{1,0:T(8,128)(2,1)S(1)}, u32[]{:S(2)}, u32[]{:S(2)}) collective-permute-start(bf16[2048,128]{1,0:T(8,128)(2,1)} %bitcast.142), channel_id=1, source_target_pairs={{0,24},{1,25},{2,26},{3,27},{4,28},{5,29},{6,30},{7,31},{8,16},{9,... | collective-permute-start | bytes 1572872 | tf_op jit(solution)/shard_map/ppermute | solution.py:940
  293.7 29.4 %collective-permute-start.16 = (bf16[16,2,2,128,128]{4,3,2,1,0:T(8,128)(2,1)}, bf16[16,2,2,128,128]{4,3,2,1,0:T(8,128)(2,1)}, u32[]{:S(2)}, u32[]{:S(2)}) collective-permute-start(bf16[16,2,2,128,128]{4,3,2,1,0:T(8,128)(2,1)} %get-tuple-element.247), channel_id=1, source_target_pairs={{0,1},{1,0},{2,3},{3,2},{4,5},{5,4},{6,7},{7,6},{8,9},{9,8},{10,11... | collective-permute-start | bytes 6291464 | tf_op jit(solution)/shard_map/ppermute | solution.py:940
  298.3 20.5 %collective-permute-start.13 = (bf16[2048,128]{1,0:T(8,128)(2,1)}, bf16[2048,128]{1,0:T(8,128)(2,1)S(1)}, u32[]{:S(2)}, u32[]{:S(2)}) collective-permute-start(bf16[2048,128]{1,0:T(8,128)(2,1)} %bitcast.143), channel_id=1, source_target_pairs={{0,8},{1,9},{2,10},{3,11},{4,12},{5,13},{6,14},{7,15},{8,0},{9,1},... | collective-permute-start | bytes 1572872 | tf_op jit(solution)/shard_map/ppermute | solution.py:940
  299.4 20.2 %collective-permute-start.14 = (bf16[2048,128]{1,0:T(8,128)(2,1)}, bf16[2048,128]{1,0:T(8,128)(2,1)S(1)}, u32[]{:S(2)}, u32[]{:S(2)}) collective-permute-start(bf16[2048,128]{1,0:T(8,128)(2,1)} %bitcast.141), channel_id=1, source_target_pairs={{0,16},{1,17},{2,18},{3,19},{4,20},{5,21},{6,22},{7,23},{8,24},{9,... | collective-permute-start | bytes 1572872 | tf_op jit(solution)/shard_map/ppermute | solution.py:940
  299.8 23.4 %collective-permute-start.15 = (bf16[2048,128]{1,0:T(8,128)(2,1)}, bf16[2048,128]{1,0:T(8,128)(2,1)S(1)}, u32[]{:S(2)}, u32[]{:S(2)}) collective-permute-start(bf16[2048,128]{1,0:T(8,128)(2,1)} %bitcast.140), channel_id=1, source_target_pairs={{0,24},{1,25},{2,26},{3,27},{4,28},{5,29},{6,30},{7,31},{8,16},{9,... | collective-permute-start | bytes 1572872 | tf_op jit(solution)/shard_map/ppermute | solution.py:940
  323.9 51.3 %all-to-all-start.4 = ((bf16[4,2048,128]{2,1,0:T(8,128)(2,1)}), bf16[4,2048,128]{2,1,0:T(8,128)(2,1)S(1)}, u32[]{:S(2)}, u32[]{:S(2)}) async-start(bf16[4,2048,128]{2,1,0:T(8,128)(2,1)} %bitcast.113), calls=%async_computation.4 | async-start | bytes 4194304 | tf_op jit(solution)/shard_map/all_to_all | solution.py:979
  327.5 31.3 %collective-permute-start.17 = (bf16[16,2,2,128,128]{4,3,2,1,0:T(8,128)(2,1)}, bf16[16,2,2,128,128]{4,3,2,1,0:T(8,128)(2,1)}, u32[]{:S(2)}, u32[]{:S(2)}) collective-permute-start(bf16[16,2,2,128,128]{4,3,2,1,0:T(8,128)(2,1)} %get-tuple-element.249), channel_id=1, source_target_pairs={{0,1},{1,0},{2,3},{3,2},{4,5},{5,4},{6,7},{7,6},{8,9},{9,8},{10,11... | collective-permute-start | bytes 6291464 | tf_op jit(solution)/shard_map/ppermute | solution.py:940
  333.8 13.7 %collective-permute-start.18 = (bf16[2048,128]{1,0:T(8,128)(2,1)}, bf16[2048,128]{1,0:T(8,128)(2,1)S(1)}, u32[]{:S(2)}, u32[]{:S(2)}) collective-permute-start(bf16[2048,128]{1,0:T(8,128)(2,1)} %bitcast.150), channel_id=1, source_target_pairs={{0,8},{1,9},{2,10},{3,11},{4,12},{5,13},{6,14},{7,15},{8,0},{9,1},... | collective-permute-start | bytes 1572872 | tf_op jit(solution)/shard_map/ppermute | solution.py:940
  334.2 13.4 %collective-permute-start.19 = (bf16[2048,128]{1,0:T(8,128)(2,1)}, bf16[2048,128]{1,0:T(8,128)(2,1)S(1)}, u32[]{:S(2)}, u32[]{:S(2)}) collective-permute-start(bf16[2048,128]{1,0:T(8,128)(2,1)} %bitcast.148), channel_id=1, source_target_pairs={{0,16},{1,17},{2,18},{3,19},{4,20},{5,21},{6,22},{7,23},{8,24},{9,... | collective-permute-start | bytes 1572872 | tf_op jit(solution)/shard_map/ppermute | solution.py:940
  335.3 23.5 %collective-permute-start.20 = (bf16[2048,128]{1,0:T(8,128)(2,1)}, bf16[2048,128]{1,0:T(8,128)(2,1)S(1)}, u32[]{:S(2)}, u32[]{:S(2)}) collective-permute-start(bf16[2048,128]{1,0:T(8,128)(2,1)} %bitcast.146), channel_id=1, source_target_pairs={{0,24},{1,25},{2,26},{3,27},{4,28},{5,29},{6,30},{7,31},{8,16},{9,... | collective-permute-start | bytes 1572872 | tf_op jit(solution)/shard_map/ppermute | solution.py:940
  375.2 40.9 %all-to-all-start.5 = ((bf16[4,1536,128]{2,1,0:T(8,128)(2,1)}), bf16[4,1536,128]{2,1,0:T(8,128)(2,1)}, u32[]{:S(2)}, u32[]{:S(2)}) async-start(bf16[4,1536,128]{2,1,0:T(8,128)(2,1)} %bitcast.107), calls=%async_computation.5 | async-start | bytes 3145728 | tf_op jit(solution)/shard_map/all_to_all | solution.py:979
  382.9 12.3 %collective-permute-start.21 = (bf16[2048,128]{1,0:T(8,128)(2,1)}, bf16[2048,128]{1,0:T(8,128)(2,1)S(1)}, u32[]{:S(2)}, u32[]{:S(2)}) collective-permute-start(bf16[2048,128]{1,0:T(8,128)(2,1)} %bitcast.151), channel_id=1, source_target_pairs={{0,8},{1,9},{2,10},{3,11},{4,12},{5,13},{6,14},{7,15},{8,0},{9,1},... | collective-permute-start | bytes 1572872 | tf_op jit(solution)/shard_map/ppermute | solution.py:940
  383.1 12.1 %collective-permute-start.22 = (bf16[2048,128]{1,0:T(8,128)(2,1)}, bf16[2048,128]{1,0:T(8,128)(2,1)S(1)}, u32[]{:S(2)}, u32[]{:S(2)}) collective-permute-start(bf16[2048,128]{1,0:T(8,128)(2,1)} %bitcast.149), channel_id=1, source_target_pairs={{0,16},{1,17},{2,18},{3,19},{4,20},{5,21},{6,22},{7,23},{8,24},{9,... | collective-permute-start | bytes 1572872 | tf_op jit(solution)/shard_map/ppermute | solution.py:940
  384.1 22.2 %collective-permute-start.23 = (bf16[2048,128]{1,0:T(8,128)(2,1)}, bf16[2048,128]{1,0:T(8,128)(2,1)S(1)}, u32[]{:S(2)}, u32[]{:S(2)}) collective-permute-start(bf16[2048,128]{1,0:T(8,128)(2,1)} %bitcast.147), channel_id=1, source_target_pairs={{0,24},{1,25},{2,26},{3,27},{4,28},{5,29},{6,30},{7,31},{8,16},{9,... | collective-permute-start | bytes 1572872 | tf_op jit(solution)/shard_map/ppermute | solution.py:940
  416.1 29.0 %all-to-all-start.6 = ((bf16[4,1536,128]{2,1,0:T(8,128)(2,1)}), bf16[4,1536,128]{2,1,0:T(8,128)(2,1)S(1)}, u32[]{:S(2)}, u32[]{:S(2)}) async-start(bf16[4,1536,128]{2,1,0:T(8,128)(2,1)} %all-to-all-done.5), calls=%async_computation.6 | async-start | bytes 3145728 | tf_op jit(solution)/shard_map/all_to_all | solution.py:982
  422.2 17.1 %collective-permute-start.25 = (bf16[512,128]{1,0:T(8,128)(2,1)}, bf16[512,128]{1,0:T(8,128)(2,1)S(1)}, u32[]{:S(2)}, u32[]{:S(2)}) collective-permute-start(bf16[512,128]{1,0:T(8,128)(2,1)} %bitcast.155), channel_id=1, source_target_pairs={{0,2},{1,3},{2,8},{3,9},{4,22},{5,23},{6,28},{7,29},{8,0},{9,1},{1... | collective-permute-start | bytes 393224 | tf_op jit(solution)/shard_map/ppermute | solution.py:940
  424.1 15.2 %collective-permute-start.24 = (bf16[512,128]{1,0:T(8,128)(2,1)}, bf16[512,128]{1,0:T(8,128)(2,1)S(1)}, u32[]{:S(2)}, u32[]{:S(2)}) collective-permute-start(bf16[512,128]{1,0:T(8,128)(2,1)} %bitcast.154), channel_id=1, source_target_pairs={{0,0},{1,1},{2,10},{3,11},{4,20},{5,21},{6,30},{7,31},{8,2},{9,3},... | collective-permute-start | bytes 393224 | tf_op jit(solution)/shard_map/ppermute | solution.py:940
  429.4 15.8 %collective-permute-start.27 = (bf16[512,128]{1,0:T(8,128)(2,1)}, bf16[512,128]{1,0:T(8,128)(2,1)}, u32[]{:S(2)}, u32[]{:S(2)}) collective-permute-start(bf16[512,128]{1,0:T(8,128)(2,1)} %bitcast.152), channel_id=1, source_target_pairs={{0,6},{1,7},{2,12},{3,13},{4,18},{5,19},{6,24},{7,25},{8,4},{9,5},... | collective-permute-start | bytes 393224 | tf_op jit(solution)/shard_map/ppermute | solution.py:940
  (28 other events, 282.2 us)

commit v13 on v12

--- a/solution.py
+++ b/solution.py
@@ -298,8 +298,11 @@
 
 
 def column(gain_ref, block, at, slots):
-    gains = gain_ref[block // gain_ref.shape[2]]
-    return jnp.broadcast_to(gains[:, at : at + 1], (gains.shape[0], slots))
+    if len(gain_ref.shape) == 3:
+        gains = gain_ref[block // gain_ref.shape[2]]
+        return jnp.broadcast_to(gains[:, at : at + 1], (gains.shape[0], slots))
+    picked = lax.broadcasted_iota(jnp.int32, (gain_ref.shape[1], slots), 0) == block
+    return inner_dot(gain_ref[...], picked.astype(jnp.bfloat16), 1, 0)
 
 
 def chunk_copy(source, target, sems, chunk):
@@ -688,6 +691,38 @@
     )(*parts)
 
 
+def order_kernel(ranges, place_ref, *refs):
+    sources, whole, sems = refs[:-2], refs[-2], refs[-1]
+    copies = []
+    for distance, source in enumerate(sources):
+        row = 0
+        for start, count in ranges:
+            target = whole.at[place_ref[0] ^ distance, pl.ds(row, count)]
+            copies.append(pltpu.make_async_copy(source.at[pl.ds(start, count)], target, sems.at[len(copies)]))
+            row += count
+    for copy in copies:
+        copy.start()
+    for copy in copies:
+        copy.wait()
+
+
+def by_section(place, parts, ranges):
+    rows = sum(count for _, count in ranges)
+    whole = shape_of((len(parts), rows) + parts[0].shape[1:], parts[0].dtype)
+    return pl.pallas_call(
+        lambda *refs: order_kernel(ranges, *refs),
+        in_specs=[SMEM] + [OUTSIDE] * len(parts),
+        out_specs=INSIDE,
+        out_shape=whole,
+        scratch_shapes=[pltpu.SemaphoreType.DMA((len(parts) * len(ranges),))],
+        compiler_params=pltpu.CompilerParams(vmem_limit_bytes=VMEM_LIMIT),
+        cost_estimate=pl.CostEstimate(
+            flops=0, bytes_accessed=4 * math.prod(whole.shape), transcendentals=0
+        ),
+        name="by_section",
+    )(place, *parts)
+
+
 def sum_kernel(terms, inputs, *refs):
     sources, outs = refs[:inputs], refs[inputs:]
     for group in range(inputs // terms):
@@ -725,33 +760,35 @@
     return [out.reshape(-1, lanes) for out in sums] if apart else sums[0].reshape(parts, -1, lanes)
 
 
-def pieces_kernel(chunk, place_ref, order_ref, left_ref, right_ref, gain_ref, out_ref, held, left_sem, sems):
+def pieces_kernel(chunk, place_ref, order_ref, left_ref, right_ref, gain_ref, *refs):
+    outs, (held, left_sem, sems) = refs[:-3], refs[-3:]
     layer_count, half, size = held.shape[:3]
     first = place_ref[2] * half
     lefts = pltpu.make_async_copy(left_ref.at[:, pl.ds(first, half)], held, left_sem.at[0])
     lefts.start()
     copies = []
     turns = []
-    for section in range(out_ref.shape[0]):
+    for distance, out in enumerate(outs):
+        start = (place_ref[0] ^ distance) * chunk
         row = 0
         for layer in range(layer_count):
             for inside in range(chunk):
-                turns.append((layer, section * chunk + inside, section, row))
+                turns.append((layer, start + inside, out, row))
                 row += size
             for inside in range(chunk):
-                source = right_ref.at[layer, first + section * chunk + inside]
-                copies.append((source, out_ref.at[section, pl.ds(row, size)]))
+                source = right_ref.at[layer, first + start + inside]
+                copies.append((source, out.at[pl.ds(row, size)]))
                 row += size
-        copies.append((gain_ref, out_ref.at[section, pl.ds(row, gain_ref.shape[0])]))
+        copies.append((gain_ref, out.at[pl.ds(row, gain_ref.shape[0])]))
     copies = [
         pltpu.make_async_copy(source, target, sems.at[at]) for at, (source, target) in enumerate(copies)
     ]
     for copy in copies:
         copy.start()
     lefts.wait()
-    for layer, block, section, row in turns:
+    for layer, block, out, row in turns:
         turned = inner_dot(held[layer, block], order_ref[...], 1, 0)
-        out_ref[section, pl.ds(row, size), :] = turned.astype(jnp.bfloat16)
+        out[pl.ds(row, size), :] = turned.astype(jnp.bfloat16)
     for copy in copies:
         copy.wait()
 
@@ -762,8 +799,8 @@
     return pl.pallas_call(
         lambda *refs: pieces_kernel(chunk, *refs),
         in_specs=[SMEM, INSIDE] + [OUTSIDE] * 3,
-        out_specs=INSIDE,
-        out_shape=shape_of((width, rows, size), jnp.bfloat16),
+        out_specs=[INSIDE] * width,
+        out_shape=[shape_of((rows, size), jnp.bfloat16)] * width,
         scratch_shapes=[
             pltpu.VMEM((layer_count, blocks // 2, size, size), jnp.bfloat16),
             pltpu.SemaphoreType.DMA((1,)),
@@ -987,30 +1024,34 @@
     columns = jnp.arange(size)
     order = (columns[:, None] == (columns % blocks) * fold + columns // blocks).astype(jnp.bfloat16)
     gain_rows = norm_gains[0].reshape(-1, size)
-    pieces = factor_pieces(place, order, left_factors[0], right_factors[0], gain_rows, chunk, width)
-    pieces, patches, teacher = tie((pieces, patches, teacher))
-    spread = to_sections(pieces)
     patch_sent = run_pick(critic_pairs, patches, width, wide)
+    patch_sent, left, right, teacher = tie((patch_sent, left_factors[0], right_factors[0], teacher))
+    patch_came = to_planes(patch_sent).reshape(-1, wide)
+    pieces = factor_pieces(place, order, left, right, gain_rows, chunk, width)
+    spread = send(pieces, "sections")
+    cut, end = half_layers * layer_rows, layer_count * layer_rows
+    first = by_section(place, spread, [(0, cut), (end, gain_rows.shape[0])])
+    second = by_section(place, spread, [(cut, end - cut)])
     target_sent = run_pick(critic_pairs, teacher, width, wide)
-    spread, patch_sent, target_sent = tie((spread, patch_sent, target_sent))
-    lifted = to_planes(spread)
-    lifted, patch_sent = tie((lifted, patch_sent))
-    patch_came = to_planes(patch_sent).reshape(-1, wide)
-    lowest = [lifted[:, group[0] * layer_rows : (group[-1] + 1) * layer_rows] for group in groups]
-    beside = move(lowest[0], routes["across"][0])
-    gains = lifted[:, layer_count * layer_rows :].reshape(width, layer_count + 1, local_blocks, size)
-    gains = gains.transpose(1, 3, 0, 2).reshape(layer_count + 1, size, CHUNKS, blocks // CHUNKS)
-    gains = gains.transpose(0, 2, 1, 3).astype(jnp.float32)
-    later = (lowest[1], move(lowest[1], routes["across"][0]))
-    lowest[0], beside, later, gains = tie((lowest[0], beside, later, gains))
-    first_two = gather_two(joined([lowest[0], beside]))
-    later = joined(list(later))
-    first_two, later, patch_came = tie((first_two, later, patch_came))
+    patch_came, first, second, target_sent = tie((patch_came, first, second, target_sent))
+    first = to_planes(first)
+    first, second = tie((first, second))
+    second = to_planes(second)
+    lowest = first[:, :cut]
+    beside = move(lowest, routes["across"][0])
+    gains = first[:, cut:].reshape(width, layer_count + 1, local_blocks, size)
+    gains = gains.transpose(1, 3, 0, 2).reshape(layer_count + 1, size, blocks)
+    end_gain = gains[layer_count].reshape(size, CHUNKS, blocks // CHUNKS).transpose(1, 0, 2)
+    end_gain = end_gain.astype(jnp.float32)
+    lowest, beside, gains, end_gain = tie((lowest, beside, gains, end_gain))
+    first_two = gather_two(joined([lowest, beside]))
+    first_two, second, target_sent = tie((first_two, second, target_sent))
+    target = to_planes(target_sent).reshape(-1, wide)
     weights = [as_weights(gather_three(*first_two))]
+    later = gather_one(second)
     weights, later = tie((weights, later))
 
-    residual, target_sent = tie((patch_came, target_sent))
-    target = to_planes(target_sent).reshape(-1, wide)
+    residual = patch_came
     flying = gather_two(later)
     sums = jnp.zeros((8, wide), jnp.float32)
     stored = []
@@ -1055,7 +1096,7 @@
         gradient, mine, other = run_backward(
             table,
             gains[layer],
-            gains[layer_count],
+            end_gain,
             scale,
             kept,
             weights[group],

time: 461 us -> 462 us (level)
  waiting for transfers between devices: 142 us -> 134 us
  blocking collectives: 53.8 us -> 58.9 us
    ppermute x30 -> x33, waiting for transfers between devices: 85.5 us -> 105 us  [move(): return lax.ppermute(value, AXES, route)]
    all_to_all x2 -> x1, waiting for transfers between devices: 16.2 us -> 0.01 us  [to_sections(): lax.all_to_all(value, 'section', split_axis=0, concat_axis=0, tiled=True)]
    all_to_all x4, waiting for transfers between devices: 40.7 us -> 29 us  [to_planes(): lax.all_to_all(value, 'tensor', split_axis=0, concat_axis=0, tiled=True)]
    pallas_call x0 -> x2, Pallas kernels: none -> 5.82 us  [by_section(): pl.pallas_call(lambda *refs: order_kernel(ranges, *refs), in_specs=[SMEM]...]
    ppermute x30 -> x33, starting transfers between devices: 38.3 us -> 43.5 us  [move(): return lax.ppermute(value, AXES, route)]
    all_to_all x1 -> x2, blocking collectives: 53.8 us -> 58.9 us  [to_planes(): lax.all_to_all(value, 'tensor', split_axis=0, concat_axis=0, tiled=True)]
    unnamed x49 -> x67, local copies, waits for them, and re-layouts: 8.3 us -> 9.81 us
  transfers between devices with their start and end apart: 36 -> 38, of which waited for: 18 -> 18; matrix products, arithmetic and copies ran while one was open for 1% -> 1% of each run, Pallas kernels for 30% -> 30%
where the time goes in v13:
time: 462 us; the launch traced here: 460 us
  Pallas kernels  185 us (40%)
  waiting for transfers between devices  134 us (29%)
  starting transfers between devices  65.3 us (14%)
  blocking collectives  58.9 us (13%)
  local copies, waits for them, and re-layouts  13.8 us (3%)
    ppermute x33, waiting for transfers between devices, move(): return lax.ppermute(value, AXES, route)  105 us
    pallas_call x4, Pallas kernels, run_backward(): pl.pallas_call(lambda *refs: backward_kernel(turning, last, layer, len(so...  73.3 us
    all_to_all x2, blocking collectives, to_planes(): lax.all_to_all(value, 'tensor', split_axis=0, concat_axis=0, tiled=True)  58.9 us
    pallas_call x4, Pallas kernels, run_forward(): pl.pallas_call(lambda *refs: forward_kernel(first, layer, len(sources), *...  55.5 us
    ppermute x33, starting transfers between devices, move(): return lax.ppermute(value, AXES, route)  43.5 us
    all_to_all x4, waiting for transfers between devices, to_planes(): lax.all_to_all(value, 'tensor', split_axis=0, concat_axis=0, tiled=True)  29 us
    pallas_call x6, Pallas kernels, run_sum(): pl.pallas_call(lambda *refs: sum_kernel(len(groups[0]), len(flat), *refs)...  19.8 us
    all_to_all x4, starting transfers between devices, to_planes(): lax.all_to_all(value, 'tensor', split_axis=0, concat_axis=0, tiled=True)  17.3 us
  transfers between devices with their start and end apart: 38, of which 18 were waited for; matrix products, arithmetic and copies ran while one was open for 1% of the time, Pallas kernels for 30%

profile of v13, /device:TPU:5, one launch (start us, length us, event | category | flops | bytes accessed | tf_op | source)
XLA Modules:
  0.0 460.3 jit_solution(11390993966269491296)
XLA Ops:
  2.1 4.1 pick.2
  6.2 4.7 %all-to-all-start = ((bf16[4,2048,128]{2,1,0:T(8,128)(2,1)}), bf16[4,2048,128]{2,1,0:T(8,128)(2,1)S(1)}, u32[]{:S(2)}, u32[]{:S(2)}) async-start(bf16[4,2048,128]{2,1,0:T(8,128)(2,1)} %pick.2), calls=%async_computation | async-start | bytes 4194304 | tf_op jit(solution)/shard_map/all_to_all | solution.py:1016
  12.8 4.6 %pieces.1 = (bf16[2128,128]{1,0:T(8,128)(2,1)}, bf16[2128,128]{1,0:T(8,128)(2,1)}, bf16[2128,128]{1,0:T(8,128)(2,1)}, bf16[2128,128]{1,0:T(8,128)(2,1)}) custom-call(s32[3]{0:T(128)} %pad_add_fusion.1.refs_0_, bf16[128,128]{1,0:T(8,128)(2,1)} %fusion.refs_1_, bf16[4,16,128,128]{3,2,1,0:T(8,128)(2,1)} %bitcast.118, bf16[4,16,128,128]{3,2,1,0:T(8,128)(2,1)} %bitcast.119, ...), custom_call_target="tpu_custom_call" | custom-call | flops 134217728 | bytes 4194304 | tf_op jit(solution)/shard_map/pieces/pallas_call | solution.py:799
  20.1 4.1 pick.3
  24.3 6.3 %collective-permute-done.refs_2_ = bf16[2128,128]{1,0:T(8,128)(2,1)S(1)} collective-permute-done((bf16[2128,128]{1,0:T(8,128)(2,1)}, bf16[2128,128]{1,0:T(8,128)(2,1)S(1)}, u32[]{:S(2)}, u32[]{:S(2)}) %collective-permute-start) | collective-permute-done | bytes 544800 | tf_op jit(solution)/shard_map/ppermute | solution.py:977
  32.5 9.7 %collective-permute-done.2.refs_4_ = bf16[2128,128]{1,0:T(8,128)(2,1)S(1)} collective-permute-done((bf16[2128,128]{1,0:T(8,128)(2,1)}, bf16[2128,128]{1,0:T(8,128)(2,1)S(1)}, u32[]{:S(2)}, u32[]{:S(2)}) %collective-permute-start.2) | collective-permute-done | bytes 544800 | tf_op jit(solution)/shard_map/ppermute | solution.py:977
  48.9 9.7 %all-to-all-done = bf16[4,2048,128]{2,1,0:T(8,128)(2,1)S(1)} async-done(((bf16[4,2048,128]{2,1,0:T(8,128)(2,1)}), bf16[4,2048,128]{2,1,0:T(8,128)(2,1)S(1)}, u32[]{:S(2)}, u32[]{:S(2)}) %all-to-all-start) | async-done | bytes 2097184 | tf_op jit(solution)/shard_map/all_to_all | solution.py:1016
  58.6 30.2 %all_to_all.35 = bf16[4,1104,128]{2,1,0:T(8,128)(2,1)S(1)} all-to-all(bf16[4,1104,128]{2,1,0:T(8,128)(2,1)} %by_section.2), channel_id=1, replica_groups=mesh['section'=4,'tensor'=4,'dp'=2] {'tensor'}, dimensions={0} | all-to-all | bytes 2260992 | tf_op jit(solution)/shard_map/all_to_all | solution.py:1016
  90.2 12.9 %collective-permute-done.3.refs_1_ = bf16[4,1024,128]{2,1,0:T(8,128)(2,1)} collective-permute-done((bf16[4,1024,128]{2,1,0:T(8,128)(2,1)S(1)}, bf16[4,1024,128]{2,1,0:T(8,128)(2,1)}, u32[]{:S(2)}, u32[]{:S(2)}) %collective-permute-start.3) | collective-permute-done | bytes 1048608 | tf_op jit(solution)/shard_map/ppermute | solution.py:977
  109.9 28.7 %all_to_all.36.refs_0_ = bf16[4,1024,128]{2,1,0:T(8,128)(2,1)S(1)} all-to-all(bf16[4,1024,128]{2,1,0:T(8,128)(2,1)S(1)} %copy-done.6), channel_id=1, replica_groups=mesh['section'=4,'tensor'=4,'dp'=2] {'tensor'}, dimensions={0} | all-to-all | bytes 2097152 | tf_op jit(solution)/shard_map/all_to_all | solution.py:1016
  139.5 13.9 %collective-permute-done.7.refs_1_ = bf16[4,1024,128]{2,1,0:T(8,128)(2,1)S(1)} collective-permute-done((bf16[4,1024,128]{2,1,0:T(8,128)(2,1)S(1)}, bf16[4,1024,128]{2,1,0:T(8,128)(2,1)S(1)}, u32[]{:S(2)}, u32[]{:S(2)}) %collective-permute-start.7) | collective-permute-done | bytes 1048608 | tf_op jit(solution)/shard_map/ppermute | solution.py:977
  159.9 4.6 %all-to-all-start.3 = ((bf16[4,2048,128]{2,1,0:T(8,128)(2,1)}), bf16[4,2048,128]{2,1,0:T(8,128)(2,1)}, u32[]{:S(2)}, u32[]{:S(2)}) async-start(bf16[4,2048,128]{2,1,0:T(8,128)(2,1)} %pick.3), calls=%async_computation.3 | async-start | bytes 4194304 | tf_op jit(solution)/shard_map/all_to_all | solution.py:1016
  166.6 14.4 %forward_layer.4 = (f32[8192,128]{1,0:T(8,128)}, bf16[8192,128]{1,0:T(8,128)(2,1)}, bf16[8192,128]{1,0:T(8,128)(2,1)}, bf16[8192,128]{1,0:T(8,128)(2,1)}, f32[8,128]{1,0:T(8,128)}, /*index=5*/f32[8,128]{1,0:T(8,128)}) custom-call(s32[3,64]{1,0:T(4,128)} %pad_add_fusion.refs_0_, f32[8,128]{1,0:T(8,128)} %broadcast_in_dim.6.refs_1_, ...), custom_call_target="tpu_custom_call" | custom-call | flops 4000000000 | bytes 20971520 | tf_op jit(solution)/shard_map/forward_layer/pallas_call | solution.py:605
  185.1 13.7 %forward_layer.5 = (f32[8192,128]{1,0:T(8,128)}, bf16[8192,128]{1,0:T(8,128)(2,1)}, bf16[8192,128]{1,0:T(8,128)(2,1)}, bf16[8192,128]{1,0:T(8,128)(2,1)}, f32[8,128]{1,0:T(8,128)}, /*index=5*/f32[8,128]{1,0:T(8,128)}) custom-call(s32[3,64]{1,0:T(4,128)} %pad_add_fusion.refs_0_, f32[8,128]{1,0:T(8,128)} %get-tuple-element.188.refs_1_, ...), custom_call_target="tpu_custom_call" | custom-call | flops 4000000000 | bytes 20971520 | tf_op jit(solution)/shard_map/forward_layer/pallas_call | solution.py:605
  198.8 13.8 %forward_layer.6 = (f32[8192,128]{1,0:T(8,128)}, bf16[8192,128]{1,0:T(8,128)(2,1)}, bf16[8192,128]{1,0:T(8,128)(2,1)}, bf16[8192,128]{1,0:T(8,128)(2,1)}, f32[8,128]{1,0:T(8,128)}, /*index=5*/f32[8,128]{1,0:T(8,128)}) custom-call(s32[3,64]{1,0:T(4,128)} %pad_add_fusion.refs_0_, f32[8,128]{1,0:T(8,128)} %get-tuple-element.199.refs_1_, ...), custom_call_target="tpu_custom_call" | custom-call | flops 4000000000 | bytes 20971520 | tf_op jit(solution)/shard_map/forward_layer/pallas_call | solution.py:605
  212.6 13.7 %forward_layer.7 = (f32[8192,128]{1,0:T(8,128)}, bf16[8192,128]{1,0:T(8,128)(2,1)}, bf16[8192,128]{1,0:T(8,128)(2,1)}, bf16[8192,128]{1,0:T(8,128)(2,1)}, f32[8,128]{1,0:T(8,128)}, /*index=5*/f32[8,128]{1,0:T(8,128)}) custom-call(s32[3,64]{1,0:T(4,128)} %pad_add_fusion.refs_0_, f32[8,128]{1,0:T(8,128)} %get-tuple-element.212.refs_1_, ...), custom_call_target="tpu_custom_call" | custom-call | flops 4000000000 | bytes 20971520 | tf_op jit(solution)/shard_map/forward_layer/pallas_call | solution.py:605
  226.3 19.5 %backward_layer.4 = (f32[8192,128]{1,0:T(8,128)}, bf16[16,2,2,128,128]{4,3,2,1,0:T(8,128)(2,1)}, bf16[16,2,2,128,128]{4,3,2,1,0:T(8,128)(2,1)}) custom-call(s32[3,64]{1,0:T(4,128)} %pad_add_fusion.refs_0_, f32[8,128]{1,0:T(8,128)} %get-tuple-element.214.refs_1_, bf16[128,64]{1,0:T(8,128)(2,1)} %get-tuple-element.307.refs_2_, f32[8,128,8]{2,1,0:T(8,128)} %bitcast.102, ...), custom_call_target="tpu_custom_call" | custom-call | flops 5000000000 | bytes 31457280 | tf_op jit(solution)/shard_map/backward_layer/pallas_call | solution.py:636
  246.9 18.0 %backward_layer.5 = (f32[8192,128]{1,0:T(8,128)}, bf16[16,2,2,128,128]{4,3,2,1,0:T(8,128)(2,1)}, bf16[16,2,2,128,128]{4,3,2,1,0:T(8,128)(2,1)}) custom-call(s32[3,64]{1,0:T(4,128)} %pad_add_fusion.refs_0_, f32[8,128]{1,0:T(8,128)} %get-tuple-element.205.refs_1_, bf16[128,64]{1,0:T(8,128)(2,1)} %get-tuple-element.308.refs_2_, f32[8,128,8]{2,1,0:T(8,128)} %bitcast.103, ...), custom_call_target="tpu_custom_call" | custom-call | flops 5000000000 | bytes 31457280 | tf_op jit(solution)/shard_map/backward_layer/pallas_call | solution.py:636
  272.2 17.9 %backward_layer.6 = (f32[8192,128]{1,0:T(8,128)}, bf16[16,2,2,128,128]{4,3,2,1,0:T(8,128)(2,1)}, bf16[16,2,2,128,128]{4,3,2,1,0:T(8,128)(2,1)}) custom-call(s32[3,64]{1,0:T(4,128)} %pad_add_fusion.refs_0_, f32[8,128]{1,0:T(8,128)} %get-tuple-element.190.refs_1_, bf16[128,64]{1,0:T(8,128)(2,1)} %get-tuple-element.309.refs_2_, f32[8,128,8]{2,1,0:T(8,128)} %bitcast.104, ...), custom_call_target="tpu_custom_call" | custom-call | flops 5000000000 | bytes 31457280 | tf_op jit(solution)/shard_map/backward_layer/pallas_call | solution.py:636
  302.5 17.9 %backward_layer.7 = (bf16[8192,128]{1,0:T(8,128)(2,1)}, bf16[16,2,2,128,128]{4,3,2,1,0:T(8,128)(2,1)}, bf16[16,2,2,128,128]{4,3,2,1,0:T(8,128)(2,1)}) custom-call(s32[3,64]{1,0:T(4,128)} %pad_add_fusion.refs_0_, f32[8,128]{1,0:T(8,128)} %get-tuple-element.180.refs_1_, bf16[128,64]{1,0:T(8,128)(2,1)} %get-tuple-element.310.refs_2_, f32[8,128,8]{2,1,0:T(8,128)} %bitcast.105, ...), custom_call_target="tpu_custom_call" | custom-call | flops 5000000000 | bytes 31457280 | tf_op jit(solution)/shard_map/backward_layer/pallas_call | solution.py:636
  337.3 11.1 %collective-permute-done.21 = bf16[2048,128]{1,0:T(8,128)(2,1)S(1)} collective-permute-done((bf16[2048,128]{1,0:T(8,128)(2,1)}, bf16[2048,128]{1,0:T(8,128)(2,1)S(1)}, u32[]{:S(2)}, u32[]{:S(2)}) %collective-permute-start.21) | collective-permute-done | bytes 524320 | tf_op jit(solution)/shard_map/ppermute | solution.py:977
  348.4 11.9 %collective-permute-done.22 = bf16[2048,128]{1,0:T(8,128)(2,1)S(1)} collective-permute-done((bf16[2048,128]{1,0:T(8,128)(2,1)}, bf16[2048,128]{1,0:T(8,128)(2,1)S(1)}, u32[]{:S(2)}, u32[]{:S(2)}) %collective-permute-start.22) | collective-permute-done | bytes 524320 | tf_op jit(solution)/shard_map/ppermute | solution.py:977
  361.3 4.1 sum.10
  365.4 10.3 %all-to-all-done.4.came_ref = bf16[4,2048,128]{2,1,0:T(8,128)(2,1)S(1)} async-done(((bf16[4,2048,128]{2,1,0:T(8,128)(2,1)}), bf16[4,2048,128]{2,1,0:T(8,128)(2,1)S(1)}, u32[]{:S(2)}, u32[]{:S(2)}) %all-to-all-start.4) | async-done | bytes 2097184 | tf_op jit(solution)/shard_map/all_to_all | solution.py:1016
  375.7 4.3 all-to-all-start.5
  386.1 9.6 %collective-permute-done.24 = bf16[2048,128]{1,0:T(8,128)(2,1)S(1)} collective-permute-done((bf16[2048,128]{1,0:T(8,128)(2,1)}, bf16[2048,128]{1,0:T(8,128)(2,1)S(1)}, u32[]{:S(2)}, u32[]{:S(2)}) %collective-permute-start.24) | collective-permute-done | bytes 524320 | tf_op jit(solution)/shard_map/ppermute | solution.py:977
  396.2 11.4 %collective-permute-done.26 = bf16[2048,128]{1,0:T(8,128)(2,1)S(1)} collective-permute-done((bf16[2048,128]{1,0:T(8,128)(2,1)}, bf16[2048,128]{1,0:T(8,128)(2,1)S(1)}, u32[]{:S(2)}, u32[]{:S(2)}) %collective-permute-start.26) | collective-permute-done | bytes 524320 | tf_op jit(solution)/shard_map/ppermute | solution.py:977
  407.6 9.0 %all-to-all-done.5 = bf16[4,1536,128]{2,1,0:T(8,128)(2,1)} async-done(((bf16[4,1536,128]{2,1,0:T(8,128)(2,1)}), bf16[4,1536,128]{2,1,0:T(8,128)(2,1)}, u32[]{:S(2)}, u32[]{:S(2)}) %all-to-all-start.5) | async-done | bytes 1572896 | tf_op jit(solution)/shard_map/all_to_all | solution.py:1016
  416.5 4.5 all-to-all-start.6
  430.6 6.1 %collective-permute-start.30 = (bf16[512,128]{1,0:T(8,128)(2,1)}, bf16[512,128]{1,0:T(8,128)(2,1)}, u32[]{:S(2)}, u32[]{:S(2)}) collective-permute-start(bf16[512,128]{1,0:T(8,128)(2,1)} %bitcast.164), channel_id=1, source_target_pairs={{0,6},{1,7},{2,12},{3,13},{4,18},{5,19},{6,24},{7,25},{8,4},{9,5},... | collective-permute-start | bytes 393224 | tf_op jit(solution)/shard_map/ppermute | solution.py:977
  440.6 5.8 %collective-permute-done.30.refs_3_ = bf16[512,128]{1,0:T(8,128)(2,1)} collective-permute-done((bf16[512,128]{1,0:T(8,128)(2,1)}, bf16[512,128]{1,0:T(8,128)(2,1)}, u32[]{:S(2)}, u32[]{:S(2)}) %collective-permute-start.30) | collective-permute-done | bytes 131104 | tf_op jit(solution)/shard_map/ppermute | solution.py:977
  454.3 5.9 %assemble.1 = (f32[4,16,128,128]{3,2,1,0:T(8,128)}, f32[4,16,128,128]{3,2,1,0:T(8,128)}) custom-call(s32[3]{0:T(128)} %pad_add_fusion.1.refs_0_, bf16[128,128]{1,0:T(8,128)(2,1)} %fusion.refs_1_, bf16[4,1,2,2,128,128]{5,4,3,2,1,0:T(8,128)(2,1)} %bitcast.120, bf16[4,1,2,2,128,128]{5,4,3,2,1,0:T(8,128)(2,1)} %bitcast.129, ...), custom_call_target="tpu_custom_call" | custom-call | bytes 12582912 | tf_op jit(solution)/shard_map/assemble/pallas_call | solution.py:920
  (154 shorter events, 102.6 us)
Async XLA Ops:
  6.2 52.4 %all-to-all-start = ((bf16[4,2048,128]{2,1,0:T(8,128)(2,1)}), bf16[4,2048,128]{2,1,0:T(8,128)(2,1)S(1)}, u32[]{:S(2)}, u32[]{:S(2)}) async-start(bf16[4,2048,128]{2,1,0:T(8,128)(2,1)} %pick.2), calls=%async_computation | async-start | bytes 4194304 | tf_op jit(solution)/shard_map/all_to_all | solution.py:1016
  18.7 13.8 %collective-permute-start.1 = (bf16[2128,128]{1,0:T(8,128)(2,1)}, bf16[2128,128]{1,0:T(8,128)(2,1)S(1)}, u32[]{:S(2)}, u32[]{:S(2)}) collective-permute-start(bf16[2128,128]{1,0:T(8,128)(2,1)} %get-tuple-element.160), channel_id=1, source_target_pairs={{0,16},{1,17},{2,18},{3,19},{4,20},{5,21},{6,22},{7,23},{8,24},{9,... | collective-permute-start | bytes 1634312 | tf_op jit(solution)/shard_map/ppermute | solution.py:977
  18.9 23.3 %collective-permute-start.2 = (bf16[2128,128]{1,0:T(8,128)(2,1)}, bf16[2128,128]{1,0:T(8,128)(2,1)S(1)}, u32[]{:S(2)}, u32[]{:S(2)}) collective-permute-start(bf16[2128,128]{1,0:T(8,128)(2,1)} %get-tuple-element.161), channel_id=1, source_target_pairs={{0,24},{1,25},{2,26},{3,27},{4,28},{5,29},{6,30},{7,31},{8,16},{9,... | collective-permute-start | bytes 1634312 | tf_op jit(solution)/shard_map/ppermute | solution.py:977
  88.9 14.1 %collective-permute-start.3 = (bf16[4,1024,128]{2,1,0:T(8,128)(2,1)S(1)}, bf16[4,1024,128]{2,1,0:T(8,128)(2,1)}, u32[]{:S(2)}, u32[]{:S(2)}) collective-permute-start(bf16[4,1024,128]{2,1,0:T(8,128)(2,1)S(1)} %slice.26.refs_0_), channel_id=1, source_target_pairs={{0,8},{1,17},{2,10},{3,19},{4,12},{5,21},{6,14},{7,23},{8,0},{9,25... | collective-permute-start | bytes 3145736 | tf_op jit(solution)/shard_map/ppermute | solution.py:977
  106.0 32.5 %collective-permute-start.5 = (bf16[8,1024,128]{2,1,0:T(8,128)(2,1)}, bf16[8,1024,128]{2,1,0:T(8,128)(2,1)S(1)}, u32[]{:S(2)}, u32[]{:S(2)}) collective-permute-start(bf16[8,1024,128]{2,1,0:T(8,128)(2,1)} %join.3), channel_id=1, source_target_pairs={{0,1},{1,0},{2,3},{3,2},{4,5},{5,4},{6,7},{7,6},{8,9},{9,8},{10,11... | collective-permute-start | bytes 6291464 | tf_op jit(solution)/shard_map/ppermute | solution.py:977
  108.7 29.9 %collective-permute-start.4 = (bf16[8,1024,128]{2,1,0:T(8,128)(2,1)}, bf16[8,1024,128]{2,1,0:T(8,128)(2,1)}, u32[]{:S(2)}, u32[]{:S(2)}) collective-permute-start(bf16[8,1024,128]{2,1,0:T(8,128)(2,1)} %join.3), channel_id=1, source_target_pairs={{0,16},{1,9},{2,18},{3,11},{4,20},{5,13},{6,22},{7,15},{8,24},{9,1... | collective-permute-start | bytes 6291464 | tf_op jit(solution)/shard_map/ppermute | solution.py:977
  138.6 18.8 %collective-permute-start.6 = (bf16[8,1024,128]{2,1,0:T(8,128)(2,1)}, bf16[8,1024,128]{2,1,0:T(8,128)(2,1)}, u32[]{:S(2)}, u32[]{:S(2)}) collective-permute-start(bf16[8,1024,128]{2,1,0:T(8,128)(2,1)} %collective-permute-done.4), channel_id=1, source_target_pairs={{0,1},{1,0},{2,3},{3,2},{4,5},{5,4},{6,7},{7,6},{8,9},{9,8},{10,11... | collective-permute-start | bytes 6291464 | tf_op jit(solution)/shard_map/ppermute | solution.py:977
  139.5 13.9 %collective-permute-start.7 = (bf16[4,1024,128]{2,1,0:T(8,128)(2,1)S(1)}, bf16[4,1024,128]{2,1,0:T(8,128)(2,1)S(1)}, u32[]{:S(2)}, u32[]{:S(2)}) collective-permute-start(bf16[4,1024,128]{2,1,0:T(8,128)(2,1)S(1)} %all_to_all.36.refs_0_), channel_id=1, source_target_pairs={{0,8},{1,17},{2,10},{3,19},{4,12},{5,21},{6,14},{7,23},{8,0},{9,25... | collective-permute-start | bytes 3145736 | tf_op jit(solution)/shard_map/ppermute | solution.py:977
  157.3 23.6 %collective-permute-start.9 = (bf16[8,1024,128]{2,1,0:T(8,128)(2,1)}, bf16[8,1024,128]{2,1,0:T(8,128)(2,1)S(1)}, u32[]{:S(2)}, u32[]{:S(2)}) collective-permute-start(bf16[8,1024,128]{2,1,0:T(8,128)(2,1)} %join.4), channel_id=1, source_target_pairs={{0,1},{1,0},{2,3},{3,2},{4,5},{5,4},{6,7},{7,6},{8,9},{9,8},{10,11... | collective-permute-start | bytes 6291464 | tf_op jit(solution)/shard_map/ppermute | solution.py:977
  158.7 25.5 %collective-permute-start.8 = (bf16[8,1024,128]{2,1,0:T(8,128)(2,1)}, bf16[8,1024,128]{2,1,0:T(8,128)(2,1)}, u32[]{:S(2)}, u32[]{:S(2)}) collective-permute-start(bf16[8,1024,128]{2,1,0:T(8,128)(2,1)} %join.4), channel_id=1, source_target_pairs={{0,16},{1,9},{2,18},{3,11},{4,20},{5,13},{6,22},{7,15},{8,24},{9,1... | collective-permute-start | bytes 6291464 | tf_op jit(solution)/shard_map/ppermute | solution.py:977
  159.9 52.7 %all-to-all-start.3 = ((bf16[4,2048,128]{2,1,0:T(8,128)(2,1)}), bf16[4,2048,128]{2,1,0:T(8,128)(2,1)}, u32[]{:S(2)}, u32[]{:S(2)}) async-start(bf16[4,2048,128]{2,1,0:T(8,128)(2,1)} %pick.3), calls=%async_computation.3 | async-start | bytes 4194304 | tf_op jit(solution)/shard_map/all_to_all | solution.py:1016
  184.1 14.6 %collective-permute-start.10 = (bf16[8,1024,128]{2,1,0:T(8,128)(2,1)}, bf16[8,1024,128]{2,1,0:T(8,128)(2,1)}, u32[]{:S(2)}, u32[]{:S(2)}) collective-permute-start(bf16[8,1024,128]{2,1,0:T(8,128)(2,1)} %collective-permute-done.8), channel_id=1, source_target_pairs={{0,1},{1,0},{2,3},{3,2},{4,5},{5,4},{6,7},{7,6},{8,9},{9,8},{10,11... | collective-permute-start | bytes 6291464 | tf_op jit(solution)/shard_map/ppermute | solution.py:977
  245.8 19.0 %collective-permute-start.11 = (bf16[16,2,2,128,128]{4,3,2,1,0:T(8,128)(2,1)}, bf16[16,2,2,128,128]{4,3,2,1,0:T(8,128)(2,1)S(1)}, u32[]{:S(2)}, u32[]{:S(2)}) collective-permute-start(bf16[16,2,2,128,128]{4,3,2,1,0:T(8,128)(2,1)} %get-tuple-element.225), channel_id=1, source_target_pairs={{0,1},{1,0},{2,3},{3,2},{4,5},{5,4},{6,7},{7,6},{8,9},{9,8},{10,11... | collective-permute-start | bytes 6291464 | tf_op jit(solution)/shard_map/ppermute | solution.py:977
  266.2 27.8 %collective-permute-start.15 = (bf16[16,2,2,128,128]{4,3,2,1,0:T(8,128)(2,1)}, bf16[16,2,2,128,128]{4,3,2,1,0:T(8,128)(2,1)S(1)}, u32[]{:S(2)}, u32[]{:S(2)}) collective-permute-start(bf16[16,2,2,128,128]{4,3,2,1,0:T(8,128)(2,1)} %get-tuple-element.237), channel_id=1, source_target_pairs={{0,1},{1,0},{2,3},{3,2},{4,5},{5,4},{6,7},{7,6},{8,9},{9,8},{10,11... | collective-permute-start | bytes 6291464 | tf_op jit(solution)/shard_map/ppermute | solution.py:977
  269.6 20.6 %collective-permute-start.12 = (bf16[2048,128]{1,0:T(8,128)(2,1)}, bf16[2048,128]{1,0:T(8,128)(2,1)S(1)}, u32[]{:S(2)}, u32[]{:S(2)}) collective-permute-start(bf16[2048,128]{1,0:T(8,128)(2,1)} %bitcast.157), channel_id=1, source_target_pairs={{0,8},{1,9},{2,10},{3,11},{4,12},{5,13},{6,14},{7,15},{8,0},{9,1},... | collective-permute-start | bytes 1572872 | tf_op jit(solution)/shard_map/ppermute | solution.py:977
  270.6 19.6 %collective-permute-start.13 = (bf16[2048,128]{1,0:T(8,128)(2,1)}, bf16[2048,128]{1,0:T(8,128)(2,1)S(1)}, u32[]{:S(2)}, u32[]{:S(2)}) collective-permute-start(bf16[2048,128]{1,0:T(8,128)(2,1)} %bitcast.156), channel_id=1, source_target_pairs={{0,16},{1,17},{2,18},{3,19},{4,20},{5,21},{6,22},{7,23},{8,24},{9,... | collective-permute-start | bytes 1572872 | tf_op jit(solution)/shard_map/ppermute | solution.py:977
  271.0 23.0 %collective-permute-start.14 = (bf16[2048,128]{1,0:T(8,128)(2,1)}, bf16[2048,128]{1,0:T(8,128)(2,1)S(1)}, u32[]{:S(2)}, u32[]{:S(2)}) collective-permute-start(bf16[2048,128]{1,0:T(8,128)(2,1)} %bitcast.154), channel_id=1, source_target_pairs={{0,24},{1,25},{2,26},{3,27},{4,28},{5,29},{6,30},{7,31},{8,16},{9,... | collective-permute-start | bytes 1572872 | tf_op jit(solution)/shard_map/ppermute | solution.py:977
  294.0 29.6 %collective-permute-start.19 = (bf16[16,2,2,128,128]{4,3,2,1,0:T(8,128)(2,1)}, bf16[16,2,2,128,128]{4,3,2,1,0:T(8,128)(2,1)}, u32[]{:S(2)}, u32[]{:S(2)}) collective-permute-start(bf16[16,2,2,128,128]{4,3,2,1,0:T(8,128)(2,1)} %get-tuple-element.253), channel_id=1, source_target_pairs={{0,1},{1,0},{2,3},{3,2},{4,5},{5,4},{6,7},{7,6},{8,9},{9,8},{10,11... | collective-permute-start | bytes 6291464 | tf_op jit(solution)/shard_map/ppermute | solution.py:977
  299.8 20.6 %collective-permute-start.16 = (bf16[2048,128]{1,0:T(8,128)(2,1)}, bf16[2048,128]{1,0:T(8,128)(2,1)S(1)}, u32[]{:S(2)}, u32[]{:S(2)}) collective-permute-start(bf16[2048,128]{1,0:T(8,128)(2,1)} %bitcast.155), channel_id=1, source_target_pairs={{0,8},{1,9},{2,10},{3,11},{4,12},{5,13},{6,14},{7,15},{8,0},{9,1},... | collective-permute-start | bytes 1572872 | tf_op jit(solution)/shard_map/ppermute | solution.py:977
  300.3 20.9 %collective-permute-start.17 = (bf16[2048,128]{1,0:T(8,128)(2,1)}, bf16[2048,128]{1,0:T(8,128)(2,1)S(1)}, u32[]{:S(2)}, u32[]{:S(2)}) collective-permute-start(bf16[2048,128]{1,0:T(8,128)(2,1)} %bitcast.153), channel_id=1, source_target_pairs={{0,16},{1,17},{2,18},{3,19},{4,20},{5,21},{6,22},{7,23},{8,24},{9,... | collective-permute-start | bytes 1572872 | tf_op jit(solution)/shard_map/ppermute | solution.py:977
  301.0 22.6 %collective-permute-start.18 = (bf16[2048,128]{1,0:T(8,128)(2,1)}, bf16[2048,128]{1,0:T(8,128)(2,1)S(1)}, u32[]{:S(2)}, u32[]{:S(2)}) collective-permute-start(bf16[2048,128]{1,0:T(8,128)(2,1)} %bitcast.152), channel_id=1, source_target_pairs={{0,24},{1,25},{2,26},{3,27},{4,28},{5,29},{6,30},{7,31},{8,16},{9,... | collective-permute-start | bytes 1572872 | tf_op jit(solution)/shard_map/ppermute | solution.py:977
  324.4 51.3 %all-to-all-start.4 = ((bf16[4,2048,128]{2,1,0:T(8,128)(2,1)}), bf16[4,2048,128]{2,1,0:T(8,128)(2,1)S(1)}, u32[]{:S(2)}, u32[]{:S(2)}) async-start(bf16[4,2048,128]{2,1,0:T(8,128)(2,1)} %bitcast.123), calls=%async_computation.4 | async-start | bytes 4194304 | tf_op jit(solution)/shard_map/all_to_all | solution.py:1016
  328.0 32.3 %collective-permute-start.20 = (bf16[16,2,2,128,128]{4,3,2,1,0:T(8,128)(2,1)}, bf16[16,2,2,128,128]{4,3,2,1,0:T(8,128)(2,1)}, u32[]{:S(2)}, u32[]{:S(2)}) collective-permute-start(bf16[16,2,2,128,128]{4,3,2,1,0:T(8,128)(2,1)} %get-tuple-element.255), channel_id=1, source_target_pairs={{0,1},{1,0},{2,3},{3,2},{4,5},{5,4},{6,7},{7,6},{8,9},{9,8},{10,11... | collective-permute-start | bytes 6291464 | tf_op jit(solution)/shard_map/ppermute | solution.py:977
  334.7 13.7 %collective-permute-start.21 = (bf16[2048,128]{1,0:T(8,128)(2,1)}, bf16[2048,128]{1,0:T(8,128)(2,1)S(1)}, u32[]{:S(2)}, u32[]{:S(2)}) collective-permute-start(bf16[2048,128]{1,0:T(8,128)(2,1)} %bitcast.162), channel_id=1, source_target_pairs={{0,8},{1,9},{2,10},{3,11},{4,12},{5,13},{6,14},{7,15},{8,0},{9,1},... | collective-permute-start | bytes 1572872 | tf_op jit(solution)/shard_map/ppermute | solution.py:977
  335.7 24.6 %collective-permute-start.22 = (bf16[2048,128]{1,0:T(8,128)(2,1)}, bf16[2048,128]{1,0:T(8,128)(2,1)S(1)}, u32[]{:S(2)}, u32[]{:S(2)}) collective-permute-start(bf16[2048,128]{1,0:T(8,128)(2,1)} %bitcast.160), channel_id=1, source_target_pairs={{0,16},{1,17},{2,18},{3,19},{4,20},{5,21},{6,22},{7,23},{8,24},{9,... | collective-permute-start | bytes 1572872 | tf_op jit(solution)/shard_map/ppermute | solution.py:977
  336.1 24.2 %collective-permute-start.23 = (bf16[2048,128]{1,0:T(8,128)(2,1)}, bf16[2048,128]{1,0:T(8,128)(2,1)S(1)}, u32[]{:S(2)}, u32[]{:S(2)}) collective-permute-start(bf16[2048,128]{1,0:T(8,128)(2,1)} %bitcast.158), channel_id=1, source_target_pairs={{0,24},{1,25},{2,26},{3,27},{4,28},{5,29},{6,30},{7,31},{8,16},{9,... | collective-permute-start | bytes 1572872 | tf_op jit(solution)/shard_map/ppermute | solution.py:977
  375.7 40.9 %all-to-all-start.5 = ((bf16[4,1536,128]{2,1,0:T(8,128)(2,1)}), bf16[4,1536,128]{2,1,0:T(8,128)(2,1)}, u32[]{:S(2)}, u32[]{:S(2)}) async-start(bf16[4,1536,128]{2,1,0:T(8,128)(2,1)} %bitcast.117), calls=%async_computation.5 | async-start | bytes 3145728 | tf_op jit(solution)/shard_map/all_to_all | solution.py:1016
  384.9 22.7 %collective-permute-start.26 = (bf16[2048,128]{1,0:T(8,128)(2,1)}, bf16[2048,128]{1,0:T(8,128)(2,1)S(1)}, u32[]{:S(2)}, u32[]{:S(2)}) collective-permute-start(bf16[2048,128]{1,0:T(8,128)(2,1)} %bitcast.159), channel_id=1, source_target_pairs={{0,24},{1,25},{2,26},{3,27},{4,28},{5,29},{6,30},{7,31},{8,16},{9,... | collective-permute-start | bytes 1572872 | tf_op jit(solution)/shard_map/ppermute | solution.py:977
  416.5 29.8 %all-to-all-start.6 = ((bf16[4,1536,128]{2,1,0:T(8,128)(2,1)}), bf16[4,1536,128]{2,1,0:T(8,128)(2,1)S(1)}, u32[]{:S(2)}, u32[]{:S(2)}) async-start(bf16[4,1536,128]{2,1,0:T(8,128)(2,1)} %all-to-all-done.5), calls=%async_computation.6 | async-start | bytes 3145728 | tf_op jit(solution)/shard_map/all_to_all | solution.py:1019
  423.4 17.1 %collective-permute-start.28 = (bf16[512,128]{1,0:T(8,128)(2,1)}, bf16[512,128]{1,0:T(8,128)(2,1)S(1)}, u32[]{:S(2)}, u32[]{:S(2)}) collective-permute-start(bf16[512,128]{1,0:T(8,128)(2,1)} %bitcast.167), channel_id=1, source_target_pairs={{0,2},{1,3},{2,8},{3,9},{4,22},{5,23},{6,28},{7,29},{8,0},{9,1},{1... | collective-permute-start | bytes 393224 | tf_op jit(solution)/shard_map/ppermute | solution.py:977
  425.3 15.2 %collective-permute-start.27 = (bf16[512,128]{1,0:T(8,128)(2,1)}, bf16[512,128]{1,0:T(8,128)(2,1)S(1)}, u32[]{:S(2)}, u32[]{:S(2)}) collective-permute-start(bf16[512,128]{1,0:T(8,128)(2,1)} %bitcast.166), channel_id=1, source_target_pairs={{0,0},{1,1},{2,10},{3,11},{4,20},{5,21},{6,30},{7,31},{8,2},{9,3},... | collective-permute-start | bytes 393224 | tf_op jit(solution)/shard_map/ppermute | solution.py:977
  430.6 15.8 %collective-permute-start.30 = (bf16[512,128]{1,0:T(8,128)(2,1)}, bf16[512,128]{1,0:T(8,128)(2,1)}, u32[]{:S(2)}, u32[]{:S(2)}) collective-permute-start(bf16[512,128]{1,0:T(8,128)(2,1)} %bitcast.164), channel_id=1, source_target_pairs={{0,6},{1,7},{2,12},{3,13},{4,18},{5,19},{6,24},{7,25},{8,4},{9,5},... | collective-permute-start | bytes 393224 | tf_op jit(solution)/shard_map/ppermute | solution.py:977
  (39 other events, 406.7 us)

commit v14 on v13

--- a/solution.py
+++ b/solution.py
@@ -1019,7 +1019,6 @@
         return lax.all_to_all(value, "section", split_axis=0, concat_axis=0, tiled=True)
 
     half_layers = layer_count // 2
-    groups = [tuple(range(half_layers)), tuple(range(half_layers, layer_count))]
     fold = size // blocks
     columns = jnp.arange(size)
     order = (columns[:, None] == (columns % blocks) * fold + columns // blocks).astype(jnp.bfloat16)
@@ -1037,36 +1036,46 @@
     first = to_planes(first)
     first, second = tie((first, second))
     second = to_planes(second)
-    lowest = first[:, :cut]
-    beside = move(lowest, routes["across"][0])
+    lowest = [first[:, at * layer_rows : (at + 1) * layer_rows] for at in range(half_layers)]
+    beside = [move(value, routes["across"][0]) for value in lowest[:2]]
     gains = first[:, cut:].reshape(width, layer_count + 1, local_blocks, size)
     gains = gains.transpose(1, 3, 0, 2).reshape(layer_count + 1, size, blocks)
     end_gain = gains[layer_count].reshape(size, CHUNKS, blocks // CHUNKS).transpose(1, 0, 2)
     end_gain = end_gain.astype(jnp.float32)
     lowest, beside, gains, end_gain = tie((lowest, beside, gains, end_gain))
-    first_two = gather_two(joined([lowest, beside]))
-    first_two, second, target_sent = tie((first_two, second, target_sent))
+    flying = {0: gather_two(joined([lowest[0], beside[0]]))}
+    flying, second, target_sent = tie((flying, second, target_sent))
+    for layer in range(half_layers, layer_count):
+        at = (layer - half_layers) * layer_rows
+        lowest.append(second[:, at : at + layer_rows])
     target = to_planes(target_sent).reshape(-1, wide)
-    weights = [as_weights(gather_three(*first_two))]
-    later = gather_one(second)
-    weights, later = tie((weights, later))
+    weights = [as_weights(gather_three(*flying.pop(0)))]
+    flying[1] = gather_two(joined([lowest[1], beside[1]]))
+    steps = {2: (lowest[2], move(lowest[2], routes["across"][0]))}
+    weights, flying, steps = tie((weights, flying, steps))
 
     residual = patch_came
-    flying = gather_two(later)
     sums = jnp.zeros((8, wide), jnp.float32)
     stored = []
     for layer in range(layer_count):
-        group = 0 if layer in groups[0] else 1
+        ahead = {}
+        if layer + 1 < layer_count:
+            ahead["weights"] = gather_three(*flying.pop(layer + 1))
+        if layer + 2 < layer_count:
+            ahead["two"] = gather_two(joined(list(steps.pop(layer + 2))))
+        if layer + 3 < layer_count:
+            ahead["one"] = (lowest[layer + 3], move(lowest[layer + 3], routes["across"][0]))
         following, u, z, slope, scale, sums = run_forward(
-            table, gains[layer], sums, residual, weights[group], layer - groups[group][0]
+            table, gains[layer], sums, residual, weights[layer], 0
         )
         stored.append(((slope, z, u), scale, residual))
-        residual = following
-        if layer == 0:
-            residual, sums, flying = tie((residual, sums, flying))
-            weights.append(as_weights(gather_three(*flying)))
-        if layer == groups[0][-1]:
-            residual, sums, weights[1] = tie((residual, sums, weights[1]))
+        residual, sums, ahead = tie((following, sums, ahead))
+        if layer + 1 < layer_count:
+            weights.append(as_weights(ahead["weights"]))
+        if layer + 2 < layer_count:
+            flying[layer + 2] = ahead["two"]
+        if layer + 3 < layer_count:
+            steps[layer + 3] = ahead["one"]
         if layer == layer_count - 2:
             residual, sums, target = tie((residual, sums, target))
 
@@ -1075,9 +1084,6 @@
 
     def plane_sum(mine, other):
         return send(run_sum([(mine, other)], width), "sections")
-
-    def homeward(parts):
-        return move_all(run_sum(parts, width), "homes")
 
     def both_halves(whole):
         pair = (whole, move(whole, routes["cores"]))
@@ -1090,7 +1096,6 @@
         turning = layer == layer_count - 1
         last = layer == 0
         kept, scale, inputs = stored[layer]
-        group = 0 if layer in groups[0] else 1
         sources = (gradient, inputs, target) if turning else (gradient, inputs)
         underway = [(at + 1, steps[at](*state)) if at < len(steps) else (at, state) for at, state in underway]
         gradient, mine, other = run_backward(
@@ -1099,8 +1104,8 @@
             end_gain,
             scale,
             kept,
-            weights[group],
-            layer - groups[group][0],
+            weights[layer],
+            0,
             sources,
             turning,
             last,
@@ -1114,8 +1119,9 @@
     ended = tie(ended)
     ended[0] = plane_sum(*ended[0])
     others = to_planes(run_sum(ended[1:], width, apart=False))
-    ended[0], returned, others = tie((ended[0], returned, others))
-    home = homeward(ended[:1])
+    home = run_sum(ended[:1], width)
+    home, returned, others = tie((home, returned, others))
+    home = move_all(home, "homes")
     d_patches = run_combine(critic_pairs, returned)
     others = to_sections(others)
     d_patches, home, others = tie((d_patches, home, others))

time: 462 us -> 446 us (0.965)
  blocking collectives: 58.9 us -> 30.2 us
  starting transfers between devices: 65.3 us -> 71.1 us
    all_to_all x2 -> x1, blocking collectives: 58.9 us -> 30.2 us  [to_planes(): lax.all_to_all(value, 'tensor', split_axis=0, concat_axis=0, tiled=True)]
    ppermute x33 -> x41, waiting for transfers between devices: 105 us -> 100 us  [move(): return lax.ppermute(value, AXES, route)]
    all_to_all x4 -> x5, waiting for transfers between devices: 29 us -> 33.8 us  [to_planes(): lax.all_to_all(value, 'tensor', split_axis=0, concat_axis=0, tiled=True)]
    ppermute x33 -> x41, starting transfers between devices: 43.5 us -> 47 us  [move(): return lax.ppermute(value, AXES, route)]
    pallas_call x3 -> x5, Pallas kernels: 7.79 us -> 10.7 us  [joined(): pl.pallas_call(lambda *refs: join_kernel(rows, *refs), in_specs=[OUTSIDE]...]
    all_to_all x4 -> x5, starting transfers between devices: 17.3 us -> 20 us  [to_planes(): lax.all_to_all(value, 'tensor', split_axis=0, concat_axis=0, tiled=True)]
    unnamed x67 -> x79, local copies, waits for them, and re-layouts: 9.81 us -> 10.9 us
  transfers between devices with their start and end apart: 38 -> 47, of which waited for: 18 -> 22; matrix products, arithmetic and copies ran while one was open for 1% -> 1% of each run, Pallas kernels for 30% -> 33%
where the time goes in v14:
time: 446 us; the launch traced here: 441 us
  Pallas kernels  188 us (42%)
  waiting for transfers between devices  134 us (30%)
  starting transfers between devices  71.1 us (16%)
  blocking collectives  30.2 us (7%)
  local copies, waits for them, and re-layouts  14.9 us (3%)
    ppermute x41, waiting for transfers between devices, move(): return lax.ppermute(value, AXES, route)  100 us
    pallas_call x4, Pallas kernels, run_backward(): pl.pallas_call(lambda *refs: backward_kernel(turning, last, layer, len(so...  73 us
    pallas_call x4, Pallas kernels, run_forward(): pl.pallas_call(lambda *refs: forward_kernel(first, layer, len(sources), *...  55.6 us
    ppermute x41, starting transfers between devices, move(): return lax.ppermute(value, AXES, route)  47 us
    all_to_all x5, waiting for transfers between devices, to_planes(): lax.all_to_all(value, 'tensor', split_axis=0, concat_axis=0, tiled=True)  33.8 us
    all_to_all x1, blocking collectives, to_planes(): lax.all_to_all(value, 'tensor', split_axis=0, concat_axis=0, tiled=True)  30.2 us
    all_to_all x5, starting transfers between devices, to_planes(): lax.all_to_all(value, 'tensor', split_axis=0, concat_axis=0, tiled=True)  20 us
    pallas_call x6, Pallas kernels, run_sum(): pl.pallas_call(lambda *refs: sum_kernel(len(groups[0]), len(flat), *refs)...  19.7 us
  transfers between devices with their start and end apart: 47, of which 22 were waited for; matrix products, arithmetic and copies ran while one was open for 1% of the time, Pallas kernels for 33%

profile of v14, /device:TPU:5, one launch (start us, length us, event | category | flops | bytes accessed | tf_op | source)
XLA Modules:
  0.0 441.0 jit_solution(14361069050040355815)
XLA Ops:
  2.1 4.1 pick.2
  6.2 4.7 %all-to-all-start = ((bf16[4,2048,128]{2,1,0:T(8,128)(2,1)}), bf16[4,2048,128]{2,1,0:T(8,128)(2,1)S(1)}, u32[]{:S(2)}, u32[]{:S(2)}) async-start(bf16[4,2048,128]{2,1,0:T(8,128)(2,1)} %pick.2), calls=%async_computation | async-start | bytes 4194304 | tf_op jit(solution)/shard_map/all_to_all | solution.py:1016
  12.8 4.7 %pieces.1 = (bf16[2128,128]{1,0:T(8,128)(2,1)}, bf16[2128,128]{1,0:T(8,128)(2,1)}, bf16[2128,128]{1,0:T(8,128)(2,1)}, bf16[2128,128]{1,0:T(8,128)(2,1)}) custom-call(s32[3]{0:T(128)} %pad_add_fusion.1.refs_0_, bf16[128,128]{1,0:T(8,128)(2,1)} %fusion.refs_1_, bf16[4,16,128,128]{3,2,1,0:T(8,128)(2,1)} %bitcast.114, bf16[4,16,128,128]{3,2,1,0:T(8,128)(2,1)} %bitcast.115, ...), custom_call_target="tpu_custom_call" | custom-call | flops 134217728 | bytes 4194304 | tf_op jit(solution)/shard_map/pieces/pallas_call | solution.py:799
  20.2 4.1 pick.3
  24.3 6.3 %collective-permute-done.refs_2_ = bf16[2128,128]{1,0:T(8,128)(2,1)S(1)} collective-permute-done((bf16[2128,128]{1,0:T(8,128)(2,1)}, bf16[2128,128]{1,0:T(8,128)(2,1)S(1)}, u32[]{:S(2)}, u32[]{:S(2)}) %collective-permute-start) | collective-permute-done | bytes 544800 | tf_op jit(solution)/shard_map/ppermute | solution.py:977
  32.5 9.8 %collective-permute-done.2.refs_4_ = bf16[2128,128]{1,0:T(8,128)(2,1)S(1)} collective-permute-done((bf16[2128,128]{1,0:T(8,128)(2,1)}, bf16[2128,128]{1,0:T(8,128)(2,1)S(1)}, u32[]{:S(2)}, u32[]{:S(2)}) %collective-permute-start.2) | collective-permute-done | bytes 544800 | tf_op jit(solution)/shard_map/ppermute | solution.py:977
  49.0 9.6 %all-to-all-done = bf16[4,2048,128]{2,1,0:T(8,128)(2,1)S(1)} async-done(((bf16[4,2048,128]{2,1,0:T(8,128)(2,1)}), bf16[4,2048,128]{2,1,0:T(8,128)(2,1)S(1)}, u32[]{:S(2)}, u32[]{:S(2)}) %all-to-all-start) | async-done | bytes 2097184 | tf_op jit(solution)/shard_map/all_to_all | solution.py:1016
  60.0 30.2 %all_to_all.35 = bf16[4,1104,128]{2,1,0:T(8,128)(2,1)S(1)} all-to-all(bf16[4,1104,128]{2,1,0:T(8,128)(2,1)} %by_section.2), channel_id=1, replica_groups=mesh['section'=4,'tensor'=4,'dp'=2] {'tensor'}, dimensions={0} | all-to-all | bytes 2260992 | tf_op jit(solution)/shard_map/all_to_all | solution.py:1016
  98.8 5.6 %collective-permute-done.3.refs_1_ = bf16[4,512,128]{2,1,0:T(8,128)(2,1)} collective-permute-done((bf16[4,512,128]{2,1,0:T(8,128)(2,1)S(1)}, bf16[4,512,128]{2,1,0:T(8,128)(2,1)}, u32[]{:S(2)}, u32[]{:S(2)}) %collective-permute-start.3) | collective-permute-done | bytes 524320 | tf_op jit(solution)/shard_map/ppermute | solution.py:977
  113.3 7.2 %all-to-all-done.2 = bf16[4,1024,128]{2,1,0:T(8,128)(2,1)S(1)} async-done(((bf16[4,1024,128]{2,1,0:T(8,128)(2,1)}), bf16[4,1024,128]{2,1,0:T(8,128)(2,1)S(1)}, u32[]{:S(2)}, u32[]{:S(2)}) %all-to-all-start.2) | async-done | bytes 1048608 | tf_op jit(solution)/shard_map/all_to_all | solution.py:1016
  129.5 10.8 %collective-permute-done.8 = bf16[8,512,128]{2,1,0:T(8,128)(2,1)} collective-permute-done((bf16[8,512,128]{2,1,0:T(8,128)(2,1)}, bf16[8,512,128]{2,1,0:T(8,128)(2,1)}, u32[]{:S(2)}, u32[]{:S(2)}) %collective-permute-start.8) | collective-permute-done | bytes 1048608 | tf_op jit(solution)/shard_map/ppermute | solution.py:977
  147.5 14.4 %forward_layer.4 = (f32[8192,128]{1,0:T(8,128)}, bf16[8192,128]{1,0:T(8,128)(2,1)}, bf16[8192,128]{1,0:T(8,128)(2,1)}, bf16[8192,128]{1,0:T(8,128)(2,1)}, f32[8,128]{1,0:T(8,128)}, /*index=5*/f32[8,128]{1,0:T(8,128)}) custom-call(s32[3,64]{1,0:T(4,128)} %pad_add_fusion.refs_0_, f32[8,128]{1,0:T(8,128)} %broadcast_in_dim.6.refs_1_, ...), custom_call_target="tpu_custom_call" | custom-call | flops 4000000000 | bytes 20971520 | tf_op jit(solution)/shard_map/forward_layer/pallas_call | solution.py:605
  167.9 13.7 %forward_layer.5 = (f32[8192,128]{1,0:T(8,128)}, bf16[8192,128]{1,0:T(8,128)(2,1)}, bf16[8192,128]{1,0:T(8,128)(2,1)}, bf16[8192,128]{1,0:T(8,128)(2,1)}, f32[8,128]{1,0:T(8,128)}, /*index=5*/f32[8,128]{1,0:T(8,128)}) custom-call(s32[3,64]{1,0:T(4,128)} %pad_add_fusion.refs_0_, f32[8,128]{1,0:T(8,128)} %get-tuple-element.215.refs_1_, ...), custom_call_target="tpu_custom_call" | custom-call | flops 4000000000 | bytes 20971520 | tf_op jit(solution)/shard_map/forward_layer/pallas_call | solution.py:605
  182.6 13.8 %forward_layer.6 = (f32[8192,128]{1,0:T(8,128)}, bf16[8192,128]{1,0:T(8,128)(2,1)}, bf16[8192,128]{1,0:T(8,128)(2,1)}, bf16[8192,128]{1,0:T(8,128)(2,1)}, f32[8,128]{1,0:T(8,128)}, /*index=5*/f32[8,128]{1,0:T(8,128)}) custom-call(s32[3,64]{1,0:T(4,128)} %pad_add_fusion.refs_0_, f32[8,128]{1,0:T(8,128)} %get-tuple-element.232.refs_1_, ...), custom_call_target="tpu_custom_call" | custom-call | flops 4000000000 | bytes 20971520 | tf_op jit(solution)/shard_map/forward_layer/pallas_call | solution.py:605
  196.4 13.8 %forward_layer.7 = (f32[8192,128]{1,0:T(8,128)}, bf16[8192,128]{1,0:T(8,128)(2,1)}, bf16[8192,128]{1,0:T(8,128)(2,1)}, bf16[8192,128]{1,0:T(8,128)(2,1)}, f32[8,128]{1,0:T(8,128)}, /*index=5*/f32[8,128]{1,0:T(8,128)}) custom-call(s32[3,64]{1,0:T(4,128)} %pad_add_fusion.refs_0_, f32[8,128]{1,0:T(8,128)} %get-tuple-element.250.refs_1_, ...), custom_call_target="tpu_custom_call" | custom-call | flops 4000000000 | bytes 20971520 | tf_op jit(solution)/shard_map/forward_layer/pallas_call | solution.py:605
  210.2 19.6 %backward_layer.4 = (f32[8192,128]{1,0:T(8,128)}, bf16[16,2,2,128,128]{4,3,2,1,0:T(8,128)(2,1)}, bf16[16,2,2,128,128]{4,3,2,1,0:T(8,128)(2,1)}) custom-call(s32[3,64]{1,0:T(4,128)} %pad_add_fusion.refs_0_, f32[8,128]{1,0:T(8,128)} %get-tuple-element.256.refs_1_, bf16[128,64]{1,0:T(8,128)(2,1)} %get-tuple-element.353.refs_2_, f32[8,128,8]{2,1,0:T(8,128)} %bitcast.101, ...), custom_call_target="tpu_custom_call" | custom-call | flops 5000000000 | bytes 31457280 | tf_op jit(solution)/shard_map/backward_layer/pallas_call | solution.py:636
  230.4 17.9 %backward_layer.5 = (f32[8192,128]{1,0:T(8,128)}, bf16[16,2,2,128,128]{4,3,2,1,0:T(8,128)(2,1)}, bf16[16,2,2,128,128]{4,3,2,1,0:T(8,128)(2,1)}) custom-call(s32[3,64]{1,0:T(4,128)} %pad_add_fusion.refs_0_, f32[8,128]{1,0:T(8,128)} %get-tuple-element.238.refs_1_, bf16[128,64]{1,0:T(8,128)(2,1)} %get-tuple-element.354.refs_2_, f32[8,128,8]{2,1,0:T(8,128)} %bitcast.102, ...), custom_call_target="tpu_custom_call" | custom-call | flops 5000000000 | bytes 31457280 | tf_op jit(solution)/shard_map/backward_layer/pallas_call | solution.py:636
  255.7 17.8 %backward_layer.6 = (f32[8192,128]{1,0:T(8,128)}, bf16[16,2,2,128,128]{4,3,2,1,0:T(8,128)(2,1)}, bf16[16,2,2,128,128]{4,3,2,1,0:T(8,128)(2,1)}) custom-call(s32[3,64]{1,0:T(4,128)} %pad_add_fusion.refs_0_, f32[8,128]{1,0:T(8,128)} %get-tuple-element.221.refs_1_, bf16[128,64]{1,0:T(8,128)(2,1)} %get-tuple-element.355.refs_2_, f32[8,128,8]{2,1,0:T(8,128)} %bitcast.103, ...), custom_call_target="tpu_custom_call" | custom-call | flops 5000000000 | bytes 31457280 | tf_op jit(solution)/shard_map/backward_layer/pallas_call | solution.py:636
  273.6 4.8 %collective-permute-done.22 = bf16[2048,128]{1,0:T(8,128)(2,1)S(1)} collective-permute-done((bf16[2048,128]{1,0:T(8,128)(2,1)}, bf16[2048,128]{1,0:T(8,128)(2,1)S(1)}, u32[]{:S(2)}, u32[]{:S(2)}) %collective-permute-start.22) | collective-permute-done | bytes 524320 | tf_op jit(solution)/shard_map/ppermute | solution.py:977
  285.9 17.6 %backward_layer.7 = (bf16[8192,128]{1,0:T(8,128)(2,1)}, bf16[16,2,2,128,128]{4,3,2,1,0:T(8,128)(2,1)}, bf16[16,2,2,128,128]{4,3,2,1,0:T(8,128)(2,1)}) custom-call(s32[3,64]{1,0:T(4,128)} %pad_add_fusion.refs_0_, f32[8,128]{1,0:T(8,128)} %get-tuple-element.203.refs_1_, bf16[128,64]{1,0:T(8,128)(2,1)} %get-tuple-element.356.refs_2_, f32[8,128,8]{2,1,0:T(8,128)} %bitcast.104, ...), custom_call_target="tpu_custom_call" | custom-call | flops 5000000000 | bytes 31457280 | tf_op jit(solution)/shard_map/backward_layer/pallas_call | solution.py:636
  321.2 11.1 %collective-permute-done.29 = bf16[2048,128]{1,0:T(8,128)(2,1)S(1)} collective-permute-done((bf16[2048,128]{1,0:T(8,128)(2,1)}, bf16[2048,128]{1,0:T(8,128)(2,1)S(1)}, u32[]{:S(2)}, u32[]{:S(2)}) %collective-permute-start.29) | collective-permute-done | bytes 524320 | tf_op jit(solution)/shard_map/ppermute | solution.py:977
  332.3 11.4 %collective-permute-done.30 = bf16[2048,128]{1,0:T(8,128)(2,1)S(1)} collective-permute-done((bf16[2048,128]{1,0:T(8,128)(2,1)}, bf16[2048,128]{1,0:T(8,128)(2,1)S(1)}, u32[]{:S(2)}, u32[]{:S(2)}) %collective-permute-start.30) | collective-permute-done | bytes 524320 | tf_op jit(solution)/shard_map/ppermute | solution.py:977
  348.8 10.7 %all-to-all-done.4.came_ref = bf16[4,2048,128]{2,1,0:T(8,128)(2,1)S(1)} async-done(((bf16[4,2048,128]{2,1,0:T(8,128)(2,1)}), bf16[4,2048,128]{2,1,0:T(8,128)(2,1)S(1)}, u32[]{:S(2)}, u32[]{:S(2)}) %all-to-all-start.4) | async-done | bytes 2097184 | tf_op jit(solution)/shard_map/all_to_all | solution.py:1016
  359.5 4.4 all-to-all-start.5
  369.9 9.6 %collective-permute-done.32 = bf16[2048,128]{1,0:T(8,128)(2,1)S(1)} collective-permute-done((bf16[2048,128]{1,0:T(8,128)(2,1)}, bf16[2048,128]{1,0:T(8,128)(2,1)S(1)}, u32[]{:S(2)}, u32[]{:S(2)}) %collective-permute-start.32) | collective-permute-done | bytes 524320 | tf_op jit(solution)/shard_map/ppermute | solution.py:977
  380.4 10.6 %collective-permute-done.34 = bf16[2048,128]{1,0:T(8,128)(2,1)S(1)} collective-permute-done((bf16[2048,128]{1,0:T(8,128)(2,1)}, bf16[2048,128]{1,0:T(8,128)(2,1)S(1)}, u32[]{:S(2)}, u32[]{:S(2)}) %collective-permute-start.34) | collective-permute-done | bytes 524320 | tf_op jit(solution)/shard_map/ppermute | solution.py:977
  394.2 6.2 %all-to-all-done.5 = bf16[4,1536,128]{2,1,0:T(8,128)(2,1)} async-done(((bf16[4,1536,128]{2,1,0:T(8,128)(2,1)}), bf16[4,1536,128]{2,1,0:T(8,128)(2,1)}, u32[]{:S(2)}, u32[]{:S(2)}) %all-to-all-start.5) | async-done | bytes 1572896 | tf_op jit(solution)/shard_map/all_to_all | solution.py:1016
  400.4 4.1 all-to-all-start.6
  406.5 4.2 collective-permute-start.36
  412.6 5.2 %collective-permute-start.38 = (bf16[512,128]{1,0:T(8,128)(2,1)S(1)}, bf16[512,128]{1,0:T(8,128)(2,1)}, u32[]{:S(2)}, u32[]{:S(2)}) collective-permute-start(bf16[512,128]{1,0:T(8,128)(2,1)S(1)} %bitcast.168), channel_id=1, source_target_pairs={{0,6},{1,7},{2,12},{3,13},{4,18},{5,19},{6,24},{7,25},{8,4},{9,5},... | collective-permute-start | bytes 393224 | tf_op jit(solution)/shard_map/ppermute | solution.py:977
  423.8 4.1 collective-permute-done.38.refs_3_
  434.9 5.9 %assemble.1 = (f32[4,16,128,128]{3,2,1,0:T(8,128)}, f32[4,16,128,128]{3,2,1,0:T(8,128)}) custom-call(s32[3]{0:T(128)} %pad_add_fusion.1.refs_0_, bf16[128,128]{1,0:T(8,128)(2,1)} %fusion.refs_1_, bf16[4,1,2,2,128,128]{5,4,3,2,1,0:T(8,128)(2,1)} %bitcast.116, bf16[4,1,2,2,128,128]{5,4,3,2,1,0:T(8,128)(2,1)} %bitcast.131, ...), custom_call_target="tpu_custom_call" | custom-call | bytes 12582912 | tf_op jit(solution)/shard_map/assemble/pallas_call | solution.py:920
  (186 shorter events, 121.3 us)
Async XLA Ops:
  6.2 52.4 %all-to-all-start = ((bf16[4,2048,128]{2,1,0:T(8,128)(2,1)}), bf16[4,2048,128]{2,1,0:T(8,128)(2,1)S(1)}, u32[]{:S(2)}, u32[]{:S(2)}) async-start(bf16[4,2048,128]{2,1,0:T(8,128)(2,1)} %pick.2), calls=%async_computation | async-start | bytes 4194304 | tf_op jit(solution)/shard_map/all_to_all | solution.py:1016
  19.0 23.3 %collective-permute-start.2 = (bf16[2128,128]{1,0:T(8,128)(2,1)}, bf16[2128,128]{1,0:T(8,128)(2,1)S(1)}, u32[]{:S(2)}, u32[]{:S(2)}) collective-permute-start(bf16[2128,128]{1,0:T(8,128)(2,1)} %get-tuple-element.182), channel_id=1, source_target_pairs={{0,24},{1,25},{2,26},{3,27},{4,28},{5,29},{6,30},{7,31},{8,16},{9,... | collective-permute-start | bytes 1634312 | tf_op jit(solution)/shard_map/ppermute | solution.py:977
  91.8 28.7 %all-to-all-start.2 = ((bf16[4,1024,128]{2,1,0:T(8,128)(2,1)}), bf16[4,1024,128]{2,1,0:T(8,128)(2,1)S(1)}, u32[]{:S(2)}, u32[]{:S(2)}) async-start(bf16[4,1024,128]{2,1,0:T(8,128)(2,1)} %by_section.3), calls=%async_computation.2 | async-start | bytes 2097152 | tf_op jit(solution)/shard_map/all_to_all | solution.py:1016
  112.6 16.9 %collective-permute-start.9 = (bf16[8,512,128]{2,1,0:T(8,128)(2,1)}, bf16[8,512,128]{2,1,0:T(8,128)(2,1)}, u32[]{:S(2)}, u32[]{:S(2)}) collective-permute-start(bf16[8,512,128]{2,1,0:T(8,128)(2,1)} %join.6), channel_id=1, source_target_pairs={{0,1},{1,0},{2,3},{3,2},{4,5},{5,4},{6,7},{7,6},{8,9},{9,8},{10,11... | collective-permute-start | bytes 3145736 | tf_op jit(solution)/shard_map/ppermute | solution.py:977
  112.7 27.6 %collective-permute-start.8 = (bf16[8,512,128]{2,1,0:T(8,128)(2,1)}, bf16[8,512,128]{2,1,0:T(8,128)(2,1)}, u32[]{:S(2)}, u32[]{:S(2)}) collective-permute-start(bf16[8,512,128]{2,1,0:T(8,128)(2,1)} %join.6), channel_id=1, source_target_pairs={{0,16},{1,9},{2,18},{3,11},{4,20},{5,13},{6,22},{7,15},{8,24},{9,1... | collective-permute-start | bytes 3145736 | tf_op jit(solution)/shard_map/ppermute | solution.py:977
  123.5 16.9 %collective-permute-start.7 = (bf16[8,512,128]{2,1,0:T(8,128)(2,1)}, bf16[8,512,128]{2,1,0:T(8,128)(2,1)}, u32[]{:S(2)}, u32[]{:S(2)}) collective-permute-start(bf16[8,512,128]{2,1,0:T(8,128)(2,1)} %collective-permute-done.5), channel_id=1, source_target_pairs={{0,1},{1,0},{2,3},{3,2},{4,5},{5,4},{6,7},{7,6},{8,9},{9,8},{10,11... | collective-permute-start | bytes 3145736 | tf_op jit(solution)/shard_map/ppermute | solution.py:977
  124.5 15.8 %collective-permute-start.10 = (bf16[4,512,128]{2,1,0:T(8,128)(2,1)S(1)}, bf16[4,512,128]{2,1,0:T(8,128)(2,1)}, u32[]{:S(2)}, u32[]{:S(2)}) collective-permute-start(bf16[4,512,128]{2,1,0:T(8,128)(2,1)S(1)} %get-tuple-element.210.refs_0_), channel_id=1, source_target_pairs={{0,8},{1,17},{2,10},{3,19},{4,12},{5,21},{6,14},{7,23},{8,0},{9,25... | collective-permute-start | bytes 1572872 | tf_op jit(solution)/shard_map/ppermute | solution.py:977
  125.7 70.7 %all-to-all-start.3 = ((bf16[4,2048,128]{2,1,0:T(8,128)(2,1)}), bf16[4,2048,128]{2,1,0:T(8,128)(2,1)S(1)}, u32[]{:S(2)}, u32[]{:S(2)}) async-start(bf16[4,2048,128]{2,1,0:T(8,128)(2,1)} %pick.3), calls=%async_computation.3 | async-start | bytes 4194304 | tf_op jit(solution)/shard_map/all_to_all | solution.py:1016
  142.6 19.4 %collective-permute-start.13 = (bf16[8,512,128]{2,1,0:T(8,128)(2,1)}, bf16[8,512,128]{2,1,0:T(8,128)(2,1)}, u32[]{:S(2)}, u32[]{:S(2)}) collective-permute-start(bf16[8,512,128]{2,1,0:T(8,128)(2,1)} %join.7), channel_id=1, source_target_pairs={{0,1},{1,0},{2,3},{3,2},{4,5},{5,4},{6,7},{7,6},{8,9},{9,8},{10,11... | collective-permute-start | bytes 3145736 | tf_op jit(solution)/shard_map/ppermute | solution.py:977
  143.6 19.9 %collective-permute-start.12 = (bf16[8,512,128]{2,1,0:T(8,128)(2,1)}, bf16[8,512,128]{2,1,0:T(8,128)(2,1)}, u32[]{:S(2)}, u32[]{:S(2)}) collective-permute-start(bf16[8,512,128]{2,1,0:T(8,128)(2,1)} %join.7), channel_id=1, source_target_pairs={{0,16},{1,9},{2,18},{3,11},{4,20},{5,13},{6,22},{7,15},{8,24},{9,1... | collective-permute-start | bytes 3145736 | tf_op jit(solution)/shard_map/ppermute | solution.py:977
  144.8 18.7 %collective-permute-start.14 = (bf16[8,512,128]{2,1,0:T(8,128)(2,1)}, bf16[8,512,128]{2,1,0:T(8,128)(2,1)}, u32[]{:S(2)}, u32[]{:S(2)}) collective-permute-start(bf16[8,512,128]{2,1,0:T(8,128)(2,1)} %collective-permute-done.8), channel_id=1, source_target_pairs={{0,1},{1,0},{2,3},{3,2},{4,5},{5,4},{6,7},{7,6},{8,9},{9,8},{10,11... | collective-permute-start | bytes 3145736 | tf_op jit(solution)/shard_map/ppermute | solution.py:977
  145.6 16.3 %collective-permute-start.11 = (bf16[4,512,128]{2,1,0:T(8,128)(2,1)S(1)}, bf16[4,512,128]{2,1,0:T(8,128)(2,1)S(1)}, u32[]{:S(2)}, u32[]{:S(2)}) collective-permute-start(bf16[4,512,128]{2,1,0:T(8,128)(2,1)S(1)} %get-tuple-element.227.refs_0_), channel_id=1, source_target_pairs={{0,8},{1,17},{2,10},{3,19},{4,12},{5,21},{6,14},{7,23},{8,0},{9,25... | collective-permute-start | bytes 1572872 | tf_op jit(solution)/shard_map/ppermute | solution.py:977
  165.7 15.9 %collective-permute-start.16 = (bf16[8,512,128]{2,1,0:T(8,128)(2,1)}, bf16[8,512,128]{2,1,0:T(8,128)(2,1)}, u32[]{:S(2)}, u32[]{:S(2)}) collective-permute-start(bf16[8,512,128]{2,1,0:T(8,128)(2,1)} %join.8), channel_id=1, source_target_pairs={{0,1},{1,0},{2,3},{3,2},{4,5},{5,4},{6,7},{7,6},{8,9},{9,8},{10,11... | collective-permute-start | bytes 3145736 | tf_op jit(solution)/shard_map/ppermute | solution.py:977
  229.9 18.5 %collective-permute-start.19 = (bf16[16,2,2,128,128]{4,3,2,1,0:T(8,128)(2,1)}, bf16[16,2,2,128,128]{4,3,2,1,0:T(8,128)(2,1)S(1)}, u32[]{:S(2)}, u32[]{:S(2)}) collective-permute-start(bf16[16,2,2,128,128]{4,3,2,1,0:T(8,128)(2,1)} %get-tuple-element.267), channel_id=1, source_target_pairs={{0,1},{1,0},{2,3},{3,2},{4,5},{5,4},{6,7},{7,6},{8,9},{9,8},{10,11... | collective-permute-start | bytes 6291464 | tf_op jit(solution)/shard_map/ppermute | solution.py:977
  249.7 28.7 %collective-permute-start.23 = (bf16[16,2,2,128,128]{4,3,2,1,0:T(8,128)(2,1)}, bf16[16,2,2,128,128]{4,3,2,1,0:T(8,128)(2,1)S(1)}, u32[]{:S(2)}, u32[]{:S(2)}) collective-permute-start(bf16[16,2,2,128,128]{4,3,2,1,0:T(8,128)(2,1)} %get-tuple-element.279), channel_id=1, source_target_pairs={{0,1},{1,0},{2,3},{3,2},{4,5},{5,4},{6,7},{7,6},{8,9},{9,8},{10,11... | collective-permute-start | bytes 6291464 | tf_op jit(solution)/shard_map/ppermute | solution.py:977
  253.1 20.5 %collective-permute-start.20 = (bf16[2048,128]{1,0:T(8,128)(2,1)}, bf16[2048,128]{1,0:T(8,128)(2,1)S(1)}, u32[]{:S(2)}, u32[]{:S(2)}) collective-permute-start(bf16[2048,128]{1,0:T(8,128)(2,1)} %bitcast.161), channel_id=1, source_target_pairs={{0,8},{1,9},{2,10},{3,11},{4,12},{5,13},{6,14},{7,15},{8,0},{9,1},... | collective-permute-start | bytes 1572872 | tf_op jit(solution)/shard_map/ppermute | solution.py:977
  254.0 19.5 %collective-permute-start.21 = (bf16[2048,128]{1,0:T(8,128)(2,1)}, bf16[2048,128]{1,0:T(8,128)(2,1)S(1)}, u32[]{:S(2)}, u32[]{:S(2)}) collective-permute-start(bf16[2048,128]{1,0:T(8,128)(2,1)} %bitcast.159), channel_id=1, source_target_pairs={{0,16},{1,17},{2,18},{3,19},{4,20},{5,21},{6,22},{7,23},{8,24},{9,... | collective-permute-start | bytes 1572872 | tf_op jit(solution)/shard_map/ppermute | solution.py:977
  254.9 23.5 %collective-permute-start.22 = (bf16[2048,128]{1,0:T(8,128)(2,1)}, bf16[2048,128]{1,0:T(8,128)(2,1)S(1)}, u32[]{:S(2)}, u32[]{:S(2)}) collective-permute-start(bf16[2048,128]{1,0:T(8,128)(2,1)} %bitcast.157), channel_id=1, source_target_pairs={{0,24},{1,25},{2,26},{3,27},{4,28},{5,29},{6,30},{7,31},{8,16},{9,... | collective-permute-start | bytes 1572872 | tf_op jit(solution)/shard_map/ppermute | solution.py:977
  278.4 29.1 %collective-permute-start.27 = (bf16[16,2,2,128,128]{4,3,2,1,0:T(8,128)(2,1)}, bf16[16,2,2,128,128]{4,3,2,1,0:T(8,128)(2,1)}, u32[]{:S(2)}, u32[]{:S(2)}) collective-permute-start(bf16[16,2,2,128,128]{4,3,2,1,0:T(8,128)(2,1)} %get-tuple-element.295), channel_id=1, source_target_pairs={{0,1},{1,0},{2,3},{3,2},{4,5},{5,4},{6,7},{7,6},{8,9},{9,8},{10,11... | collective-permute-start | bytes 6291464 | tf_op jit(solution)/shard_map/ppermute | solution.py:977
  283.3 20.3 %collective-permute-start.24 = (bf16[2048,128]{1,0:T(8,128)(2,1)}, bf16[2048,128]{1,0:T(8,128)(2,1)S(1)}, u32[]{:S(2)}, u32[]{:S(2)}) collective-permute-start(bf16[2048,128]{1,0:T(8,128)(2,1)} %bitcast.160), channel_id=1, source_target_pairs={{0,8},{1,9},{2,10},{3,11},{4,12},{5,13},{6,14},{7,15},{8,0},{9,1},... | collective-permute-start | bytes 1572872 | tf_op jit(solution)/shard_map/ppermute | solution.py:977
  284.2 20.2 %collective-permute-start.25 = (bf16[2048,128]{1,0:T(8,128)(2,1)}, bf16[2048,128]{1,0:T(8,128)(2,1)S(1)}, u32[]{:S(2)}, u32[]{:S(2)}) collective-permute-start(bf16[2048,128]{1,0:T(8,128)(2,1)} %bitcast.158), channel_id=1, source_target_pairs={{0,16},{1,17},{2,18},{3,19},{4,20},{5,21},{6,22},{7,23},{8,24},{9,... | collective-permute-start | bytes 1572872 | tf_op jit(solution)/shard_map/ppermute | solution.py:977
  284.4 23.0 %collective-permute-start.26 = (bf16[2048,128]{1,0:T(8,128)(2,1)}, bf16[2048,128]{1,0:T(8,128)(2,1)S(1)}, u32[]{:S(2)}, u32[]{:S(2)}) collective-permute-start(bf16[2048,128]{1,0:T(8,128)(2,1)} %bitcast.156), channel_id=1, source_target_pairs={{0,24},{1,25},{2,26},{3,27},{4,28},{5,29},{6,30},{7,31},{8,16},{9,... | collective-permute-start | bytes 1572872 | tf_op jit(solution)/shard_map/ppermute | solution.py:977
  308.3 51.3 %all-to-all-start.4 = ((bf16[4,2048,128]{2,1,0:T(8,128)(2,1)}), bf16[4,2048,128]{2,1,0:T(8,128)(2,1)S(1)}, u32[]{:S(2)}, u32[]{:S(2)}) async-start(bf16[4,2048,128]{2,1,0:T(8,128)(2,1)} %bitcast.121), calls=%async_computation.4 | async-start | bytes 4194304 | tf_op jit(solution)/shard_map/all_to_all | solution.py:1016
  311.9 31.9 %collective-permute-start.28 = (bf16[16,2,2,128,128]{4,3,2,1,0:T(8,128)(2,1)}, bf16[16,2,2,128,128]{4,3,2,1,0:T(8,128)(2,1)}, u32[]{:S(2)}, u32[]{:S(2)}) collective-permute-start(bf16[16,2,2,128,128]{4,3,2,1,0:T(8,128)(2,1)} %get-tuple-element.297), channel_id=1, source_target_pairs={{0,1},{1,0},{2,3},{3,2},{4,5},{5,4},{6,7},{7,6},{8,9},{9,8},{10,11... | collective-permute-start | bytes 6291464 | tf_op jit(solution)/shard_map/ppermute | solution.py:977
  319.1 24.6 %collective-permute-start.30 = (bf16[2048,128]{1,0:T(8,128)(2,1)}, bf16[2048,128]{1,0:T(8,128)(2,1)S(1)}, u32[]{:S(2)}, u32[]{:S(2)}) collective-permute-start(bf16[2048,128]{1,0:T(8,128)(2,1)} %bitcast.164), channel_id=1, source_target_pairs={{0,16},{1,17},{2,18},{3,19},{4,20},{5,21},{6,22},{7,23},{8,24},{9,... | collective-permute-start | bytes 1572872 | tf_op jit(solution)/shard_map/ppermute | solution.py:977
  319.9 23.8 %collective-permute-start.31 = (bf16[2048,128]{1,0:T(8,128)(2,1)}, bf16[2048,128]{1,0:T(8,128)(2,1)S(1)}, u32[]{:S(2)}, u32[]{:S(2)}) collective-permute-start(bf16[2048,128]{1,0:T(8,128)(2,1)} %bitcast.162), channel_id=1, source_target_pairs={{0,24},{1,25},{2,26},{3,27},{4,28},{5,29},{6,30},{7,31},{8,16},{9,... | collective-permute-start | bytes 1572872 | tf_op jit(solution)/shard_map/ppermute | solution.py:977
  359.5 40.9 %all-to-all-start.5 = ((bf16[4,1536,128]{2,1,0:T(8,128)(2,1)}), bf16[4,1536,128]{2,1,0:T(8,128)(2,1)}, u32[]{:S(2)}, u32[]{:S(2)}) async-start(bf16[4,1536,128]{2,1,0:T(8,128)(2,1)} %bitcast.107), calls=%async_computation.5 | async-start | bytes 3145728 | tf_op jit(solution)/shard_map/all_to_all | solution.py:1016
  369.3 21.7 %collective-permute-start.34 = (bf16[2048,128]{1,0:T(8,128)(2,1)}, bf16[2048,128]{1,0:T(8,128)(2,1)S(1)}, u32[]{:S(2)}, u32[]{:S(2)}) collective-permute-start(bf16[2048,128]{1,0:T(8,128)(2,1)} %bitcast.163), channel_id=1, source_target_pairs={{0,24},{1,25},{2,26},{3,27},{4,28},{5,29},{6,30},{7,31},{8,16},{9,... | collective-permute-start | bytes 1572872 | tf_op jit(solution)/shard_map/ppermute | solution.py:977
  400.4 27.6 %all-to-all-start.6 = ((bf16[4,1536,128]{2,1,0:T(8,128)(2,1)}), bf16[4,1536,128]{2,1,0:T(8,128)(2,1)S(1)}, u32[]{:S(2)}, u32[]{:S(2)}) async-start(bf16[4,1536,128]{2,1,0:T(8,128)(2,1)} %all-to-all-done.5), calls=%async_computation.6 | async-start | bytes 3145728 | tf_op jit(solution)/shard_map/all_to_all | solution.py:1019
  404.5 17.2 %collective-permute-start.35 = (bf16[512,128]{1,0:T(8,128)(2,1)S(1)}, bf16[512,128]{1,0:T(8,128)(2,1)S(1)}, u32[]{:S(2)}, u32[]{:S(2)}) collective-permute-start(bf16[512,128]{1,0:T(8,128)(2,1)S(1)} %bitcast.171), channel_id=1, source_target_pairs={{0,0},{1,1},{2,10},{3,11},{4,20},{5,21},{6,30},{7,31},{8,2},{9,3},... | collective-permute-start | bytes 393224 | tf_op jit(solution)/shard_map/ppermute | solution.py:977
  406.5 15.2 %collective-permute-start.36 = (bf16[512,128]{1,0:T(8,128)(2,1)S(1)}, bf16[512,128]{1,0:T(8,128)(2,1)S(1)}, u32[]{:S(2)}, u32[]{:S(2)}) collective-permute-start(bf16[512,128]{1,0:T(8,128)(2,1)S(1)} %bitcast.170), channel_id=1, source_target_pairs={{0,2},{1,3},{2,8},{3,9},{4,22},{5,23},{6,28},{7,29},{8,0},{9,1},{1... | collective-permute-start | bytes 393224 | tf_op jit(solution)/shard_map/ppermute | solution.py:977
  412.6 15.3 %collective-permute-start.38 = (bf16[512,128]{1,0:T(8,128)(2,1)S(1)}, bf16[512,128]{1,0:T(8,128)(2,1)}, u32[]{:S(2)}, u32[]{:S(2)}) collective-permute-start(bf16[512,128]{1,0:T(8,128)(2,1)S(1)} %bitcast.168), channel_id=1, source_target_pairs={{0,6},{1,7},{2,12},{3,13},{4,18},{5,19},{6,24},{7,25},{8,4},{9,5},... | collective-permute-start | bytes 393224 | tf_op jit(solution)/shard_map/ppermute | solution.py:977
  (54 other events, 521.4 us)

commit v15 on v14

--- a/solution.py
+++ b/solution.py
@@ -455,7 +455,7 @@
         wait_chunks(source, target, out_sems.at[at])
 
 
-def backward_kernel(turning, last, layer, inputs, table_ref, scale_ref, gain_ref, end_gain_ref, *refs):
+def backward_kernel(turning, last, home_row, layer, inputs, table_ref, scale_ref, gain_ref, end_gain_ref, *refs):
     sources, refs = refs[:inputs], refs[inputs:]
     slope_ref, z_ref, u_ref = sources[:3]
     parts, sources = sources[3 : 3 + PARTS], sources[3 + PARTS :]
@@ -521,7 +521,7 @@
 
     def right(block, nth, total):
         rows = block_rows(block, size)
-        place, home = table_ref[0, block], table_ref[2 if last else 1, block]
+        place, home = table_ref[0, block], table_ref[home_row, block]
         at = (place // chunk_blocks, 1, place % chunk_blocks)
         to = (home // chunk_blocks, 1, home % chunk_blocks)
         if turning:
@@ -555,7 +555,7 @@
 
     def left(block, nth, carry):
         rows = block_rows(block, size)
-        place, home = table_ref[0, block], table_ref[2 if last else 1, block]
+        place, home = table_ref[0, block], table_ref[home_row, block]
         at = (place // chunk_blocks, 0, place % chunk_blocks)
         to = (home // chunk_blocks, 0, home % chunk_blocks)
         arrived = [mid[pl.ds(q * blocks + block, blocks, stride=size), :] for q in range(fold)]
@@ -627,14 +627,14 @@
     )(table, sums, gain, *sources)
 
 
-def run_backward(table, gain, end_gain, scale, kept, weights, layer, sources, turning, last):
+def run_backward(table, gain, end_gain, scale, kept, weights, layer, sources, turning, last, home_row):
     whole = kept[0].shape
     sources = (*kept, *weights, *sources)
     held = (PARTS * weights[0].shape[0],) + weights[0].shape[2:]
     half = (held[0] // 2,) + held[1:]
     out_shape = [shape_of(whole, jnp.bfloat16 if last else jnp.float32)] + [shape_of(half, jnp.bfloat16)] * 2
     return pl.pallas_call(
-        lambda *refs: backward_kernel(turning, last, layer, len(sources), *refs),
+        lambda *refs: backward_kernel(turning, last, home_row, layer, len(sources), *refs),
         in_specs=[SMEM] + [INSIDE] * 3 + [OUTSIDE] * len(sources),
         out_specs=[OUTSIDE] * len(out_shape),
         out_shape=out_shape,
@@ -982,9 +982,6 @@
     def send(values, name):
         return [values[0]] + [move(values[k], routes[name][k]) for k in range(1, width)]
 
-    def gather_one(mine):
-        return joined([mine, move(mine, routes["across"][0])])
-
     def gather_two(pair):
         return pair, move(pair, routes["across"][1]), move(pair, routes["cores"])
 
@@ -1019,6 +1016,7 @@
         return lax.all_to_all(value, "section", split_axis=0, concat_axis=0, tiled=True)
 
     half_layers = layer_count // 2
+    groups = [tuple(range(half_layers)), tuple(range(half_layers, layer_count))]
     fold = size // blocks
     columns = jnp.arange(size)
     order = (columns[:, None] == (columns % blocks) * fold + columns // blocks).astype(jnp.bfloat16)
@@ -1109,6 +1107,7 @@
             sources,
             turning,
             last,
+            2 if layer < half_layers else 1,
         )
         gradient, mine, other, states = tie((gradient, mine, other, [state for _, state in underway]))
         underway = [(at, state) for (at, _), state in zip(underway, states)]
@@ -1116,10 +1115,13 @@
 
     returned = to_planes(gradient.reshape(width, feat_local, wide))
     ended = [steps[at](*state) if at < len(steps) else state for at, state in underway][::-1]
-    ended = tie(ended)
-    ended[0] = plane_sum(*ended[0])
-    others = to_planes(run_sum(ended[1:], width, apart=False))
-    home = run_sum(ended[:1], width)
+    others = run_sum(ended[half_layers:], width, apart=False)
+    ended, others = tie((ended, others))
+    payload = run_sum([ended[0]], width)
+    payload, others = tie((payload, others))
+    ended[0] = send(payload, "sections")
+    others = to_planes(others)
+    home = run_sum(ended[:half_layers], width)
     home, returned, others = tie((home, returned, others))
     home = move_all(home, "homes")
     d_patches = run_combine(critic_pairs, returned)
@@ -1128,7 +1130,7 @@
     homes_of = both_halves(joined(home)) + both_halves(others)
     grad_factor = 1.0 / math.sqrt(2 * tok_rows * width * replicas)
     grad_left, grad_right = run_assemble(
-        place, order, homes_of, [(0,), tuple(range(1, layer_count))], grad_factor
+        place, order, homes_of, groups, grad_factor
     )
     return (d_patches, grad_left[None], grad_right[None])
 

time: 446 us -> 451 us (1.011)
  waiting for transfers between devices: 134 us -> 140 us
    ppermute x41, waiting for transfers between devices: 100 us -> 111 us  [move(): return lax.ppermute(value, AXES, route)]
    all_to_all x5, waiting for transfers between devices: 33.8 us -> 28.9 us  [to_planes(): lax.all_to_all(value, 'tensor', split_axis=0, concat_axis=0, tiled=True)]
    unnamed x79 -> x81, local copies, waits for them, and re-layouts: 10.9 us -> 10.3 us
  transfers between devices with their start and end apart: 47 -> 47, of which waited for: 22 -> 24; matrix products, arithmetic and copies ran while one was open for 1% -> 1% of each run, Pallas kernels for 33% -> 32%
where the time goes in v15:
time: 451 us; the launch traced here: 449 us
  Pallas kernels  189 us (42%)
  waiting for transfers between devices  140 us (31%)
  starting transfers between devices  72.2 us (16%)
  blocking collectives  30.2 us (7%)
  local copies, waits for them, and re-layouts  14.3 us (3%)
    ppermute x41, waiting for transfers between devices, move(): return lax.ppermute(value, AXES, route)  111 us
    pallas_call x4, Pallas kernels, run_backward(): pl.pallas_call(lambda *refs: backward_kernel(turning, last, home_row, lay...  72.9 us
    pallas_call x4, Pallas kernels, run_forward(): pl.pallas_call(lambda *refs: forward_kernel(first, layer, len(sources), *...  55.6 us
    ppermute x41, starting transfers between devices, move(): return lax.ppermute(value, AXES, route)  47.8 us
    all_to_all x1, blocking collectives, to_planes(): lax.all_to_all(value, 'tensor', split_axis=0, concat_axis=0, tiled=True)  30.2 us
    all_to_all x5, waiting for transfers between devices, to_planes(): lax.all_to_all(value, 'tensor', split_axis=0, concat_axis=0, tiled=True)  28.9 us
    pallas_call x6, Pallas kernels, run_sum(): pl.pallas_call(lambda *refs: sum_kernel(len(groups[0]), len(flat), *refs)...  20.1 us
    all_to_all x5, starting transfers between devices, to_planes(): lax.all_to_all(value, 'tensor', split_axis=0, concat_axis=0, tiled=True)  19.9 us
  transfers between devices with their start and end apart: 47, of which 24 were waited for; matrix products, arithmetic and copies ran while one was open for 1% of the time, Pallas kernels for 32%

profile of v15, /device:TPU:5, one launch (start us, length us, event | category | flops | bytes accessed | tf_op | source)
XLA Modules:
  0.0 449.0 jit_solution(8891377110237631943)
XLA Ops:
  2.1 4.1 pick.2
  6.2 4.7 %all-to-all-start = ((bf16[4,2048,128]{2,1,0:T(8,128)(2,1)}), bf16[4,2048,128]{2,1,0:T(8,128)(2,1)S(1)}, u32[]{:S(2)}, u32[]{:S(2)}) async-start(bf16[4,2048,128]{2,1,0:T(8,128)(2,1)} %pick.2), calls=%async_computation | async-start | bytes 4194304 | tf_op jit(solution)/shard_map/all_to_all | solution.py:1013
  12.8 4.6 %pieces.1 = (bf16[2128,128]{1,0:T(8,128)(2,1)}, bf16[2128,128]{1,0:T(8,128)(2,1)}, bf16[2128,128]{1,0:T(8,128)(2,1)}, bf16[2128,128]{1,0:T(8,128)(2,1)}) custom-call(s32[3]{0:T(128)} %pad_add_fusion.1.refs_0_, bf16[128,128]{1,0:T(8,128)(2,1)} %fusion.refs_1_, bf16[4,16,128,128]{3,2,1,0:T(8,128)(2,1)} %bitcast.115, bf16[4,16,128,128]{3,2,1,0:T(8,128)(2,1)} %bitcast.116, ...), custom_call_target="tpu_custom_call" | custom-call | flops 134217728 | bytes 4194304 | tf_op jit(solution)/shard_map/pieces/pallas_call | solution.py:799
  20.2 4.1 pick.3
  24.3 6.3 %collective-permute-done.refs_2_ = bf16[2128,128]{1,0:T(8,128)(2,1)S(1)} collective-permute-done((bf16[2128,128]{1,0:T(8,128)(2,1)}, bf16[2128,128]{1,0:T(8,128)(2,1)S(1)}, u32[]{:S(2)}, u32[]{:S(2)}) %collective-permute-start) | collective-permute-done | bytes 544800 | tf_op jit(solution)/shard_map/ppermute | solution.py:977
  32.6 9.7 %collective-permute-done.2.refs_4_ = bf16[2128,128]{1,0:T(8,128)(2,1)S(1)} collective-permute-done((bf16[2128,128]{1,0:T(8,128)(2,1)}, bf16[2128,128]{1,0:T(8,128)(2,1)S(1)}, u32[]{:S(2)}, u32[]{:S(2)}) %collective-permute-start.2) | collective-permute-done | bytes 544800 | tf_op jit(solution)/shard_map/ppermute | solution.py:977
  49.0 9.6 %all-to-all-done = bf16[4,2048,128]{2,1,0:T(8,128)(2,1)S(1)} async-done(((bf16[4,2048,128]{2,1,0:T(8,128)(2,1)}), bf16[4,2048,128]{2,1,0:T(8,128)(2,1)S(1)}, u32[]{:S(2)}, u32[]{:S(2)}) %all-to-all-start) | async-done | bytes 2097184 | tf_op jit(solution)/shard_map/all_to_all | solution.py:1013
  59.9 30.2 %all_to_all.35 = bf16[4,1104,128]{2,1,0:T(8,128)(2,1)S(1)} all-to-all(bf16[4,1104,128]{2,1,0:T(8,128)(2,1)} %by_section.2), channel_id=1, replica_groups=mesh['section'=4,'tensor'=4,'dp'=2] {'tensor'}, dimensions={0} | all-to-all | bytes 2260992 | tf_op jit(solution)/shard_map/all_to_all | solution.py:1013
  98.8 5.6 %collective-permute-done.3.refs_1_ = bf16[4,512,128]{2,1,0:T(8,128)(2,1)} collective-permute-done((bf16[4,512,128]{2,1,0:T(8,128)(2,1)S(1)}, bf16[4,512,128]{2,1,0:T(8,128)(2,1)}, u32[]{:S(2)}, u32[]{:S(2)}) %collective-permute-start.3) | collective-permute-done | bytes 524320 | tf_op jit(solution)/shard_map/ppermute | solution.py:977
  113.3 7.2 %all-to-all-done.2 = bf16[4,1024,128]{2,1,0:T(8,128)(2,1)S(1)} async-done(((bf16[4,1024,128]{2,1,0:T(8,128)(2,1)}), bf16[4,1024,128]{2,1,0:T(8,128)(2,1)S(1)}, u32[]{:S(2)}, u32[]{:S(2)}) %all-to-all-start.2) | async-done | bytes 1048608 | tf_op jit(solution)/shard_map/all_to_all | solution.py:1013
  129.5 10.8 %collective-permute-done.8 = bf16[8,512,128]{2,1,0:T(8,128)(2,1)} collective-permute-done((bf16[8,512,128]{2,1,0:T(8,128)(2,1)}, bf16[8,512,128]{2,1,0:T(8,128)(2,1)}, u32[]{:S(2)}, u32[]{:S(2)}) %collective-permute-start.8) | collective-permute-done | bytes 1048608 | tf_op jit(solution)/shard_map/ppermute | solution.py:977
  147.5 14.4 %forward_layer.4 = (f32[8192,128]{1,0:T(8,128)}, bf16[8192,128]{1,0:T(8,128)(2,1)}, bf16[8192,128]{1,0:T(8,128)(2,1)}, bf16[8192,128]{1,0:T(8,128)(2,1)}, f32[8,128]{1,0:T(8,128)}, /*index=5*/f32[8,128]{1,0:T(8,128)}) custom-call(s32[3,64]{1,0:T(4,128)} %pad_add_fusion.refs_0_, f32[8,128]{1,0:T(8,128)} %broadcast_in_dim.6.refs_1_, ...), custom_call_target="tpu_custom_call" | custom-call | flops 4000000000 | bytes 20971520 | tf_op jit(solution)/shard_map/forward_layer/pallas_call | solution.py:605
  167.9 13.7 %forward_layer.5 = (f32[8192,128]{1,0:T(8,128)}, bf16[8192,128]{1,0:T(8,128)(2,1)}, bf16[8192,128]{1,0:T(8,128)(2,1)}, bf16[8192,128]{1,0:T(8,128)(2,1)}, f32[8,128]{1,0:T(8,128)}, /*index=5*/f32[8,128]{1,0:T(8,128)}) custom-call(s32[3,64]{1,0:T(4,128)} %pad_add_fusion.refs_0_, f32[8,128]{1,0:T(8,128)} %get-tuple-element.213.refs_1_, ...), custom_call_target="tpu_custom_call" | custom-call | flops 4000000000 | bytes 20971520 | tf_op jit(solution)/shard_map/forward_layer/pallas_call | solution.py:605
  182.6 13.8 %forward_layer.6 = (f32[8192,128]{1,0:T(8,128)}, bf16[8192,128]{1,0:T(8,128)(2,1)}, bf16[8192,128]{1,0:T(8,128)(2,1)}, bf16[8192,128]{1,0:T(8,128)(2,1)}, f32[8,128]{1,0:T(8,128)}, /*index=5*/f32[8,128]{1,0:T(8,128)}) custom-call(s32[3,64]{1,0:T(4,128)} %pad_add_fusion.refs_0_, f32[8,128]{1,0:T(8,128)} %get-tuple-element.230.refs_1_, ...), custom_call_target="tpu_custom_call" | custom-call | flops 4000000000 | bytes 20971520 | tf_op jit(solution)/shard_map/forward_layer/pallas_call | solution.py:605
  196.4 13.8 %forward_layer.7 = (f32[8192,128]{1,0:T(8,128)}, bf16[8192,128]{1,0:T(8,128)(2,1)}, bf16[8192,128]{1,0:T(8,128)(2,1)}, bf16[8192,128]{1,0:T(8,128)(2,1)}, f32[8,128]{1,0:T(8,128)}, /*index=5*/f32[8,128]{1,0:T(8,128)}) custom-call(s32[3,64]{1,0:T(4,128)} %pad_add_fusion.refs_0_, f32[8,128]{1,0:T(8,128)} %get-tuple-element.248.refs_1_, ...), custom_call_target="tpu_custom_call" | custom-call | flops 4000000000 | bytes 20971520 | tf_op jit(solution)/shard_map/forward_layer/pallas_call | solution.py:605
  210.2 19.5 %backward_layer.4 = (f32[8192,128]{1,0:T(8,128)}, bf16[16,2,2,128,128]{4,3,2,1,0:T(8,128)(2,1)}, bf16[16,2,2,128,128]{4,3,2,1,0:T(8,128)(2,1)}) custom-call(s32[3,64]{1,0:T(4,128)} %pad_add_fusion.refs_0_, f32[8,128]{1,0:T(8,128)} %get-tuple-element.254.refs_1_, bf16[128,64]{1,0:T(8,128)(2,1)} %get-tuple-element.349.refs_2_, f32[8,128,8]{2,1,0:T(8,128)} %bitcast.102, ...), custom_call_target="tpu_custom_call" | custom-call | flops 5000000000 | bytes 31457280 | tf_op jit(solution)/shard_map/backward_layer/pallas_call | solution.py:636
  230.3 17.9 %backward_layer.5 = (f32[8192,128]{1,0:T(8,128)}, bf16[16,2,2,128,128]{4,3,2,1,0:T(8,128)(2,1)}, bf16[16,2,2,128,128]{4,3,2,1,0:T(8,128)(2,1)}) custom-call(s32[3,64]{1,0:T(4,128)} %pad_add_fusion.refs_0_, f32[8,128]{1,0:T(8,128)} %get-tuple-element.236.refs_1_, bf16[128,64]{1,0:T(8,128)(2,1)} %get-tuple-element.350.refs_2_, f32[8,128,8]{2,1,0:T(8,128)} %bitcast.103, ...), custom_call_target="tpu_custom_call" | custom-call | flops 5000000000 | bytes 31457280 | tf_op jit(solution)/shard_map/backward_layer/pallas_call | solution.py:636
  255.6 17.8 %backward_layer.6 = (f32[8192,128]{1,0:T(8,128)}, bf16[16,2,2,128,128]{4,3,2,1,0:T(8,128)(2,1)}, bf16[16,2,2,128,128]{4,3,2,1,0:T(8,128)(2,1)}) custom-call(s32[3,64]{1,0:T(4,128)} %pad_add_fusion.refs_0_, f32[8,128]{1,0:T(8,128)} %get-tuple-element.219.refs_1_, bf16[128,64]{1,0:T(8,128)(2,1)} %get-tuple-element.351.refs_2_, f32[8,128,8]{2,1,0:T(8,128)} %bitcast.104, ...), custom_call_target="tpu_custom_call" | custom-call | flops 5000000000 | bytes 31457280 | tf_op jit(solution)/shard_map/backward_layer/pallas_call | solution.py:636
  273.5 4.6 %collective-permute-done.22 = bf16[2048,128]{1,0:T(8,128)(2,1)S(1)} collective-permute-done((bf16[2048,128]{1,0:T(8,128)(2,1)}, bf16[2048,128]{1,0:T(8,128)(2,1)S(1)}, u32[]{:S(2)}, u32[]{:S(2)}) %collective-permute-start.22) | collective-permute-done | bytes 524320 | tf_op jit(solution)/shard_map/ppermute | solution.py:977
  285.8 17.6 %backward_layer.7 = (bf16[8192,128]{1,0:T(8,128)(2,1)}, bf16[16,2,2,128,128]{4,3,2,1,0:T(8,128)(2,1)}, bf16[16,2,2,128,128]{4,3,2,1,0:T(8,128)(2,1)}) custom-call(s32[3,64]{1,0:T(4,128)} %pad_add_fusion.refs_0_, f32[8,128]{1,0:T(8,128)} %get-tuple-element.201.refs_1_, bf16[128,64]{1,0:T(8,128)(2,1)} %get-tuple-element.352.refs_2_, f32[8,128,8]{2,1,0:T(8,128)} %bitcast.105, ...), custom_call_target="tpu_custom_call" | custom-call | flops 5000000000 | bytes 31457280 | tf_op jit(solution)/shard_map/backward_layer/pallas_call | solution.py:636
  324.4 7.9 %collective-permute-done.29 = bf16[2048,128]{1,0:T(8,128)(2,1)S(1)} collective-permute-done((bf16[2048,128]{1,0:T(8,128)(2,1)}, bf16[2048,128]{1,0:T(8,128)(2,1)S(1)}, u32[]{:S(2)}, u32[]{:S(2)}) %collective-permute-start.29) | collective-permute-done | bytes 524320 | tf_op jit(solution)/shard_map/ppermute | solution.py:977
  332.2 11.4 %collective-permute-done.30 = bf16[2048,128]{1,0:T(8,128)(2,1)S(1)} collective-permute-done((bf16[2048,128]{1,0:T(8,128)(2,1)}, bf16[2048,128]{1,0:T(8,128)(2,1)S(1)}, u32[]{:S(2)}, u32[]{:S(2)}) %collective-permute-start.30) | collective-permute-done | bytes 524320 | tf_op jit(solution)/shard_map/ppermute | solution.py:977
  347.4 12.1 %all-to-all-done.4.came_ref = bf16[4,2048,128]{2,1,0:T(8,128)(2,1)S(1)} async-done(((bf16[4,2048,128]{2,1,0:T(8,128)(2,1)}), bf16[4,2048,128]{2,1,0:T(8,128)(2,1)S(1)}, u32[]{:S(2)}, u32[]{:S(2)}) %all-to-all-start.4) | async-done | bytes 2097184 | tf_op jit(solution)/shard_map/all_to_all | solution.py:1013
  359.4 4.3 all-to-all-start.5
  366.4 9.6 %collective-permute-done.32 = bf16[2048,128]{1,0:T(8,128)(2,1)S(1)} collective-permute-done((bf16[2048,128]{1,0:T(8,128)(2,1)}, bf16[2048,128]{1,0:T(8,128)(2,1)S(1)}, u32[]{:S(2)}, u32[]{:S(2)}) %collective-permute-start.32) | collective-permute-done | bytes 524320 | tf_op jit(solution)/shard_map/ppermute | solution.py:977
  376.9 10.7 %collective-permute-done.34 = bf16[2048,128]{1,0:T(8,128)(2,1)S(1)} collective-permute-done((bf16[2048,128]{1,0:T(8,128)(2,1)}, bf16[2048,128]{1,0:T(8,128)(2,1)S(1)}, u32[]{:S(2)}, u32[]{:S(2)}) %collective-permute-start.34) | collective-permute-done | bytes 524320 | tf_op jit(solution)/shard_map/ppermute | solution.py:977
  391.8 4.5 all-to-all-start.6
  399.8 5.2 %collective-permute-start.36 = (bf16[1024,128]{1,0:T(8,128)(2,1)S(1)}, bf16[1024,128]{1,0:T(8,128)(2,1)S(1)}, u32[]{:S(2)}, u32[]{:S(2)}) collective-permute-start(bf16[1024,128]{1,0:T(8,128)(2,1)S(1)} %bitcast.168), channel_id=1, source_target_pairs={{0,2},{1,3},{2,8},{3,9},{4,22},{5,23},{6,28},{7,29},{8,0},{9,1},{1... | collective-permute-start | bytes 786440 | tf_op jit(solution)/shard_map/ppermute | solution.py:977
  409.6 3.8 combine.1
  415.7 8.0 %collective-permute-done.36.refs_1_ = bf16[1024,128]{1,0:T(8,128)(2,1)S(1)} collective-permute-done((bf16[1024,128]{1,0:T(8,128)(2,1)S(1)}, bf16[1024,128]{1,0:T(8,128)(2,1)S(1)}, u32[]{:S(2)}, u32[]{:S(2)}) %collective-permute-start.36) | collective-permute-done | bytes 262176 | tf_op jit(solution)/shard_map/ppermute | solution.py:977
  425.8 6.4 %collective-permute-done.38.refs_3_ = bf16[1024,128]{1,0:T(8,128)(2,1)S(1)} collective-permute-done((bf16[1024,128]{1,0:T(8,128)(2,1)S(1)}, bf16[1024,128]{1,0:T(8,128)(2,1)S(1)}, u32[]{:S(2)}, u32[]{:S(2)}) %collective-permute-start.38) | collective-permute-done | bytes 262176 | tf_op jit(solution)/shard_map/ppermute | solution.py:977
  442.8 6.0 %assemble.1 = (f32[4,16,128,128]{3,2,1,0:T(8,128)}, f32[4,16,128,128]{3,2,1,0:T(8,128)}) custom-call(s32[3]{0:T(128)} %pad_add_fusion.1.refs_0_, bf16[128,128]{1,0:T(8,128)(2,1)} %fusion.refs_1_, bf16[4,2,2,2,128,128]{5,4,3,2,1,0:T(8,128)(2,1)} %bitcast.114, bf16[4,2,2,2,128,128]{5,4,3,2,1,0:T(8,128)(2,1)} %bitcast.128, ...), custom_call_target="tpu_custom_call" | custom-call | bytes 12582912 | tf_op jit(solution)/shard_map/assemble/pallas_call | solution.py:920
  (188 shorter events, 127.2 us)
Async XLA Ops:
  6.2 52.4 %all-to-all-start = ((bf16[4,2048,128]{2,1,0:T(8,128)(2,1)}), bf16[4,2048,128]{2,1,0:T(8,128)(2,1)S(1)}, u32[]{:S(2)}, u32[]{:S(2)}) async-start(bf16[4,2048,128]{2,1,0:T(8,128)(2,1)} %pick.2), calls=%async_computation | async-start | bytes 4194304 | tf_op jit(solution)/shard_map/all_to_all | solution.py:1013
  19.0 23.3 %collective-permute-start.2 = (bf16[2128,128]{1,0:T(8,128)(2,1)}, bf16[2128,128]{1,0:T(8,128)(2,1)S(1)}, u32[]{:S(2)}, u32[]{:S(2)}) collective-permute-start(bf16[2128,128]{1,0:T(8,128)(2,1)} %get-tuple-element.180), channel_id=1, source_target_pairs={{0,24},{1,25},{2,26},{3,27},{4,28},{5,29},{6,30},{7,31},{8,16},{9,... | collective-permute-start | bytes 1634312 | tf_op jit(solution)/shard_map/ppermute | solution.py:977
  91.8 28.7 %all-to-all-start.2 = ((bf16[4,1024,128]{2,1,0:T(8,128)(2,1)}), bf16[4,1024,128]{2,1,0:T(8,128)(2,1)S(1)}, u32[]{:S(2)}, u32[]{:S(2)}) async-start(bf16[4,1024,128]{2,1,0:T(8,128)(2,1)} %by_section.3), calls=%async_computation.2 | async-start | bytes 2097152 | tf_op jit(solution)/shard_map/all_to_all | solution.py:1013
  112.6 16.9 %collective-permute-start.9 = (bf16[8,512,128]{2,1,0:T(8,128)(2,1)}, bf16[8,512,128]{2,1,0:T(8,128)(2,1)}, u32[]{:S(2)}, u32[]{:S(2)}) collective-permute-start(bf16[8,512,128]{2,1,0:T(8,128)(2,1)} %join.6), channel_id=1, source_target_pairs={{0,1},{1,0},{2,3},{3,2},{4,5},{5,4},{6,7},{7,6},{8,9},{9,8},{10,11... | collective-permute-start | bytes 3145736 | tf_op jit(solution)/shard_map/ppermute | solution.py:977
  112.7 27.6 %collective-permute-start.8 = (bf16[8,512,128]{2,1,0:T(8,128)(2,1)}, bf16[8,512,128]{2,1,0:T(8,128)(2,1)}, u32[]{:S(2)}, u32[]{:S(2)}) collective-permute-start(bf16[8,512,128]{2,1,0:T(8,128)(2,1)} %join.6), channel_id=1, source_target_pairs={{0,16},{1,9},{2,18},{3,11},{4,20},{5,13},{6,22},{7,15},{8,24},{9,1... | collective-permute-start | bytes 3145736 | tf_op jit(solution)/shard_map/ppermute | solution.py:977
  123.5 16.9 %collective-permute-start.7 = (bf16[8,512,128]{2,1,0:T(8,128)(2,1)}, bf16[8,512,128]{2,1,0:T(8,128)(2,1)}, u32[]{:S(2)}, u32[]{:S(2)}) collective-permute-start(bf16[8,512,128]{2,1,0:T(8,128)(2,1)} %collective-permute-done.5), channel_id=1, source_target_pairs={{0,1},{1,0},{2,3},{3,2},{4,5},{5,4},{6,7},{7,6},{8,9},{9,8},{10,11... | collective-permute-start | bytes 3145736 | tf_op jit(solution)/shard_map/ppermute | solution.py:977
  125.7 70.6 %all-to-all-start.3 = ((bf16[4,2048,128]{2,1,0:T(8,128)(2,1)}), bf16[4,2048,128]{2,1,0:T(8,128)(2,1)S(1)}, u32[]{:S(2)}, u32[]{:S(2)}) async-start(bf16[4,2048,128]{2,1,0:T(8,128)(2,1)} %pick.3), calls=%async_computation.3 | async-start | bytes 4194304 | tf_op jit(solution)/shard_map/all_to_all | solution.py:1013
  142.6 19.4 %collective-permute-start.13 = (bf16[8,512,128]{2,1,0:T(8,128)(2,1)}, bf16[8,512,128]{2,1,0:T(8,128)(2,1)}, u32[]{:S(2)}, u32[]{:S(2)}) collective-permute-start(bf16[8,512,128]{2,1,0:T(8,128)(2,1)} %join.7), channel_id=1, source_target_pairs={{0,1},{1,0},{2,3},{3,2},{4,5},{5,4},{6,7},{7,6},{8,9},{9,8},{10,11... | collective-permute-start | bytes 3145736 | tf_op jit(solution)/shard_map/ppermute | solution.py:977
  143.6 19.9 %collective-permute-start.12 = (bf16[8,512,128]{2,1,0:T(8,128)(2,1)}, bf16[8,512,128]{2,1,0:T(8,128)(2,1)}, u32[]{:S(2)}, u32[]{:S(2)}) collective-permute-start(bf16[8,512,128]{2,1,0:T(8,128)(2,1)} %join.7), channel_id=1, source_target_pairs={{0,16},{1,9},{2,18},{3,11},{4,20},{5,13},{6,22},{7,15},{8,24},{9,1... | collective-permute-start | bytes 3145736 | tf_op jit(solution)/shard_map/ppermute | solution.py:977
  144.8 18.7 %collective-permute-start.14 = (bf16[8,512,128]{2,1,0:T(8,128)(2,1)}, bf16[8,512,128]{2,1,0:T(8,128)(2,1)}, u32[]{:S(2)}, u32[]{:S(2)}) collective-permute-start(bf16[8,512,128]{2,1,0:T(8,128)(2,1)} %collective-permute-done.8), channel_id=1, source_target_pairs={{0,1},{1,0},{2,3},{3,2},{4,5},{5,4},{6,7},{7,6},{8,9},{9,8},{10,11... | collective-permute-start | bytes 3145736 | tf_op jit(solution)/shard_map/ppermute | solution.py:977
  145.6 16.3 %collective-permute-start.11 = (bf16[4,512,128]{2,1,0:T(8,128)(2,1)S(1)}, bf16[4,512,128]{2,1,0:T(8,128)(2,1)S(1)}, u32[]{:S(2)}, u32[]{:S(2)}) collective-permute-start(bf16[4,512,128]{2,1,0:T(8,128)(2,1)S(1)} %get-tuple-element.225.refs_0_), channel_id=1, source_target_pairs={{0,8},{1,17},{2,10},{3,19},{4,12},{5,21},{6,14},{7,23},{8,0},{9,25... | collective-permute-start | bytes 1572872 | tf_op jit(solution)/shard_map/ppermute | solution.py:977
  165.7 15.9 %collective-permute-start.16 = (bf16[8,512,128]{2,1,0:T(8,128)(2,1)}, bf16[8,512,128]{2,1,0:T(8,128)(2,1)}, u32[]{:S(2)}, u32[]{:S(2)}) collective-permute-start(bf16[8,512,128]{2,1,0:T(8,128)(2,1)} %join.8), channel_id=1, source_target_pairs={{0,1},{1,0},{2,3},{3,2},{4,5},{5,4},{6,7},{7,6},{8,9},{9,8},{10,11... | collective-permute-start | bytes 3145736 | tf_op jit(solution)/shard_map/ppermute | solution.py:977
  229.8 18.5 %collective-permute-start.19 = (bf16[16,2,2,128,128]{4,3,2,1,0:T(8,128)(2,1)}, bf16[16,2,2,128,128]{4,3,2,1,0:T(8,128)(2,1)S(1)}, u32[]{:S(2)}, u32[]{:S(2)}) collective-permute-start(bf16[16,2,2,128,128]{4,3,2,1,0:T(8,128)(2,1)} %get-tuple-element.265), channel_id=1, source_target_pairs={{0,1},{1,0},{2,3},{3,2},{4,5},{5,4},{6,7},{7,6},{8,9},{9,8},{10,11... | collective-permute-start | bytes 6291464 | tf_op jit(solution)/shard_map/ppermute | solution.py:977
  249.6 28.5 %collective-permute-start.23 = (bf16[16,2,2,128,128]{4,3,2,1,0:T(8,128)(2,1)}, bf16[16,2,2,128,128]{4,3,2,1,0:T(8,128)(2,1)S(1)}, u32[]{:S(2)}, u32[]{:S(2)}) collective-permute-start(bf16[16,2,2,128,128]{4,3,2,1,0:T(8,128)(2,1)} %get-tuple-element.277), channel_id=1, source_target_pairs={{0,1},{1,0},{2,3},{3,2},{4,5},{5,4},{6,7},{7,6},{8,9},{9,8},{10,11... | collective-permute-start | bytes 6291464 | tf_op jit(solution)/shard_map/ppermute | solution.py:977
  253.0 20.5 %collective-permute-start.20 = (bf16[2048,128]{1,0:T(8,128)(2,1)}, bf16[2048,128]{1,0:T(8,128)(2,1)S(1)}, u32[]{:S(2)}, u32[]{:S(2)}) collective-permute-start(bf16[2048,128]{1,0:T(8,128)(2,1)} %bitcast.161), channel_id=1, source_target_pairs={{0,8},{1,9},{2,10},{3,11},{4,12},{5,13},{6,14},{7,15},{8,0},{9,1},... | collective-permute-start | bytes 1572872 | tf_op jit(solution)/shard_map/ppermute | solution.py:977
  253.9 19.6 %collective-permute-start.21 = (bf16[2048,128]{1,0:T(8,128)(2,1)}, bf16[2048,128]{1,0:T(8,128)(2,1)S(1)}, u32[]{:S(2)}, u32[]{:S(2)}) collective-permute-start(bf16[2048,128]{1,0:T(8,128)(2,1)} %bitcast.159), channel_id=1, source_target_pairs={{0,16},{1,17},{2,18},{3,19},{4,20},{5,21},{6,22},{7,23},{8,24},{9,... | collective-permute-start | bytes 1572872 | tf_op jit(solution)/shard_map/ppermute | solution.py:977
  254.8 23.4 %collective-permute-start.22 = (bf16[2048,128]{1,0:T(8,128)(2,1)}, bf16[2048,128]{1,0:T(8,128)(2,1)S(1)}, u32[]{:S(2)}, u32[]{:S(2)}) collective-permute-start(bf16[2048,128]{1,0:T(8,128)(2,1)} %bitcast.157), channel_id=1, source_target_pairs={{0,24},{1,25},{2,26},{3,27},{4,28},{5,29},{6,30},{7,31},{8,16},{9,... | collective-permute-start | bytes 1572872 | tf_op jit(solution)/shard_map/ppermute | solution.py:977
  278.2 29.2 %collective-permute-start.27 = (bf16[16,2,2,128,128]{4,3,2,1,0:T(8,128)(2,1)}, bf16[16,2,2,128,128]{4,3,2,1,0:T(8,128)(2,1)}, u32[]{:S(2)}, u32[]{:S(2)}) collective-permute-start(bf16[16,2,2,128,128]{4,3,2,1,0:T(8,128)(2,1)} %get-tuple-element.293), channel_id=1, source_target_pairs={{0,1},{1,0},{2,3},{3,2},{4,5},{5,4},{6,7},{7,6},{8,9},{9,8},{10,11... | collective-permute-start | bytes 6291464 | tf_op jit(solution)/shard_map/ppermute | solution.py:977
  283.1 20.3 %collective-permute-start.24 = (bf16[2048,128]{1,0:T(8,128)(2,1)}, bf16[2048,128]{1,0:T(8,128)(2,1)S(1)}, u32[]{:S(2)}, u32[]{:S(2)}) collective-permute-start(bf16[2048,128]{1,0:T(8,128)(2,1)} %bitcast.160), channel_id=1, source_target_pairs={{0,8},{1,9},{2,10},{3,11},{4,12},{5,13},{6,14},{7,15},{8,0},{9,1},... | collective-permute-start | bytes 1572872 | tf_op jit(solution)/shard_map/ppermute | solution.py:977
  284.1 20.1 %collective-permute-start.25 = (bf16[2048,128]{1,0:T(8,128)(2,1)}, bf16[2048,128]{1,0:T(8,128)(2,1)S(1)}, u32[]{:S(2)}, u32[]{:S(2)}) collective-permute-start(bf16[2048,128]{1,0:T(8,128)(2,1)} %bitcast.158), channel_id=1, source_target_pairs={{0,16},{1,17},{2,18},{3,19},{4,20},{5,21},{6,22},{7,23},{8,24},{9,... | collective-permute-start | bytes 1572872 | tf_op jit(solution)/shard_map/ppermute | solution.py:977
  284.3 23.0 %collective-permute-start.26 = (bf16[2048,128]{1,0:T(8,128)(2,1)}, bf16[2048,128]{1,0:T(8,128)(2,1)S(1)}, u32[]{:S(2)}, u32[]{:S(2)}) collective-permute-start(bf16[2048,128]{1,0:T(8,128)(2,1)} %bitcast.156), channel_id=1, source_target_pairs={{0,24},{1,25},{2,26},{3,27},{4,28},{5,29},{6,30},{7,31},{8,16},{9,... | collective-permute-start | bytes 1572872 | tf_op jit(solution)/shard_map/ppermute | solution.py:977
  308.2 51.3 %all-to-all-start.4 = ((bf16[4,2048,128]{2,1,0:T(8,128)(2,1)}), bf16[4,2048,128]{2,1,0:T(8,128)(2,1)S(1)}, u32[]{:S(2)}, u32[]{:S(2)}) async-start(bf16[4,2048,128]{2,1,0:T(8,128)(2,1)} %bitcast.120), calls=%async_computation.4 | async-start | bytes 4194304 | tf_op jit(solution)/shard_map/all_to_all | solution.py:1013
  311.8 31.9 %collective-permute-start.28 = (bf16[16,2,2,128,128]{4,3,2,1,0:T(8,128)(2,1)}, bf16[16,2,2,128,128]{4,3,2,1,0:T(8,128)(2,1)}, u32[]{:S(2)}, u32[]{:S(2)}) collective-permute-start(bf16[16,2,2,128,128]{4,3,2,1,0:T(8,128)(2,1)} %get-tuple-element.295), channel_id=1, source_target_pairs={{0,1},{1,0},{2,3},{3,2},{4,5},{5,4},{6,7},{7,6},{8,9},{9,8},{10,11... | collective-permute-start | bytes 6291464 | tf_op jit(solution)/shard_map/ppermute | solution.py:977
  319.0 24.6 %collective-permute-start.30 = (bf16[2048,128]{1,0:T(8,128)(2,1)}, bf16[2048,128]{1,0:T(8,128)(2,1)S(1)}, u32[]{:S(2)}, u32[]{:S(2)}) collective-permute-start(bf16[2048,128]{1,0:T(8,128)(2,1)} %bitcast.164), channel_id=1, source_target_pairs={{0,16},{1,17},{2,18},{3,19},{4,20},{5,21},{6,22},{7,23},{8,24},{9,... | collective-permute-start | bytes 1572872 | tf_op jit(solution)/shard_map/ppermute | solution.py:977
  319.8 23.8 %collective-permute-start.31 = (bf16[2048,128]{1,0:T(8,128)(2,1)}, bf16[2048,128]{1,0:T(8,128)(2,1)S(1)}, u32[]{:S(2)}, u32[]{:S(2)}) collective-permute-start(bf16[2048,128]{1,0:T(8,128)(2,1)} %bitcast.163), channel_id=1, source_target_pairs={{0,24},{1,25},{2,26},{3,27},{4,28},{5,29},{6,30},{7,31},{8,16},{9,... | collective-permute-start | bytes 1572872 | tf_op jit(solution)/shard_map/ppermute | solution.py:977
  359.4 32.3 %all-to-all-start.5 = ((bf16[4,1024,128]{2,1,0:T(8,128)(2,1)}), bf16[4,1024,128]{2,1,0:T(8,128)(2,1)}, u32[]{:S(2)}, u32[]{:S(2)}) async-start(bf16[4,1024,128]{2,1,0:T(8,128)(2,1)} %bitcast.60), calls=%async_computation.5 | async-start | bytes 2097152 | tf_op jit(solution)/shard_map/all_to_all | solution.py:1013
  365.8 21.8 %collective-permute-start.34 = (bf16[2048,128]{1,0:T(8,128)(2,1)}, bf16[2048,128]{1,0:T(8,128)(2,1)S(1)}, u32[]{:S(2)}, u32[]{:S(2)}) collective-permute-start(bf16[2048,128]{1,0:T(8,128)(2,1)} %bitcast.162), channel_id=1, source_target_pairs={{0,24},{1,25},{2,26},{3,27},{4,28},{5,29},{6,30},{7,31},{8,16},{9,... | collective-permute-start | bytes 1572872 | tf_op jit(solution)/shard_map/ppermute | solution.py:977
  391.8 40.4 %all-to-all-start.6 = ((bf16[4,1024,128]{2,1,0:T(8,128)(2,1)}), bf16[4,1024,128]{2,1,0:T(8,128)(2,1)S(1)}, u32[]{:S(2)}, u32[]{:S(2)}) async-start(bf16[4,1024,128]{2,1,0:T(8,128)(2,1)} %all-to-all-done.5), calls=%async_computation.6 | async-start | bytes 2097152 | tf_op jit(solution)/shard_map/all_to_all | solution.py:1016
  396.3 19.4 %collective-permute-start.35 = (bf16[1024,128]{1,0:T(8,128)(2,1)S(1)}, bf16[1024,128]{1,0:T(8,128)(2,1)S(1)}, u32[]{:S(2)}, u32[]{:S(2)}) collective-permute-start(bf16[1024,128]{1,0:T(8,128)(2,1)S(1)} %bitcast.169), channel_id=1, source_target_pairs={{0,0},{1,1},{2,10},{3,11},{4,20},{5,21},{6,30},{7,31},{8,2},{9,3},... | collective-permute-start | bytes 786440 | tf_op jit(solution)/shard_map/ppermute | solution.py:977
  399.8 23.9 %collective-permute-start.36 = (bf16[1024,128]{1,0:T(8,128)(2,1)S(1)}, bf16[1024,128]{1,0:T(8,128)(2,1)S(1)}, u32[]{:S(2)}, u32[]{:S(2)}) collective-permute-start(bf16[1024,128]{1,0:T(8,128)(2,1)S(1)} %bitcast.168), channel_id=1, source_target_pairs={{0,2},{1,3},{2,8},{3,9},{4,22},{5,23},{6,28},{7,29},{8,0},{9,1},{1... | collective-permute-start | bytes 786440 | tf_op jit(solution)/shard_map/ppermute | solution.py:977
  405.1 20.7 %collective-permute-start.37 = (bf16[1024,128]{1,0:T(8,128)(2,1)S(1)}, bf16[1024,128]{1,0:T(8,128)(2,1)S(1)}, u32[]{:S(2)}, u32[]{:S(2)}) collective-permute-start(bf16[1024,128]{1,0:T(8,128)(2,1)S(1)} %bitcast.167), channel_id=1, source_target_pairs={{0,4},{1,5},{2,14},{3,15},{4,16},{5,17},{6,26},{7,27},{8,6},{9,7},... | collective-permute-start | bytes 786440 | tf_op jit(solution)/shard_map/ppermute | solution.py:977
  407.0 25.2 %collective-permute-start.38 = (bf16[1024,128]{1,0:T(8,128)(2,1)S(1)}, bf16[1024,128]{1,0:T(8,128)(2,1)S(1)}, u32[]{:S(2)}, u32[]{:S(2)}) collective-permute-start(bf16[1024,128]{1,0:T(8,128)(2,1)S(1)} %bitcast.166), channel_id=1, source_target_pairs={{0,6},{1,7},{2,12},{3,13},{4,18},{5,19},{6,24},{7,25},{8,4},{9,5},... | collective-permute-start | bytes 786440 | tf_op jit(solution)/shard_map/ppermute | solution.py:977
  (55 other events, 557.8 us)

commit v16 on v14

--- a/solution.py
+++ b/solution.py
@@ -426,13 +426,17 @@
     for copy in right_in:
         copy.wait()
 
+    eye = lax.broadcasted_iota(jnp.int32, (size, size), 0) == lax.broadcasted_iota(jnp.int32, (size, size), 1)
+    eye = eye.astype(jnp.bfloat16)
+
     def right(block, nth, total):
         rows = block_rows(block, size)
         place = table_ref[0, block]
         moved = [mid[pl.ds(q * blocks + block, blocks, stride=size), :] for q in range(fold)]
         moved = jnp.concatenate(moved, axis=0).astype(jnp.bfloat16)
         weight = w[place // chunk_blocks, 1, place % chunk_blocks]
-        mixture = inner_dot(weight, moved, 0, 0)
+        turned = inner_dot(eye, weight, 1, 1).astype(jnp.bfloat16)
+        mixture = inner_dot(turned, moved, 1, 0)
         squared = mixture * mixture
         tangent = jnp.tanh(mixture * (TANH_SLOPE + (TANH_SLOPE * CUBIC_TERM) * squared))
         half = 0.5 + 0.5 * tangent
@@ -981,9 +985,6 @@
 
     def send(values, name):
         return [values[0]] + [move(values[k], routes[name][k]) for k in range(1, width)]
-
-    def gather_one(mine):
-        return joined([mine, move(mine, routes["across"][0])])
 
     def gather_two(pair):
         return pair, move(pair, routes["across"][1]), move(pair, routes["cores"])

time: 446 us -> 467 us (1.047)
  Pallas kernels: 188 us -> 210 us
    pallas_call x4, Pallas kernels: 55.6 us -> 78.5 us  [run_forward(): pl.pallas_call(lambda *refs: forward_kernel(first, layer, len(sources), *...]
  transfers between devices with their start and end apart: 47 -> 47, of which waited for: 22 -> 21; matrix products, arithmetic and copies ran while one was open for 1% -> 1% of each run, Pallas kernels for 33% -> 35%
where the time goes in v16:
time: 467 us; the launch traced here: 462 us
  Pallas kernels  210 us (45%)
  waiting for transfers between devices  132 us (28%)
  starting transfers between devices  70.2 us (15%)
  blocking collectives  30.2 us (6%)
  local copies, waits for them, and re-layouts  15.8 us (3%)
    ppermute x41, waiting for transfers between devices, move(): return lax.ppermute(value, AXES, route)  98.1 us
    pallas_call x4, Pallas kernels, run_forward(): pl.pallas_call(lambda *refs: forward_kernel(first, layer, len(sources), *...  78.5 us
    pallas_call x4, Pallas kernels, run_backward(): pl.pallas_call(lambda *refs: backward_kernel(turning, last, layer, len(so...  73.1 us
    ppermute x41, starting transfers between devices, move(): return lax.ppermute(value, AXES, route)  46.4 us
    all_to_all x5, waiting for transfers between devices, to_planes(): lax.all_to_all(value, 'tensor', split_axis=0, concat_axis=0, tiled=True)  34.2 us
    all_to_all x1, blocking collectives, to_planes(): lax.all_to_all(value, 'tensor', split_axis=0, concat_axis=0, tiled=True)  30.2 us
    all_to_all x5, starting transfers between devices, to_planes(): lax.all_to_all(value, 'tensor', split_axis=0, concat_axis=0, tiled=True)  20 us
    pallas_call x6, Pallas kernels, run_sum(): pl.pallas_call(lambda *refs: sum_kernel(len(groups[0]), len(flat), *refs)...  19.7 us
  transfers between devices with their start and end apart: 47, of which 21 were waited for; matrix products, arithmetic and copies ran while one was open for 1% of the time, Pallas kernels for 35%

profile of v16, /device:TPU:5, one launch (start us, length us, event | category | flops | bytes accessed | tf_op | source)
XLA Modules:
  0.0 462.3 jit_solution(17035463095282541536)
XLA Ops:
  2.1 4.1 pick.2
  6.2 4.7 %all-to-all-start = ((bf16[4,2048,128]{2,1,0:T(8,128)(2,1)}), bf16[4,2048,128]{2,1,0:T(8,128)(2,1)S(1)}, u32[]{:S(2)}, u32[]{:S(2)}) async-start(bf16[4,2048,128]{2,1,0:T(8,128)(2,1)} %pick.2), calls=%async_computation | async-start | bytes 4194304 | tf_op jit(solution)/shard_map/all_to_all | solution.py:1017
  12.8 4.7 %pieces.1 = (bf16[2128,128]{1,0:T(8,128)(2,1)}, bf16[2128,128]{1,0:T(8,128)(2,1)}, bf16[2128,128]{1,0:T(8,128)(2,1)}, bf16[2128,128]{1,0:T(8,128)(2,1)}) custom-call(s32[3]{0:T(128)} %pad_add_fusion.1.refs_0_, bf16[128,128]{1,0:T(8,128)(2,1)} %fusion.refs_1_, bf16[4,16,128,128]{3,2,1,0:T(8,128)(2,1)} %bitcast.114, bf16[4,16,128,128]{3,2,1,0:T(8,128)(2,1)} %bitcast.115, ...), custom_call_target="tpu_custom_call" | custom-call | flops 134217728 | bytes 4194304 | tf_op jit(solution)/shard_map/pieces/pallas_call | solution.py:803
  20.2 4.1 pick.3
  24.3 6.3 %collective-permute-done.refs_2_ = bf16[2128,128]{1,0:T(8,128)(2,1)S(1)} collective-permute-done((bf16[2128,128]{1,0:T(8,128)(2,1)}, bf16[2128,128]{1,0:T(8,128)(2,1)S(1)}, u32[]{:S(2)}, u32[]{:S(2)}) %collective-permute-start) | collective-permute-done | bytes 544800 | tf_op jit(solution)/shard_map/ppermute | solution.py:981
  32.5 9.8 %collective-permute-done.2.refs_4_ = bf16[2128,128]{1,0:T(8,128)(2,1)S(1)} collective-permute-done((bf16[2128,128]{1,0:T(8,128)(2,1)}, bf16[2128,128]{1,0:T(8,128)(2,1)S(1)}, u32[]{:S(2)}, u32[]{:S(2)}) %collective-permute-start.2) | collective-permute-done | bytes 544800 | tf_op jit(solution)/shard_map/ppermute | solution.py:981
  49.0 9.6 %all-to-all-done = bf16[4,2048,128]{2,1,0:T(8,128)(2,1)S(1)} async-done(((bf16[4,2048,128]{2,1,0:T(8,128)(2,1)}), bf16[4,2048,128]{2,1,0:T(8,128)(2,1)S(1)}, u32[]{:S(2)}, u32[]{:S(2)}) %all-to-all-start) | async-done | bytes 2097184 | tf_op jit(solution)/shard_map/all_to_all | solution.py:1017
  60.0 30.2 %all_to_all.35 = bf16[4,1104,128]{2,1,0:T(8,128)(2,1)S(1)} all-to-all(bf16[4,1104,128]{2,1,0:T(8,128)(2,1)} %by_section.2), channel_id=1, replica_groups=mesh['section'=4,'tensor'=4,'dp'=2] {'tensor'}, dimensions={0} | all-to-all | bytes 2260992 | tf_op jit(solution)/shard_map/all_to_all | solution.py:1017
  98.8 5.6 %collective-permute-done.3.refs_1_ = bf16[4,512,128]{2,1,0:T(8,128)(2,1)} collective-permute-done((bf16[4,512,128]{2,1,0:T(8,128)(2,1)S(1)}, bf16[4,512,128]{2,1,0:T(8,128)(2,1)}, u32[]{:S(2)}, u32[]{:S(2)}) %collective-permute-start.3) | collective-permute-done | bytes 524320 | tf_op jit(solution)/shard_map/ppermute | solution.py:981
  113.3 7.2 %all-to-all-done.2 = bf16[4,1024,128]{2,1,0:T(8,128)(2,1)S(1)} async-done(((bf16[4,1024,128]{2,1,0:T(8,128)(2,1)}), bf16[4,1024,128]{2,1,0:T(8,128)(2,1)S(1)}, u32[]{:S(2)}, u32[]{:S(2)}) %all-to-all-start.2) | async-done | bytes 1048608 | tf_op jit(solution)/shard_map/all_to_all | solution.py:1017
  129.5 10.8 %collective-permute-done.8 = bf16[8,512,128]{2,1,0:T(8,128)(2,1)} collective-permute-done((bf16[8,512,128]{2,1,0:T(8,128)(2,1)}, bf16[8,512,128]{2,1,0:T(8,128)(2,1)}, u32[]{:S(2)}, u32[]{:S(2)}) %collective-permute-start.8) | collective-permute-done | bytes 1048608 | tf_op jit(solution)/shard_map/ppermute | solution.py:981
  147.5 20.1 %forward_layer.4 = (f32[8192,128]{1,0:T(8,128)}, bf16[8192,128]{1,0:T(8,128)(2,1)}, bf16[8192,128]{1,0:T(8,128)(2,1)}, bf16[8192,128]{1,0:T(8,128)(2,1)}, f32[8,128]{1,0:T(8,128)}, /*index=5*/f32[8,128]{1,0:T(8,128)}) custom-call(s32[3,64]{1,0:T(4,128)} %pad_add_fusion.refs_0_, f32[8,128]{1,0:T(8,128)} %broadcast_in_dim.6.refs_1_, ...), custom_call_target="tpu_custom_call" | custom-call | flops 4000000000 | bytes 20971520 | tf_op jit(solution)/shard_map/forward_layer/pallas_call | solution.py:609
  172.5 19.4 %forward_layer.5 = (f32[8192,128]{1,0:T(8,128)}, bf16[8192,128]{1,0:T(8,128)(2,1)}, bf16[8192,128]{1,0:T(8,128)(2,1)}, bf16[8192,128]{1,0:T(8,128)(2,1)}, f32[8,128]{1,0:T(8,128)}, /*index=5*/f32[8,128]{1,0:T(8,128)}) custom-call(s32[3,64]{1,0:T(4,128)} %pad_add_fusion.refs_0_, f32[8,128]{1,0:T(8,128)} %get-tuple-element.215.refs_1_, ...), custom_call_target="tpu_custom_call" | custom-call | flops 4000000000 | bytes 20971520 | tf_op jit(solution)/shard_map/forward_layer/pallas_call | solution.py:609
  193.0 19.5 %forward_layer.6 = (f32[8192,128]{1,0:T(8,128)}, bf16[8192,128]{1,0:T(8,128)(2,1)}, bf16[8192,128]{1,0:T(8,128)(2,1)}, bf16[8192,128]{1,0:T(8,128)(2,1)}, f32[8,128]{1,0:T(8,128)}, /*index=5*/f32[8,128]{1,0:T(8,128)}) custom-call(s32[3,64]{1,0:T(4,128)} %pad_add_fusion.refs_0_, f32[8,128]{1,0:T(8,128)} %get-tuple-element.232.refs_1_, ...), custom_call_target="tpu_custom_call" | custom-call | flops 4000000000 | bytes 20971520 | tf_op jit(solution)/shard_map/forward_layer/pallas_call | solution.py:609
  212.5 19.5 %forward_layer.7 = (f32[8192,128]{1,0:T(8,128)}, bf16[8192,128]{1,0:T(8,128)(2,1)}, bf16[8192,128]{1,0:T(8,128)(2,1)}, bf16[8192,128]{1,0:T(8,128)(2,1)}, f32[8,128]{1,0:T(8,128)}, /*index=5*/f32[8,128]{1,0:T(8,128)}) custom-call(s32[3,64]{1,0:T(4,128)} %pad_add_fusion.refs_0_, f32[8,128]{1,0:T(8,128)} %get-tuple-element.250.refs_1_, ...), custom_call_target="tpu_custom_call" | custom-call | flops 4000000000 | bytes 20971520 | tf_op jit(solution)/shard_map/forward_layer/pallas_call | solution.py:609
  232.1 19.6 %backward_layer.4 = (f32[8192,128]{1,0:T(8,128)}, bf16[16,2,2,128,128]{4,3,2,1,0:T(8,128)(2,1)}, bf16[16,2,2,128,128]{4,3,2,1,0:T(8,128)(2,1)}) custom-call(s32[3,64]{1,0:T(4,128)} %pad_add_fusion.refs_0_, f32[8,128]{1,0:T(8,128)} %get-tuple-element.256.refs_1_, bf16[128,64]{1,0:T(8,128)(2,1)} %get-tuple-element.353.refs_2_, f32[8,128,8]{2,1,0:T(8,128)} %bitcast.101, ...), custom_call_target="tpu_custom_call" | custom-call | flops 5000000000 | bytes 31457280 | tf_op jit(solution)/shard_map/backward_layer/pallas_call | solution.py:640
  252.1 18.0 %backward_layer.5 = (f32[8192,128]{1,0:T(8,128)}, bf16[16,2,2,128,128]{4,3,2,1,0:T(8,128)(2,1)}, bf16[16,2,2,128,128]{4,3,2,1,0:T(8,128)(2,1)}) custom-call(s32[3,64]{1,0:T(4,128)} %pad_add_fusion.refs_0_, f32[8,128]{1,0:T(8,128)} %get-tuple-element.238.refs_1_, bf16[128,64]{1,0:T(8,128)(2,1)} %get-tuple-element.354.refs_2_, f32[8,128,8]{2,1,0:T(8,128)} %bitcast.102, ...), custom_call_target="tpu_custom_call" | custom-call | flops 5000000000 | bytes 31457280 | tf_op jit(solution)/shard_map/backward_layer/pallas_call | solution.py:640
  277.5 17.8 %backward_layer.6 = (f32[8192,128]{1,0:T(8,128)}, bf16[16,2,2,128,128]{4,3,2,1,0:T(8,128)(2,1)}, bf16[16,2,2,128,128]{4,3,2,1,0:T(8,128)(2,1)}) custom-call(s32[3,64]{1,0:T(4,128)} %pad_add_fusion.refs_0_, f32[8,128]{1,0:T(8,128)} %get-tuple-element.221.refs_1_, bf16[128,64]{1,0:T(8,128)(2,1)} %get-tuple-element.355.refs_2_, f32[8,128,8]{2,1,0:T(8,128)} %bitcast.103, ...), custom_call_target="tpu_custom_call" | custom-call | flops 5000000000 | bytes 31457280 | tf_op jit(solution)/shard_map/backward_layer/pallas_call | solution.py:640
  295.4 4.5 collective-permute-done.22
  307.2 17.6 %backward_layer.7 = (bf16[8192,128]{1,0:T(8,128)(2,1)}, bf16[16,2,2,128,128]{4,3,2,1,0:T(8,128)(2,1)}, bf16[16,2,2,128,128]{4,3,2,1,0:T(8,128)(2,1)}) custom-call(s32[3,64]{1,0:T(4,128)} %pad_add_fusion.refs_0_, f32[8,128]{1,0:T(8,128)} %get-tuple-element.203.refs_1_, bf16[128,64]{1,0:T(8,128)(2,1)} %get-tuple-element.356.refs_2_, f32[8,128,8]{2,1,0:T(8,128)} %bitcast.104, ...), custom_call_target="tpu_custom_call" | custom-call | flops 5000000000 | bytes 31457280 | tf_op jit(solution)/shard_map/backward_layer/pallas_call | solution.py:640
  342.9 11.1 %collective-permute-done.29 = bf16[2048,128]{1,0:T(8,128)(2,1)S(1)} collective-permute-done((bf16[2048,128]{1,0:T(8,128)(2,1)}, bf16[2048,128]{1,0:T(8,128)(2,1)S(1)}, u32[]{:S(2)}, u32[]{:S(2)}) %collective-permute-start.29) | collective-permute-done | bytes 524320 | tf_op jit(solution)/shard_map/ppermute | solution.py:981
  354.0 11.1 %collective-permute-done.31 = bf16[2048,128]{1,0:T(8,128)(2,1)S(1)} collective-permute-done((bf16[2048,128]{1,0:T(8,128)(2,1)}, bf16[2048,128]{1,0:T(8,128)(2,1)S(1)}, u32[]{:S(2)}, u32[]{:S(2)}) %collective-permute-start.31) | collective-permute-done | bytes 524320 | tf_op jit(solution)/shard_map/ppermute | solution.py:981
  365.9 4.1 sum.11
  370.0 11.2 %all-to-all-done.4.came_ref = bf16[4,2048,128]{2,1,0:T(8,128)(2,1)S(1)} async-done(((bf16[4,2048,128]{2,1,0:T(8,128)(2,1)}), bf16[4,2048,128]{2,1,0:T(8,128)(2,1)S(1)}, u32[]{:S(2)}, u32[]{:S(2)}) %all-to-all-start.4) | async-done | bytes 2097184 | tf_op jit(solution)/shard_map/all_to_all | solution.py:1017
  381.2 4.4 all-to-all-start.5
  391.6 9.6 %collective-permute-done.32 = bf16[2048,128]{1,0:T(8,128)(2,1)S(1)} collective-permute-done((bf16[2048,128]{1,0:T(8,128)(2,1)}, bf16[2048,128]{1,0:T(8,128)(2,1)S(1)}, u32[]{:S(2)}, u32[]{:S(2)}) %collective-permute-start.32) | collective-permute-done | bytes 524320 | tf_op jit(solution)/shard_map/ppermute | solution.py:981
  401.8 10.9 %collective-permute-done.34 = bf16[2048,128]{1,0:T(8,128)(2,1)S(1)} collective-permute-done((bf16[2048,128]{1,0:T(8,128)(2,1)}, bf16[2048,128]{1,0:T(8,128)(2,1)S(1)}, u32[]{:S(2)}, u32[]{:S(2)}) %collective-permute-start.34) | collective-permute-done | bytes 524320 | tf_op jit(solution)/shard_map/ppermute | solution.py:981
  415.9 6.2 %all-to-all-done.5 = bf16[4,1536,128]{2,1,0:T(8,128)(2,1)} async-done(((bf16[4,1536,128]{2,1,0:T(8,128)(2,1)}), bf16[4,1536,128]{2,1,0:T(8,128)(2,1)}, u32[]{:S(2)}, u32[]{:S(2)}) %all-to-all-start.5) | async-done | bytes 1572896 | tf_op jit(solution)/shard_map/all_to_all | solution.py:1017
  427.9 4.2 collective-permute-start.36
  434.1 5.2 %collective-permute-start.38 = (bf16[512,128]{1,0:T(8,128)(2,1)S(1)}, bf16[512,128]{1,0:T(8,128)(2,1)}, u32[]{:S(2)}, u32[]{:S(2)}) collective-permute-start(bf16[512,128]{1,0:T(8,128)(2,1)S(1)} %bitcast.168), channel_id=1, source_target_pairs={{0,6},{1,7},{2,12},{3,13},{4,18},{5,19},{6,24},{7,25},{8,4},{9,5},... | collective-permute-start | bytes 393224 | tf_op jit(solution)/shard_map/ppermute | solution.py:981
  445.3 3.9 collective-permute-done.38.refs_3_
  456.3 5.9 %assemble.1 = (f32[4,16,128,128]{3,2,1,0:T(8,128)}, f32[4,16,128,128]{3,2,1,0:T(8,128)}) custom-call(s32[3]{0:T(128)} %pad_add_fusion.1.refs_0_, bf16[128,128]{1,0:T(8,128)(2,1)} %fusion.refs_1_, bf16[4,1,2,2,128,128]{5,4,3,2,1,0:T(8,128)(2,1)} %bitcast.116, bf16[4,1,2,2,128,128]{5,4,3,2,1,0:T(8,128)(2,1)} %bitcast.131, ...), custom_call_target="tpu_custom_call" | custom-call | bytes 12582912 | tf_op jit(solution)/shard_map/assemble/pallas_call | solution.py:924
  (186 shorter events, 119.9 us)
Async XLA Ops:
  6.2 52.4 %all-to-all-start = ((bf16[4,2048,128]{2,1,0:T(8,128)(2,1)}), bf16[4,2048,128]{2,1,0:T(8,128)(2,1)S(1)}, u32[]{:S(2)}, u32[]{:S(2)}) async-start(bf16[4,2048,128]{2,1,0:T(8,128)(2,1)} %pick.2), calls=%async_computation | async-start | bytes 4194304 | tf_op jit(solution)/shard_map/all_to_all | solution.py:1017
  19.0 23.3 %collective-permute-start.2 = (bf16[2128,128]{1,0:T(8,128)(2,1)}, bf16[2128,128]{1,0:T(8,128)(2,1)S(1)}, u32[]{:S(2)}, u32[]{:S(2)}) collective-permute-start(bf16[2128,128]{1,0:T(8,128)(2,1)} %get-tuple-element.182), channel_id=1, source_target_pairs={{0,24},{1,25},{2,26},{3,27},{4,28},{5,29},{6,30},{7,31},{8,16},{9,... | collective-permute-start | bytes 1634312 | tf_op jit(solution)/shard_map/ppermute | solution.py:981
  91.8 28.7 %all-to-all-start.2 = ((bf16[4,1024,128]{2,1,0:T(8,128)(2,1)}), bf16[4,1024,128]{2,1,0:T(8,128)(2,1)S(1)}, u32[]{:S(2)}, u32[]{:S(2)}) async-start(bf16[4,1024,128]{2,1,0:T(8,128)(2,1)} %by_section.3), calls=%async_computation.2 | async-start | bytes 2097152 | tf_op jit(solution)/shard_map/all_to_all | solution.py:1017
  112.6 16.9 %collective-permute-start.9 = (bf16[8,512,128]{2,1,0:T(8,128)(2,1)}, bf16[8,512,128]{2,1,0:T(8,128)(2,1)}, u32[]{:S(2)}, u32[]{:S(2)}) collective-permute-start(bf16[8,512,128]{2,1,0:T(8,128)(2,1)} %join.6), channel_id=1, source_target_pairs={{0,1},{1,0},{2,3},{3,2},{4,5},{5,4},{6,7},{7,6},{8,9},{9,8},{10,11... | collective-permute-start | bytes 3145736 | tf_op jit(solution)/shard_map/ppermute | solution.py:981
  112.7 27.6 %collective-permute-start.8 = (bf16[8,512,128]{2,1,0:T(8,128)(2,1)}, bf16[8,512,128]{2,1,0:T(8,128)(2,1)}, u32[]{:S(2)}, u32[]{:S(2)}) collective-permute-start(bf16[8,512,128]{2,1,0:T(8,128)(2,1)} %join.6), channel_id=1, source_target_pairs={{0,16},{1,9},{2,18},{3,11},{4,20},{5,13},{6,22},{7,15},{8,24},{9,1... | collective-permute-start | bytes 3145736 | tf_op jit(solution)/shard_map/ppermute | solution.py:981
  123.5 16.9 %collective-permute-start.7 = (bf16[8,512,128]{2,1,0:T(8,128)(2,1)}, bf16[8,512,128]{2,1,0:T(8,128)(2,1)}, u32[]{:S(2)}, u32[]{:S(2)}) collective-permute-start(bf16[8,512,128]{2,1,0:T(8,128)(2,1)} %collective-permute-done.5), channel_id=1, source_target_pairs={{0,1},{1,0},{2,3},{3,2},{4,5},{5,4},{6,7},{7,6},{8,9},{9,8},{10,11... | collective-permute-start | bytes 3145736 | tf_op jit(solution)/shard_map/ppermute | solution.py:981
  124.5 15.8 %collective-permute-start.10 = (bf16[4,512,128]{2,1,0:T(8,128)(2,1)S(1)}, bf16[4,512,128]{2,1,0:T(8,128)(2,1)}, u32[]{:S(2)}, u32[]{:S(2)}) collective-permute-start(bf16[4,512,128]{2,1,0:T(8,128)(2,1)S(1)} %get-tuple-element.210.refs_0_), channel_id=1, source_target_pairs={{0,8},{1,17},{2,10},{3,19},{4,12},{5,21},{6,14},{7,23},{8,0},{9,25... | collective-permute-start | bytes 1572872 | tf_op jit(solution)/shard_map/ppermute | solution.py:981
  125.7 86.8 %all-to-all-start.3 = ((bf16[4,2048,128]{2,1,0:T(8,128)(2,1)}), bf16[4,2048,128]{2,1,0:T(8,128)(2,1)S(1)}, u32[]{:S(2)}, u32[]{:S(2)}) async-start(bf16[4,2048,128]{2,1,0:T(8,128)(2,1)} %pick.3), calls=%async_computation.3 | async-start | bytes 4194304 | tf_op jit(solution)/shard_map/all_to_all | solution.py:1017
  142.6 25.0 %collective-permute-start.13 = (bf16[8,512,128]{2,1,0:T(8,128)(2,1)}, bf16[8,512,128]{2,1,0:T(8,128)(2,1)}, u32[]{:S(2)}, u32[]{:S(2)}) collective-permute-start(bf16[8,512,128]{2,1,0:T(8,128)(2,1)} %join.7), channel_id=1, source_target_pairs={{0,1},{1,0},{2,3},{3,2},{4,5},{5,4},{6,7},{7,6},{8,9},{9,8},{10,11... | collective-permute-start | bytes 3145736 | tf_op jit(solution)/shard_map/ppermute | solution.py:981
  143.6 24.0 %collective-permute-start.12 = (bf16[8,512,128]{2,1,0:T(8,128)(2,1)}, bf16[8,512,128]{2,1,0:T(8,128)(2,1)}, u32[]{:S(2)}, u32[]{:S(2)}) collective-permute-start(bf16[8,512,128]{2,1,0:T(8,128)(2,1)} %join.7), channel_id=1, source_target_pairs={{0,16},{1,9},{2,18},{3,11},{4,20},{5,13},{6,22},{7,15},{8,24},{9,1... | collective-permute-start | bytes 3145736 | tf_op jit(solution)/shard_map/ppermute | solution.py:981
  144.8 22.8 %collective-permute-start.14 = (bf16[8,512,128]{2,1,0:T(8,128)(2,1)}, bf16[8,512,128]{2,1,0:T(8,128)(2,1)}, u32[]{:S(2)}, u32[]{:S(2)}) collective-permute-start(bf16[8,512,128]{2,1,0:T(8,128)(2,1)} %collective-permute-done.8), channel_id=1, source_target_pairs={{0,1},{1,0},{2,3},{3,2},{4,5},{5,4},{6,7},{7,6},{8,9},{9,8},{10,11... | collective-permute-start | bytes 3145736 | tf_op jit(solution)/shard_map/ppermute | solution.py:981
  145.6 22.0 %collective-permute-start.11 = (bf16[4,512,128]{2,1,0:T(8,128)(2,1)S(1)}, bf16[4,512,128]{2,1,0:T(8,128)(2,1)S(1)}, u32[]{:S(2)}, u32[]{:S(2)}) collective-permute-start(bf16[4,512,128]{2,1,0:T(8,128)(2,1)S(1)} %get-tuple-element.227.refs_0_), channel_id=1, source_target_pairs={{0,8},{1,17},{2,10},{3,19},{4,12},{5,21},{6,14},{7,23},{8,0},{9,25... | collective-permute-start | bytes 1572872 | tf_op jit(solution)/shard_map/ppermute | solution.py:981
  170.6 21.4 %collective-permute-start.16 = (bf16[8,512,128]{2,1,0:T(8,128)(2,1)}, bf16[8,512,128]{2,1,0:T(8,128)(2,1)}, u32[]{:S(2)}, u32[]{:S(2)}) collective-permute-start(bf16[8,512,128]{2,1,0:T(8,128)(2,1)} %join.8), channel_id=1, source_target_pairs={{0,1},{1,0},{2,3},{3,2},{4,5},{5,4},{6,7},{7,6},{8,9},{9,8},{10,11... | collective-permute-start | bytes 3145736 | tf_op jit(solution)/shard_map/ppermute | solution.py:981
  171.1 20.9 %collective-permute-start.15 = (bf16[8,512,128]{2,1,0:T(8,128)(2,1)}, bf16[8,512,128]{2,1,0:T(8,128)(2,1)}, u32[]{:S(2)}, u32[]{:S(2)}) collective-permute-start(bf16[8,512,128]{2,1,0:T(8,128)(2,1)} %join.8), channel_id=1, source_target_pairs={{0,16},{1,9},{2,18},{3,11},{4,20},{5,13},{6,22},{7,15},{8,24},{9,1... | collective-permute-start | bytes 3145736 | tf_op jit(solution)/shard_map/ppermute | solution.py:981
  172.3 19.7 %collective-permute-start.17 = (bf16[8,512,128]{2,1,0:T(8,128)(2,1)}, bf16[8,512,128]{2,1,0:T(8,128)(2,1)S(1)}, u32[]{:S(2)}, u32[]{:S(2)}) collective-permute-start(bf16[8,512,128]{2,1,0:T(8,128)(2,1)} %collective-permute-done.12), channel_id=1, source_target_pairs={{0,1},{1,0},{2,3},{3,2},{4,5},{5,4},{6,7},{7,6},{8,9},{9,8},{10,11... | collective-permute-start | bytes 3145736 | tf_op jit(solution)/shard_map/ppermute | solution.py:981
  192.0 20.5 %collective-permute-start.18 = (bf16[8,512,128]{2,1,0:T(8,128)(2,1)}, bf16[8,512,128]{2,1,0:T(8,128)(2,1)}, u32[]{:S(2)}, u32[]{:S(2)}) collective-permute-start(bf16[8,512,128]{2,1,0:T(8,128)(2,1)} %collective-permute-done.15), channel_id=1, source_target_pairs={{0,1},{1,0},{2,3},{3,2},{4,5},{5,4},{6,7},{7,6},{8,9},{9,8},{10,11... | collective-permute-start | bytes 3145736 | tf_op jit(solution)/shard_map/ppermute | solution.py:981
  251.7 18.3 %collective-permute-start.19 = (bf16[16,2,2,128,128]{4,3,2,1,0:T(8,128)(2,1)}, bf16[16,2,2,128,128]{4,3,2,1,0:T(8,128)(2,1)S(1)}, u32[]{:S(2)}, u32[]{:S(2)}) collective-permute-start(bf16[16,2,2,128,128]{4,3,2,1,0:T(8,128)(2,1)} %get-tuple-element.267), channel_id=1, source_target_pairs={{0,1},{1,0},{2,3},{3,2},{4,5},{5,4},{6,7},{7,6},{8,9},{9,8},{10,11... | collective-permute-start | bytes 6291464 | tf_op jit(solution)/shard_map/ppermute | solution.py:981
  271.4 28.5 %collective-permute-start.23 = (bf16[16,2,2,128,128]{4,3,2,1,0:T(8,128)(2,1)}, bf16[16,2,2,128,128]{4,3,2,1,0:T(8,128)(2,1)S(1)}, u32[]{:S(2)}, u32[]{:S(2)}) collective-permute-start(bf16[16,2,2,128,128]{4,3,2,1,0:T(8,128)(2,1)} %get-tuple-element.279), channel_id=1, source_target_pairs={{0,1},{1,0},{2,3},{3,2},{4,5},{5,4},{6,7},{7,6},{8,9},{9,8},{10,11... | collective-permute-start | bytes 6291464 | tf_op jit(solution)/shard_map/ppermute | solution.py:981
  274.9 20.5 %collective-permute-start.20 = (bf16[2048,128]{1,0:T(8,128)(2,1)}, bf16[2048,128]{1,0:T(8,128)(2,1)S(1)}, u32[]{:S(2)}, u32[]{:S(2)}) collective-permute-start(bf16[2048,128]{1,0:T(8,128)(2,1)} %bitcast.161), channel_id=1, source_target_pairs={{0,8},{1,9},{2,10},{3,11},{4,12},{5,13},{6,14},{7,15},{8,0},{9,1},... | collective-permute-start | bytes 1572872 | tf_op jit(solution)/shard_map/ppermute | solution.py:981
  275.3 20.1 %collective-permute-start.21 = (bf16[2048,128]{1,0:T(8,128)(2,1)}, bf16[2048,128]{1,0:T(8,128)(2,1)S(1)}, u32[]{:S(2)}, u32[]{:S(2)}) collective-permute-start(bf16[2048,128]{1,0:T(8,128)(2,1)} %bitcast.159), channel_id=1, source_target_pairs={{0,16},{1,17},{2,18},{3,19},{4,20},{5,21},{6,22},{7,23},{8,24},{9,... | collective-permute-start | bytes 1572872 | tf_op jit(solution)/shard_map/ppermute | solution.py:981
  276.5 23.4 %collective-permute-start.22 = (bf16[2048,128]{1,0:T(8,128)(2,1)}, bf16[2048,128]{1,0:T(8,128)(2,1)S(1)}, u32[]{:S(2)}, u32[]{:S(2)}) collective-permute-start(bf16[2048,128]{1,0:T(8,128)(2,1)} %bitcast.157), channel_id=1, source_target_pairs={{0,24},{1,25},{2,26},{3,27},{4,28},{5,29},{6,30},{7,31},{8,16},{9,... | collective-permute-start | bytes 1572872 | tf_op jit(solution)/shard_map/ppermute | solution.py:981
  299.9 29.2 %collective-permute-start.27 = (bf16[16,2,2,128,128]{4,3,2,1,0:T(8,128)(2,1)}, bf16[16,2,2,128,128]{4,3,2,1,0:T(8,128)(2,1)}, u32[]{:S(2)}, u32[]{:S(2)}) collective-permute-start(bf16[16,2,2,128,128]{4,3,2,1,0:T(8,128)(2,1)} %get-tuple-element.295), channel_id=1, source_target_pairs={{0,1},{1,0},{2,3},{3,2},{4,5},{5,4},{6,7},{7,6},{8,9},{9,8},{10,11... | collective-permute-start | bytes 6291464 | tf_op jit(solution)/shard_map/ppermute | solution.py:981
  304.6 20.3 %collective-permute-start.24 = (bf16[2048,128]{1,0:T(8,128)(2,1)}, bf16[2048,128]{1,0:T(8,128)(2,1)S(1)}, u32[]{:S(2)}, u32[]{:S(2)}) collective-permute-start(bf16[2048,128]{1,0:T(8,128)(2,1)} %bitcast.160), channel_id=1, source_target_pairs={{0,8},{1,9},{2,10},{3,11},{4,12},{5,13},{6,14},{7,15},{8,0},{9,1},... | collective-permute-start | bytes 1572872 | tf_op jit(solution)/shard_map/ppermute | solution.py:981
  305.9 19.8 %collective-permute-start.25 = (bf16[2048,128]{1,0:T(8,128)(2,1)}, bf16[2048,128]{1,0:T(8,128)(2,1)S(1)}, u32[]{:S(2)}, u32[]{:S(2)}) collective-permute-start(bf16[2048,128]{1,0:T(8,128)(2,1)} %bitcast.158), channel_id=1, source_target_pairs={{0,16},{1,17},{2,18},{3,19},{4,20},{5,21},{6,22},{7,23},{8,24},{9,... | collective-permute-start | bytes 1572872 | tf_op jit(solution)/shard_map/ppermute | solution.py:981
  306.0 23.1 %collective-permute-start.26 = (bf16[2048,128]{1,0:T(8,128)(2,1)}, bf16[2048,128]{1,0:T(8,128)(2,1)S(1)}, u32[]{:S(2)}, u32[]{:S(2)}) collective-permute-start(bf16[2048,128]{1,0:T(8,128)(2,1)} %bitcast.156), channel_id=1, source_target_pairs={{0,24},{1,25},{2,26},{3,27},{4,28},{5,29},{6,30},{7,31},{8,16},{9,... | collective-permute-start | bytes 1572872 | tf_op jit(solution)/shard_map/ppermute | solution.py:981
  329.9 51.3 %all-to-all-start.4 = ((bf16[4,2048,128]{2,1,0:T(8,128)(2,1)}), bf16[4,2048,128]{2,1,0:T(8,128)(2,1)S(1)}, u32[]{:S(2)}, u32[]{:S(2)}) async-start(bf16[4,2048,128]{2,1,0:T(8,128)(2,1)} %bitcast.121), calls=%async_computation.4 | async-start | bytes 4194304 | tf_op jit(solution)/shard_map/all_to_all | solution.py:1017
  333.5 31.6 %collective-permute-start.28 = (bf16[16,2,2,128,128]{4,3,2,1,0:T(8,128)(2,1)}, bf16[16,2,2,128,128]{4,3,2,1,0:T(8,128)(2,1)}, u32[]{:S(2)}, u32[]{:S(2)}) collective-permute-start(bf16[16,2,2,128,128]{4,3,2,1,0:T(8,128)(2,1)} %get-tuple-element.297), channel_id=1, source_target_pairs={{0,1},{1,0},{2,3},{3,2},{4,5},{5,4},{6,7},{7,6},{8,9},{9,8},{10,11... | collective-permute-start | bytes 6291464 | tf_op jit(solution)/shard_map/ppermute | solution.py:981
  340.8 24.3 %collective-permute-start.31 = (bf16[2048,128]{1,0:T(8,128)(2,1)}, bf16[2048,128]{1,0:T(8,128)(2,1)S(1)}, u32[]{:S(2)}, u32[]{:S(2)}) collective-permute-start(bf16[2048,128]{1,0:T(8,128)(2,1)} %bitcast.162), channel_id=1, source_target_pairs={{0,24},{1,25},{2,26},{3,27},{4,28},{5,29},{6,30},{7,31},{8,16},{9,... | collective-permute-start | bytes 1572872 | tf_op jit(solution)/shard_map/ppermute | solution.py:981
  381.2 40.9 %all-to-all-start.5 = ((bf16[4,1536,128]{2,1,0:T(8,128)(2,1)}), bf16[4,1536,128]{2,1,0:T(8,128)(2,1)}, u32[]{:S(2)}, u32[]{:S(2)}) async-start(bf16[4,1536,128]{2,1,0:T(8,128)(2,1)} %bitcast.107), calls=%async_computation.5 | async-start | bytes 3145728 | tf_op jit(solution)/shard_map/all_to_all | solution.py:1017
  390.9 21.8 %collective-permute-start.34 = (bf16[2048,128]{1,0:T(8,128)(2,1)}, bf16[2048,128]{1,0:T(8,128)(2,1)S(1)}, u32[]{:S(2)}, u32[]{:S(2)}) collective-permute-start(bf16[2048,128]{1,0:T(8,128)(2,1)} %bitcast.163), channel_id=1, source_target_pairs={{0,24},{1,25},{2,26},{3,27},{4,28},{5,29},{6,30},{7,31},{8,16},{9,... | collective-permute-start | bytes 1572872 | tf_op jit(solution)/shard_map/ppermute | solution.py:981
  422.0 27.2 %all-to-all-start.6 = ((bf16[4,1536,128]{2,1,0:T(8,128)(2,1)}), bf16[4,1536,128]{2,1,0:T(8,128)(2,1)S(1)}, u32[]{:S(2)}, u32[]{:S(2)}) async-start(bf16[4,1536,128]{2,1,0:T(8,128)(2,1)} %all-to-all-done.5), calls=%async_computation.6 | async-start | bytes 3145728 | tf_op jit(solution)/shard_map/all_to_all | solution.py:1020
  426.0 17.2 %collective-permute-start.35 = (bf16[512,128]{1,0:T(8,128)(2,1)S(1)}, bf16[512,128]{1,0:T(8,128)(2,1)S(1)}, u32[]{:S(2)}, u32[]{:S(2)}) collective-permute-start(bf16[512,128]{1,0:T(8,128)(2,1)S(1)} %bitcast.171), channel_id=1, source_target_pairs={{0,0},{1,1},{2,10},{3,11},{4,20},{5,21},{6,30},{7,31},{8,2},{9,3},... | collective-permute-start | bytes 393224 | tf_op jit(solution)/shard_map/ppermute | solution.py:981
  (54 other events, 534.3 us)

commit v17 on v14

--- a/solution.py
+++ b/solution.py
@@ -614,7 +614,7 @@
             pltpu.VMEM(whole, jnp.bfloat16),
             pltpu.VMEM(whole, jnp.bfloat16),
             pltpu.VMEM(whole, jnp.bfloat16),
-            pltpu.VMEM(whole, jnp.float32),
+            pltpu.VMEM((whole[0] + held[-1], whole[1]), jnp.float32),
             pltpu.SemaphoreType.DMA((CHUNKS,)),
             pltpu.SemaphoreType.DMA((2, PARTS)),
             pltpu.SemaphoreType.DMA((4, CHUNKS)),
@@ -646,7 +646,7 @@
             pltpu.VMEM(whole, jnp.bfloat16 if last else jnp.float32),
             pltpu.VMEM(held, jnp.bfloat16),
             pltpu.VMEM(held, jnp.bfloat16),
-            pltpu.VMEM(whole, jnp.float32),
+            pltpu.VMEM((whole[0] + held[-1], whole[1]), jnp.float32),
             pltpu.VMEM(whole if turning else SMALL, jnp.float32),
             pltpu.VMEM(whole if turning else SMALL, jnp.bfloat16),
             pltpu.SemaphoreType.DMA((6, CHUNKS)),
@@ -981,9 +981,6 @@
 
     def send(values, name):
         return [values[0]] + [move(values[k], routes[name][k]) for k in range(1, width)]
-
-    def gather_one(mine):
-        return joined([mine, move(mine, routes["across"][0])])
 
     def gather_two(pair):
         return pair, move(pair, routes["across"][1]), move(pair, routes["cores"])

time: 446 us -> 446 us (level)
  no operation moved by 1% of the time
where the time goes in v17:
time: 446 us; the launch traced here: 441 us
  Pallas kernels  188 us (42%)
  waiting for transfers between devices  134 us (30%)
  starting transfers between devices  71.1 us (16%)
  blocking collectives  30.2 us (7%)
  local copies, waits for them, and re-layouts  14.9 us (3%)
    ppermute x41, waiting for transfers between devices, move(): return lax.ppermute(value, AXES, route)  100 us
    pallas_call x4, Pallas kernels, run_backward(): pl.pallas_call(lambda *refs: backward_kernel(turning, last, layer, len(so...  73 us
    pallas_call x4, Pallas kernels, run_forward(): pl.pallas_call(lambda *refs: forward_kernel(first, layer, len(sources), *...  55.6 us
    ppermute x41, starting transfers between devices, move(): return lax.ppermute(value, AXES, route)  47 us
    all_to_all x5, waiting for transfers between devices, to_planes(): lax.all_to_all(value, 'tensor', split_axis=0, concat_axis=0, tiled=True)  33.8 us
    all_to_all x1, blocking collectives, to_planes(): lax.all_to_all(value, 'tensor', split_axis=0, concat_axis=0, tiled=True)  30.2 us
    all_to_all x5, starting transfers between devices, to_planes(): lax.all_to_all(value, 'tensor', split_axis=0, concat_axis=0, tiled=True)  20 us
    pallas_call x6, Pallas kernels, run_sum(): pl.pallas_call(lambda *refs: sum_kernel(len(groups[0]), len(flat), *refs)...  19.7 us
  transfers between devices with their start and end apart: 47, of which 22 were waited for; matrix products, arithmetic and copies ran while one was open for 1% of the time, Pallas kernels for 33%

profile of v17, /device:TPU:5, one launch (start us, length us, event | category | flops | bytes accessed | tf_op | source)
XLA Modules:
  0.0 441.0 jit_solution(6362211386123357582)
XLA Ops:
  2.1 4.1 pick.2
  6.2 4.7 %all-to-all-start = ((bf16[4,2048,128]{2,1,0:T(8,128)(2,1)}), bf16[4,2048,128]{2,1,0:T(8,128)(2,1)S(1)}, u32[]{:S(2)}, u32[]{:S(2)}) async-start(bf16[4,2048,128]{2,1,0:T(8,128)(2,1)} %pick.2), calls=%async_computation | async-start | bytes 4194304 | tf_op jit(solution)/shard_map/all_to_all | solution.py:1013
  12.8 4.7 %pieces.1 = (bf16[2128,128]{1,0:T(8,128)(2,1)}, bf16[2128,128]{1,0:T(8,128)(2,1)}, bf16[2128,128]{1,0:T(8,128)(2,1)}, bf16[2128,128]{1,0:T(8,128)(2,1)}) custom-call(s32[3]{0:T(128)} %pad_add_fusion.1.refs_0_, bf16[128,128]{1,0:T(8,128)(2,1)} %fusion.refs_1_, bf16[4,16,128,128]{3,2,1,0:T(8,128)(2,1)} %bitcast.114, bf16[4,16,128,128]{3,2,1,0:T(8,128)(2,1)} %bitcast.115, ...), custom_call_target="tpu_custom_call" | custom-call | flops 134217728 | bytes 4194304 | tf_op jit(solution)/shard_map/pieces/pallas_call | solution.py:799
  20.2 4.1 pick.3
  24.3 6.3 %collective-permute-done.refs_2_ = bf16[2128,128]{1,0:T(8,128)(2,1)S(1)} collective-permute-done((bf16[2128,128]{1,0:T(8,128)(2,1)}, bf16[2128,128]{1,0:T(8,128)(2,1)S(1)}, u32[]{:S(2)}, u32[]{:S(2)}) %collective-permute-start) | collective-permute-done | bytes 544800 | tf_op jit(solution)/shard_map/ppermute | solution.py:977
  32.5 9.8 %collective-permute-done.2.refs_4_ = bf16[2128,128]{1,0:T(8,128)(2,1)S(1)} collective-permute-done((bf16[2128,128]{1,0:T(8,128)(2,1)}, bf16[2128,128]{1,0:T(8,128)(2,1)S(1)}, u32[]{:S(2)}, u32[]{:S(2)}) %collective-permute-start.2) | collective-permute-done | bytes 544800 | tf_op jit(solution)/shard_map/ppermute | solution.py:977
  49.0 9.6 %all-to-all-done = bf16[4,2048,128]{2,1,0:T(8,128)(2,1)S(1)} async-done(((bf16[4,2048,128]{2,1,0:T(8,128)(2,1)}), bf16[4,2048,128]{2,1,0:T(8,128)(2,1)S(1)}, u32[]{:S(2)}, u32[]{:S(2)}) %all-to-all-start) | async-done | bytes 2097184 | tf_op jit(solution)/shard_map/all_to_all | solution.py:1013
  60.0 30.2 %all_to_all.35 = bf16[4,1104,128]{2,1,0:T(8,128)(2,1)S(1)} all-to-all(bf16[4,1104,128]{2,1,0:T(8,128)(2,1)} %by_section.2), channel_id=1, replica_groups=mesh['section'=4,'tensor'=4,'dp'=2] {'tensor'}, dimensions={0} | all-to-all | bytes 2260992 | tf_op jit(solution)/shard_map/all_to_all | solution.py:1013
  98.8 5.6 %collective-permute-done.3.refs_1_ = bf16[4,512,128]{2,1,0:T(8,128)(2,1)} collective-permute-done((bf16[4,512,128]{2,1,0:T(8,128)(2,1)S(1)}, bf16[4,512,128]{2,1,0:T(8,128)(2,1)}, u32[]{:S(2)}, u32[]{:S(2)}) %collective-permute-start.3) | collective-permute-done | bytes 524320 | tf_op jit(solution)/shard_map/ppermute | solution.py:977
  113.3 7.2 %all-to-all-done.2 = bf16[4,1024,128]{2,1,0:T(8,128)(2,1)S(1)} async-done(((bf16[4,1024,128]{2,1,0:T(8,128)(2,1)}), bf16[4,1024,128]{2,1,0:T(8,128)(2,1)S(1)}, u32[]{:S(2)}, u32[]{:S(2)}) %all-to-all-start.2) | async-done | bytes 1048608 | tf_op jit(solution)/shard_map/all_to_all | solution.py:1013
  129.5 10.8 %collective-permute-done.8 = bf16[8,512,128]{2,1,0:T(8,128)(2,1)} collective-permute-done((bf16[8,512,128]{2,1,0:T(8,128)(2,1)}, bf16[8,512,128]{2,1,0:T(8,128)(2,1)}, u32[]{:S(2)}, u32[]{:S(2)}) %collective-permute-start.8) | collective-permute-done | bytes 1048608 | tf_op jit(solution)/shard_map/ppermute | solution.py:977
  147.5 14.4 %forward_layer.4 = (f32[8192,128]{1,0:T(8,128)}, bf16[8192,128]{1,0:T(8,128)(2,1)}, bf16[8192,128]{1,0:T(8,128)(2,1)}, bf16[8192,128]{1,0:T(8,128)(2,1)}, f32[8,128]{1,0:T(8,128)}, /*index=5*/f32[8,128]{1,0:T(8,128)}) custom-call(s32[3,64]{1,0:T(4,128)} %pad_add_fusion.refs_0_, f32[8,128]{1,0:T(8,128)} %broadcast_in_dim.6.refs_1_, ...), custom_call_target="tpu_custom_call" | custom-call | flops 4000000000 | bytes 20971520 | tf_op jit(solution)/shard_map/forward_layer/pallas_call | solution.py:605
  167.9 13.7 %forward_layer.5 = (f32[8192,128]{1,0:T(8,128)}, bf16[8192,128]{1,0:T(8,128)(2,1)}, bf16[8192,128]{1,0:T(8,128)(2,1)}, bf16[8192,128]{1,0:T(8,128)(2,1)}, f32[8,128]{1,0:T(8,128)}, /*index=5*/f32[8,128]{1,0:T(8,128)}) custom-call(s32[3,64]{1,0:T(4,128)} %pad_add_fusion.refs_0_, f32[8,128]{1,0:T(8,128)} %get-tuple-element.215.refs_1_, ...), custom_call_target="tpu_custom_call" | custom-call | flops 4000000000 | bytes 20971520 | tf_op jit(solution)/shard_map/forward_layer/pallas_call | solution.py:605
  182.6 13.8 %forward_layer.6 = (f32[8192,128]{1,0:T(8,128)}, bf16[8192,128]{1,0:T(8,128)(2,1)}, bf16[8192,128]{1,0:T(8,128)(2,1)}, bf16[8192,128]{1,0:T(8,128)(2,1)}, f32[8,128]{1,0:T(8,128)}, /*index=5*/f32[8,128]{1,0:T(8,128)}) custom-call(s32[3,64]{1,0:T(4,128)} %pad_add_fusion.refs_0_, f32[8,128]{1,0:T(8,128)} %get-tuple-element.232.refs_1_, ...), custom_call_target="tpu_custom_call" | custom-call | flops 4000000000 | bytes 20971520 | tf_op jit(solution)/shard_map/forward_layer/pallas_call | solution.py:605
  196.4 13.8 %forward_layer.7 = (f32[8192,128]{1,0:T(8,128)}, bf16[8192,128]{1,0:T(8,128)(2,1)}, bf16[8192,128]{1,0:T(8,128)(2,1)}, bf16[8192,128]{1,0:T(8,128)(2,1)}, f32[8,128]{1,0:T(8,128)}, /*index=5*/f32[8,128]{1,0:T(8,128)}) custom-call(s32[3,64]{1,0:T(4,128)} %pad_add_fusion.refs_0_, f32[8,128]{1,0:T(8,128)} %get-tuple-element.250.refs_1_, ...), custom_call_target="tpu_custom_call" | custom-call | flops 4000000000 | bytes 20971520 | tf_op jit(solution)/shard_map/forward_layer/pallas_call | solution.py:605
  210.2 19.6 %backward_layer.4 = (f32[8192,128]{1,0:T(8,128)}, bf16[16,2,2,128,128]{4,3,2,1,0:T(8,128)(2,1)}, bf16[16,2,2,128,128]{4,3,2,1,0:T(8,128)(2,1)}) custom-call(s32[3,64]{1,0:T(4,128)} %pad_add_fusion.refs_0_, f32[8,128]{1,0:T(8,128)} %get-tuple-element.256.refs_1_, bf16[128,64]{1,0:T(8,128)(2,1)} %get-tuple-element.353.refs_2_, f32[8,128,8]{2,1,0:T(8,128)} %bitcast.101, ...), custom_call_target="tpu_custom_call" | custom-call | flops 5000000000 | bytes 31457280 | tf_op jit(solution)/shard_map/backward_layer/pallas_call | solution.py:636
  230.4 17.9 %backward_layer.5 = (f32[8192,128]{1,0:T(8,128)}, bf16[16,2,2,128,128]{4,3,2,1,0:T(8,128)(2,1)}, bf16[16,2,2,128,128]{4,3,2,1,0:T(8,128)(2,1)}) custom-call(s32[3,64]{1,0:T(4,128)} %pad_add_fusion.refs_0_, f32[8,128]{1,0:T(8,128)} %get-tuple-element.238.refs_1_, bf16[128,64]{1,0:T(8,128)(2,1)} %get-tuple-element.354.refs_2_, f32[8,128,8]{2,1,0:T(8,128)} %bitcast.102, ...), custom_call_target="tpu_custom_call" | custom-call | flops 5000000000 | bytes 31457280 | tf_op jit(solution)/shard_map/backward_layer/pallas_call | solution.py:636
  255.7 17.8 %backward_layer.6 = (f32[8192,128]{1,0:T(8,128)}, bf16[16,2,2,128,128]{4,3,2,1,0:T(8,128)(2,1)}, bf16[16,2,2,128,128]{4,3,2,1,0:T(8,128)(2,1)}) custom-call(s32[3,64]{1,0:T(4,128)} %pad_add_fusion.refs_0_, f32[8,128]{1,0:T(8,128)} %get-tuple-element.221.refs_1_, bf16[128,64]{1,0:T(8,128)(2,1)} %get-tuple-element.355.refs_2_, f32[8,128,8]{2,1,0:T(8,128)} %bitcast.103, ...), custom_call_target="tpu_custom_call" | custom-call | flops 5000000000 | bytes 31457280 | tf_op jit(solution)/shard_map/backward_layer/pallas_call | solution.py:636
  273.6 4.8 %collective-permute-done.22 = bf16[2048,128]{1,0:T(8,128)(2,1)S(1)} collective-permute-done((bf16[2048,128]{1,0:T(8,128)(2,1)}, bf16[2048,128]{1,0:T(8,128)(2,1)S(1)}, u32[]{:S(2)}, u32[]{:S(2)}) %collective-permute-start.22) | collective-permute-done | bytes 524320 | tf_op jit(solution)/shard_map/ppermute | solution.py:977
  285.9 17.6 %backward_layer.7 = (bf16[8192,128]{1,0:T(8,128)(2,1)}, bf16[16,2,2,128,128]{4,3,2,1,0:T(8,128)(2,1)}, bf16[16,2,2,128,128]{4,3,2,1,0:T(8,128)(2,1)}) custom-call(s32[3,64]{1,0:T(4,128)} %pad_add_fusion.refs_0_, f32[8,128]{1,0:T(8,128)} %get-tuple-element.203.refs_1_, bf16[128,64]{1,0:T(8,128)(2,1)} %get-tuple-element.356.refs_2_, f32[8,128,8]{2,1,0:T(8,128)} %bitcast.104, ...), custom_call_target="tpu_custom_call" | custom-call | flops 5000000000 | bytes 31457280 | tf_op jit(solution)/shard_map/backward_layer/pallas_call | solution.py:636
  321.2 11.1 %collective-permute-done.29 = bf16[2048,128]{1,0:T(8,128)(2,1)S(1)} collective-permute-done((bf16[2048,128]{1,0:T(8,128)(2,1)}, bf16[2048,128]{1,0:T(8,128)(2,1)S(1)}, u32[]{:S(2)}, u32[]{:S(2)}) %collective-permute-start.29) | collective-permute-done | bytes 524320 | tf_op jit(solution)/shard_map/ppermute | solution.py:977
  332.3 11.4 %collective-permute-done.30 = bf16[2048,128]{1,0:T(8,128)(2,1)S(1)} collective-permute-done((bf16[2048,128]{1,0:T(8,128)(2,1)}, bf16[2048,128]{1,0:T(8,128)(2,1)S(1)}, u32[]{:S(2)}, u32[]{:S(2)}) %collective-permute-start.30) | collective-permute-done | bytes 524320 | tf_op jit(solution)/shard_map/ppermute | solution.py:977
  348.8 10.7 %all-to-all-done.4.came_ref = bf16[4,2048,128]{2,1,0:T(8,128)(2,1)S(1)} async-done(((bf16[4,2048,128]{2,1,0:T(8,128)(2,1)}), bf16[4,2048,128]{2,1,0:T(8,128)(2,1)S(1)}, u32[]{:S(2)}, u32[]{:S(2)}) %all-to-all-start.4) | async-done | bytes 2097184 | tf_op jit(solution)/shard_map/all_to_all | solution.py:1013
  359.5 4.4 all-to-all-start.5
  369.9 9.6 %collective-permute-done.32 = bf16[2048,128]{1,0:T(8,128)(2,1)S(1)} collective-permute-done((bf16[2048,128]{1,0:T(8,128)(2,1)}, bf16[2048,128]{1,0:T(8,128)(2,1)S(1)}, u32[]{:S(2)}, u32[]{:S(2)}) %collective-permute-start.32) | collective-permute-done | bytes 524320 | tf_op jit(solution)/shard_map/ppermute | solution.py:977
  380.4 10.6 %collective-permute-done.34 = bf16[2048,128]{1,0:T(8,128)(2,1)S(1)} collective-permute-done((bf16[2048,128]{1,0:T(8,128)(2,1)}, bf16[2048,128]{1,0:T(8,128)(2,1)S(1)}, u32[]{:S(2)}, u32[]{:S(2)}) %collective-permute-start.34) | collective-permute-done | bytes 524320 | tf_op jit(solution)/shard_map/ppermute | solution.py:977
  394.2 6.2 %all-to-all-done.5 = bf16[4,1536,128]{2,1,0:T(8,128)(2,1)} async-done(((bf16[4,1536,128]{2,1,0:T(8,128)(2,1)}), bf16[4,1536,128]{2,1,0:T(8,128)(2,1)}, u32[]{:S(2)}, u32[]{:S(2)}) %all-to-all-start.5) | async-done | bytes 1572896 | tf_op jit(solution)/shard_map/all_to_all | solution.py:1013
  400.4 4.1 all-to-all-start.6
  406.5 4.2 collective-permute-start.36
  412.6 5.2 %collective-permute-start.38 = (bf16[512,128]{1,0:T(8,128)(2,1)S(1)}, bf16[512,128]{1,0:T(8,128)(2,1)}, u32[]{:S(2)}, u32[]{:S(2)}) collective-permute-start(bf16[512,128]{1,0:T(8,128)(2,1)S(1)} %bitcast.168), channel_id=1, source_target_pairs={{0,6},{1,7},{2,12},{3,13},{4,18},{5,19},{6,24},{7,25},{8,4},{9,5},... | collective-permute-start | bytes 393224 | tf_op jit(solution)/shard_map/ppermute | solution.py:977
  423.8 4.1 collective-permute-done.38.refs_3_
  434.9 5.9 %assemble.1 = (f32[4,16,128,128]{3,2,1,0:T(8,128)}, f32[4,16,128,128]{3,2,1,0:T(8,128)}) custom-call(s32[3]{0:T(128)} %pad_add_fusion.1.refs_0_, bf16[128,128]{1,0:T(8,128)(2,1)} %fusion.refs_1_, bf16[4,1,2,2,128,128]{5,4,3,2,1,0:T(8,128)(2,1)} %bitcast.116, bf16[4,1,2,2,128,128]{5,4,3,2,1,0:T(8,128)(2,1)} %bitcast.131, ...), custom_call_target="tpu_custom_call" | custom-call | bytes 12582912 | tf_op jit(solution)/shard_map/assemble/pallas_call | solution.py:920
  (186 shorter events, 121.3 us)
Async XLA Ops:
  6.2 52.4 %all-to-all-start = ((bf16[4,2048,128]{2,1,0:T(8,128)(2,1)}), bf16[4,2048,128]{2,1,0:T(8,128)(2,1)S(1)}, u32[]{:S(2)}, u32[]{:S(2)}) async-start(bf16[4,2048,128]{2,1,0:T(8,128)(2,1)} %pick.2), calls=%async_computation | async-start | bytes 4194304 | tf_op jit(solution)/shard_map/all_to_all | solution.py:1013
  19.0 23.3 %collective-permute-start.2 = (bf16[2128,128]{1,0:T(8,128)(2,1)}, bf16[2128,128]{1,0:T(8,128)(2,1)S(1)}, u32[]{:S(2)}, u32[]{:S(2)}) collective-permute-start(bf16[2128,128]{1,0:T(8,128)(2,1)} %get-tuple-element.182), channel_id=1, source_target_pairs={{0,24},{1,25},{2,26},{3,27},{4,28},{5,29},{6,30},{7,31},{8,16},{9,... | collective-permute-start | bytes 1634312 | tf_op jit(solution)/shard_map/ppermute | solution.py:977
  91.8 28.7 %all-to-all-start.2 = ((bf16[4,1024,128]{2,1,0:T(8,128)(2,1)}), bf16[4,1024,128]{2,1,0:T(8,128)(2,1)S(1)}, u32[]{:S(2)}, u32[]{:S(2)}) async-start(bf16[4,1024,128]{2,1,0:T(8,128)(2,1)} %by_section.3), calls=%async_computation.2 | async-start | bytes 2097152 | tf_op jit(solution)/shard_map/all_to_all | solution.py:1013
  112.6 16.9 %collective-permute-start.9 = (bf16[8,512,128]{2,1,0:T(8,128)(2,1)}, bf16[8,512,128]{2,1,0:T(8,128)(2,1)}, u32[]{:S(2)}, u32[]{:S(2)}) collective-permute-start(bf16[8,512,128]{2,1,0:T(8,128)(2,1)} %join.6), channel_id=1, source_target_pairs={{0,1},{1,0},{2,3},{3,2},{4,5},{5,4},{6,7},{7,6},{8,9},{9,8},{10,11... | collective-permute-start | bytes 3145736 | tf_op jit(solution)/shard_map/ppermute | solution.py:977
  112.7 27.6 %collective-permute-start.8 = (bf16[8,512,128]{2,1,0:T(8,128)(2,1)}, bf16[8,512,128]{2,1,0:T(8,128)(2,1)}, u32[]{:S(2)}, u32[]{:S(2)}) collective-permute-start(bf16[8,512,128]{2,1,0:T(8,128)(2,1)} %join.6), channel_id=1, source_target_pairs={{0,16},{1,9},{2,18},{3,11},{4,20},{5,13},{6,22},{7,15},{8,24},{9,1... | collective-permute-start | bytes 3145736 | tf_op jit(solution)/shard_map/ppermute | solution.py:977
  123.5 16.9 %collective-permute-start.7 = (bf16[8,512,128]{2,1,0:T(8,128)(2,1)}, bf16[8,512,128]{2,1,0:T(8,128)(2,1)}, u32[]{:S(2)}, u32[]{:S(2)}) collective-permute-start(bf16[8,512,128]{2,1,0:T(8,128)(2,1)} %collective-permute-done.5), channel_id=1, source_target_pairs={{0,1},{1,0},{2,3},{3,2},{4,5},{5,4},{6,7},{7,6},{8,9},{9,8},{10,11... | collective-permute-start | bytes 3145736 | tf_op jit(solution)/shard_map/ppermute | solution.py:977
  124.5 15.8 %collective-permute-start.10 = (bf16[4,512,128]{2,1,0:T(8,128)(2,1)S(1)}, bf16[4,512,128]{2,1,0:T(8,128)(2,1)}, u32[]{:S(2)}, u32[]{:S(2)}) collective-permute-start(bf16[4,512,128]{2,1,0:T(8,128)(2,1)S(1)} %get-tuple-element.210.refs_0_), channel_id=1, source_target_pairs={{0,8},{1,17},{2,10},{3,19},{4,12},{5,21},{6,14},{7,23},{8,0},{9,25... | collective-permute-start | bytes 1572872 | tf_op jit(solution)/shard_map/ppermute | solution.py:977
  125.7 70.7 %all-to-all-start.3 = ((bf16[4,2048,128]{2,1,0:T(8,128)(2,1)}), bf16[4,2048,128]{2,1,0:T(8,128)(2,1)S(1)}, u32[]{:S(2)}, u32[]{:S(2)}) async-start(bf16[4,2048,128]{2,1,0:T(8,128)(2,1)} %pick.3), calls=%async_computation.3 | async-start | bytes 4194304 | tf_op jit(solution)/shard_map/all_to_all | solution.py:1013
  142.6 19.4 %collective-permute-start.13 = (bf16[8,512,128]{2,1,0:T(8,128)(2,1)}, bf16[8,512,128]{2,1,0:T(8,128)(2,1)}, u32[]{:S(2)}, u32[]{:S(2)}) collective-permute-start(bf16[8,512,128]{2,1,0:T(8,128)(2,1)} %join.7), channel_id=1, source_target_pairs={{0,1},{1,0},{2,3},{3,2},{4,5},{5,4},{6,7},{7,6},{8,9},{9,8},{10,11... | collective-permute-start | bytes 3145736 | tf_op jit(solution)/shard_map/ppermute | solution.py:977
  143.6 19.9 %collective-permute-start.12 = (bf16[8,512,128]{2,1,0:T(8,128)(2,1)}, bf16[8,512,128]{2,1,0:T(8,128)(2,1)}, u32[]{:S(2)}, u32[]{:S(2)}) collective-permute-start(bf16[8,512,128]{2,1,0:T(8,128)(2,1)} %join.7), channel_id=1, source_target_pairs={{0,16},{1,9},{2,18},{3,11},{4,20},{5,13},{6,22},{7,15},{8,24},{9,1... | collective-permute-start | bytes 3145736 | tf_op jit(solution)/shard_map/ppermute | solution.py:977
  144.8 18.7 %collective-permute-start.14 = (bf16[8,512,128]{2,1,0:T(8,128)(2,1)}, bf16[8,512,128]{2,1,0:T(8,128)(2,1)}, u32[]{:S(2)}, u32[]{:S(2)}) collective-permute-start(bf16[8,512,128]{2,1,0:T(8,128)(2,1)} %collective-permute-done.8), channel_id=1, source_target_pairs={{0,1},{1,0},{2,3},{3,2},{4,5},{5,4},{6,7},{7,6},{8,9},{9,8},{10,11... | collective-permute-start | bytes 3145736 | tf_op jit(solution)/shard_map/ppermute | solution.py:977
  145.6 16.3 %collective-permute-start.11 = (bf16[4,512,128]{2,1,0:T(8,128)(2,1)S(1)}, bf16[4,512,128]{2,1,0:T(8,128)(2,1)S(1)}, u32[]{:S(2)}, u32[]{:S(2)}) collective-permute-start(bf16[4,512,128]{2,1,0:T(8,128)(2,1)S(1)} %get-tuple-element.227.refs_0_), channel_id=1, source_target_pairs={{0,8},{1,17},{2,10},{3,19},{4,12},{5,21},{6,14},{7,23},{8,0},{9,25... | collective-permute-start | bytes 1572872 | tf_op jit(solution)/shard_map/ppermute | solution.py:977
  165.7 15.9 %collective-permute-start.16 = (bf16[8,512,128]{2,1,0:T(8,128)(2,1)}, bf16[8,512,128]{2,1,0:T(8,128)(2,1)}, u32[]{:S(2)}, u32[]{:S(2)}) collective-permute-start(bf16[8,512,128]{2,1,0:T(8,128)(2,1)} %join.8), channel_id=1, source_target_pairs={{0,1},{1,0},{2,3},{3,2},{4,5},{5,4},{6,7},{7,6},{8,9},{9,8},{10,11... | collective-permute-start | bytes 3145736 | tf_op jit(solution)/shard_map/ppermute | solution.py:977
  229.9 18.5 %collective-permute-start.19 = (bf16[16,2,2,128,128]{4,3,2,1,0:T(8,128)(2,1)}, bf16[16,2,2,128,128]{4,3,2,1,0:T(8,128)(2,1)S(1)}, u32[]{:S(2)}, u32[]{:S(2)}) collective-permute-start(bf16[16,2,2,128,128]{4,3,2,1,0:T(8,128)(2,1)} %get-tuple-element.267), channel_id=1, source_target_pairs={{0,1},{1,0},{2,3},{3,2},{4,5},{5,4},{6,7},{7,6},{8,9},{9,8},{10,11... | collective-permute-start | bytes 6291464 | tf_op jit(solution)/shard_map/ppermute | solution.py:977
  249.7 28.7 %collective-permute-start.23 = (bf16[16,2,2,128,128]{4,3,2,1,0:T(8,128)(2,1)}, bf16[16,2,2,128,128]{4,3,2,1,0:T(8,128)(2,1)S(1)}, u32[]{:S(2)}, u32[]{:S(2)}) collective-permute-start(bf16[16,2,2,128,128]{4,3,2,1,0:T(8,128)(2,1)} %get-tuple-element.279), channel_id=1, source_target_pairs={{0,1},{1,0},{2,3},{3,2},{4,5},{5,4},{6,7},{7,6},{8,9},{9,8},{10,11... | collective-permute-start | bytes 6291464 | tf_op jit(solution)/shard_map/ppermute | solution.py:977
  253.1 20.5 %collective-permute-start.20 = (bf16[2048,128]{1,0:T(8,128)(2,1)}, bf16[2048,128]{1,0:T(8,128)(2,1)S(1)}, u32[]{:S(2)}, u32[]{:S(2)}) collective-permute-start(bf16[2048,128]{1,0:T(8,128)(2,1)} %bitcast.161), channel_id=1, source_target_pairs={{0,8},{1,9},{2,10},{3,11},{4,12},{5,13},{6,14},{7,15},{8,0},{9,1},... | collective-permute-start | bytes 1572872 | tf_op jit(solution)/shard_map/ppermute | solution.py:977
  254.0 19.5 %collective-permute-start.21 = (bf16[2048,128]{1,0:T(8,128)(2,1)}, bf16[2048,128]{1,0:T(8,128)(2,1)S(1)}, u32[]{:S(2)}, u32[]{:S(2)}) collective-permute-start(bf16[2048,128]{1,0:T(8,128)(2,1)} %bitcast.159), channel_id=1, source_target_pairs={{0,16},{1,17},{2,18},{3,19},{4,20},{5,21},{6,22},{7,23},{8,24},{9,... | collective-permute-start | bytes 1572872 | tf_op jit(solution)/shard_map/ppermute | solution.py:977
  254.9 23.5 %collective-permute-start.22 = (bf16[2048,128]{1,0:T(8,128)(2,1)}, bf16[2048,128]{1,0:T(8,128)(2,1)S(1)}, u32[]{:S(2)}, u32[]{:S(2)}) collective-permute-start(bf16[2048,128]{1,0:T(8,128)(2,1)} %bitcast.157), channel_id=1, source_target_pairs={{0,24},{1,25},{2,26},{3,27},{4,28},{5,29},{6,30},{7,31},{8,16},{9,... | collective-permute-start | bytes 1572872 | tf_op jit(solution)/shard_map/ppermute | solution.py:977
  278.4 29.1 %collective-permute-start.27 = (bf16[16,2,2,128,128]{4,3,2,1,0:T(8,128)(2,1)}, bf16[16,2,2,128,128]{4,3,2,1,0:T(8,128)(2,1)}, u32[]{:S(2)}, u32[]{:S(2)}) collective-permute-start(bf16[16,2,2,128,128]{4,3,2,1,0:T(8,128)(2,1)} %get-tuple-element.295), channel_id=1, source_target_pairs={{0,1},{1,0},{2,3},{3,2},{4,5},{5,4},{6,7},{7,6},{8,9},{9,8},{10,11... | collective-permute-start | bytes 6291464 | tf_op jit(solution)/shard_map/ppermute | solution.py:977
  283.3 20.3 %collective-permute-start.24 = (bf16[2048,128]{1,0:T(8,128)(2,1)}, bf16[2048,128]{1,0:T(8,128)(2,1)S(1)}, u32[]{:S(2)}, u32[]{:S(2)}) collective-permute-start(bf16[2048,128]{1,0:T(8,128)(2,1)} %bitcast.160), channel_id=1, source_target_pairs={{0,8},{1,9},{2,10},{3,11},{4,12},{5,13},{6,14},{7,15},{8,0},{9,1},... | collective-permute-start | bytes 1572872 | tf_op jit(solution)/shard_map/ppermute | solution.py:977
  284.2 20.2 %collective-permute-start.25 = (bf16[2048,128]{1,0:T(8,128)(2,1)}, bf16[2048,128]{1,0:T(8,128)(2,1)S(1)}, u32[]{:S(2)}, u32[]{:S(2)}) collective-permute-start(bf16[2048,128]{1,0:T(8,128)(2,1)} %bitcast.158), channel_id=1, source_target_pairs={{0,16},{1,17},{2,18},{3,19},{4,20},{5,21},{6,22},{7,23},{8,24},{9,... | collective-permute-start | bytes 1572872 | tf_op jit(solution)/shard_map/ppermute | solution.py:977
  284.4 23.0 %collective-permute-start.26 = (bf16[2048,128]{1,0:T(8,128)(2,1)}, bf16[2048,128]{1,0:T(8,128)(2,1)S(1)}, u32[]{:S(2)}, u32[]{:S(2)}) collective-permute-start(bf16[2048,128]{1,0:T(8,128)(2,1)} %bitcast.156), channel_id=1, source_target_pairs={{0,24},{1,25},{2,26},{3,27},{4,28},{5,29},{6,30},{7,31},{8,16},{9,... | collective-permute-start | bytes 1572872 | tf_op jit(solution)/shard_map/ppermute | solution.py:977
  308.3 51.3 %all-to-all-start.4 = ((bf16[4,2048,128]{2,1,0:T(8,128)(2,1)}), bf16[4,2048,128]{2,1,0:T(8,128)(2,1)S(1)}, u32[]{:S(2)}, u32[]{:S(2)}) async-start(bf16[4,2048,128]{2,1,0:T(8,128)(2,1)} %bitcast.121), calls=%async_computation.4 | async-start | bytes 4194304 | tf_op jit(solution)/shard_map/all_to_all | solution.py:1013
  311.9 31.9 %collective-permute-start.28 = (bf16[16,2,2,128,128]{4,3,2,1,0:T(8,128)(2,1)}, bf16[16,2,2,128,128]{4,3,2,1,0:T(8,128)(2,1)}, u32[]{:S(2)}, u32[]{:S(2)}) collective-permute-start(bf16[16,2,2,128,128]{4,3,2,1,0:T(8,128)(2,1)} %get-tuple-element.297), channel_id=1, source_target_pairs={{0,1},{1,0},{2,3},{3,2},{4,5},{5,4},{6,7},{7,6},{8,9},{9,8},{10,11... | collective-permute-start | bytes 6291464 | tf_op jit(solution)/shard_map/ppermute | solution.py:977
  319.1 24.6 %collective-permute-start.30 = (bf16[2048,128]{1,0:T(8,128)(2,1)}, bf16[2048,128]{1,0:T(8,128)(2,1)S(1)}, u32[]{:S(2)}, u32[]{:S(2)}) collective-permute-start(bf16[2048,128]{1,0:T(8,128)(2,1)} %bitcast.164), channel_id=1, source_target_pairs={{0,16},{1,17},{2,18},{3,19},{4,20},{5,21},{6,22},{7,23},{8,24},{9,... | collective-permute-start | bytes 1572872 | tf_op jit(solution)/shard_map/ppermute | solution.py:977
  319.9 23.8 %collective-permute-start.31 = (bf16[2048,128]{1,0:T(8,128)(2,1)}, bf16[2048,128]{1,0:T(8,128)(2,1)S(1)}, u32[]{:S(2)}, u32[]{:S(2)}) collective-permute-start(bf16[2048,128]{1,0:T(8,128)(2,1)} %bitcast.162), channel_id=1, source_target_pairs={{0,24},{1,25},{2,26},{3,27},{4,28},{5,29},{6,30},{7,31},{8,16},{9,... | collective-permute-start | bytes 1572872 | tf_op jit(solution)/shard_map/ppermute | solution.py:977
  359.5 40.9 %all-to-all-start.5 = ((bf16[4,1536,128]{2,1,0:T(8,128)(2,1)}), bf16[4,1536,128]{2,1,0:T(8,128)(2,1)}, u32[]{:S(2)}, u32[]{:S(2)}) async-start(bf16[4,1536,128]{2,1,0:T(8,128)(2,1)} %bitcast.107), calls=%async_computation.5 | async-start | bytes 3145728 | tf_op jit(solution)/shard_map/all_to_all | solution.py:1013
  369.3 21.7 %collective-permute-start.34 = (bf16[2048,128]{1,0:T(8,128)(2,1)}, bf16[2048,128]{1,0:T(8,128)(2,1)S(1)}, u32[]{:S(2)}, u32[]{:S(2)}) collective-permute-start(bf16[2048,128]{1,0:T(8,128)(2,1)} %bitcast.163), channel_id=1, source_target_pairs={{0,24},{1,25},{2,26},{3,27},{4,28},{5,29},{6,30},{7,31},{8,16},{9,... | collective-permute-start | bytes 1572872 | tf_op jit(solution)/shard_map/ppermute | solution.py:977
  400.4 27.6 %all-to-all-start.6 = ((bf16[4,1536,128]{2,1,0:T(8,128)(2,1)}), bf16[4,1536,128]{2,1,0:T(8,128)(2,1)S(1)}, u32[]{:S(2)}, u32[]{:S(2)}) async-start(bf16[4,1536,128]{2,1,0:T(8,128)(2,1)} %all-to-all-done.5), calls=%async_computation.6 | async-start | bytes 3145728 | tf_op jit(solution)/shard_map/all_to_all | solution.py:1016
  404.5 17.2 %collective-permute-start.35 = (bf16[512,128]{1,0:T(8,128)(2,1)S(1)}, bf16[512,128]{1,0:T(8,128)(2,1)S(1)}, u32[]{:S(2)}, u32[]{:S(2)}) collective-permute-start(bf16[512,128]{1,0:T(8,128)(2,1)S(1)} %bitcast.171), channel_id=1, source_target_pairs={{0,0},{1,1},{2,10},{3,11},{4,20},{5,21},{6,30},{7,31},{8,2},{9,3},... | collective-permute-start | bytes 393224 | tf_op jit(solution)/shard_map/ppermute | solution.py:977
  406.5 15.2 %collective-permute-start.36 = (bf16[512,128]{1,0:T(8,128)(2,1)S(1)}, bf16[512,128]{1,0:T(8,128)(2,1)S(1)}, u32[]{:S(2)}, u32[]{:S(2)}) collective-permute-start(bf16[512,128]{1,0:T(8,128)(2,1)S(1)} %bitcast.170), channel_id=1, source_target_pairs={{0,2},{1,3},{2,8},{3,9},{4,22},{5,23},{6,28},{7,29},{8,0},{9,1},{1... | collective-permute-start | bytes 393224 | tf_op jit(solution)/shard_map/ppermute | solution.py:977
  412.6 15.3 %collective-permute-start.38 = (bf16[512,128]{1,0:T(8,128)(2,1)S(1)}, bf16[512,128]{1,0:T(8,128)(2,1)}, u32[]{:S(2)}, u32[]{:S(2)}) collective-permute-start(bf16[512,128]{1,0:T(8,128)(2,1)S(1)} %bitcast.168), channel_id=1, source_target_pairs={{0,6},{1,7},{2,12},{3,13},{4,18},{5,19},{6,24},{7,25},{8,4},{9,5},... | collective-permute-start | bytes 393224 | tf_op jit(solution)/shard_map/ppermute | solution.py:977
  (54 other events, 521.4 us)

commit v18 on v17

--- a/solution.py
+++ b/solution.py
@@ -1117,7 +1117,7 @@
     ended[0] = plane_sum(*ended[0])
     others = to_planes(run_sum(ended[1:], width, apart=False))
     home = run_sum(ended[:1], width)
-    home, returned, others = tie((home, returned, others))
+    home, returned = tie((home, returned))
     home = move_all(home, "homes")
     d_patches = run_combine(critic_pairs, returned)
     others = to_sections(others)

time: 446 us -> 488 us (1.094)
  blocking collectives: 30.2 us -> 70.7 us
  waiting for transfers between devices: 134 us -> 143 us
    all_to_all x1 -> x2, blocking collectives: 30.2 us -> 70.7 us  [to_planes(): lax.all_to_all(value, 'tensor', split_axis=0, concat_axis=0, tiled=True)]
    ppermute x41, waiting for transfers between devices: 100 us -> 115 us  [move(): return lax.ppermute(value, AXES, route)]
    all_to_all x5 -> x4, waiting for transfers between devices: 33.8 us -> 27.5 us  [to_planes(): lax.all_to_all(value, 'tensor', split_axis=0, concat_axis=0, tiled=True)]
    all_to_all x5 -> x4, starting transfers between devices: 20 us -> 15.6 us  [to_planes(): lax.all_to_all(value, 'tensor', split_axis=0, concat_axis=0, tiled=True)]
    unnamed x79 -> x71, local copies, waits for them, and re-layouts: 10.9 us -> 10.9 us
  transfers between devices with their start and end apart: 47 -> 46, of which waited for: 22 -> 21; matrix products, arithmetic and copies ran while one was open for 1% -> 1% of each run, Pallas kernels for 33% -> 30%
where the time goes in v18:
time: 488 us; the launch traced here: 486 us
  Pallas kernels  188 us (39%)
  waiting for transfers between devices  143 us (29%)
  blocking collectives  70.7 us (14%)
  starting transfers between devices  66.9 us (14%)
  local copies, waits for them, and re-layouts  14.9 us (3%)
    ppermute x41, waiting for transfers between devices, move(): return lax.ppermute(value, AXES, route)  115 us
    pallas_call x4, Pallas kernels, run_backward(): pl.pallas_call(lambda *refs: backward_kernel(turning, last, layer, len(so...  73.1 us
    all_to_all x2, blocking collectives, to_planes(): lax.all_to_all(value, 'tensor', split_axis=0, concat_axis=0, tiled=True)  70.7 us
    pallas_call x4, Pallas kernels, run_forward(): pl.pallas_call(lambda *refs: forward_kernel(first, layer, len(sources), *...  55.6 us
    ppermute x41, starting transfers between devices, move(): return lax.ppermute(value, AXES, route)  46.4 us
    all_to_all x4, waiting for transfers between devices, to_planes(): lax.all_to_all(value, 'tensor', split_axis=0, concat_axis=0, tiled=True)  27.5 us
    pallas_call x6, Pallas kernels, run_sum(): pl.pallas_call(lambda *refs: sum_kernel(len(groups[0]), len(flat), *refs)...  19.7 us
    all_to_all x4, starting transfers between devices, to_planes(): lax.all_to_all(value, 'tensor', split_axis=0, concat_axis=0, tiled=True)  15.6 us
  transfers between devices with their start and end apart: 46, of which 21 were waited for; matrix products, arithmetic and copies ran while one was open for 1% of the time, Pallas kernels for 30%

profile of v18, /device:TPU:5, one launch (start us, length us, event | category | flops | bytes accessed | tf_op | source)
XLA Modules:
  0.0 486.2 jit_solution(17776035480833929450)
XLA Ops:
  2.1 4.1 pick.2
  6.2 4.7 all-to-all-start
  12.9 4.6 pieces.1
  20.2 4.1 pick.3
  24.3 6.4 %collective-permute-done.refs_2_ = bf16[2128,128]{1,0:T(8,128)(2,1)S(1)} collective-permute-done((bf16[2128,128]{1,0:T(8,128)(2,1)}, bf16[2128,128]{1,0:T(8,128)(2,1)S(1)}, u32[]{:S(2)}, u32[]{:S(2)}) %collective-permute-start) | collective-permute-done | bytes 544800 | tf_op jit(solution)/shard_map/ppermute | solution.py:977
  32.5 9.8 %collective-permute-done.2.refs_4_ = bf16[2128,128]{1,0:T(8,128)(2,1)S(1)} collective-permute-done((bf16[2128,128]{1,0:T(8,128)(2,1)}, bf16[2128,128]{1,0:T(8,128)(2,1)S(1)}, u32[]{:S(2)}, u32[]{:S(2)}) %collective-permute-start.2) | collective-permute-done | bytes 544800 | tf_op jit(solution)/shard_map/ppermute | solution.py:977
  49.0 9.6 %all-to-all-done = bf16[4,2048,128]{2,1,0:T(8,128)(2,1)S(1)} async-done(((bf16[4,2048,128]{2,1,0:T(8,128)(2,1)}), bf16[4,2048,128]{2,1,0:T(8,128)(2,1)S(1)}, u32[]{:S(2)}, u32[]{:S(2)}) %all-to-all-start) | async-done | bytes 2097184 | tf_op jit(solution)/shard_map/all_to_all | solution.py:1013
  60.0 30.2 %all_to_all.35 = bf16[4,1104,128]{2,1,0:T(8,128)(2,1)S(1)} all-to-all(bf16[4,1104,128]{2,1,0:T(8,128)(2,1)} %by_section.2), channel_id=1, replica_groups=mesh['section'=4,'tensor'=4,'dp'=2] {'tensor'}, dimensions={0} | all-to-all | bytes 2260992 | tf_op jit(solution)/shard_map/all_to_all | solution.py:1013
  98.8 5.6 %collective-permute-done.3.refs_1_ = bf16[4,512,128]{2,1,0:T(8,128)(2,1)} collective-permute-done((bf16[4,512,128]{2,1,0:T(8,128)(2,1)S(1)}, bf16[4,512,128]{2,1,0:T(8,128)(2,1)}, u32[]{:S(2)}, u32[]{:S(2)}) %collective-permute-start.3) | collective-permute-done | bytes 524320 | tf_op jit(solution)/shard_map/ppermute | solution.py:977
  113.3 7.2 %all-to-all-done.2 = bf16[4,1024,128]{2,1,0:T(8,128)(2,1)S(1)} async-done(((bf16[4,1024,128]{2,1,0:T(8,128)(2,1)}), bf16[4,1024,128]{2,1,0:T(8,128)(2,1)S(1)}, u32[]{:S(2)}, u32[]{:S(2)}) %all-to-all-start.2) | async-done | bytes 1048608 | tf_op jit(solution)/shard_map/all_to_all | solution.py:1013
  129.6 10.8 %collective-permute-done.8 = bf16[8,512,128]{2,1,0:T(8,128)(2,1)} collective-permute-done((bf16[8,512,128]{2,1,0:T(8,128)(2,1)}, bf16[8,512,128]{2,1,0:T(8,128)(2,1)}, u32[]{:S(2)}, u32[]{:S(2)}) %collective-permute-start.8) | collective-permute-done | bytes 1048608 | tf_op jit(solution)/shard_map/ppermute | solution.py:977
  147.5 14.4 %forward_layer.4 = (f32[8192,128]{1,0:T(8,128)}, bf16[8192,128]{1,0:T(8,128)(2,1)}, bf16[8192,128]{1,0:T(8,128)(2,1)}, bf16[8192,128]{1,0:T(8,128)(2,1)}, f32[8,128]{1,0:T(8,128)}, /*index=5*/f32[8,128]{1,0:T(8,128)}) custom-call(s32[3,64]{1,0:T(4,128)} %pad_add_fusion.refs_0_, f32[8,128]{1,0:T(8,128)} %broadcast_in_dim.6.refs_1_, ...), custom_call_target="tpu_custom_call" | custom-call | flops 4000000000 | bytes 20971520 | tf_op jit(solution)/shard_map/forward_layer/pallas_call | solution.py:605
  167.9 13.7 %forward_layer.5 = (f32[8192,128]{1,0:T(8,128)}, bf16[8192,128]{1,0:T(8,128)(2,1)}, bf16[8192,128]{1,0:T(8,128)(2,1)}, bf16[8192,128]{1,0:T(8,128)(2,1)}, f32[8,128]{1,0:T(8,128)}, /*index=5*/f32[8,128]{1,0:T(8,128)}) custom-call(s32[3,64]{1,0:T(4,128)} %pad_add_fusion.refs_0_, f32[8,128]{1,0:T(8,128)} %get-tuple-element.214.refs_1_, ...), custom_call_target="tpu_custom_call" | custom-call | flops 4000000000 | bytes 20971520 | tf_op jit(solution)/shard_map/forward_layer/pallas_call | solution.py:605
  182.6 13.7 %forward_layer.6 = (f32[8192,128]{1,0:T(8,128)}, bf16[8192,128]{1,0:T(8,128)(2,1)}, bf16[8192,128]{1,0:T(8,128)(2,1)}, bf16[8192,128]{1,0:T(8,128)(2,1)}, f32[8,128]{1,0:T(8,128)}, /*index=5*/f32[8,128]{1,0:T(8,128)}) custom-call(s32[3,64]{1,0:T(4,128)} %pad_add_fusion.refs_0_, f32[8,128]{1,0:T(8,128)} %get-tuple-element.231.refs_1_, ...), custom_call_target="tpu_custom_call" | custom-call | flops 4000000000 | bytes 20971520 | tf_op jit(solution)/shard_map/forward_layer/pallas_call | solution.py:605
  196.4 13.8 %forward_layer.7 = (f32[8192,128]{1,0:T(8,128)}, bf16[8192,128]{1,0:T(8,128)(2,1)}, bf16[8192,128]{1,0:T(8,128)(2,1)}, bf16[8192,128]{1,0:T(8,128)(2,1)}, f32[8,128]{1,0:T(8,128)}, /*index=5*/f32[8,128]{1,0:T(8,128)}) custom-call(s32[3,64]{1,0:T(4,128)} %pad_add_fusion.refs_0_, f32[8,128]{1,0:T(8,128)} %get-tuple-element.249.refs_1_, ...), custom_call_target="tpu_custom_call" | custom-call | flops 4000000000 | bytes 20971520 | tf_op jit(solution)/shard_map/forward_layer/pallas_call | solution.py:605
  210.2 19.6 %backward_layer.4 = (f32[8192,128]{1,0:T(8,128)}, bf16[16,2,2,128,128]{4,3,2,1,0:T(8,128)(2,1)}, bf16[16,2,2,128,128]{4,3,2,1,0:T(8,128)(2,1)}) custom-call(s32[3,64]{1,0:T(4,128)} %pad_add_fusion.refs_0_, f32[8,128]{1,0:T(8,128)} %get-tuple-element.255.refs_1_, bf16[128,64]{1,0:T(8,128)(2,1)} %get-tuple-element.351.refs_2_, f32[8,128,8]{2,1,0:T(8,128)} %bitcast.101, ...), custom_call_target="tpu_custom_call" | custom-call | flops 5000000000 | bytes 31457280 | tf_op jit(solution)/shard_map/backward_layer/pallas_call | solution.py:636
  230.4 18.0 %backward_layer.5 = (f32[8192,128]{1,0:T(8,128)}, bf16[16,2,2,128,128]{4,3,2,1,0:T(8,128)(2,1)}, bf16[16,2,2,128,128]{4,3,2,1,0:T(8,128)(2,1)}) custom-call(s32[3,64]{1,0:T(4,128)} %pad_add_fusion.refs_0_, f32[8,128]{1,0:T(8,128)} %get-tuple-element.237.refs_1_, bf16[128,64]{1,0:T(8,128)(2,1)} %get-tuple-element.352.refs_2_, f32[8,128,8]{2,1,0:T(8,128)} %bitcast.102, ...), custom_call_target="tpu_custom_call" | custom-call | flops 5000000000 | bytes 31457280 | tf_op jit(solution)/shard_map/backward_layer/pallas_call | solution.py:636
  255.7 17.9 %backward_layer.6 = (f32[8192,128]{1,0:T(8,128)}, bf16[16,2,2,128,128]{4,3,2,1,0:T(8,128)(2,1)}, bf16[16,2,2,128,128]{4,3,2,1,0:T(8,128)(2,1)}) custom-call(s32[3,64]{1,0:T(4,128)} %pad_add_fusion.refs_0_, f32[8,128]{1,0:T(8,128)} %get-tuple-element.220.refs_1_, bf16[128,64]{1,0:T(8,128)(2,1)} %get-tuple-element.353.refs_2_, f32[8,128,8]{2,1,0:T(8,128)} %bitcast.103, ...), custom_call_target="tpu_custom_call" | custom-call | flops 5000000000 | bytes 31457280 | tf_op jit(solution)/shard_map/backward_layer/pallas_call | solution.py:636
  273.6 4.7 collective-permute-done.22
  285.9 17.7 %backward_layer.7 = (bf16[8192,128]{1,0:T(8,128)(2,1)}, bf16[16,2,2,128,128]{4,3,2,1,0:T(8,128)(2,1)}, bf16[16,2,2,128,128]{4,3,2,1,0:T(8,128)(2,1)}) custom-call(s32[3,64]{1,0:T(4,128)} %pad_add_fusion.refs_0_, f32[8,128]{1,0:T(8,128)} %get-tuple-element.202.refs_1_, bf16[128,64]{1,0:T(8,128)(2,1)} %get-tuple-element.354.refs_2_, f32[8,128,8]{2,1,0:T(8,128)} %bitcast.104, ...), custom_call_target="tpu_custom_call" | custom-call | flops 5000000000 | bytes 31457280 | tf_op jit(solution)/shard_map/backward_layer/pallas_call | solution.py:636
  321.3 11.1 %collective-permute-done.29 = bf16[2048,128]{1,0:T(8,128)(2,1)S(1)} collective-permute-done((bf16[2048,128]{1,0:T(8,128)(2,1)}, bf16[2048,128]{1,0:T(8,128)(2,1)S(1)}, u32[]{:S(2)}, u32[]{:S(2)}) %collective-permute-start.29) | collective-permute-done | bytes 524320 | tf_op jit(solution)/shard_map/ppermute | solution.py:977
  332.3 11.4 %collective-permute-done.30 = bf16[2048,128]{1,0:T(8,128)(2,1)S(1)} collective-permute-done((bf16[2048,128]{1,0:T(8,128)(2,1)}, bf16[2048,128]{1,0:T(8,128)(2,1)S(1)}, u32[]{:S(2)}, u32[]{:S(2)}) %collective-permute-start.30) | collective-permute-done | bytes 524320 | tf_op jit(solution)/shard_map/ppermute | solution.py:977
  344.7 4.1 sum.11
  348.8 10.7 %all-to-all-done.4.came_ref = bf16[4,2048,128]{2,1,0:T(8,128)(2,1)S(1)} async-done(((bf16[4,2048,128]{2,1,0:T(8,128)(2,1)}), bf16[4,2048,128]{2,1,0:T(8,128)(2,1)S(1)}, u32[]{:S(2)}, u32[]{:S(2)}) %all-to-all-start.4) | async-done | bytes 2097184 | tf_op jit(solution)/shard_map/all_to_all | solution.py:1013
  359.5 40.4 %all_to_all.36 = bf16[4,1536,128]{2,1,0:T(8,128)(2,1)} all-to-all(bf16[4,1536,128]{2,1,0:T(8,128)(2,1)} %bitcast.106), channel_id=1, replica_groups=mesh['section'=4,'tensor'=4,'dp'=2] {'tensor'}, dimensions={0} | all-to-all | bytes 3145728 | tf_op jit(solution)/shard_map/all_to_all | solution.py:1013
  400.0 4.9 %all-to-all-start.6 = ((bf16[4,1536,128]{2,1,0:T(8,128)(2,1)}), bf16[4,1536,128]{2,1,0:T(8,128)(2,1)}, u32[]{:S(2)}, u32[]{:S(2)}) async-start(bf16[4,1536,128]{2,1,0:T(8,128)(2,1)} %all_to_all.36), calls=%async_computation.6 | async-start | bytes 3145728 | tf_op jit(solution)/shard_map/all_to_all | solution.py:1016
  410.8 22.4 %collective-permute-done.32 = bf16[2048,128]{1,0:T(8,128)(2,1)S(1)} collective-permute-done((bf16[2048,128]{1,0:T(8,128)(2,1)}, bf16[2048,128]{1,0:T(8,128)(2,1)S(1)}, u32[]{:S(2)}, u32[]{:S(2)}) %collective-permute-start.32) | collective-permute-done | bytes 524320 | tf_op jit(solution)/shard_map/ppermute | solution.py:977
  433.3 11.3 %collective-permute-done.34 = bf16[2048,128]{1,0:T(8,128)(2,1)S(1)} collective-permute-done((bf16[2048,128]{1,0:T(8,128)(2,1)}, bf16[2048,128]{1,0:T(8,128)(2,1)S(1)}, u32[]{:S(2)}, u32[]{:S(2)}) %collective-permute-start.34) | collective-permute-done | bytes 524320 | tf_op jit(solution)/shard_map/ppermute | solution.py:977
  451.1 4.2 collective-permute-start.36
  460.0 3.9 combine.1
  464.3 8.6 %collective-permute-done.38.refs_3_ = bf16[512,128]{1,0:T(8,128)(2,1)S(1)} collective-permute-done((bf16[512,128]{1,0:T(8,128)(2,1)}, bf16[512,128]{1,0:T(8,128)(2,1)S(1)}, u32[]{:S(2)}, u32[]{:S(2)}) %collective-permute-start.38) | collective-permute-done | bytes 131104 | tf_op jit(solution)/shard_map/ppermute | solution.py:977
  480.2 5.9 %assemble.1 = (f32[4,16,128,128]{3,2,1,0:T(8,128)}, f32[4,16,128,128]{3,2,1,0:T(8,128)}) custom-call(s32[3]{0:T(128)} %pad_add_fusion.1.refs_0_, bf16[128,128]{1,0:T(8,128)(2,1)} %fusion.refs_1_, bf16[4,1,2,2,128,128]{5,4,3,2,1,0:T(8,128)(2,1)} %bitcast.115, bf16[4,1,2,2,128,128]{5,4,3,2,1,0:T(8,128)(2,1)} %bitcast.130, ...), custom_call_target="tpu_custom_call" | custom-call | bytes 12582912 | tf_op jit(solution)/shard_map/assemble/pallas_call | solution.py:920
  (177 shorter events, 115.5 us)
Async XLA Ops:
  6.2 52.4 %all-to-all-start = ((bf16[4,2048,128]{2,1,0:T(8,128)(2,1)}), bf16[4,2048,128]{2,1,0:T(8,128)(2,1)S(1)}, u32[]{:S(2)}, u32[]{:S(2)}) async-start(bf16[4,2048,128]{2,1,0:T(8,128)(2,1)} %pick.2), calls=%async_computation | async-start | bytes 4194304 | tf_op jit(solution)/shard_map/all_to_all | solution.py:1013
  19.0 23.4 %collective-permute-start.2 = (bf16[2128,128]{1,0:T(8,128)(2,1)}, bf16[2128,128]{1,0:T(8,128)(2,1)S(1)}, u32[]{:S(2)}, u32[]{:S(2)}) collective-permute-start(bf16[2128,128]{1,0:T(8,128)(2,1)} %get-tuple-element.181), channel_id=1, source_target_pairs={{0,24},{1,25},{2,26},{3,27},{4,28},{5,29},{6,30},{7,31},{8,16},{9,... | collective-permute-start | bytes 1634312 | tf_op jit(solution)/shard_map/ppermute | solution.py:977
  91.8 28.7 %all-to-all-start.2 = ((bf16[4,1024,128]{2,1,0:T(8,128)(2,1)}), bf16[4,1024,128]{2,1,0:T(8,128)(2,1)S(1)}, u32[]{:S(2)}, u32[]{:S(2)}) async-start(bf16[4,1024,128]{2,1,0:T(8,128)(2,1)} %by_section.3), calls=%async_computation.2 | async-start | bytes 2097152 | tf_op jit(solution)/shard_map/all_to_all | solution.py:1013
  112.7 16.9 %collective-permute-start.9 = (bf16[8,512,128]{2,1,0:T(8,128)(2,1)}, bf16[8,512,128]{2,1,0:T(8,128)(2,1)}, u32[]{:S(2)}, u32[]{:S(2)}) collective-permute-start(bf16[8,512,128]{2,1,0:T(8,128)(2,1)} %join.6), channel_id=1, source_target_pairs={{0,1},{1,0},{2,3},{3,2},{4,5},{5,4},{6,7},{7,6},{8,9},{9,8},{10,11... | collective-permute-start | bytes 3145736 | tf_op jit(solution)/shard_map/ppermute | solution.py:977
  112.7 27.6 %collective-permute-start.8 = (bf16[8,512,128]{2,1,0:T(8,128)(2,1)}, bf16[8,512,128]{2,1,0:T(8,128)(2,1)}, u32[]{:S(2)}, u32[]{:S(2)}) collective-permute-start(bf16[8,512,128]{2,1,0:T(8,128)(2,1)} %join.6), channel_id=1, source_target_pairs={{0,16},{1,9},{2,18},{3,11},{4,20},{5,13},{6,22},{7,15},{8,24},{9,1... | collective-permute-start | bytes 3145736 | tf_op jit(solution)/shard_map/ppermute | solution.py:977
  123.5 16.9 %collective-permute-start.7 = (bf16[8,512,128]{2,1,0:T(8,128)(2,1)}, bf16[8,512,128]{2,1,0:T(8,128)(2,1)}, u32[]{:S(2)}, u32[]{:S(2)}) collective-permute-start(bf16[8,512,128]{2,1,0:T(8,128)(2,1)} %collective-permute-done.5), channel_id=1, source_target_pairs={{0,1},{1,0},{2,3},{3,2},{4,5},{5,4},{6,7},{7,6},{8,9},{9,8},{10,11... | collective-permute-start | bytes 3145736 | tf_op jit(solution)/shard_map/ppermute | solution.py:977
  124.5 15.8 %collective-permute-start.10 = (bf16[4,512,128]{2,1,0:T(8,128)(2,1)S(1)}, bf16[4,512,128]{2,1,0:T(8,128)(2,1)}, u32[]{:S(2)}, u32[]{:S(2)}) collective-permute-start(bf16[4,512,128]{2,1,0:T(8,128)(2,1)S(1)} %get-tuple-element.209.refs_0_), channel_id=1, source_target_pairs={{0,8},{1,17},{2,10},{3,19},{4,12},{5,21},{6,14},{7,23},{8,0},{9,25... | collective-permute-start | bytes 1572872 | tf_op jit(solution)/shard_map/ppermute | solution.py:977
  125.7 70.6 %all-to-all-start.3 = ((bf16[4,2048,128]{2,1,0:T(8,128)(2,1)}), bf16[4,2048,128]{2,1,0:T(8,128)(2,1)S(1)}, u32[]{:S(2)}, u32[]{:S(2)}) async-start(bf16[4,2048,128]{2,1,0:T(8,128)(2,1)} %pick.3), calls=%async_computation.3 | async-start | bytes 4194304 | tf_op jit(solution)/shard_map/all_to_all | solution.py:1013
  142.6 19.4 %collective-permute-start.13 = (bf16[8,512,128]{2,1,0:T(8,128)(2,1)}, bf16[8,512,128]{2,1,0:T(8,128)(2,1)}, u32[]{:S(2)}, u32[]{:S(2)}) collective-permute-start(bf16[8,512,128]{2,1,0:T(8,128)(2,1)} %join.7), channel_id=1, source_target_pairs={{0,1},{1,0},{2,3},{3,2},{4,5},{5,4},{6,7},{7,6},{8,9},{9,8},{10,11... | collective-permute-start | bytes 3145736 | tf_op jit(solution)/shard_map/ppermute | solution.py:977
  143.6 19.9 %collective-permute-start.12 = (bf16[8,512,128]{2,1,0:T(8,128)(2,1)}, bf16[8,512,128]{2,1,0:T(8,128)(2,1)}, u32[]{:S(2)}, u32[]{:S(2)}) collective-permute-start(bf16[8,512,128]{2,1,0:T(8,128)(2,1)} %join.7), channel_id=1, source_target_pairs={{0,16},{1,9},{2,18},{3,11},{4,20},{5,13},{6,22},{7,15},{8,24},{9,1... | collective-permute-start | bytes 3145736 | tf_op jit(solution)/shard_map/ppermute | solution.py:977
  144.8 18.7 %collective-permute-start.14 = (bf16[8,512,128]{2,1,0:T(8,128)(2,1)}, bf16[8,512,128]{2,1,0:T(8,128)(2,1)}, u32[]{:S(2)}, u32[]{:S(2)}) collective-permute-start(bf16[8,512,128]{2,1,0:T(8,128)(2,1)} %collective-permute-done.8), channel_id=1, source_target_pairs={{0,1},{1,0},{2,3},{3,2},{4,5},{5,4},{6,7},{7,6},{8,9},{9,8},{10,11... | collective-permute-start | bytes 3145736 | tf_op jit(solution)/shard_map/ppermute | solution.py:977
  145.6 16.3 %collective-permute-start.11 = (bf16[4,512,128]{2,1,0:T(8,128)(2,1)S(1)}, bf16[4,512,128]{2,1,0:T(8,128)(2,1)S(1)}, u32[]{:S(2)}, u32[]{:S(2)}) collective-permute-start(bf16[4,512,128]{2,1,0:T(8,128)(2,1)S(1)} %get-tuple-element.226.refs_0_), channel_id=1, source_target_pairs={{0,8},{1,17},{2,10},{3,19},{4,12},{5,21},{6,14},{7,23},{8,0},{9,25... | collective-permute-start | bytes 1572872 | tf_op jit(solution)/shard_map/ppermute | solution.py:977
  165.7 15.9 %collective-permute-start.16 = (bf16[8,512,128]{2,1,0:T(8,128)(2,1)}, bf16[8,512,128]{2,1,0:T(8,128)(2,1)}, u32[]{:S(2)}, u32[]{:S(2)}) collective-permute-start(bf16[8,512,128]{2,1,0:T(8,128)(2,1)} %join.8), channel_id=1, source_target_pairs={{0,1},{1,0},{2,3},{3,2},{4,5},{5,4},{6,7},{7,6},{8,9},{9,8},{10,11... | collective-permute-start | bytes 3145736 | tf_op jit(solution)/shard_map/ppermute | solution.py:977
  229.8 18.5 %collective-permute-start.19 = (bf16[16,2,2,128,128]{4,3,2,1,0:T(8,128)(2,1)}, bf16[16,2,2,128,128]{4,3,2,1,0:T(8,128)(2,1)S(1)}, u32[]{:S(2)}, u32[]{:S(2)}) collective-permute-start(bf16[16,2,2,128,128]{4,3,2,1,0:T(8,128)(2,1)} %get-tuple-element.266), channel_id=1, source_target_pairs={{0,1},{1,0},{2,3},{3,2},{4,5},{5,4},{6,7},{7,6},{8,9},{9,8},{10,11... | collective-permute-start | bytes 6291464 | tf_op jit(solution)/shard_map/ppermute | solution.py:977
  249.7 28.7 %collective-permute-start.23 = (bf16[16,2,2,128,128]{4,3,2,1,0:T(8,128)(2,1)}, bf16[16,2,2,128,128]{4,3,2,1,0:T(8,128)(2,1)S(1)}, u32[]{:S(2)}, u32[]{:S(2)}) collective-permute-start(bf16[16,2,2,128,128]{4,3,2,1,0:T(8,128)(2,1)} %get-tuple-element.278), channel_id=1, source_target_pairs={{0,1},{1,0},{2,3},{3,2},{4,5},{5,4},{6,7},{7,6},{8,9},{9,8},{10,11... | collective-permute-start | bytes 6291464 | tf_op jit(solution)/shard_map/ppermute | solution.py:977
  253.0 20.5 %collective-permute-start.20 = (bf16[2048,128]{1,0:T(8,128)(2,1)}, bf16[2048,128]{1,0:T(8,128)(2,1)S(1)}, u32[]{:S(2)}, u32[]{:S(2)}) collective-permute-start(bf16[2048,128]{1,0:T(8,128)(2,1)} %bitcast.160), channel_id=1, source_target_pairs={{0,8},{1,9},{2,10},{3,11},{4,12},{5,13},{6,14},{7,15},{8,0},{9,1},... | collective-permute-start | bytes 1572872 | tf_op jit(solution)/shard_map/ppermute | solution.py:977
  254.0 19.6 %collective-permute-start.21 = (bf16[2048,128]{1,0:T(8,128)(2,1)}, bf16[2048,128]{1,0:T(8,128)(2,1)S(1)}, u32[]{:S(2)}, u32[]{:S(2)}) collective-permute-start(bf16[2048,128]{1,0:T(8,128)(2,1)} %bitcast.158), channel_id=1, source_target_pairs={{0,16},{1,17},{2,18},{3,19},{4,20},{5,21},{6,22},{7,23},{8,24},{9,... | collective-permute-start | bytes 1572872 | tf_op jit(solution)/shard_map/ppermute | solution.py:977
  254.8 23.5 %collective-permute-start.22 = (bf16[2048,128]{1,0:T(8,128)(2,1)}, bf16[2048,128]{1,0:T(8,128)(2,1)S(1)}, u32[]{:S(2)}, u32[]{:S(2)}) collective-permute-start(bf16[2048,128]{1,0:T(8,128)(2,1)} %bitcast.156), channel_id=1, source_target_pairs={{0,24},{1,25},{2,26},{3,27},{4,28},{5,29},{6,30},{7,31},{8,16},{9,... | collective-permute-start | bytes 1572872 | tf_op jit(solution)/shard_map/ppermute | solution.py:977
  278.3 29.1 %collective-permute-start.27 = (bf16[16,2,2,128,128]{4,3,2,1,0:T(8,128)(2,1)}, bf16[16,2,2,128,128]{4,3,2,1,0:T(8,128)(2,1)}, u32[]{:S(2)}, u32[]{:S(2)}) collective-permute-start(bf16[16,2,2,128,128]{4,3,2,1,0:T(8,128)(2,1)} %get-tuple-element.294), channel_id=1, source_target_pairs={{0,1},{1,0},{2,3},{3,2},{4,5},{5,4},{6,7},{7,6},{8,9},{9,8},{10,11... | collective-permute-start | bytes 6291464 | tf_op jit(solution)/shard_map/ppermute | solution.py:977
  283.2 20.4 %collective-permute-start.24 = (bf16[2048,128]{1,0:T(8,128)(2,1)}, bf16[2048,128]{1,0:T(8,128)(2,1)S(1)}, u32[]{:S(2)}, u32[]{:S(2)}) collective-permute-start(bf16[2048,128]{1,0:T(8,128)(2,1)} %bitcast.159), channel_id=1, source_target_pairs={{0,8},{1,9},{2,10},{3,11},{4,12},{5,13},{6,14},{7,15},{8,0},{9,1},... | collective-permute-start | bytes 1572872 | tf_op jit(solution)/shard_map/ppermute | solution.py:977
  284.2 20.2 %collective-permute-start.25 = (bf16[2048,128]{1,0:T(8,128)(2,1)}, bf16[2048,128]{1,0:T(8,128)(2,1)S(1)}, u32[]{:S(2)}, u32[]{:S(2)}) collective-permute-start(bf16[2048,128]{1,0:T(8,128)(2,1)} %bitcast.157), channel_id=1, source_target_pairs={{0,16},{1,17},{2,18},{3,19},{4,20},{5,21},{6,22},{7,23},{8,24},{9,... | collective-permute-start | bytes 1572872 | tf_op jit(solution)/shard_map/ppermute | solution.py:977
  284.4 23.1 %collective-permute-start.26 = (bf16[2048,128]{1,0:T(8,128)(2,1)}, bf16[2048,128]{1,0:T(8,128)(2,1)S(1)}, u32[]{:S(2)}, u32[]{:S(2)}) collective-permute-start(bf16[2048,128]{1,0:T(8,128)(2,1)} %bitcast.155), channel_id=1, source_target_pairs={{0,24},{1,25},{2,26},{3,27},{4,28},{5,29},{6,30},{7,31},{8,16},{9,... | collective-permute-start | bytes 1572872 | tf_op jit(solution)/shard_map/ppermute | solution.py:977
  308.2 51.3 %all-to-all-start.4 = ((bf16[4,2048,128]{2,1,0:T(8,128)(2,1)}), bf16[4,2048,128]{2,1,0:T(8,128)(2,1)S(1)}, u32[]{:S(2)}, u32[]{:S(2)}) async-start(bf16[4,2048,128]{2,1,0:T(8,128)(2,1)} %bitcast.120), calls=%async_computation.4 | async-start | bytes 4194304 | tf_op jit(solution)/shard_map/all_to_all | solution.py:1013
  311.9 31.9 %collective-permute-start.28 = (bf16[16,2,2,128,128]{4,3,2,1,0:T(8,128)(2,1)}, bf16[16,2,2,128,128]{4,3,2,1,0:T(8,128)(2,1)}, u32[]{:S(2)}, u32[]{:S(2)}) collective-permute-start(bf16[16,2,2,128,128]{4,3,2,1,0:T(8,128)(2,1)} %get-tuple-element.296), channel_id=1, source_target_pairs={{0,1},{1,0},{2,3},{3,2},{4,5},{5,4},{6,7},{7,6},{8,9},{9,8},{10,11... | collective-permute-start | bytes 6291464 | tf_op jit(solution)/shard_map/ppermute | solution.py:977
  319.1 24.6 %collective-permute-start.30 = (bf16[2048,128]{1,0:T(8,128)(2,1)}, bf16[2048,128]{1,0:T(8,128)(2,1)S(1)}, u32[]{:S(2)}, u32[]{:S(2)}) collective-permute-start(bf16[2048,128]{1,0:T(8,128)(2,1)} %bitcast.163), channel_id=1, source_target_pairs={{0,16},{1,17},{2,18},{3,19},{4,20},{5,21},{6,22},{7,23},{8,24},{9,... | collective-permute-start | bytes 1572872 | tf_op jit(solution)/shard_map/ppermute | solution.py:977
  319.9 23.8 %collective-permute-start.31 = (bf16[2048,128]{1,0:T(8,128)(2,1)}, bf16[2048,128]{1,0:T(8,128)(2,1)S(1)}, u32[]{:S(2)}, u32[]{:S(2)}) collective-permute-start(bf16[2048,128]{1,0:T(8,128)(2,1)} %bitcast.161), channel_id=1, source_target_pairs={{0,24},{1,25},{2,26},{3,27},{4,28},{5,29},{6,30},{7,31},{8,16},{9,... | collective-permute-start | bytes 1572872 | tf_op jit(solution)/shard_map/ppermute | solution.py:977
  400.0 73.0 %all-to-all-start.6 = ((bf16[4,1536,128]{2,1,0:T(8,128)(2,1)}), bf16[4,1536,128]{2,1,0:T(8,128)(2,1)}, u32[]{:S(2)}, u32[]{:S(2)}) async-start(bf16[4,1536,128]{2,1,0:T(8,128)(2,1)} %all_to_all.36), calls=%async_computation.6 | async-start | bytes 3145728 | tf_op jit(solution)/shard_map/all_to_all | solution.py:1016
  408.2 25.1 %collective-permute-start.32 = (bf16[2048,128]{1,0:T(8,128)(2,1)}, bf16[2048,128]{1,0:T(8,128)(2,1)S(1)}, u32[]{:S(2)}, u32[]{:S(2)}) collective-permute-start(bf16[2048,128]{1,0:T(8,128)(2,1)} %bitcast.166), channel_id=1, source_target_pairs={{0,8},{1,9},{2,10},{3,11},{4,12},{5,13},{6,14},{7,15},{8,0},{9,1},... | collective-permute-start | bytes 1572872 | tf_op jit(solution)/shard_map/ppermute | solution.py:977
  409.4 23.9 %collective-permute-start.33 = (bf16[2048,128]{1,0:T(8,128)(2,1)}, bf16[2048,128]{1,0:T(8,128)(2,1)S(1)}, u32[]{:S(2)}, u32[]{:S(2)}) collective-permute-start(bf16[2048,128]{1,0:T(8,128)(2,1)} %bitcast.164), channel_id=1, source_target_pairs={{0,16},{1,17},{2,18},{3,19},{4,20},{5,21},{6,22},{7,23},{8,24},{9,... | collective-permute-start | bytes 1572872 | tf_op jit(solution)/shard_map/ppermute | solution.py:977
  409.7 34.8 %collective-permute-start.34 = (bf16[2048,128]{1,0:T(8,128)(2,1)}, bf16[2048,128]{1,0:T(8,128)(2,1)S(1)}, u32[]{:S(2)}, u32[]{:S(2)}) collective-permute-start(bf16[2048,128]{1,0:T(8,128)(2,1)} %bitcast.162), channel_id=1, source_target_pairs={{0,24},{1,25},{2,26},{3,27},{4,28},{5,29},{6,30},{7,31},{8,16},{9,... | collective-permute-start | bytes 1572872 | tf_op jit(solution)/shard_map/ppermute | solution.py:977
  447.7 16.2 %collective-permute-start.35 = (bf16[512,128]{1,0:T(8,128)(2,1)}, bf16[512,128]{1,0:T(8,128)(2,1)S(1)}, u32[]{:S(2)}, u32[]{:S(2)}) collective-permute-start(bf16[512,128]{1,0:T(8,128)(2,1)} %bitcast.170), channel_id=1, source_target_pairs={{0,0},{1,1},{2,10},{3,11},{4,20},{5,21},{6,30},{7,31},{8,2},{9,3},... | collective-permute-start | bytes 393224 | tf_op jit(solution)/shard_map/ppermute | solution.py:977
  457.2 15.7 %collective-permute-start.38 = (bf16[512,128]{1,0:T(8,128)(2,1)}, bf16[512,128]{1,0:T(8,128)(2,1)S(1)}, u32[]{:S(2)}, u32[]{:S(2)}) collective-permute-start(bf16[512,128]{1,0:T(8,128)(2,1)} %bitcast.167), channel_id=1, source_target_pairs={{0,6},{1,7},{2,12},{3,13},{4,18},{5,19},{6,24},{7,25},{8,4},{9,5},... | collective-permute-start | bytes 393224 | tf_op jit(solution)/shard_map/ppermute | solution.py:977
  (49 other events, 487.5 us)
